TPU v7x, 32 devices: a whole 2x2x4 slice. The times are simulated.
32 devices in a mesh: segment: 2 (over x), expert: 16 (over z, y, core).
Axes of the slice: x: 2, y: 2, z: 4, core: 2. Of those that a mesh axis runs over, the one named last changes fastest.
Arguments:
- states: bfloat16 [2, 64, 7168], P('segment', 'expert'), may hold values from -6 to 6
- routing: int32 [2, 2, 64, 2], P('segment', None, 'expert'), may hold values from 0 to 3, all different within a row; in each aligned block of 4 rows (0 to 3, 4 to 7, ..., all dimensions but the last counted through in order) at most 4 rows name the same one
- route_weight: bfloat16 [2, 2, 64, 2], P('segment', None, 'expert'), may hold values from 0.19921875 to 1
- norm_gain: float32 [2, 7168], P('segment'), may hold values from 0.1 to 1.9
- gate_proj: bfloat16 [2, 7168, 4096], P('segment', None, 'expert'), may hold values from -0.0625 to 0.0625
- up_proj: bfloat16 [2, 7168, 4096], P('segment', None, 'expert'), may hold values from -0.0625 to 0.0625
- down_proj: bfloat16 [2, 4096, 7168], P('segment', 'expert'), may hold values from -0.1875 to 0.1875
Outputs:
- new_states: bfloat16 [2, 64, 7168], P('segment', 'expert')
Inputs may be any that keep to these rules, and one draw needn't show every extreme that they name: `routing`: in each aligned block of 4 rows (the rows of one device for one layer and pass) no expert is named by more than 4 rows, and some block reaches 4; each row names 2 different experts.
All inputs are finite; a program needn't handle non-finite values.
Results may differ from a plain program's by a relative error of at most 0.015.
Values may be sent and summed in bfloat16 or wider, within the bound.
No kernel may reach another device: no remote copies, remote signals or barrier semaphores. Data moves between devices by JAX's collectives and lax.ppermute only.
A program may use at most 64 MiB of HBM per device.

v0:
```python
import jax
import jax.numpy as jnp
from jax import lax
from jax.sharding import PartitionSpec as P

GROUP = 4


def shifted(value, axis, steps):
    count = lax.axis_size(axis)
    pairs = [(source, (source + steps) % count) for source in range(count)]
    return lax.ppermute(value, axis, pairs)


def on_device(states, routing, route_weight, norm_gain, gate_proj, up_proj, down_proj):
    owners = lax.axis_size("expert")
    experts = owners // GROUP
    row_dev = states.shape[1]
    model_dim = states.shape[2]
    passes_count = routing.shape[1]
    top_k = routing.shape[3]
    capacity = max(2, min(row_dev, 2 * row_dev * top_k // experts))
    gain_row = norm_gain[0]
    gate_mat = gate_proj[0]
    up_mat = up_proj[0]
    down_mat = down_proj[0]
    expert_ids = jnp.arange(experts, dtype=jnp.int32)
    slot_ids = jnp.arange(capacity, dtype=jnp.int32)

    def expert_terms(slot_rows, slot_weight):
        lead_shape = slot_rows.shape[:2]
        flat_rows = slot_rows.reshape(-1, model_dim)
        gated = jnp.dot(flat_rows, gate_mat, preferred_element_type=jnp.float32)
        up_part = jnp.dot(flat_rows, up_mat, preferred_element_type=jnp.float32)
        inner_act = (jax.nn.silu(gated) * up_part).astype(jnp.bfloat16)
        partial_out = jnp.dot(inner_act, down_mat, preferred_element_type=jnp.float32)
        scaled = slot_weight.reshape(-1, 1).astype(jnp.float32) * partial_out
        return scaled.astype(jnp.bfloat16).reshape(lead_shape + (model_dim,))

    def advance(step_no, current):
        chosen = lax.dynamic_index_in_dim(routing[0], step_no, 0, keepdims=False)
        weights_now = lax.dynamic_index_in_dim(route_weight[0], step_no, 0, keepdims=False)
        picked = chosen[:, :, None] == expert_ids[None, None, :]
        dense_weight = jnp.sum(
            jnp.where(picked, weights_now[:, :, None].astype(jnp.float32), jnp.float32(0.0)), axis=1
        )
        current_f = current.astype(jnp.float32)
        inv_rms = lax.rsqrt(jnp.mean(current_f * current_f, axis=1, keepdims=True) + 1e-06)
        normed = (current_f * inv_rms * gain_row).astype(jnp.bfloat16)
        member = (dense_weight > 0.0).T
        slot_rank = jnp.cumsum(member.astype(jnp.int32), axis=1) - 1
        placer = (member[:, None, :] & (slot_rank[:, None, :] == slot_ids[None, :, None])).astype(
            jnp.bfloat16
        )
        packed = jnp.einsum(
            "ecr,rd->ecd", placer, normed, preferred_element_type=jnp.float32
        ).astype(jnp.bfloat16)
        packed_weight = jnp.sum(
            placer.astype(jnp.float32) * dense_weight.T[:, None, :], axis=2
        ).astype(jnp.bfloat16)
        outgoing = jnp.repeat(packed, GROUP, axis=0)
        outgoing_weight = jnp.repeat(packed_weight, GROUP, axis=0)
        term_rows = expert_terms(
            lax.all_to_all(outgoing, "expert", split_axis=0, concat_axis=0, tiled=True),
            lax.all_to_all(outgoing_weight, "expert", split_axis=0, concat_axis=0, tiled=True),
        )
        returned = lax.all_to_all(term_rows, "expert", split_axis=0, concat_axis=0, tiled=True)
        returned = returned.reshape(experts, GROUP, capacity, model_dim)
        branch_sum = jnp.einsum(
            "ecr,egcd->rd", placer, returned, preferred_element_type=jnp.float32
        )
        updated = (current_f + branch_sum).astype(jnp.bfloat16)
        return shifted(updated, "segment", 1)

    finished = lax.fori_loop(0, passes_count, advance, states[0])
    return finished[None]


def solution(mesh):
    return jax.shard_map(
        on_device,
        mesh=mesh,
        in_specs=(
            P("segment", "expert", None),
            P("segment", None, "expert", None),
            P("segment", None, "expert", None),
            P("segment", None),
            P("segment", None, "expert"),
            P("segment", None, "expert"),
            P("segment", "expert", None),
        ),
        out_specs=P("segment", "expert", None),
        check_vma=False,
    )
```

profile of v0, /device:TPU:0, one launch (start us, length us, event | category | flops | bytes accessed | tf_op | source)
XLA Modules:
  0.0 167.0 jit_solution(6025319647179167514)
XLA Ops:
  0.0 0.8 copy.40
  0.8 165.5 %while.17 = (s32[]{:T(128)}, bf16[4,7168]{1,0:T(4,128)(2,1)S(1)}, s32[1,2,4,2]{2,3,1,0:T(2,128)}, bf16[1,2,4,2]{2,3,1,0:T(2,128)(2,1)}, f32[1,7168]{1,0:T(1,128)...) while((s32[]{:T(128)}, bf16[4,7168]{1,0:T(4,128)(2,1)S(1)}, ...), condition=%wide.region_6.7_spmd.clone.clone, body=%wide.region_0.6_spmd.clone.clone.sunk | while | flops 708698752 | bytes 25410856 | solution.py:75
  0.8 0.7 bitcast_convert_fusion.2
  1.5 0.7 dynamic-slice_bitcast_fusion.2
  2.2 0.1 select_reduce_fusion.2
  2.3 0.1 broadcast_in_dim.84
  2.4 0.1 all_to_all.43
  2.5 0.7 copy.31
  3.2 7.4 %all-to-all-start.1 = ((bf16[16,1,4]{2,1,0:T(2,128)(2,1)}), bf16[16,1,4]{2,1,0:T(2,128)(2,1)S(1)}, u32[]{:S(2)}, u32[]{:S(2)}) async-start(bf16[16,1,4]{2,1,0:T(2,128)(2,1)} %copy.31), calls=%async_computation.1 | async-start | bytes 16384 | tf_op jit(solution)/shard_map/while/body/eval_jaxpr/all_to_all | solution.py:65
  10.6 0.2 fusion.56
  10.8 0.1 copy.30
  10.9 1.0 convolution_convert_fusion.2
  11.9 5.0 %all-to-all-done.1 = bf16[16,1,4]{2,1,0:T(2,128)(2,1)S(1)} async-done(((bf16[16,1,4]{2,1,0:T(2,128)(2,1)}), bf16[16,1,4]{2,1,0:T(2,128)(2,1)S(1)}, u32[]{:S(2)}, u32[]{:S(2)}) %all-to-all-start.1) | async-done | bytes 160 | tf_op jit(solution)/shard_map/while/body/eval_jaxpr/all_to_all | solution.py:65
  16.9 1.2 broadcast_in_dim.83
  18.1 3.6 %all-to-all-start = ((bf16[16,4,7168]{2,1,0:T(4,128)(2,1)}), bf16[16,4,7168]{2,1,0:T(4,128)(2,1)S(1)}, u32[]{:S(2)}, u32[]{:S(2)}) async-start(bf16[16,4,7168]{2,1,0:T(4,128)(2,1)} %bitcast.65), calls=%async_computation | async-start | bytes 1835008 | tf_op jit(solution)/shard_map/while/body/eval_jaxpr/all_to_all | solution.py:64
  21.8 0.1 reshape.134
  21.9 20.6 %all-to-all-done = bf16[16,4,7168]{2,1,0:T(4,128)(2,1)S(1)} async-done(((bf16[16,4,7168]{2,1,0:T(4,128)(2,1)}), bf16[16,4,7168]{2,1,0:T(4,128)(2,1)S(1)}, u32[]{:S(2)}, u32[]{:S(2)}) %all-to-all-start) | async-done | bytes 917536 | tf_op jit(solution)/shard_map/while/body/eval_jaxpr/all_to_all | solution.py:64
  42.5 0.2 reshape.133
  42.7 2.8 %fusion.57 = f32[64,256]{1,0:T(8,128)S(1)} fusion(bf16[64,7168]{1,0:T(8,128)(2,1)S(1)} %reshape.133, bf16[7168,256]{1,0:T(8,128)(2,1)} %get-tuple-element.405), kind=kOutput, calls=%fused_computation.38.clone.1 | convolution fusion | flops 234881024 | bytes 4653056 | tf_op jit(solution)/shard_map/while/body/eval_jaxpr/dot_general | solution.py:33
  45.5 5.5 %fusion.58 = bf16[64,7168]{1,0:T(8,128)(2,1)S(1)} fusion(bf16[256,7168]{1,0:T(8,128)(2,1)} %get-tuple-element.407, bf16[64,7168]{1,0:T(8,128)(2,1)S(1)} %reshape.133, bf16[7168,256]{1,0:T(8,128)(2,1)} %get-tuple-element.406, f32[64]{0:T(128)S(1)} %reshape.134, f32[64,256]{1,0:T(8,128)S(1)} %fusion.57), kind=kOutput, calls=%fused_computation.2.clone.1 | convolution fusion | flops 470777856 | bytes 9240832 | tf_op jit(solution)/shard_map/while/body/eval_jaxpr/dot_general | solution.py:36
  51.0 0.3 reshape.135
  51.3 28.5 %all_to_all.49 = bf16[16,4,7168]{2,1,0:T(4,128)(2,1)S(1)} all-to-all(bf16[16,4,7168]{2,1,0:T(4,128)(2,1)S(1)} %reshape.135), channel_id=1, replica_groups=mesh['segment'=2,'expert'=16] {'expert'}, dimensions={0} | all-to-all | bytes 1835008 | tf_op jit(solution)/shard_map/while/body/eval_jaxpr/all_to_all | solution.py:67
  79.8 0.5 convert_reduce_fusion.5
  80.2 0.3 fusion.59
  80.6 1.6 collective-permute-start
  82.1 3.1 %collective-permute-done = bf16[4,7168]{1,0:T(4,128)(2,1)S(1)} collective-permute-done((bf16[4,7168]{1,0:T(4,128)(2,1)S(1)}, bf16[4,7168]{1,0:T(4,128)(2,1)S(1)}, u32[]{:S(2)}, u32[]{:S(2)}) %collective-permute-start) | collective-permute-done | bytes 57376 | tf_op jit(solution)/shard_map/while/body/eval_jaxpr/ppermute | solution.py:12
  85.2 0.7 bitcast_convert_fusion.2
  85.9 0.7 dynamic-slice_bitcast_fusion.2
  86.6 0.1 select_reduce_fusion.2
  86.7 0.1 broadcast_in_dim.84
  86.8 0.1 all_to_all.43
  86.9 0.7 copy.31
  87.6 4.1 %all-to-all-start.1 = ((bf16[16,1,4]{2,1,0:T(2,128)(2,1)}), bf16[16,1,4]{2,1,0:T(2,128)(2,1)S(1)}, u32[]{:S(2)}, u32[]{:S(2)}) async-start(bf16[16,1,4]{2,1,0:T(2,128)(2,1)} %copy.31), calls=%async_computation.1 | async-start | bytes 16384 | tf_op jit(solution)/shard_map/while/body/eval_jaxpr/all_to_all | solution.py:65
  91.7 0.2 fusion.56
  91.9 0.1 copy.30
  92.0 1.0 convolution_convert_fusion.2
  93.0 5.0 %all-to-all-done.1 = bf16[16,1,4]{2,1,0:T(2,128)(2,1)S(1)} async-done(((bf16[16,1,4]{2,1,0:T(2,128)(2,1)}), bf16[16,1,4]{2,1,0:T(2,128)(2,1)S(1)}, u32[]{:S(2)}, u32[]{:S(2)}) %all-to-all-start.1) | async-done | bytes 160 | tf_op jit(solution)/shard_map/while/body/eval_jaxpr/all_to_all | solution.py:65
  98.0 1.2 broadcast_in_dim.83
  99.2 3.6 %all-to-all-start = ((bf16[16,4,7168]{2,1,0:T(4,128)(2,1)}), bf16[16,4,7168]{2,1,0:T(4,128)(2,1)S(1)}, u32[]{:S(2)}, u32[]{:S(2)}) async-start(bf16[16,4,7168]{2,1,0:T(4,128)(2,1)} %bitcast.65), calls=%async_computation | async-start | bytes 1835008 | tf_op jit(solution)/shard_map/while/body/eval_jaxpr/all_to_all | solution.py:64
  102.9 0.1 reshape.134
  103.0 20.6 %all-to-all-done = bf16[16,4,7168]{2,1,0:T(4,128)(2,1)S(1)} async-done(((bf16[16,4,7168]{2,1,0:T(4,128)(2,1)}), bf16[16,4,7168]{2,1,0:T(4,128)(2,1)S(1)}, u32[]{:S(2)}, u32[]{:S(2)}) %all-to-all-start) | async-done | bytes 917536 | tf_op jit(solution)/shard_map/while/body/eval_jaxpr/all_to_all | solution.py:64
  123.6 0.2 reshape.133
  123.8 2.8 %fusion.57 = f32[64,256]{1,0:T(8,128)S(1)} fusion(bf16[64,7168]{1,0:T(8,128)(2,1)S(1)} %reshape.133, bf16[7168,256]{1,0:T(8,128)(2,1)} %get-tuple-element.405), kind=kOutput, calls=%fused_computation.38.clone.1 | convolution fusion | flops 234881024 | bytes 4653056 | tf_op jit(solution)/shard_map/while/body/eval_jaxpr/dot_general | solution.py:33
  126.6 5.5 %fusion.58 = bf16[64,7168]{1,0:T(8,128)(2,1)S(1)} fusion(bf16[256,7168]{1,0:T(8,128)(2,1)} %get-tuple-element.407, bf16[64,7168]{1,0:T(8,128)(2,1)S(1)} %reshape.133, bf16[7168,256]{1,0:T(8,128)(2,1)} %get-tuple-element.406, f32[64]{0:T(128)S(1)} %reshape.134, f32[64,256]{1,0:T(8,128)S(1)} %fusion.57), kind=kOutput, calls=%fused_computation.2.clone.1 | convolution fusion | flops 470777856 | bytes 9240832 | tf_op jit(solution)/shard_map/while/body/eval_jaxpr/dot_general | solution.py:36
  132.0 0.3 reshape.135
  132.4 28.5 %all_to_all.49 = bf16[16,4,7168]{2,1,0:T(4,128)(2,1)S(1)} all-to-all(bf16[16,4,7168]{2,1,0:T(4,128)(2,1)S(1)} %reshape.135), channel_id=1, replica_groups=mesh['segment'=2,'expert'=16] {'expert'}, dimensions={0} | all-to-all | bytes 1835008 | tf_op jit(solution)/shard_map/while/body/eval_jaxpr/all_to_all | solution.py:67
  160.9 0.5 convert_reduce_fusion.5
  161.3 0.3 fusion.59
  161.7 1.6 collective-permute-start
  163.2 3.1 %collective-permute-done = bf16[4,7168]{1,0:T(4,128)(2,1)S(1)} collective-permute-done((bf16[4,7168]{1,0:T(4,128)(2,1)S(1)}, bf16[4,7168]{1,0:T(4,128)(2,1)S(1)}, u32[]{:S(2)}, u32[]{:S(2)}) %collective-permute-start) | collective-permute-done | bytes 57376 | tf_op jit(solution)/shard_map/while/body/eval_jaxpr/ppermute | solution.py:12
  166.3 0.6 copy.41
  (12 shorter events, 0.2 us)
Async XLA Ops:
  3.2 13.7 %all-to-all-start.1 = ((bf16[16,1,4]{2,1,0:T(2,128)(2,1)}), bf16[16,1,4]{2,1,0:T(2,128)(2,1)S(1)}, u32[]{:S(2)}, u32[]{:S(2)}) async-start(bf16[16,1,4]{2,1,0:T(2,128)(2,1)} %copy.31), calls=%async_computation.1 | async-start | bytes 16384 | tf_op jit(solution)/shard_map/while/body/eval_jaxpr/all_to_all | solution.py:65
  18.1 24.4 %all-to-all-start = ((bf16[16,4,7168]{2,1,0:T(4,128)(2,1)}), bf16[16,4,7168]{2,1,0:T(4,128)(2,1)S(1)}, u32[]{:S(2)}, u32[]{:S(2)}) async-start(bf16[16,4,7168]{2,1,0:T(4,128)(2,1)} %bitcast.65), calls=%async_computation | async-start | bytes 1835008 | tf_op jit(solution)/shard_map/while/body/eval_jaxpr/all_to_all | solution.py:64
  80.6 4.7 %collective-permute-start = (bf16[4,7168]{1,0:T(4,128)(2,1)S(1)}, bf16[4,7168]{1,0:T(4,128)(2,1)S(1)}, u32[]{:S(2)}, u32[]{:S(2)}) collective-permute-start(bf16[4,7168]{1,0:T(4,128)(2,1)S(1)} %fusion.59), channel_id=1, source_target_pairs={{0,16},{16,0},{1,17},{17,1},{2,18},{18,2},{3,19},{19,3},{4,20},{20... | collective-permute-start | bytes 172040 | tf_op jit(solution)/shard_map/while/body/eval_jaxpr/ppermute | solution.py:12
  87.6 10.4 %all-to-all-start.1 = ((bf16[16,1,4]{2,1,0:T(2,128)(2,1)}), bf16[16,1,4]{2,1,0:T(2,128)(2,1)S(1)}, u32[]{:S(2)}, u32[]{:S(2)}) async-start(bf16[16,1,4]{2,1,0:T(2,128)(2,1)} %copy.31), calls=%async_computation.1 | async-start | bytes 16384 | tf_op jit(solution)/shard_map/while/body/eval_jaxpr/all_to_all | solution.py:65
  99.2 24.4 %all-to-all-start = ((bf16[16,4,7168]{2,1,0:T(4,128)(2,1)}), bf16[16,4,7168]{2,1,0:T(4,128)(2,1)S(1)}, u32[]{:S(2)}, u32[]{:S(2)}) async-start(bf16[16,4,7168]{2,1,0:T(4,128)(2,1)} %bitcast.65), calls=%async_computation | async-start | bytes 1835008 | tf_op jit(solution)/shard_map/while/body/eval_jaxpr/all_to_all | solution.py:64
  161.7 4.7 %collective-permute-start = (bf16[4,7168]{1,0:T(4,128)(2,1)S(1)}, bf16[4,7168]{1,0:T(4,128)(2,1)S(1)}, u32[]{:S(2)}, u32[]{:S(2)}) collective-permute-start(bf16[4,7168]{1,0:T(4,128)(2,1)S(1)} %fusion.59), channel_id=1, source_target_pairs={{0,16},{16,0},{1,17},{17,1},{2,18},{18,2},{3,19},{19,3},{4,20},{20... | collective-permute-start | bytes 172040 | tf_op jit(solution)/shard_map/while/body/eval_jaxpr/ppermute | solution.py:12
where the time goes:
time: 168 us; the launch traced here: 167 us
  waiting for transfers between devices  57.5 us (34%)
  blocking collectives  57 us (34%)
  starting transfers between devices  21.8 us (13%)
  matrix products  19.2 us (11%)
  local copies, waits for them, and re-layouts  8.38 us (5%)
  other arithmetic  2.96 us (2%)
    all_to_all x2, blocking collectives, advance(): lax.all_to_all(term_rows, 'expert', split_axis=0, concat_axis=0, tiled=True)  57 us
    all_to_all x2, waiting for transfers between devices, advance(): lax.all_to_all(outgoing, 'expert', split_axis=0, concat_axis=0, tiled=True)  41.3 us
    all_to_all x2, starting transfers between devices, advance(): lax.all_to_all(outgoing_weight, 'expert', split_axis=0, concat_axis=0, ti...  11.4 us
    dot_general x2, matrix products, expert_terms(): jnp.dot(inner_act, down_mat, preferred_element_type=jnp.float32)  10.9 us
    all_to_all x2, waiting for transfers between devices, advance(): lax.all_to_all(outgoing_weight, 'expert', split_axis=0, concat_axis=0, ti...  10 us
    all_to_all x2, starting transfers between devices, advance(): lax.all_to_all(outgoing, 'expert', split_axis=0, concat_axis=0, tiled=True)  7.27 us
    ppermute x2, waiting for transfers between devices, shifted(): return lax.ppermute(value, axis, pairs)  6.2 us
    dot_general x2, matrix products, expert_terms(): gated = jnp.dot(flat_rows, gate_mat, preferred_element_type=jnp.float32)  5.52 us
  transfers between devices with their start and end apart: 6, of which 6 were waited for; matrix products, arithmetic and copies ran while one was open for 2% of the time, Pallas kernels for 0%

commit v1 on v0

v1 whole, which is shorter than its diff:
```python
import jax
import jax.numpy as jnp
from jax import lax
from jax.sharding import PartitionSpec as P

GROUP = 4


def shifted(value, axis, steps):
    count = lax.axis_size(axis)
    pairs = [(source, (source + steps) % count) for source in range(count)]
    return lax.ppermute(value, axis, pairs)


def on_device(states, routing, route_weight, norm_gain, gate_proj, up_proj, down_proj):
    owners = lax.axis_size("expert")
    experts = owners // GROUP
    passes_count = routing.shape[1]
    gain_row = norm_gain[0]
    gate_mat = gate_proj[0]
    up_mat = up_proj[0]
    down_mat = down_proj[0]
    expert_ids = jnp.arange(experts, dtype=jnp.int32)

    picked = routing[0][..., None] == expert_ids
    dense = jnp.sum(jnp.where(picked, route_weight[0][..., None].astype(jnp.float32), 0.0), axis=2)
    dense = lax.all_gather(dense.astype(jnp.bfloat16), "expert", axis=1, tiled=True)
    mine = lax.axis_index("expert") // GROUP
    row_weight = lax.dynamic_index_in_dim(dense, mine, 2, keepdims=True).astype(jnp.float32)

    current = states[0]
    for step_no in range(passes_count):
        current_f = current.astype(jnp.float32)
        inv_rms = lax.rsqrt(jnp.mean(current_f * current_f, axis=1, keepdims=True) + 1e-06)
        normed = (current_f * inv_rms * gain_row).astype(jnp.bfloat16)
        rows = lax.all_gather(normed, "expert", axis=0, tiled=True)
        gated = jnp.dot(rows, gate_mat, preferred_element_type=jnp.float32)
        up_part = jnp.dot(rows, up_mat, preferred_element_type=jnp.float32)
        inner_act = (jax.nn.silu(gated) * up_part).astype(jnp.bfloat16)
        partial_out = jnp.dot(inner_act, down_mat, preferred_element_type=jnp.float32)
        weight = row_weight[step_no]
        terms = jnp.where(weight > 0.0, weight * partial_out, 0.0).astype(jnp.bfloat16)
        branch_sum = lax.psum_scatter(terms, "expert", scatter_dimension=0, tiled=True)
        updated = (current_f + branch_sum.astype(jnp.float32)).astype(jnp.bfloat16)
        current = shifted(updated, "segment", 1)
    return current[None]


def solution(mesh):
    return jax.shard_map(
        on_device,
        mesh=mesh,
        in_specs=(
            P("segment", "expert", None),
            P("segment", None, "expert", None),
            P("segment", None, "expert", None),
            P("segment", None),
            P("segment", None, "expert"),
            P("segment", None, "expert"),
            P("segment", "expert", None),
        ),
        out_specs=P("segment", "expert", None),
        check_vma=False,
    )
```

time: 168 us -> 294 us (1.75)
  waiting for transfers between devices: 57.5 us -> 184 us
  starting transfers between devices: 21.8 us -> 3.11 us
  between operations: 0.01 us -> 14.2 us
  blocking collectives: 57 us -> 66.4 us
  local copies, waits for them, and re-layouts: 8.38 us -> 2.21 us
    unnamed x0 -> x4, waiting for transfers between devices: none -> 178 us
    all_gather x0 -> x3, blocking collectives: none -> 66.4 us  [the longest x2 43.2 us: on_device(): rows = lax.all_gather(normed, 'expert', axis=0, tiled=True)]
    all_to_all x2 -> x0, blocking collectives: 57 us -> none  [advance(): lax.all_to_all(term_rows, 'expert', split_axis=0, concat_axis=0, tiled=True)]
    all_to_all x4 -> x0, waiting for transfers between devices: 51.3 us -> none  [the longest x2 41.3 us: advance(): lax.all_to_all(outgoing, 'expert', split_axis=0, concat_axis=0, tiled=True)]
    all_to_all x4 -> x0, starting transfers between devices: 18.7 us -> none  [the longest x2 11.4 us: advance(): lax.all_to_all(outgoing_weight, 'expert', split_axis=0, concat_axis=0, ti...]
    dot_general x8 -> x4, matrix products: 19.2 us -> 18.4 us  [the longest x2 12.9 us: on_device(): jnp.dot(inner_act, down_mat, preferred_element_type=jnp.float32)]
  transfers between devices with their start and end apart: 6 -> 4, of which waited for: 6 -> 4; matrix products, arithmetic and copies ran while one was open for 2% -> 0% of each run, Pallas kernels for 0% -> 0%
where the time goes in v1:
time: 294 us
  waiting for transfers between devices  184 us (63%)
  blocking collectives  66.4 us (23%)
  matrix products  18.4 us (6%)
  between operations  14.2 us (5%)
  other arithmetic  5.66 us (2%)
  starting transfers between devices  3.11 us (1%)
    unnamed x4, waiting for transfers between devices  178 us
    all_gather x2, blocking collectives, on_device(): rows = lax.all_gather(normed, 'expert', axis=0, tiled=True)  43.2 us
    all_gather x1, blocking collectives, on_device(): lax.all_gather(dense.astype(jnp.bfloat16), 'expert', axis=1, tiled=True)  23.2 us
    dot_general x2, matrix products, on_device(): jnp.dot(inner_act, down_mat, preferred_element_type=jnp.float32)  12.9 us
  transfers between devices with their start and end apart: 4, of which 4 were waited for; matrix products, arithmetic and copies ran while one was open for 0% of the time, Pallas kernels for 0%

profile of v1, /device:TPU:0, one launch (start us, length us, event | category | flops | bytes accessed | tf_op | source)
XLA Modules:
  0.0 293.6 jit_solution(2080023691113734254)
XLA Ops:
  6.5 0.0 all-reduce.5.cloned.1.call-start
  6.5 1.0 fusion.34
  7.5 0.7 bitcast_convert_fusion
  8.2 0.8 select_reduce_fusion
  9.0 23.2 %all_gather.9 = bf16[2,64,4]{2,0,1:T(2,128)(2,1)S(1)} all-gather(bf16[2,4,4]{2,0,1:T(2,128)(2,1)S(1)} %copy.14), channel_id=1, replica_groups=mesh['segment'=2,'expert'=16] {'expert'}, dimensions={1}, use_global_device_ids=true | all-gather | bytes 1088 | tf_op jit(solution)/shard_map/all_gather | solution.py:27
  32.2 0.1 dynamic-slice_convert_fusion
  32.3 0.6 slice_reduce_fusion
  32.9 0.9 fusion.48
  33.8 20.0 %all-gather = bf16[16,4,7168]{2,1,0:T(4,128)(2,1)S(1)} all-gather(bf16[1,4,7168]{2,1,0:T(4,128)(2,1)S(1)} %fusion.48), channel_id=1, replica_groups=mesh['segment'=2,'expert'=16] {'expert'}, dimensions={0}, use_global_device_ids=true | all-gather | bytes 974848 | tf_op jit(solution)/shard_map/all_gather | solution.py:36
  53.8 0.2 reshape.47
  54.0 2.8 fusion.12
  56.8 0.0 copy-start.2
  56.8 0.0 copy-start
  56.8 0.0 copy-start.1
  56.8 6.4 %fusion.2 = bf16[64,7168]{1,0:T(8,128)(2,1)} fusion(bf16[1,256,7168]{2,1,0:T(8,128)(2,1)} %param.13, f32[64]{0:T(128)S(1)} %get-tuple-element.6, pred[64]{0:T(512)(128)(4,1)S(1)} %broadcast_compare_fusion.1, bf16[64,7168]{1,0:T(8,128)(2,1)S(1)} %reshape.47, bf16[1,7168,256]{2,1,0:T(8,128)(2,1)} %param.12, f32[64,256]{1,0:T(8,128)S(1)} %fusion.12), kind=kOutput, calls=%fused_computation.4 | convolution fusion | flops 471236608 | bytes 9240896 | tf_op jit(solution)/shard_map/dot_general | solution.py:40
  63.3 0.0 all-reduce.5.cloned.1.call-update
  63.3 0.0 all-reduce.7.cloned.1.call-start
  63.4 0.0 copy-done.2
  63.4 0.6 dynamic-slice
  64.6 89.1 %all-reduce.5.cloned.1.call-done = bf16[64,7168]{1,0:T(8,128)(2,1)} async-done(((bf16[64,7168]{1,0:T(8,128)(2,1)}), bf16[64,7168]{1,0:T(8,128)(2,1)}) %all-reduce.5.cloned.1.call-update) | async-done | bytes 917520
  153.7 0.0 copy-done
  153.7 0.9 fusion.37
  154.7 1.5 collective-permute-start
  156.2 2.7 collective-permute-done
  158.9 0.2 fusion.30
  159.1 0.0 copy-done.1
  159.1 0.1 fusion.49
  159.2 23.2 %all-gather.1 = bf16[16,4,7168]{2,1,0:T(4,128)(2,1)S(1)} all-gather(bf16[1,4,7168]{2,1,0:T(4,128)(2,1)S(1)} %fusion.49), channel_id=1, replica_groups=mesh['segment'=2,'expert'=16] {'expert'}, dimensions={0}, use_global_device_ids=true | all-gather | bytes 974848 | tf_op jit(solution)/shard_map/all_gather | solution.py:36
  182.4 0.2 reshape.49
  182.6 2.8 fusion.10
  185.4 6.4 %fusion.3 = bf16[64,7168]{1,0:T(8,128)(2,1)} fusion(bf16[1,256,7168]{2,1,0:T(8,128)(2,1)} %param.13, f32[64]{0:T(128)S(1)} %get-tuple-element.5, pred[64]{0:T(512)(128)(4,1)S(1)} %broadcast_compare_fusion, bf16[64,7168]{1,0:T(8,128)(2,1)S(1)} %reshape.49, bf16[1,7168,256]{2,1,0:T(8,128)(2,1)} %param.12, f32[64,256]{1,0:T(8,128)S(1)} %fusion.10), kind=kOutput, calls=%fused_computation.5 | convolution fusion | flops 471236608 | bytes 9240896 | tf_op jit(solution)/shard_map/dot_general | solution.py:40
  191.8 0.0 all-reduce.7.cloned.1.call-update
  191.8 89.1 %all-reduce.7.cloned.1.call-done = bf16[64,7168]{1,0:T(8,128)(2,1)} async-done(((bf16[64,7168]{1,0:T(8,128)(2,1)}), bf16[64,7168]{1,0:T(8,128)(2,1)}) %all-reduce.7.cloned.1.call-update) | async-done | bytes 917520
  280.9 0.9 fusion.33
  281.9 1.5 collective-permute-start.1
  283.4 2.7 collective-permute-done.1
  286.1 0.6 copy.18
  (5 shorter events, 0.0 us)
Async XLA Ops:
  6.5 147.2 %all-reduce.5.cloned.1.call-start = ((), (), s32[]{:S(2)}) async-start(), calls=%async_computation | async-start | bytes 1835008
  56.8 6.6 %copy-start.2 = (u32[32]{0:T(128)S(1)}, u32[32]{0:T(128)}, u32[]{:S(2)}) copy-start(u32[32]{0:T(128)} %constant.47) | copy-start | bytes 388
  56.8 96.9 %copy-start = (bf16[1,4,7168]{2,1,0:T(4,128)(2,1)S(1)}, bf16[1,4,7168]{2,1,0:T(4,128)(2,1)}, u32[]{:S(2)}) copy-start(bf16[1,4,7168]{2,1,0:T(4,128)(2,1)} %param.7) | copy-start | bytes 172036
  56.8 102.3 %copy-start.1 = (f32[1,7168]{1,0:T(1,128)S(1)}, f32[1,7168]{1,0:T(1,128)}, u32[]{:S(2)}) copy-start(f32[1,7168]{1,0:T(1,128)} %param.10) | copy-start | bytes 86020
  63.3 217.6 %all-reduce.7.cloned.1.call-start = ((), (), s32[]{:S(2)}) async-start(), calls=%async_computation.1 | async-start | bytes 1835008
  154.7 4.2 %collective-permute-start = (bf16[4,7168]{1,0:T(4,128)(2,1)S(1)}, bf16[4,7168]{1,0:T(4,128)(2,1)S(1)}, u32[]{:S(2)}, u32[]{:S(2)}) collective-permute-start(bf16[4,7168]{1,0:T(4,128)(2,1)S(1)} %fusion.37), channel_id=1, source_target_pairs={{0,16},{16,0},{1,17},{17,1},{2,18},{18,2},{3,19},{19,3},{4,20},{20... | collective-permute-start | bytes 172040 | tf_op jit(solution)/shard_map/ppermute | solution.py:12
  281.9 4.2 %collective-permute-start.1 = (bf16[4,7168]{1,0:T(4,128)(2,1)S(1)}, bf16[4,7168]{1,0:T(4,128)(2,1)S(1)}, u32[]{:S(2)}, u32[]{:S(2)}) collective-permute-start(bf16[4,7168]{1,0:T(4,128)(2,1)S(1)} %fusion.33), channel_id=1, source_target_pairs={{0,16},{16,0},{1,17},{17,1},{2,18},{18,2},{3,19},{19,3},{4,20},{20... | collective-permute-start | bytes 172040 | tf_op jit(solution)/shard_map/ppermute | solution.py:12
Sparse Core Ops, SparseCore 0:
  63.4 90.2 all-reduce.4
  191.9 88.9 all-reduce.6

commit v2 on v1

v2 whole, which is shorter than its diff:
```python
import jax
import jax.numpy as jnp
from jax import lax
from jax.sharding import PartitionSpec as P

GROUP = 4
LANES = 128


def exchange(value, flip, hop):
    segments, owners = lax.axis_size("segment"), lax.axis_size("expert")
    if flip == 0 and hop % segments == 0:
        return value
    pairs = []
    for seg in range(segments):
        for own in range(owners):
            target = (seg + hop) % segments * owners + (own ^ flip)
            pairs.append((seg * owners + own, target))
    return lax.ppermute(value, ("segment", "expert"), pairs)


def gather(block, hop):
    depth = lax.axis_size("expert") // GROUP
    columns = [exchange(block, dz * GROUP, hop) for dz in range(depth)]
    planes = []
    for got in columns:
        planes.append((got, exchange(got, 2, 0)))
    blocks = []
    for near, far in planes:
        blocks += [near, exchange(near, 1, 0), far, exchange(far, 1, 0)]
    return blocks


def on_device(states, routing, route_weight, norm_gain, gate_proj, up_proj, down_proj):
    owners = lax.axis_size("expert")
    experts = owners // GROUP
    depth = owners // GROUP
    row_dev = states.shape[1]
    model_dim = states.shape[2]
    passes_count = routing.shape[1]
    gain_row = norm_gain[0]
    gate_mat = gate_proj[0]
    up_mat = up_proj[0]
    down_mat = down_proj[0]
    expert_ids = jnp.arange(experts, dtype=jnp.int32)

    picked = routing[0][..., None] == expert_ids
    dense = jnp.sum(jnp.where(picked, route_weight[0][..., None].astype(jnp.float32), 0.0), axis=2)
    dense = jnp.moveaxis(dense, 0, 1).reshape(row_dev, passes_count * experts).astype(jnp.bfloat16)
    dense = jnp.pad(dense, ((0, 0), (0, LANES - passes_count * experts)))
    mine = lax.axis_index("expert") // GROUP

    current = states[0]
    blocks = gather(jnp.concatenate([current, dense], axis=1), 0)
    tail = jnp.concatenate([block[:, model_dim:] for block in blocks], axis=0)
    blocks = [block[:, :model_dim] for block in blocks]

    for step_no in range(passes_count):
        if step_no > 0:
            blocks = gather(current, 1)
            current = blocks[0]
        hidden = jnp.concatenate(blocks, axis=0).astype(jnp.float32)
        inv_rms = lax.rsqrt(jnp.mean(hidden * hidden, axis=1, keepdims=True) + 1e-06)
        rows = (hidden * inv_rms * gain_row).astype(jnp.bfloat16)
        gated = jnp.dot(rows, gate_mat, preferred_element_type=jnp.float32)
        up_part = jnp.dot(rows, up_mat, preferred_element_type=jnp.float32)
        inner_act = (jax.nn.silu(gated) * up_part).astype(jnp.bfloat16)
        partial_out = jnp.dot(inner_act, down_mat, preferred_element_type=jnp.float32)
        weight = lax.dynamic_slice_in_dim(tail, step_no * experts + mine, 1, 1).astype(jnp.float32)
        terms = jnp.where(weight > 0.0, weight * partial_out, 0.0).astype(jnp.bfloat16)

        terms = terms.reshape(depth, 2, 2, row_dev, model_dim)
        other = exchange(terms[:, :, 1], 1, 0)
        chip = terms[:, :, 0].astype(jnp.float32) + other.astype(jnp.float32)
        other = exchange(chip[:, 1].astype(jnp.bfloat16), 2, 0)
        plane = chip[:, 0] + other.astype(jnp.float32)
        last = step_no == passes_count - 1
        if last:
            current = exchange(current, 0, 1)
        total = current.astype(jnp.float32)
        for dz in range(depth):
            part = plane[dz] if dz == 0 and not last else plane[dz].astype(jnp.bfloat16)
            total = total + exchange(part, dz * GROUP, 1 if last else 0).astype(jnp.float32)
        current = total.astype(jnp.bfloat16)
    return current[None]


def solution(mesh):
    return jax.shard_map(
        on_device,
        mesh=mesh,
        in_specs=(
            P("segment", "expert", None),
            P("segment", None, "expert", None),
            P("segment", None, "expert", None),
            P("segment", None),
            P("segment", None, "expert"),
            P("segment", None, "expert"),
            P("segment", "expert", None),
        ),
        out_specs=P("segment", "expert", None),
        check_vma=False,
    )
```

time: 294 us -> 98.7 us (0.34)
  waiting for transfers between devices: 184 us -> 33 us
  blocking collectives: 66.4 us -> 0 us
  starting transfers between devices: 3.11 us -> 39.5 us
  between operations: 14.2 us -> 0.48 us
    unnamed x4 -> x0, waiting for transfers between devices: 178 us -> none
    all_gather x3 -> x0, blocking collectives: 66.4 us -> none  [the longest x2 43.2 us: on_device(): rows = lax.all_gather(normed, 'expert', axis=0, tiled=True)]
    ppermute x2 -> x43, starting transfers between devices: 3.07 us -> 39.5 us  [exchange(): return lax.ppermute(value, ('segment', 'expert'), pairs)]
    ppermute x2 -> x43, waiting for transfers between devices: 5.41 us -> 33 us  [exchange(): return lax.ppermute(value, ('segment', 'expert'), pairs)]
  transfers between devices with their start and end apart: 4 -> 43, of which waited for: 4 -> 23; matrix products, arithmetic and copies ran while one was open for 0% -> 1% of each run, Pallas kernels for 0% -> 0%
where the time goes in v2:
time: 98.7 us; the launch traced here: 98.4 us
  starting transfers between devices  39.5 us (40%)
  waiting for transfers between devices  33 us (33%)
  matrix products  16.7 us (17%)
  other arithmetic  4.8 us (5%)
  local copies, waits for them, and re-layouts  3.88 us (4%)
    ppermute x43, starting transfers between devices, exchange(): return lax.ppermute(value, ('segment', 'expert'), pairs)  39.5 us
    ppermute x43, waiting for transfers between devices, exchange(): return lax.ppermute(value, ('segment', 'expert'), pairs)  33 us
    dot_general x2, matrix products, on_device(): jnp.dot(inner_act, down_mat, preferred_element_type=jnp.float32)  11 us
    dot_general x2, matrix products, on_device(): up_part = jnp.dot(rows, up_mat, preferred_element_type=jnp.float32)  5.69 us
  transfers between devices with their start and end apart: 43, of which 23 were waited for; matrix products, arithmetic and copies ran while one was open for 1% of the time, Pallas kernels for 0%

profile of v2, /device:TPU:0, one launch (start us, length us, event | category | flops | bytes accessed | tf_op | source)
XLA Modules:
  0.0 98.4 jit_solution(11542933913994824440)
XLA Ops:
  0.0 0.7 bitcast_convert_fusion
  0.7 0.8 select_reduce_fusion
  1.6 0.8 pad_maximum_fusion
  2.4 5.1 %collective-permute-start.11 = (bf16[4,7296]{1,0:T(4,128)(2,1)S(1)}, bf16[4,7296]{1,0:T(4,128)(2,1)S(1)}, u32[]{:S(2)}, u32[]{:S(2)}) collective-permute-start(bf16[4,7296]{1,0:T(4,128)(2,1)S(1)} %pad_maximum_fusion), channel_id=1, source_target_pairs={{0,12},{1,13},{2,14},{3,15},{4,8},{5,9},{6,10},{7,11},{8,4},{9,5},... | collective-permute-start | bytes 175112 | tf_op jit(solution)/shard_map/ppermute | solution.py:19
  7.5 0.6 collective-permute-start.3
  8.2 1.7 %collective-permute-start.1 = (bf16[4,7296]{1,0:T(4,128)(2,1)S(1)}, bf16[4,7296]{1,0:T(4,128)(2,1)S(1)}, u32[]{:S(2)}, u32[]{:S(2)}) collective-permute-start(bf16[4,7296]{1,0:T(4,128)(2,1)S(1)} %pad_maximum_fusion), channel_id=1, source_target_pairs={{0,2},{1,3},{2,0},{3,1},{4,6},{5,7},{6,4},{7,5},{8,10},{9,11},{10,... | collective-permute-start | bytes 175112 | tf_op jit(solution)/shard_map/ppermute | solution.py:19
  10.0 1.9 %collective-permute-start.13 = (bf16[4,7296]{1,0:T(4,128)(2,1)S(1)}, bf16[4,7296]{1,0:T(4,128)(2,1)S(1)}, u32[]{:S(2)}, u32[]{:S(2)}) collective-permute-start(bf16[4,7296]{1,0:T(4,128)(2,1)S(1)} %collective-permute-done.11), channel_id=1, source_target_pairs={{0,2},{1,3},{2,0},{3,1},{4,6},{5,7},{6,4},{7,5},{8,10},{9,11},{10,... | collective-permute-start | bytes 175112 | tf_op jit(solution)/shard_map/ppermute | solution.py:19
  11.8 0.8 collective-permute-done.7
  12.6 1.6 %collective-permute-start.9 = (bf16[4,7296]{1,0:T(4,128)(2,1)S(1)}, bf16[4,7296]{1,0:T(4,128)(2,1)S(1)}, u32[]{:S(2)}, u32[]{:S(2)}) collective-permute-start(bf16[4,7296]{1,0:T(4,128)(2,1)S(1)} %collective-permute-done.7), channel_id=1, source_target_pairs={{0,2},{1,3},{2,0},{3,1},{4,6},{5,7},{6,4},{7,5},{8,10},{9,11},{10,... | collective-permute-start | bytes 175112 | tf_op jit(solution)/shard_map/ppermute | solution.py:19
  14.2 0.2 collective-permute-start.8
  14.5 0.4 collective-permute-start.5
  14.9 0.5 collective-permute-start.2
  15.4 1.6 %collective-permute-done.9 = bf16[4,7296]{1,0:T(4,128)(2,1)S(1)} collective-permute-done((bf16[4,7296]{1,0:T(4,128)(2,1)S(1)}, bf16[4,7296]{1,0:T(4,128)(2,1)S(1)}, u32[]{:S(2)}, u32[]{:S(2)}) %collective-permute-start.9) | collective-permute-done | bytes 58400 | tf_op jit(solution)/shard_map/ppermute | solution.py:19
  17.0 0.5 collective-permute-start.10
  17.5 1.2 %collective-permute-done.5 = bf16[4,7296]{1,0:T(4,128)(2,1)S(1)} collective-permute-done((bf16[4,7296]{1,0:T(4,128)(2,1)S(1)}, bf16[4,7296]{1,0:T(4,128)(2,1)S(1)}, u32[]{:S(2)}, u32[]{:S(2)}) %collective-permute-start.5) | collective-permute-done | bytes 58400 | tf_op jit(solution)/shard_map/ppermute | solution.py:19
  19.2 0.7 collective-permute-done.6
  19.9 0.2 concatenate.13
  20.6 0.6 concatenate.14
  21.2 0.3 fusion.14
  21.5 2.8 %fusion.8 = f32[64,256]{1,0:T(8,128)S(1)} fusion(bf16[1,7168,256]{2,1,0:T(8,128)(2,1)} %param.12, bf16[64,7168]{1,0:T(8,128)(2,1)S(1)} %concatenate.14, f32[7168]{0:T(1024)S(1)} %bitcast.96, f32[64]{0:T(128)S(1)} %add_rsqrt_fusion.1), kind=kOutput, calls=%fused_computation.10 | convolution fusion | flops 236716032 | bytes 4681984 | tf_op jit(solution)/shard_map/dot_general | solution.py:66
  24.4 5.5 %fusion.2 = bf16[64,7168]{1,0:T(8,128)(2,1)S(1)} fusion(bf16[1,256,7168]{2,1,0:T(8,128)(2,1)} %param.13, f32[64]{0:T(128)S(1)} %get-tuple-element.7, pred[64]{0:T(512)(128)(4,1)S(1)} %get-tuple-element.5, f32[64,256]{1,0:T(8,128)S(1)} %fusion.8, bf16[1,7168,256]{2,1,0:T(8,128)(2,1)} %param.11, bf16[64,7168]{1,0:T(8,128)(2,1)S(1)} %concatenate.14, ...), kind=kOutput, calls=%fused_computation.4 | convolution fusion | flops 473071616 | bytes 9269824 | tf_op jit(solution)/shard_map/dot_general | solution.py:68
  29.9 0.3 reshape.47
  30.3 0.3 fusion.60
  31.0 1.7 %collective-permute-done.15 = bf16[4,2,4,7168]{3,2,0,1:T(4,128)(2,1)S(1)} collective-permute-done((bf16[4,2,4,7168]{3,2,0,1:T(4,128)(2,1)S(1)}, bf16[4,2,4,7168]{3,2,0,1:T(4,128)(2,1)S(1)}, u32[]{:S(2)}, u32[]{:S(2)}) %collective-permute-start.15) | collective-permute-done | bytes 458784 | tf_op jit(solution)/shard_map/ppermute | solution.py:19
  32.6 0.2 convert_add_fusion.1
  33.0 1.2 %collective-permute-start.16 = (bf16[4,4,7168]{2,1,0:T(4,128)(2,1)S(1)}, bf16[4,4,7168]{2,1,0:T(4,128)(2,1)S(1)}, u32[]{:S(2)}, u32[]{:S(2)}) collective-permute-start(bf16[4,4,7168]{2,1,0:T(4,128)(2,1)S(1)} %fusion.27), channel_id=1, source_target_pairs={{0,2},{1,3},{2,0},{3,1},{4,6},{5,7},{6,4},{7,5},{8,10},{9,11},{10,... | collective-permute-start | bytes 688136 | tf_op jit(solution)/shard_map/ppermute | solution.py:19
  34.2 6.5 %collective-permute-done.16 = bf16[4,4,7168]{2,1,0:T(4,128)(2,1)S(1)} collective-permute-done((bf16[4,4,7168]{2,1,0:T(4,128)(2,1)S(1)}, bf16[4,4,7168]{2,1,0:T(4,128)(2,1)S(1)}, u32[]{:S(2)}, u32[]{:S(2)}) %collective-permute-start.16) | collective-permute-done | bytes 229408 | tf_op jit(solution)/shard_map/ppermute | solution.py:19
  40.9 1.1 %collective-permute-start.17 = (bf16[4,7168]{1,0:T(4,128)(2,1)S(1)}, bf16[4,7168]{1,0:T(4,128)(2,1)S(1)}, u32[]{:S(2)}, u32[]{:S(2)}) collective-permute-start(bf16[4,7168]{1,0:T(4,128)(2,1)S(1)} %get-tuple-element.19), channel_id=1, source_target_pairs={{0,4},{1,5},{2,6},{3,7},{4,0},{5,1},{6,2},{7,3},{8,12},{9,13},{10,... | collective-permute-start | bytes 172040 | tf_op jit(solution)/shard_map/ppermute | solution.py:19
  42.0 2.3 %collective-permute-start.19 = (bf16[4,7168]{1,0:T(4,128)(2,1)S(1)}, bf16[4,7168]{1,0:T(4,128)(2,1)S(1)}, u32[]{:S(2)}, u32[]{:S(2)}) collective-permute-start(bf16[4,7168]{1,0:T(4,128)(2,1)S(1)} %get-tuple-element.20), channel_id=1, source_target_pairs={{0,12},{1,13},{2,14},{3,15},{4,8},{5,9},{6,10},{7,11},{8,4},{9,5},... | collective-permute-start | bytes 172040 | tf_op jit(solution)/shard_map/ppermute | solution.py:19
  44.5 0.7 collective-permute-done.17
  45.2 2.8 %collective-permute-done.19 = bf16[4,7168]{1,0:T(4,128)(2,1)S(1)} collective-permute-done((bf16[4,7168]{1,0:T(4,128)(2,1)S(1)}, bf16[4,7168]{1,0:T(4,128)(2,1)S(1)}, u32[]{:S(2)}, u32[]{:S(2)}) %collective-permute-start.19) | collective-permute-done | bytes 57376 | tf_op jit(solution)/shard_map/ppermute | solution.py:19
  48.0 1.9 %collective-permute-done.18 = bf16[4,7168]{1,0:T(4,128)(2,1)S(1)} collective-permute-done((bf16[4,7168]{1,0:T(4,128)(2,1)S(1)}, bf16[4,7168]{1,0:T(4,128)(2,1)S(1)}, u32[]{:S(2)}, u32[]{:S(2)}) %collective-permute-start.18) | collective-permute-done | bytes 57376 | tf_op jit(solution)/shard_map/ppermute | solution.py:19
  50.0 3.5 %collective-permute-start.33 = (bf16[4,7168]{1,0:T(4,128)(2,1)S(1)}, bf16[4,7168]{1,0:T(4,128)(2,1)S(1)}, u32[]{:S(2)}, u32[]{:S(2)}) collective-permute-start(bf16[4,7168]{1,0:T(4,128)(2,1)S(1)} %fusion.33), channel_id=1, source_target_pairs={{0,28},{1,29},{2,30},{3,31},{4,24},{5,25},{6,26},{7,27},{8,20},{9,... | collective-permute-start | bytes 172040 | tf_op jit(solution)/shard_map/ppermute | solution.py:19
  53.5 2.8 %collective-permute-start.25 = (bf16[4,7168]{1,0:T(4,128)(2,1)S(1)}, bf16[4,7168]{1,0:T(4,128)(2,1)S(1)}, u32[]{:S(2)}, u32[]{:S(2)}) collective-permute-start(bf16[4,7168]{1,0:T(4,128)(2,1)S(1)} %fusion.33), channel_id=1, source_target_pairs={{0,20},{1,21},{2,22},{3,23},{4,16},{5,17},{6,18},{7,19},{8,28},{9,... | collective-permute-start | bytes 172040 | tf_op jit(solution)/shard_map/ppermute | solution.py:19
  56.3 0.5 collective-permute-start.20
  56.8 0.2 collective-permute-done.33
  57.0 1.2 %collective-permute-start.35 = (bf16[4,7168]{1,0:T(4,128)(2,1)S(1)}, bf16[4,7168]{1,0:T(4,128)(2,1)S(1)}, u32[]{:S(2)}, u32[]{:S(2)}) collective-permute-start(bf16[4,7168]{1,0:T(4,128)(2,1)S(1)} %collective-permute-done.33), channel_id=1, source_target_pairs={{0,2},{1,3},{2,0},{3,1},{4,6},{5,7},{6,4},{7,5},{8,10},{9,11},{10,... | collective-permute-start | bytes 172040 | tf_op jit(solution)/shard_map/ppermute | solution.py:19
  58.3 1.2 %collective-permute-done.29 = bf16[4,7168]{1,0:T(4,128)(2,1)S(1)} collective-permute-done((bf16[4,7168]{1,0:T(4,128)(2,1)S(1)}, bf16[4,7168]{1,0:T(4,128)(2,1)S(1)}, u32[]{:S(2)}, u32[]{:S(2)}) %collective-permute-start.29) | collective-permute-done | bytes 57376 | tf_op jit(solution)/shard_map/ppermute | solution.py:19
  59.4 1.1 %collective-permute-start.31 = (bf16[4,7168]{1,0:T(4,128)(2,1)S(1)}, bf16[4,7168]{1,0:T(4,128)(2,1)S(1)}, u32[]{:S(2)}, u32[]{:S(2)}) collective-permute-start(bf16[4,7168]{1,0:T(4,128)(2,1)S(1)} %collective-permute-done.29), channel_id=1, source_target_pairs={{0,2},{1,3},{2,0},{3,1},{4,6},{5,7},{6,4},{7,5},{8,10},{9,11},{10,... | collective-permute-start | bytes 172040 | tf_op jit(solution)/shard_map/ppermute | solution.py:19
  60.6 1.1 %collective-permute-start.27 = (bf16[4,7168]{1,0:T(4,128)(2,1)S(1)}, bf16[4,7168]{1,0:T(4,128)(2,1)S(1)}, u32[]{:S(2)}, u32[]{:S(2)}) collective-permute-start(bf16[4,7168]{1,0:T(4,128)(2,1)S(1)} %collective-permute-done.25), channel_id=1, source_target_pairs={{0,2},{1,3},{2,0},{3,1},{4,6},{5,7},{6,4},{7,5},{8,10},{9,11},{10,... | collective-permute-start | bytes 172040 | tf_op jit(solution)/shard_map/ppermute | solution.py:19
  61.7 1.1 %collective-permute-start.23 = (bf16[4,7168]{1,0:T(4,128)(2,1)S(1)}, bf16[4,7168]{1,0:T(4,128)(2,1)S(1)}, u32[]{:S(2)}, u32[]{:S(2)}) collective-permute-start(bf16[4,7168]{1,0:T(4,128)(2,1)S(1)} %collective-permute-done.20), channel_id=1, source_target_pairs={{0,2},{1,3},{2,0},{3,1},{4,6},{5,7},{6,4},{7,5},{8,10},{9,11},{10,... | collective-permute-start | bytes 172040 | tf_op jit(solution)/shard_map/ppermute | solution.py:19
  62.8 0.8 collective-permute-done.31
  63.6 0.5 collective-permute-start.36
  64.1 1.0 collective-permute-done.27
  65.1 0.5 collective-permute-start.28
  65.6 0.5 collective-permute-done.23
  66.5 0.9 collective-permute-done.24
  67.4 0.6 concatenate.15
  68.0 0.3 fusion.17
  68.3 2.8 %fusion.6 = f32[64,256]{1,0:T(8,128)S(1)} fusion(bf16[1,7168,256]{2,1,0:T(8,128)(2,1)} %param.12, bf16[64,7168]{1,0:T(8,128)(2,1)S(1)} %concatenate.15, f32[64]{0:T(128)S(1)} %add_rsqrt_fusion, f32[7168]{0:T(1024)S(1)} %bitcast.98), kind=kOutput, calls=%fused_computation.8 | convolution fusion | flops 236716032 | bytes 4681984 | tf_op jit(solution)/shard_map/dot_general | solution.py:66
  71.1 5.5 %fusion.3 = bf16[64,7168]{1,0:T(8,128)(2,1)S(1)} fusion(bf16[1,256,7168]{2,1,0:T(8,128)(2,1)} %param.13, f32[64]{0:T(128)S(1)} %get-tuple-element.8, pred[64]{0:T(512)(128)(4,1)S(1)} %get-tuple-element.6, f32[64,256]{1,0:T(8,128)S(1)} %fusion.6, bf16[1,7168,256]{2,1,0:T(8,128)(2,1)} %param.11, bf16[64,7168]{1,0:T(8,128)(2,1)S(1)} %concatenate.15, ...), kind=kOutput, calls=%fused_computation.5 | convolution fusion | flops 473071616 | bytes 9269824 | tf_op jit(solution)/shard_map/dot_general | solution.py:68
  76.7 0.3 reshape.48
  77.0 0.3 fusion.59
  77.7 1.7 %collective-permute-done.37 = bf16[4,2,4,7168]{3,2,0,1:T(4,128)(2,1)S(1)} collective-permute-done((bf16[4,2,4,7168]{3,2,0,1:T(4,128)(2,1)S(1)}, bf16[4,2,4,7168]{3,2,0,1:T(4,128)(2,1)S(1)}, u32[]{:S(2)}, u32[]{:S(2)}) %collective-permute-start.37) | collective-permute-done | bytes 458784 | tf_op jit(solution)/shard_map/ppermute | solution.py:19
  79.4 0.2 convert_add_fusion
  79.7 1.1 %collective-permute-start.38 = (bf16[4,4,7168]{2,1,0:T(4,128)(2,1)S(1)}, bf16[4,4,7168]{2,1,0:T(4,128)(2,1)S(1)}, u32[]{:S(2)}, u32[]{:S(2)}) collective-permute-start(bf16[4,4,7168]{2,1,0:T(4,128)(2,1)S(1)} %fusion.28), channel_id=1, source_target_pairs={{0,2},{1,3},{2,0},{3,1},{4,6},{5,7},{6,4},{7,5},{8,10},{9,11},{10,... | collective-permute-start | bytes 688136 | tf_op jit(solution)/shard_map/ppermute | solution.py:19
  80.8 1.3 %collective-permute-start.21 = (bf16[4,7168]{1,0:T(4,128)(2,1)S(1)}, bf16[4,7168]{1,0:T(4,128)(2,1)S(1)}, u32[]{:S(2)}, u32[]{:S(2)}) collective-permute-start(bf16[4,7168]{1,0:T(4,128)(2,1)S(1)} %collective-permute-done.20), channel_id=1, source_target_pairs={{0,16},{1,17},{2,18},{3,19},{4,20},{5,21},{6,22},{7,23},{8,24},{9,... | collective-permute-start | bytes 172040 | tf_op jit(solution)/shard_map/ppermute | solution.py:19
  82.1 5.3 %collective-permute-done.38 = bf16[4,4,7168]{2,1,0:T(4,128)(2,1)S(1)} collective-permute-done((bf16[4,4,7168]{2,1,0:T(4,128)(2,1)S(1)}, bf16[4,4,7168]{2,1,0:T(4,128)(2,1)S(1)}, u32[]{:S(2)}, u32[]{:S(2)}) %collective-permute-start.38) | collective-permute-done | bytes 229408 | tf_op jit(solution)/shard_map/ppermute | solution.py:19
  87.7 1.0 collective-permute-start.39
  88.6 2.9 %collective-permute-start.42 = (bf16[4,7168]{1,0:T(4,128)(2,1)S(1)}, bf16[4,7168]{1,0:T(4,128)(2,1)S(1)}, u32[]{:S(2)}, u32[]{:S(2)}) collective-permute-start(bf16[4,7168]{1,0:T(4,128)(2,1)S(1)} %get-tuple-element.16), channel_id=1, source_target_pairs={{0,28},{1,29},{2,30},{3,31},{4,24},{5,25},{6,26},{7,27},{8,20},{9,... | collective-permute-start | bytes 172040 | tf_op jit(solution)/shard_map/ppermute | solution.py:19
  91.5 3.0 %collective-permute-start.40 = (bf16[4,7168]{1,0:T(4,128)(2,1)S(1)}, bf16[4,7168]{1,0:T(4,128)(2,1)S(1)}, u32[]{:S(2)}, u32[]{:S(2)}) collective-permute-start(bf16[4,7168]{1,0:T(4,128)(2,1)S(1)} %get-tuple-element.18), channel_id=1, source_target_pairs={{0,20},{1,21},{2,22},{3,23},{4,16},{5,17},{6,18},{7,19},{8,28},{9,... | collective-permute-start | bytes 172040 | tf_op jit(solution)/shard_map/ppermute | solution.py:19
  94.5 1.1 %collective-permute-done.42 = bf16[4,7168]{1,0:T(4,128)(2,1)S(1)} collective-permute-done((bf16[4,7168]{1,0:T(4,128)(2,1)S(1)}, bf16[4,7168]{1,0:T(4,128)(2,1)S(1)}, u32[]{:S(2)}, u32[]{:S(2)}) %collective-permute-start.42) | collective-permute-done | bytes 57376 | tf_op jit(solution)/shard_map/ppermute | solution.py:19
  95.6 1.9 %collective-permute-done.41 = bf16[4,7168]{1,0:T(4,128)(2,1)S(1)} collective-permute-done((bf16[4,7168]{1,0:T(4,128)(2,1)S(1)}, bf16[4,7168]{1,0:T(4,128)(2,1)S(1)}, u32[]{:S(2)}, u32[]{:S(2)}) %collective-permute-start.41) | collective-permute-done | bytes 57376 | tf_op jit(solution)/shard_map/ppermute | solution.py:19
  97.7 0.7 fusion.34
  (91 shorter events, 3.3 us)
Async XLA Ops:
  0.0 20.6 %copy-start = (bf16[1,4,7168]{2,1,0:T(4,128)(2,1)S(1)}, bf16[1,4,7168]{2,1,0:T(4,128)(2,1)}, u32[]{:S(2)}) copy-start(bf16[1,4,7168]{2,1,0:T(4,128)(2,1)} %param.7) | copy-start | bytes 172036
  2.4 7.5 %collective-permute-start.11 = (bf16[4,7296]{1,0:T(4,128)(2,1)S(1)}, bf16[4,7296]{1,0:T(4,128)(2,1)S(1)}, u32[]{:S(2)}, u32[]{:S(2)}) collective-permute-start(bf16[4,7296]{1,0:T(4,128)(2,1)S(1)} %pad_maximum_fusion), channel_id=1, source_target_pairs={{0,12},{1,13},{2,14},{3,15},{4,8},{5,9},{6,10},{7,11},{8,4},{9,5},... | collective-permute-start | bytes 175112 | tf_op jit(solution)/shard_map/ppermute | solution.py:19
  7.5 5.1 %collective-permute-start.7 = (bf16[4,7296]{1,0:T(4,128)(2,1)S(1)}, bf16[4,7296]{1,0:T(4,128)(2,1)S(1)}, u32[]{:S(2)}, u32[]{:S(2)}) collective-permute-start(bf16[4,7296]{1,0:T(4,128)(2,1)S(1)} %pad_maximum_fusion), channel_id=1, source_target_pairs={{0,8},{1,9},{2,10},{3,11},{4,12},{5,13},{6,14},{7,15},{8,0},{9,1},... | collective-permute-start | bytes 175112 | tf_op jit(solution)/shard_map/ppermute | solution.py:19
  7.5 5.1 %collective-permute-start.3 = (bf16[4,7296]{1,0:T(4,128)(2,1)S(1)}, bf16[4,7296]{1,0:T(4,128)(2,1)S(1)}, u32[]{:S(2)}, u32[]{:S(2)}) collective-permute-start(bf16[4,7296]{1,0:T(4,128)(2,1)S(1)} %pad_maximum_fusion), channel_id=1, source_target_pairs={{0,4},{1,5},{2,6},{3,7},{4,0},{5,1},{6,2},{7,3},{8,12},{9,13},{10,... | collective-permute-start | bytes 175112 | tf_op jit(solution)/shard_map/ppermute | solution.py:19
  8.2 6.1 %collective-permute-start.1 = (bf16[4,7296]{1,0:T(4,128)(2,1)S(1)}, bf16[4,7296]{1,0:T(4,128)(2,1)S(1)}, u32[]{:S(2)}, u32[]{:S(2)}) collective-permute-start(bf16[4,7296]{1,0:T(4,128)(2,1)S(1)} %pad_maximum_fusion), channel_id=1, source_target_pairs={{0,2},{1,3},{2,0},{3,1},{4,6},{5,7},{6,4},{7,5},{8,10},{9,11},{10,... | collective-permute-start | bytes 175112 | tf_op jit(solution)/shard_map/ppermute | solution.py:19
  9.8 4.6 %collective-permute-start = (bf16[4,7296]{1,0:T(4,128)(2,1)S(1)}, bf16[4,7296]{1,0:T(4,128)(2,1)S(1)}, u32[]{:S(2)}, u32[]{:S(2)}) collective-permute-start(bf16[4,7296]{1,0:T(4,128)(2,1)S(1)} %pad_maximum_fusion), channel_id=1, source_target_pairs={{0,1},{1,0},{2,3},{3,2},{4,5},{5,4},{6,7},{7,6},{8,9},{9,8},{10,11... | collective-permute-start | bytes 175112 | tf_op jit(solution)/shard_map/ppermute | solution.py:19
  10.0 4.9 %collective-permute-start.13 = (bf16[4,7296]{1,0:T(4,128)(2,1)S(1)}, bf16[4,7296]{1,0:T(4,128)(2,1)S(1)}, u32[]{:S(2)}, u32[]{:S(2)}) collective-permute-start(bf16[4,7296]{1,0:T(4,128)(2,1)S(1)} %collective-permute-done.11), channel_id=1, source_target_pairs={{0,2},{1,3},{2,0},{3,1},{4,6},{5,7},{6,4},{7,5},{8,10},{9,11},{10,... | collective-permute-start | bytes 175112 | tf_op jit(solution)/shard_map/ppermute | solution.py:19
  12.6 2.3 %collective-permute-start.12 = (bf16[4,7296]{1,0:T(4,128)(2,1)S(1)}, bf16[4,7296]{1,0:T(4,128)(2,1)S(1)}, u32[]{:S(2)}, u32[]{:S(2)}) collective-permute-start(bf16[4,7296]{1,0:T(4,128)(2,1)S(1)} %collective-permute-done.11), channel_id=1, source_target_pairs={{0,1},{1,0},{2,3},{3,2},{4,5},{5,4},{6,7},{7,6},{8,9},{9,8},{10,11... | collective-permute-start | bytes 175112 | tf_op jit(solution)/shard_map/ppermute | solution.py:19
  12.6 4.4 %collective-permute-start.9 = (bf16[4,7296]{1,0:T(4,128)(2,1)S(1)}, bf16[4,7296]{1,0:T(4,128)(2,1)S(1)}, u32[]{:S(2)}, u32[]{:S(2)}) collective-permute-start(bf16[4,7296]{1,0:T(4,128)(2,1)S(1)} %collective-permute-done.7), channel_id=1, source_target_pairs={{0,2},{1,3},{2,0},{3,1},{4,6},{5,7},{6,4},{7,5},{8,10},{9,11},{10,... | collective-permute-start | bytes 175112 | tf_op jit(solution)/shard_map/ppermute | solution.py:19
  14.2 2.7 %collective-permute-start.8 = (bf16[4,7296]{1,0:T(4,128)(2,1)S(1)}, bf16[4,7296]{1,0:T(4,128)(2,1)S(1)}, u32[]{:S(2)}, u32[]{:S(2)}) collective-permute-start(bf16[4,7296]{1,0:T(4,128)(2,1)S(1)} %collective-permute-done.7), channel_id=1, source_target_pairs={{0,1},{1,0},{2,3},{3,2},{4,5},{5,4},{6,7},{7,6},{8,9},{9,8},{10,11... | collective-permute-start | bytes 175112 | tf_op jit(solution)/shard_map/ppermute | solution.py:19
  14.5 4.2 %collective-permute-start.5 = (bf16[4,7296]{1,0:T(4,128)(2,1)S(1)}, bf16[4,7296]{1,0:T(4,128)(2,1)S(1)}, u32[]{:S(2)}, u32[]{:S(2)}) collective-permute-start(bf16[4,7296]{1,0:T(4,128)(2,1)S(1)} %collective-permute-done.3), channel_id=1, source_target_pairs={{0,2},{1,3},{2,0},{3,1},{4,6},{5,7},{6,4},{7,5},{8,10},{9,11},{10,... | collective-permute-start | bytes 175112 | tf_op jit(solution)/shard_map/ppermute | solution.py:19
  14.9 4.2 %collective-permute-start.4 = (bf16[4,7296]{1,0:T(4,128)(2,1)S(1)}, bf16[4,7296]{1,0:T(4,128)(2,1)S(1)}, u32[]{:S(2)}, u32[]{:S(2)}) collective-permute-start(bf16[4,7296]{1,0:T(4,128)(2,1)S(1)} %collective-permute-done.3), channel_id=1, source_target_pairs={{0,1},{1,0},{2,3},{3,2},{4,5},{5,4},{6,7},{7,6},{8,9},{9,8},{10,11... | collective-permute-start | bytes 175112 | tf_op jit(solution)/shard_map/ppermute | solution.py:19
  14.9 4.2 %collective-permute-start.2 = (bf16[4,7296]{1,0:T(4,128)(2,1)S(1)}, bf16[4,7296]{1,0:T(4,128)(2,1)S(1)}, u32[]{:S(2)}, u32[]{:S(2)}) collective-permute-start(bf16[4,7296]{1,0:T(4,128)(2,1)S(1)} %collective-permute-done.1), channel_id=1, source_target_pairs={{0,1},{1,0},{2,3},{3,2},{4,5},{5,4},{6,7},{7,6},{8,9},{9,8},{10,11... | collective-permute-start | bytes 175112 | tf_op jit(solution)/shard_map/ppermute | solution.py:19
  17.0 2.2 %collective-permute-start.14 = (bf16[4,7296]{1,0:T(4,128)(2,1)S(1)}, bf16[4,7296]{1,0:T(4,128)(2,1)S(1)}, u32[]{:S(2)}, u32[]{:S(2)}) collective-permute-start(bf16[4,7296]{1,0:T(4,128)(2,1)S(1)} %collective-permute-done.13), channel_id=1, source_target_pairs={{0,1},{1,0},{2,3},{3,2},{4,5},{5,4},{6,7},{7,6},{8,9},{9,8},{10,11... | collective-permute-start | bytes 175112 | tf_op jit(solution)/shard_map/ppermute | solution.py:19
  17.0 2.2 %collective-permute-start.10 = (bf16[4,7296]{1,0:T(4,128)(2,1)S(1)}, bf16[4,7296]{1,0:T(4,128)(2,1)S(1)}, u32[]{:S(2)}, u32[]{:S(2)}) collective-permute-start(bf16[4,7296]{1,0:T(4,128)(2,1)S(1)} %collective-permute-done.9), channel_id=1, source_target_pairs={{0,1},{1,0},{2,3},{3,2},{4,5},{5,4},{6,7},{7,6},{8,9},{9,8},{10,11... | collective-permute-start | bytes 175112 | tf_op jit(solution)/shard_map/ppermute | solution.py:19
  18.7 1.2 %collective-permute-start.6 = (bf16[4,7296]{1,0:T(4,128)(2,1)S(1)}, bf16[4,7296]{1,0:T(4,128)(2,1)S(1)}, u32[]{:S(2)}, u32[]{:S(2)}) collective-permute-start(bf16[4,7296]{1,0:T(4,128)(2,1)S(1)} %collective-permute-done.5), channel_id=1, source_target_pairs={{0,1},{1,0},{2,3},{3,2},{4,5},{5,4},{6,7},{7,6},{8,9},{9,8},{10,11... | collective-permute-start | bytes 175112 | tf_op jit(solution)/shard_map/ppermute | solution.py:19
  19.0 2.6 %copy-start.1 = (f32[1,7168]{1,0:T(1,128)S(1)}, f32[1,7168]{1,0:T(1,128)}, u32[]{:S(2)}) copy-start(f32[1,7168]{1,0:T(1,128)} %param.10) | copy-start | bytes 86020
  30.7 1.9 %collective-permute-start.15 = (bf16[4,2,4,7168]{3,2,0,1:T(4,128)(2,1)S(1)}, bf16[4,2,4,7168]{3,2,0,1:T(4,128)(2,1)S(1)}, u32[]{:S(2)}, u32[]{:S(2)}) collective-permute-start(bf16[4,2,4,7168]{3,2,0,1:T(4,128)(2,1)S(1)} %bitcast.94), channel_id=1, source_target_pairs={{0,1},{1,0},{2,3},{3,2},{4,5},{5,4},{6,7},{7,6},{8,9},{9,8},{10,11... | collective-permute-start | bytes 1376264 | tf_op jit(solution)/shard_map/ppermute | solution.py:19
  33.0 7.7 %collective-permute-start.16 = (bf16[4,4,7168]{2,1,0:T(4,128)(2,1)S(1)}, bf16[4,4,7168]{2,1,0:T(4,128)(2,1)S(1)}, u32[]{:S(2)}, u32[]{:S(2)}) collective-permute-start(bf16[4,4,7168]{2,1,0:T(4,128)(2,1)S(1)} %fusion.27), channel_id=1, source_target_pairs={{0,2},{1,3},{2,0},{3,1},{4,6},{5,7},{6,4},{7,5},{8,10},{9,11},{10,... | collective-permute-start | bytes 688136 | tf_op jit(solution)/shard_map/ppermute | solution.py:19
  40.9 4.2 %collective-permute-start.17 = (bf16[4,7168]{1,0:T(4,128)(2,1)S(1)}, bf16[4,7168]{1,0:T(4,128)(2,1)S(1)}, u32[]{:S(2)}, u32[]{:S(2)}) collective-permute-start(bf16[4,7168]{1,0:T(4,128)(2,1)S(1)} %get-tuple-element.19), channel_id=1, source_target_pairs={{0,4},{1,5},{2,6},{3,7},{4,0},{5,1},{6,2},{7,3},{8,12},{9,13},{10,... | collective-permute-start | bytes 172040 | tf_op jit(solution)/shard_map/ppermute | solution.py:19
  42.0 6.0 %collective-permute-start.19 = (bf16[4,7168]{1,0:T(4,128)(2,1)S(1)}, bf16[4,7168]{1,0:T(4,128)(2,1)S(1)}, u32[]{:S(2)}, u32[]{:S(2)}) collective-permute-start(bf16[4,7168]{1,0:T(4,128)(2,1)S(1)} %get-tuple-element.20), channel_id=1, source_target_pairs={{0,12},{1,13},{2,14},{3,15},{4,8},{5,9},{6,10},{7,11},{8,4},{9,5},... | collective-permute-start | bytes 172040 | tf_op jit(solution)/shard_map/ppermute | solution.py:19
  44.3 5.6 %collective-permute-start.18 = (bf16[4,7168]{1,0:T(4,128)(2,1)S(1)}, bf16[4,7168]{1,0:T(4,128)(2,1)S(1)}, u32[]{:S(2)}, u32[]{:S(2)}) collective-permute-start(bf16[4,7168]{1,0:T(4,128)(2,1)S(1)} %get-tuple-element.21), channel_id=1, source_target_pairs={{0,8},{1,9},{2,10},{3,11},{4,12},{5,13},{6,14},{7,15},{8,0},{9,1},... | collective-permute-start | bytes 172040 | tf_op jit(solution)/shard_map/ppermute | solution.py:19
  50.0 7.0 %collective-permute-start.33 = (bf16[4,7168]{1,0:T(4,128)(2,1)S(1)}, bf16[4,7168]{1,0:T(4,128)(2,1)S(1)}, u32[]{:S(2)}, u32[]{:S(2)}) collective-permute-start(bf16[4,7168]{1,0:T(4,128)(2,1)S(1)} %fusion.33), channel_id=1, source_target_pairs={{0,28},{1,29},{2,30},{3,31},{4,24},{5,25},{6,26},{7,27},{8,20},{9,... | collective-permute-start | bytes 172040 | tf_op jit(solution)/shard_map/ppermute | solution.py:19
  53.5 6.0 %collective-permute-start.29 = (bf16[4,7168]{1,0:T(4,128)(2,1)S(1)}, bf16[4,7168]{1,0:T(4,128)(2,1)S(1)}, u32[]{:S(2)}, u32[]{:S(2)}) collective-permute-start(bf16[4,7168]{1,0:T(4,128)(2,1)S(1)} %fusion.33), channel_id=1, source_target_pairs={{0,24},{1,25},{2,26},{3,27},{4,28},{5,29},{6,30},{7,31},{8,16},{9,... | collective-permute-start | bytes 172040 | tf_op jit(solution)/shard_map/ppermute | solution.py:19
  53.5 7.1 %collective-permute-start.25 = (bf16[4,7168]{1,0:T(4,128)(2,1)S(1)}, bf16[4,7168]{1,0:T(4,128)(2,1)S(1)}, u32[]{:S(2)}, u32[]{:S(2)}) collective-permute-start(bf16[4,7168]{1,0:T(4,128)(2,1)S(1)} %fusion.33), channel_id=1, source_target_pairs={{0,20},{1,21},{2,22},{3,23},{4,16},{5,17},{6,18},{7,19},{8,28},{9,... | collective-permute-start | bytes 172040 | tf_op jit(solution)/shard_map/ppermute | solution.py:19
  56.3 4.3 %collective-permute-start.20 = (bf16[4,7168]{1,0:T(4,128)(2,1)S(1)}, bf16[4,7168]{1,0:T(4,128)(2,1)S(1)}, u32[]{:S(2)}, u32[]{:S(2)}) collective-permute-start(bf16[4,7168]{1,0:T(4,128)(2,1)S(1)} %fusion.33), channel_id=1, source_target_pairs={{0,16},{1,17},{2,18},{3,19},{4,20},{5,21},{6,22},{7,23},{8,24},{9,... | collective-permute-start | bytes 172040 | tf_op jit(solution)/shard_map/ppermute | solution.py:19
  57.0 4.6 %collective-permute-start.35 = (bf16[4,7168]{1,0:T(4,128)(2,1)S(1)}, bf16[4,7168]{1,0:T(4,128)(2,1)S(1)}, u32[]{:S(2)}, u32[]{:S(2)}) collective-permute-start(bf16[4,7168]{1,0:T(4,128)(2,1)S(1)} %collective-permute-done.33), channel_id=1, source_target_pairs={{0,2},{1,3},{2,0},{3,1},{4,6},{5,7},{6,4},{7,5},{8,10},{9,11},{10,... | collective-permute-start | bytes 172040 | tf_op jit(solution)/shard_map/ppermute | solution.py:19
  58.3 3.4 %collective-permute-start.34 = (bf16[4,7168]{1,0:T(4,128)(2,1)S(1)}, bf16[4,7168]{1,0:T(4,128)(2,1)S(1)}, u32[]{:S(2)}, u32[]{:S(2)}) collective-permute-start(bf16[4,7168]{1,0:T(4,128)(2,1)S(1)} %collective-permute-done.33), channel_id=1, source_target_pairs={{0,1},{1,0},{2,3},{3,2},{4,5},{5,4},{6,7},{7,6},{8,9},{9,8},{10,11... | collective-permute-start | bytes 172040 | tf_op jit(solution)/shard_map/ppermute | solution.py:19
  59.4 4.2 %collective-permute-start.31 = (bf16[4,7168]{1,0:T(4,128)(2,1)S(1)}, bf16[4,7168]{1,0:T(4,128)(2,1)S(1)}, u32[]{:S(2)}, u32[]{:S(2)}) collective-permute-start(bf16[4,7168]{1,0:T(4,128)(2,1)S(1)} %collective-permute-done.29), channel_id=1, source_target_pairs={{0,2},{1,3},{2,0},{3,1},{4,6},{5,7},{6,4},{7,5},{8,10},{9,11},{10,... | collective-permute-start | bytes 172040 | tf_op jit(solution)/shard_map/ppermute | solution.py:19
  60.6 3.1 %collective-permute-start.30 = (bf16[4,7168]{1,0:T(4,128)(2,1)S(1)}, bf16[4,7168]{1,0:T(4,128)(2,1)S(1)}, u32[]{:S(2)}, u32[]{:S(2)}) collective-permute-start(bf16[4,7168]{1,0:T(4,128)(2,1)S(1)} %collective-permute-done.29), channel_id=1, source_target_pairs={{0,1},{1,0},{2,3},{3,2},{4,5},{5,4},{6,7},{7,6},{8,9},{9,8},{10,11... | collective-permute-start | bytes 172040 | tf_op jit(solution)/shard_map/ppermute | solution.py:19
  60.6 4.5 %collective-permute-start.27 = (bf16[4,7168]{1,0:T(4,128)(2,1)S(1)}, bf16[4,7168]{1,0:T(4,128)(2,1)S(1)}, u32[]{:S(2)}, u32[]{:S(2)}) collective-permute-start(bf16[4,7168]{1,0:T(4,128)(2,1)S(1)} %collective-permute-done.25), channel_id=1, source_target_pairs={{0,2},{1,3},{2,0},{3,1},{4,6},{5,7},{6,4},{7,5},{8,10},{9,11},{10,... | collective-permute-start | bytes 172040 | tf_op jit(solution)/shard_map/ppermute | solution.py:19
  61.6 3.5 %collective-permute-start.26 = (bf16[4,7168]{1,0:T(4,128)(2,1)S(1)}, bf16[4,7168]{1,0:T(4,128)(2,1)S(1)}, u32[]{:S(2)}, u32[]{:S(2)}) collective-permute-start(bf16[4,7168]{1,0:T(4,128)(2,1)S(1)} %collective-permute-done.25), channel_id=1, source_target_pairs={{0,1},{1,0},{2,3},{3,2},{4,5},{5,4},{6,7},{7,6},{8,9},{9,8},{10,11... | collective-permute-start | bytes 172040 | tf_op jit(solution)/shard_map/ppermute | solution.py:19
  61.7 4.4 %collective-permute-start.23 = (bf16[4,7168]{1,0:T(4,128)(2,1)S(1)}, bf16[4,7168]{1,0:T(4,128)(2,1)S(1)}, u32[]{:S(2)}, u32[]{:S(2)}) collective-permute-start(bf16[4,7168]{1,0:T(4,128)(2,1)S(1)} %collective-permute-done.20), channel_id=1, source_target_pairs={{0,2},{1,3},{2,0},{3,1},{4,6},{5,7},{6,4},{7,5},{8,10},{9,11},{10,... | collective-permute-start | bytes 172040 | tf_op jit(solution)/shard_map/ppermute | solution.py:19
  63.6 2.5 %collective-permute-start.22 = (bf16[4,7168]{1,0:T(4,128)(2,1)S(1)}, bf16[4,7168]{1,0:T(4,128)(2,1)S(1)}, u32[]{:S(2)}, u32[]{:S(2)}) collective-permute-start(bf16[4,7168]{1,0:T(4,128)(2,1)S(1)} %collective-permute-done.20), channel_id=1, source_target_pairs={{0,1},{1,0},{2,3},{3,2},{4,5},{5,4},{6,7},{7,6},{8,9},{9,8},{10,11... | collective-permute-start | bytes 172040 | tf_op jit(solution)/shard_map/ppermute | solution.py:19
  63.6 2.5 %collective-permute-start.36 = (bf16[4,7168]{1,0:T(4,128)(2,1)S(1)}, bf16[4,7168]{1,0:T(4,128)(2,1)S(1)}, u32[]{:S(2)}, u32[]{:S(2)}) collective-permute-start(bf16[4,7168]{1,0:T(4,128)(2,1)S(1)} %collective-permute-done.35), channel_id=1, source_target_pairs={{0,1},{1,0},{2,3},{3,2},{4,5},{5,4},{6,7},{7,6},{8,9},{9,8},{10,11... | collective-permute-start | bytes 172040 | tf_op jit(solution)/shard_map/ppermute | solution.py:19
  65.1 1.2 %collective-permute-start.32 = (bf16[4,7168]{1,0:T(4,128)(2,1)S(1)}, bf16[4,7168]{1,0:T(4,128)(2,1)S(1)}, u32[]{:S(2)}, u32[]{:S(2)}) collective-permute-start(bf16[4,7168]{1,0:T(4,128)(2,1)S(1)} %collective-permute-done.31), channel_id=1, source_target_pairs={{0,1},{1,0},{2,3},{3,2},{4,5},{5,4},{6,7},{7,6},{8,9},{9,8},{10,11... | collective-permute-start | bytes 172040 | tf_op jit(solution)/shard_map/ppermute | solution.py:19
  65.1 1.4 %collective-permute-start.28 = (bf16[4,7168]{1,0:T(4,128)(2,1)S(1)}, bf16[4,7168]{1,0:T(4,128)(2,1)S(1)}, u32[]{:S(2)}, u32[]{:S(2)}) collective-permute-start(bf16[4,7168]{1,0:T(4,128)(2,1)S(1)} %collective-permute-done.27), channel_id=1, source_target_pairs={{0,1},{1,0},{2,3},{3,2},{4,5},{5,4},{6,7},{7,6},{8,9},{9,8},{10,11... | collective-permute-start | bytes 172040 | tf_op jit(solution)/shard_map/ppermute | solution.py:19
  66.1 1.2 %collective-permute-start.24 = (bf16[4,7168]{1,0:T(4,128)(2,1)S(1)}, bf16[4,7168]{1,0:T(4,128)(2,1)S(1)}, u32[]{:S(2)}, u32[]{:S(2)}) collective-permute-start(bf16[4,7168]{1,0:T(4,128)(2,1)S(1)} %collective-permute-done.23), channel_id=1, source_target_pairs={{0,1},{1,0},{2,3},{3,2},{4,5},{5,4},{6,7},{7,6},{8,9},{9,8},{10,11... | collective-permute-start | bytes 172040 | tf_op jit(solution)/shard_map/ppermute | solution.py:19
  77.5 1.9 %collective-permute-start.37 = (bf16[4,2,4,7168]{3,2,0,1:T(4,128)(2,1)S(1)}, bf16[4,2,4,7168]{3,2,0,1:T(4,128)(2,1)S(1)}, u32[]{:S(2)}, u32[]{:S(2)}) collective-permute-start(bf16[4,2,4,7168]{3,2,0,1:T(4,128)(2,1)S(1)} %bitcast.95), channel_id=1, source_target_pairs={{0,1},{1,0},{2,3},{3,2},{4,5},{5,4},{6,7},{7,6},{8,9},{9,8},{10,11... | collective-permute-start | bytes 1376264 | tf_op jit(solution)/shard_map/ppermute | solution.py:19
  79.7 7.7 %collective-permute-start.38 = (bf16[4,4,7168]{2,1,0:T(4,128)(2,1)S(1)}, bf16[4,4,7168]{2,1,0:T(4,128)(2,1)S(1)}, u32[]{:S(2)}, u32[]{:S(2)}) collective-permute-start(bf16[4,4,7168]{2,1,0:T(4,128)(2,1)S(1)} %fusion.28), channel_id=1, source_target_pairs={{0,2},{1,3},{2,0},{3,1},{4,6},{5,7},{6,4},{7,5},{8,10},{9,11},{10,... | collective-permute-start | bytes 688136 | tf_op jit(solution)/shard_map/ppermute | solution.py:19
  80.8 13.6 %collective-permute-start.21 = (bf16[4,7168]{1,0:T(4,128)(2,1)S(1)}, bf16[4,7168]{1,0:T(4,128)(2,1)S(1)}, u32[]{:S(2)}, u32[]{:S(2)}) collective-permute-start(bf16[4,7168]{1,0:T(4,128)(2,1)S(1)} %collective-permute-done.20), channel_id=1, source_target_pairs={{0,16},{1,17},{2,18},{3,19},{4,20},{5,21},{6,22},{7,23},{8,24},{9,... | collective-permute-start | bytes 172040 | tf_op jit(solution)/shard_map/ppermute | solution.py:19
  87.7 6.8 %collective-permute-start.39 = (bf16[4,7168]{1,0:T(4,128)(2,1)S(1)}, bf16[4,7168]{1,0:T(4,128)(2,1)S(1)}, u32[]{:S(2)}, u32[]{:S(2)}) collective-permute-start(bf16[4,7168]{1,0:T(4,128)(2,1)S(1)} %get-tuple-element.15), channel_id=1, source_target_pairs={{0,16},{1,17},{2,18},{3,19},{4,20},{5,21},{6,22},{7,23},{8,24},{9,... | collective-permute-start | bytes 172040 | tf_op jit(solution)/shard_map/ppermute | solution.py:19
  88.6 7.0 %collective-permute-start.42 = (bf16[4,7168]{1,0:T(4,128)(2,1)S(1)}, bf16[4,7168]{1,0:T(4,128)(2,1)S(1)}, u32[]{:S(2)}, u32[]{:S(2)}) collective-permute-start(bf16[4,7168]{1,0:T(4,128)(2,1)S(1)} %get-tuple-element.16), channel_id=1, source_target_pairs={{0,28},{1,29},{2,30},{3,31},{4,24},{5,25},{6,26},{7,27},{8,20},{9,... | collective-permute-start | bytes 172040 | tf_op jit(solution)/shard_map/ppermute | solution.py:19
  91.5 6.0 %collective-permute-start.41 = (bf16[4,7168]{1,0:T(4,128)(2,1)S(1)}, bf16[4,7168]{1,0:T(4,128)(2,1)S(1)}, u32[]{:S(2)}, u32[]{:S(2)}) collective-permute-start(bf16[4,7168]{1,0:T(4,128)(2,1)S(1)} %get-tuple-element.17), channel_id=1, source_target_pairs={{0,24},{1,25},{2,26},{3,27},{4,28},{5,29},{6,30},{7,31},{8,16},{9,... | collective-permute-start | bytes 172040 | tf_op jit(solution)/shard_map/ppermute | solution.py:19
  91.5 6.2 %collective-permute-start.40 = (bf16[4,7168]{1,0:T(4,128)(2,1)S(1)}, bf16[4,7168]{1,0:T(4,128)(2,1)S(1)}, u32[]{:S(2)}, u32[]{:S(2)}) collective-permute-start(bf16[4,7168]{1,0:T(4,128)(2,1)S(1)} %get-tuple-element.18), channel_id=1, source_target_pairs={{0,20},{1,21},{2,22},{3,23},{4,16},{5,17},{6,18},{7,19},{8,28},{9,... | collective-permute-start | bytes 172040 | tf_op jit(solution)/shard_map/ppermute | solution.py:19

commit v3 on v1

v3 whole, which is shorter than its diff:
```python
import jax
import jax.numpy as jnp
from jax import lax
from jax.experimental import pallas as pl
from jax.experimental.pallas import tpu as pltpu
from jax.sharding import PartitionSpec as P

GROUP = 4
LANES = 128
CHUNK = 1024


def step_flips(owners):
    bits = [1 << place for place in range(1, owners.bit_length() - 1)]
    even = bits[::-1]
    odd = bits[:1] + bits[:0:-1]
    return list(zip(even, odd))


def exchange(value, flips, hop):
    segments, owners = lax.axis_size("segment"), lax.axis_size("expert")
    if flips == (0, 0) and hop % segments == 0:
        return value
    pairs = []
    for seg in range(segments):
        for own in range(owners):
            target = (seg + hop) % segments * owners + (own ^ flips[own % 2])
            pairs.append((seg * owners + own, target))
    return lax.ppermute(value, ("segment", "expert"), pairs)


def mlp_kernel(col_ref, own_ref, far_ref, own_w_ref, far_w_ref, gain_ref, gate_ref, up_ref, down_ref,
               own_out, far_out, rows_ref):
    half = own_ref.shape[0]
    dim = gate_ref.shape[1]
    for part, ref in enumerate((own_ref, far_ref)):
        square = jnp.zeros((half, LANES), jnp.float32)
        for start in range(0, dim, LANES):
            piece = ref[:, start:start + LANES].astype(jnp.float32)
            square += piece * piece
        inv = lax.rsqrt(jnp.sum(square, axis=1, keepdims=True) / dim + 1e-06)
        for start in range(0, dim, CHUNK):
            piece = ref[:, start:start + CHUNK].astype(jnp.float32)
            scaled = piece * inv * gain_ref[:, start:start + CHUNK]
            rows_ref[part * half:(part + 1) * half, start:start + CHUNK] = scaled.astype(jnp.bfloat16)
    gated = jnp.zeros((2 * half, gate_ref.shape[2]), jnp.float32)
    up_part = jnp.zeros((2 * half, gate_ref.shape[2]), jnp.float32)
    for start in range(0, dim, CHUNK):
        rows = rows_ref[:, start:start + CHUNK]
        gated += jnp.dot(rows, gate_ref[0, start:start + CHUNK, :], preferred_element_type=jnp.float32)
        up_part += jnp.dot(rows, up_ref[0, start:start + CHUNK, :], preferred_element_type=jnp.float32)
    inner = (gated / (1.0 + jnp.exp(-gated)) * up_part).astype(jnp.bfloat16)
    lane = lax.broadcasted_iota(jnp.int32, (half, LANES), 1)
    weights = []
    for ref in (own_w_ref, far_w_ref):
        here = jnp.where(lane == col_ref[0], ref[...].astype(jnp.float32), 0.0)
        weights.append(jnp.sum(here, axis=1, keepdims=True))
    for start in range(0, dim, CHUNK):
        terms = jnp.dot(inner, down_ref[0, :, start:start + CHUNK], preferred_element_type=jnp.float32)
        for part, out in enumerate((own_out, far_out)):
            weight = weights[part]
            chosen = jnp.where(weight > 0.0, weight * terms[part * half:(part + 1) * half], 0.0)
            out[:, start:start + CHUNK] = chosen.astype(jnp.bfloat16)


def mlp(col, own, far, own_w, far_w, gain, gate, up, down):
    half, dim = own.shape[0], gate.shape[1]
    vmem = pl.BlockSpec(memory_space=pltpu.VMEM)
    return pl.pallas_call(
        mlp_kernel,
        out_shape=[jax.ShapeDtypeStruct((half, dim), jnp.bfloat16)] * 2,
        in_specs=[pl.BlockSpec(memory_space=pltpu.SMEM)] + [vmem] * 8,
        out_specs=[vmem] * 2,
        scratch_shapes=[pltpu.VMEM((2 * half, dim), jnp.bfloat16)],
        compiler_params=pltpu.CompilerParams(vmem_limit_bytes=24 * 1024 * 1024),
        cost_estimate=pl.CostEstimate(
            flops=12 * half * dim * gate.shape[2], bytes_accessed=6 * dim * gate.shape[2], transcendentals=0
        ),
    )(col, own, far, own_w, far_w, gain, gate, up, down)


def on_device(states, routing, route_weight, norm_gain, gate_proj, up_proj, down_proj):
    owners = lax.axis_size("expert")
    experts = owners // GROUP
    row_dev = states.shape[1]
    model_dim = states.shape[2]
    passes_count = routing.shape[1]
    expert_ids = jnp.arange(experts, dtype=jnp.int32)
    steps = step_flips(owners)
    gate, up, down = [
        pltpu.with_memory_space_constraint(w, pltpu.VMEM) for w in (gate_proj, up_proj, down_proj)
    ]

    picked = routing[0][..., None] == expert_ids
    dense = jnp.sum(jnp.where(picked, route_weight[0][..., None].astype(jnp.float32), 0.0), axis=2)
    dense = jnp.moveaxis(dense, 0, 1).reshape(row_dev, passes_count * experts).astype(jnp.bfloat16)
    dense = jnp.pad(dense, ((0, 0), (0, LANES - passes_count * experts)))
    mine = lax.axis_index("expert") // GROUP

    current = states[0]
    for step_no in range(passes_count):
        hop = 1 if step_no > 0 else 0
        last = step_no == passes_count - 1
        block = exchange(current, (0, 0), hop)
        own = jnp.concatenate([block, exchange(current, steps[0], hop)], axis=0)
        if step_no == 0:
            tail = jnp.concatenate([dense, exchange(dense, steps[0], 0)], axis=0)
            own = jnp.concatenate([own, tail], axis=1)
        for flips in steps[1:]:
            own = jnp.concatenate([own, exchange(own, flips, 0)], axis=0)
        far = exchange(own, (1, 1), 0)
        if step_no == 0:
            own_w, far_w = own[:, model_dim:], far[:, model_dim:]
        col = (step_no * experts + mine).astype(jnp.int32).reshape(1)
        kept, sent = mlp(col, own, far, own_w, far_w, norm_gain, gate, up, down)

        kept = kept.astype(jnp.float32) + exchange(sent, (1, 1), 0).astype(jnp.float32)
        for flips in steps[:0:-1]:
            middle = kept.shape[0] // 2
            sent = kept[middle:].astype(jnp.bfloat16)
            kept = kept[:middle] + exchange(sent, flips, 0).astype(jnp.float32)
        if last:
            block = exchange(block, (0, 0), 1)
            near = exchange(kept[:row_dev].astype(jnp.bfloat16), (0, 0), 1)
        else:
            near = kept[:row_dev]
        other = exchange(kept[row_dev:].astype(jnp.bfloat16), steps[0], 1 if last else 0)
        total = block.astype(jnp.float32) + near.astype(jnp.float32) + other.astype(jnp.float32)
        current = total.astype(jnp.bfloat16)
    return current[None]


def solution(mesh):
    return jax.shard_map(
        on_device,
        mesh=mesh,
        in_specs=(
            P("segment", "expert", None),
            P("segment", None, "expert", None),
            P("segment", None, "expert", None),
            P("segment", None),
            P("segment", None, "expert"),
            P("segment", None, "expert"),
            P("segment", "expert", None),
        ),
        out_specs=P("segment", "expert", None),
        check_vma=False,
    )
```

time: 294 us -> 106 us (0.36)
  waiting for transfers between devices: 184 us -> 51.6 us
  blocking collectives: 66.4 us -> 0 us
  starting transfers between devices: 3.11 us -> 29.6 us
  matrix products: 18.4 us -> 0 us
  between operations: 14.2 us -> 0.2 us
  local copies, waits for them, and re-layouts: 2.21 us -> 13.2 us
  Pallas kernels: 0 us -> 4.75 us
    unnamed x4 -> x0, waiting for transfers between devices: 178 us -> none
    all_gather x3 -> x0, blocking collectives: 66.4 us -> none  [the longest x2 43.2 us: on_device(): rows = lax.all_gather(normed, 'expert', axis=0, tiled=True)]
    ppermute x2 -> x20, waiting for transfers between devices: 5.41 us -> 51.6 us  [exchange(): return lax.ppermute(value, ('segment', 'expert'), pairs)]
    ppermute x2 -> x20, starting transfers between devices: 3.07 us -> 29.6 us  [exchange(): return lax.ppermute(value, ('segment', 'expert'), pairs)]
    dot_general x4 -> x0, matrix products: 18.4 us -> none  [the longest x2 12.9 us: on_device(): jnp.dot(inner_act, down_mat, preferred_element_type=jnp.float32)]
    unnamed x10 -> x18, local copies, waits for them, and re-layouts: 1.64 us -> 13 us
    pallas_call x0 -> x2, Pallas kernels: none -> 4.75 us  [mlp(): pl.pallas_call(mlp_kernel, out_shape=[jax.ShapeDtypeStruct((half, dim), j...]
    concatenate x0 -> x6, other arithmetic: none -> 2.97 us  [the longest x4 2.03 us: on_device(): own = jnp.concatenate([own, exchange(own, flips, 0)], axis=0)]
  transfers between devices with their start and end apart: 4 -> 20, of which waited for: 4 -> 18; matrix products, arithmetic and copies ran while one was open for 0% -> 2% of each run, Pallas kernels for 0% -> 0%
where the time goes in v3:
time: 106 us; the launch traced here: 105 us
  waiting for transfers between devices  51.6 us (49%)
  starting transfers between devices  29.6 us (28%)
  local copies, waits for them, and re-layouts  13.2 us (12%)
  other arithmetic  5.48 us (5%)
  Pallas kernels  4.75 us (4%)
    ppermute x20, waiting for transfers between devices, exchange(): return lax.ppermute(value, ('segment', 'expert'), pairs)  51.6 us
    ppermute x20, starting transfers between devices, exchange(): return lax.ppermute(value, ('segment', 'expert'), pairs)  29.6 us
    unnamed x18, local copies, waits for them, and re-layouts  13 us
    pallas_call x2, Pallas kernels, mlp(): pl.pallas_call(mlp_kernel, out_shape=[jax.ShapeDtypeStruct((half, dim), j...  4.75 us
  transfers between devices with their start and end apart: 20, of which 18 were waited for; matrix products, arithmetic and copies ran while one was open for 2% of the time, Pallas kernels for 0%

profile of v3, /device:TPU:0, one launch (start us, length us, event | category | flops | bytes accessed | tf_op | source)
XLA Modules:
  0.0 104.9 jit_solution(14207137760138688965)
XLA Ops:
  0.0 4.0 %collective-permute-start = (bf16[4,7168]{1,0:T(4,128)(2,1)}, bf16[4,7168]{1,0:T(4,128)(2,1)S(1)}, u32[]{:S(2)}, u32[]{:S(2)}) collective-permute-start(bf16[4,7168]{1,0:T(4,128)(2,1)} %bitcast.13), channel_id=1, source_target_pairs={{0,8},{1,3},{2,10},{3,1},{4,12},{5,7},{6,14},{7,5},{8,0},{9,11},{1... | collective-permute-start | bytes 172040 | tf_op jit(solution)/shard_map/ppermute | solution.py:29
  4.0 0.7 bitcast_convert_fusion
  4.7 0.8 select_reduce_fusion
  5.5 0.1 convert_element_type.79
  5.6 0.0 collective-permute-start.1
  5.6 4.5 %collective-permute-done.1 = bf16[4,128]{1,0:T(4,128)(2,1)S(1)} collective-permute-done((bf16[4,128]{1,0:T(4,128)(2,1)S(1)}, bf16[4,128]{1,0:T(4,128)(2,1)S(1)}, u32[]{:S(2)}, u32[]{:S(2)}) %collective-permute-start.1) | collective-permute-done | bytes 1056 | tf_op jit(solution)/shard_map/ppermute | solution.py:29
  10.1 0.9 maximum_maximum_fusion
  11.0 1.6 %collective-permute-start.2 = (bf16[8,7296]{1,0:T(8,128)(2,1)S(1)}, bf16[8,7296]{1,0:T(8,128)(2,1)S(1)}, u32[]{:S(2)}, u32[]{:S(2)}) collective-permute-start(bf16[8,7296]{1,0:T(8,128)(2,1)S(1)} %maximum_maximum_fusion), channel_id=1, source_target_pairs={{0,4},{1,9},{2,6},{3,11},{4,0},{5,13},{6,2},{7,15},{8,12},{9,1},{1... | collective-permute-start | bytes 350216 | tf_op jit(solution)/shard_map/ppermute | solution.py:29
  12.6 3.2 %collective-permute-done.2 = bf16[8,7296]{1,0:T(8,128)(2,1)S(1)} collective-permute-done((bf16[8,7296]{1,0:T(8,128)(2,1)S(1)}, bf16[8,7296]{1,0:T(8,128)(2,1)S(1)}, u32[]{:S(2)}, u32[]{:S(2)}) %collective-permute-start.2) | collective-permute-done | bytes 116768 | tf_op jit(solution)/shard_map/ppermute | solution.py:29
  15.8 0.9 pad_maximum_fusion.2
  16.8 1.6 %collective-permute-start.3 = (bf16[16,7296]{1,0:T(8,128)(2,1)S(1)}, bf16[16,7296]{1,0:T(8,128)(2,1)S(1)}, u32[]{:S(2)}, u32[]{:S(2)}) collective-permute-start(bf16[16,7296]{1,0:T(8,128)(2,1)S(1)} %pad_maximum_fusion.2), channel_id=1, source_target_pairs={{0,2},{1,5},{2,0},{3,7},{4,6},{5,1},{6,4},{7,3},{8,10},{9,13},{10,... | collective-permute-start | bytes 700424 | tf_op jit(solution)/shard_map/ppermute | solution.py:29
  18.3 4.5 %collective-permute-done.3 = bf16[16,7296]{1,0:T(8,128)(2,1)S(1)} collective-permute-done((bf16[16,7296]{1,0:T(8,128)(2,1)S(1)}, bf16[16,7296]{1,0:T(8,128)(2,1)S(1)}, u32[]{:S(2)}, u32[]{:S(2)}) %collective-permute-start.3) | collective-permute-done | bytes 233504 | tf_op jit(solution)/shard_map/ppermute | solution.py:29
  22.9 0.9 pad_maximum_fusion.own_ref
  23.8 0.1 collective-permute-start.4
  23.9 1.8 %collective-permute-done.4.far_ref = bf16[32,7296]{1,0:T(8,128)(2,1)S(1)} collective-permute-done((bf16[32,7296]{1,0:T(8,128)(2,1)S(1)}, bf16[32,7296]{1,0:T(8,128)(2,1)S(1)}, u32[]{:S(2)}, u32[]{:S(2)}) %collective-permute-start.4) | collective-permute-done | bytes 466976 | tf_op jit(solution)/shard_map/ppermute | solution.py:29
  25.7 2.0 %copy-done = bf16[1,7168,256]{2,1,0:T(8,128)(2,1)S(1)} copy-done((bf16[1,7168,256]{2,1,0:T(8,128)(2,1)S(1)}, bf16[1,7168,256]{2,1,0:T(8,128)(2,1)}, u32[]{:S(2)}) %copy-start) | copy-done | bytes 3670040
  27.7 2.0 %copy-done.2 = bf16[1,7168,256]{2,1,0:T(8,128)(2,1)S(1)} copy-done((bf16[1,7168,256]{2,1,0:T(8,128)(2,1)S(1)}, bf16[1,7168,256]{2,1,0:T(8,128)(2,1)}, u32[]{:S(2)}) %copy-start.2) | copy-done | bytes 3670040
  29.8 2.0 %copy-done.4 = bf16[1,256,7168]{2,1,0:T(8,128)(2,1)S(1)} copy-done((bf16[1,256,7168]{2,1,0:T(8,128)(2,1)S(1)}, bf16[1,256,7168]{2,1,0:T(8,128)(2,1)}, u32[]{:S(2)}) %copy-start.4) | copy-done | bytes 3670040
  31.8 0.7 copy-done.6
  32.6 2.4 %shard_map.73 = (bf16[32,7168]{1,0:T(8,128)(2,1)S(1)}, bf16[32,7168]{1,0:T(8,128)(2,1)S(1)}) custom-call(s32[1]{0:T(128)} %bitcast.1.col_ref, bf16[32,7296]{1,0:T(8,128)(2,1)S(1)} %pad_maximum_fusion.own_ref, bf16[32,7296]{1,0:T(8,128)(2,1)S(1)} %collective-permute-done.4.far_ref, bf16[32,128]{1,0:T(8,128)(2,1)S(1)} %slice.63.own_w_ref, ...), custom_call_target="tpu_custom_call" | custom-call | flops 704643072 | bytes 11010048 | tf_op jit(solution)/shard_map/pallas_call | solution.py:69
  35.0 0.0 copy-start.8
  35.0 0.0 copy-start.7
  35.0 0.2 collective-permute-start.5
  35.2 1.7 %collective-permute-done.5 = bf16[32,7168]{1,0:T(8,128)(2,1)S(1)} collective-permute-done((bf16[32,7168]{1,0:T(8,128)(2,1)S(1)}, bf16[32,7168]{1,0:T(8,128)(2,1)S(1)}, u32[]{:S(2)}, u32[]{:S(2)}) %collective-permute-start.5) | collective-permute-done | bytes 458784 | tf_op jit(solution)/shard_map/ppermute | solution.py:29
  36.9 0.1 convert_add_fusion.1
  37.0 1.6 %collective-permute-start.6 = (bf16[16,7168]{1,0:T(8,128)(2,1)S(1)}, bf16[16,7168]{1,0:T(8,128)(2,1)S(1)}, u32[]{:S(2)}, u32[]{:S(2)}) collective-permute-start(bf16[16,7168]{1,0:T(8,128)(2,1)S(1)} %slice.94), channel_id=1, source_target_pairs={{0,2},{1,5},{2,0},{3,7},{4,6},{5,1},{6,4},{7,3},{8,10},{9,13},{10,... | collective-permute-start | bytes 688136 | tf_op jit(solution)/shard_map/ppermute | solution.py:29
  38.6 4.5 %collective-permute-done.6 = bf16[16,7168]{1,0:T(8,128)(2,1)S(1)} collective-permute-done((bf16[16,7168]{1,0:T(8,128)(2,1)S(1)}, bf16[16,7168]{1,0:T(8,128)(2,1)S(1)}, u32[]{:S(2)}, u32[]{:S(2)}) %collective-permute-start.6) | collective-permute-done | bytes 229408 | tf_op jit(solution)/shard_map/ppermute | solution.py:29
  43.1 0.1 slice_add_fusion.1
  43.2 2.0 %collective-permute-start.7 = (bf16[8,7168]{1,0:T(8,128)(2,1)S(1)}, bf16[8,7168]{1,0:T(8,128)(2,1)S(1)}, u32[]{:S(2)}, u32[]{:S(2)}) collective-permute-start(bf16[8,7168]{1,0:T(8,128)(2,1)S(1)} %slice.96), channel_id=1, source_target_pairs={{0,4},{1,9},{2,6},{3,11},{4,0},{5,13},{6,2},{7,15},{8,12},{9,1},{1... | collective-permute-start | bytes 344072 | tf_op jit(solution)/shard_map/ppermute | solution.py:29
  45.2 3.5 %collective-permute-done.7 = bf16[8,7168]{1,0:T(8,128)(2,1)S(1)} collective-permute-done((bf16[8,7168]{1,0:T(8,128)(2,1)S(1)}, bf16[8,7168]{1,0:T(8,128)(2,1)S(1)}, u32[]{:S(2)}, u32[]{:S(2)}) %collective-permute-start.7) | collective-permute-done | bytes 114720 | tf_op jit(solution)/shard_map/ppermute | solution.py:29
  48.7 1.5 %collective-permute-start.8 = (bf16[4,7168]{1,0:T(4,128)(2,1)S(1)}, bf16[4,7168]{1,0:T(4,128)(2,1)S(1)}, u32[]{:S(2)}, u32[]{:S(2)}) collective-permute-start(bf16[4,7168]{1,0:T(4,128)(2,1)S(1)} %slice.97), channel_id=1, source_target_pairs={{0,8},{1,3},{2,10},{3,1},{4,12},{5,7},{6,14},{7,5},{8,0},{9,11},{1... | collective-permute-start | bytes 172040 | tf_op jit(solution)/shard_map/ppermute | solution.py:29
  50.3 3.6 %collective-permute-done.8 = bf16[4,7168]{1,0:T(4,128)(2,1)S(1)} collective-permute-done((bf16[4,7168]{1,0:T(4,128)(2,1)S(1)}, bf16[4,7168]{1,0:T(4,128)(2,1)S(1)}, u32[]{:S(2)}, u32[]{:S(2)}) %collective-permute-start.8) | collective-permute-done | bytes 57376 | tf_op jit(solution)/shard_map/ppermute | solution.py:29
  53.9 0.1 fusion.2
  53.9 2.5 %collective-permute-start.11 = (bf16[4,7168]{1,0:T(4,128)(2,1)S(1)}, bf16[4,7168]{1,0:T(4,128)(2,1)S(1)}, u32[]{:S(2)}, u32[]{:S(2)}) collective-permute-start(bf16[4,7168]{1,0:T(4,128)(2,1)S(1)} %fusion.2), channel_id=1, source_target_pairs={{0,24},{1,19},{2,26},{3,17},{4,28},{5,23},{6,30},{7,21},{8,16},{9,... | collective-permute-start | bytes 172040 | tf_op jit(solution)/shard_map/ppermute | solution.py:29
  56.4 0.5 collective-permute-start.9
  56.9 3.0 %collective-permute-done.11 = bf16[4,7168]{1,0:T(4,128)(2,1)S(1)} collective-permute-done((bf16[4,7168]{1,0:T(4,128)(2,1)S(1)}, bf16[4,7168]{1,0:T(4,128)(2,1)S(1)}, u32[]{:S(2)}, u32[]{:S(2)}) %collective-permute-start.11) | collective-permute-done | bytes 57376 | tf_op jit(solution)/shard_map/ppermute | solution.py:29
  60.0 0.6 collective-permute-done.9
  60.6 0.1 pad_maximum_fusion.4
  60.7 2.1 %collective-permute-start.12 = (bf16[8,7168]{1,0:T(8,128)(2,1)S(1)}, bf16[8,7168]{1,0:T(8,128)(2,1)S(1)}, u32[]{:S(2)}, u32[]{:S(2)}) collective-permute-start(bf16[8,7168]{1,0:T(8,128)(2,1)S(1)} %pad_maximum_fusion.4), channel_id=1, source_target_pairs={{0,4},{1,9},{2,6},{3,11},{4,0},{5,13},{6,2},{7,15},{8,12},{9,1},{1... | collective-permute-start | bytes 344072 | tf_op jit(solution)/shard_map/ppermute | solution.py:29
  62.8 3.4 %collective-permute-done.12 = bf16[8,7168]{1,0:T(8,128)(2,1)S(1)} collective-permute-done((bf16[8,7168]{1,0:T(8,128)(2,1)S(1)}, bf16[8,7168]{1,0:T(8,128)(2,1)S(1)}, u32[]{:S(2)}, u32[]{:S(2)}) %collective-permute-start.12) | collective-permute-done | bytes 114720 | tf_op jit(solution)/shard_map/ppermute | solution.py:29
  66.2 0.1 pad_maximum_fusion.3
  66.3 3.2 %collective-permute-start.13 = (bf16[16,7168]{1,0:T(8,128)(2,1)S(1)}, bf16[16,7168]{1,0:T(8,128)(2,1)S(1)}, u32[]{:S(2)}, u32[]{:S(2)}) collective-permute-start(bf16[16,7168]{1,0:T(8,128)(2,1)S(1)} %pad_maximum_fusion.3), channel_id=1, source_target_pairs={{0,2},{1,5},{2,0},{3,7},{4,6},{5,1},{6,4},{7,3},{8,10},{9,13},{10,... | collective-permute-start | bytes 688136 | tf_op jit(solution)/shard_map/ppermute | solution.py:29
  69.5 4.0 %collective-permute-done.13 = bf16[16,7168]{1,0:T(8,128)(2,1)S(1)} collective-permute-done((bf16[16,7168]{1,0:T(8,128)(2,1)S(1)}, bf16[16,7168]{1,0:T(8,128)(2,1)S(1)}, u32[]{:S(2)}, u32[]{:S(2)}) %collective-permute-start.13) | collective-permute-done | bytes 229408 | tf_op jit(solution)/shard_map/ppermute | solution.py:29
  73.5 0.1 pad_maximum_fusion.1.own_ref
  73.6 0.1 collective-permute-start.14
  73.7 1.8 %collective-permute-done.14.far_ref = bf16[32,7168]{1,0:T(8,128)(2,1)S(1)} collective-permute-done((bf16[32,7168]{1,0:T(8,128)(2,1)S(1)}, bf16[32,7168]{1,0:T(8,128)(2,1)S(1)}, u32[]{:S(2)}, u32[]{:S(2)}) %collective-permute-start.14) | collective-permute-done | bytes 458784 | tf_op jit(solution)/shard_map/ppermute | solution.py:29
  75.5 2.0 %copy-done.1 = bf16[1,7168,256]{2,1,0:T(8,128)(2,1)S(1)} copy-done((bf16[1,7168,256]{2,1,0:T(8,128)(2,1)S(1)}, bf16[1,7168,256]{2,1,0:T(8,128)(2,1)}, u32[]{:S(2)}) %copy-start.1) | copy-done | bytes 3670040
  77.6 2.0 %copy-done.3 = bf16[1,7168,256]{2,1,0:T(8,128)(2,1)S(1)} copy-done((bf16[1,7168,256]{2,1,0:T(8,128)(2,1)S(1)}, bf16[1,7168,256]{2,1,0:T(8,128)(2,1)}, u32[]{:S(2)}) %copy-start.3) | copy-done | bytes 3670040
  79.6 2.0 %copy-done.5 = bf16[1,256,7168]{2,1,0:T(8,128)(2,1)S(1)} copy-done((bf16[1,256,7168]{2,1,0:T(8,128)(2,1)S(1)}, bf16[1,256,7168]{2,1,0:T(8,128)(2,1)}, u32[]{:S(2)}) %copy-start.5) | copy-done | bytes 3670040
  81.6 2.4 %shard_map.74 = (bf16[32,7168]{1,0:T(8,128)(2,1)S(1)}, bf16[32,7168]{1,0:T(8,128)(2,1)S(1)}) custom-call(s32[1]{0:T(128)} %bitcast.5.col_ref, bf16[32,7168]{1,0:T(8,128)(2,1)S(1)} %pad_maximum_fusion.1.own_ref, bf16[32,7168]{1,0:T(8,128)(2,1)S(1)} %collective-permute-done.14.far_ref, bf16[32,128]{1,0:T(8,128)(2,1)S(1)} %slice.63.own_w_ref, ...), custom_call_target="tpu_custom_call" | custom-call | flops 704643072 | bytes 11010048 | tf_op jit(solution)/shard_map/pallas_call | solution.py:69
  84.0 0.2 collective-permute-start.15
  84.2 1.7 %collective-permute-done.15 = bf16[32,7168]{1,0:T(8,128)(2,1)S(1)} collective-permute-done((bf16[32,7168]{1,0:T(8,128)(2,1)S(1)}, bf16[32,7168]{1,0:T(8,128)(2,1)S(1)}, u32[]{:S(2)}, u32[]{:S(2)}) %collective-permute-start.15) | collective-permute-done | bytes 458784 | tf_op jit(solution)/shard_map/ppermute | solution.py:29
  85.9 0.1 convert_add_fusion
  86.0 2.1 %collective-permute-start.16 = (bf16[16,7168]{1,0:T(8,128)(2,1)S(1)}, bf16[16,7168]{1,0:T(8,128)(2,1)S(1)}, u32[]{:S(2)}, u32[]{:S(2)}) collective-permute-start(bf16[16,7168]{1,0:T(8,128)(2,1)S(1)} %slice.93), channel_id=1, source_target_pairs={{0,2},{1,5},{2,0},{3,7},{4,6},{5,1},{6,4},{7,3},{8,10},{9,13},{10,... | collective-permute-start | bytes 688136 | tf_op jit(solution)/shard_map/ppermute | solution.py:29
  88.1 4.0 %collective-permute-done.16 = bf16[16,7168]{1,0:T(8,128)(2,1)S(1)} collective-permute-done((bf16[16,7168]{1,0:T(8,128)(2,1)S(1)}, bf16[16,7168]{1,0:T(8,128)(2,1)S(1)}, u32[]{:S(2)}, u32[]{:S(2)}) %collective-permute-start.16) | collective-permute-done | bytes 229408 | tf_op jit(solution)/shard_map/ppermute | solution.py:29
  92.1 0.1 slice_add_fusion
  92.2 1.4 %collective-permute-start.17 = (bf16[8,7168]{1,0:T(8,128)(2,1)S(1)}, bf16[8,7168]{1,0:T(8,128)(2,1)S(1)}, u32[]{:S(2)}, u32[]{:S(2)}) collective-permute-start(bf16[8,7168]{1,0:T(8,128)(2,1)S(1)} %slice.95), channel_id=1, source_target_pairs={{0,4},{1,9},{2,6},{3,11},{4,0},{5,13},{6,2},{7,15},{8,12},{9,1},{1... | collective-permute-start | bytes 344072 | tf_op jit(solution)/shard_map/ppermute | solution.py:29
  93.6 0.9 collective-permute-start.10
  94.5 2.7 %collective-permute-done.17 = bf16[8,7168]{1,0:T(8,128)(2,1)S(1)} collective-permute-done((bf16[8,7168]{1,0:T(8,128)(2,1)S(1)}, bf16[8,7168]{1,0:T(8,128)(2,1)S(1)}, u32[]{:S(2)}, u32[]{:S(2)}) %collective-permute-start.17) | collective-permute-done | bytes 114720 | tf_op jit(solution)/shard_map/ppermute | solution.py:29
  97.3 1.0 collective-permute-start.18
  98.3 2.9 %collective-permute-start.19 = (bf16[4,7168]{1,0:T(4,128)(2,1)S(1)}, bf16[4,7168]{1,0:T(4,128)(2,1)S(1)}, u32[]{:S(2)}, u32[]{:S(2)}) collective-permute-start(bf16[4,7168]{1,0:T(4,128)(2,1)S(1)} %get-tuple-element.14), channel_id=1, source_target_pairs={{0,24},{1,19},{2,26},{3,17},{4,28},{5,23},{6,30},{7,21},{8,16},{9,... | collective-permute-start | bytes 172040 | tf_op jit(solution)/shard_map/ppermute | solution.py:29
  101.2 0.6 collective-permute-done.18
  101.8 2.4 %collective-permute-done.19 = bf16[4,7168]{1,0:T(4,128)(2,1)S(1)} collective-permute-done((bf16[4,7168]{1,0:T(4,128)(2,1)S(1)}, bf16[4,7168]{1,0:T(4,128)(2,1)S(1)}, u32[]{:S(2)}, u32[]{:S(2)}) %collective-permute-start.19) | collective-permute-done | bytes 57376 | tf_op jit(solution)/shard_map/ppermute | solution.py:29
  104.3 0.7 fusion.3
  (23 shorter events, 0.2 us)
Async XLA Ops:
  0.0 10.1 %collective-permute-start = (bf16[4,7168]{1,0:T(4,128)(2,1)}, bf16[4,7168]{1,0:T(4,128)(2,1)S(1)}, u32[]{:S(2)}, u32[]{:S(2)}) collective-permute-start(bf16[4,7168]{1,0:T(4,128)(2,1)} %bitcast.13), channel_id=1, source_target_pairs={{0,8},{1,3},{2,10},{3,1},{4,12},{5,7},{6,14},{7,5},{8,0},{9,11},{1... | collective-permute-start | bytes 172040 | tf_op jit(solution)/shard_map/ppermute | solution.py:29
  5.6 4.5 %collective-permute-start.1 = (bf16[4,128]{1,0:T(4,128)(2,1)S(1)}, bf16[4,128]{1,0:T(4,128)(2,1)S(1)}, u32[]{:S(2)}, u32[]{:S(2)}) collective-permute-start(bf16[4,128]{1,0:T(4,128)(2,1)S(1)} %pad.4), channel_id=1, source_target_pairs={{0,8},{1,3},{2,10},{3,1},{4,12},{5,7},{6,14},{7,5},{8,0},{9,11},{1... | collective-permute-start | bytes 3080 | tf_op jit(solution)/shard_map/ppermute | solution.py:29
  11.0 4.9 %collective-permute-start.2 = (bf16[8,7296]{1,0:T(8,128)(2,1)S(1)}, bf16[8,7296]{1,0:T(8,128)(2,1)S(1)}, u32[]{:S(2)}, u32[]{:S(2)}) collective-permute-start(bf16[8,7296]{1,0:T(8,128)(2,1)S(1)} %maximum_maximum_fusion), channel_id=1, source_target_pairs={{0,4},{1,9},{2,6},{3,11},{4,0},{5,13},{6,2},{7,15},{8,12},{9,1},{1... | collective-permute-start | bytes 350216 | tf_op jit(solution)/shard_map/ppermute | solution.py:29
  16.8 6.1 %collective-permute-start.3 = (bf16[16,7296]{1,0:T(8,128)(2,1)S(1)}, bf16[16,7296]{1,0:T(8,128)(2,1)S(1)}, u32[]{:S(2)}, u32[]{:S(2)}) collective-permute-start(bf16[16,7296]{1,0:T(8,128)(2,1)S(1)} %pad_maximum_fusion.2), channel_id=1, source_target_pairs={{0,2},{1,5},{2,0},{3,7},{4,6},{5,1},{6,4},{7,3},{8,10},{9,13},{10,... | collective-permute-start | bytes 700424 | tf_op jit(solution)/shard_map/ppermute | solution.py:29
  23.8 1.9 %collective-permute-start.4 = (bf16[32,7296]{1,0:T(8,128)(2,1)S(1)}, bf16[32,7296]{1,0:T(8,128)(2,1)S(1)}, u32[]{:S(2)}, u32[]{:S(2)}) collective-permute-start(bf16[32,7296]{1,0:T(8,128)(2,1)S(1)} %pad_maximum_fusion.own_ref), channel_id=1, source_target_pairs={{0,1},{1,0},{2,3},{3,2},{4,5},{5,4},{6,7},{7,6},{8,9},{9,8},{10,11... | collective-permute-start | bytes 1400840 | tf_op jit(solution)/shard_map/ppermute | solution.py:29
  25.7 2.0 %copy-start = (bf16[1,7168,256]{2,1,0:T(8,128)(2,1)S(1)}, bf16[1,7168,256]{2,1,0:T(8,128)(2,1)}, u32[]{:S(2)}) copy-start(bf16[1,7168,256]{2,1,0:T(8,128)(2,1)} %gate_ref.3) | copy-start | bytes 11010052
  27.7 2.0 %copy-start.2 = (bf16[1,7168,256]{2,1,0:T(8,128)(2,1)S(1)}, bf16[1,7168,256]{2,1,0:T(8,128)(2,1)}, u32[]{:S(2)}) copy-start(bf16[1,7168,256]{2,1,0:T(8,128)(2,1)} %up_ref.3) | copy-start | bytes 11010052
  29.8 2.0 %copy-start.4 = (bf16[1,256,7168]{2,1,0:T(8,128)(2,1)S(1)}, bf16[1,256,7168]{2,1,0:T(8,128)(2,1)}, u32[]{:S(2)}) copy-start(bf16[1,256,7168]{2,1,0:T(8,128)(2,1)} %down_ref.3) | copy-start | bytes 11010052
  31.8 0.7 copy-start.6
  35.0 18.9 %copy-start.8 = (bf16[1,4,7168]{2,1,0:T(4,128)(2,1)S(1)}, bf16[1,4,7168]{2,1,0:T(4,128)(2,1)}, u32[]{:S(2)}) copy-start(bf16[1,4,7168]{2,1,0:T(4,128)(2,1)} %param.7) | copy-start | bytes 172036
  35.0 40.6 %copy-start.7 = (f32[1,7168]{1,0:T(1,128)S(1)}, f32[1,7168]{1,0:T(1,128)}, u32[]{:S(2)}) copy-start(f32[1,7168]{1,0:T(1,128)} %gain_ref.3) | copy-start | bytes 86020
  35.0 1.9 %collective-permute-start.5 = (bf16[32,7168]{1,0:T(8,128)(2,1)S(1)}, bf16[32,7168]{1,0:T(8,128)(2,1)S(1)}, u32[]{:S(2)}, u32[]{:S(2)}) collective-permute-start(bf16[32,7168]{1,0:T(8,128)(2,1)S(1)} %get-tuple-element.10), channel_id=1, source_target_pairs={{0,1},{1,0},{2,3},{3,2},{4,5},{5,4},{6,7},{7,6},{8,9},{9,8},{10,11... | collective-permute-start | bytes 1376264 | tf_op jit(solution)/shard_map/ppermute | solution.py:29
  37.0 6.1 %collective-permute-start.6 = (bf16[16,7168]{1,0:T(8,128)(2,1)S(1)}, bf16[16,7168]{1,0:T(8,128)(2,1)S(1)}, u32[]{:S(2)}, u32[]{:S(2)}) collective-permute-start(bf16[16,7168]{1,0:T(8,128)(2,1)S(1)} %slice.94), channel_id=1, source_target_pairs={{0,2},{1,5},{2,0},{3,7},{4,6},{5,1},{6,4},{7,3},{8,10},{9,13},{10,... | collective-permute-start | bytes 688136 | tf_op jit(solution)/shard_map/ppermute | solution.py:29
  43.2 5.5 %collective-permute-start.7 = (bf16[8,7168]{1,0:T(8,128)(2,1)S(1)}, bf16[8,7168]{1,0:T(8,128)(2,1)S(1)}, u32[]{:S(2)}, u32[]{:S(2)}) collective-permute-start(bf16[8,7168]{1,0:T(8,128)(2,1)S(1)} %slice.96), channel_id=1, source_target_pairs={{0,4},{1,9},{2,6},{3,11},{4,0},{5,13},{6,2},{7,15},{8,12},{9,1},{1... | collective-permute-start | bytes 344072 | tf_op jit(solution)/shard_map/ppermute | solution.py:29
  48.7 5.1 %collective-permute-start.8 = (bf16[4,7168]{1,0:T(4,128)(2,1)S(1)}, bf16[4,7168]{1,0:T(4,128)(2,1)S(1)}, u32[]{:S(2)}, u32[]{:S(2)}) collective-permute-start(bf16[4,7168]{1,0:T(4,128)(2,1)S(1)} %slice.97), channel_id=1, source_target_pairs={{0,8},{1,3},{2,10},{3,1},{4,12},{5,7},{6,14},{7,5},{8,0},{9,11},{1... | collective-permute-start | bytes 172040 | tf_op jit(solution)/shard_map/ppermute | solution.py:29
  53.9 6.0 %collective-permute-start.11 = (bf16[4,7168]{1,0:T(4,128)(2,1)S(1)}, bf16[4,7168]{1,0:T(4,128)(2,1)S(1)}, u32[]{:S(2)}, u32[]{:S(2)}) collective-permute-start(bf16[4,7168]{1,0:T(4,128)(2,1)S(1)} %fusion.2), channel_id=1, source_target_pairs={{0,24},{1,19},{2,26},{3,17},{4,28},{5,23},{6,30},{7,21},{8,16},{9,... | collective-permute-start | bytes 172040 | tf_op jit(solution)/shard_map/ppermute | solution.py:29
  56.4 4.2 %collective-permute-start.9 = (bf16[4,7168]{1,0:T(4,128)(2,1)S(1)}, bf16[4,7168]{1,0:T(4,128)(2,1)S(1)}, u32[]{:S(2)}, u32[]{:S(2)}) collective-permute-start(bf16[4,7168]{1,0:T(4,128)(2,1)S(1)} %fusion.2), channel_id=1, source_target_pairs={{0,16},{1,17},{2,18},{3,19},{4,20},{5,21},{6,22},{7,23},{8,24},{9,... | collective-permute-start | bytes 172040 | tf_op jit(solution)/shard_map/ppermute | solution.py:29
  60.7 5.6 %collective-permute-start.12 = (bf16[8,7168]{1,0:T(8,128)(2,1)S(1)}, bf16[8,7168]{1,0:T(8,128)(2,1)S(1)}, u32[]{:S(2)}, u32[]{:S(2)}) collective-permute-start(bf16[8,7168]{1,0:T(8,128)(2,1)S(1)} %pad_maximum_fusion.4), channel_id=1, source_target_pairs={{0,4},{1,9},{2,6},{3,11},{4,0},{5,13},{6,2},{7,15},{8,12},{9,1},{1... | collective-permute-start | bytes 344072 | tf_op jit(solution)/shard_map/ppermute | solution.py:29
  66.3 7.2 %collective-permute-start.13 = (bf16[16,7168]{1,0:T(8,128)(2,1)S(1)}, bf16[16,7168]{1,0:T(8,128)(2,1)S(1)}, u32[]{:S(2)}, u32[]{:S(2)}) collective-permute-start(bf16[16,7168]{1,0:T(8,128)(2,1)S(1)} %pad_maximum_fusion.3), channel_id=1, source_target_pairs={{0,2},{1,5},{2,0},{3,7},{4,6},{5,1},{6,4},{7,3},{8,10},{9,13},{10,... | collective-permute-start | bytes 688136 | tf_op jit(solution)/shard_map/ppermute | solution.py:29
  73.6 1.9 %collective-permute-start.14 = (bf16[32,7168]{1,0:T(8,128)(2,1)S(1)}, bf16[32,7168]{1,0:T(8,128)(2,1)S(1)}, u32[]{:S(2)}, u32[]{:S(2)}) collective-permute-start(bf16[32,7168]{1,0:T(8,128)(2,1)S(1)} %pad_maximum_fusion.1.own_ref), channel_id=1, source_target_pairs={{0,1},{1,0},{2,3},{3,2},{4,5},{5,4},{6,7},{7,6},{8,9},{9,8},{10,11... | collective-permute-start | bytes 1376264 | tf_op jit(solution)/shard_map/ppermute | solution.py:29
  75.5 2.0 %copy-start.1 = (bf16[1,7168,256]{2,1,0:T(8,128)(2,1)S(1)}, bf16[1,7168,256]{2,1,0:T(8,128)(2,1)}, u32[]{:S(2)}) copy-start(bf16[1,7168,256]{2,1,0:T(8,128)(2,1)} %gate_ref.3) | copy-start | bytes 11010052
  77.6 2.0 %copy-start.3 = (bf16[1,7168,256]{2,1,0:T(8,128)(2,1)S(1)}, bf16[1,7168,256]{2,1,0:T(8,128)(2,1)}, u32[]{:S(2)}) copy-start(bf16[1,7168,256]{2,1,0:T(8,128)(2,1)} %up_ref.3) | copy-start | bytes 11010052
  79.6 2.0 %copy-start.5 = (bf16[1,256,7168]{2,1,0:T(8,128)(2,1)S(1)}, bf16[1,256,7168]{2,1,0:T(8,128)(2,1)}, u32[]{:S(2)}) copy-start(bf16[1,256,7168]{2,1,0:T(8,128)(2,1)} %down_ref.3) | copy-start | bytes 11010052
  84.0 1.9 %collective-permute-start.15 = (bf16[32,7168]{1,0:T(8,128)(2,1)S(1)}, bf16[32,7168]{1,0:T(8,128)(2,1)S(1)}, u32[]{:S(2)}, u32[]{:S(2)}) collective-permute-start(bf16[32,7168]{1,0:T(8,128)(2,1)S(1)} %get-tuple-element.12), channel_id=1, source_target_pairs={{0,1},{1,0},{2,3},{3,2},{4,5},{5,4},{6,7},{7,6},{8,9},{9,8},{10,11... | collective-permute-start | bytes 1376264 | tf_op jit(solution)/shard_map/ppermute | solution.py:29
  86.0 6.1 %collective-permute-start.16 = (bf16[16,7168]{1,0:T(8,128)(2,1)S(1)}, bf16[16,7168]{1,0:T(8,128)(2,1)S(1)}, u32[]{:S(2)}, u32[]{:S(2)}) collective-permute-start(bf16[16,7168]{1,0:T(8,128)(2,1)S(1)} %slice.93), channel_id=1, source_target_pairs={{0,2},{1,5},{2,0},{3,7},{4,6},{5,1},{6,4},{7,3},{8,10},{9,13},{10,... | collective-permute-start | bytes 688136 | tf_op jit(solution)/shard_map/ppermute | solution.py:29
  92.2 5.0 %collective-permute-start.17 = (bf16[8,7168]{1,0:T(8,128)(2,1)S(1)}, bf16[8,7168]{1,0:T(8,128)(2,1)S(1)}, u32[]{:S(2)}, u32[]{:S(2)}) collective-permute-start(bf16[8,7168]{1,0:T(8,128)(2,1)S(1)} %slice.95), channel_id=1, source_target_pairs={{0,4},{1,9},{2,6},{3,11},{4,0},{5,13},{6,2},{7,15},{8,12},{9,1},{1... | collective-permute-start | bytes 344072 | tf_op jit(solution)/shard_map/ppermute | solution.py:29
  93.6 7.6 %collective-permute-start.10 = (bf16[4,7168]{1,0:T(4,128)(2,1)S(1)}, bf16[4,7168]{1,0:T(4,128)(2,1)S(1)}, u32[]{:S(2)}, u32[]{:S(2)}) collective-permute-start(bf16[4,7168]{1,0:T(4,128)(2,1)S(1)} %collective-permute-done.9), channel_id=1, source_target_pairs={{0,16},{1,17},{2,18},{3,19},{4,20},{5,21},{6,22},{7,23},{8,24},{9,... | collective-permute-start | bytes 172040 | tf_op jit(solution)/shard_map/ppermute | solution.py:29
  97.3 4.6 %collective-permute-start.18 = (bf16[4,7168]{1,0:T(4,128)(2,1)S(1)}, bf16[4,7168]{1,0:T(4,128)(2,1)S(1)}, u32[]{:S(2)}, u32[]{:S(2)}) collective-permute-start(bf16[4,7168]{1,0:T(4,128)(2,1)S(1)} %get-tuple-element.13), channel_id=1, source_target_pairs={{0,16},{1,17},{2,18},{3,19},{4,20},{5,21},{6,22},{7,23},{8,24},{9,... | collective-permute-start | bytes 172040 | tf_op jit(solution)/shard_map/ppermute | solution.py:29
  98.3 6.0 %collective-permute-start.19 = (bf16[4,7168]{1,0:T(4,128)(2,1)S(1)}, bf16[4,7168]{1,0:T(4,128)(2,1)S(1)}, u32[]{:S(2)}, u32[]{:S(2)}) collective-permute-start(bf16[4,7168]{1,0:T(4,128)(2,1)S(1)} %get-tuple-element.14), channel_id=1, source_target_pairs={{0,24},{1,19},{2,26},{3,17},{4,28},{5,23},{6,30},{7,21},{8,16},{9,... | collective-permute-start | bytes 172040 | tf_op jit(solution)/shard_map/ppermute | solution.py:29

commit v4 on v3

v4 whole, which is shorter than its diff:
```python
import jax
import jax.numpy as jnp
from jax import lax
from jax.experimental import pallas as pl
from jax.experimental.pallas import tpu as pltpu
from jax.sharding import PartitionSpec as P

GROUP = 4
LANES = 128
CHUNK = 1024
VMEM_LIMIT = 24 * 1024 * 1024


def exchange(value, flip, hop):
    segments, owners = lax.axis_size("segment"), lax.axis_size("expert")
    if flip == 0 and hop % segments == 0:
        return value
    pairs = []
    for seg in range(segments):
        for own in range(owners):
            target = (seg + hop) % segments * owners + (own ^ flip)
            pairs.append((seg * owners + own, target))
    return lax.ppermute(value, ("segment", "expert"), pairs)


def load_kernel(gate_ref, up_ref, down_ref, gate_out, up_out, down_out, sems):
    copies = [
        pltpu.make_async_copy(source, target, sems.at[place])
        for place, (source, target) in enumerate(((gate_ref, gate_out), (up_ref, up_out), (down_ref, down_out)))
    ]
    for copy in copies:
        copy.start()
    for copy in copies:
        copy.wait()


def load(weights):
    return pl.pallas_call(
        load_kernel,
        out_shape=[pltpu.VMEM(w.shape, w.dtype) for w in weights],
        in_specs=[pl.BlockSpec(memory_space=pltpu.HBM)] * 3,
        out_specs=[pl.BlockSpec(memory_space=pltpu.VMEM)] * 3,
        scratch_shapes=[pltpu.SemaphoreType.DMA((3,))],
        compiler_params=pltpu.CompilerParams(vmem_limit_bytes=VMEM_LIMIT),
        cost_estimate=pl.CostEstimate(
            flops=0, bytes_accessed=sum(2 * w.size for w in weights), transcendentals=0
        ),
    )(*[pltpu.with_memory_space_constraint(w, pltpu.HBM) for w in weights])


def mlp_kernel(own_ref, far_ref, gain_ref, gate_ref, up_ref, down_ref, own_out, far_out, rows_ref):
    half = own_ref.shape[0]
    dim = gate_ref.shape[1]
    for part, ref in enumerate((own_ref, far_ref)):
        square = jnp.zeros((half, LANES), jnp.float32)
        for start in range(0, dim, LANES):
            piece = ref[:, start:start + LANES].astype(jnp.float32)
            square += piece * piece
        inv = lax.rsqrt(jnp.sum(square, axis=1, keepdims=True) / dim + 1e-06)
        for start in range(0, dim, CHUNK):
            piece = ref[:, start:start + CHUNK].astype(jnp.float32)
            scaled = piece * inv * gain_ref[:, start:start + CHUNK]
            rows_ref[part * half:(part + 1) * half, start:start + CHUNK] = scaled.astype(jnp.bfloat16)
    gated = jnp.zeros((2 * half, gate_ref.shape[2]), jnp.float32)
    up_part = jnp.zeros((2 * half, gate_ref.shape[2]), jnp.float32)
    for start in range(0, dim, CHUNK):
        rows = rows_ref[:, start:start + CHUNK]
        gated += jnp.dot(rows, gate_ref[0, start:start + CHUNK, :], preferred_element_type=jnp.float32)
        up_part += jnp.dot(rows, up_ref[0, start:start + CHUNK, :], preferred_element_type=jnp.float32)
    inner = (gated / (1.0 + jnp.exp(-gated)) * up_part).astype(jnp.bfloat16)
    for start in range(0, dim, CHUNK):
        terms = jnp.dot(inner, down_ref[0, :, start:start + CHUNK], preferred_element_type=jnp.float32)
        own_out[:, start:start + CHUNK] = terms[:half].astype(jnp.bfloat16)
        far_out[:, start:start + CHUNK] = terms[half:].astype(jnp.bfloat16)


def mlp(own, far, gain, gate, up, down):
    half, dim = own.shape
    vmem = pl.BlockSpec(memory_space=pltpu.VMEM)
    gate, up, down = [pltpu.with_memory_space_constraint(w, pltpu.VMEM) for w in (gate, up, down)]
    return pl.pallas_call(
        mlp_kernel,
        out_shape=[jax.ShapeDtypeStruct((half, dim), jnp.bfloat16)] * 2,
        in_specs=[vmem] * 6,
        out_specs=[vmem] * 2,
        scratch_shapes=[pltpu.VMEM((2 * half, dim), jnp.bfloat16)],
        compiler_params=pltpu.CompilerParams(vmem_limit_bytes=VMEM_LIMIT),
        cost_estimate=pl.CostEstimate(
            flops=12 * half * dim * gate.shape[2], bytes_accessed=6 * dim * gate.shape[2], transcendentals=0
        ),
    )(own, far, gain, gate, up, down)


def on_device(states, routing, route_weight, norm_gain, gate_proj, up_proj, down_proj):
    owners = lax.axis_size("expert")
    experts = owners // GROUP
    row_dev = states.shape[1]
    passes_count = routing.shape[1]
    flips = range(0, owners, 2)
    mine = lax.axis_index("expert") // GROUP
    expert_ids = jnp.arange(experts, dtype=jnp.int32)
    gate, up, down = load((gate_proj, up_proj, down_proj))

    picked = routing[0][..., None] == expert_ids
    dense = jnp.sum(jnp.where(picked, route_weight[0][..., None].astype(jnp.float32), 0.0), axis=2)
    last_dense = exchange(dense[-1].astype(jnp.bfloat16), 0, 1).astype(jnp.float32)

    current = states[0]
    for step_no in range(passes_count):
        last = step_no == passes_count - 1
        hop, out_hop = int(step_no > 0), int(last)
        blocks = [exchange(current, flip, hop) for flip in flips]
        own = jnp.concatenate(blocks, axis=0)
        if step_no == 0:
            own, gate, up, down = lax.optimization_barrier((own, gate, up, down))
        far = exchange(own, 1, 0)
        kept, sent = mlp(own, far, norm_gain, gate, up, down)
        chip = kept.astype(jnp.float32) + exchange(sent, 1, 0).astype(jnp.float32)
        chip = chip.astype(jnp.bfloat16)

        total = exchange(current, 0, hop + out_hop).astype(jnp.float32)
        weights = last_dense if last else dense[step_no]
        for place, flip in enumerate(flips):
            part = exchange(chip[place * row_dev:(place + 1) * row_dev], flip, out_hop).astype(jnp.float32)
            here = expert_ids == (mine ^ (flip // GROUP))
            weight = jnp.sum(jnp.where(here, weights, 0.0), axis=1, keepdims=True)
            total = total + jnp.where(weight > 0.0, weight * part, 0.0)
        current = total.astype(jnp.bfloat16)
    return current[None]


def solution(mesh):
    return jax.shard_map(
        on_device,
        mesh=mesh,
        in_specs=(
            P("segment", "expert", None),
            P("segment", None, "expert", None),
            P("segment", None, "expert", None),
            P("segment", None),
            P("segment", None, "expert"),
            P("segment", None, "expert"),
            P("segment", "expert", None),
        ),
        out_specs=P("segment", "expert", None),
        check_vma=False,
    )
```

time: 106 us -> 107 us (level)
  waiting for transfers between devices: 51.6 us -> 20.2 us
  starting transfers between devices: 29.6 us -> 56.8 us
  local copies, waits for them, and re-layouts: 13.2 us -> 18.7 us
  Pallas kernels: 4.75 us -> 8.93 us
  other arithmetic: 5.48 us -> 1.81 us
    ppermute x20 -> x35, waiting for transfers between devices: 51.6 us -> 20.2 us  [exchange(): return lax.ppermute(value, ('segment', 'expert'), pairs)]
    ppermute x20 -> x35, starting transfers between devices: 29.6 us -> 56.8 us  [exchange(): return lax.ppermute(value, ('segment', 'expert'), pairs)]
    unnamed x18 -> x26, local copies, waits for them, and re-layouts: 13 us -> 17.8 us
    pallas_call x0 -> x1, Pallas kernels: none -> 4.23 us  [load(): pl.pallas_call(load_kernel, out_shape=[pltpu.VMEM(w.shape, w.dtype) for w...]
    concatenate x6 -> x0, other arithmetic: 2.97 us -> none  [the longest x4 2.03 us: on_device(): own = jnp.concatenate([own, exchange(own, flips, 0)], axis=0)]
  transfers between devices with their start and end apart: 20 -> 35, of which waited for: 18 -> 10; matrix products, arithmetic and copies ran while one was open for 2% -> 0% of each run, Pallas kernels for 0% -> 6%
where the time goes in v4:
time: 107 us
  starting transfers between devices  56.8 us (53%)
  waiting for transfers between devices  20.2 us (19%)
  local copies, waits for them, and re-layouts  18.7 us (17%)
  Pallas kernels  8.93 us (8%)
  other arithmetic  1.81 us (2%)
    ppermute x35, starting transfers between devices, exchange(): return lax.ppermute(value, ('segment', 'expert'), pairs)  56.8 us
    ppermute x35, waiting for transfers between devices, exchange(): return lax.ppermute(value, ('segment', 'expert'), pairs)  20.2 us
    unnamed x26, local copies, waits for them, and re-layouts  17.8 us
    pallas_call x2, Pallas kernels, mlp(): pl.pallas_call(mlp_kernel, out_shape=[jax.ShapeDtypeStruct((half, dim), j...  4.71 us
    pallas_call x1, Pallas kernels, load(): pl.pallas_call(load_kernel, out_shape=[pltpu.VMEM(w.shape, w.dtype) for w...  4.23 us
  transfers between devices with their start and end apart: 35, of which 10 were waited for; matrix products, arithmetic and copies ran while one was open for 0% of the time, Pallas kernels for 6%

profile of v4, /device:TPU:0, one launch (start us, length us, event | category | flops | bytes accessed | tf_op | source)
XLA Modules:
  0.0 106.6 jit_solution(11817675201457689488)
XLA Ops:
  0.0 3.0 %collective-permute-start = (bf16[4,7168]{1,0:T(4,128)(2,1)}, bf16[4,7168]{1,0:T(4,128)(2,1)S(1)}, u32[]{:S(2)}, u32[]{:S(2)}) collective-permute-start(bf16[4,7168]{1,0:T(4,128)(2,1)} %bitcast.20), channel_id=1, source_target_pairs={{0,2},{1,3},{2,0},{3,1},{4,6},{5,7},{6,4},{7,5},{8,10},{9,11},{10,... | collective-permute-start | bytes 172040 | tf_op jit(solution)/shard_map/ppermute | solution.py:23
  3.1 1.6 %collective-permute-start.1 = (bf16[4,7168]{1,0:T(4,128)(2,1)}, bf16[4,7168]{1,0:T(4,128)(2,1)S(1)}, u32[]{:S(2)}, u32[]{:S(2)}) collective-permute-start(bf16[4,7168]{1,0:T(4,128)(2,1)} %bitcast.21), channel_id=1, source_target_pairs={{0,4},{1,5},{2,6},{3,7},{4,0},{5,1},{6,2},{7,3},{8,12},{9,13},{10,... | collective-permute-start | bytes 172040 | tf_op jit(solution)/shard_map/ppermute | solution.py:23
  4.6 3.0 %collective-permute-start.3 = (bf16[4,7168]{1,0:T(4,128)(2,1)}, bf16[4,7168]{1,0:T(4,128)(2,1)S(1)}, u32[]{:S(2)}, u32[]{:S(2)}) collective-permute-start(bf16[4,7168]{1,0:T(4,128)(2,1)} %bitcast.23), channel_id=1, source_target_pairs={{0,8},{1,9},{2,10},{3,11},{4,12},{5,13},{6,14},{7,15},{8,0},{9,1},... | collective-permute-start | bytes 172040 | tf_op jit(solution)/shard_map/ppermute | solution.py:23
  7.6 1.3 %collective-permute-start.4 = (bf16[4,7168]{1,0:T(4,128)(2,1)}, bf16[4,7168]{1,0:T(4,128)(2,1)S(1)}, u32[]{:S(2)}, u32[]{:S(2)}) collective-permute-start(bf16[4,7168]{1,0:T(4,128)(2,1)} %bitcast.24), channel_id=1, source_target_pairs={{0,10},{1,11},{2,8},{3,9},{4,14},{5,15},{6,12},{7,13},{8,2},{9,3},... | collective-permute-start | bytes 172040 | tf_op jit(solution)/shard_map/ppermute | solution.py:23
  8.9 3.6 %collective-permute-start.5 = (bf16[4,7168]{1,0:T(4,128)(2,1)}, bf16[4,7168]{1,0:T(4,128)(2,1)S(1)}, u32[]{:S(2)}, u32[]{:S(2)}) collective-permute-start(bf16[4,7168]{1,0:T(4,128)(2,1)} %bitcast.25), channel_id=1, source_target_pairs={{0,12},{1,13},{2,14},{3,15},{4,8},{5,9},{6,10},{7,11},{8,4},{9,5},... | collective-permute-start | bytes 172040 | tf_op jit(solution)/shard_map/ppermute | solution.py:23
  12.5 4.2 %shard_map.73 = (bf16[1,7168,256]{2,1,0:T(8,128)(2,1)S(1)}, bf16[1,7168,256]{2,1,0:T(8,128)(2,1)S(1)}, bf16[1,256,7168]{2,1,0:T(8,128)(2,1)S(1)}) custom-call(bf16[1,7168,256]{2,1,0:T(8,128)(2,1)} %gate_ref.1, bf16[1,7168,256]{2,1,0:T(8,128)(2,1)} %up_ref.1, bf16[1,256,7168]{2,1,0:T(8,128)(2,1)} %down_ref.1), custom_call_target="tpu_custom_call" | custom-call | bytes 11010048 | tf_op jit(solution)/shard_map/pallas_call | solution.py:38
  16.8 1.8 %copy-done = bf16[1,7168,256]{2,1,0:T(8,128)(2,1)} copy-done((bf16[1,7168,256]{2,1,0:T(8,128)(2,1)}, bf16[1,7168,256]{2,1,0:T(8,128)(2,1)S(1)}, u32[]{:S(2)}) %copy-start) | copy-done | bytes 3670040
  18.5 1.8 %copy-done.3 = bf16[1,7168,256]{2,1,0:T(8,128)(2,1)} copy-done((bf16[1,7168,256]{2,1,0:T(8,128)(2,1)}, bf16[1,7168,256]{2,1,0:T(8,128)(2,1)S(1)}, u32[]{:S(2)}) %copy-start.3) | copy-done | bytes 3670040
  20.4 1.9 %copy-done.6 = bf16[1,256,7168]{2,1,0:T(8,128)(2,1)} copy-done((bf16[1,256,7168]{2,1,0:T(8,128)(2,1)}, bf16[1,256,7168]{2,1,0:T(8,128)(2,1)S(1)}, u32[]{:S(2)}) %copy-start.6) | copy-done | bytes 3670040
  22.3 0.3 concatenate.6.own_ref
  22.6 0.1 collective-permute-start.7
  22.8 0.1 select_reduce_fusion
  22.8 1.7 %collective-permute-start.16 = (bf16[4,4]{1,0:T(4,128)(2,1)S(1)}, bf16[4,4]{1,0:T(4,128)(2,1)S(1)}, u32[]{:S(2)}, u32[]{:S(2)}) collective-permute-start(bf16[4,4]{1,0:T(4,128)(2,1)S(1)} %fusion.5), channel_id=1, source_target_pairs={{0,16},{1,17},{2,18},{3,19},{4,20},{5,21},{6,22},{7,23},{8,24},{9,... | collective-permute-start | bytes 104 | tf_op jit(solution)/shard_map/ppermute | solution.py:23
  24.6 2.0 %copy-done.1 = bf16[1,7168,256]{2,1,0:T(8,128)(2,1)S(1)} copy-done((bf16[1,7168,256]{2,1,0:T(8,128)(2,1)S(1)}, bf16[1,7168,256]{2,1,0:T(8,128)(2,1)}, u32[]{:S(2)}) %copy-start.1) | copy-done | bytes 3670040
  26.6 2.0 %copy-done.4 = bf16[1,7168,256]{2,1,0:T(8,128)(2,1)S(1)} copy-done((bf16[1,7168,256]{2,1,0:T(8,128)(2,1)S(1)}, bf16[1,7168,256]{2,1,0:T(8,128)(2,1)}, u32[]{:S(2)}) %copy-start.4) | copy-done | bytes 3670040
  28.6 2.0 %copy-done.7 = bf16[1,256,7168]{2,1,0:T(8,128)(2,1)S(1)} copy-done((bf16[1,256,7168]{2,1,0:T(8,128)(2,1)S(1)}, bf16[1,256,7168]{2,1,0:T(8,128)(2,1)}, u32[]{:S(2)}) %copy-start.7) | copy-done | bytes 3670040
  30.7 2.4 %shard_map.74 = (bf16[32,7168]{1,0:T(8,128)(2,1)S(1)}, bf16[32,7168]{1,0:T(8,128)(2,1)S(1)}) custom-call(bf16[32,7168]{1,0:T(8,128)(2,1)S(1)} %concatenate.6.own_ref, bf16[32,7168]{1,0:T(8,128)(2,1)S(1)} %collective-permute-done.7.far_ref, f32[1,7168]{1,0:T(1,128)S(1)} %copy-done.9, bf16[1,7168,256]{2,1,0:T(8,128)(2,1)S(1)} %copy-done.1, ...), custom_call_target="tpu_custom_call" | custom-call | flops 704643072 | bytes 11010048 | tf_op jit(solution)/shard_map/pallas_call | solution.py:81
  33.0 0.3 collective-permute-start.8
  33.3 0.2 fusion.1
  33.5 1.4 %collective-permute-done.8 = bf16[32,7168]{1,0:T(8,128)(2,1)S(1)} collective-permute-done((bf16[32,7168]{1,0:T(8,128)(2,1)S(1)}, bf16[32,7168]{1,0:T(8,128)(2,1)S(1)}, u32[]{:S(2)}, u32[]{:S(2)}) %collective-permute-start.8) | collective-permute-done | bytes 458784 | tf_op jit(solution)/shard_map/ppermute | solution.py:23
  34.9 0.1 add_convert_fusion.1
  35.0 0.1 fusion.7
  35.3 3.1 %collective-permute-start.11 = (bf16[4,7168]{1,0:T(4,128)(2,1)S(1)}, bf16[4,7168]{1,0:T(4,128)(2,1)S(1)}, u32[]{:S(2)}, u32[]{:S(2)}) collective-permute-start(bf16[4,7168]{1,0:T(4,128)(2,1)S(1)} %get-tuple-element.52), channel_id=1, source_target_pairs={{0,6},{1,7},{2,4},{3,5},{4,2},{5,3},{6,0},{7,1},{8,14},{9,15},{10,... | collective-permute-start | bytes 172040 | tf_op jit(solution)/shard_map/ppermute | solution.py:23
  38.4 2.2 %collective-permute-start.12 = (bf16[4,7168]{1,0:T(4,128)(2,1)S(1)}, bf16[4,7168]{1,0:T(4,128)(2,1)S(1)}, u32[]{:S(2)}, u32[]{:S(2)}) collective-permute-start(bf16[4,7168]{1,0:T(4,128)(2,1)S(1)} %get-tuple-element.51), channel_id=1, source_target_pairs={{0,8},{1,9},{2,10},{3,11},{4,12},{5,13},{6,14},{7,15},{8,0},{9,1},... | collective-permute-start | bytes 172040 | tf_op jit(solution)/shard_map/ppermute | solution.py:23
  40.6 0.5 collective-permute-start.13
  41.1 3.7 %collective-permute-start.14 = (bf16[4,7168]{1,0:T(4,128)(2,1)S(1)}, bf16[4,7168]{1,0:T(4,128)(2,1)S(1)}, u32[]{:S(2)}, u32[]{:S(2)}) collective-permute-start(bf16[4,7168]{1,0:T(4,128)(2,1)S(1)} %get-tuple-element.49), channel_id=1, source_target_pairs={{0,12},{1,13},{2,14},{3,15},{4,8},{5,9},{6,10},{7,11},{8,4},{9,5},... | collective-permute-start | bytes 172040 | tf_op jit(solution)/shard_map/ppermute | solution.py:23
  44.8 1.2 %collective-permute-start.15 = (bf16[4,7168]{1,0:T(4,128)(2,1)S(1)}, bf16[4,7168]{1,0:T(4,128)(2,1)S(1)}, u32[]{:S(2)}, u32[]{:S(2)}) collective-permute-start(bf16[4,7168]{1,0:T(4,128)(2,1)S(1)} %get-tuple-element.48), channel_id=1, source_target_pairs={{0,14},{1,15},{2,12},{3,13},{4,10},{5,11},{6,8},{7,9},{8,6},{9,7},... | collective-permute-start | bytes 172040 | tf_op jit(solution)/shard_map/ppermute | solution.py:23
  46.0 0.4 collective-permute-start.9
  46.4 3.7 %collective-permute-done.13 = bf16[4,7168]{1,0:T(4,128)(2,1)S(1)} collective-permute-done((bf16[4,7168]{1,0:T(4,128)(2,1)S(1)}, bf16[4,7168]{1,0:T(4,128)(2,1)S(1)}, u32[]{:S(2)}, u32[]{:S(2)}) %collective-permute-start.13) | collective-permute-done | bytes 57376 | tf_op jit(solution)/shard_map/ppermute | solution.py:23
  50.1 1.7 %collective-permute-done.15 = bf16[4,7168]{1,0:T(4,128)(2,1)S(1)} collective-permute-done((bf16[4,7168]{1,0:T(4,128)(2,1)S(1)}, bf16[4,7168]{1,0:T(4,128)(2,1)S(1)}, u32[]{:S(2)}, u32[]{:S(2)}) %collective-permute-start.15) | collective-permute-done | bytes 57376 | tf_op jit(solution)/shard_map/ppermute | solution.py:23
  51.8 0.3 add_convert_fusion.3
  52.1 1.6 %collective-permute-start.17 = (bf16[4,7168]{1,0:T(4,128)(2,1)S(1)}, bf16[4,7168]{1,0:T(4,128)(2,1)S(1)}, u32[]{:S(2)}, u32[]{:S(2)}) collective-permute-start(bf16[4,7168]{1,0:T(4,128)(2,1)S(1)} %add_convert_fusion.3), channel_id=1, source_target_pairs={{0,16},{1,17},{2,18},{3,19},{4,20},{5,21},{6,22},{7,23},{8,24},{9,... | collective-permute-start | bytes 172040 | tf_op jit(solution)/shard_map/ppermute | solution.py:23
  53.7 1.5 %collective-permute-start.18 = (bf16[4,7168]{1,0:T(4,128)(2,1)S(1)}, bf16[4,7168]{1,0:T(4,128)(2,1)S(1)}, u32[]{:S(2)}, u32[]{:S(2)}) collective-permute-start(bf16[4,7168]{1,0:T(4,128)(2,1)S(1)} %add_convert_fusion.3), channel_id=1, source_target_pairs={{0,18},{1,19},{2,16},{3,17},{4,22},{5,23},{6,20},{7,21},{8,26},{9,... | collective-permute-start | bytes 172040 | tf_op jit(solution)/shard_map/ppermute | solution.py:23
  55.2 1.7 %collective-permute-start.19 = (bf16[4,7168]{1,0:T(4,128)(2,1)S(1)}, bf16[4,7168]{1,0:T(4,128)(2,1)S(1)}, u32[]{:S(2)}, u32[]{:S(2)}) collective-permute-start(bf16[4,7168]{1,0:T(4,128)(2,1)S(1)} %add_convert_fusion.3), channel_id=1, source_target_pairs={{0,20},{1,21},{2,22},{3,23},{4,16},{5,17},{6,18},{7,19},{8,28},{9,... | collective-permute-start | bytes 172040 | tf_op jit(solution)/shard_map/ppermute | solution.py:23
  56.9 1.2 %collective-permute-start.20 = (bf16[4,7168]{1,0:T(4,128)(2,1)S(1)}, bf16[4,7168]{1,0:T(4,128)(2,1)S(1)}, u32[]{:S(2)}, u32[]{:S(2)}) collective-permute-start(bf16[4,7168]{1,0:T(4,128)(2,1)S(1)} %add_convert_fusion.3), channel_id=1, source_target_pairs={{0,22},{1,23},{2,20},{3,21},{4,18},{5,19},{6,16},{7,17},{8,30},{9,... | collective-permute-start | bytes 172040 | tf_op jit(solution)/shard_map/ppermute | solution.py:23
  58.1 2.9 %collective-permute-start.21 = (bf16[4,7168]{1,0:T(4,128)(2,1)S(1)}, bf16[4,7168]{1,0:T(4,128)(2,1)S(1)}, u32[]{:S(2)}, u32[]{:S(2)}) collective-permute-start(bf16[4,7168]{1,0:T(4,128)(2,1)S(1)} %add_convert_fusion.3), channel_id=1, source_target_pairs={{0,24},{1,25},{2,26},{3,27},{4,28},{5,29},{6,30},{7,31},{8,16},{9,... | collective-permute-start | bytes 172040 | tf_op jit(solution)/shard_map/ppermute | solution.py:23
  60.9 1.9 %collective-permute-start.22 = (bf16[4,7168]{1,0:T(4,128)(2,1)S(1)}, bf16[4,7168]{1,0:T(4,128)(2,1)S(1)}, u32[]{:S(2)}, u32[]{:S(2)}) collective-permute-start(bf16[4,7168]{1,0:T(4,128)(2,1)S(1)} %add_convert_fusion.3), channel_id=1, source_target_pairs={{0,26},{1,27},{2,24},{3,25},{4,30},{5,31},{6,28},{7,29},{8,18},{9,... | collective-permute-start | bytes 172040 | tf_op jit(solution)/shard_map/ppermute | solution.py:23
  62.8 1.9 %collective-permute-start.23 = (bf16[4,7168]{1,0:T(4,128)(2,1)S(1)}, bf16[4,7168]{1,0:T(4,128)(2,1)S(1)}, u32[]{:S(2)}, u32[]{:S(2)}) collective-permute-start(bf16[4,7168]{1,0:T(4,128)(2,1)S(1)} %add_convert_fusion.3), channel_id=1, source_target_pairs={{0,28},{1,29},{2,30},{3,31},{4,24},{5,25},{6,26},{7,27},{8,20},{9,... | collective-permute-start | bytes 172040 | tf_op jit(solution)/shard_map/ppermute | solution.py:23
  64.8 2.7 %collective-permute-start.24 = (bf16[4,7168]{1,0:T(4,128)(2,1)S(1)}, bf16[4,7168]{1,0:T(4,128)(2,1)S(1)}, u32[]{:S(2)}, u32[]{:S(2)}) collective-permute-start(bf16[4,7168]{1,0:T(4,128)(2,1)S(1)} %add_convert_fusion.3), channel_id=1, source_target_pairs={{0,30},{1,31},{2,28},{3,29},{4,26},{5,27},{6,24},{7,25},{8,22},{9,... | collective-permute-start | bytes 172040 | tf_op jit(solution)/shard_map/ppermute | solution.py:23
  67.5 2.8 %collective-permute-done.22 = bf16[4,7168]{1,0:T(4,128)(2,1)S(1)} collective-permute-done((bf16[4,7168]{1,0:T(4,128)(2,1)S(1)}, bf16[4,7168]{1,0:T(4,128)(2,1)S(1)}, u32[]{:S(2)}, u32[]{:S(2)}) %collective-permute-start.22) | collective-permute-done | bytes 57376 | tf_op jit(solution)/shard_map/ppermute | solution.py:23
  70.3 2.2 %collective-permute-done.24 = bf16[4,7168]{1,0:T(4,128)(2,1)S(1)} collective-permute-done((bf16[4,7168]{1,0:T(4,128)(2,1)S(1)}, bf16[4,7168]{1,0:T(4,128)(2,1)S(1)}, u32[]{:S(2)}, u32[]{:S(2)}) %collective-permute-start.24) | collective-permute-done | bytes 57376 | tf_op jit(solution)/shard_map/ppermute | solution.py:23
  72.6 0.3 concatenate.7.own_ref
  72.9 0.1 collective-permute-start.25
  72.9 1.8 %collective-permute-done.25.far_ref = bf16[32,7168]{1,0:T(8,128)(2,1)S(1)} collective-permute-done((bf16[32,7168]{1,0:T(8,128)(2,1)S(1)}, bf16[32,7168]{1,0:T(8,128)(2,1)S(1)}, u32[]{:S(2)}, u32[]{:S(2)}) %collective-permute-start.25) | collective-permute-done | bytes 458784 | tf_op jit(solution)/shard_map/ppermute | solution.py:23
  74.8 2.0 %copy-done.2 = bf16[1,7168,256]{2,1,0:T(8,128)(2,1)S(1)} copy-done((bf16[1,7168,256]{2,1,0:T(8,128)(2,1)S(1)}, bf16[1,7168,256]{2,1,0:T(8,128)(2,1)}, u32[]{:S(2)}) %copy-start.2) | copy-done | bytes 3670040
  76.8 2.0 %copy-done.5 = bf16[1,7168,256]{2,1,0:T(8,128)(2,1)S(1)} copy-done((bf16[1,7168,256]{2,1,0:T(8,128)(2,1)S(1)}, bf16[1,7168,256]{2,1,0:T(8,128)(2,1)}, u32[]{:S(2)}) %copy-start.5) | copy-done | bytes 3670040
  78.8 2.0 %copy-done.8 = bf16[1,256,7168]{2,1,0:T(8,128)(2,1)S(1)} copy-done((bf16[1,256,7168]{2,1,0:T(8,128)(2,1)S(1)}, bf16[1,256,7168]{2,1,0:T(8,128)(2,1)}, u32[]{:S(2)}) %copy-start.8) | copy-done | bytes 3670040
  80.9 2.4 %shard_map.75 = (bf16[32,7168]{1,0:T(8,128)(2,1)S(1)}, bf16[32,7168]{1,0:T(8,128)(2,1)S(1)}) custom-call(bf16[32,7168]{1,0:T(8,128)(2,1)S(1)} %concatenate.7.own_ref, bf16[32,7168]{1,0:T(8,128)(2,1)S(1)} %collective-permute-done.25.far_ref, f32[1,7168]{1,0:T(1,128)S(1)} %copy-done.9, bf16[1,7168,256]{2,1,0:T(8,128)(2,1)S(1)} %copy-done.2, ...), custom_call_target="tpu_custom_call" | custom-call | flops 704643072 | bytes 11010048 | tf_op jit(solution)/shard_map/pallas_call | solution.py:81
  83.2 0.2 collective-permute-start.26
  83.4 1.7 %collective-permute-done.26 = bf16[32,7168]{1,0:T(8,128)(2,1)S(1)} collective-permute-done((bf16[32,7168]{1,0:T(8,128)(2,1)S(1)}, bf16[32,7168]{1,0:T(8,128)(2,1)S(1)}, u32[]{:S(2)}, u32[]{:S(2)}) %collective-permute-start.26) | collective-permute-done | bytes 458784 | tf_op jit(solution)/shard_map/ppermute | solution.py:23
  85.1 0.1 add_convert_fusion
  85.2 0.2 fusion.6
  85.4 1.1 collective-permute-start.27
  86.4 2.0 %collective-permute-start.28 = (bf16[4,7168]{1,0:T(4,128)(2,1)S(1)}, bf16[4,7168]{1,0:T(4,128)(2,1)S(1)}, u32[]{:S(2)}, u32[]{:S(2)}) collective-permute-start(bf16[4,7168]{1,0:T(4,128)(2,1)S(1)} %get-tuple-element.46), channel_id=1, source_target_pairs={{0,18},{1,19},{2,16},{3,17},{4,22},{5,23},{6,20},{7,21},{8,26},{9,... | collective-permute-start | bytes 172040 | tf_op jit(solution)/shard_map/ppermute | solution.py:23
  88.4 0.9 collective-permute-start.29
  89.4 2.0 %collective-permute-start.30 = (bf16[4,7168]{1,0:T(4,128)(2,1)S(1)}, bf16[4,7168]{1,0:T(4,128)(2,1)S(1)}, u32[]{:S(2)}, u32[]{:S(2)}) collective-permute-start(bf16[4,7168]{1,0:T(4,128)(2,1)S(1)} %get-tuple-element.44), channel_id=1, source_target_pairs={{0,22},{1,23},{2,20},{3,21},{4,18},{5,19},{6,16},{7,17},{8,30},{9,... | collective-permute-start | bytes 172040 | tf_op jit(solution)/shard_map/ppermute | solution.py:23
  91.3 1.4 %collective-permute-start.31 = (bf16[4,7168]{1,0:T(4,128)(2,1)S(1)}, bf16[4,7168]{1,0:T(4,128)(2,1)S(1)}, u32[]{:S(2)}, u32[]{:S(2)}) collective-permute-start(bf16[4,7168]{1,0:T(4,128)(2,1)S(1)} %get-tuple-element.43), channel_id=1, source_target_pairs={{0,24},{1,25},{2,26},{3,27},{4,28},{5,29},{6,30},{7,31},{8,16},{9,... | collective-permute-start | bytes 172040 | tf_op jit(solution)/shard_map/ppermute | solution.py:23
  92.7 3.3 %collective-permute-start.32 = (bf16[4,7168]{1,0:T(4,128)(2,1)S(1)}, bf16[4,7168]{1,0:T(4,128)(2,1)S(1)}, u32[]{:S(2)}, u32[]{:S(2)}) collective-permute-start(bf16[4,7168]{1,0:T(4,128)(2,1)S(1)} %get-tuple-element.42), channel_id=1, source_target_pairs={{0,26},{1,27},{2,24},{3,25},{4,30},{5,31},{6,28},{7,29},{8,18},{9,... | collective-permute-start | bytes 172040 | tf_op jit(solution)/shard_map/ppermute | solution.py:23
  96.1 1.8 %collective-permute-start.33 = (bf16[4,7168]{1,0:T(4,128)(2,1)S(1)}, bf16[4,7168]{1,0:T(4,128)(2,1)S(1)}, u32[]{:S(2)}, u32[]{:S(2)}) collective-permute-start(bf16[4,7168]{1,0:T(4,128)(2,1)S(1)} %get-tuple-element.41), channel_id=1, source_target_pairs={{0,28},{1,29},{2,30},{3,31},{4,24},{5,25},{6,26},{7,27},{8,20},{9,... | collective-permute-start | bytes 172040 | tf_op jit(solution)/shard_map/ppermute | solution.py:23
  97.9 2.9 %collective-permute-start.34 = (bf16[4,7168]{1,0:T(4,128)(2,1)S(1)}, bf16[4,7168]{1,0:T(4,128)(2,1)S(1)}, u32[]{:S(2)}, u32[]{:S(2)}) collective-permute-start(bf16[4,7168]{1,0:T(4,128)(2,1)S(1)} %get-tuple-element.40), channel_id=1, source_target_pairs={{0,30},{1,31},{2,28},{3,29},{4,26},{5,27},{6,24},{7,25},{8,22},{9,... | collective-permute-start | bytes 172040 | tf_op jit(solution)/shard_map/ppermute | solution.py:23
  100.8 1.0 collective-permute-done.32
  101.8 1.8 %collective-permute-done.33 = bf16[4,7168]{1,0:T(4,128)(2,1)S(1)} collective-permute-done((bf16[4,7168]{1,0:T(4,128)(2,1)S(1)}, bf16[4,7168]{1,0:T(4,128)(2,1)S(1)}, u32[]{:S(2)}, u32[]{:S(2)}) %collective-permute-start.33) | collective-permute-done | bytes 57376 | tf_op jit(solution)/shard_map/ppermute | solution.py:23
  103.6 2.0 %collective-permute-done.34 = bf16[4,7168]{1,0:T(4,128)(2,1)S(1)} collective-permute-done((bf16[4,7168]{1,0:T(4,128)(2,1)S(1)}, bf16[4,7168]{1,0:T(4,128)(2,1)S(1)}, u32[]{:S(2)}, u32[]{:S(2)}) %collective-permute-start.34) | collective-permute-done | bytes 57376 | tf_op jit(solution)/shard_map/ppermute | solution.py:23
  105.7 0.9 fusion
  (55 shorter events, 0.2 us)
Async XLA Ops:
  0.0 22.3 %copy-start.10 = (bf16[1,4,7168]{2,1,0:T(4,128)(2,1)S(1)}, bf16[1,4,7168]{2,1,0:T(4,128)(2,1)}, u32[]{:S(2)}) copy-start(bf16[1,4,7168]{2,1,0:T(4,128)(2,1)} %param.7) | copy-start | bytes 172036
  0.0 22.7 %copy-start.12 = (bf16[1,2,4,2]{2,3,1,0:T(2,128)(2,1)S(1)}, bf16[1,2,4,2]{2,3,1,0:T(2,128)(2,1)}, u32[]{:S(2)}) copy-start(bf16[1,2,4,2]{2,3,1,0:T(2,128)(2,1)} %param.9) | copy-start | bytes 100
  0.0 22.7 %copy-start.11 = (s32[1,2,4,2]{2,3,1,0:T(2,128)S(1)}, s32[1,2,4,2]{2,3,1,0:T(2,128)}, u32[]{:S(2)}) copy-start(s32[1,2,4,2]{2,3,1,0:T(2,128)} %param.8) | copy-start | bytes 196
  0.0 24.5 %copy-start.9 = (f32[1,7168]{1,0:T(1,128)S(1)}, f32[1,7168]{1,0:T(1,128)}, u32[]{:S(2)}) copy-start(f32[1,7168]{1,0:T(1,128)} %gain_ref.3) | copy-start | bytes 86020
  0.0 8.9 %collective-permute-start = (bf16[4,7168]{1,0:T(4,128)(2,1)}, bf16[4,7168]{1,0:T(4,128)(2,1)S(1)}, u32[]{:S(2)}, u32[]{:S(2)}) collective-permute-start(bf16[4,7168]{1,0:T(4,128)(2,1)} %bitcast.20), channel_id=1, source_target_pairs={{0,2},{1,3},{2,0},{3,1},{4,6},{5,7},{6,4},{7,5},{8,10},{9,11},{10,... | collective-permute-start | bytes 172040 | tf_op jit(solution)/shard_map/ppermute | solution.py:23
  3.1 9.5 %collective-permute-start.1 = (bf16[4,7168]{1,0:T(4,128)(2,1)}, bf16[4,7168]{1,0:T(4,128)(2,1)S(1)}, u32[]{:S(2)}, u32[]{:S(2)}) collective-permute-start(bf16[4,7168]{1,0:T(4,128)(2,1)} %bitcast.21), channel_id=1, source_target_pairs={{0,4},{1,5},{2,6},{3,7},{4,0},{5,1},{6,2},{7,3},{8,12},{9,13},{10,... | collective-permute-start | bytes 172040 | tf_op jit(solution)/shard_map/ppermute | solution.py:23
  4.6 17.7 %collective-permute-start.2 = (bf16[4,7168]{1,0:T(4,128)(2,1)}, bf16[4,7168]{1,0:T(4,128)(2,1)S(1)}, u32[]{:S(2)}, u32[]{:S(2)}) collective-permute-start(bf16[4,7168]{1,0:T(4,128)(2,1)} %bitcast.22), channel_id=1, source_target_pairs={{0,6},{1,7},{2,4},{3,5},{4,2},{5,3},{6,0},{7,1},{8,14},{9,15},{10,... | collective-permute-start | bytes 172040 | tf_op jit(solution)/shard_map/ppermute | solution.py:23
  4.6 17.7 %collective-permute-start.3 = (bf16[4,7168]{1,0:T(4,128)(2,1)}, bf16[4,7168]{1,0:T(4,128)(2,1)S(1)}, u32[]{:S(2)}, u32[]{:S(2)}) collective-permute-start(bf16[4,7168]{1,0:T(4,128)(2,1)} %bitcast.23), channel_id=1, source_target_pairs={{0,8},{1,9},{2,10},{3,11},{4,12},{5,13},{6,14},{7,15},{8,0},{9,1},... | collective-permute-start | bytes 172040 | tf_op jit(solution)/shard_map/ppermute | solution.py:23
  7.6 14.7 %collective-permute-start.4 = (bf16[4,7168]{1,0:T(4,128)(2,1)}, bf16[4,7168]{1,0:T(4,128)(2,1)S(1)}, u32[]{:S(2)}, u32[]{:S(2)}) collective-permute-start(bf16[4,7168]{1,0:T(4,128)(2,1)} %bitcast.24), channel_id=1, source_target_pairs={{0,10},{1,11},{2,8},{3,9},{4,14},{5,15},{6,12},{7,13},{8,2},{9,3},... | collective-permute-start | bytes 172040 | tf_op jit(solution)/shard_map/ppermute | solution.py:23
  8.9 13.4 %collective-permute-start.5 = (bf16[4,7168]{1,0:T(4,128)(2,1)}, bf16[4,7168]{1,0:T(4,128)(2,1)S(1)}, u32[]{:S(2)}, u32[]{:S(2)}) collective-permute-start(bf16[4,7168]{1,0:T(4,128)(2,1)} %bitcast.25), channel_id=1, source_target_pairs={{0,12},{1,13},{2,14},{3,15},{4,8},{5,9},{6,10},{7,11},{8,4},{9,5},... | collective-permute-start | bytes 172040 | tf_op jit(solution)/shard_map/ppermute | solution.py:23
  12.5 9.8 %collective-permute-start.6 = (bf16[4,7168]{1,0:T(4,128)(2,1)}, bf16[4,7168]{1,0:T(4,128)(2,1)S(1)}, u32[]{:S(2)}, u32[]{:S(2)}) collective-permute-start(bf16[4,7168]{1,0:T(4,128)(2,1)} %bitcast.26), channel_id=1, source_target_pairs={{0,14},{1,15},{2,12},{3,13},{4,10},{5,11},{6,8},{7,9},{8,6},{9,7},... | collective-permute-start | bytes 172040 | tf_op jit(solution)/shard_map/ppermute | solution.py:23
  16.8 1.8 %copy-start = (bf16[1,7168,256]{2,1,0:T(8,128)(2,1)}, bf16[1,7168,256]{2,1,0:T(8,128)(2,1)S(1)}, u32[]{:S(2)}) copy-start(bf16[1,7168,256]{2,1,0:T(8,128)(2,1)S(1)} %get-tuple-element.20.gate_ref) | copy-start | bytes 11010052
  18.5 1.8 %copy-start.3 = (bf16[1,7168,256]{2,1,0:T(8,128)(2,1)}, bf16[1,7168,256]{2,1,0:T(8,128)(2,1)S(1)}, u32[]{:S(2)}) copy-start(bf16[1,7168,256]{2,1,0:T(8,128)(2,1)S(1)} %get-tuple-element.21.up_ref) | copy-start | bytes 11010052
  20.4 1.9 %copy-start.6 = (bf16[1,256,7168]{2,1,0:T(8,128)(2,1)}, bf16[1,256,7168]{2,1,0:T(8,128)(2,1)S(1)}, u32[]{:S(2)}) copy-start(bf16[1,256,7168]{2,1,0:T(8,128)(2,1)S(1)} %get-tuple-element.22.down_ref) | copy-start | bytes 11010052
  22.6 1.9 %collective-permute-start.7 = (bf16[32,7168]{1,0:T(8,128)(2,1)S(1)}, bf16[32,7168]{1,0:T(8,128)(2,1)S(1)}, u32[]{:S(2)}, u32[]{:S(2)}) collective-permute-start(bf16[32,7168]{1,0:T(8,128)(2,1)S(1)} %concatenate.6.own_ref), channel_id=1, source_target_pairs={{0,1},{1,0},{2,3},{3,2},{4,5},{5,4},{6,7},{7,6},{8,9},{9,8},{10,11... | collective-permute-start | bytes 1376264 | tf_op jit(solution)/shard_map/ppermute | solution.py:23
  22.8 10.5 %collective-permute-start.16 = (bf16[4,4]{1,0:T(4,128)(2,1)S(1)}, bf16[4,4]{1,0:T(4,128)(2,1)S(1)}, u32[]{:S(2)}, u32[]{:S(2)}) collective-permute-start(bf16[4,4]{1,0:T(4,128)(2,1)S(1)} %fusion.5), channel_id=1, source_target_pairs={{0,16},{1,17},{2,18},{3,19},{4,20},{5,21},{6,22},{7,23},{8,24},{9,... | collective-permute-start | bytes 104 | tf_op jit(solution)/shard_map/ppermute | solution.py:23
  24.6 2.0 %copy-start.1 = (bf16[1,7168,256]{2,1,0:T(8,128)(2,1)S(1)}, bf16[1,7168,256]{2,1,0:T(8,128)(2,1)}, u32[]{:S(2)}) copy-start(bf16[1,7168,256]{2,1,0:T(8,128)(2,1)} %copy-done) | copy-start | bytes 11010052
  26.6 2.0 %copy-start.4 = (bf16[1,7168,256]{2,1,0:T(8,128)(2,1)S(1)}, bf16[1,7168,256]{2,1,0:T(8,128)(2,1)}, u32[]{:S(2)}) copy-start(bf16[1,7168,256]{2,1,0:T(8,128)(2,1)} %copy-done.3) | copy-start | bytes 11010052
  28.6 2.0 %copy-start.7 = (bf16[1,256,7168]{2,1,0:T(8,128)(2,1)S(1)}, bf16[1,256,7168]{2,1,0:T(8,128)(2,1)}, u32[]{:S(2)}) copy-start(bf16[1,256,7168]{2,1,0:T(8,128)(2,1)} %copy-done.6) | copy-start | bytes 11010052
  33.0 1.9 %collective-permute-start.8 = (bf16[32,7168]{1,0:T(8,128)(2,1)S(1)}, bf16[32,7168]{1,0:T(8,128)(2,1)S(1)}, u32[]{:S(2)}, u32[]{:S(2)}) collective-permute-start(bf16[32,7168]{1,0:T(8,128)(2,1)S(1)} %get-tuple-element.24), channel_id=1, source_target_pairs={{0,1},{1,0},{2,3},{3,2},{4,5},{5,4},{6,7},{7,6},{8,9},{9,8},{10,11... | collective-permute-start | bytes 1376264 | tf_op jit(solution)/shard_map/ppermute | solution.py:23
  35.2 9.7 %collective-permute-start.10 = (bf16[4,7168]{1,0:T(4,128)(2,1)S(1)}, bf16[4,7168]{1,0:T(4,128)(2,1)S(1)}, u32[]{:S(2)}, u32[]{:S(2)}) collective-permute-start(bf16[4,7168]{1,0:T(4,128)(2,1)S(1)} %get-tuple-element.53), channel_id=1, source_target_pairs={{0,4},{1,5},{2,6},{3,7},{4,0},{5,1},{6,2},{7,3},{8,12},{9,13},{10,... | collective-permute-start | bytes 172040 | tf_op jit(solution)/shard_map/ppermute | solution.py:23
  35.3 10.8 %collective-permute-start.11 = (bf16[4,7168]{1,0:T(4,128)(2,1)S(1)}, bf16[4,7168]{1,0:T(4,128)(2,1)S(1)}, u32[]{:S(2)}, u32[]{:S(2)}) collective-permute-start(bf16[4,7168]{1,0:T(4,128)(2,1)S(1)} %get-tuple-element.52), channel_id=1, source_target_pairs={{0,6},{1,7},{2,4},{3,5},{4,2},{5,3},{6,0},{7,1},{8,14},{9,15},{10,... | collective-permute-start | bytes 172040 | tf_op jit(solution)/shard_map/ppermute | solution.py:23
  38.4 8.1 %collective-permute-start.12 = (bf16[4,7168]{1,0:T(4,128)(2,1)S(1)}, bf16[4,7168]{1,0:T(4,128)(2,1)S(1)}, u32[]{:S(2)}, u32[]{:S(2)}) collective-permute-start(bf16[4,7168]{1,0:T(4,128)(2,1)S(1)} %get-tuple-element.51), channel_id=1, source_target_pairs={{0,8},{1,9},{2,10},{3,11},{4,12},{5,13},{6,14},{7,15},{8,0},{9,1},... | collective-permute-start | bytes 172040 | tf_op jit(solution)/shard_map/ppermute | solution.py:23
  40.6 9.5 %collective-permute-start.13 = (bf16[4,7168]{1,0:T(4,128)(2,1)S(1)}, bf16[4,7168]{1,0:T(4,128)(2,1)S(1)}, u32[]{:S(2)}, u32[]{:S(2)}) collective-permute-start(bf16[4,7168]{1,0:T(4,128)(2,1)S(1)} %get-tuple-element.50), channel_id=1, source_target_pairs={{0,10},{1,11},{2,8},{3,9},{4,14},{5,15},{6,12},{7,13},{8,2},{9,3},... | collective-permute-start | bytes 172040 | tf_op jit(solution)/shard_map/ppermute | solution.py:23
  41.1 9.0 %collective-permute-start.14 = (bf16[4,7168]{1,0:T(4,128)(2,1)S(1)}, bf16[4,7168]{1,0:T(4,128)(2,1)S(1)}, u32[]{:S(2)}, u32[]{:S(2)}) collective-permute-start(bf16[4,7168]{1,0:T(4,128)(2,1)S(1)} %get-tuple-element.49), channel_id=1, source_target_pairs={{0,12},{1,13},{2,14},{3,15},{4,8},{5,9},{6,10},{7,11},{8,4},{9,5},... | collective-permute-start | bytes 172040 | tf_op jit(solution)/shard_map/ppermute | solution.py:23
  44.8 7.0 %collective-permute-start.15 = (bf16[4,7168]{1,0:T(4,128)(2,1)S(1)}, bf16[4,7168]{1,0:T(4,128)(2,1)S(1)}, u32[]{:S(2)}, u32[]{:S(2)}) collective-permute-start(bf16[4,7168]{1,0:T(4,128)(2,1)S(1)} %get-tuple-element.48), channel_id=1, source_target_pairs={{0,14},{1,15},{2,12},{3,13},{4,10},{5,11},{6,8},{7,9},{8,6},{9,7},... | collective-permute-start | bytes 172040 | tf_op jit(solution)/shard_map/ppermute | solution.py:23
  46.0 5.8 %collective-permute-start.9 = (bf16[4,7168]{1,0:T(4,128)(2,1)S(1)}, bf16[4,7168]{1,0:T(4,128)(2,1)S(1)}, u32[]{:S(2)}, u32[]{:S(2)}) collective-permute-start(bf16[4,7168]{1,0:T(4,128)(2,1)S(1)} %get-tuple-element.47), channel_id=1, source_target_pairs={{0,2},{1,3},{2,0},{3,1},{4,6},{5,7},{6,4},{7,5},{8,10},{9,11},{10,... | collective-permute-start | bytes 172040 | tf_op jit(solution)/shard_map/ppermute | solution.py:23
  52.1 8.8 %collective-permute-start.17 = (bf16[4,7168]{1,0:T(4,128)(2,1)S(1)}, bf16[4,7168]{1,0:T(4,128)(2,1)S(1)}, u32[]{:S(2)}, u32[]{:S(2)}) collective-permute-start(bf16[4,7168]{1,0:T(4,128)(2,1)S(1)} %add_convert_fusion.3), channel_id=1, source_target_pairs={{0,16},{1,17},{2,18},{3,19},{4,20},{5,21},{6,22},{7,23},{8,24},{9,... | collective-permute-start | bytes 172040 | tf_op jit(solution)/shard_map/ppermute | solution.py:23
  53.7 9.1 %collective-permute-start.18 = (bf16[4,7168]{1,0:T(4,128)(2,1)S(1)}, bf16[4,7168]{1,0:T(4,128)(2,1)S(1)}, u32[]{:S(2)}, u32[]{:S(2)}) collective-permute-start(bf16[4,7168]{1,0:T(4,128)(2,1)S(1)} %add_convert_fusion.3), channel_id=1, source_target_pairs={{0,18},{1,19},{2,16},{3,17},{4,22},{5,23},{6,20},{7,21},{8,26},{9,... | collective-permute-start | bytes 172040 | tf_op jit(solution)/shard_map/ppermute | solution.py:23
  55.2 9.6 %collective-permute-start.19 = (bf16[4,7168]{1,0:T(4,128)(2,1)S(1)}, bf16[4,7168]{1,0:T(4,128)(2,1)S(1)}, u32[]{:S(2)}, u32[]{:S(2)}) collective-permute-start(bf16[4,7168]{1,0:T(4,128)(2,1)S(1)} %add_convert_fusion.3), channel_id=1, source_target_pairs={{0,20},{1,21},{2,22},{3,23},{4,16},{5,17},{6,18},{7,19},{8,28},{9,... | collective-permute-start | bytes 172040 | tf_op jit(solution)/shard_map/ppermute | solution.py:23
  56.9 10.7 %collective-permute-start.20 = (bf16[4,7168]{1,0:T(4,128)(2,1)S(1)}, bf16[4,7168]{1,0:T(4,128)(2,1)S(1)}, u32[]{:S(2)}, u32[]{:S(2)}) collective-permute-start(bf16[4,7168]{1,0:T(4,128)(2,1)S(1)} %add_convert_fusion.3), channel_id=1, source_target_pairs={{0,22},{1,23},{2,20},{3,21},{4,18},{5,19},{6,16},{7,17},{8,30},{9,... | collective-permute-start | bytes 172040 | tf_op jit(solution)/shard_map/ppermute | solution.py:23
  58.1 9.5 %collective-permute-start.21 = (bf16[4,7168]{1,0:T(4,128)(2,1)S(1)}, bf16[4,7168]{1,0:T(4,128)(2,1)S(1)}, u32[]{:S(2)}, u32[]{:S(2)}) collective-permute-start(bf16[4,7168]{1,0:T(4,128)(2,1)S(1)} %add_convert_fusion.3), channel_id=1, source_target_pairs={{0,24},{1,25},{2,26},{3,27},{4,28},{5,29},{6,30},{7,31},{8,16},{9,... | collective-permute-start | bytes 172040 | tf_op jit(solution)/shard_map/ppermute | solution.py:23
  60.9 9.4 %collective-permute-start.22 = (bf16[4,7168]{1,0:T(4,128)(2,1)S(1)}, bf16[4,7168]{1,0:T(4,128)(2,1)S(1)}, u32[]{:S(2)}, u32[]{:S(2)}) collective-permute-start(bf16[4,7168]{1,0:T(4,128)(2,1)S(1)} %add_convert_fusion.3), channel_id=1, source_target_pairs={{0,26},{1,27},{2,24},{3,25},{4,30},{5,31},{6,28},{7,29},{8,18},{9,... | collective-permute-start | bytes 172040 | tf_op jit(solution)/shard_map/ppermute | solution.py:23
  62.8 7.5 %collective-permute-start.23 = (bf16[4,7168]{1,0:T(4,128)(2,1)S(1)}, bf16[4,7168]{1,0:T(4,128)(2,1)S(1)}, u32[]{:S(2)}, u32[]{:S(2)}) collective-permute-start(bf16[4,7168]{1,0:T(4,128)(2,1)S(1)} %add_convert_fusion.3), channel_id=1, source_target_pairs={{0,28},{1,29},{2,30},{3,31},{4,24},{5,25},{6,26},{7,27},{8,20},{9,... | collective-permute-start | bytes 172040 | tf_op jit(solution)/shard_map/ppermute | solution.py:23
  64.8 7.8 %collective-permute-start.24 = (bf16[4,7168]{1,0:T(4,128)(2,1)S(1)}, bf16[4,7168]{1,0:T(4,128)(2,1)S(1)}, u32[]{:S(2)}, u32[]{:S(2)}) collective-permute-start(bf16[4,7168]{1,0:T(4,128)(2,1)S(1)} %add_convert_fusion.3), channel_id=1, source_target_pairs={{0,30},{1,31},{2,28},{3,29},{4,26},{5,27},{6,24},{7,25},{8,22},{9,... | collective-permute-start | bytes 172040 | tf_op jit(solution)/shard_map/ppermute | solution.py:23
  72.9 1.9 %collective-permute-start.25 = (bf16[32,7168]{1,0:T(8,128)(2,1)S(1)}, bf16[32,7168]{1,0:T(8,128)(2,1)S(1)}, u32[]{:S(2)}, u32[]{:S(2)}) collective-permute-start(bf16[32,7168]{1,0:T(8,128)(2,1)S(1)} %concatenate.7.own_ref), channel_id=1, source_target_pairs={{0,1},{1,0},{2,3},{3,2},{4,5},{5,4},{6,7},{7,6},{8,9},{9,8},{10,11... | collective-permute-start | bytes 1376264 | tf_op jit(solution)/shard_map/ppermute | solution.py:23
  74.8 2.0 %copy-start.2 = (bf16[1,7168,256]{2,1,0:T(8,128)(2,1)S(1)}, bf16[1,7168,256]{2,1,0:T(8,128)(2,1)}, u32[]{:S(2)}) copy-start(bf16[1,7168,256]{2,1,0:T(8,128)(2,1)} %copy-done) | copy-start | bytes 11010052
  76.8 2.0 %copy-start.5 = (bf16[1,7168,256]{2,1,0:T(8,128)(2,1)S(1)}, bf16[1,7168,256]{2,1,0:T(8,128)(2,1)}, u32[]{:S(2)}) copy-start(bf16[1,7168,256]{2,1,0:T(8,128)(2,1)} %copy-done.3) | copy-start | bytes 11010052
  78.8 2.0 %copy-start.8 = (bf16[1,256,7168]{2,1,0:T(8,128)(2,1)S(1)}, bf16[1,256,7168]{2,1,0:T(8,128)(2,1)}, u32[]{:S(2)}) copy-start(bf16[1,256,7168]{2,1,0:T(8,128)(2,1)} %copy-done.6) | copy-start | bytes 11010052
  83.2 1.9 %collective-permute-start.26 = (bf16[32,7168]{1,0:T(8,128)(2,1)S(1)}, bf16[32,7168]{1,0:T(8,128)(2,1)S(1)}, u32[]{:S(2)}, u32[]{:S(2)}) collective-permute-start(bf16[32,7168]{1,0:T(8,128)(2,1)S(1)} %get-tuple-element.26), channel_id=1, source_target_pairs={{0,1},{1,0},{2,3},{3,2},{4,5},{5,4},{6,7},{7,6},{8,9},{9,8},{10,11... | collective-permute-start | bytes 1376264 | tf_op jit(solution)/shard_map/ppermute | solution.py:23
  85.4 7.4 %collective-permute-start.27 = (bf16[4,7168]{1,0:T(4,128)(2,1)S(1)}, bf16[4,7168]{1,0:T(4,128)(2,1)S(1)}, u32[]{:S(2)}, u32[]{:S(2)}) collective-permute-start(bf16[4,7168]{1,0:T(4,128)(2,1)S(1)} %get-tuple-element.39), channel_id=1, source_target_pairs={{0,16},{1,17},{2,18},{3,19},{4,20},{5,21},{6,22},{7,23},{8,24},{9,... | collective-permute-start | bytes 172040 | tf_op jit(solution)/shard_map/ppermute | solution.py:23
  86.4 9.6 %collective-permute-start.28 = (bf16[4,7168]{1,0:T(4,128)(2,1)S(1)}, bf16[4,7168]{1,0:T(4,128)(2,1)S(1)}, u32[]{:S(2)}, u32[]{:S(2)}) collective-permute-start(bf16[4,7168]{1,0:T(4,128)(2,1)S(1)} %get-tuple-element.46), channel_id=1, source_target_pairs={{0,18},{1,19},{2,16},{3,17},{4,22},{5,23},{6,20},{7,21},{8,26},{9,... | collective-permute-start | bytes 172040 | tf_op jit(solution)/shard_map/ppermute | solution.py:23
  88.4 9.5 %collective-permute-start.29 = (bf16[4,7168]{1,0:T(4,128)(2,1)S(1)}, bf16[4,7168]{1,0:T(4,128)(2,1)S(1)}, u32[]{:S(2)}, u32[]{:S(2)}) collective-permute-start(bf16[4,7168]{1,0:T(4,128)(2,1)S(1)} %get-tuple-element.45), channel_id=1, source_target_pairs={{0,20},{1,21},{2,22},{3,23},{4,16},{5,17},{6,18},{7,19},{8,28},{9,... | collective-permute-start | bytes 172040 | tf_op jit(solution)/shard_map/ppermute | solution.py:23
  89.4 11.4 %collective-permute-start.30 = (bf16[4,7168]{1,0:T(4,128)(2,1)S(1)}, bf16[4,7168]{1,0:T(4,128)(2,1)S(1)}, u32[]{:S(2)}, u32[]{:S(2)}) collective-permute-start(bf16[4,7168]{1,0:T(4,128)(2,1)S(1)} %get-tuple-element.44), channel_id=1, source_target_pairs={{0,22},{1,23},{2,20},{3,21},{4,18},{5,19},{6,16},{7,17},{8,30},{9,... | collective-permute-start | bytes 172040 | tf_op jit(solution)/shard_map/ppermute | solution.py:23
  91.3 9.5 %collective-permute-start.31 = (bf16[4,7168]{1,0:T(4,128)(2,1)S(1)}, bf16[4,7168]{1,0:T(4,128)(2,1)S(1)}, u32[]{:S(2)}, u32[]{:S(2)}) collective-permute-start(bf16[4,7168]{1,0:T(4,128)(2,1)S(1)} %get-tuple-element.43), channel_id=1, source_target_pairs={{0,24},{1,25},{2,26},{3,27},{4,28},{5,29},{6,30},{7,31},{8,16},{9,... | collective-permute-start | bytes 172040 | tf_op jit(solution)/shard_map/ppermute | solution.py:23
  92.7 9.1 %collective-permute-start.32 = (bf16[4,7168]{1,0:T(4,128)(2,1)S(1)}, bf16[4,7168]{1,0:T(4,128)(2,1)S(1)}, u32[]{:S(2)}, u32[]{:S(2)}) collective-permute-start(bf16[4,7168]{1,0:T(4,128)(2,1)S(1)} %get-tuple-element.42), channel_id=1, source_target_pairs={{0,26},{1,27},{2,24},{3,25},{4,30},{5,31},{6,28},{7,29},{8,18},{9,... | collective-permute-start | bytes 172040 | tf_op jit(solution)/shard_map/ppermute | solution.py:23
  96.1 7.6 %collective-permute-start.33 = (bf16[4,7168]{1,0:T(4,128)(2,1)S(1)}, bf16[4,7168]{1,0:T(4,128)(2,1)S(1)}, u32[]{:S(2)}, u32[]{:S(2)}) collective-permute-start(bf16[4,7168]{1,0:T(4,128)(2,1)S(1)} %get-tuple-element.41), channel_id=1, source_target_pairs={{0,28},{1,29},{2,30},{3,31},{4,24},{5,25},{6,26},{7,27},{8,20},{9,... | collective-permute-start | bytes 172040 | tf_op jit(solution)/shard_map/ppermute | solution.py:23
  97.9 7.8 %collective-permute-start.34 = (bf16[4,7168]{1,0:T(4,128)(2,1)S(1)}, bf16[4,7168]{1,0:T(4,128)(2,1)S(1)}, u32[]{:S(2)}, u32[]{:S(2)}) collective-permute-start(bf16[4,7168]{1,0:T(4,128)(2,1)S(1)} %get-tuple-element.40), channel_id=1, source_target_pairs={{0,30},{1,31},{2,28},{3,29},{4,26},{5,27},{6,24},{7,25},{8,22},{9,... | collective-permute-start | bytes 172040 | tf_op jit(solution)/shard_map/ppermute | solution.py:23

commit v5 on v4

v5 whole, which is shorter than its diff:
```python
import jax
import jax.numpy as jnp
from jax import lax
from jax.experimental import pallas as pl
from jax.experimental.pallas import tpu as pltpu
from jax.sharding import PartitionSpec as P

GROUP = 4
LANES = 128
CHUNK = 1024
VMEM_LIMIT = 24 * 1024 * 1024


def exchange(value, flip, hop):
    segments, owners = lax.axis_size("segment"), lax.axis_size("expert")
    if flip == 0 and hop % segments == 0:
        return value
    pairs = []
    for seg in range(segments):
        for own in range(owners):
            target = (seg + hop) % segments * owners + (own ^ flip)
            pairs.append((seg * owners + own, target))
    return lax.ppermute(value, ("segment", "expert"), pairs)


def mlp_kernel(own_ref, far_ref, gain_ref, gate_hbm, up_hbm, down_hbm, own_out, far_out,
               rows_ref, gate_ref, up_ref, down_ref, sems):
    half, dim = own_ref.shape
    starts = range(0, dim, CHUNK)
    loads = {}
    for place, start in enumerate(starts):
        span = pl.ds(start, CHUNK)
        loads["gate", start] = pltpu.make_async_copy(gate_hbm.at[0, span, :], gate_ref.at[span, :], sems.at[0, place])
        loads["up", start] = pltpu.make_async_copy(up_hbm.at[0, span, :], up_ref.at[span, :], sems.at[1, place])
        loads["gate", start].start()
        loads["up", start].start()
    for place, start in enumerate(starts):
        span = pl.ds(start, CHUNK)
        loads["down", start] = pltpu.make_async_copy(
            down_hbm.at[0, :, span], down_ref.at[:, span], sems.at[2, place])
        loads["down", start].start()
    for part, ref in enumerate((own_ref, far_ref)):
        square = jnp.zeros((half, LANES), jnp.float32)
        for start in range(0, dim, LANES):
            piece = ref[:, start:start + LANES].astype(jnp.float32)
            square += piece * piece
        inv = lax.rsqrt(jnp.sum(square, axis=1, keepdims=True) / dim + 1e-06)
        for start in starts:
            piece = ref[:, start:start + CHUNK].astype(jnp.float32)
            scaled = piece * inv * gain_ref[:, start:start + CHUNK]
            rows_ref[part * half:(part + 1) * half, start:start + CHUNK] = scaled.astype(jnp.bfloat16)
    gated = jnp.zeros((2 * half, gate_ref.shape[1]), jnp.float32)
    up_part = jnp.zeros((2 * half, gate_ref.shape[1]), jnp.float32)
    for start in starts:
        rows = rows_ref[:, start:start + CHUNK]
        loads["gate", start].wait()
        gated += jnp.dot(rows, gate_ref[start:start + CHUNK, :], preferred_element_type=jnp.float32)
        loads["up", start].wait()
        up_part += jnp.dot(rows, up_ref[start:start + CHUNK, :], preferred_element_type=jnp.float32)
    inner = (gated / (1.0 + jnp.exp(-gated)) * up_part).astype(jnp.bfloat16)
    for start in starts:
        loads["down", start].wait()
        terms = jnp.dot(inner, down_ref[:, start:start + CHUNK], preferred_element_type=jnp.float32)
        own_out[:, start:start + CHUNK] = terms[:half].astype(jnp.bfloat16)
        far_out[:, start:start + CHUNK] = terms[half:].astype(jnp.bfloat16)


def mlp(own, far, gain, gate, up, down):
    half, dim = own.shape
    hidden = gate.shape[2]
    vmem = pl.BlockSpec(memory_space=pltpu.VMEM)
    hbm = pl.BlockSpec(memory_space=pltpu.HBM)
    gate, up, down = [pltpu.with_memory_space_constraint(w, pltpu.HBM) for w in (gate, up, down)]
    return pl.pallas_call(
        mlp_kernel,
        out_shape=[jax.ShapeDtypeStruct((half, dim), jnp.bfloat16)] * 2,
        in_specs=[vmem] * 3 + [hbm] * 3,
        out_specs=[vmem] * 2,
        scratch_shapes=[
            pltpu.VMEM((2 * half, dim), jnp.bfloat16),
            pltpu.VMEM((dim, hidden), jnp.bfloat16),
            pltpu.VMEM((dim, hidden), jnp.bfloat16),
            pltpu.VMEM((hidden, dim), jnp.bfloat16),
            pltpu.SemaphoreType.DMA((3, dim // CHUNK)),
        ],
        compiler_params=pltpu.CompilerParams(vmem_limit_bytes=VMEM_LIMIT),
        cost_estimate=pl.CostEstimate(flops=12 * half * dim * hidden, bytes_accessed=6 * dim * hidden, transcendentals=0),
    )(own, far, gain, gate, up, down)


def on_device(states, routing, route_weight, norm_gain, gate_proj, up_proj, down_proj):
    owners = lax.axis_size("expert")
    experts = owners // GROUP
    row_dev, model_dim = states.shape[1:]
    passes_count = routing.shape[1]
    groups = [list(range(core, owners, 2)) for core in range(2)]
    expert_ids = jnp.arange(experts, dtype=jnp.int32)

    picked = routing[0][..., None] == expert_ids
    dense = jnp.sum(jnp.where(picked, route_weight[0][..., None].astype(jnp.float32), 0.0), axis=2)

    current = states[0]
    for step_no in range(passes_count):
        own = lax.all_gather(current, "expert", axis=0, tiled=True, axis_index_groups=groups)
        far = exchange(own, 1, 0)
        kept, sent = mlp(own, far, norm_gain, gate_proj, up_proj, down_proj)
        chip = kept.astype(jnp.float32) + exchange(sent, 1, 0).astype(jnp.float32)
        chip = chip.astype(jnp.bfloat16).reshape(owners // 2, row_dev, model_dim)
        parts = lax.all_to_all(chip, "expert", split_axis=0, concat_axis=0, tiled=True, axis_index_groups=groups)
        total = current.astype(jnp.float32)
        for place in range(owners // 2):
            weight = dense[step_no, :, place * 2 // GROUP, None]
            total = total + jnp.where(weight > 0.0, weight * parts[place].astype(jnp.float32), 0.0)
        current = exchange(total.astype(jnp.bfloat16), 0, 1)
    return current[None]


def solution(mesh):
    return jax.shard_map(
        on_device,
        mesh=mesh,
        in_specs=(
            P("segment", "expert", None),
            P("segment", None, "expert", None),
            P("segment", None, "expert", None),
            P("segment", None),
            P("segment", None, "expert"),
            P("segment", None, "expert"),
            P("segment", "expert", None),
        ),
        out_specs=P("segment", "expert", None),
        check_vma=False,
    )
```

time: 107 us -> 134 us (1.25)
  blocking collectives: 0 us -> 65.6 us
  starting transfers between devices: 56.8 us -> 12.7 us
  waiting for transfers between devices: 20.2 us -> 38.8 us
  local copies, waits for them, and re-layouts: 18.7 us -> 4.73 us
  Pallas kernels: 8.93 us -> 11 us
    all_gather x0 -> x2, blocking collectives: none -> 65.6 us  [on_device(): lax.all_gather(current, 'expert', axis=0, tiled=True, axis_index_groups=g...]
    ppermute x35 -> x6, starting transfers between devices: 56.8 us -> 3.66 us  [exchange(): return lax.ppermute(value, ('segment', 'expert'), pairs)]
    all_to_all x0 -> x2, waiting for transfers between devices: none -> 26.4 us  [on_device(): lax.all_to_all(chip, 'expert', split_axis=0, concat_axis=0, tiled=True, a...]
    unnamed x26 -> x14, local copies, waits for them, and re-layouts: 17.8 us -> 2.55 us
    all_to_all x0 -> x2, starting transfers between devices: none -> 9.06 us  [on_device(): lax.all_to_all(chip, 'expert', split_axis=0, concat_axis=0, tiled=True, a...]
    ppermute x35 -> x6, waiting for transfers between devices: 20.2 us -> 12.3 us  [exchange(): return lax.ppermute(value, ('segment', 'expert'), pairs)]
    pallas_call x2, Pallas kernels: 4.71 us -> 11 us  [mlp(): pl.pallas_call(mlp_kernel, out_shape=[jax.ShapeDtypeStruct((half, dim), j...]
    pallas_call x1 -> x0, Pallas kernels: 4.23 us -> none  [load(): pl.pallas_call(load_kernel, out_shape=[pltpu.VMEM(w.shape, w.dtype) for w...]
  transfers between devices with their start and end apart: 35 -> 8, of which waited for: 10 -> 8; matrix products, arithmetic and copies ran while one was open for 0% -> 0% of each run, Pallas kernels for 6% -> 0%
where the time goes in v5:
time: 134 us
  blocking collectives  65.6 us (49%)
  waiting for transfers between devices  38.8 us (29%)
  starting transfers between devices  12.7 us (9%)
  Pallas kernels  11 us (8%)
  local copies, waits for them, and re-layouts  4.73 us (4%)
    all_gather x2, blocking collectives, on_device(): lax.all_gather(current, 'expert', axis=0, tiled=True, axis_index_groups=g...  65.6 us
    all_to_all x2, waiting for transfers between devices, on_device(): lax.all_to_all(chip, 'expert', split_axis=0, concat_axis=0, tiled=True, a...  26.4 us
    ppermute x6, waiting for transfers between devices, exchange(): return lax.ppermute(value, ('segment', 'expert'), pairs)  12.3 us
    pallas_call x2, Pallas kernels, mlp(): pl.pallas_call(mlp_kernel, out_shape=[jax.ShapeDtypeStruct((half, dim), j...  11 us
    all_to_all x2, starting transfers between devices, on_device(): lax.all_to_all(chip, 'expert', split_axis=0, concat_axis=0, tiled=True, a...  9.06 us
    ppermute x6, starting transfers between devices, exchange(): return lax.ppermute(value, ('segment', 'expert'), pairs)  3.66 us
  transfers between devices with their start and end apart: 8, of which 8 were waited for; matrix products, arithmetic and copies ran while one was open for 0% of the time, Pallas kernels for 0%

profile of v5, /device:TPU:0, one launch (start us, length us, event | category | flops | bytes accessed | tf_op | source)
XLA Modules:
  0.0 133.9 jit_solution(17005348453339982639)
XLA Ops:
  0.0 0.9 copy.17
  0.9 34.2 %all-gather = bf16[1,32,7168]{2,0,1:T(2,128)(2,1)S(1)} all-gather(bf16[1,4,7168]{2,0,1:T(2,128)(2,1)S(1)} %copy.17), channel_id=2, replica_groups={{0,2,4,6,8,10,12,14},{1,3,5,7,9,11,13,15},{16,18,20,22,24,26,28,30},{17..., dimensions={1}, use_global_device_ids=true | all-gather | bytes 516096 | tf_op jit(solution)/shard_map/all_gather | solution.py:104
  35.1 0.2 copy.20
  35.3 0.0 copy-start.4
  35.3 0.1 collective-permute-start
  35.4 1.8 %collective-permute-done.far_ref = bf16[32,7168]{1,0:T(8,128)(2,1)S(1)} collective-permute-done((bf16[32,7168]{1,0:T(8,128)(2,1)S(1)}, bf16[32,7168]{1,0:T(8,128)(2,1)S(1)}, u32[]{:S(2)}, u32[]{:S(2)}) %collective-permute-start) | collective-permute-done | bytes 458784 | tf_op jit(solution)/shard_map/ppermute | solution.py:23
  37.2 0.0 copy-start
  37.2 0.7 copy-done
  37.9 0.0 copy-start.3
  37.9 0.0 copy-start.2
  37.9 5.5 %shard_map.73 = (bf16[32,7168]{1,0:T(8,128)(2,1)S(1)}, bf16[32,7168]{1,0:T(8,128)(2,1)S(1)}) custom-call(bf16[32,7168]{1,0:T(8,128)(2,1)S(1)} %bitcast.93, bf16[32,7168]{1,0:T(8,128)(2,1)S(1)} %collective-permute-done.far_ref, f32[1,7168]{1,0:T(1,128)S(1)} %copy-done, bf16[1,7168,256]{2,1,0:T(8,128)(2,1)} %gate_hbm.3, bf16[1,7168,256]{2,1,0:T(8,128)(2,1)} %up_hbm.3, ...), custom_call_target="tpu_custom_call" | custom-call | flops 704643072 | bytes 11010048 | tf_op jit(solution)/shard_map/pallas_call | solution.py:74
  43.5 0.0 copy-start.1
  43.5 0.2 collective-permute-start.1
  43.7 1.7 %collective-permute-done.1 = bf16[32,7168]{1,0:T(8,128)(2,1)S(1)} collective-permute-done((bf16[32,7168]{1,0:T(8,128)(2,1)S(1)}, bf16[32,7168]{1,0:T(8,128)(2,1)S(1)}, u32[]{:S(2)}, u32[]{:S(2)}) %collective-permute-start.1) | collective-permute-done | bytes 458784 | tf_op jit(solution)/shard_map/ppermute | solution.py:23
  45.4 0.1 add_convert_fusion.1
  45.5 0.9 reshape.112
  46.4 5.5 %all-to-all-start = ((bf16[8,4,7168]{2,1,0:T(4,128)(2,1)}), bf16[8,4,7168]{2,1,0:T(4,128)(2,1)S(1)}, u32[]{:S(2)}, u32[]{:S(2)}) async-start(bf16[8,4,7168]{2,1,0:T(4,128)(2,1)} %reshape.112), calls=%async_computation | async-start | bytes 917504 | tf_op jit(solution)/shard_map/all_to_all | solution.py:109
  51.9 0.0 copy-done.4
  51.9 0.0 copy-done.3
  51.9 0.1 select_reduce_fusion
  52.0 0.3 slice_reduce_fusion.3
  52.4 13.0 %all-to-all-done = bf16[8,4,7168]{2,1,0:T(4,128)(2,1)S(1)} async-done(((bf16[8,4,7168]{2,1,0:T(4,128)(2,1)}), bf16[8,4,7168]{2,1,0:T(4,128)(2,1)S(1)}, u32[]{:S(2)}, u32[]{:S(2)}) %all-to-all-start) | async-done | bytes 458784 | tf_op jit(solution)/shard_map/all_to_all | solution.py:109
  65.3 0.0 copy-done.2
  65.3 0.3 fusion.19
  65.6 1.6 %collective-permute-start.2 = (bf16[4,7168]{1,0:T(4,128)(2,1)S(1)}, bf16[4,7168]{1,0:T(4,128)(2,1)S(1)}, u32[]{:S(2)}, u32[]{:S(2)}) collective-permute-start(bf16[4,7168]{1,0:T(4,128)(2,1)S(1)} %fusion.19), channel_id=1, source_target_pairs={{0,16},{1,17},{2,18},{3,19},{4,20},{5,21},{6,22},{7,23},{8,24},{9,... | collective-permute-start | bytes 172040 | tf_op jit(solution)/shard_map/ppermute | solution.py:23
  67.2 2.7 %collective-permute-done.2 = bf16[4,7168]{1,0:T(4,128)(2,1)S(1)} collective-permute-done((bf16[4,7168]{1,0:T(4,128)(2,1)S(1)}, bf16[4,7168]{1,0:T(4,128)(2,1)S(1)}, u32[]{:S(2)}, u32[]{:S(2)}) %collective-permute-start.2) | collective-permute-done | bytes 57376 | tf_op jit(solution)/shard_map/ppermute | solution.py:23
  69.9 31.3 %all-gather.1 = bf16[8,4,7168]{2,1,0:T(4,128)(2,1)S(1)} all-gather(bf16[1,4,7168]{2,1,0:T(4,128)(2,1)S(1)} %bitcast.94), channel_id=1, replica_groups={{0,2,4,6,8,10,12,14},{1,3,5,7,9,11,13,15},{16,18,20,22,24,26,28,30},{17..., dimensions={0}, use_global_device_ids=true | all-gather | bytes 516096 | tf_op jit(solution)/shard_map/all_gather | solution.py:104
  101.2 0.1 reshape.134.own_ref
  101.3 0.1 collective-permute-start.3
  101.4 1.8 %collective-permute-done.3.far_ref = bf16[32,7168]{1,0:T(8,128)(2,1)S(1)} collective-permute-done((bf16[32,7168]{1,0:T(8,128)(2,1)S(1)}, bf16[32,7168]{1,0:T(8,128)(2,1)S(1)}, u32[]{:S(2)}, u32[]{:S(2)}) %collective-permute-start.3) | collective-permute-done | bytes 458784 | tf_op jit(solution)/shard_map/ppermute | solution.py:23
  103.2 0.0 copy-done.1
  103.2 5.5 %shard_map.74 = (bf16[32,7168]{1,0:T(8,128)(2,1)S(1)}, bf16[32,7168]{1,0:T(8,128)(2,1)S(1)}) custom-call(bf16[32,7168]{1,0:T(8,128)(2,1)S(1)} %reshape.134.own_ref, bf16[32,7168]{1,0:T(8,128)(2,1)S(1)} %collective-permute-done.3.far_ref, f32[1,7168]{1,0:T(1,128)S(1)} %copy-done.1, bf16[1,7168,256]{2,1,0:T(8,128)(2,1)} %gate_hbm.3, ...), custom_call_target="tpu_custom_call" | custom-call | flops 704643072 | bytes 11010048 | tf_op jit(solution)/shard_map/pallas_call | solution.py:74
  108.7 0.2 collective-permute-start.4
  108.9 1.7 %collective-permute-done.4 = bf16[32,7168]{1,0:T(8,128)(2,1)S(1)} collective-permute-done((bf16[32,7168]{1,0:T(8,128)(2,1)S(1)}, bf16[32,7168]{1,0:T(8,128)(2,1)S(1)}, u32[]{:S(2)}, u32[]{:S(2)}) %collective-permute-start.4) | collective-permute-done | bytes 458784 | tf_op jit(solution)/shard_map/ppermute | solution.py:23
  110.6 0.1 add_convert_fusion
  110.7 0.9 reshape.113
  111.6 3.6 %all-to-all-start.1 = ((bf16[8,4,7168]{2,1,0:T(4,128)(2,1)}), bf16[8,4,7168]{2,1,0:T(4,128)(2,1)S(1)}, u32[]{:S(2)}, u32[]{:S(2)}) async-start(bf16[8,4,7168]{2,1,0:T(4,128)(2,1)} %reshape.113), calls=%async_computation.1 | async-start | bytes 917504 | tf_op jit(solution)/shard_map/all_to_all | solution.py:109
  115.2 13.5 %all-to-all-done.1 = bf16[8,4,7168]{2,1,0:T(4,128)(2,1)S(1)} async-done(((bf16[8,4,7168]{2,1,0:T(4,128)(2,1)}), bf16[8,4,7168]{2,1,0:T(4,128)(2,1)S(1)}, u32[]{:S(2)}, u32[]{:S(2)}) %all-to-all-start.1) | async-done | bytes 458784 | tf_op jit(solution)/shard_map/all_to_all | solution.py:109
  128.7 0.3 fusion.2
  129.0 1.6 %collective-permute-start.5 = (bf16[4,7168]{1,0:T(4,128)(2,1)S(1)}, bf16[4,7168]{1,0:T(4,128)(2,1)S(1)}, u32[]{:S(2)}, u32[]{:S(2)}) collective-permute-start(bf16[4,7168]{1,0:T(4,128)(2,1)S(1)} %fusion.2), channel_id=1, source_target_pairs={{0,16},{1,17},{2,18},{3,19},{4,20},{5,21},{6,22},{7,23},{8,24},{9,... | collective-permute-start | bytes 172040 | tf_op jit(solution)/shard_map/ppermute | solution.py:23
  130.6 2.7 %collective-permute-done.5 = bf16[4,7168]{1,0:T(4,128)(2,1)S(1)} collective-permute-done((bf16[4,7168]{1,0:T(4,128)(2,1)S(1)}, bf16[4,7168]{1,0:T(4,128)(2,1)S(1)}, u32[]{:S(2)}, u32[]{:S(2)}) %collective-permute-start.5) | collective-permute-done | bytes 57376 | tf_op jit(solution)/shard_map/ppermute | solution.py:23
  133.3 0.6 copy.22
  (5 shorter events, 0.0 us)
Async XLA Ops:
  35.3 16.6 %copy-start.4 = (bf16[1,2,4,2]{2,3,1,0:T(2,128)(2,1)S(1)}, bf16[1,2,4,2]{2,3,1,0:T(2,128)(2,1)}, u32[]{:S(2)}) copy-start(bf16[1,2,4,2]{2,3,1,0:T(2,128)(2,1)} %param.9) | copy-start | bytes 100
  35.3 1.9 %collective-permute-start = (bf16[32,7168]{1,0:T(8,128)(2,1)S(1)}, bf16[32,7168]{1,0:T(8,128)(2,1)S(1)}, u32[]{:S(2)}, u32[]{:S(2)}) collective-permute-start(bf16[32,7168]{1,0:T(8,128)(2,1)S(1)} %bitcast.92), channel_id=1, source_target_pairs={{0,1},{1,0},{2,3},{3,2},{4,5},{5,4},{6,7},{7,6},{8,9},{9,8},{10,11... | collective-permute-start | bytes 1376264 | tf_op jit(solution)/shard_map/ppermute | solution.py:23
  37.2 0.7 copy-start
  37.9 14.0 %copy-start.3 = (s32[1,2,4,2]{2,3,1,0:T(2,128)S(1)}, s32[1,2,4,2]{2,3,1,0:T(2,128)}, u32[]{:S(2)}) copy-start(s32[1,2,4,2]{2,3,1,0:T(2,128)} %param.8) | copy-start | bytes 196
  37.9 27.4 %copy-start.2 = (bf16[1,4,7168]{2,1,0:T(4,128)(2,1)S(1)}, bf16[1,4,7168]{2,1,0:T(4,128)(2,1)}, u32[]{:S(2)}) copy-start(bf16[1,4,7168]{2,1,0:T(4,128)(2,1)} %param.7) | copy-start | bytes 172036
  43.5 59.7 %copy-start.1 = (f32[1,7168]{1,0:T(1,128)S(1)}, f32[1,7168]{1,0:T(1,128)}, u32[]{:S(2)}) copy-start(f32[1,7168]{1,0:T(1,128)} %gain_ref.3) | copy-start | bytes 86020
  43.5 1.9 %collective-permute-start.1 = (bf16[32,7168]{1,0:T(8,128)(2,1)S(1)}, bf16[32,7168]{1,0:T(8,128)(2,1)S(1)}, u32[]{:S(2)}, u32[]{:S(2)}) collective-permute-start(bf16[32,7168]{1,0:T(8,128)(2,1)S(1)} %get-tuple-element.10), channel_id=1, source_target_pairs={{0,1},{1,0},{2,3},{3,2},{4,5},{5,4},{6,7},{7,6},{8,9},{9,8},{10,11... | collective-permute-start | bytes 1376264 | tf_op jit(solution)/shard_map/ppermute | solution.py:23
  46.4 18.9 %all-to-all-start = ((bf16[8,4,7168]{2,1,0:T(4,128)(2,1)}), bf16[8,4,7168]{2,1,0:T(4,128)(2,1)S(1)}, u32[]{:S(2)}, u32[]{:S(2)}) async-start(bf16[8,4,7168]{2,1,0:T(4,128)(2,1)} %reshape.112), calls=%async_computation | async-start | bytes 917504 | tf_op jit(solution)/shard_map/all_to_all | solution.py:109
  65.6 4.2 %collective-permute-start.2 = (bf16[4,7168]{1,0:T(4,128)(2,1)S(1)}, bf16[4,7168]{1,0:T(4,128)(2,1)S(1)}, u32[]{:S(2)}, u32[]{:S(2)}) collective-permute-start(bf16[4,7168]{1,0:T(4,128)(2,1)S(1)} %fusion.19), channel_id=1, source_target_pairs={{0,16},{1,17},{2,18},{3,19},{4,20},{5,21},{6,22},{7,23},{8,24},{9,... | collective-permute-start | bytes 172040 | tf_op jit(solution)/shard_map/ppermute | solution.py:23
  101.3 1.9 %collective-permute-start.3 = (bf16[32,7168]{1,0:T(8,128)(2,1)S(1)}, bf16[32,7168]{1,0:T(8,128)(2,1)S(1)}, u32[]{:S(2)}, u32[]{:S(2)}) collective-permute-start(bf16[32,7168]{1,0:T(8,128)(2,1)S(1)} %reshape.134.own_ref), channel_id=1, source_target_pairs={{0,1},{1,0},{2,3},{3,2},{4,5},{5,4},{6,7},{7,6},{8,9},{9,8},{10,11... | collective-permute-start | bytes 1376264 | tf_op jit(solution)/shard_map/ppermute | solution.py:23
  108.7 1.9 %collective-permute-start.4 = (bf16[32,7168]{1,0:T(8,128)(2,1)S(1)}, bf16[32,7168]{1,0:T(8,128)(2,1)S(1)}, u32[]{:S(2)}, u32[]{:S(2)}) collective-permute-start(bf16[32,7168]{1,0:T(8,128)(2,1)S(1)} %get-tuple-element.12), channel_id=1, source_target_pairs={{0,1},{1,0},{2,3},{3,2},{4,5},{5,4},{6,7},{7,6},{8,9},{9,8},{10,11... | collective-permute-start | bytes 1376264 | tf_op jit(solution)/shard_map/ppermute | solution.py:23
  111.6 17.1 %all-to-all-start.1 = ((bf16[8,4,7168]{2,1,0:T(4,128)(2,1)}), bf16[8,4,7168]{2,1,0:T(4,128)(2,1)S(1)}, u32[]{:S(2)}, u32[]{:S(2)}) async-start(bf16[8,4,7168]{2,1,0:T(4,128)(2,1)} %reshape.113), calls=%async_computation.1 | async-start | bytes 917504 | tf_op jit(solution)/shard_map/all_to_all | solution.py:109
  129.0 4.2 %collective-permute-start.5 = (bf16[4,7168]{1,0:T(4,128)(2,1)S(1)}, bf16[4,7168]{1,0:T(4,128)(2,1)S(1)}, u32[]{:S(2)}, u32[]{:S(2)}) collective-permute-start(bf16[4,7168]{1,0:T(4,128)(2,1)S(1)} %fusion.2), channel_id=1, source_target_pairs={{0,16},{1,17},{2,18},{3,19},{4,20},{5,21},{6,22},{7,23},{8,24},{9,... | collective-permute-start | bytes 172040 | tf_op jit(solution)/shard_map/ppermute | solution.py:23

commit v6 on v4

v6 whole, which is shorter than its diff:
```python
import functools

import jax
import jax.numpy as jnp
from jax import lax
from jax.experimental import pallas as pl
from jax.experimental.pallas import tpu as pltpu
from jax.sharding import PartitionSpec as P

GROUP = 4
LANES = 128
CHUNK = 1024
VMEM_LIMIT = 16 * 1024 * 1024
VMEM = pl.BlockSpec(memory_space=pltpu.VMEM)


def exchange(value, flips, hop):
    segments, owners = lax.axis_size("segment"), lax.axis_size("expert")
    if flips == (0, 0) and hop % segments == 0:
        return value
    pairs = []
    for seg in range(segments):
        for own in range(owners):
            target = (seg + hop) % segments * owners + (own ^ flips[own % 2])
            pairs.append((seg * owners + own, target))
    return lax.ppermute(value, ("segment", "expert"), pairs)


def direct_flips(owners):
    bits = [1 << place for place in range(1, owners.bit_length() - 1)]
    even, odd = bits[1:], bits[:1] + bits[2:]
    flips = []
    for number in range(owners // 4):
        chosen = [place for place in range(len(even)) if number >> place & 1]
        flips.append((sum(even[place] for place in chosen), sum(odd[place] for place in chosen)))
    return flips


BIG = (2, 4)
CORE = (1, 1)


def spans(dim):
    return [slice(start, min(start + CHUNK, dim)) for start in range(0, dim, CHUNK)]


def call(kernel, outs, *args, **more):
    return pl.pallas_call(
        kernel,
        out_shape=[jax.ShapeDtypeStruct(shape, jnp.bfloat16) for shape in outs],
        in_specs=more.pop("in_specs", [VMEM] * len(args)),
        out_specs=[VMEM] * len(outs),
        compiler_params=pltpu.CompilerParams(vmem_limit_bytes=VMEM_LIMIT),
        **more,
    )(*args)


def load_kernel(gate_ref, up_ref, down_ref, gate_out, up_out, down_out, sems):
    copies = [
        pltpu.make_async_copy(source, target, sems.at[place])
        for place, (source, target) in enumerate(((gate_ref, gate_out), (up_ref, up_out), (down_ref, down_out)))
    ]
    for copy in copies:
        copy.start()
    for copy in copies:
        copy.wait()


def load(weights):
    return pl.pallas_call(
        load_kernel,
        out_shape=[pltpu.VMEM(w.shape, w.dtype) for w in weights],
        in_specs=[pl.BlockSpec(memory_space=pltpu.HBM)] * 3,
        out_specs=[VMEM] * 3,
        scratch_shapes=[pltpu.SemaphoreType.DMA((3,))],
        compiler_params=pltpu.CompilerParams(vmem_limit_bytes=VMEM_LIMIT),
        cost_estimate=pl.CostEstimate(
            flops=0, bytes_accessed=sum(2 * w.size for w in weights), transcendentals=0
        ),
    )(*[pltpu.with_memory_space_constraint(w, pltpu.HBM) for w in weights])


def prepare_kernel(experts, states_ref, routing_ref, weight_ref, out_ref):
    rows, dim = states_ref.shape[1:]
    for span in spans(dim):
        out_ref[:, span] = states_ref[0, :, span]
    lane = lax.broadcasted_iota(jnp.int32, (rows, LANES), 1).astype(jnp.float32)
    diagonal = lax.broadcasted_iota(jnp.int32, (rows, rows), 0) == lax.broadcasted_iota(jnp.int32, (rows, rows), 1)

    def upright(line):
        return jnp.sum(jnp.where(diagonal, line.astype(jnp.float32), 0.0), axis=1, keepdims=True)

    total = jnp.zeros((rows, LANES), jnp.float32)
    for step in range(routing_ref.shape[1]):
        for k in range(routing_ref.shape[2]):
            column = upright(routing_ref[0, step, k:k + 1, :]) + step * experts
            total += jnp.where(lane == column, upright(weight_ref[0, step, k:k + 1, :]), 0.0)
    out_ref[:, dim:] = total.astype(jnp.bfloat16)


def join_kernel(*refs):
    *parts, out_ref = refs
    for span in spans(out_ref.shape[1]):
        rows = [part[:, span].astype(jnp.float32) for part in parts]
        out_ref[:, span] = jnp.concatenate(rows, axis=0).astype(jnp.bfloat16)


def add_kernel(*refs):
    *parts, out_ref = refs
    for span in spans(out_ref.shape[1]):
        out_ref[:, span] = sum(part[:, span].astype(jnp.float32) for part in parts).astype(jnp.bfloat16)


def split_kernel(count, *refs):
    parts, outs = refs[:-count], refs[-count:]
    rows = outs[0].shape[0]
    for span in spans(outs[0].shape[1]):
        total = sum(part[:, span].astype(jnp.float32) for part in parts)
        for place, out_ref in enumerate(outs):
            out_ref[:, span] = total[place * rows:(place + 1) * rows].astype(jnp.bfloat16)


def mlp_kernel(step_no, *refs):
    x_refs, refs = refs[:4], refs[4:]
    if step_no > 0:
        tail_ref, refs = refs[0], refs[1:]
    (gain_ref, gate_ref, up_ref, down_ref), outs, refs = refs[:4], refs[4:8], refs[8:]
    rows_ref = refs[-1]
    part = outs[0].shape[0]
    dim, hidden = gate_ref.shape[1:]
    experts = lax.axis_size("expert") // GROUP
    column = step_no * experts + lax.axis_index("expert") // GROUP
    lane = lax.broadcasted_iota(jnp.int32, (part, LANES), 1)
    weights = []
    for place, ref in enumerate(x_refs):
        band = slice(place * part, (place + 1) * part)
        square = jnp.zeros((part, LANES), jnp.float32)
        for start in range(0, dim, LANES):
            piece = ref[:, start:start + LANES].astype(jnp.float32)
            square += piece * piece
        inv = lax.rsqrt(jnp.sum(square, axis=1, keepdims=True) / dim + 1e-06)
        for span in spans(dim):
            scaled = ref[:, span].astype(jnp.float32) * inv * gain_ref[:, span]
            rows_ref[band, span] = scaled.astype(jnp.bfloat16)
        if step_no == 0:
            tail = ref[:, dim:]
            refs[0][band, :] = tail
        else:
            tail = tail_ref[band, :]
        chosen = jnp.where(lane == column, tail.astype(jnp.float32), 0.0)
        weights.append(jnp.sum(chosen, axis=1, keepdims=True))
    gated = jnp.zeros((4 * part, hidden), jnp.float32)
    up_part = jnp.zeros((4 * part, hidden), jnp.float32)
    for span in spans(dim):
        rows = rows_ref[:, span]
        gated += jnp.dot(rows, gate_ref[0, span, :], preferred_element_type=jnp.float32)
        up_part += jnp.dot(rows, up_ref[0, span, :], preferred_element_type=jnp.float32)
    inner = (gated / (1.0 + jnp.exp(-gated)) * up_part).astype(jnp.bfloat16)
    for span in spans(dim):
        terms = jnp.dot(inner, down_ref[0, :, span], preferred_element_type=jnp.float32)
        for place, out_ref in enumerate(outs):
            weight = weights[place]
            mine = terms[place * part:(place + 1) * part]
            out_ref[:, span] = jnp.where(weight > 0.0, weight * mine, 0.0).astype(jnp.bfloat16)


def mlp(step_no, xs, tail, gain, gate, up, down):
    dim, hidden = gate.shape[1:]
    part = xs[0].shape[0]
    gate, up, down = [pltpu.with_memory_space_constraint(w, pltpu.VMEM) for w in (gate, up, down)]
    first = step_no == 0
    args = list(xs) + ([] if first else [tail]) + [gain, gate, up, down]
    result = call(
        functools.partial(mlp_kernel, step_no), [(part, dim)] * 4 + [(4 * part, LANES)] * first, *args,
        scratch_shapes=[pltpu.VMEM((4 * part, dim), jnp.bfloat16)],
        cost_estimate=pl.CostEstimate(
            flops=24 * part * dim * hidden, bytes_accessed=6 * dim * hidden, transcendentals=0
        ),
    )
    return result[:4], result[4] if first else tail


def on_device(states, routing, route_weight, norm_gain, gate_proj, up_proj, down_proj):
    owners = lax.axis_size("expert")
    experts = owners // GROUP
    row_dev, dim = states.shape[1:]
    passes_count = routing.shape[1]
    directs = direct_flips(owners)
    part = len(directs) * row_dev

    current, tail = states[0], None
    gate, up, down = load((gate_proj, up_proj, down_proj))
    (block,) = call(
        functools.partial(prepare_kernel, experts), [(row_dev, dim + LANES)],
        states, jnp.swapaxes(routing, 2, 3), jnp.swapaxes(route_weight, 2, 3),
    )
    for step_no in range(passes_count):
        last = step_no == passes_count - 1
        hop, out_hop = int(step_no > 0), int(last)
        if step_no > 0:
            block = current
        blocks = [exchange(block, flips, hop) for flips in directs]
        if step_no == 0:
            blocks, gate, up, down = lax.optimization_barrier((blocks, gate, up, down))
        (own_0,) = call(join_kernel, [(part, block.shape[1])], *blocks)
        own_1 = exchange(own_0, BIG, 0)
        far_0 = exchange(own_0, CORE, 0)
        far_1 = exchange(own_1, CORE, 0)
        xs = (own_0, own_1, far_0, far_1)
        outs, tail = mlp(step_no, xs, tail, norm_gain, gate, up, down)
        kept_0, kept_1, sent_0, sent_1 = outs

        (half,) = call(add_kernel, [(part, dim)], kept_1, exchange(sent_1, CORE, 0))
        near = exchange(sent_0, CORE, 0)
        pieces = call(
            functools.partial(split_kernel, len(directs)), [(row_dev, dim)] * len(directs),
            kept_0, near, exchange(half, BIG, 0),
        )
        terms = [exchange(piece, flips, out_hop) for piece, flips in zip(pieces, directs)]
        (current,) = call(add_kernel, [(row_dev, dim)], exchange(current, (0, 0), hop + out_hop), *terms)
    return current[None]


def solution(mesh):
    return jax.shard_map(
        on_device,
        mesh=mesh,
        in_specs=(
            P("segment", "expert", None),
            P("segment", None, "expert", None),
            P("segment", None, "expert", None),
            P("segment", None),
            P("segment", None, "expert"),
            P("segment", None, "expert"),
            P("segment", "expert", None),
        ),
        out_specs=P("segment", "expert", None),
        check_vma=False,
    )
```

time: 107 us -> 81.4 us (0.76)
  starting transfers between devices: 56.8 us -> 30.1 us
  waiting for transfers between devices: 20.2 us -> 38.5 us
  local copies, waits for them, and re-layouts: 18.7 us -> 2.19 us
  other arithmetic: 1.81 us -> 0 us
  Pallas kernels: 8.93 us -> 10.2 us
    ppermute x35 -> x26, starting transfers between devices: 56.8 us -> 30.1 us  [exchange(): return lax.ppermute(value, ('segment', 'expert'), pairs)]
    ppermute x35 -> x26, waiting for transfers between devices: 20.2 us -> 38.5 us  [exchange(): return lax.ppermute(value, ('segment', 'expert'), pairs)]
    unnamed x26 -> x10, local copies, waits for them, and re-layouts: 17.8 us -> 2.19 us
    pallas_call x2 -> x11, Pallas kernels: 4.71 us -> 6.01 us  [call(): pl.pallas_call(kernel, out_shape=[jax.ShapeDtypeStruct(shape, jnp.bfloat1...]
  transfers between devices with their start and end apart: 35 -> 26, of which waited for: 10 -> 17; matrix products, arithmetic and copies ran while one was open for 0% -> 0% of each run, Pallas kernels for 6% -> 5%
where the time goes in v6:
time: 81.4 us; the launch traced here: 81.2 us
  waiting for transfers between devices  38.5 us (47%)
  starting transfers between devices  30.1 us (37%)
  Pallas kernels  10.2 us (13%)
  local copies, waits for them, and re-layouts  2.19 us (3%)
    ppermute x26, waiting for transfers between devices, exchange(): return lax.ppermute(value, ('segment', 'expert'), pairs)  38.5 us
    ppermute x26, starting transfers between devices, exchange(): return lax.ppermute(value, ('segment', 'expert'), pairs)  30.1 us
    pallas_call x11, Pallas kernels, call(): pl.pallas_call(kernel, out_shape=[jax.ShapeDtypeStruct(shape, jnp.bfloat1...  6.01 us
    pallas_call x1, Pallas kernels, load(): pl.pallas_call(load_kernel, out_shape=[pltpu.VMEM(w.shape, w.dtype) for w...  4.23 us
    unnamed x10, local copies, waits for them, and re-layouts  2.19 us
  transfers between devices with their start and end apart: 26, of which 17 were waited for; matrix products, arithmetic and copies ran while one was open for 0% of the time, Pallas kernels for 5%

profile of v6, /device:TPU:0, one launch (start us, length us, event | category | flops | bytes accessed | tf_op | source)
XLA Modules:
  0.0 81.2 jit_solution(16440783645010409585)
XLA Ops:
  0.0 0.8 %copy-done = bf16[1,4,7168]{2,1,0:T(4,128)(2,1)S(1)} copy-done((bf16[1,4,7168]{2,1,0:T(4,128)(2,1)S(1)}, bf16[1,4,7168]{2,1,0:T(4,128)(2,1)}, u32[]{:S(2)}) %copy-start) | copy-done | bytes 57368
  0.8 0.7 copy-done.3
  1.5 0.7 copy-done.4
  2.2 0.1 shard_map.73.refs_0_
  2.3 5.1 %collective-permute-start.2 = (bf16[4,7296]{1,0:T(4,128)(2,1)S(1)}, bf16[4,7296]{1,0:T(4,128)(2,1)S(1)}, u32[]{:S(2)}, u32[]{:S(2)}) collective-permute-start(bf16[4,7296]{1,0:T(4,128)(2,1)S(1)} %shard_map.73.refs_0_), channel_id=1, source_target_pairs={{0,12},{1,11},{2,14},{3,9},{4,8},{5,15},{6,10},{7,13},{8,4},{9,3},... | collective-permute-start | bytes 175112 | tf_op jit(solution)/shard_map/ppermute | solution.py:26
  7.4 0.0 collective-permute-start.1
  7.4 0.6 collective-permute-start
  8.0 4.2 %shard_map.74 = (bf16[1,7168,256]{2,1,0:T(8,128)(2,1)S(1)}, bf16[1,7168,256]{2,1,0:T(8,128)(2,1)S(1)}, bf16[1,256,7168]{2,1,0:T(8,128)(2,1)S(1)}) custom-call(bf16[1,7168,256]{2,1,0:T(8,128)(2,1)} %gate_ref.1, bf16[1,7168,256]{2,1,0:T(8,128)(2,1)} %up_ref.1, bf16[1,256,7168]{2,1,0:T(8,128)(2,1)} %down_ref.1), custom_call_target="tpu_custom_call" | custom-call | bytes 11010048 | tf_op jit(solution)/shard_map/pallas_call | solution.py:70
  12.3 0.0 collective-permute-done.2.refs_3_
  12.3 0.8 collective-permute-done.1.refs_2_
  13.1 0.0 collective-permute-done.refs_1_
  13.1 0.1 shard_map.75.refs_0_
  13.1 0.0 copy-start.1
  13.2 1.0 %collective-permute-start.3 = (bf16[16,7296]{1,0:T(8,128)(2,1)S(1)}, bf16[16,7296]{1,0:T(8,128)(2,1)S(1)}, u32[]{:S(2)}, u32[]{:S(2)}) collective-permute-start(bf16[16,7296]{1,0:T(8,128)(2,1)S(1)} %shard_map.75.refs_0_), channel_id=1, source_target_pairs={{0,2},{1,5},{2,0},{3,7},{4,6},{5,1},{6,4},{7,3},{8,10},{9,13},{10,... | collective-permute-start | bytes 700424 | tf_op jit(solution)/shard_map/ppermute | solution.py:26
  14.1 0.0 collective-permute-start.4
  14.1 5.1 %collective-permute-done.3.refs_1_ = bf16[16,7296]{1,0:T(8,128)(2,1)S(1)} collective-permute-done((bf16[16,7296]{1,0:T(8,128)(2,1)S(1)}, bf16[16,7296]{1,0:T(8,128)(2,1)S(1)}, u32[]{:S(2)}, u32[]{:S(2)}) %collective-permute-start.3) | collective-permute-done | bytes 233504 | tf_op jit(solution)/shard_map/ppermute | solution.py:26
  19.3 0.0 collective-permute-start.5
  19.3 1.5 %collective-permute-done.5.refs_3_ = bf16[16,7296]{1,0:T(8,128)(2,1)S(1)} collective-permute-done((bf16[16,7296]{1,0:T(8,128)(2,1)S(1)}, bf16[16,7296]{1,0:T(8,128)(2,1)S(1)}, u32[]{:S(2)}, u32[]{:S(2)}) %collective-permute-start.5) | collective-permute-done | bytes 233504 | tf_op jit(solution)/shard_map/ppermute | solution.py:26
  20.8 2.4 %shard_map.76 = (bf16[16,7168]{1,0:T(8,128)(2,1)S(1)}, bf16[16,7168]{1,0:T(8,128)(2,1)S(1)}, bf16[16,7168]{1,0:T(8,128)(2,1)S(1)}, bf16[16,7168]{1,0:T(8,128)(2,1)S(1)}, bf16[64,128]{1,0:T(8,128)(2,1)S(1)}) custom-call(bf16[16,7296]{1,0:T(8,128)(2,1)S(1)} %shard_map.75.refs_0_, bf16[16,7296]{1,0:T(8,128)(2,1)S(1)} %collective-permute-done.3.refs_1_, ...), custom_call_target="tpu_custom_call" | custom-call | flops 704643072 | bytes 11010048 | tf_op jit(solution)/shard_map/pallas_call | solution.py:48
  23.2 0.2 collective-permute-start.7
  23.4 0.4 collective-permute-start.6
  23.7 1.0 %collective-permute-done.7.refs_1_ = bf16[16,7168]{1,0:T(8,128)(2,1)S(1)} collective-permute-done((bf16[16,7168]{1,0:T(8,128)(2,1)S(1)}, bf16[16,7168]{1,0:T(8,128)(2,1)S(1)}, u32[]{:S(2)}, u32[]{:S(2)}) %collective-permute-start.7) | collective-permute-done | bytes 229408 | tf_op jit(solution)/shard_map/ppermute | solution.py:26
  24.7 0.1 shard_map.77
  24.8 1.0 %collective-permute-start.8 = (bf16[16,7168]{1,0:T(8,128)(2,1)S(1)}, bf16[16,7168]{1,0:T(8,128)(2,1)S(1)}, u32[]{:S(2)}, u32[]{:S(2)}) collective-permute-start(bf16[16,7168]{1,0:T(8,128)(2,1)S(1)} %shard_map.77), channel_id=1, source_target_pairs={{0,2},{1,5},{2,0},{3,7},{4,6},{5,1},{6,4},{7,3},{8,10},{9,13},{10,... | collective-permute-start | bytes 688136 | tf_op jit(solution)/shard_map/ppermute | solution.py:26
  25.8 0.0 collective-permute-done.6.refs_1_
  25.8 5.1 %collective-permute-done.8.refs_2_ = bf16[16,7168]{1,0:T(8,128)(2,1)S(1)} collective-permute-done((bf16[16,7168]{1,0:T(8,128)(2,1)S(1)}, bf16[16,7168]{1,0:T(8,128)(2,1)S(1)}, u32[]{:S(2)}, u32[]{:S(2)}) %collective-permute-start.8) | collective-permute-done | bytes 229408 | tf_op jit(solution)/shard_map/ppermute | solution.py:26
  30.9 0.1 shard_map.78
  31.0 0.7 collective-permute-start.9
  31.7 2.9 %collective-permute-start.10 = (bf16[4,7168]{1,0:T(4,128)(2,1)S(1)}, bf16[4,7168]{1,0:T(4,128)(2,1)S(1)}, u32[]{:S(2)}, u32[]{:S(2)}) collective-permute-start(bf16[4,7168]{1,0:T(4,128)(2,1)S(1)} %get-tuple-element.48), channel_id=1, source_target_pairs={{0,8},{1,9},{2,10},{3,11},{4,12},{5,13},{6,14},{7,15},{8,0},{9,1},... | collective-permute-start | bytes 172040 | tf_op jit(solution)/shard_map/ppermute | solution.py:26
  34.6 0.9 %collective-permute-start.11 = (bf16[4,7168]{1,0:T(4,128)(2,1)S(1)}, bf16[4,7168]{1,0:T(4,128)(2,1)S(1)}, u32[]{:S(2)}, u32[]{:S(2)}) collective-permute-start(bf16[4,7168]{1,0:T(4,128)(2,1)S(1)} %get-tuple-element.49), channel_id=1, source_target_pairs={{0,12},{1,11},{2,14},{3,9},{4,8},{5,15},{6,10},{7,13},{8,4},{9,3},... | collective-permute-start | bytes 172040 | tf_op jit(solution)/shard_map/ppermute | solution.py:26
  35.4 0.3 collective-permute-done.9.refs_2_
  35.7 2.8 %collective-permute-done.10.refs_3_ = bf16[4,7168]{1,0:T(4,128)(2,1)S(1)} collective-permute-done((bf16[4,7168]{1,0:T(4,128)(2,1)S(1)}, bf16[4,7168]{1,0:T(4,128)(2,1)S(1)}, u32[]{:S(2)}, u32[]{:S(2)}) %collective-permute-start.10) | collective-permute-done | bytes 57376 | tf_op jit(solution)/shard_map/ppermute | solution.py:26
  38.5 2.0 %collective-permute-done.11.refs_4_ = bf16[4,7168]{1,0:T(4,128)(2,1)S(1)} collective-permute-done((bf16[4,7168]{1,0:T(4,128)(2,1)S(1)}, bf16[4,7168]{1,0:T(4,128)(2,1)S(1)}, u32[]{:S(2)}, u32[]{:S(2)}) %collective-permute-start.11) | collective-permute-done | bytes 57376 | tf_op jit(solution)/shard_map/ppermute | solution.py:26
  40.6 0.1 shard_map.79.refs_0_
  40.6 2.1 %collective-permute-start.15 = (bf16[4,7168]{1,0:T(4,128)(2,1)S(1)}, bf16[4,7168]{1,0:T(4,128)(2,1)S(1)}, u32[]{:S(2)}, u32[]{:S(2)}) collective-permute-start(bf16[4,7168]{1,0:T(4,128)(2,1)S(1)} %shard_map.79.refs_0_), channel_id=1, source_target_pairs={{0,28},{1,27},{2,30},{3,25},{4,24},{5,31},{6,26},{7,29},{8,20},{9,... | collective-permute-start | bytes 172040 | tf_op jit(solution)/shard_map/ppermute | solution.py:26
  42.7 0.2 collective-permute-start.14
  42.9 4.0 %collective-permute-start.13 = (bf16[4,7168]{1,0:T(4,128)(2,1)S(1)}, bf16[4,7168]{1,0:T(4,128)(2,1)S(1)}, u32[]{:S(2)}, u32[]{:S(2)}) collective-permute-start(bf16[4,7168]{1,0:T(4,128)(2,1)S(1)} %shard_map.79.refs_0_), channel_id=1, source_target_pairs={{0,20},{1,19},{2,22},{3,17},{4,16},{5,23},{6,18},{7,21},{8,28},{9,... | collective-permute-start | bytes 172040 | tf_op jit(solution)/shard_map/ppermute | solution.py:26
  46.9 0.5 collective-permute-start.12
  47.4 0.2 collective-permute-done.15.refs_3_
  47.7 2.2 %collective-permute-done.14.refs_2_ = bf16[4,7168]{1,0:T(4,128)(2,1)S(1)} collective-permute-done((bf16[4,7168]{1,0:T(4,128)(2,1)S(1)}, bf16[4,7168]{1,0:T(4,128)(2,1)S(1)}, u32[]{:S(2)}, u32[]{:S(2)}) %collective-permute-start.14) | collective-permute-done | bytes 57376 | tf_op jit(solution)/shard_map/ppermute | solution.py:26
  49.9 0.0 collective-permute-done.13.refs_1_
  49.9 1.2 %collective-permute-done.12.refs_0_ = bf16[4,7168]{1,0:T(4,128)(2,1)S(1)} collective-permute-done((bf16[4,7168]{1,0:T(4,128)(2,1)S(1)}, bf16[4,7168]{1,0:T(4,128)(2,1)S(1)}, u32[]{:S(2)}, u32[]{:S(2)}) %collective-permute-start.12) | collective-permute-done | bytes 57376 | tf_op jit(solution)/shard_map/ppermute | solution.py:26
  51.1 0.1 shard_map.80.refs_0_
  51.1 1.6 %collective-permute-start.16 = (bf16[16,7168]{1,0:T(8,128)(2,1)S(1)}, bf16[16,7168]{1,0:T(8,128)(2,1)S(1)}, u32[]{:S(2)}, u32[]{:S(2)}) collective-permute-start(bf16[16,7168]{1,0:T(8,128)(2,1)S(1)} %shard_map.80.refs_0_), channel_id=1, source_target_pairs={{0,2},{1,5},{2,0},{3,7},{4,6},{5,1},{6,4},{7,3},{8,10},{9,13},{10,... | collective-permute-start | bytes 688136 | tf_op jit(solution)/shard_map/ppermute | solution.py:26
  52.7 0.0 collective-permute-start.17
  52.7 4.5 %collective-permute-done.16.refs_1_ = bf16[16,7168]{1,0:T(8,128)(2,1)S(1)} collective-permute-done((bf16[16,7168]{1,0:T(8,128)(2,1)S(1)}, bf16[16,7168]{1,0:T(8,128)(2,1)S(1)}, u32[]{:S(2)}, u32[]{:S(2)}) %collective-permute-start.16) | collective-permute-done | bytes 229408 | tf_op jit(solution)/shard_map/ppermute | solution.py:26
  57.2 1.5 %collective-permute-done.18.refs_3_ = bf16[16,7168]{1,0:T(8,128)(2,1)S(1)} collective-permute-done((bf16[16,7168]{1,0:T(8,128)(2,1)S(1)}, bf16[16,7168]{1,0:T(8,128)(2,1)S(1)}, u32[]{:S(2)}, u32[]{:S(2)}) %collective-permute-start.18) | collective-permute-done | bytes 229408 | tf_op jit(solution)/shard_map/ppermute | solution.py:26
  58.7 2.4 %shard_map.81 = (bf16[16,7168]{1,0:T(8,128)(2,1)S(1)}, bf16[16,7168]{1,0:T(8,128)(2,1)S(1)}, bf16[16,7168]{1,0:T(8,128)(2,1)S(1)}, bf16[16,7168]{1,0:T(8,128)(2,1)S(1)}) custom-call(bf16[16,7168]{1,0:T(8,128)(2,1)S(1)} %shard_map.80.refs_0_, bf16[16,7168]{1,0:T(8,128)(2,1)S(1)} %collective-permute-done.16.refs_1_, ...), custom_call_target="tpu_custom_call" | custom-call | flops 704643072 | bytes 11010048 | tf_op jit(solution)/shard_map/pallas_call | solution.py:48
  61.1 0.2 collective-permute-start.20
  61.3 0.4 collective-permute-start.19
  61.7 1.0 %collective-permute-done.20.refs_1_ = bf16[16,7168]{1,0:T(8,128)(2,1)S(1)} collective-permute-done((bf16[16,7168]{1,0:T(8,128)(2,1)S(1)}, bf16[16,7168]{1,0:T(8,128)(2,1)S(1)}, u32[]{:S(2)}, u32[]{:S(2)}) %collective-permute-start.20) | collective-permute-done | bytes 229408 | tf_op jit(solution)/shard_map/ppermute | solution.py:26
  62.6 0.1 shard_map.82
  62.7 1.6 %collective-permute-start.21 = (bf16[16,7168]{1,0:T(8,128)(2,1)S(1)}, bf16[16,7168]{1,0:T(8,128)(2,1)S(1)}, u32[]{:S(2)}, u32[]{:S(2)}) collective-permute-start(bf16[16,7168]{1,0:T(8,128)(2,1)S(1)} %shard_map.82), channel_id=1, source_target_pairs={{0,2},{1,5},{2,0},{3,7},{4,6},{5,1},{6,4},{7,3},{8,10},{9,13},{10,... | collective-permute-start | bytes 688136 | tf_op jit(solution)/shard_map/ppermute | solution.py:26
  64.3 0.0 collective-permute-done.19.refs_1_
  64.3 4.5 %collective-permute-done.21.refs_2_ = bf16[16,7168]{1,0:T(8,128)(2,1)S(1)} collective-permute-done((bf16[16,7168]{1,0:T(8,128)(2,1)S(1)}, bf16[16,7168]{1,0:T(8,128)(2,1)S(1)}, u32[]{:S(2)}, u32[]{:S(2)}) %collective-permute-start.21) | collective-permute-done | bytes 229408 | tf_op jit(solution)/shard_map/ppermute | solution.py:26
  68.8 0.1 shard_map.83
  68.9 0.7 collective-permute-start.22
  69.6 1.1 %collective-permute-start.23 = (bf16[4,7168]{1,0:T(4,128)(2,1)S(1)}, bf16[4,7168]{1,0:T(4,128)(2,1)S(1)}, u32[]{:S(2)}, u32[]{:S(2)}) collective-permute-start(bf16[4,7168]{1,0:T(4,128)(2,1)S(1)} %get-tuple-element.56), channel_id=1, source_target_pairs={{0,20},{1,19},{2,22},{3,17},{4,16},{5,23},{6,18},{7,21},{8,28},{9,... | collective-permute-start | bytes 172040 | tf_op jit(solution)/shard_map/ppermute | solution.py:26
  70.7 3.0 %collective-permute-start.24 = (bf16[4,7168]{1,0:T(4,128)(2,1)S(1)}, bf16[4,7168]{1,0:T(4,128)(2,1)S(1)}, u32[]{:S(2)}, u32[]{:S(2)}) collective-permute-start(bf16[4,7168]{1,0:T(4,128)(2,1)S(1)} %get-tuple-element.57), channel_id=1, source_target_pairs={{0,24},{1,25},{2,26},{3,27},{4,28},{5,29},{6,30},{7,31},{8,16},{9,... | collective-permute-start | bytes 172040 | tf_op jit(solution)/shard_map/ppermute | solution.py:26
  73.6 2.1 %collective-permute-start.25 = (bf16[4,7168]{1,0:T(4,128)(2,1)S(1)}, bf16[4,7168]{1,0:T(4,128)(2,1)S(1)}, u32[]{:S(2)}, u32[]{:S(2)}) collective-permute-start(bf16[4,7168]{1,0:T(4,128)(2,1)S(1)} %get-tuple-element.58), channel_id=1, source_target_pairs={{0,28},{1,27},{2,30},{3,25},{4,24},{5,31},{6,26},{7,29},{8,20},{9,... | collective-permute-start | bytes 172040 | tf_op jit(solution)/shard_map/ppermute | solution.py:26
  75.7 0.0 collective-permute-done.22.refs_1_
  75.7 1.5 %collective-permute-done.24.refs_3_ = bf16[4,7168]{1,0:T(4,128)(2,1)S(1)} collective-permute-done((bf16[4,7168]{1,0:T(4,128)(2,1)S(1)}, bf16[4,7168]{1,0:T(4,128)(2,1)S(1)}, u32[]{:S(2)}, u32[]{:S(2)}) %collective-permute-start.24) | collective-permute-done | bytes 57376 | tf_op jit(solution)/shard_map/ppermute | solution.py:26
  77.2 3.3 %collective-permute-done.25.refs_4_ = bf16[4,7168]{1,0:T(4,128)(2,1)S(1)} collective-permute-done((bf16[4,7168]{1,0:T(4,128)(2,1)S(1)}, bf16[4,7168]{1,0:T(4,128)(2,1)S(1)}, u32[]{:S(2)}, u32[]{:S(2)}) %collective-permute-start.25) | collective-permute-done | bytes 57376 | tf_op jit(solution)/shard_map/ppermute | solution.py:26
  80.5 0.7 shard_map.84
  (10 shorter events, 0.0 us)
Async XLA Ops:
  0.0 0.8 %copy-start = (bf16[1,4,7168]{2,1,0:T(4,128)(2,1)S(1)}, bf16[1,4,7168]{2,1,0:T(4,128)(2,1)}, u32[]{:S(2)}) copy-start(bf16[1,4,7168]{2,1,0:T(4,128)(2,1)} %states_ref.1) | copy-start | bytes 172036
  0.8 0.7 copy-start.3
  1.5 0.7 copy-start.4
  2.3 18.5 %copy-start.2 = (f32[1,7168]{1,0:T(1,128)S(1)}, f32[1,7168]{1,0:T(1,128)}, u32[]{:S(2)}) copy-start(f32[1,7168]{1,0:T(1,128)} %refs_5_.1) | copy-start | bytes 86020
  2.3 10.0 %collective-permute-start.2 = (bf16[4,7296]{1,0:T(4,128)(2,1)S(1)}, bf16[4,7296]{1,0:T(4,128)(2,1)S(1)}, u32[]{:S(2)}, u32[]{:S(2)}) collective-permute-start(bf16[4,7296]{1,0:T(4,128)(2,1)S(1)} %shard_map.73.refs_0_), channel_id=1, source_target_pairs={{0,12},{1,11},{2,14},{3,9},{4,8},{5,15},{6,10},{7,13},{8,4},{9,3},... | collective-permute-start | bytes 175112 | tf_op jit(solution)/shard_map/ppermute | solution.py:26
  7.4 5.7 %collective-permute-start.1 = (bf16[4,7296]{1,0:T(4,128)(2,1)S(1)}, bf16[4,7296]{1,0:T(4,128)(2,1)S(1)}, u32[]{:S(2)}, u32[]{:S(2)}) collective-permute-start(bf16[4,7296]{1,0:T(4,128)(2,1)S(1)} %shard_map.73.refs_0_), channel_id=1, source_target_pairs={{0,8},{1,9},{2,10},{3,11},{4,12},{5,13},{6,14},{7,15},{8,0},{9,1},... | collective-permute-start | bytes 175112 | tf_op jit(solution)/shard_map/ppermute | solution.py:26
  7.4 5.7 %collective-permute-start = (bf16[4,7296]{1,0:T(4,128)(2,1)S(1)}, bf16[4,7296]{1,0:T(4,128)(2,1)S(1)}, u32[]{:S(2)}, u32[]{:S(2)}) collective-permute-start(bf16[4,7296]{1,0:T(4,128)(2,1)S(1)} %shard_map.73.refs_0_), channel_id=1, source_target_pairs={{0,4},{1,3},{2,6},{3,1},{4,0},{5,7},{6,2},{7,5},{8,12},{9,11},{10,... | collective-permute-start | bytes 175112 | tf_op jit(solution)/shard_map/ppermute | solution.py:26
  13.1 27.4 %copy-start.1 = (bf16[1,4,7168]{2,1,0:T(4,128)(2,1)S(1)}, bf16[1,4,7168]{2,1,0:T(4,128)(2,1)}, u32[]{:S(2)}) copy-start(bf16[1,4,7168]{2,1,0:T(4,128)(2,1)} %states_ref.1) | copy-start | bytes 172036
  13.2 6.1 %collective-permute-start.3 = (bf16[16,7296]{1,0:T(8,128)(2,1)S(1)}, bf16[16,7296]{1,0:T(8,128)(2,1)S(1)}, u32[]{:S(2)}, u32[]{:S(2)}) collective-permute-start(bf16[16,7296]{1,0:T(8,128)(2,1)S(1)} %shard_map.75.refs_0_), channel_id=1, source_target_pairs={{0,2},{1,5},{2,0},{3,7},{4,6},{5,1},{6,4},{7,3},{8,10},{9,13},{10,... | collective-permute-start | bytes 700424 | tf_op jit(solution)/shard_map/ppermute | solution.py:26
  14.1 5.1 %collective-permute-start.4 = (bf16[16,7296]{1,0:T(8,128)(2,1)S(1)}, bf16[16,7296]{1,0:T(8,128)(2,1)S(1)}, u32[]{:S(2)}, u32[]{:S(2)}) collective-permute-start(bf16[16,7296]{1,0:T(8,128)(2,1)S(1)} %shard_map.75.refs_0_), channel_id=1, source_target_pairs={{0,1},{1,0},{2,3},{3,2},{4,5},{5,4},{6,7},{7,6},{8,9},{9,8},{10,11... | collective-permute-start | bytes 700424 | tf_op jit(solution)/shard_map/ppermute | solution.py:26
  19.3 1.5 %collective-permute-start.5 = (bf16[16,7296]{1,0:T(8,128)(2,1)S(1)}, bf16[16,7296]{1,0:T(8,128)(2,1)S(1)}, u32[]{:S(2)}, u32[]{:S(2)}) collective-permute-start(bf16[16,7296]{1,0:T(8,128)(2,1)S(1)} %collective-permute-done.3.refs_1_), channel_id=1, source_target_pairs={{0,1},{1,0},{2,3},{3,2},{4,5},{5,4},{6,7},{7,6},{8,9},{9,8},{10,11... | collective-permute-start | bytes 700424 | tf_op jit(solution)/shard_map/ppermute | solution.py:26
  23.2 1.6 %collective-permute-start.7 = (bf16[16,7168]{1,0:T(8,128)(2,1)S(1)}, bf16[16,7168]{1,0:T(8,128)(2,1)S(1)}, u32[]{:S(2)}, u32[]{:S(2)}) collective-permute-start(bf16[16,7168]{1,0:T(8,128)(2,1)S(1)} %get-tuple-element.45), channel_id=1, source_target_pairs={{0,1},{1,0},{2,3},{3,2},{4,5},{5,4},{6,7},{7,6},{8,9},{9,8},{10,11... | collective-permute-start | bytes 688136 | tf_op jit(solution)/shard_map/ppermute | solution.py:26
  23.4 2.4 %collective-permute-start.6 = (bf16[16,7168]{1,0:T(8,128)(2,1)S(1)}, bf16[16,7168]{1,0:T(8,128)(2,1)S(1)}, u32[]{:S(2)}, u32[]{:S(2)}) collective-permute-start(bf16[16,7168]{1,0:T(8,128)(2,1)S(1)} %get-tuple-element.43), channel_id=1, source_target_pairs={{0,1},{1,0},{2,3},{3,2},{4,5},{5,4},{6,7},{7,6},{8,9},{9,8},{10,11... | collective-permute-start | bytes 688136 | tf_op jit(solution)/shard_map/ppermute | solution.py:26
  24.8 6.1 %collective-permute-start.8 = (bf16[16,7168]{1,0:T(8,128)(2,1)S(1)}, bf16[16,7168]{1,0:T(8,128)(2,1)S(1)}, u32[]{:S(2)}, u32[]{:S(2)}) collective-permute-start(bf16[16,7168]{1,0:T(8,128)(2,1)S(1)} %shard_map.77), channel_id=1, source_target_pairs={{0,2},{1,5},{2,0},{3,7},{4,6},{5,1},{6,4},{7,3},{8,10},{9,13},{10,... | collective-permute-start | bytes 688136 | tf_op jit(solution)/shard_map/ppermute | solution.py:26
  31.0 4.7 %collective-permute-start.9 = (bf16[4,7168]{1,0:T(4,128)(2,1)S(1)}, bf16[4,7168]{1,0:T(4,128)(2,1)S(1)}, u32[]{:S(2)}, u32[]{:S(2)}) collective-permute-start(bf16[4,7168]{1,0:T(4,128)(2,1)S(1)} %get-tuple-element.47), channel_id=1, source_target_pairs={{0,4},{1,3},{2,6},{3,1},{4,0},{5,7},{6,2},{7,5},{8,12},{9,11},{10,... | collective-permute-start | bytes 172040 | tf_op jit(solution)/shard_map/ppermute | solution.py:26
  31.7 6.8 %collective-permute-start.10 = (bf16[4,7168]{1,0:T(4,128)(2,1)S(1)}, bf16[4,7168]{1,0:T(4,128)(2,1)S(1)}, u32[]{:S(2)}, u32[]{:S(2)}) collective-permute-start(bf16[4,7168]{1,0:T(4,128)(2,1)S(1)} %get-tuple-element.48), channel_id=1, source_target_pairs={{0,8},{1,9},{2,10},{3,11},{4,12},{5,13},{6,14},{7,15},{8,0},{9,1},... | collective-permute-start | bytes 172040 | tf_op jit(solution)/shard_map/ppermute | solution.py:26
  34.6 6.0 %collective-permute-start.11 = (bf16[4,7168]{1,0:T(4,128)(2,1)S(1)}, bf16[4,7168]{1,0:T(4,128)(2,1)S(1)}, u32[]{:S(2)}, u32[]{:S(2)}) collective-permute-start(bf16[4,7168]{1,0:T(4,128)(2,1)S(1)} %get-tuple-element.49), channel_id=1, source_target_pairs={{0,12},{1,11},{2,14},{3,9},{4,8},{5,15},{6,10},{7,13},{8,4},{9,3},... | collective-permute-start | bytes 172040 | tf_op jit(solution)/shard_map/ppermute | solution.py:26
  40.6 7.0 %collective-permute-start.15 = (bf16[4,7168]{1,0:T(4,128)(2,1)S(1)}, bf16[4,7168]{1,0:T(4,128)(2,1)S(1)}, u32[]{:S(2)}, u32[]{:S(2)}) collective-permute-start(bf16[4,7168]{1,0:T(4,128)(2,1)S(1)} %shard_map.79.refs_0_), channel_id=1, source_target_pairs={{0,28},{1,27},{2,30},{3,25},{4,24},{5,31},{6,26},{7,29},{8,20},{9,... | collective-permute-start | bytes 172040 | tf_op jit(solution)/shard_map/ppermute | solution.py:26
  42.7 7.2 %collective-permute-start.14 = (bf16[4,7168]{1,0:T(4,128)(2,1)S(1)}, bf16[4,7168]{1,0:T(4,128)(2,1)S(1)}, u32[]{:S(2)}, u32[]{:S(2)}) collective-permute-start(bf16[4,7168]{1,0:T(4,128)(2,1)S(1)} %shard_map.79.refs_0_), channel_id=1, source_target_pairs={{0,24},{1,25},{2,26},{3,27},{4,28},{5,29},{6,30},{7,31},{8,16},{9,... | collective-permute-start | bytes 172040 | tf_op jit(solution)/shard_map/ppermute | solution.py:26
  42.9 7.0 %collective-permute-start.13 = (bf16[4,7168]{1,0:T(4,128)(2,1)S(1)}, bf16[4,7168]{1,0:T(4,128)(2,1)S(1)}, u32[]{:S(2)}, u32[]{:S(2)}) collective-permute-start(bf16[4,7168]{1,0:T(4,128)(2,1)S(1)} %shard_map.79.refs_0_), channel_id=1, source_target_pairs={{0,20},{1,19},{2,22},{3,17},{4,16},{5,23},{6,18},{7,21},{8,28},{9,... | collective-permute-start | bytes 172040 | tf_op jit(solution)/shard_map/ppermute | solution.py:26
  46.9 4.2 %collective-permute-start.12 = (bf16[4,7168]{1,0:T(4,128)(2,1)S(1)}, bf16[4,7168]{1,0:T(4,128)(2,1)S(1)}, u32[]{:S(2)}, u32[]{:S(2)}) collective-permute-start(bf16[4,7168]{1,0:T(4,128)(2,1)S(1)} %shard_map.79.refs_0_), channel_id=1, source_target_pairs={{0,16},{1,17},{2,18},{3,19},{4,20},{5,21},{6,22},{7,23},{8,24},{9,... | collective-permute-start | bytes 172040 | tf_op jit(solution)/shard_map/ppermute | solution.py:26
  51.1 6.1 %collective-permute-start.16 = (bf16[16,7168]{1,0:T(8,128)(2,1)S(1)}, bf16[16,7168]{1,0:T(8,128)(2,1)S(1)}, u32[]{:S(2)}, u32[]{:S(2)}) collective-permute-start(bf16[16,7168]{1,0:T(8,128)(2,1)S(1)} %shard_map.80.refs_0_), channel_id=1, source_target_pairs={{0,2},{1,5},{2,0},{3,7},{4,6},{5,1},{6,4},{7,3},{8,10},{9,13},{10,... | collective-permute-start | bytes 688136 | tf_op jit(solution)/shard_map/ppermute | solution.py:26
  52.7 4.5 %collective-permute-start.17 = (bf16[16,7168]{1,0:T(8,128)(2,1)S(1)}, bf16[16,7168]{1,0:T(8,128)(2,1)S(1)}, u32[]{:S(2)}, u32[]{:S(2)}) collective-permute-start(bf16[16,7168]{1,0:T(8,128)(2,1)S(1)} %shard_map.80.refs_0_), channel_id=1, source_target_pairs={{0,1},{1,0},{2,3},{3,2},{4,5},{5,4},{6,7},{7,6},{8,9},{9,8},{10,11... | collective-permute-start | bytes 688136 | tf_op jit(solution)/shard_map/ppermute | solution.py:26
  57.2 1.5 %collective-permute-start.18 = (bf16[16,7168]{1,0:T(8,128)(2,1)S(1)}, bf16[16,7168]{1,0:T(8,128)(2,1)S(1)}, u32[]{:S(2)}, u32[]{:S(2)}) collective-permute-start(bf16[16,7168]{1,0:T(8,128)(2,1)S(1)} %collective-permute-done.16.refs_1_), channel_id=1, source_target_pairs={{0,1},{1,0},{2,3},{3,2},{4,5},{5,4},{6,7},{7,6},{8,9},{9,8},{10,11... | collective-permute-start | bytes 688136 | tf_op jit(solution)/shard_map/ppermute | solution.py:26
  61.1 1.6 %collective-permute-start.20 = (bf16[16,7168]{1,0:T(8,128)(2,1)S(1)}, bf16[16,7168]{1,0:T(8,128)(2,1)S(1)}, u32[]{:S(2)}, u32[]{:S(2)}) collective-permute-start(bf16[16,7168]{1,0:T(8,128)(2,1)S(1)} %get-tuple-element.54), channel_id=1, source_target_pairs={{0,1},{1,0},{2,3},{3,2},{4,5},{5,4},{6,7},{7,6},{8,9},{9,8},{10,11... | collective-permute-start | bytes 688136 | tf_op jit(solution)/shard_map/ppermute | solution.py:26
  61.3 3.0 %collective-permute-start.19 = (bf16[16,7168]{1,0:T(8,128)(2,1)S(1)}, bf16[16,7168]{1,0:T(8,128)(2,1)S(1)}, u32[]{:S(2)}, u32[]{:S(2)}) collective-permute-start(bf16[16,7168]{1,0:T(8,128)(2,1)S(1)} %get-tuple-element.52), channel_id=1, source_target_pairs={{0,1},{1,0},{2,3},{3,2},{4,5},{5,4},{6,7},{7,6},{8,9},{9,8},{10,11... | collective-permute-start | bytes 688136 | tf_op jit(solution)/shard_map/ppermute | solution.py:26
  62.7 6.1 %collective-permute-start.21 = (bf16[16,7168]{1,0:T(8,128)(2,1)S(1)}, bf16[16,7168]{1,0:T(8,128)(2,1)S(1)}, u32[]{:S(2)}, u32[]{:S(2)}) collective-permute-start(bf16[16,7168]{1,0:T(8,128)(2,1)S(1)} %shard_map.82), channel_id=1, source_target_pairs={{0,2},{1,5},{2,0},{3,7},{4,6},{5,1},{6,4},{7,3},{8,10},{9,13},{10,... | collective-permute-start | bytes 688136 | tf_op jit(solution)/shard_map/ppermute | solution.py:26
  68.9 6.8 %collective-permute-start.22 = (bf16[4,7168]{1,0:T(4,128)(2,1)S(1)}, bf16[4,7168]{1,0:T(4,128)(2,1)S(1)}, u32[]{:S(2)}, u32[]{:S(2)}) collective-permute-start(bf16[4,7168]{1,0:T(4,128)(2,1)S(1)} %get-tuple-element.55), channel_id=1, source_target_pairs={{0,16},{1,17},{2,18},{3,19},{4,20},{5,21},{6,22},{7,23},{8,24},{9,... | collective-permute-start | bytes 172040 | tf_op jit(solution)/shard_map/ppermute | solution.py:26
  69.6 6.1 %collective-permute-start.23 = (bf16[4,7168]{1,0:T(4,128)(2,1)S(1)}, bf16[4,7168]{1,0:T(4,128)(2,1)S(1)}, u32[]{:S(2)}, u32[]{:S(2)}) collective-permute-start(bf16[4,7168]{1,0:T(4,128)(2,1)S(1)} %get-tuple-element.56), channel_id=1, source_target_pairs={{0,20},{1,19},{2,22},{3,17},{4,16},{5,23},{6,18},{7,21},{8,28},{9,... | collective-permute-start | bytes 172040 | tf_op jit(solution)/shard_map/ppermute | solution.py:26
  70.7 6.6 %collective-permute-start.24 = (bf16[4,7168]{1,0:T(4,128)(2,1)S(1)}, bf16[4,7168]{1,0:T(4,128)(2,1)S(1)}, u32[]{:S(2)}, u32[]{:S(2)}) collective-permute-start(bf16[4,7168]{1,0:T(4,128)(2,1)S(1)} %get-tuple-element.57), channel_id=1, source_target_pairs={{0,24},{1,25},{2,26},{3,27},{4,28},{5,29},{6,30},{7,31},{8,16},{9,... | collective-permute-start | bytes 172040 | tf_op jit(solution)/shard_map/ppermute | solution.py:26
  73.6 6.9 %collective-permute-start.25 = (bf16[4,7168]{1,0:T(4,128)(2,1)S(1)}, bf16[4,7168]{1,0:T(4,128)(2,1)S(1)}, u32[]{:S(2)}, u32[]{:S(2)}) collective-permute-start(bf16[4,7168]{1,0:T(4,128)(2,1)S(1)} %get-tuple-element.58), channel_id=1, source_target_pairs={{0,28},{1,27},{2,30},{3,25},{4,24},{5,31},{6,26},{7,29},{8,20},{9,... | collective-permute-start | bytes 172040 | tf_op jit(solution)/shard_map/ppermute | solution.py:26

commit v7 on v6

--- a/solution.py
+++ b/solution.py
@@ -26,18 +26,14 @@
     return lax.ppermute(value, ("segment", "expert"), pairs)
 
 
-def direct_flips(owners):
-    bits = [1 << place for place in range(1, owners.bit_length() - 1)]
-    even, odd = bits[1:], bits[:1] + bits[2:]
-    flips = []
-    for number in range(owners // 4):
-        chosen = [place for place in range(len(even)) if number >> place & 1]
-        flips.append((sum(even[place] for place in chosen), sum(odd[place] for place in chosen)))
-    return flips
-
-
+def upper_flips(owners):
+    return [(1 << place,) * 2 for place in range(owners.bit_length() - 2, 2, -1)]
+
+
+CORE = (1, 1)
+NEAR = (4, 2)
 BIG = (2, 4)
-CORE = (1, 1)
+STAY = (0, 0)
 
 
 def spans(dim):
@@ -80,7 +76,13 @@
     )(*[pltpu.with_memory_space_constraint(w, pltpu.HBM) for w in weights])
 
 
-def prepare_kernel(experts, states_ref, routing_ref, weight_ref, out_ref):
+def prepare_kernel(experts, states_hbm, routing_hbm, weight_hbm, out_ref, states_ref, routing_ref, weight_ref, sems):
+    pairs = ((routing_hbm, routing_ref), (weight_hbm, weight_ref), (states_hbm, states_ref))
+    copies = [pltpu.make_async_copy(source, target, sems.at[place]) for place, (source, target) in enumerate(pairs)]
+    for copy in copies:
+        copy.start()
+    for copy in copies:
+        copy.wait()
     rows, dim = states_ref.shape[1:]
     for span in spans(dim):
         out_ref[:, span] = states_ref[0, :, span]
@@ -96,6 +98,18 @@
             column = upright(routing_ref[0, step, k:k + 1, :]) + step * experts
             total += jnp.where(lane == column, upright(weight_ref[0, step, k:k + 1, :]), 0.0)
     out_ref[:, dim:] = total.astype(jnp.bfloat16)
+
+
+def prepare(experts, states, routing, weight):
+    args = [states, jnp.swapaxes(routing, 2, 3), jnp.swapaxes(weight, 2, 3)]
+    rows, dim = states.shape[1:]
+    (block,) = call(
+        functools.partial(prepare_kernel, experts), [(rows, dim + LANES)],
+        *[pltpu.with_memory_space_constraint(x, pltpu.HBM) for x in args],
+        in_specs=[pl.BlockSpec(memory_space=pltpu.HBM)] * 3,
+        scratch_shapes=[pltpu.VMEM(x.shape, x.dtype) for x in args] + [pltpu.SemaphoreType.DMA((3,))],
+    )
+    return block
 
 
 def join_kernel(*refs):
@@ -120,11 +134,21 @@
             out_ref[:, span] = total[place * rows:(place + 1) * rows].astype(jnp.bfloat16)
 
 
+def meet_kernel(rest_ref, near_ref, far_ref, out_ref, own_ref):
+    half = own_ref.shape[0]
+    for span in spans(out_ref.shape[1]):
+        far = far_ref[:, span].astype(jnp.float32)
+        total = rest_ref[:, span].astype(jnp.float32) + near_ref[:, span].astype(jnp.float32)
+        total = (total + jnp.concatenate([far[half:], far[:half]], axis=0)).astype(jnp.bfloat16)
+        out_ref[:, span] = total
+        own_ref[:, span] = total[:half]
+
+
 def mlp_kernel(step_no, *refs):
-    x_refs, refs = refs[:4], refs[4:]
+    x_refs, refs = refs[:8], refs[8:]
     if step_no > 0:
         tail_ref, refs = refs[0], refs[1:]
-    (gain_ref, gate_ref, up_ref, down_ref), outs, refs = refs[:4], refs[4:8], refs[8:]
+    (gain_ref, gate_ref, up_ref, down_ref), outs, refs = refs[:4], refs[4:12], refs[12:]
     rows_ref = refs[-1]
     part = outs[0].shape[0]
     dim, hidden = gate_ref.shape[1:]
@@ -149,8 +173,8 @@
             tail = tail_ref[band, :]
         chosen = jnp.where(lane == column, tail.astype(jnp.float32), 0.0)
         weights.append(jnp.sum(chosen, axis=1, keepdims=True))
-    gated = jnp.zeros((4 * part, hidden), jnp.float32)
-    up_part = jnp.zeros((4 * part, hidden), jnp.float32)
+    gated = jnp.zeros((8 * part, hidden), jnp.float32)
+    up_part = jnp.zeros((8 * part, hidden), jnp.float32)
     for span in spans(dim):
         rows = rows_ref[:, span]
         gated += jnp.dot(rows, gate_ref[0, span, :], preferred_element_type=jnp.float32)
@@ -171,54 +195,71 @@
     first = step_no == 0
     args = list(xs) + ([] if first else [tail]) + [gain, gate, up, down]
     result = call(
-        functools.partial(mlp_kernel, step_no), [(part, dim)] * 4 + [(4 * part, LANES)] * first, *args,
-        scratch_shapes=[pltpu.VMEM((4 * part, dim), jnp.bfloat16)],
+        functools.partial(mlp_kernel, step_no), [(part, dim)] * 8 + [(8 * part, LANES)] * first, *args,
+        scratch_shapes=[pltpu.VMEM((8 * part, dim), jnp.bfloat16)],
         cost_estimate=pl.CostEstimate(
-            flops=24 * part * dim * hidden, bytes_accessed=6 * dim * hidden, transcendentals=0
+            flops=48 * part * dim * hidden, bytes_accessed=6 * dim * hidden, transcendentals=0
         ),
     )
-    return result[:4], result[4] if first else tail
+    return result[:8], result[8] if first else tail
+
+
+def add(*parts):
+    rows = parts[0].shape[0]
+    dim = parts[-1].shape[1]
+    return call(add_kernel, [(rows, dim)], *parts)[0]
+
+
+def split(*parts):
+    rows, dim = parts[0].shape
+    return call(functools.partial(split_kernel, 2), [(rows // 2, dim)] * 2, *parts)
+
+
+def join(*parts):
+    return call(join_kernel, [(sum(part.shape[0] for part in parts), parts[0].shape[1])], *parts)[0]
 
 
 def on_device(states, routing, route_weight, norm_gain, gate_proj, up_proj, down_proj):
     owners = lax.axis_size("expert")
-    experts = owners // GROUP
     row_dev, dim = states.shape[1:]
     passes_count = routing.shape[1]
-    directs = direct_flips(owners)
-    part = len(directs) * row_dev
-
-    current, tail = states[0], None
-    gate, up, down = load((gate_proj, up_proj, down_proj))
-    (block,) = call(
-        functools.partial(prepare_kernel, experts), [(row_dev, dim + LANES)],
-        states, jnp.swapaxes(routing, 2, 3), jnp.swapaxes(route_weight, 2, 3),
-    )
+    top, *middle = upper_flips(owners)
+
+    weights = load((gate_proj, up_proj, down_proj))
+    block = prepare(owners // GROUP, states, routing, route_weight)
+    other = exchange(block, top, 0)
+    block, other, *weights = lax.optimization_barrier((block, other, *weights))
+    pair, own, tail = join(block, other), states[0], None
     for step_no in range(passes_count):
-        last = step_no == passes_count - 1
-        hop, out_hop = int(step_no > 0), int(last)
-        if step_no > 0:
-            block = current
-        blocks = [exchange(block, flips, hop) for flips in directs]
-        if step_no == 0:
-            blocks, gate, up, down = lax.optimization_barrier((blocks, gate, up, down))
-        (own_0,) = call(join_kernel, [(part, block.shape[1])], *blocks)
-        own_1 = exchange(own_0, BIG, 0)
-        far_0 = exchange(own_0, CORE, 0)
-        far_1 = exchange(own_1, CORE, 0)
-        xs = (own_0, own_1, far_0, far_1)
-        outs, tail = mlp(step_no, xs, tail, norm_gain, gate, up, down)
-        kept_0, kept_1, sent_0, sent_1 = outs
-
-        (half,) = call(add_kernel, [(part, dim)], kept_1, exchange(sent_1, CORE, 0))
-        near = exchange(sent_0, CORE, 0)
-        pieces = call(
-            functools.partial(split_kernel, len(directs)), [(row_dev, dim)] * len(directs),
-            kept_0, near, exchange(half, BIG, 0),
-        )
-        terms = [exchange(piece, flips, out_hop) for piece, flips in zip(pieces, directs)]
-        (current,) = call(add_kernel, [(row_dev, dim)], exchange(current, (0, 0), hop + out_hop), *terms)
-    return current[None]
+        rows_a = pair
+        for flips in middle:
+            rows_a = join(rows_a, exchange(rows_a, flips, 0))
+        rows_b = exchange(rows_a, NEAR, 0)
+        rows_c = exchange(rows_a, BIG, 0)
+        rows_d = exchange(rows_b, BIG, 0)
+        mine = [rows_a, rows_b, rows_c, rows_d]
+        outs, tail = mlp(step_no, mine + [exchange(rows, CORE, 0) for rows in mine], tail, norm_gain, *weights)
+
+        kept_a, kept_b, kept_c, kept_d = outs[:4]
+        far_a, far_b, far_c, far_d = [exchange(rows, CORE, 0) for rows in outs[4:]]
+        big_b = exchange(add(kept_d, far_d), BIG, 0)
+        big_a = exchange(add(kept_c, far_c), BIG, 0)
+        near_a = exchange(add(kept_b, far_b, big_b), NEAR, 0)
+        parts = [kept_a, far_a, big_a, near_a]
+        for flips in middle[::-1]:
+            low, high = split(*parts)
+            parts = [low, exchange(high, flips, 0)]
+        if step_no < passes_count - 1:
+            total = add(*parts)
+            rest = exchange(pair, STAY, 1)
+            pair, own = call(
+                meet_kernel, [(2 * row_dev, dim), (row_dev, dim)], rest, exchange(total, STAY, 1), exchange(total, top, 1)
+            )
+        else:
+            low, high = split(*parts)
+            rest = exchange(own, STAY, 1)
+            own = add(rest, exchange(low, STAY, 1), exchange(high, top, 1))
+    return own[None]
 
 
 def solution(mesh):

time: 81.4 us -> 77.5 us (0.952)
  local copies, waits for them, and re-layouts: 2.19 us -> 0.01 us
  starting transfers between devices: 30.1 us -> 28.4 us
    unnamed x10 -> x2, local copies, waits for them, and re-layouts: 2.19 us -> 0.01 us
    ppermute x26 -> x35, starting transfers between devices: 30.1 us -> 28.4 us  [exchange(): return lax.ppermute(value, ('segment', 'expert'), pairs)]
    pallas_call x11 -> x14, Pallas kernels: 6.01 us -> 6.81 us  [call(): pl.pallas_call(kernel, out_shape=[jax.ShapeDtypeStruct(shape, jnp.bfloat1...]
    ppermute x26 -> x35, waiting for transfers between devices: 38.5 us -> 37.8 us  [exchange(): return lax.ppermute(value, ('segment', 'expert'), pairs)]
  transfers between devices with their start and end apart: 26 -> 35, of which waited for: 17 -> 15; matrix products, arithmetic and copies ran while one was open for 0% -> 0% of each run, Pallas kernels for 5% -> 6%
where the time goes in v7:
time: 77.5 us; the launch traced here: 77.4 us
  waiting for transfers between devices  37.8 us (49%)
  starting transfers between devices  28.4 us (37%)
  Pallas kernels  11 us (14%)
    ppermute x35, waiting for transfers between devices, exchange(): return lax.ppermute(value, ('segment', 'expert'), pairs)  37.8 us
    ppermute x35, starting transfers between devices, exchange(): return lax.ppermute(value, ('segment', 'expert'), pairs)  28.4 us
    pallas_call x14, Pallas kernels, call(): pl.pallas_call(kernel, out_shape=[jax.ShapeDtypeStruct(shape, jnp.bfloat1...  6.81 us
    pallas_call x1, Pallas kernels, load(): pl.pallas_call(load_kernel, out_shape=[pltpu.VMEM(w.shape, w.dtype) for w...  4.23 us
  transfers between devices with their start and end apart: 35, of which 15 were waited for; matrix products, arithmetic and copies ran while one was open for 0% of the time, Pallas kernels for 6%

profile of v7, /device:TPU:0, one launch (start us, length us, event | category | flops | bytes accessed | tf_op | source)
XLA Modules:
  0.0 77.4 jit_solution(8714546139874789624)
XLA Ops:
  0.0 1.0 %shard_map.73.refs_0_ = bf16[4,7296]{1,0:T(4,128)(2,1)S(1)} custom-call(bf16[1,4,7168]{2,1,0:T(4,128)(2,1)} %states_hbm.1, s32[1,2,2,4]{3,2,1,0:T(2,128)} %bitcast.3, bf16[1,2,2,4]{3,2,1,0:T(2,128)(2,1)} %bitcast.4), custom_call_target="tpu_custom_call" | custom-call | tf_op jit(solution)/shard_map/pallas_call | solution.py:44
  1.0 0.0 copy-start
  1.0 4.1 %collective-permute-start = (bf16[4,7296]{1,0:T(4,128)(2,1)S(1)}, bf16[4,7296]{1,0:T(4,128)(2,1)S(1)}, u32[]{:S(2)}, u32[]{:S(2)}) collective-permute-start(bf16[4,7296]{1,0:T(4,128)(2,1)S(1)} %shard_map.73.refs_0_), channel_id=1, source_target_pairs={{0,8},{1,9},{2,10},{3,11},{4,12},{5,13},{6,14},{7,15},{8,0},{9,1},... | collective-permute-start | bytes 175112 | tf_op jit(solution)/shard_map/ppermute | solution.py:26
  5.1 4.2 %shard_map.74 = (bf16[1,7168,256]{2,1,0:T(8,128)(2,1)S(1)}, bf16[1,7168,256]{2,1,0:T(8,128)(2,1)S(1)}, bf16[1,256,7168]{2,1,0:T(8,128)(2,1)S(1)}) custom-call(bf16[1,7168,256]{2,1,0:T(8,128)(2,1)} %gate_ref.1, bf16[1,7168,256]{2,1,0:T(8,128)(2,1)} %up_ref.1, bf16[1,256,7168]{2,1,0:T(8,128)(2,1)} %down_ref.1), custom_call_target="tpu_custom_call" | custom-call | bytes 11010048 | tf_op jit(solution)/shard_map/pallas_call | solution.py:66
  9.3 0.0 collective-permute-done.refs_1_
  9.4 1.6 %collective-permute-start.2 = (bf16[8,7296]{1,0:T(8,128)(2,1)S(1)}, bf16[8,7296]{1,0:T(8,128)(2,1)S(1)}, u32[]{:S(2)}, u32[]{:S(2)}) collective-permute-start(bf16[8,7296]{1,0:T(8,128)(2,1)S(1)} %shard_map.75.refs_0_), channel_id=1, source_target_pairs={{0,4},{1,3},{2,6},{3,1},{4,0},{5,7},{6,2},{7,5},{8,12},{9,11},{10,... | collective-permute-start | bytes 350216 | tf_op jit(solution)/shard_map/ppermute | solution.py:26
  11.0 1.5 %collective-permute-start.3 = (bf16[8,7296]{1,0:T(8,128)(2,1)S(1)}, bf16[8,7296]{1,0:T(8,128)(2,1)S(1)}, u32[]{:S(2)}, u32[]{:S(2)}) collective-permute-start(bf16[8,7296]{1,0:T(8,128)(2,1)S(1)} %shard_map.75.refs_0_), channel_id=1, source_target_pairs={{0,2},{1,5},{2,0},{3,7},{4,6},{5,1},{6,4},{7,3},{8,10},{9,13},{10,... | collective-permute-start | bytes 350216 | tf_op jit(solution)/shard_map/ppermute | solution.py:26
  12.5 2.8 %collective-permute-done.2.refs_1_ = bf16[8,7296]{1,0:T(8,128)(2,1)S(1)} collective-permute-done((bf16[8,7296]{1,0:T(8,128)(2,1)S(1)}, bf16[8,7296]{1,0:T(8,128)(2,1)S(1)}, u32[]{:S(2)}, u32[]{:S(2)}) %collective-permute-start.2) | collective-permute-done | bytes 116768 | tf_op jit(solution)/shard_map/ppermute | solution.py:26
  15.3 0.5 collective-permute-start.4
  15.8 0.5 collective-permute-start.6
  16.3 0.0 collective-permute-done.3.refs_2_
  16.4 0.0 collective-permute-start.7
  16.4 3.8 %collective-permute-done.4.refs_3_ = bf16[8,7296]{1,0:T(8,128)(2,1)S(1)} collective-permute-done((bf16[8,7296]{1,0:T(8,128)(2,1)S(1)}, bf16[8,7296]{1,0:T(8,128)(2,1)S(1)}, u32[]{:S(2)}, u32[]{:S(2)}) %collective-permute-start.4) | collective-permute-done | bytes 116768 | tf_op jit(solution)/shard_map/ppermute | solution.py:26
  20.2 0.0 collective-permute-start.8
  20.2 0.0 collective-permute-done.5.refs_4_
  20.2 0.0 collective-permute-done.7.refs_6_
  20.2 0.0 collective-permute-done.6.refs_5_
  20.2 1.3 %collective-permute-done.8.refs_7_ = bf16[8,7296]{1,0:T(8,128)(2,1)S(1)} collective-permute-done((bf16[8,7296]{1,0:T(8,128)(2,1)S(1)}, bf16[8,7296]{1,0:T(8,128)(2,1)S(1)}, u32[]{:S(2)}, u32[]{:S(2)}) %collective-permute-start.8) | collective-permute-done | bytes 116768 | tf_op jit(solution)/shard_map/ppermute | solution.py:26
  21.5 2.4 %shard_map.76 = (bf16[8,7168]{1,0:T(8,128)(2,1)S(1)}, bf16[8,7168]{1,0:T(8,128)(2,1)S(1)}, bf16[8,7168]{1,0:T(8,128)(2,1)S(1)}, bf16[8,7168]{1,0:T(8,128)(2,1)S(...) custom-call(bf16[8,7296]{1,0:T(8,128)(2,1)S(1)} %shard_map.75.refs_0, ...), custom_call_target="tpu_custom_call" | custom-call | flops 704643072 | bytes 11010048 | tf_op jit(solution)/shard_map/pallas_call | solution.py:44
  23.9 0.2 collective-permute-start.13
  24.1 0.4 collective-permute-start.10
  24.4 0.1 collective-permute-start.12
  24.6 0.7 collective-permute-done.13.refs_1_
  25.3 0.6 collective-permute-start.14
  25.9 0.9 %collective-permute-start.9 = (bf16[8,7168]{1,0:T(8,128)(2,1)S(1)}, bf16[8,7168]{1,0:T(8,128)(2,1)S(1)}, u32[]{:S(2)}, u32[]{:S(2)}) collective-permute-start(bf16[8,7168]{1,0:T(8,128)(2,1)S(1)} %get-tuple-element.43), channel_id=1, source_target_pairs={{0,1},{1,0},{2,3},{3,2},{4,5},{5,4},{6,7},{7,6},{8,9},{9,8},{10,11... | collective-permute-start | bytes 344072 | tf_op jit(solution)/shard_map/ppermute | solution.py:26
  26.8 0.0 collective-permute-done.10.refs_1_
  26.8 0.6 collective-permute-start.11
  27.5 2.7 %collective-permute-done.14.refs_2_ = bf16[8,7168]{1,0:T(8,128)(2,1)S(1)} collective-permute-done((bf16[8,7168]{1,0:T(8,128)(2,1)S(1)}, bf16[8,7168]{1,0:T(8,128)(2,1)S(1)}, u32[]{:S(2)}, u32[]{:S(2)}) %collective-permute-start.14) | collective-permute-done | bytes 114720 | tf_op jit(solution)/shard_map/ppermute | solution.py:26
  30.2 1.6 %collective-permute-start.15 = (bf16[8,7168]{1,0:T(8,128)(2,1)S(1)}, bf16[8,7168]{1,0:T(8,128)(2,1)S(1)}, u32[]{:S(2)}, u32[]{:S(2)}) collective-permute-start(bf16[8,7168]{1,0:T(8,128)(2,1)S(1)} %shard_map.79), channel_id=1, source_target_pairs={{0,4},{1,3},{2,6},{3,1},{4,0},{5,7},{6,2},{7,5},{8,12},{9,11},{10,... | collective-permute-start | bytes 344072 | tf_op jit(solution)/shard_map/ppermute | solution.py:26
  31.8 1.5 %collective-permute-start.1 = (bf16[8,7296]{1,0:T(8,128)(2,1)S(1)}, bf16[8,7296]{1,0:T(8,128)(2,1)S(1)}, u32[]{:S(2)}, u32[]{:S(2)}) collective-permute-start(bf16[8,7296]{1,0:T(8,128)(2,1)S(1)} %shard_map.75.refs_0_), channel_id=1, source_target_pairs={{0,16},{1,17},{2,18},{3,19},{4,20},{5,21},{6,22},{7,23},{8,24},{9,... | collective-permute-start | bytes 350216 | tf_op jit(solution)/shard_map/ppermute | solution.py:26
  33.3 0.0 collective-permute-done.9.refs_1_
  33.3 0.0 collective-permute-done.11.refs_2_
  33.3 1.7 %collective-permute-done.15.refs_3_ = bf16[8,7168]{1,0:T(8,128)(2,1)S(1)} collective-permute-done((bf16[8,7168]{1,0:T(8,128)(2,1)S(1)}, bf16[8,7168]{1,0:T(8,128)(2,1)S(1)}, u32[]{:S(2)}, u32[]{:S(2)}) %collective-permute-start.15) | collective-permute-done | bytes 114720 | tf_op jit(solution)/shard_map/ppermute | solution.py:26
  35.1 0.1 shard_map.80
  35.1 1.9 %collective-permute-start.17 = (bf16[8,7168]{1,0:T(8,128)(2,1)S(1)}, bf16[8,7168]{1,0:T(8,128)(2,1)S(1)}, u32[]{:S(2)}, u32[]{:S(2)}) collective-permute-start(bf16[8,7168]{1,0:T(8,128)(2,1)S(1)} %shard_map.80), channel_id=1, source_target_pairs={{0,24},{1,25},{2,26},{3,27},{4,28},{5,29},{6,30},{7,31},{8,16},{9,... | collective-permute-start | bytes 344072 | tf_op jit(solution)/shard_map/ppermute | solution.py:26
  37.1 0.5 collective-permute-start.16
  37.6 5.4 %collective-permute-done.17.far_ref = bf16[8,7168]{1,0:T(8,128)(2,1)S(1)} collective-permute-done((bf16[8,7168]{1,0:T(8,128)(2,1)S(1)}, bf16[8,7168]{1,0:T(8,128)(2,1)S(1)}, u32[]{:S(2)}, u32[]{:S(2)}) %collective-permute-start.17) | collective-permute-done | bytes 114720 | tf_op jit(solution)/shard_map/ppermute | solution.py:26
  43.0 0.1 shard_map.81
  43.1 1.7 %collective-permute-start.19 = (bf16[8,7168]{1,0:T(8,128)(2,1)S(1)}, bf16[8,7168]{1,0:T(8,128)(2,1)S(1)}, u32[]{:S(2)}, u32[]{:S(2)}) collective-permute-start(bf16[8,7168]{1,0:T(8,128)(2,1)S(1)} %get-tuple-element.51.refs_0_), channel_id=1, source_target_pairs={{0,4},{1,3},{2,6},{3,1},{4,0},{5,7},{6,2},{7,5},{8,12},{9,11},{10,... | collective-permute-start | bytes 344072 | tf_op jit(solution)/shard_map/ppermute | solution.py:26
  44.8 0.5 collective-permute-start.20
  45.3 3.5 %collective-permute-done.19.refs_1_ = bf16[8,7168]{1,0:T(8,128)(2,1)S(1)} collective-permute-done((bf16[8,7168]{1,0:T(8,128)(2,1)S(1)}, bf16[8,7168]{1,0:T(8,128)(2,1)S(1)}, u32[]{:S(2)}, u32[]{:S(2)}) %collective-permute-start.19) | collective-permute-done | bytes 114720 | tf_op jit(solution)/shard_map/ppermute | solution.py:26
  48.8 0.5 collective-permute-start.21
  49.3 0.5 collective-permute-start.23
  49.8 0.0 collective-permute-start.24
  49.8 3.8 %collective-permute-done.21.refs_3_ = bf16[8,7168]{1,0:T(8,128)(2,1)S(1)} collective-permute-done((bf16[8,7168]{1,0:T(8,128)(2,1)S(1)}, bf16[8,7168]{1,0:T(8,128)(2,1)S(1)}, u32[]{:S(2)}, u32[]{:S(2)}) %collective-permute-start.21) | collective-permute-done | bytes 114720 | tf_op jit(solution)/shard_map/ppermute | solution.py:26
  53.6 1.3 %collective-permute-done.25.refs_7_ = bf16[8,7168]{1,0:T(8,128)(2,1)S(1)} collective-permute-done((bf16[8,7168]{1,0:T(8,128)(2,1)S(1)}, bf16[8,7168]{1,0:T(8,128)(2,1)S(1)}, u32[]{:S(2)}, u32[]{:S(2)}) %collective-permute-start.25) | collective-permute-done | bytes 114720 | tf_op jit(solution)/shard_map/ppermute | solution.py:26
  54.9 2.4 %shard_map.82 = (bf16[8,7168]{1,0:T(8,128)(2,1)S(1)}, bf16[8,7168]{1,0:T(8,128)(2,1)S(1)}, bf16[8,7168]{1,0:T(8,128)(2,1)S(1)}, bf16[8,7168]{1,0:T(8,128)(2,1)S(...) custom-call(bf16[8,7168]{1,0:T(8,128)(2,1)S(1)} %get-tuple-element.5, ...), custom_call_target="tpu_custom_call" | custom-call | flops 704643072 | bytes 11010048 | tf_op jit(solution)/shard_map/pallas_call | solution.py:44
  57.3 0.2 collective-permute-start.30
  57.5 0.4 collective-permute-start.27
  57.9 0.1 collective-permute-start.29
  58.0 0.7 collective-permute-done.30.refs_1_
  58.7 0.6 collective-permute-start.31
  59.3 0.9 %collective-permute-start.26 = (bf16[8,7168]{1,0:T(8,128)(2,1)S(1)}, bf16[8,7168]{1,0:T(8,128)(2,1)S(1)}, u32[]{:S(2)}, u32[]{:S(2)}) collective-permute-start(bf16[8,7168]{1,0:T(8,128)(2,1)S(1)} %get-tuple-element.54), channel_id=1, source_target_pairs={{0,1},{1,0},{2,3},{3,2},{4,5},{5,4},{6,7},{7,6},{8,9},{9,8},{10,11... | collective-permute-start | bytes 344072 | tf_op jit(solution)/shard_map/ppermute | solution.py:26
  60.2 0.7 collective-permute-start.28
  61.0 2.6 %collective-permute-done.31.refs_2_ = bf16[8,7168]{1,0:T(8,128)(2,1)S(1)} collective-permute-done((bf16[8,7168]{1,0:T(8,128)(2,1)S(1)}, bf16[8,7168]{1,0:T(8,128)(2,1)S(1)}, u32[]{:S(2)}, u32[]{:S(2)}) %collective-permute-start.31) | collective-permute-done | bytes 114720 | tf_op jit(solution)/shard_map/ppermute | solution.py:26
  63.6 1.6 %collective-permute-start.32 = (bf16[8,7168]{1,0:T(8,128)(2,1)S(1)}, bf16[8,7168]{1,0:T(8,128)(2,1)S(1)}, u32[]{:S(2)}, u32[]{:S(2)}) collective-permute-start(bf16[8,7168]{1,0:T(8,128)(2,1)S(1)} %shard_map.85), channel_id=1, source_target_pairs={{0,4},{1,3},{2,6},{3,1},{4,0},{5,7},{6,2},{7,5},{8,12},{9,11},{10,... | collective-permute-start | bytes 344072 | tf_op jit(solution)/shard_map/ppermute | solution.py:26
  65.2 0.5 collective-permute-start.18
  65.8 2.7 %collective-permute-done.32.refs_3_ = bf16[8,7168]{1,0:T(8,128)(2,1)S(1)} collective-permute-done((bf16[8,7168]{1,0:T(8,128)(2,1)S(1)}, bf16[8,7168]{1,0:T(8,128)(2,1)S(1)}, u32[]{:S(2)}, u32[]{:S(2)}) %collective-permute-start.32) | collective-permute-done | bytes 114720 | tf_op jit(solution)/shard_map/ppermute | solution.py:26
  68.5 0.1 shard_map.86
  68.6 1.7 %collective-permute-start.33 = (bf16[4,7168]{1,0:T(4,128)(2,1)S(1)}, bf16[4,7168]{1,0:T(4,128)(2,1)S(1)}, u32[]{:S(2)}, u32[]{:S(2)}) collective-permute-start(bf16[4,7168]{1,0:T(4,128)(2,1)S(1)} %get-tuple-element.61), channel_id=1, source_target_pairs={{0,16},{1,17},{2,18},{3,19},{4,20},{5,21},{6,22},{7,23},{8,24},{9,... | collective-permute-start | bytes 172040 | tf_op jit(solution)/shard_map/ppermute | solution.py:26
  70.2 1.7 %collective-permute-start.34 = (bf16[4,7168]{1,0:T(4,128)(2,1)S(1)}, bf16[4,7168]{1,0:T(4,128)(2,1)S(1)}, u32[]{:S(2)}, u32[]{:S(2)}) collective-permute-start(bf16[4,7168]{1,0:T(4,128)(2,1)S(1)} %get-tuple-element.62), channel_id=1, source_target_pairs={{0,24},{1,25},{2,26},{3,27},{4,28},{5,29},{6,30},{7,31},{8,16},{9,... | collective-permute-start | bytes 172040 | tf_op jit(solution)/shard_map/ppermute | solution.py:26
  71.9 0.9 %collective-permute-done.33.refs_1_ = bf16[4,7168]{1,0:T(4,128)(2,1)S(1)} collective-permute-done((bf16[4,7168]{1,0:T(4,128)(2,1)S(1)}, bf16[4,7168]{1,0:T(4,128)(2,1)S(1)}, u32[]{:S(2)}, u32[]{:S(2)}) %collective-permute-start.33) | collective-permute-done | bytes 57376 | tf_op jit(solution)/shard_map/ppermute | solution.py:26
  72.9 3.9 %collective-permute-done.34.refs_2_ = bf16[4,7168]{1,0:T(4,128)(2,1)S(1)} collective-permute-done((bf16[4,7168]{1,0:T(4,128)(2,1)S(1)}, bf16[4,7168]{1,0:T(4,128)(2,1)S(1)}, u32[]{:S(2)}, u32[]{:S(2)}) %collective-permute-start.34) | collective-permute-done | bytes 57376 | tf_op jit(solution)/shard_map/ppermute | solution.py:26
  76.7 0.7 shard_map.87
  (23 shorter events, 0.3 us)
Async XLA Ops:
  1.0 20.5 %copy-start = (f32[1,7168]{1,0:T(1,128)S(1)}, f32[1,7168]{1,0:T(1,128)}, u32[]{:S(2)}) copy-start(f32[1,7168]{1,0:T(1,128)} %refs_9_.1) | copy-start | bytes 86020
  1.0 8.3 %collective-permute-start = (bf16[4,7296]{1,0:T(4,128)(2,1)S(1)}, bf16[4,7296]{1,0:T(4,128)(2,1)S(1)}, u32[]{:S(2)}, u32[]{:S(2)}) collective-permute-start(bf16[4,7296]{1,0:T(4,128)(2,1)S(1)} %shard_map.73.refs_0_), channel_id=1, source_target_pairs={{0,8},{1,9},{2,10},{3,11},{4,12},{5,13},{6,14},{7,15},{8,0},{9,1},... | collective-permute-start | bytes 175112 | tf_op jit(solution)/shard_map/ppermute | solution.py:26
  9.4 6.0 %collective-permute-start.2 = (bf16[8,7296]{1,0:T(8,128)(2,1)S(1)}, bf16[8,7296]{1,0:T(8,128)(2,1)S(1)}, u32[]{:S(2)}, u32[]{:S(2)}) collective-permute-start(bf16[8,7296]{1,0:T(8,128)(2,1)S(1)} %shard_map.75.refs_0_), channel_id=1, source_target_pairs={{0,4},{1,3},{2,6},{3,1},{4,0},{5,7},{6,2},{7,5},{8,12},{9,11},{10,... | collective-permute-start | bytes 350216 | tf_op jit(solution)/shard_map/ppermute | solution.py:26
  11.0 5.3 %collective-permute-start.3 = (bf16[8,7296]{1,0:T(8,128)(2,1)S(1)}, bf16[8,7296]{1,0:T(8,128)(2,1)S(1)}, u32[]{:S(2)}, u32[]{:S(2)}) collective-permute-start(bf16[8,7296]{1,0:T(8,128)(2,1)S(1)} %shard_map.75.refs_0_), channel_id=1, source_target_pairs={{0,2},{1,5},{2,0},{3,7},{4,6},{5,1},{6,4},{7,3},{8,10},{9,13},{10,... | collective-permute-start | bytes 350216 | tf_op jit(solution)/shard_map/ppermute | solution.py:26
  15.3 4.8 %collective-permute-start.4 = (bf16[8,7296]{1,0:T(8,128)(2,1)S(1)}, bf16[8,7296]{1,0:T(8,128)(2,1)S(1)}, u32[]{:S(2)}, u32[]{:S(2)}) collective-permute-start(bf16[8,7296]{1,0:T(8,128)(2,1)S(1)} %collective-permute-done.2.refs_1_), channel_id=1, source_target_pairs={{0,2},{1,5},{2,0},{3,7},{4,6},{5,1},{6,4},{7,3},{8,10},{9,13},{10,... | collective-permute-start | bytes 350216 | tf_op jit(solution)/shard_map/ppermute | solution.py:26
  15.8 4.3 %collective-permute-start.5 = (bf16[8,7296]{1,0:T(8,128)(2,1)S(1)}, bf16[8,7296]{1,0:T(8,128)(2,1)S(1)}, u32[]{:S(2)}, u32[]{:S(2)}) collective-permute-start(bf16[8,7296]{1,0:T(8,128)(2,1)S(1)} %shard_map.75.refs_0_), channel_id=1, source_target_pairs={{0,1},{1,0},{2,3},{3,2},{4,5},{5,4},{6,7},{7,6},{8,9},{9,8},{10,11... | collective-permute-start | bytes 350216 | tf_op jit(solution)/shard_map/ppermute | solution.py:26
  15.8 4.3 %collective-permute-start.6 = (bf16[8,7296]{1,0:T(8,128)(2,1)S(1)}, bf16[8,7296]{1,0:T(8,128)(2,1)S(1)}, u32[]{:S(2)}, u32[]{:S(2)}) collective-permute-start(bf16[8,7296]{1,0:T(8,128)(2,1)S(1)} %collective-permute-done.2.refs_1_), channel_id=1, source_target_pairs={{0,1},{1,0},{2,3},{3,2},{4,5},{5,4},{6,7},{7,6},{8,9},{9,8},{10,11... | collective-permute-start | bytes 350216 | tf_op jit(solution)/shard_map/ppermute | solution.py:26
  16.4 3.8 %collective-permute-start.7 = (bf16[8,7296]{1,0:T(8,128)(2,1)S(1)}, bf16[8,7296]{1,0:T(8,128)(2,1)S(1)}, u32[]{:S(2)}, u32[]{:S(2)}) collective-permute-start(bf16[8,7296]{1,0:T(8,128)(2,1)S(1)} %collective-permute-done.3.refs_2_), channel_id=1, source_target_pairs={{0,1},{1,0},{2,3},{3,2},{4,5},{5,4},{6,7},{7,6},{8,9},{9,8},{10,11... | collective-permute-start | bytes 350216 | tf_op jit(solution)/shard_map/ppermute | solution.py:26
  20.2 1.3 %collective-permute-start.8 = (bf16[8,7296]{1,0:T(8,128)(2,1)S(1)}, bf16[8,7296]{1,0:T(8,128)(2,1)S(1)}, u32[]{:S(2)}, u32[]{:S(2)}) collective-permute-start(bf16[8,7296]{1,0:T(8,128)(2,1)S(1)} %collective-permute-done.4.refs_3_), channel_id=1, source_target_pairs={{0,1},{1,0},{2,3},{3,2},{4,5},{5,4},{6,7},{7,6},{8,9},{9,8},{10,11... | collective-permute-start | bytes 350216 | tf_op jit(solution)/shard_map/ppermute | solution.py:26
  23.9 1.4 %collective-permute-start.13 = (bf16[8,7168]{1,0:T(8,128)(2,1)S(1)}, bf16[8,7168]{1,0:T(8,128)(2,1)S(1)}, u32[]{:S(2)}, u32[]{:S(2)}) collective-permute-start(bf16[8,7168]{1,0:T(8,128)(2,1)S(1)} %get-tuple-element.49), channel_id=1, source_target_pairs={{0,1},{1,0},{2,3},{3,2},{4,5},{5,4},{6,7},{7,6},{8,9},{9,8},{10,11... | collective-permute-start | bytes 344072 | tf_op jit(solution)/shard_map/ppermute | solution.py:26
  24.1 2.7 %collective-permute-start.10 = (bf16[8,7168]{1,0:T(8,128)(2,1)S(1)}, bf16[8,7168]{1,0:T(8,128)(2,1)S(1)}, u32[]{:S(2)}, u32[]{:S(2)}) collective-permute-start(bf16[8,7168]{1,0:T(8,128)(2,1)S(1)} %get-tuple-element.45), channel_id=1, source_target_pairs={{0,1},{1,0},{2,3},{3,2},{4,5},{5,4},{6,7},{7,6},{8,9},{9,8},{10,11... | collective-permute-start | bytes 344072 | tf_op jit(solution)/shard_map/ppermute | solution.py:26
  24.4 3.0 %collective-permute-start.12 = (bf16[8,7168]{1,0:T(8,128)(2,1)S(1)}, bf16[8,7168]{1,0:T(8,128)(2,1)S(1)}, u32[]{:S(2)}, u32[]{:S(2)}) collective-permute-start(bf16[8,7168]{1,0:T(8,128)(2,1)S(1)} %get-tuple-element.47), channel_id=1, source_target_pairs={{0,1},{1,0},{2,3},{3,2},{4,5},{5,4},{6,7},{7,6},{8,9},{9,8},{10,11... | collective-permute-start | bytes 344072 | tf_op jit(solution)/shard_map/ppermute | solution.py:26
  25.3 4.9 %collective-permute-start.14 = (bf16[8,7168]{1,0:T(8,128)(2,1)S(1)}, bf16[8,7168]{1,0:T(8,128)(2,1)S(1)}, u32[]{:S(2)}, u32[]{:S(2)}) collective-permute-start(bf16[8,7168]{1,0:T(8,128)(2,1)S(1)} %shard_map.78), channel_id=1, source_target_pairs={{0,2},{1,5},{2,0},{3,7},{4,6},{5,1},{6,4},{7,3},{8,10},{9,13},{10,... | collective-permute-start | bytes 344072 | tf_op jit(solution)/shard_map/ppermute | solution.py:26
  25.9 7.5 %collective-permute-start.9 = (bf16[8,7168]{1,0:T(8,128)(2,1)S(1)}, bf16[8,7168]{1,0:T(8,128)(2,1)S(1)}, u32[]{:S(2)}, u32[]{:S(2)}) collective-permute-start(bf16[8,7168]{1,0:T(8,128)(2,1)S(1)} %get-tuple-element.43), channel_id=1, source_target_pairs={{0,1},{1,0},{2,3},{3,2},{4,5},{5,4},{6,7},{7,6},{8,9},{9,8},{10,11... | collective-permute-start | bytes 344072 | tf_op jit(solution)/shard_map/ppermute | solution.py:26
  26.8 6.5 %collective-permute-start.11 = (bf16[8,7168]{1,0:T(8,128)(2,1)S(1)}, bf16[8,7168]{1,0:T(8,128)(2,1)S(1)}, u32[]{:S(2)}, u32[]{:S(2)}) collective-permute-start(bf16[8,7168]{1,0:T(8,128)(2,1)S(1)} %shard_map.77), channel_id=1, source_target_pairs={{0,2},{1,5},{2,0},{3,7},{4,6},{5,1},{6,4},{7,3},{8,10},{9,13},{10,... | collective-permute-start | bytes 344072 | tf_op jit(solution)/shard_map/ppermute | solution.py:26
  30.2 4.9 %collective-permute-start.15 = (bf16[8,7168]{1,0:T(8,128)(2,1)S(1)}, bf16[8,7168]{1,0:T(8,128)(2,1)S(1)}, u32[]{:S(2)}, u32[]{:S(2)}) collective-permute-start(bf16[8,7168]{1,0:T(8,128)(2,1)S(1)} %shard_map.79), channel_id=1, source_target_pairs={{0,4},{1,3},{2,6},{3,1},{4,0},{5,7},{6,2},{7,5},{8,12},{9,11},{10,... | collective-permute-start | bytes 344072 | tf_op jit(solution)/shard_map/ppermute | solution.py:26
  31.8 5.8 %collective-permute-start.1 = (bf16[8,7296]{1,0:T(8,128)(2,1)S(1)}, bf16[8,7296]{1,0:T(8,128)(2,1)S(1)}, u32[]{:S(2)}, u32[]{:S(2)}) collective-permute-start(bf16[8,7296]{1,0:T(8,128)(2,1)S(1)} %shard_map.75.refs_0_), channel_id=1, source_target_pairs={{0,16},{1,17},{2,18},{3,19},{4,20},{5,21},{6,22},{7,23},{8,24},{9,... | collective-permute-start | bytes 350216 | tf_op jit(solution)/shard_map/ppermute | solution.py:26
  35.1 7.9 %collective-permute-start.17 = (bf16[8,7168]{1,0:T(8,128)(2,1)S(1)}, bf16[8,7168]{1,0:T(8,128)(2,1)S(1)}, u32[]{:S(2)}, u32[]{:S(2)}) collective-permute-start(bf16[8,7168]{1,0:T(8,128)(2,1)S(1)} %shard_map.80), channel_id=1, source_target_pairs={{0,24},{1,25},{2,26},{3,27},{4,28},{5,29},{6,30},{7,31},{8,16},{9,... | collective-permute-start | bytes 344072 | tf_op jit(solution)/shard_map/ppermute | solution.py:26
  37.1 6.0 %collective-permute-start.16 = (bf16[8,7168]{1,0:T(8,128)(2,1)S(1)}, bf16[8,7168]{1,0:T(8,128)(2,1)S(1)}, u32[]{:S(2)}, u32[]{:S(2)}) collective-permute-start(bf16[8,7168]{1,0:T(8,128)(2,1)S(1)} %shard_map.80), channel_id=1, source_target_pairs={{0,16},{1,17},{2,18},{3,19},{4,20},{5,21},{6,22},{7,23},{8,24},{9,... | collective-permute-start | bytes 344072 | tf_op jit(solution)/shard_map/ppermute | solution.py:26
  43.1 5.8 %collective-permute-start.19 = (bf16[8,7168]{1,0:T(8,128)(2,1)S(1)}, bf16[8,7168]{1,0:T(8,128)(2,1)S(1)}, u32[]{:S(2)}, u32[]{:S(2)}) collective-permute-start(bf16[8,7168]{1,0:T(8,128)(2,1)S(1)} %get-tuple-element.51.refs_0_), channel_id=1, source_target_pairs={{0,4},{1,3},{2,6},{3,1},{4,0},{5,7},{6,2},{7,5},{8,12},{9,11},{10,... | collective-permute-start | bytes 344072 | tf_op jit(solution)/shard_map/ppermute | solution.py:26
  44.8 5.0 %collective-permute-start.20 = (bf16[8,7168]{1,0:T(8,128)(2,1)S(1)}, bf16[8,7168]{1,0:T(8,128)(2,1)S(1)}, u32[]{:S(2)}, u32[]{:S(2)}) collective-permute-start(bf16[8,7168]{1,0:T(8,128)(2,1)S(1)} %get-tuple-element.51.refs_0_), channel_id=1, source_target_pairs={{0,2},{1,5},{2,0},{3,7},{4,6},{5,1},{6,4},{7,3},{8,10},{9,13},{10,... | collective-permute-start | bytes 344072 | tf_op jit(solution)/shard_map/ppermute | solution.py:26
  48.8 4.8 %collective-permute-start.21 = (bf16[8,7168]{1,0:T(8,128)(2,1)S(1)}, bf16[8,7168]{1,0:T(8,128)(2,1)S(1)}, u32[]{:S(2)}, u32[]{:S(2)}) collective-permute-start(bf16[8,7168]{1,0:T(8,128)(2,1)S(1)} %collective-permute-done.19.refs_1_), channel_id=1, source_target_pairs={{0,2},{1,5},{2,0},{3,7},{4,6},{5,1},{6,4},{7,3},{8,10},{9,13},{10,... | collective-permute-start | bytes 344072 | tf_op jit(solution)/shard_map/ppermute | solution.py:26
  49.3 4.3 %collective-permute-start.22 = (bf16[8,7168]{1,0:T(8,128)(2,1)S(1)}, bf16[8,7168]{1,0:T(8,128)(2,1)S(1)}, u32[]{:S(2)}, u32[]{:S(2)}) collective-permute-start(bf16[8,7168]{1,0:T(8,128)(2,1)S(1)} %get-tuple-element.51.refs_0_), channel_id=1, source_target_pairs={{0,1},{1,0},{2,3},{3,2},{4,5},{5,4},{6,7},{7,6},{8,9},{9,8},{10,11... | collective-permute-start | bytes 344072 | tf_op jit(solution)/shard_map/ppermute | solution.py:26
  49.3 4.3 %collective-permute-start.23 = (bf16[8,7168]{1,0:T(8,128)(2,1)S(1)}, bf16[8,7168]{1,0:T(8,128)(2,1)S(1)}, u32[]{:S(2)}, u32[]{:S(2)}) collective-permute-start(bf16[8,7168]{1,0:T(8,128)(2,1)S(1)} %collective-permute-done.19.refs_1_), channel_id=1, source_target_pairs={{0,1},{1,0},{2,3},{3,2},{4,5},{5,4},{6,7},{7,6},{8,9},{9,8},{10,11... | collective-permute-start | bytes 344072 | tf_op jit(solution)/shard_map/ppermute | solution.py:26
  49.8 3.8 %collective-permute-start.24 = (bf16[8,7168]{1,0:T(8,128)(2,1)S(1)}, bf16[8,7168]{1,0:T(8,128)(2,1)S(1)}, u32[]{:S(2)}, u32[]{:S(2)}) collective-permute-start(bf16[8,7168]{1,0:T(8,128)(2,1)S(1)} %collective-permute-done.20.refs_2_), channel_id=1, source_target_pairs={{0,1},{1,0},{2,3},{3,2},{4,5},{5,4},{6,7},{7,6},{8,9},{9,8},{10,11... | collective-permute-start | bytes 344072 | tf_op jit(solution)/shard_map/ppermute | solution.py:26
  53.6 1.3 %collective-permute-start.25 = (bf16[8,7168]{1,0:T(8,128)(2,1)S(1)}, bf16[8,7168]{1,0:T(8,128)(2,1)S(1)}, u32[]{:S(2)}, u32[]{:S(2)}) collective-permute-start(bf16[8,7168]{1,0:T(8,128)(2,1)S(1)} %collective-permute-done.21.refs_3_), channel_id=1, source_target_pairs={{0,1},{1,0},{2,3},{3,2},{4,5},{5,4},{6,7},{7,6},{8,9},{9,8},{10,11... | collective-permute-start | bytes 344072 | tf_op jit(solution)/shard_map/ppermute | solution.py:26
  57.3 1.4 %collective-permute-start.30 = (bf16[8,7168]{1,0:T(8,128)(2,1)S(1)}, bf16[8,7168]{1,0:T(8,128)(2,1)S(1)}, u32[]{:S(2)}, u32[]{:S(2)}) collective-permute-start(bf16[8,7168]{1,0:T(8,128)(2,1)S(1)} %get-tuple-element.60), channel_id=1, source_target_pairs={{0,1},{1,0},{2,3},{3,2},{4,5},{5,4},{6,7},{7,6},{8,9},{9,8},{10,11... | collective-permute-start | bytes 344072 | tf_op jit(solution)/shard_map/ppermute | solution.py:26
  57.5 2.7 %collective-permute-start.27 = (bf16[8,7168]{1,0:T(8,128)(2,1)S(1)}, bf16[8,7168]{1,0:T(8,128)(2,1)S(1)}, u32[]{:S(2)}, u32[]{:S(2)}) collective-permute-start(bf16[8,7168]{1,0:T(8,128)(2,1)S(1)} %get-tuple-element.56), channel_id=1, source_target_pairs={{0,1},{1,0},{2,3},{3,2},{4,5},{5,4},{6,7},{7,6},{8,9},{9,8},{10,11... | collective-permute-start | bytes 344072 | tf_op jit(solution)/shard_map/ppermute | solution.py:26
  57.9 3.1 %collective-permute-start.29 = (bf16[8,7168]{1,0:T(8,128)(2,1)S(1)}, bf16[8,7168]{1,0:T(8,128)(2,1)S(1)}, u32[]{:S(2)}, u32[]{:S(2)}) collective-permute-start(bf16[8,7168]{1,0:T(8,128)(2,1)S(1)} %get-tuple-element.58), channel_id=1, source_target_pairs={{0,1},{1,0},{2,3},{3,2},{4,5},{5,4},{6,7},{7,6},{8,9},{9,8},{10,11... | collective-permute-start | bytes 344072 | tf_op jit(solution)/shard_map/ppermute | solution.py:26
  58.7 4.9 %collective-permute-start.31 = (bf16[8,7168]{1,0:T(8,128)(2,1)S(1)}, bf16[8,7168]{1,0:T(8,128)(2,1)S(1)}, u32[]{:S(2)}, u32[]{:S(2)}) collective-permute-start(bf16[8,7168]{1,0:T(8,128)(2,1)S(1)} %shard_map.84), channel_id=1, source_target_pairs={{0,2},{1,5},{2,0},{3,7},{4,6},{5,1},{6,4},{7,3},{8,10},{9,13},{10,... | collective-permute-start | bytes 344072 | tf_op jit(solution)/shard_map/ppermute | solution.py:26
  59.3 6.5 %collective-permute-start.26 = (bf16[8,7168]{1,0:T(8,128)(2,1)S(1)}, bf16[8,7168]{1,0:T(8,128)(2,1)S(1)}, u32[]{:S(2)}, u32[]{:S(2)}) collective-permute-start(bf16[8,7168]{1,0:T(8,128)(2,1)S(1)} %get-tuple-element.54), channel_id=1, source_target_pairs={{0,1},{1,0},{2,3},{3,2},{4,5},{5,4},{6,7},{7,6},{8,9},{9,8},{10,11... | collective-permute-start | bytes 344072 | tf_op jit(solution)/shard_map/ppermute | solution.py:26
  60.2 5.5 %collective-permute-start.28 = (bf16[8,7168]{1,0:T(8,128)(2,1)S(1)}, bf16[8,7168]{1,0:T(8,128)(2,1)S(1)}, u32[]{:S(2)}, u32[]{:S(2)}) collective-permute-start(bf16[8,7168]{1,0:T(8,128)(2,1)S(1)} %shard_map.83), channel_id=1, source_target_pairs={{0,2},{1,5},{2,0},{3,7},{4,6},{5,1},{6,4},{7,3},{8,10},{9,13},{10,... | collective-permute-start | bytes 344072 | tf_op jit(solution)/shard_map/ppermute | solution.py:26
  63.6 4.9 %collective-permute-start.32 = (bf16[8,7168]{1,0:T(8,128)(2,1)S(1)}, bf16[8,7168]{1,0:T(8,128)(2,1)S(1)}, u32[]{:S(2)}, u32[]{:S(2)}) collective-permute-start(bf16[8,7168]{1,0:T(8,128)(2,1)S(1)} %shard_map.85), channel_id=1, source_target_pairs={{0,4},{1,3},{2,6},{3,1},{4,0},{5,7},{6,2},{7,5},{8,12},{9,11},{10,... | collective-permute-start | bytes 344072 | tf_op jit(solution)/shard_map/ppermute | solution.py:26
  65.2 6.7 %collective-permute-start.18 = (bf16[4,7168]{1,0:T(4,128)(2,1)S(1)}, bf16[4,7168]{1,0:T(4,128)(2,1)S(1)}, u32[]{:S(2)}, u32[]{:S(2)}) collective-permute-start(bf16[4,7168]{1,0:T(4,128)(2,1)S(1)} %get-tuple-element.50), channel_id=1, source_target_pairs={{0,16},{1,17},{2,18},{3,19},{4,20},{5,21},{6,22},{7,23},{8,24},{9,... | collective-permute-start | bytes 172040 | tf_op jit(solution)/shard_map/ppermute | solution.py:26
  68.6 4.3 %collective-permute-start.33 = (bf16[4,7168]{1,0:T(4,128)(2,1)S(1)}, bf16[4,7168]{1,0:T(4,128)(2,1)S(1)}, u32[]{:S(2)}, u32[]{:S(2)}) collective-permute-start(bf16[4,7168]{1,0:T(4,128)(2,1)S(1)} %get-tuple-element.61), channel_id=1, source_target_pairs={{0,16},{1,17},{2,18},{3,19},{4,20},{5,21},{6,22},{7,23},{8,24},{9,... | collective-permute-start | bytes 172040 | tf_op jit(solution)/shard_map/ppermute | solution.py:26
  70.2 6.5 %collective-permute-start.34 = (bf16[4,7168]{1,0:T(4,128)(2,1)S(1)}, bf16[4,7168]{1,0:T(4,128)(2,1)S(1)}, u32[]{:S(2)}, u32[]{:S(2)}) collective-permute-start(bf16[4,7168]{1,0:T(4,128)(2,1)S(1)} %get-tuple-element.62), channel_id=1, source_target_pairs={{0,24},{1,25},{2,26},{3,27},{4,28},{5,29},{6,30},{7,31},{8,16},{9,... | collective-permute-start | bytes 172040 | tf_op jit(solution)/shard_map/ppermute | solution.py:26

commit v8 on v7

--- a/solution.py
+++ b/solution.py
@@ -31,8 +31,7 @@
 
 
 CORE = (1, 1)
-NEAR = (4, 2)
-BIG = (2, 4)
+SQUARE = ((4, 2), (2, 4), (6, 6))
 STAY = (0, 0)
 
 
@@ -76,16 +75,14 @@
     )(*[pltpu.with_memory_space_constraint(w, pltpu.HBM) for w in weights])
 
 
-def prepare_kernel(experts, states_hbm, routing_hbm, weight_hbm, out_ref, states_ref, routing_ref, weight_ref, sems):
-    pairs = ((routing_hbm, routing_ref), (weight_hbm, weight_ref), (states_hbm, states_ref))
+def route_kernel(experts, routing_hbm, weight_hbm, out_ref, routing_ref, weight_ref, sems):
+    pairs = ((routing_hbm, routing_ref), (weight_hbm, weight_ref))
     copies = [pltpu.make_async_copy(source, target, sems.at[place]) for place, (source, target) in enumerate(pairs)]
     for copy in copies:
         copy.start()
     for copy in copies:
         copy.wait()
-    rows, dim = states_ref.shape[1:]
-    for span in spans(dim):
-        out_ref[:, span] = states_ref[0, :, span]
+    rows = out_ref.shape[0]
     lane = lax.broadcasted_iota(jnp.int32, (rows, LANES), 1).astype(jnp.float32)
     diagonal = lax.broadcasted_iota(jnp.int32, (rows, rows), 0) == lax.broadcasted_iota(jnp.int32, (rows, rows), 1)
 
@@ -97,19 +94,26 @@
         for k in range(routing_ref.shape[2]):
             column = upright(routing_ref[0, step, k:k + 1, :]) + step * experts
             total += jnp.where(lane == column, upright(weight_ref[0, step, k:k + 1, :]), 0.0)
-    out_ref[:, dim:] = total.astype(jnp.bfloat16)
-
-
-def prepare(experts, states, routing, weight):
-    args = [states, jnp.swapaxes(routing, 2, 3), jnp.swapaxes(weight, 2, 3)]
-    rows, dim = states.shape[1:]
-    (block,) = call(
-        functools.partial(prepare_kernel, experts), [(rows, dim + LANES)],
+    out_ref[...] = total.astype(jnp.bfloat16)
+
+
+def route(experts, routing, weight):
+    args = [jnp.swapaxes(routing, 2, 3), jnp.swapaxes(weight, 2, 3)]
+    return call(
+        functools.partial(route_kernel, experts), [(routing.shape[2], LANES)],
         *[pltpu.with_memory_space_constraint(x, pltpu.HBM) for x in args],
-        in_specs=[pl.BlockSpec(memory_space=pltpu.HBM)] * 3,
-        scratch_shapes=[pltpu.VMEM(x.shape, x.dtype) for x in args] + [pltpu.SemaphoreType.DMA((3,))],
-    )
-    return block
+        in_specs=[pl.BlockSpec(memory_space=pltpu.HBM)] * 2,
+        scratch_shapes=[pltpu.VMEM(x.shape, x.dtype) for x in args] + [pltpu.SemaphoreType.DMA((2,))],
+    )[0]
+
+
+def first_kernel(own_ref, far_ref, own_tail_ref, far_tail_ref, out_ref):
+    dim = own_ref.shape[1]
+    for span in spans(dim):
+        rows = [ref[:, span].astype(jnp.float32) for ref in (own_ref, far_ref)]
+        out_ref[:, span] = jnp.concatenate(rows, axis=0).astype(jnp.bfloat16)
+    tails = [ref[...].astype(jnp.float32) for ref in (own_tail_ref, far_tail_ref)]
+    out_ref[:, dim:] = jnp.concatenate(tails, axis=0).astype(jnp.bfloat16)
 
 
 def join_kernel(*refs):
@@ -226,26 +230,22 @@
     top, *middle = upper_flips(owners)
 
     weights = load((gate_proj, up_proj, down_proj))
-    block = prepare(owners // GROUP, states, routing, route_weight)
-    other = exchange(block, top, 0)
-    block, other, *weights = lax.optimization_barrier((block, other, *weights))
-    pair, own, tail = join(block, other), states[0], None
+    own, tail = states[0], None
+    lanes = route(owners // GROUP, routing, route_weight)
+    other, other_lanes = exchange(own, top, 0), exchange(lanes, top, 0)
+    other, other_lanes, *weights = lax.optimization_barrier((other, other_lanes, *weights))
+    (pair,) = call(first_kernel, [(2 * row_dev, dim + LANES)], own, other, lanes, other_lanes)
     for step_no in range(passes_count):
         rows_a = pair
         for flips in middle:
             rows_a = join(rows_a, exchange(rows_a, flips, 0))
-        rows_b = exchange(rows_a, NEAR, 0)
-        rows_c = exchange(rows_a, BIG, 0)
-        rows_d = exchange(rows_b, BIG, 0)
-        mine = [rows_a, rows_b, rows_c, rows_d]
+        mine = [rows_a] + [exchange(rows_a, flips, 0) for flips in SQUARE]
         outs, tail = mlp(step_no, mine + [exchange(rows, CORE, 0) for rows in mine], tail, norm_gain, *weights)
 
-        kept_a, kept_b, kept_c, kept_d = outs[:4]
-        far_a, far_b, far_c, far_d = [exchange(rows, CORE, 0) for rows in outs[4:]]
-        big_b = exchange(add(kept_d, far_d), BIG, 0)
-        big_a = exchange(add(kept_c, far_c), BIG, 0)
-        near_a = exchange(add(kept_b, far_b, big_b), NEAR, 0)
-        parts = [kept_a, far_a, big_a, near_a]
+        kept, sent = outs[:4], [exchange(rows, CORE, 0) for rows in outs[4:]]
+        parts = [kept[0], sent[0]]
+        for place in (3, 2, 1):
+            parts.append(exchange(add(kept[place], sent[place]), SQUARE[place - 1], 0))
         for flips in middle[::-1]:
             low, high = split(*parts)
             parts = [low, exchange(high, flips, 0)]

time: 77.5 us -> 72.8 us (0.939)
  waiting for transfers between devices: 37.8 us -> 29.3 us
  starting transfers between devices: 28.4 us -> 32.3 us
    ppermute x35 -> x36, waiting for transfers between devices: 37.8 us -> 29.3 us  [exchange(): return lax.ppermute(value, ('segment', 'expert'), pairs)]
    ppermute x35 -> x36, starting transfers between devices: 28.4 us -> 32.3 us  [exchange(): return lax.ppermute(value, ('segment', 'expert'), pairs)]
  transfers between devices with their start and end apart: 35 -> 36, of which waited for: 15 -> 19; matrix products, arithmetic and copies ran while one was open for 0% -> 0% of each run, Pallas kernels for 6% -> 7%
where the time goes in v8:
time: 72.8 us; the launch traced here: 72.6 us
  starting transfers between devices  32.3 us (44%)
  waiting for transfers between devices  29.3 us (40%)
  Pallas kernels  10.8 us (15%)
    ppermute x36, starting transfers between devices, exchange(): return lax.ppermute(value, ('segment', 'expert'), pairs)  32.3 us
    ppermute x36, waiting for transfers between devices, exchange(): return lax.ppermute(value, ('segment', 'expert'), pairs)  29.3 us
    pallas_call x14, Pallas kernels, call(): pl.pallas_call(kernel, out_shape=[jax.ShapeDtypeStruct(shape, jnp.bfloat1...  6.62 us
    pallas_call x1, Pallas kernels, load(): pl.pallas_call(load_kernel, out_shape=[pltpu.VMEM(w.shape, w.dtype) for w...  4.23 us
  transfers between devices with their start and end apart: 36, of which 19 were waited for; matrix products, arithmetic and copies ran while one was open for 0% of the time, Pallas kernels for 7%

profile of v8, /device:TPU:0, one launch (start us, length us, event | category | flops | bytes accessed | tf_op | source)
XLA Modules:
  0.0 72.6 jit_solution(9746522065138787116)
XLA Ops:
  0.0 4.0 %collective-permute-start = (bf16[4,7168]{1,0:T(4,128)(2,1)}, bf16[4,7168]{1,0:T(4,128)(2,1)S(1)}, u32[]{:S(2)}, u32[]{:S(2)}) collective-permute-start(bf16[4,7168]{1,0:T(4,128)(2,1)} %bitcast.4), channel_id=1, source_target_pairs={{0,8},{1,9},{2,10},{3,11},{4,12},{5,13},{6,14},{7,15},{8,0},{9,1},... | collective-permute-start | bytes 172040 | tf_op jit(solution)/shard_map/ppermute | solution.py:26
  4.0 0.8 %shard_map.73.own_tail_ref = bf16[4,128]{1,0:T(4,128)(2,1)S(1)} custom-call(s32[1,2,2,4]{3,2,1,0:T(2,128)} %bitcast.6, bf16[1,2,2,4]{3,2,1,0:T(2,128)(2,1)} %bitcast.7), custom_call_target="tpu_custom_call" | custom-call | tf_op jit(solution)/shard_map/pallas_call | solution.py:43
  4.8 0.0 copy-start.1
  4.9 0.0 copy-start
  4.9 0.1 collective-permute-start.1
  4.9 4.2 %shard_map.74 = (bf16[1,7168,256]{2,1,0:T(8,128)(2,1)S(1)}, bf16[1,7168,256]{2,1,0:T(8,128)(2,1)S(1)}, bf16[1,256,7168]{2,1,0:T(8,128)(2,1)S(1)}) custom-call(bf16[1,7168,256]{2,1,0:T(8,128)(2,1)} %gate_ref.1, bf16[1,7168,256]{2,1,0:T(8,128)(2,1)} %up_ref.1, bf16[1,256,7168]{2,1,0:T(8,128)(2,1)} %down_ref.1), custom_call_target="tpu_custom_call" | custom-call | bytes 11010048 | tf_op jit(solution)/shard_map/pallas_call | solution.py:65
  9.2 0.2 collective-permute-done.1.far_tail_ref
  9.4 2.7 %collective-permute-start.5 = (bf16[8,7296]{1,0:T(8,128)(2,1)S(1)}, bf16[8,7296]{1,0:T(8,128)(2,1)S(1)}, u32[]{:S(2)}, u32[]{:S(2)}) collective-permute-start(bf16[8,7296]{1,0:T(8,128)(2,1)S(1)} %shard_map.75.refs_0_), channel_id=1, source_target_pairs={{0,6},{1,7},{2,4},{3,5},{4,2},{5,3},{6,0},{7,1},{8,14},{9,15},{10,... | collective-permute-start | bytes 350216 | tf_op jit(solution)/shard_map/ppermute | solution.py:26
  12.2 0.5 collective-permute-start.4
  12.7 0.3 collective-permute-start.3
  13.0 0.0 collective-permute-start.6
  13.0 3.3 %collective-permute-done.5.refs_3_ = bf16[8,7296]{1,0:T(8,128)(2,1)S(1)} collective-permute-done((bf16[8,7296]{1,0:T(8,128)(2,1)S(1)}, bf16[8,7296]{1,0:T(8,128)(2,1)S(1)}, u32[]{:S(2)}, u32[]{:S(2)}) %collective-permute-start.5) | collective-permute-done | bytes 116768 | tf_op jit(solution)/shard_map/ppermute | solution.py:26
  16.3 0.0 collective-permute-start.9
  16.3 1.4 %collective-permute-done.4.refs_2_ = bf16[8,7296]{1,0:T(8,128)(2,1)S(1)} collective-permute-done((bf16[8,7296]{1,0:T(8,128)(2,1)S(1)}, bf16[8,7296]{1,0:T(8,128)(2,1)S(1)}, u32[]{:S(2)}, u32[]{:S(2)}) %collective-permute-start.4) | collective-permute-done | bytes 116768 | tf_op jit(solution)/shard_map/ppermute | solution.py:26
  17.7 0.0 collective-permute-start.8
  17.7 0.0 collective-permute-done.3.refs_1_
  17.7 0.5 collective-permute-start.7
  18.2 0.8 %collective-permute-done.8.refs_6_ = bf16[8,7296]{1,0:T(8,128)(2,1)S(1)} collective-permute-done((bf16[8,7296]{1,0:T(8,128)(2,1)S(1)}, bf16[8,7296]{1,0:T(8,128)(2,1)S(1)}, u32[]{:S(2)}, u32[]{:S(2)}) %collective-permute-start.8) | collective-permute-done | bytes 116768 | tf_op jit(solution)/shard_map/ppermute | solution.py:26
  19.0 0.2 collective-permute-done.7.refs_5_
  19.2 2.4 %shard_map.76 = (bf16[8,7168]{1,0:T(8,128)(2,1)S(1)}, bf16[8,7168]{1,0:T(8,128)(2,1)S(1)}, bf16[8,7168]{1,0:T(8,128)(2,1)S(1)}, bf16[8,7168]{1,0:T(8,128)(2,1)S(...) custom-call(bf16[8,7296]{1,0:T(8,128)(2,1)S(1)} %shard_map.75.refs_0, ...), custom_call_target="tpu_custom_call" | custom-call | flops 704643072 | bytes 11010048 | tf_op jit(solution)/shard_map/pallas_call | solution.py:43
  21.6 0.4 collective-permute-start.11
  22.0 0.2 collective-permute-start.13
  22.1 0.3 collective-permute-start.15
  22.5 0.2 collective-permute-start.10
  22.6 0.3 collective-permute-done.11.refs_1_
  23.0 2.3 %collective-permute-start.12 = (bf16[8,7168]{1,0:T(8,128)(2,1)S(1)}, bf16[8,7168]{1,0:T(8,128)(2,1)S(1)}, u32[]{:S(2)}, u32[]{:S(2)}) collective-permute-start(bf16[8,7168]{1,0:T(8,128)(2,1)S(1)} %shard_map.77), channel_id=1, source_target_pairs={{0,6},{1,7},{2,4},{3,5},{4,2},{5,3},{6,0},{7,1},{8,14},{9,15},{10,... | collective-permute-start | bytes 344072 | tf_op jit(solution)/shard_map/ppermute | solution.py:26
  25.3 0.8 %collective-permute-start.14 = (bf16[8,7168]{1,0:T(8,128)(2,1)S(1)}, bf16[8,7168]{1,0:T(8,128)(2,1)S(1)}, u32[]{:S(2)}, u32[]{:S(2)}) collective-permute-start(bf16[8,7168]{1,0:T(8,128)(2,1)S(1)} %shard_map.78), channel_id=1, source_target_pairs={{0,2},{1,5},{2,0},{3,7},{4,6},{5,1},{6,4},{7,3},{8,10},{9,13},{10,... | collective-permute-start | bytes 344072 | tf_op jit(solution)/shard_map/ppermute | solution.py:26
  26.2 0.0 collective-permute-done.15.refs_1_
  26.2 0.5 collective-permute-start.16
  26.7 1.5 %collective-permute-start.2 = (bf16[8,7296]{1,0:T(8,128)(2,1)S(1)}, bf16[8,7296]{1,0:T(8,128)(2,1)S(1)}, u32[]{:S(2)}, u32[]{:S(2)}) collective-permute-start(bf16[8,7296]{1,0:T(8,128)(2,1)S(1)} %shard_map.75.refs_0_), channel_id=1, source_target_pairs={{0,16},{1,17},{2,18},{3,19},{4,20},{5,21},{6,22},{7,23},{8,24},{9,... | collective-permute-start | bytes 350216 | tf_op jit(solution)/shard_map/ppermute | solution.py:26
  28.2 1.7 %collective-permute-done.12.refs_2_ = bf16[8,7168]{1,0:T(8,128)(2,1)S(1)} collective-permute-done((bf16[8,7168]{1,0:T(8,128)(2,1)S(1)}, bf16[8,7168]{1,0:T(8,128)(2,1)S(1)}, u32[]{:S(2)}, u32[]{:S(2)}) %collective-permute-start.12) | collective-permute-done | bytes 114720 | tf_op jit(solution)/shard_map/ppermute | solution.py:26
  29.9 1.9 %collective-permute-done.14.refs_3_ = bf16[8,7168]{1,0:T(8,128)(2,1)S(1)} collective-permute-done((bf16[8,7168]{1,0:T(8,128)(2,1)S(1)}, bf16[8,7168]{1,0:T(8,128)(2,1)S(1)}, u32[]{:S(2)}, u32[]{:S(2)}) %collective-permute-start.14) | collective-permute-done | bytes 114720 | tf_op jit(solution)/shard_map/ppermute | solution.py:26
  31.8 0.1 shard_map.80
  31.9 3.6 %collective-permute-start.18 = (bf16[8,7168]{1,0:T(8,128)(2,1)S(1)}, bf16[8,7168]{1,0:T(8,128)(2,1)S(1)}, u32[]{:S(2)}, u32[]{:S(2)}) collective-permute-start(bf16[8,7168]{1,0:T(8,128)(2,1)S(1)} %shard_map.80), channel_id=1, source_target_pairs={{0,24},{1,25},{2,26},{3,27},{4,28},{5,29},{6,30},{7,31},{8,16},{9,... | collective-permute-start | bytes 344072 | tf_op jit(solution)/shard_map/ppermute | solution.py:26
  35.5 0.5 collective-permute-start.17
  36.0 5.4 %collective-permute-done.18.far_ref = bf16[8,7168]{1,0:T(8,128)(2,1)S(1)} collective-permute-done((bf16[8,7168]{1,0:T(8,128)(2,1)S(1)}, bf16[8,7168]{1,0:T(8,128)(2,1)S(1)}, u32[]{:S(2)}, u32[]{:S(2)}) %collective-permute-start.18) | collective-permute-done | bytes 114720 | tf_op jit(solution)/shard_map/ppermute | solution.py:26
  41.4 0.2 collective-permute-done.17.near_ref
  41.5 0.1 shard_map.81
  41.6 2.2 %collective-permute-start.22 = (bf16[8,7168]{1,0:T(8,128)(2,1)S(1)}, bf16[8,7168]{1,0:T(8,128)(2,1)S(1)}, u32[]{:S(2)}, u32[]{:S(2)}) collective-permute-start(bf16[8,7168]{1,0:T(8,128)(2,1)S(1)} %get-tuple-element.51.refs_0_), channel_id=1, source_target_pairs={{0,6},{1,7},{2,4},{3,5},{4,2},{5,3},{6,0},{7,1},{8,14},{9,15},{10,... | collective-permute-start | bytes 344072 | tf_op jit(solution)/shard_map/ppermute | solution.py:26
  43.8 0.8 %collective-permute-start.21 = (bf16[8,7168]{1,0:T(8,128)(2,1)S(1)}, bf16[8,7168]{1,0:T(8,128)(2,1)S(1)}, u32[]{:S(2)}, u32[]{:S(2)}) collective-permute-start(bf16[8,7168]{1,0:T(8,128)(2,1)S(1)} %get-tuple-element.51.refs_0_), channel_id=1, source_target_pairs={{0,2},{1,5},{2,0},{3,7},{4,6},{5,1},{6,4},{7,3},{8,10},{9,13},{10,... | collective-permute-start | bytes 344072 | tf_op jit(solution)/shard_map/ppermute | solution.py:26
  44.6 0.6 collective-permute-start.20
  45.2 3.2 %collective-permute-done.22.refs_3_ = bf16[8,7168]{1,0:T(8,128)(2,1)S(1)} collective-permute-done((bf16[8,7168]{1,0:T(8,128)(2,1)S(1)}, bf16[8,7168]{1,0:T(8,128)(2,1)S(1)}, u32[]{:S(2)}, u32[]{:S(2)}) %collective-permute-start.22) | collective-permute-done | bytes 114720 | tf_op jit(solution)/shard_map/ppermute | solution.py:26
  48.4 1.4 %collective-permute-done.21.refs_2_ = bf16[8,7168]{1,0:T(8,128)(2,1)S(1)} collective-permute-done((bf16[8,7168]{1,0:T(8,128)(2,1)S(1)}, bf16[8,7168]{1,0:T(8,128)(2,1)S(1)}, u32[]{:S(2)}, u32[]{:S(2)}) %collective-permute-start.21) | collective-permute-done | bytes 114720 | tf_op jit(solution)/shard_map/ppermute | solution.py:26
  49.8 0.5 collective-permute-start.24
  50.3 0.8 %collective-permute-done.25.refs_6_ = bf16[8,7168]{1,0:T(8,128)(2,1)S(1)} collective-permute-done((bf16[8,7168]{1,0:T(8,128)(2,1)S(1)}, bf16[8,7168]{1,0:T(8,128)(2,1)S(1)}, u32[]{:S(2)}, u32[]{:S(2)}) %collective-permute-start.25) | collective-permute-done | bytes 114720 | tf_op jit(solution)/shard_map/ppermute | solution.py:26
  51.2 0.2 collective-permute-done.24.refs_5_
  51.3 2.4 %shard_map.82 = (bf16[8,7168]{1,0:T(8,128)(2,1)S(1)}, bf16[8,7168]{1,0:T(8,128)(2,1)S(1)}, bf16[8,7168]{1,0:T(8,128)(2,1)S(1)}, bf16[8,7168]{1,0:T(8,128)(2,1)S(...) custom-call(bf16[8,7168]{1,0:T(8,128)(2,1)S(1)} %get-tuple-element.5, ...), custom_call_target="tpu_custom_call" | custom-call | flops 704643072 | bytes 11010048 | tf_op jit(solution)/shard_map/pallas_call | solution.py:43
  53.7 0.4 collective-permute-start.28
  54.1 0.2 collective-permute-start.30
  54.3 0.3 collective-permute-start.32
  54.6 0.2 collective-permute-start.27
  54.8 0.3 collective-permute-done.28.refs_1_
  55.1 2.5 %collective-permute-start.29 = (bf16[8,7168]{1,0:T(8,128)(2,1)S(1)}, bf16[8,7168]{1,0:T(8,128)(2,1)S(1)}, u32[]{:S(2)}, u32[]{:S(2)}) collective-permute-start(bf16[8,7168]{1,0:T(8,128)(2,1)S(1)} %shard_map.83), channel_id=1, source_target_pairs={{0,6},{1,7},{2,4},{3,5},{4,2},{5,3},{6,0},{7,1},{8,14},{9,15},{10,... | collective-permute-start | bytes 344072 | tf_op jit(solution)/shard_map/ppermute | solution.py:26
  57.6 0.9 %collective-permute-start.31 = (bf16[8,7168]{1,0:T(8,128)(2,1)S(1)}, bf16[8,7168]{1,0:T(8,128)(2,1)S(1)}, u32[]{:S(2)}, u32[]{:S(2)}) collective-permute-start(bf16[8,7168]{1,0:T(8,128)(2,1)S(1)} %shard_map.84), channel_id=1, source_target_pairs={{0,2},{1,5},{2,0},{3,7},{4,6},{5,1},{6,4},{7,3},{8,10},{9,13},{10,... | collective-permute-start | bytes 344072 | tf_op jit(solution)/shard_map/ppermute | solution.py:26
  58.5 0.4 collective-permute-start.33
  58.9 1.3 %collective-permute-start.19 = (bf16[4,7168]{1,0:T(4,128)(2,1)S(1)}, bf16[4,7168]{1,0:T(4,128)(2,1)S(1)}, u32[]{:S(2)}, u32[]{:S(2)}) collective-permute-start(bf16[4,7168]{1,0:T(4,128)(2,1)S(1)} %get-tuple-element.50), channel_id=1, source_target_pairs={{0,16},{1,17},{2,18},{3,19},{4,20},{5,21},{6,22},{7,23},{8,24},{9,... | collective-permute-start | bytes 172040 | tf_op jit(solution)/shard_map/ppermute | solution.py:26
  60.1 1.9 %collective-permute-done.29.refs_2_ = bf16[8,7168]{1,0:T(8,128)(2,1)S(1)} collective-permute-done((bf16[8,7168]{1,0:T(8,128)(2,1)S(1)}, bf16[8,7168]{1,0:T(8,128)(2,1)S(1)}, u32[]{:S(2)}, u32[]{:S(2)}) %collective-permute-start.29) | collective-permute-done | bytes 114720 | tf_op jit(solution)/shard_map/ppermute | solution.py:26
  62.0 1.9 %collective-permute-done.31.refs_3_ = bf16[8,7168]{1,0:T(8,128)(2,1)S(1)} collective-permute-done((bf16[8,7168]{1,0:T(8,128)(2,1)S(1)}, bf16[8,7168]{1,0:T(8,128)(2,1)S(1)}, u32[]{:S(2)}, u32[]{:S(2)}) %collective-permute-start.31) | collective-permute-done | bytes 114720 | tf_op jit(solution)/shard_map/ppermute | solution.py:26
  63.9 0.1 shard_map.86
  64.0 1.3 %collective-permute-start.34 = (bf16[4,7168]{1,0:T(4,128)(2,1)S(1)}, bf16[4,7168]{1,0:T(4,128)(2,1)S(1)}, u32[]{:S(2)}, u32[]{:S(2)}) collective-permute-start(bf16[4,7168]{1,0:T(4,128)(2,1)S(1)} %get-tuple-element.61), channel_id=1, source_target_pairs={{0,16},{1,17},{2,18},{3,19},{4,20},{5,21},{6,22},{7,23},{8,24},{9,... | collective-permute-start | bytes 172040 | tf_op jit(solution)/shard_map/ppermute | solution.py:26
  65.3 2.4 %collective-permute-start.35 = (bf16[4,7168]{1,0:T(4,128)(2,1)S(1)}, bf16[4,7168]{1,0:T(4,128)(2,1)S(1)}, u32[]{:S(2)}, u32[]{:S(2)}) collective-permute-start(bf16[4,7168]{1,0:T(4,128)(2,1)S(1)} %get-tuple-element.62), channel_id=1, source_target_pairs={{0,24},{1,25},{2,26},{3,27},{4,28},{5,29},{6,30},{7,31},{8,16},{9,... | collective-permute-start | bytes 172040 | tf_op jit(solution)/shard_map/ppermute | solution.py:26
  67.7 0.6 collective-permute-done.34.refs_1_
  68.3 3.7 %collective-permute-done.35.refs_2_ = bf16[4,7168]{1,0:T(4,128)(2,1)S(1)} collective-permute-done((bf16[4,7168]{1,0:T(4,128)(2,1)S(1)}, bf16[4,7168]{1,0:T(4,128)(2,1)S(1)}, u32[]{:S(2)}, u32[]{:S(2)}) %collective-permute-start.35) | collective-permute-done | bytes 57376 | tf_op jit(solution)/shard_map/ppermute | solution.py:26
  71.9 0.7 shard_map.87
  (27 shorter events, 0.3 us)
Async XLA Ops:
  0.0 9.4 %collective-permute-start = (bf16[4,7168]{1,0:T(4,128)(2,1)}, bf16[4,7168]{1,0:T(4,128)(2,1)S(1)}, u32[]{:S(2)}, u32[]{:S(2)}) collective-permute-start(bf16[4,7168]{1,0:T(4,128)(2,1)} %bitcast.4), channel_id=1, source_target_pairs={{0,8},{1,9},{2,10},{3,11},{4,12},{5,13},{6,14},{7,15},{8,0},{9,1},... | collective-permute-start | bytes 172040 | tf_op jit(solution)/shard_map/ppermute | solution.py:26
  4.8 4.6 %copy-start.1 = (bf16[1,4,7168]{2,1,0:T(4,128)(2,1)S(1)}, bf16[1,4,7168]{2,1,0:T(4,128)(2,1)}, u32[]{:S(2)}) copy-start(bf16[1,4,7168]{2,1,0:T(4,128)(2,1)} %param.7) | copy-start | bytes 172036
  4.9 14.3 %copy-start = (f32[1,7168]{1,0:T(1,128)S(1)}, f32[1,7168]{1,0:T(1,128)}, u32[]{:S(2)}) copy-start(f32[1,7168]{1,0:T(1,128)} %refs_9_.1) | copy-start | bytes 86020
  4.9 4.5 %collective-permute-start.1 = (bf16[4,128]{1,0:T(4,128)(2,1)S(1)}, bf16[4,128]{1,0:T(4,128)(2,1)S(1)}, u32[]{:S(2)}, u32[]{:S(2)}) collective-permute-start(bf16[4,128]{1,0:T(4,128)(2,1)S(1)} %shard_map.73.own_tail_ref), channel_id=1, source_target_pairs={{0,8},{1,9},{2,10},{3,11},{4,12},{5,13},{6,14},{7,15},{8,0},{9,1},... | collective-permute-start | bytes 3080 | tf_op jit(solution)/shard_map/ppermute | solution.py:26
  9.4 6.9 %collective-permute-start.5 = (bf16[8,7296]{1,0:T(8,128)(2,1)S(1)}, bf16[8,7296]{1,0:T(8,128)(2,1)S(1)}, u32[]{:S(2)}, u32[]{:S(2)}) collective-permute-start(bf16[8,7296]{1,0:T(8,128)(2,1)S(1)} %shard_map.75.refs_0_), channel_id=1, source_target_pairs={{0,6},{1,7},{2,4},{3,5},{4,2},{5,3},{6,0},{7,1},{8,14},{9,15},{10,... | collective-permute-start | bytes 350216 | tf_op jit(solution)/shard_map/ppermute | solution.py:26
  12.2 5.5 %collective-permute-start.4 = (bf16[8,7296]{1,0:T(8,128)(2,1)S(1)}, bf16[8,7296]{1,0:T(8,128)(2,1)S(1)}, u32[]{:S(2)}, u32[]{:S(2)}) collective-permute-start(bf16[8,7296]{1,0:T(8,128)(2,1)S(1)} %shard_map.75.refs_0_), channel_id=1, source_target_pairs={{0,2},{1,5},{2,0},{3,7},{4,6},{5,1},{6,4},{7,3},{8,10},{9,13},{10,... | collective-permute-start | bytes 350216 | tf_op jit(solution)/shard_map/ppermute | solution.py:26
  12.7 5.0 %collective-permute-start.3 = (bf16[8,7296]{1,0:T(8,128)(2,1)S(1)}, bf16[8,7296]{1,0:T(8,128)(2,1)S(1)}, u32[]{:S(2)}, u32[]{:S(2)}) collective-permute-start(bf16[8,7296]{1,0:T(8,128)(2,1)S(1)} %shard_map.75.refs_0_), channel_id=1, source_target_pairs={{0,4},{1,3},{2,6},{3,1},{4,0},{5,7},{6,2},{7,5},{8,12},{9,11},{10,... | collective-permute-start | bytes 350216 | tf_op jit(solution)/shard_map/ppermute | solution.py:26
  13.0 5.2 %collective-permute-start.6 = (bf16[8,7296]{1,0:T(8,128)(2,1)S(1)}, bf16[8,7296]{1,0:T(8,128)(2,1)S(1)}, u32[]{:S(2)}, u32[]{:S(2)}) collective-permute-start(bf16[8,7296]{1,0:T(8,128)(2,1)S(1)} %shard_map.75.refs_0_), channel_id=1, source_target_pairs={{0,1},{1,0},{2,3},{3,2},{4,5},{5,4},{6,7},{7,6},{8,9},{9,8},{10,11... | collective-permute-start | bytes 350216 | tf_op jit(solution)/shard_map/ppermute | solution.py:26
  16.3 1.9 %collective-permute-start.9 = (bf16[8,7296]{1,0:T(8,128)(2,1)S(1)}, bf16[8,7296]{1,0:T(8,128)(2,1)S(1)}, u32[]{:S(2)}, u32[]{:S(2)}) collective-permute-start(bf16[8,7296]{1,0:T(8,128)(2,1)S(1)} %collective-permute-done.5.refs_3_), channel_id=1, source_target_pairs={{0,1},{1,0},{2,3},{3,2},{4,5},{5,4},{6,7},{7,6},{8,9},{9,8},{10,11... | collective-permute-start | bytes 350216 | tf_op jit(solution)/shard_map/ppermute | solution.py:26
  17.7 1.3 %collective-permute-start.8 = (bf16[8,7296]{1,0:T(8,128)(2,1)S(1)}, bf16[8,7296]{1,0:T(8,128)(2,1)S(1)}, u32[]{:S(2)}, u32[]{:S(2)}) collective-permute-start(bf16[8,7296]{1,0:T(8,128)(2,1)S(1)} %collective-permute-done.4.refs_2_), channel_id=1, source_target_pairs={{0,1},{1,0},{2,3},{3,2},{4,5},{5,4},{6,7},{7,6},{8,9},{9,8},{10,11... | collective-permute-start | bytes 350216 | tf_op jit(solution)/shard_map/ppermute | solution.py:26
  17.7 1.5 %collective-permute-start.7 = (bf16[8,7296]{1,0:T(8,128)(2,1)S(1)}, bf16[8,7296]{1,0:T(8,128)(2,1)S(1)}, u32[]{:S(2)}, u32[]{:S(2)}) collective-permute-start(bf16[8,7296]{1,0:T(8,128)(2,1)S(1)} %collective-permute-done.3.refs_1_), channel_id=1, source_target_pairs={{0,1},{1,0},{2,3},{3,2},{4,5},{5,4},{6,7},{7,6},{8,9},{9,8},{10,11... | collective-permute-start | bytes 350216 | tf_op jit(solution)/shard_map/ppermute | solution.py:26
  21.6 1.4 %collective-permute-start.11 = (bf16[8,7168]{1,0:T(8,128)(2,1)S(1)}, bf16[8,7168]{1,0:T(8,128)(2,1)S(1)}, u32[]{:S(2)}, u32[]{:S(2)}) collective-permute-start(bf16[8,7168]{1,0:T(8,128)(2,1)S(1)} %get-tuple-element.45), channel_id=1, source_target_pairs={{0,1},{1,0},{2,3},{3,2},{4,5},{5,4},{6,7},{7,6},{8,9},{9,8},{10,11... | collective-permute-start | bytes 344072 | tf_op jit(solution)/shard_map/ppermute | solution.py:26
  22.0 3.3 %collective-permute-start.13 = (bf16[8,7168]{1,0:T(8,128)(2,1)S(1)}, bf16[8,7168]{1,0:T(8,128)(2,1)S(1)}, u32[]{:S(2)}, u32[]{:S(2)}) collective-permute-start(bf16[8,7168]{1,0:T(8,128)(2,1)S(1)} %get-tuple-element.47), channel_id=1, source_target_pairs={{0,1},{1,0},{2,3},{3,2},{4,5},{5,4},{6,7},{7,6},{8,9},{9,8},{10,11... | collective-permute-start | bytes 344072 | tf_op jit(solution)/shard_map/ppermute | solution.py:26
  22.1 4.1 %collective-permute-start.15 = (bf16[8,7168]{1,0:T(8,128)(2,1)S(1)}, bf16[8,7168]{1,0:T(8,128)(2,1)S(1)}, u32[]{:S(2)}, u32[]{:S(2)}) collective-permute-start(bf16[8,7168]{1,0:T(8,128)(2,1)S(1)} %get-tuple-element.49), channel_id=1, source_target_pairs={{0,1},{1,0},{2,3},{3,2},{4,5},{5,4},{6,7},{7,6},{8,9},{9,8},{10,11... | collective-permute-start | bytes 344072 | tf_op jit(solution)/shard_map/ppermute | solution.py:26
  22.5 5.8 %collective-permute-start.10 = (bf16[8,7168]{1,0:T(8,128)(2,1)S(1)}, bf16[8,7168]{1,0:T(8,128)(2,1)S(1)}, u32[]{:S(2)}, u32[]{:S(2)}) collective-permute-start(bf16[8,7168]{1,0:T(8,128)(2,1)S(1)} %get-tuple-element.43), channel_id=1, source_target_pairs={{0,1},{1,0},{2,3},{3,2},{4,5},{5,4},{6,7},{7,6},{8,9},{9,8},{10,11... | collective-permute-start | bytes 344072 | tf_op jit(solution)/shard_map/ppermute | solution.py:26
  23.0 6.9 %collective-permute-start.12 = (bf16[8,7168]{1,0:T(8,128)(2,1)S(1)}, bf16[8,7168]{1,0:T(8,128)(2,1)S(1)}, u32[]{:S(2)}, u32[]{:S(2)}) collective-permute-start(bf16[8,7168]{1,0:T(8,128)(2,1)S(1)} %shard_map.77), channel_id=1, source_target_pairs={{0,6},{1,7},{2,4},{3,5},{4,2},{5,3},{6,0},{7,1},{8,14},{9,15},{10,... | collective-permute-start | bytes 344072 | tf_op jit(solution)/shard_map/ppermute | solution.py:26
  25.3 6.5 %collective-permute-start.14 = (bf16[8,7168]{1,0:T(8,128)(2,1)S(1)}, bf16[8,7168]{1,0:T(8,128)(2,1)S(1)}, u32[]{:S(2)}, u32[]{:S(2)}) collective-permute-start(bf16[8,7168]{1,0:T(8,128)(2,1)S(1)} %shard_map.78), channel_id=1, source_target_pairs={{0,2},{1,5},{2,0},{3,7},{4,6},{5,1},{6,4},{7,3},{8,10},{9,13},{10,... | collective-permute-start | bytes 344072 | tf_op jit(solution)/shard_map/ppermute | solution.py:26
  26.2 5.6 %collective-permute-start.16 = (bf16[8,7168]{1,0:T(8,128)(2,1)S(1)}, bf16[8,7168]{1,0:T(8,128)(2,1)S(1)}, u32[]{:S(2)}, u32[]{:S(2)}) collective-permute-start(bf16[8,7168]{1,0:T(8,128)(2,1)S(1)} %shard_map.79), channel_id=1, source_target_pairs={{0,4},{1,3},{2,6},{3,1},{4,0},{5,7},{6,2},{7,5},{8,12},{9,11},{10,... | collective-permute-start | bytes 344072 | tf_op jit(solution)/shard_map/ppermute | solution.py:26
  26.7 9.3 %collective-permute-start.2 = (bf16[8,7296]{1,0:T(8,128)(2,1)S(1)}, bf16[8,7296]{1,0:T(8,128)(2,1)S(1)}, u32[]{:S(2)}, u32[]{:S(2)}) collective-permute-start(bf16[8,7296]{1,0:T(8,128)(2,1)S(1)} %shard_map.75.refs_0_), channel_id=1, source_target_pairs={{0,16},{1,17},{2,18},{3,19},{4,20},{5,21},{6,22},{7,23},{8,24},{9,... | collective-permute-start | bytes 350216 | tf_op jit(solution)/shard_map/ppermute | solution.py:26
  31.9 9.5 %collective-permute-start.18 = (bf16[8,7168]{1,0:T(8,128)(2,1)S(1)}, bf16[8,7168]{1,0:T(8,128)(2,1)S(1)}, u32[]{:S(2)}, u32[]{:S(2)}) collective-permute-start(bf16[8,7168]{1,0:T(8,128)(2,1)S(1)} %shard_map.80), channel_id=1, source_target_pairs={{0,24},{1,25},{2,26},{3,27},{4,28},{5,29},{6,30},{7,31},{8,16},{9,... | collective-permute-start | bytes 344072 | tf_op jit(solution)/shard_map/ppermute | solution.py:26
  35.5 6.1 %collective-permute-start.17 = (bf16[8,7168]{1,0:T(8,128)(2,1)S(1)}, bf16[8,7168]{1,0:T(8,128)(2,1)S(1)}, u32[]{:S(2)}, u32[]{:S(2)}) collective-permute-start(bf16[8,7168]{1,0:T(8,128)(2,1)S(1)} %shard_map.80), channel_id=1, source_target_pairs={{0,16},{1,17},{2,18},{3,19},{4,20},{5,21},{6,22},{7,23},{8,24},{9,... | collective-permute-start | bytes 344072 | tf_op jit(solution)/shard_map/ppermute | solution.py:26
  41.6 6.8 %collective-permute-start.22 = (bf16[8,7168]{1,0:T(8,128)(2,1)S(1)}, bf16[8,7168]{1,0:T(8,128)(2,1)S(1)}, u32[]{:S(2)}, u32[]{:S(2)}) collective-permute-start(bf16[8,7168]{1,0:T(8,128)(2,1)S(1)} %get-tuple-element.51.refs_0_), channel_id=1, source_target_pairs={{0,6},{1,7},{2,4},{3,5},{4,2},{5,3},{6,0},{7,1},{8,14},{9,15},{10,... | collective-permute-start | bytes 344072 | tf_op jit(solution)/shard_map/ppermute | solution.py:26
  43.8 6.0 %collective-permute-start.21 = (bf16[8,7168]{1,0:T(8,128)(2,1)S(1)}, bf16[8,7168]{1,0:T(8,128)(2,1)S(1)}, u32[]{:S(2)}, u32[]{:S(2)}) collective-permute-start(bf16[8,7168]{1,0:T(8,128)(2,1)S(1)} %get-tuple-element.51.refs_0_), channel_id=1, source_target_pairs={{0,2},{1,5},{2,0},{3,7},{4,6},{5,1},{6,4},{7,3},{8,10},{9,13},{10,... | collective-permute-start | bytes 344072 | tf_op jit(solution)/shard_map/ppermute | solution.py:26
  44.6 5.2 %collective-permute-start.20 = (bf16[8,7168]{1,0:T(8,128)(2,1)S(1)}, bf16[8,7168]{1,0:T(8,128)(2,1)S(1)}, u32[]{:S(2)}, u32[]{:S(2)}) collective-permute-start(bf16[8,7168]{1,0:T(8,128)(2,1)S(1)} %get-tuple-element.51.refs_0_), channel_id=1, source_target_pairs={{0,4},{1,3},{2,6},{3,1},{4,0},{5,7},{6,2},{7,5},{8,12},{9,11},{10,... | collective-permute-start | bytes 344072 | tf_op jit(solution)/shard_map/ppermute | solution.py:26
  45.2 5.2 %collective-permute-start.23 = (bf16[8,7168]{1,0:T(8,128)(2,1)S(1)}, bf16[8,7168]{1,0:T(8,128)(2,1)S(1)}, u32[]{:S(2)}, u32[]{:S(2)}) collective-permute-start(bf16[8,7168]{1,0:T(8,128)(2,1)S(1)} %get-tuple-element.51.refs_0_), channel_id=1, source_target_pairs={{0,1},{1,0},{2,3},{3,2},{4,5},{5,4},{6,7},{7,6},{8,9},{9,8},{10,11... | collective-permute-start | bytes 344072 | tf_op jit(solution)/shard_map/ppermute | solution.py:26
  48.4 2.0 %collective-permute-start.26 = (bf16[8,7168]{1,0:T(8,128)(2,1)S(1)}, bf16[8,7168]{1,0:T(8,128)(2,1)S(1)}, u32[]{:S(2)}, u32[]{:S(2)}) collective-permute-start(bf16[8,7168]{1,0:T(8,128)(2,1)S(1)} %collective-permute-done.22.refs_3_), channel_id=1, source_target_pairs={{0,1},{1,0},{2,3},{3,2},{4,5},{5,4},{6,7},{7,6},{8,9},{9,8},{10,11... | collective-permute-start | bytes 344072 | tf_op jit(solution)/shard_map/ppermute | solution.py:26
  49.8 1.3 %collective-permute-start.25 = (bf16[8,7168]{1,0:T(8,128)(2,1)S(1)}, bf16[8,7168]{1,0:T(8,128)(2,1)S(1)}, u32[]{:S(2)}, u32[]{:S(2)}) collective-permute-start(bf16[8,7168]{1,0:T(8,128)(2,1)S(1)} %collective-permute-done.21.refs_2_), channel_id=1, source_target_pairs={{0,1},{1,0},{2,3},{3,2},{4,5},{5,4},{6,7},{7,6},{8,9},{9,8},{10,11... | collective-permute-start | bytes 344072 | tf_op jit(solution)/shard_map/ppermute | solution.py:26
  49.8 1.5 %collective-permute-start.24 = (bf16[8,7168]{1,0:T(8,128)(2,1)S(1)}, bf16[8,7168]{1,0:T(8,128)(2,1)S(1)}, u32[]{:S(2)}, u32[]{:S(2)}) collective-permute-start(bf16[8,7168]{1,0:T(8,128)(2,1)S(1)} %collective-permute-done.20.refs_1_), channel_id=1, source_target_pairs={{0,1},{1,0},{2,3},{3,2},{4,5},{5,4},{6,7},{7,6},{8,9},{9,8},{10,11... | collective-permute-start | bytes 344072 | tf_op jit(solution)/shard_map/ppermute | solution.py:26
  53.7 1.4 %collective-permute-start.28 = (bf16[8,7168]{1,0:T(8,128)(2,1)S(1)}, bf16[8,7168]{1,0:T(8,128)(2,1)S(1)}, u32[]{:S(2)}, u32[]{:S(2)}) collective-permute-start(bf16[8,7168]{1,0:T(8,128)(2,1)S(1)} %get-tuple-element.56), channel_id=1, source_target_pairs={{0,1},{1,0},{2,3},{3,2},{4,5},{5,4},{6,7},{7,6},{8,9},{9,8},{10,11... | collective-permute-start | bytes 344072 | tf_op jit(solution)/shard_map/ppermute | solution.py:26
  54.1 3.5 %collective-permute-start.30 = (bf16[8,7168]{1,0:T(8,128)(2,1)S(1)}, bf16[8,7168]{1,0:T(8,128)(2,1)S(1)}, u32[]{:S(2)}, u32[]{:S(2)}) collective-permute-start(bf16[8,7168]{1,0:T(8,128)(2,1)S(1)} %get-tuple-element.58), channel_id=1, source_target_pairs={{0,1},{1,0},{2,3},{3,2},{4,5},{5,4},{6,7},{7,6},{8,9},{9,8},{10,11... | collective-permute-start | bytes 344072 | tf_op jit(solution)/shard_map/ppermute | solution.py:26
  54.3 4.2 %collective-permute-start.32 = (bf16[8,7168]{1,0:T(8,128)(2,1)S(1)}, bf16[8,7168]{1,0:T(8,128)(2,1)S(1)}, u32[]{:S(2)}, u32[]{:S(2)}) collective-permute-start(bf16[8,7168]{1,0:T(8,128)(2,1)S(1)} %get-tuple-element.60), channel_id=1, source_target_pairs={{0,1},{1,0},{2,3},{3,2},{4,5},{5,4},{6,7},{7,6},{8,9},{9,8},{10,11... | collective-permute-start | bytes 344072 | tf_op jit(solution)/shard_map/ppermute | solution.py:26
  54.6 5.5 %collective-permute-start.27 = (bf16[8,7168]{1,0:T(8,128)(2,1)S(1)}, bf16[8,7168]{1,0:T(8,128)(2,1)S(1)}, u32[]{:S(2)}, u32[]{:S(2)}) collective-permute-start(bf16[8,7168]{1,0:T(8,128)(2,1)S(1)} %get-tuple-element.54), channel_id=1, source_target_pairs={{0,1},{1,0},{2,3},{3,2},{4,5},{5,4},{6,7},{7,6},{8,9},{9,8},{10,11... | collective-permute-start | bytes 344072 | tf_op jit(solution)/shard_map/ppermute | solution.py:26
  55.1 6.9 %collective-permute-start.29 = (bf16[8,7168]{1,0:T(8,128)(2,1)S(1)}, bf16[8,7168]{1,0:T(8,128)(2,1)S(1)}, u32[]{:S(2)}, u32[]{:S(2)}) collective-permute-start(bf16[8,7168]{1,0:T(8,128)(2,1)S(1)} %shard_map.83), channel_id=1, source_target_pairs={{0,6},{1,7},{2,4},{3,5},{4,2},{5,3},{6,0},{7,1},{8,14},{9,15},{10,... | collective-permute-start | bytes 344072 | tf_op jit(solution)/shard_map/ppermute | solution.py:26
  57.6 6.3 %collective-permute-start.31 = (bf16[8,7168]{1,0:T(8,128)(2,1)S(1)}, bf16[8,7168]{1,0:T(8,128)(2,1)S(1)}, u32[]{:S(2)}, u32[]{:S(2)}) collective-permute-start(bf16[8,7168]{1,0:T(8,128)(2,1)S(1)} %shard_map.84), channel_id=1, source_target_pairs={{0,2},{1,5},{2,0},{3,7},{4,6},{5,1},{6,4},{7,3},{8,10},{9,13},{10,... | collective-permute-start | bytes 344072 | tf_op jit(solution)/shard_map/ppermute | solution.py:26
  58.5 5.4 %collective-permute-start.33 = (bf16[8,7168]{1,0:T(8,128)(2,1)S(1)}, bf16[8,7168]{1,0:T(8,128)(2,1)S(1)}, u32[]{:S(2)}, u32[]{:S(2)}) collective-permute-start(bf16[8,7168]{1,0:T(8,128)(2,1)S(1)} %shard_map.85), channel_id=1, source_target_pairs={{0,4},{1,3},{2,6},{3,1},{4,0},{5,7},{6,2},{7,5},{8,12},{9,11},{10,... | collective-permute-start | bytes 344072 | tf_op jit(solution)/shard_map/ppermute | solution.py:26
  58.9 8.8 %collective-permute-start.19 = (bf16[4,7168]{1,0:T(4,128)(2,1)S(1)}, bf16[4,7168]{1,0:T(4,128)(2,1)S(1)}, u32[]{:S(2)}, u32[]{:S(2)}) collective-permute-start(bf16[4,7168]{1,0:T(4,128)(2,1)S(1)} %get-tuple-element.50), channel_id=1, source_target_pairs={{0,16},{1,17},{2,18},{3,19},{4,20},{5,21},{6,22},{7,23},{8,24},{9,... | collective-permute-start | bytes 172040 | tf_op jit(solution)/shard_map/ppermute | solution.py:26
  64.0 4.2 %collective-permute-start.34 = (bf16[4,7168]{1,0:T(4,128)(2,1)S(1)}, bf16[4,7168]{1,0:T(4,128)(2,1)S(1)}, u32[]{:S(2)}, u32[]{:S(2)}) collective-permute-start(bf16[4,7168]{1,0:T(4,128)(2,1)S(1)} %get-tuple-element.61), channel_id=1, source_target_pairs={{0,16},{1,17},{2,18},{3,19},{4,20},{5,21},{6,22},{7,23},{8,24},{9,... | collective-permute-start | bytes 172040 | tf_op jit(solution)/shard_map/ppermute | solution.py:26
  65.3 6.6 %collective-permute-start.35 = (bf16[4,7168]{1,0:T(4,128)(2,1)S(1)}, bf16[4,7168]{1,0:T(4,128)(2,1)S(1)}, u32[]{:S(2)}, u32[]{:S(2)}) collective-permute-start(bf16[4,7168]{1,0:T(4,128)(2,1)S(1)} %get-tuple-element.62), channel_id=1, source_target_pairs={{0,24},{1,25},{2,26},{3,27},{4,28},{5,29},{6,30},{7,31},{8,16},{9,... | collective-permute-start | bytes 172040 | tf_op jit(solution)/shard_map/ppermute | solution.py:26

commit v9 on v8

--- a/solution.py
+++ b/solution.py
@@ -31,7 +31,7 @@
 
 
 CORE = (1, 1)
-SQUARE = ((4, 2), (2, 4), (6, 6))
+SQUARE = ((6, 6), (2, 4), (4, 2))
 STAY = (0, 0)
 
 
@@ -138,7 +138,7 @@
             out_ref[:, span] = total[place * rows:(place + 1) * rows].astype(jnp.bfloat16)
 
 
-def meet_kernel(rest_ref, near_ref, far_ref, out_ref, own_ref):
+def meet_kernel(rest_ref, far_ref, near_ref, out_ref, own_ref):
     half = own_ref.shape[0]
     for span in spans(out_ref.shape[1]):
         far = far_ref[:, span].astype(jnp.float32)
@@ -148,11 +148,11 @@
         own_ref[:, span] = total[:half]
 
 
-def mlp_kernel(step_no, *refs):
-    x_refs, refs = refs[:8], refs[8:]
+def mlp_kernel(step_no, count, *refs):
+    x_refs, refs = refs[:count], refs[count:]
     if step_no > 0:
         tail_ref, refs = refs[0], refs[1:]
-    (gain_ref, gate_ref, up_ref, down_ref), outs, refs = refs[:4], refs[4:12], refs[12:]
+    (gain_ref, gate_ref, up_ref, down_ref), outs, refs = refs[:4], refs[4:4 + count], refs[4 + count:]
     rows_ref = refs[-1]
     part = outs[0].shape[0]
     dim, hidden = gate_ref.shape[1:]
@@ -177,8 +177,8 @@
             tail = tail_ref[band, :]
         chosen = jnp.where(lane == column, tail.astype(jnp.float32), 0.0)
         weights.append(jnp.sum(chosen, axis=1, keepdims=True))
-    gated = jnp.zeros((8 * part, hidden), jnp.float32)
-    up_part = jnp.zeros((8 * part, hidden), jnp.float32)
+    gated = jnp.zeros((count * part, hidden), jnp.float32)
+    up_part = jnp.zeros((count * part, hidden), jnp.float32)
     for span in spans(dim):
         rows = rows_ref[:, span]
         gated += jnp.dot(rows, gate_ref[0, span, :], preferred_element_type=jnp.float32)
@@ -194,18 +194,18 @@
 
 def mlp(step_no, xs, tail, gain, gate, up, down):
     dim, hidden = gate.shape[1:]
-    part = xs[0].shape[0]
+    part, count = xs[0].shape[0], len(xs)
     gate, up, down = [pltpu.with_memory_space_constraint(w, pltpu.VMEM) for w in (gate, up, down)]
     first = step_no == 0
     args = list(xs) + ([] if first else [tail]) + [gain, gate, up, down]
     result = call(
-        functools.partial(mlp_kernel, step_no), [(part, dim)] * 8 + [(8 * part, LANES)] * first, *args,
-        scratch_shapes=[pltpu.VMEM((8 * part, dim), jnp.bfloat16)],
+        functools.partial(mlp_kernel, step_no, count), [(part, dim)] * count + [(count * part, LANES)] * first, *args,
+        scratch_shapes=[pltpu.VMEM((count * part, dim), jnp.bfloat16)],
         cost_estimate=pl.CostEstimate(
-            flops=48 * part * dim * hidden, bytes_accessed=6 * dim * hidden, transcendentals=0
+            flops=6 * count * part * dim * hidden, bytes_accessed=6 * dim * hidden, transcendentals=0
         ),
     )
-    return result[:8], result[8] if first else tail
+    return result[:count], result[count] if first else tail
 
 
 def add(*parts):
@@ -230,7 +230,7 @@
     top, *middle = upper_flips(owners)
 
     weights = load((gate_proj, up_proj, down_proj))
-    own, tail = states[0], None
+    own, tail, tail_a = states[0], None, None
     lanes = route(owners // GROUP, routing, route_weight)
     other, other_lanes = exchange(own, top, 0), exchange(lanes, top, 0)
     other, other_lanes, *weights = lax.optimization_barrier((other, other_lanes, *weights))
@@ -239,13 +239,17 @@
         rows_a = pair
         for flips in middle:
             rows_a = join(rows_a, exchange(rows_a, flips, 0))
-        mine = [rows_a] + [exchange(rows_a, flips, 0) for flips in SQUARE]
+        (kept_a, sent_a), tail_a = mlp(
+            step_no, [rows_a, exchange(rows_a, CORE, 0)], tail_a, norm_gain, *weights
+        )
+        mine = [exchange(rows_a, flips, 0) for flips in SQUARE]
+        mine[2], kept_a, sent_a = lax.optimization_barrier((mine[2], kept_a, sent_a))
         outs, tail = mlp(step_no, mine + [exchange(rows, CORE, 0) for rows in mine], tail, norm_gain, *weights)
 
-        kept, sent = outs[:4], [exchange(rows, CORE, 0) for rows in outs[4:]]
-        parts = [kept[0], sent[0]]
-        for place in (3, 2, 1):
-            parts.append(exchange(add(kept[place], sent[place]), SQUARE[place - 1], 0))
+        parts = [kept_a, exchange(sent_a, CORE, 0)]
+        for place in range(len(SQUARE))[::-1]:
+            chip = add(outs[place], exchange(outs[place + len(SQUARE)], CORE, 0))
+            parts.append(exchange(chip, SQUARE[place], 0))
         for flips in middle[::-1]:
             low, high = split(*parts)
             parts = [low, exchange(high, flips, 0)]
@@ -253,12 +257,13 @@
             total = add(*parts)
             rest = exchange(pair, STAY, 1)
             pair, own = call(
-                meet_kernel, [(2 * row_dev, dim), (row_dev, dim)], rest, exchange(total, STAY, 1), exchange(total, top, 1)
+                meet_kernel, [(2 * row_dev, dim), (row_dev, dim)], rest, exchange(total, top, 1), exchange(total, STAY, 1)
             )
         else:
             low, high = split(*parts)
             rest = exchange(own, STAY, 1)
-            own = add(rest, exchange(low, STAY, 1), exchange(high, top, 1))
+            far = exchange(high, top, 1)
+            own = add(rest, far, exchange(low, STAY, 1))
     return own[None]
 
 

time: 72.8 us -> 74.2 us (1.019)
  Pallas kernels: 10.8 us -> 14.3 us
  waiting for transfers between devices: 29.3 us -> 27.1 us
    pallas_call x14 -> x16, Pallas kernels: 6.62 us -> 10 us  [call(): pl.pallas_call(kernel, out_shape=[jax.ShapeDtypeStruct(shape, jnp.bfloat1...]
    ppermute x36, waiting for transfers between devices: 29.3 us -> 27.1 us  [exchange(): return lax.ppermute(value, ('segment', 'expert'), pairs)]
  transfers between devices with their start and end apart: 36 -> 36, of which waited for: 19 -> 21; matrix products, arithmetic and copies ran while one was open for 0% -> 0% of each run, Pallas kernels for 7% -> 12%
where the time goes in v9:
time: 74.2 us; the launch traced here: 74.1 us
  starting transfers between devices  32.6 us (44%)
  waiting for transfers between devices  27.1 us (37%)
  Pallas kernels  14.3 us (19%)
    ppermute x36, starting transfers between devices, exchange(): return lax.ppermute(value, ('segment', 'expert'), pairs)  32.6 us
    ppermute x36, waiting for transfers between devices, exchange(): return lax.ppermute(value, ('segment', 'expert'), pairs)  27.1 us
    pallas_call x16, Pallas kernels, call(): pl.pallas_call(kernel, out_shape=[jax.ShapeDtypeStruct(shape, jnp.bfloat1...  10 us
    pallas_call x1, Pallas kernels, load(): pl.pallas_call(load_kernel, out_shape=[pltpu.VMEM(w.shape, w.dtype) for w...  4.23 us
  transfers between devices with their start and end apart: 36, of which 21 were waited for; matrix products, arithmetic and copies ran while one was open for 0% of the time, Pallas kernels for 12%

profile of v9, /device:TPU:0, one launch (start us, length us, event | category | flops | bytes accessed | tf_op | source)
XLA Modules:
  0.0 74.1 jit_solution(544878536925200657)
XLA Ops:
  0.0 4.0 %collective-permute-start = (bf16[4,7168]{1,0:T(4,128)(2,1)}, bf16[4,7168]{1,0:T(4,128)(2,1)S(1)}, u32[]{:S(2)}, u32[]{:S(2)}) collective-permute-start(bf16[4,7168]{1,0:T(4,128)(2,1)} %bitcast.4), channel_id=1, source_target_pairs={{0,8},{1,9},{2,10},{3,11},{4,12},{5,13},{6,14},{7,15},{8,0},{9,1},... | collective-permute-start | bytes 172040 | tf_op jit(solution)/shard_map/ppermute | solution.py:26
  4.0 0.8 %shard_map.73.own_tail_ref = bf16[4,128]{1,0:T(4,128)(2,1)S(1)} custom-call(s32[1,2,2,4]{3,2,1,0:T(2,128)} %bitcast.6, bf16[1,2,2,4]{3,2,1,0:T(2,128)(2,1)} %bitcast.7), custom_call_target="tpu_custom_call" | custom-call | tf_op jit(solution)/shard_map/pallas_call | solution.py:43
  4.9 0.1 collective-permute-start.1
  4.9 4.2 %shard_map.74 = (bf16[1,7168,256]{2,1,0:T(8,128)(2,1)S(1)}, bf16[1,7168,256]{2,1,0:T(8,128)(2,1)S(1)}, bf16[1,256,7168]{2,1,0:T(8,128)(2,1)S(1)}) custom-call(bf16[1,7168,256]{2,1,0:T(8,128)(2,1)} %gate_ref.1, bf16[1,7168,256]{2,1,0:T(8,128)(2,1)} %up_ref.1, bf16[1,256,7168]{2,1,0:T(8,128)(2,1)} %down_ref.1), custom_call_target="tpu_custom_call" | custom-call | bytes 11010048 | tf_op jit(solution)/shard_map/pallas_call | solution.py:65
  9.2 0.2 collective-permute-done.1.far_tail_ref
  9.4 0.1 collective-permute-start.4
  9.5 1.8 %collective-permute-start.3 = (bf16[8,7296]{1,0:T(8,128)(2,1)S(1)}, bf16[8,7296]{1,0:T(8,128)(2,1)S(1)}, u32[]{:S(2)}, u32[]{:S(2)}) collective-permute-start(bf16[8,7296]{1,0:T(8,128)(2,1)S(1)} %shard_map.75.refs_0_), channel_id=1, source_target_pairs={{0,4},{1,3},{2,6},{3,1},{4,0},{5,7},{6,2},{7,5},{8,12},{9,11},{10,... | collective-permute-start | bytes 350216 | tf_op jit(solution)/shard_map/ppermute | solution.py:26
  11.3 1.5 %collective-permute-start.7 = (bf16[8,7296]{1,0:T(8,128)(2,1)S(1)}, bf16[8,7296]{1,0:T(8,128)(2,1)S(1)}, u32[]{:S(2)}, u32[]{:S(2)}) collective-permute-start(bf16[8,7296]{1,0:T(8,128)(2,1)S(1)} %shard_map.75.refs_0_), channel_id=1, source_target_pairs={{0,2},{1,5},{2,0},{3,7},{4,6},{5,1},{6,4},{7,3},{8,10},{9,13},{10,... | collective-permute-start | bytes 350216 | tf_op jit(solution)/shard_map/ppermute | solution.py:26
  12.8 0.3 collective-permute-start.6
  13.1 1.8 %shard_map.76 = (bf16[8,7168]{1,0:T(8,128)(2,1)S(1)}, bf16[8,7168]{1,0:T(8,128)(2,1)S(1)}, bf16[16,128]{1,0:T(8,128)(2,1)S(1)}) custom-call(bf16[8,7296]{1,0:T(8,128)(2,1)S(1)} %shard_map.75.refs_0_, bf16[8,7296]{1,0:T(8,128)(2,1)S(1)} %collective-permute-done.4.refs_1_, f32[1,7168]{1,0:T(1,128)S(1)} %copy-done, ...), custom_call_target="tpu_custom_call" | custom-call | flops 176160768 | bytes 11010048 | tf_op jit(solution)/shard_map/pallas_call | solution.py:43
  14.8 2.8 %collective-permute-done.7.refs_1_ = bf16[8,7296]{1,0:T(8,128)(2,1)S(1)} collective-permute-done((bf16[8,7296]{1,0:T(8,128)(2,1)S(1)}, bf16[8,7296]{1,0:T(8,128)(2,1)S(1)}, u32[]{:S(2)}, u32[]{:S(2)}) %collective-permute-start.7) | collective-permute-done | bytes 116768 | tf_op jit(solution)/shard_map/ppermute | solution.py:26
  17.7 1.1 %collective-permute-done.6.refs_0_ = bf16[8,7296]{1,0:T(8,128)(2,1)S(1)} collective-permute-done((bf16[8,7296]{1,0:T(8,128)(2,1)S(1)}, bf16[8,7296]{1,0:T(8,128)(2,1)S(1)}, u32[]{:S(2)}, u32[]{:S(2)}) %collective-permute-start.6) | collective-permute-done | bytes 116768 | tf_op jit(solution)/shard_map/ppermute | solution.py:26
  18.8 0.5 collective-permute-start.10
  19.3 0.8 %collective-permute-done.8.refs_3_ = bf16[8,7296]{1,0:T(8,128)(2,1)S(1)} collective-permute-done((bf16[8,7296]{1,0:T(8,128)(2,1)S(1)}, bf16[8,7296]{1,0:T(8,128)(2,1)S(1)}, u32[]{:S(2)}, u32[]{:S(2)}) %collective-permute-start.8) | collective-permute-done | bytes 116768 | tf_op jit(solution)/shard_map/ppermute | solution.py:26
  20.1 0.2 collective-permute-done.10.refs_5_
  20.3 2.3 %shard_map.77 = (bf16[8,7168]{1,0:T(8,128)(2,1)S(1)}, bf16[8,7168]{1,0:T(8,128)(2,1)S(1)}, bf16[8,7168]{1,0:T(8,128)(2,1)S(1)}, bf16[8,7168]{1,0:T(8,128)(2,1)S(...) custom-call(bf16[8,7296]{1,0:T(8,128)(2,1)S(1)} %collective-permute-done.6.refs_0_, ...), custom_call_target="tpu_custom_call" | custom-call | flops 528482304 | bytes 11010048 | tf_op jit(solution)/shard_map/pallas_call | solution.py:43
  22.6 0.4 collective-permute-start.11
  23.0 0.2 collective-permute-start.13
  23.2 0.3 collective-permute-start.15
  23.5 0.2 collective-permute-start.5
  23.7 0.3 collective-permute-done.11.refs_1_
  24.0 1.8 %collective-permute-start.12 = (bf16[8,7168]{1,0:T(8,128)(2,1)S(1)}, bf16[8,7168]{1,0:T(8,128)(2,1)S(1)}, u32[]{:S(2)}, u32[]{:S(2)}) collective-permute-start(bf16[8,7168]{1,0:T(8,128)(2,1)S(1)} %shard_map.78), channel_id=1, source_target_pairs={{0,4},{1,3},{2,6},{3,1},{4,0},{5,7},{6,2},{7,5},{8,12},{9,11},{10,... | collective-permute-start | bytes 344072 | tf_op jit(solution)/shard_map/ppermute | solution.py:26
  25.8 0.5 collective-permute-start.14
  26.4 1.4 %collective-permute-start.16 = (bf16[8,7168]{1,0:T(8,128)(2,1)S(1)}, bf16[8,7168]{1,0:T(8,128)(2,1)S(1)}, u32[]{:S(2)}, u32[]{:S(2)}) collective-permute-start(bf16[8,7168]{1,0:T(8,128)(2,1)S(1)} %shard_map.80), channel_id=1, source_target_pairs={{0,6},{1,7},{2,4},{3,5},{4,2},{5,3},{6,0},{7,1},{8,14},{9,15},{10,... | collective-permute-start | bytes 344072 | tf_op jit(solution)/shard_map/ppermute | solution.py:26
  27.8 1.6 %collective-permute-start.2 = (bf16[8,7296]{1,0:T(8,128)(2,1)S(1)}, bf16[8,7296]{1,0:T(8,128)(2,1)S(1)}, u32[]{:S(2)}, u32[]{:S(2)}) collective-permute-start(bf16[8,7296]{1,0:T(8,128)(2,1)S(1)} %shard_map.75.refs_0_), channel_id=1, source_target_pairs={{0,16},{1,17},{2,18},{3,19},{4,20},{5,21},{6,22},{7,23},{8,24},{9,... | collective-permute-start | bytes 350216 | tf_op jit(solution)/shard_map/ppermute | solution.py:26
  29.4 0.1 collective-permute-done.12.refs_2_
  29.5 1.5 %collective-permute-done.14.refs_3_ = bf16[8,7168]{1,0:T(8,128)(2,1)S(1)} collective-permute-done((bf16[8,7168]{1,0:T(8,128)(2,1)S(1)}, bf16[8,7168]{1,0:T(8,128)(2,1)S(1)}, u32[]{:S(2)}, u32[]{:S(2)}) %collective-permute-start.14) | collective-permute-done | bytes 114720 | tf_op jit(solution)/shard_map/ppermute | solution.py:26
  31.0 2.2 %collective-permute-done.16.refs_4_ = bf16[8,7168]{1,0:T(8,128)(2,1)S(1)} collective-permute-done((bf16[8,7168]{1,0:T(8,128)(2,1)S(1)}, bf16[8,7168]{1,0:T(8,128)(2,1)S(1)}, u32[]{:S(2)}, u32[]{:S(2)}) %collective-permute-start.16) | collective-permute-done | bytes 114720 | tf_op jit(solution)/shard_map/ppermute | solution.py:26
  33.2 0.1 shard_map.81
  33.3 1.7 %collective-permute-start.18 = (bf16[8,7168]{1,0:T(8,128)(2,1)S(1)}, bf16[8,7168]{1,0:T(8,128)(2,1)S(1)}, u32[]{:S(2)}, u32[]{:S(2)}) collective-permute-start(bf16[8,7168]{1,0:T(8,128)(2,1)S(1)} %shard_map.81), channel_id=1, source_target_pairs={{0,16},{1,17},{2,18},{3,19},{4,20},{5,21},{6,22},{7,23},{8,24},{9,... | collective-permute-start | bytes 344072 | tf_op jit(solution)/shard_map/ppermute | solution.py:26
  35.0 2.6 %collective-permute-start.17 = (bf16[8,7168]{1,0:T(8,128)(2,1)S(1)}, bf16[8,7168]{1,0:T(8,128)(2,1)S(1)}, u32[]{:S(2)}, u32[]{:S(2)}) collective-permute-start(bf16[8,7168]{1,0:T(8,128)(2,1)S(1)} %shard_map.81), channel_id=1, source_target_pairs={{0,24},{1,25},{2,26},{3,27},{4,28},{5,29},{6,30},{7,31},{8,16},{9,... | collective-permute-start | bytes 344072 | tf_op jit(solution)/shard_map/ppermute | solution.py:26
  37.6 0.6 collective-permute-done.18.near_ref
  38.2 5.4 %collective-permute-done.17.far_ref = bf16[8,7168]{1,0:T(8,128)(2,1)S(1)} collective-permute-done((bf16[8,7168]{1,0:T(8,128)(2,1)S(1)}, bf16[8,7168]{1,0:T(8,128)(2,1)S(1)}, u32[]{:S(2)}, u32[]{:S(2)}) %collective-permute-start.17) | collective-permute-done | bytes 114720 | tf_op jit(solution)/shard_map/ppermute | solution.py:26
  43.6 0.1 shard_map.82
  43.7 0.1 collective-permute-start.21
  43.7 0.1 collective-permute-start.20
  43.8 0.6 collective-permute-start.24
  44.4 2.9 %collective-permute-start.23 = (bf16[8,7168]{1,0:T(8,128)(2,1)S(1)}, bf16[8,7168]{1,0:T(8,128)(2,1)S(1)}, u32[]{:S(2)}, u32[]{:S(2)}) collective-permute-start(bf16[8,7168]{1,0:T(8,128)(2,1)S(1)} %get-tuple-element.61.refs_0_), channel_id=1, source_target_pairs={{0,6},{1,7},{2,4},{3,5},{4,2},{5,3},{6,0},{7,1},{8,14},{9,15},{10,... | collective-permute-start | bytes 344072 | tf_op jit(solution)/shard_map/ppermute | solution.py:26
  47.3 1.8 %shard_map.83 = (bf16[8,7168]{1,0:T(8,128)(2,1)S(1)}, bf16[8,7168]{1,0:T(8,128)(2,1)S(1)}) custom-call(bf16[8,7168]{1,0:T(8,128)(2,1)S(1)} %get-tuple-element.61.refs_0_, bf16[8,7168]{1,0:T(8,128)(2,1)S(1)} %collective-permute-done.21.refs_1_, bf16[16,128]{1,0:T(8,128)(2,1)S(1)} %get-tuple-element.62.refs_2_, f32[1,7168]{1,0:T(1,128)S(1)} %copy-done, ...), custom_call_target="tpu_custom_call" | custom-call | flops 176160768 | bytes 11010048 | tf_op jit(solution)/shard_map/pallas_call | solution.py:43
  49.1 0.8 %collective-permute-done.20.refs_2_ = bf16[8,7168]{1,0:T(8,128)(2,1)S(1)} collective-permute-done((bf16[8,7168]{1,0:T(8,128)(2,1)S(1)}, bf16[8,7168]{1,0:T(8,128)(2,1)S(1)}, u32[]{:S(2)}, u32[]{:S(2)}) %collective-permute-start.20) | collective-permute-done | bytes 114720 | tf_op jit(solution)/shard_map/ppermute | solution.py:26
  49.8 1.7 %collective-permute-done.23.refs_0_ = bf16[8,7168]{1,0:T(8,128)(2,1)S(1)} collective-permute-done((bf16[8,7168]{1,0:T(8,128)(2,1)S(1)}, bf16[8,7168]{1,0:T(8,128)(2,1)S(1)}, u32[]{:S(2)}, u32[]{:S(2)}) %collective-permute-start.23) | collective-permute-done | bytes 114720 | tf_op jit(solution)/shard_map/ppermute | solution.py:26
  51.5 0.5 collective-permute-start.25
  52.0 0.0 collective-permute-start.27
  52.1 1.0 %collective-permute-done.25.refs_3_ = bf16[8,7168]{1,0:T(8,128)(2,1)S(1)} collective-permute-done((bf16[8,7168]{1,0:T(8,128)(2,1)S(1)}, bf16[8,7168]{1,0:T(8,128)(2,1)S(1)}, u32[]{:S(2)}, u32[]{:S(2)}) %collective-permute-start.25) | collective-permute-done | bytes 114720 | tf_op jit(solution)/shard_map/ppermute | solution.py:26
  53.0 0.4 collective-permute-done.27.refs_5_
  53.4 2.3 %shard_map.84 = (bf16[8,7168]{1,0:T(8,128)(2,1)S(1)}, bf16[8,7168]{1,0:T(8,128)(2,1)S(1)}, bf16[8,7168]{1,0:T(8,128)(2,1)S(1)}, bf16[8,7168]{1,0:T(8,128)(2,1)S(...) custom-call(bf16[8,7168]{1,0:T(8,128)(2,1)S(1)} %collective-permute-done.23.refs_0_, ...), custom_call_target="tpu_custom_call" | custom-call | flops 528482304 | bytes 11010048 | tf_op jit(solution)/shard_map/pallas_call | solution.py:43
  55.7 0.2 collective-permute-start.28
  55.9 0.3 collective-permute-start.30
  56.2 0.2 collective-permute-start.32
  56.4 0.3 collective-permute-start.22
  56.8 0.3 collective-permute-done.28.refs_1_
  57.1 1.6 %collective-permute-start.29 = (bf16[8,7168]{1,0:T(8,128)(2,1)S(1)}, bf16[8,7168]{1,0:T(8,128)(2,1)S(1)}, u32[]{:S(2)}, u32[]{:S(2)}) collective-permute-start(bf16[8,7168]{1,0:T(8,128)(2,1)S(1)} %shard_map.85), channel_id=1, source_target_pairs={{0,4},{1,3},{2,6},{3,1},{4,0},{5,7},{6,2},{7,5},{8,12},{9,11},{10,... | collective-permute-start | bytes 344072 | tf_op jit(solution)/shard_map/ppermute | solution.py:26
  58.8 0.3 collective-permute-start.31
  59.1 1.7 %collective-permute-start.33 = (bf16[8,7168]{1,0:T(8,128)(2,1)S(1)}, bf16[8,7168]{1,0:T(8,128)(2,1)S(1)}, u32[]{:S(2)}, u32[]{:S(2)}) collective-permute-start(bf16[8,7168]{1,0:T(8,128)(2,1)S(1)} %shard_map.87), channel_id=1, source_target_pairs={{0,6},{1,7},{2,4},{3,5},{4,2},{5,3},{6,0},{7,1},{8,14},{9,15},{10,... | collective-permute-start | bytes 344072 | tf_op jit(solution)/shard_map/ppermute | solution.py:26
  60.9 0.6 collective-permute-start.19
  61.5 1.0 %collective-permute-done.29.refs_2_ = bf16[8,7168]{1,0:T(8,128)(2,1)S(1)} collective-permute-done((bf16[8,7168]{1,0:T(8,128)(2,1)S(1)}, bf16[8,7168]{1,0:T(8,128)(2,1)S(1)}, u32[]{:S(2)}, u32[]{:S(2)}) %collective-permute-start.29) | collective-permute-done | bytes 114720 | tf_op jit(solution)/shard_map/ppermute | solution.py:26
  62.5 1.4 %collective-permute-done.31.refs_3_ = bf16[8,7168]{1,0:T(8,128)(2,1)S(1)} collective-permute-done((bf16[8,7168]{1,0:T(8,128)(2,1)S(1)}, bf16[8,7168]{1,0:T(8,128)(2,1)S(1)}, u32[]{:S(2)}, u32[]{:S(2)}) %collective-permute-start.31) | collective-permute-done | bytes 114720 | tf_op jit(solution)/shard_map/ppermute | solution.py:26
  63.9 2.3 %collective-permute-done.33.refs_4_ = bf16[8,7168]{1,0:T(8,128)(2,1)S(1)} collective-permute-done((bf16[8,7168]{1,0:T(8,128)(2,1)S(1)}, bf16[8,7168]{1,0:T(8,128)(2,1)S(1)}, u32[]{:S(2)}, u32[]{:S(2)}) %collective-permute-start.33) | collective-permute-done | bytes 114720 | tf_op jit(solution)/shard_map/ppermute | solution.py:26
  66.2 0.1 shard_map.88
  66.3 2.6 %collective-permute-start.34 = (bf16[4,7168]{1,0:T(4,128)(2,1)S(1)}, bf16[4,7168]{1,0:T(4,128)(2,1)S(1)}, u32[]{:S(2)}, u32[]{:S(2)}) collective-permute-start(bf16[4,7168]{1,0:T(4,128)(2,1)S(1)} %get-tuple-element.75), channel_id=1, source_target_pairs={{0,24},{1,25},{2,26},{3,27},{4,28},{5,29},{6,30},{7,31},{8,16},{9,... | collective-permute-start | bytes 172040 | tf_op jit(solution)/shard_map/ppermute | solution.py:26
  68.9 1.5 %collective-permute-start.35 = (bf16[4,7168]{1,0:T(4,128)(2,1)S(1)}, bf16[4,7168]{1,0:T(4,128)(2,1)S(1)}, u32[]{:S(2)}, u32[]{:S(2)}) collective-permute-start(bf16[4,7168]{1,0:T(4,128)(2,1)S(1)} %get-tuple-element.76), channel_id=1, source_target_pairs={{0,16},{1,17},{2,18},{3,19},{4,20},{5,21},{6,22},{7,23},{8,24},{9,... | collective-permute-start | bytes 172040 | tf_op jit(solution)/shard_map/ppermute | solution.py:26
  70.4 2.6 %collective-permute-done.34.refs_1_ = bf16[4,7168]{1,0:T(4,128)(2,1)S(1)} collective-permute-done((bf16[4,7168]{1,0:T(4,128)(2,1)S(1)}, bf16[4,7168]{1,0:T(4,128)(2,1)S(1)}, u32[]{:S(2)}, u32[]{:S(2)}) %collective-permute-start.34) | collective-permute-done | bytes 57376 | tf_op jit(solution)/shard_map/ppermute | solution.py:26
  73.0 0.4 collective-permute-done.35.refs_2_
  73.4 0.7 shard_map.89
  (29 shorter events, 0.3 us)
Async XLA Ops:
  0.0 9.4 %collective-permute-start = (bf16[4,7168]{1,0:T(4,128)(2,1)}, bf16[4,7168]{1,0:T(4,128)(2,1)S(1)}, u32[]{:S(2)}, u32[]{:S(2)}) collective-permute-start(bf16[4,7168]{1,0:T(4,128)(2,1)} %bitcast.4), channel_id=1, source_target_pairs={{0,8},{1,9},{2,10},{3,11},{4,12},{5,13},{6,14},{7,15},{8,0},{9,1},... | collective-permute-start | bytes 172040 | tf_op jit(solution)/shard_map/ppermute | solution.py:26
  4.8 4.6 %copy-start.1 = (bf16[1,4,7168]{2,1,0:T(4,128)(2,1)S(1)}, bf16[1,4,7168]{2,1,0:T(4,128)(2,1)}, u32[]{:S(2)}) copy-start(bf16[1,4,7168]{2,1,0:T(4,128)(2,1)} %param.7) | copy-start | bytes 172036
  4.9 8.2 %copy-start = (f32[1,7168]{1,0:T(1,128)S(1)}, f32[1,7168]{1,0:T(1,128)}, u32[]{:S(2)}) copy-start(f32[1,7168]{1,0:T(1,128)} %refs_7_.1) | copy-start | bytes 86020
  4.9 4.5 %collective-permute-start.1 = (bf16[4,128]{1,0:T(4,128)(2,1)S(1)}, bf16[4,128]{1,0:T(4,128)(2,1)S(1)}, u32[]{:S(2)}, u32[]{:S(2)}) collective-permute-start(bf16[4,128]{1,0:T(4,128)(2,1)S(1)} %shard_map.73.own_tail_ref), channel_id=1, source_target_pairs={{0,8},{1,9},{2,10},{3,11},{4,12},{5,13},{6,14},{7,15},{8,0},{9,1},... | collective-permute-start | bytes 3080 | tf_op jit(solution)/shard_map/ppermute | solution.py:26
  9.4 3.6 %collective-permute-start.4 = (bf16[8,7296]{1,0:T(8,128)(2,1)S(1)}, bf16[8,7296]{1,0:T(8,128)(2,1)S(1)}, u32[]{:S(2)}, u32[]{:S(2)}) collective-permute-start(bf16[8,7296]{1,0:T(8,128)(2,1)S(1)} %shard_map.75.refs_0_), channel_id=1, source_target_pairs={{0,1},{1,0},{2,3},{3,2},{4,5},{5,4},{6,7},{7,6},{8,9},{9,8},{10,11... | collective-permute-start | bytes 350216 | tf_op jit(solution)/shard_map/ppermute | solution.py:26
  9.5 5.3 %collective-permute-start.3 = (bf16[8,7296]{1,0:T(8,128)(2,1)S(1)}, bf16[8,7296]{1,0:T(8,128)(2,1)S(1)}, u32[]{:S(2)}, u32[]{:S(2)}) collective-permute-start(bf16[8,7296]{1,0:T(8,128)(2,1)S(1)} %shard_map.75.refs_0_), channel_id=1, source_target_pairs={{0,4},{1,3},{2,6},{3,1},{4,0},{5,7},{6,2},{7,5},{8,12},{9,11},{10,... | collective-permute-start | bytes 350216 | tf_op jit(solution)/shard_map/ppermute | solution.py:26
  11.3 6.4 %collective-permute-start.7 = (bf16[8,7296]{1,0:T(8,128)(2,1)S(1)}, bf16[8,7296]{1,0:T(8,128)(2,1)S(1)}, u32[]{:S(2)}, u32[]{:S(2)}) collective-permute-start(bf16[8,7296]{1,0:T(8,128)(2,1)S(1)} %shard_map.75.refs_0_), channel_id=1, source_target_pairs={{0,2},{1,5},{2,0},{3,7},{4,6},{5,1},{6,4},{7,3},{8,10},{9,13},{10,... | collective-permute-start | bytes 350216 | tf_op jit(solution)/shard_map/ppermute | solution.py:26
  12.8 6.0 %collective-permute-start.6 = (bf16[8,7296]{1,0:T(8,128)(2,1)S(1)}, bf16[8,7296]{1,0:T(8,128)(2,1)S(1)}, u32[]{:S(2)}, u32[]{:S(2)}) collective-permute-start(bf16[8,7296]{1,0:T(8,128)(2,1)S(1)} %shard_map.75.refs_0_), channel_id=1, source_target_pairs={{0,6},{1,7},{2,4},{3,5},{4,2},{5,3},{6,0},{7,1},{8,14},{9,15},{10,... | collective-permute-start | bytes 350216 | tf_op jit(solution)/shard_map/ppermute | solution.py:26
  17.7 1.6 %collective-permute-start.9 = (bf16[8,7296]{1,0:T(8,128)(2,1)S(1)}, bf16[8,7296]{1,0:T(8,128)(2,1)S(1)}, u32[]{:S(2)}, u32[]{:S(2)}) collective-permute-start(bf16[8,7296]{1,0:T(8,128)(2,1)S(1)} %collective-permute-done.7.refs_1_), channel_id=1, source_target_pairs={{0,1},{1,0},{2,3},{3,2},{4,5},{5,4},{6,7},{7,6},{8,9},{9,8},{10,11... | collective-permute-start | bytes 350216 | tf_op jit(solution)/shard_map/ppermute | solution.py:26
  18.8 1.3 %collective-permute-start.8 = (bf16[8,7296]{1,0:T(8,128)(2,1)S(1)}, bf16[8,7296]{1,0:T(8,128)(2,1)S(1)}, u32[]{:S(2)}, u32[]{:S(2)}) collective-permute-start(bf16[8,7296]{1,0:T(8,128)(2,1)S(1)} %collective-permute-done.6.refs_0_), channel_id=1, source_target_pairs={{0,1},{1,0},{2,3},{3,2},{4,5},{5,4},{6,7},{7,6},{8,9},{9,8},{10,11... | collective-permute-start | bytes 350216 | tf_op jit(solution)/shard_map/ppermute | solution.py:26
  18.8 1.5 %collective-permute-start.10 = (bf16[8,7296]{1,0:T(8,128)(2,1)S(1)}, bf16[8,7296]{1,0:T(8,128)(2,1)S(1)}, u32[]{:S(2)}, u32[]{:S(2)}) collective-permute-start(bf16[8,7296]{1,0:T(8,128)(2,1)S(1)} %collective-permute-done.3.refs_2_), channel_id=1, source_target_pairs={{0,1},{1,0},{2,3},{3,2},{4,5},{5,4},{6,7},{7,6},{8,9},{9,8},{10,11... | collective-permute-start | bytes 350216 | tf_op jit(solution)/shard_map/ppermute | solution.py:26
  22.6 1.4 %collective-permute-start.11 = (bf16[8,7168]{1,0:T(8,128)(2,1)S(1)}, bf16[8,7168]{1,0:T(8,128)(2,1)S(1)}, u32[]{:S(2)}, u32[]{:S(2)}) collective-permute-start(bf16[8,7168]{1,0:T(8,128)(2,1)S(1)} %get-tuple-element.55), channel_id=1, source_target_pairs={{0,1},{1,0},{2,3},{3,2},{4,5},{5,4},{6,7},{7,6},{8,9},{9,8},{10,11... | collective-permute-start | bytes 344072 | tf_op jit(solution)/shard_map/ppermute | solution.py:26
  23.0 2.8 %collective-permute-start.13 = (bf16[8,7168]{1,0:T(8,128)(2,1)S(1)}, bf16[8,7168]{1,0:T(8,128)(2,1)S(1)}, u32[]{:S(2)}, u32[]{:S(2)}) collective-permute-start(bf16[8,7168]{1,0:T(8,128)(2,1)S(1)} %get-tuple-element.57), channel_id=1, source_target_pairs={{0,1},{1,0},{2,3},{3,2},{4,5},{5,4},{6,7},{7,6},{8,9},{9,8},{10,11... | collective-permute-start | bytes 344072 | tf_op jit(solution)/shard_map/ppermute | solution.py:26
  23.2 3.2 %collective-permute-start.15 = (bf16[8,7168]{1,0:T(8,128)(2,1)S(1)}, bf16[8,7168]{1,0:T(8,128)(2,1)S(1)}, u32[]{:S(2)}, u32[]{:S(2)}) collective-permute-start(bf16[8,7168]{1,0:T(8,128)(2,1)S(1)} %get-tuple-element.59), channel_id=1, source_target_pairs={{0,1},{1,0},{2,3},{3,2},{4,5},{5,4},{6,7},{7,6},{8,9},{9,8},{10,11... | collective-permute-start | bytes 344072 | tf_op jit(solution)/shard_map/ppermute | solution.py:26
  23.5 5.9 %collective-permute-start.5 = (bf16[8,7168]{1,0:T(8,128)(2,1)S(1)}, bf16[8,7168]{1,0:T(8,128)(2,1)S(1)}, u32[]{:S(2)}, u32[]{:S(2)}) collective-permute-start(bf16[8,7168]{1,0:T(8,128)(2,1)S(1)} %get-tuple-element.52), channel_id=1, source_target_pairs={{0,1},{1,0},{2,3},{3,2},{4,5},{5,4},{6,7},{7,6},{8,9},{9,8},{10,11... | collective-permute-start | bytes 344072 | tf_op jit(solution)/shard_map/ppermute | solution.py:26
  24.0 5.4 %collective-permute-start.12 = (bf16[8,7168]{1,0:T(8,128)(2,1)S(1)}, bf16[8,7168]{1,0:T(8,128)(2,1)S(1)}, u32[]{:S(2)}, u32[]{:S(2)}) collective-permute-start(bf16[8,7168]{1,0:T(8,128)(2,1)S(1)} %shard_map.78), channel_id=1, source_target_pairs={{0,4},{1,3},{2,6},{3,1},{4,0},{5,7},{6,2},{7,5},{8,12},{9,11},{10,... | collective-permute-start | bytes 344072 | tf_op jit(solution)/shard_map/ppermute | solution.py:26
  25.8 5.2 %collective-permute-start.14 = (bf16[8,7168]{1,0:T(8,128)(2,1)S(1)}, bf16[8,7168]{1,0:T(8,128)(2,1)S(1)}, u32[]{:S(2)}, u32[]{:S(2)}) collective-permute-start(bf16[8,7168]{1,0:T(8,128)(2,1)S(1)} %shard_map.79), channel_id=1, source_target_pairs={{0,2},{1,5},{2,0},{3,7},{4,6},{5,1},{6,4},{7,3},{8,10},{9,13},{10,... | collective-permute-start | bytes 344072 | tf_op jit(solution)/shard_map/ppermute | solution.py:26
  26.4 6.8 %collective-permute-start.16 = (bf16[8,7168]{1,0:T(8,128)(2,1)S(1)}, bf16[8,7168]{1,0:T(8,128)(2,1)S(1)}, u32[]{:S(2)}, u32[]{:S(2)}) collective-permute-start(bf16[8,7168]{1,0:T(8,128)(2,1)S(1)} %shard_map.80), channel_id=1, source_target_pairs={{0,6},{1,7},{2,4},{3,5},{4,2},{5,3},{6,0},{7,1},{8,14},{9,15},{10,... | collective-permute-start | bytes 344072 | tf_op jit(solution)/shard_map/ppermute | solution.py:26
  27.8 9.8 %collective-permute-start.2 = (bf16[8,7296]{1,0:T(8,128)(2,1)S(1)}, bf16[8,7296]{1,0:T(8,128)(2,1)S(1)}, u32[]{:S(2)}, u32[]{:S(2)}) collective-permute-start(bf16[8,7296]{1,0:T(8,128)(2,1)S(1)} %shard_map.75.refs_0_), channel_id=1, source_target_pairs={{0,16},{1,17},{2,18},{3,19},{4,20},{5,21},{6,22},{7,23},{8,24},{9,... | collective-permute-start | bytes 350216 | tf_op jit(solution)/shard_map/ppermute | solution.py:26
  33.3 4.9 %collective-permute-start.18 = (bf16[8,7168]{1,0:T(8,128)(2,1)S(1)}, bf16[8,7168]{1,0:T(8,128)(2,1)S(1)}, u32[]{:S(2)}, u32[]{:S(2)}) collective-permute-start(bf16[8,7168]{1,0:T(8,128)(2,1)S(1)} %shard_map.81), channel_id=1, source_target_pairs={{0,16},{1,17},{2,18},{3,19},{4,20},{5,21},{6,22},{7,23},{8,24},{9,... | collective-permute-start | bytes 344072 | tf_op jit(solution)/shard_map/ppermute | solution.py:26
  35.0 8.6 %collective-permute-start.17 = (bf16[8,7168]{1,0:T(8,128)(2,1)S(1)}, bf16[8,7168]{1,0:T(8,128)(2,1)S(1)}, u32[]{:S(2)}, u32[]{:S(2)}) collective-permute-start(bf16[8,7168]{1,0:T(8,128)(2,1)S(1)} %shard_map.81), channel_id=1, source_target_pairs={{0,24},{1,25},{2,26},{3,27},{4,28},{5,29},{6,30},{7,31},{8,16},{9,... | collective-permute-start | bytes 344072 | tf_op jit(solution)/shard_map/ppermute | solution.py:26
  43.7 3.6 %collective-permute-start.21 = (bf16[8,7168]{1,0:T(8,128)(2,1)S(1)}, bf16[8,7168]{1,0:T(8,128)(2,1)S(1)}, u32[]{:S(2)}, u32[]{:S(2)}) collective-permute-start(bf16[8,7168]{1,0:T(8,128)(2,1)S(1)} %get-tuple-element.61.refs_0_), channel_id=1, source_target_pairs={{0,1},{1,0},{2,3},{3,2},{4,5},{5,4},{6,7},{7,6},{8,9},{9,8},{10,11... | collective-permute-start | bytes 344072 | tf_op jit(solution)/shard_map/ppermute | solution.py:26
  43.7 6.1 %collective-permute-start.20 = (bf16[8,7168]{1,0:T(8,128)(2,1)S(1)}, bf16[8,7168]{1,0:T(8,128)(2,1)S(1)}, u32[]{:S(2)}, u32[]{:S(2)}) collective-permute-start(bf16[8,7168]{1,0:T(8,128)(2,1)S(1)} %get-tuple-element.61.refs_0_), channel_id=1, source_target_pairs={{0,4},{1,3},{2,6},{3,1},{4,0},{5,7},{6,2},{7,5},{8,12},{9,11},{10,... | collective-permute-start | bytes 344072 | tf_op jit(solution)/shard_map/ppermute | solution.py:26
  43.8 6.0 %collective-permute-start.24 = (bf16[8,7168]{1,0:T(8,128)(2,1)S(1)}, bf16[8,7168]{1,0:T(8,128)(2,1)S(1)}, u32[]{:S(2)}, u32[]{:S(2)}) collective-permute-start(bf16[8,7168]{1,0:T(8,128)(2,1)S(1)} %get-tuple-element.61.refs_0_), channel_id=1, source_target_pairs={{0,2},{1,5},{2,0},{3,7},{4,6},{5,1},{6,4},{7,3},{8,10},{9,13},{10,... | collective-permute-start | bytes 344072 | tf_op jit(solution)/shard_map/ppermute | solution.py:26
  44.4 7.2 %collective-permute-start.23 = (bf16[8,7168]{1,0:T(8,128)(2,1)S(1)}, bf16[8,7168]{1,0:T(8,128)(2,1)S(1)}, u32[]{:S(2)}, u32[]{:S(2)}) collective-permute-start(bf16[8,7168]{1,0:T(8,128)(2,1)S(1)} %get-tuple-element.61.refs_0_), channel_id=1, source_target_pairs={{0,6},{1,7},{2,4},{3,5},{4,2},{5,3},{6,0},{7,1},{8,14},{9,15},{10,... | collective-permute-start | bytes 344072 | tf_op jit(solution)/shard_map/ppermute | solution.py:26
  49.8 2.2 %collective-permute-start.26 = (bf16[8,7168]{1,0:T(8,128)(2,1)S(1)}, bf16[8,7168]{1,0:T(8,128)(2,1)S(1)}, u32[]{:S(2)}, u32[]{:S(2)}) collective-permute-start(bf16[8,7168]{1,0:T(8,128)(2,1)S(1)} %collective-permute-done.24.refs_1_), channel_id=1, source_target_pairs={{0,1},{1,0},{2,3},{3,2},{4,5},{5,4},{6,7},{7,6},{8,9},{9,8},{10,11... | collective-permute-start | bytes 344072 | tf_op jit(solution)/shard_map/ppermute | solution.py:26
  51.5 1.5 %collective-permute-start.25 = (bf16[8,7168]{1,0:T(8,128)(2,1)S(1)}, bf16[8,7168]{1,0:T(8,128)(2,1)S(1)}, u32[]{:S(2)}, u32[]{:S(2)}) collective-permute-start(bf16[8,7168]{1,0:T(8,128)(2,1)S(1)} %collective-permute-done.23.refs_0_), channel_id=1, source_target_pairs={{0,1},{1,0},{2,3},{3,2},{4,5},{5,4},{6,7},{7,6},{8,9},{9,8},{10,11... | collective-permute-start | bytes 344072 | tf_op jit(solution)/shard_map/ppermute | solution.py:26
  52.0 1.3 %collective-permute-start.27 = (bf16[8,7168]{1,0:T(8,128)(2,1)S(1)}, bf16[8,7168]{1,0:T(8,128)(2,1)S(1)}, u32[]{:S(2)}, u32[]{:S(2)}) collective-permute-start(bf16[8,7168]{1,0:T(8,128)(2,1)S(1)} %collective-permute-done.20.refs_2_), channel_id=1, source_target_pairs={{0,1},{1,0},{2,3},{3,2},{4,5},{5,4},{6,7},{7,6},{8,9},{9,8},{10,11... | collective-permute-start | bytes 344072 | tf_op jit(solution)/shard_map/ppermute | solution.py:26
  55.7 1.4 %collective-permute-start.28 = (bf16[8,7168]{1,0:T(8,128)(2,1)S(1)}, bf16[8,7168]{1,0:T(8,128)(2,1)S(1)}, u32[]{:S(2)}, u32[]{:S(2)}) collective-permute-start(bf16[8,7168]{1,0:T(8,128)(2,1)S(1)} %get-tuple-element.70), channel_id=1, source_target_pairs={{0,1},{1,0},{2,3},{3,2},{4,5},{5,4},{6,7},{7,6},{8,9},{9,8},{10,11... | collective-permute-start | bytes 344072 | tf_op jit(solution)/shard_map/ppermute | solution.py:26
  55.9 2.8 %collective-permute-start.30 = (bf16[8,7168]{1,0:T(8,128)(2,1)S(1)}, bf16[8,7168]{1,0:T(8,128)(2,1)S(1)}, u32[]{:S(2)}, u32[]{:S(2)}) collective-permute-start(bf16[8,7168]{1,0:T(8,128)(2,1)S(1)} %get-tuple-element.72), channel_id=1, source_target_pairs={{0,1},{1,0},{2,3},{3,2},{4,5},{5,4},{6,7},{7,6},{8,9},{9,8},{10,11... | collective-permute-start | bytes 344072 | tf_op jit(solution)/shard_map/ppermute | solution.py:26
  56.2 2.9 %collective-permute-start.32 = (bf16[8,7168]{1,0:T(8,128)(2,1)S(1)}, bf16[8,7168]{1,0:T(8,128)(2,1)S(1)}, u32[]{:S(2)}, u32[]{:S(2)}) collective-permute-start(bf16[8,7168]{1,0:T(8,128)(2,1)S(1)} %get-tuple-element.74), channel_id=1, source_target_pairs={{0,1},{1,0},{2,3},{3,2},{4,5},{5,4},{6,7},{7,6},{8,9},{9,8},{10,11... | collective-permute-start | bytes 344072 | tf_op jit(solution)/shard_map/ppermute | solution.py:26
  56.4 5.1 %collective-permute-start.22 = (bf16[8,7168]{1,0:T(8,128)(2,1)S(1)}, bf16[8,7168]{1,0:T(8,128)(2,1)S(1)}, u32[]{:S(2)}, u32[]{:S(2)}) collective-permute-start(bf16[8,7168]{1,0:T(8,128)(2,1)S(1)} %get-tuple-element.66), channel_id=1, source_target_pairs={{0,1},{1,0},{2,3},{3,2},{4,5},{5,4},{6,7},{7,6},{8,9},{9,8},{10,11... | collective-permute-start | bytes 344072 | tf_op jit(solution)/shard_map/ppermute | solution.py:26
  57.1 5.4 %collective-permute-start.29 = (bf16[8,7168]{1,0:T(8,128)(2,1)S(1)}, bf16[8,7168]{1,0:T(8,128)(2,1)S(1)}, u32[]{:S(2)}, u32[]{:S(2)}) collective-permute-start(bf16[8,7168]{1,0:T(8,128)(2,1)S(1)} %shard_map.85), channel_id=1, source_target_pairs={{0,4},{1,3},{2,6},{3,1},{4,0},{5,7},{6,2},{7,5},{8,12},{9,11},{10,... | collective-permute-start | bytes 344072 | tf_op jit(solution)/shard_map/ppermute | solution.py:26
  58.8 5.1 %collective-permute-start.31 = (bf16[8,7168]{1,0:T(8,128)(2,1)S(1)}, bf16[8,7168]{1,0:T(8,128)(2,1)S(1)}, u32[]{:S(2)}, u32[]{:S(2)}) collective-permute-start(bf16[8,7168]{1,0:T(8,128)(2,1)S(1)} %shard_map.86), channel_id=1, source_target_pairs={{0,2},{1,5},{2,0},{3,7},{4,6},{5,1},{6,4},{7,3},{8,10},{9,13},{10,... | collective-permute-start | bytes 344072 | tf_op jit(solution)/shard_map/ppermute | solution.py:26
  59.1 7.0 %collective-permute-start.33 = (bf16[8,7168]{1,0:T(8,128)(2,1)S(1)}, bf16[8,7168]{1,0:T(8,128)(2,1)S(1)}, u32[]{:S(2)}, u32[]{:S(2)}) collective-permute-start(bf16[8,7168]{1,0:T(8,128)(2,1)S(1)} %shard_map.87), channel_id=1, source_target_pairs={{0,6},{1,7},{2,4},{3,5},{4,2},{5,3},{6,0},{7,1},{8,14},{9,15},{10,... | collective-permute-start | bytes 344072 | tf_op jit(solution)/shard_map/ppermute | solution.py:26
  60.9 9.5 %collective-permute-start.19 = (bf16[4,7168]{1,0:T(4,128)(2,1)S(1)}, bf16[4,7168]{1,0:T(4,128)(2,1)S(1)}, u32[]{:S(2)}, u32[]{:S(2)}) collective-permute-start(bf16[4,7168]{1,0:T(4,128)(2,1)S(1)} %get-tuple-element.60), channel_id=1, source_target_pairs={{0,16},{1,17},{2,18},{3,19},{4,20},{5,21},{6,22},{7,23},{8,24},{9,... | collective-permute-start | bytes 172040 | tf_op jit(solution)/shard_map/ppermute | solution.py:26
  66.3 6.8 %collective-permute-start.34 = (bf16[4,7168]{1,0:T(4,128)(2,1)S(1)}, bf16[4,7168]{1,0:T(4,128)(2,1)S(1)}, u32[]{:S(2)}, u32[]{:S(2)}) collective-permute-start(bf16[4,7168]{1,0:T(4,128)(2,1)S(1)} %get-tuple-element.75), channel_id=1, source_target_pairs={{0,24},{1,25},{2,26},{3,27},{4,28},{5,29},{6,30},{7,31},{8,16},{9,... | collective-permute-start | bytes 172040 | tf_op jit(solution)/shard_map/ppermute | solution.py:26
  68.9 4.5 %collective-permute-start.35 = (bf16[4,7168]{1,0:T(4,128)(2,1)S(1)}, bf16[4,7168]{1,0:T(4,128)(2,1)S(1)}, u32[]{:S(2)}, u32[]{:S(2)}) collective-permute-start(bf16[4,7168]{1,0:T(4,128)(2,1)S(1)} %get-tuple-element.76), channel_id=1, source_target_pairs={{0,16},{1,17},{2,18},{3,19},{4,20},{5,21},{6,22},{7,23},{8,24},{9,... | collective-permute-start | bytes 172040 | tf_op jit(solution)/shard_map/ppermute | solution.py:26

commit v10 on v8

--- a/solution.py
+++ b/solution.py
@@ -9,7 +9,8 @@
 
 GROUP = 4
 LANES = 128
-CHUNK = 1024
+CHUNK = 896
+HALVES = 2
 VMEM_LIMIT = 16 * 1024 * 1024
 VMEM = pl.BlockSpec(memory_space=pltpu.VMEM)
 
@@ -138,47 +139,61 @@
             out_ref[:, span] = total[place * rows:(place + 1) * rows].astype(jnp.bfloat16)
 
 
-def meet_kernel(rest_ref, near_ref, far_ref, out_ref, own_ref):
+def meet_kernel(offset, rest_ref, near_ref, far_ref, out_ref, own_ref):
     half = own_ref.shape[0]
     for span in spans(out_ref.shape[1]):
         far = far_ref[:, span].astype(jnp.float32)
-        total = rest_ref[:, span].astype(jnp.float32) + near_ref[:, span].astype(jnp.float32)
+        rest = rest_ref[:, offset + span.start:offset + span.stop].astype(jnp.float32)
+        total = rest + near_ref[:, span].astype(jnp.float32)
         total = (total + jnp.concatenate([far[half:], far[:half]], axis=0)).astype(jnp.bfloat16)
         out_ref[:, span] = total
         own_ref[:, span] = total[:half]
 
 
-def mlp_kernel(step_no, *refs):
-    x_refs, refs = refs[:8], refs[8:]
+def widen_kernel(*refs):
+    *parts, out_ref = refs
+    start = 0
+    for part in parts:
+        out_ref[:, start:start + part.shape[1]] = part[...]
+        start += part.shape[1]
+
+
+def mlp_kernel(step_no, count, cuts_in, cuts_out, *refs):
+    x_refs, refs = refs[:count * cuts_in], refs[count * cuts_in:]
     if step_no > 0:
         tail_ref, refs = refs[0], refs[1:]
-    (gain_ref, gate_ref, up_ref, down_ref), outs, refs = refs[:4], refs[4:12], refs[12:]
+    (gain_ref, gate_ref, up_ref, down_ref), outs, refs = refs[:4], refs[4:4 + count * cuts_out], refs[4 + count * cuts_out:]
     rows_ref = refs[-1]
     part = outs[0].shape[0]
     dim, hidden = gate_ref.shape[1:]
+    width_in, width_out = dim // cuts_in, dim // cuts_out
     experts = lax.axis_size("expert") // GROUP
     column = step_no * experts + lax.axis_index("expert") // GROUP
     lane = lax.broadcasted_iota(jnp.int32, (part, LANES), 1)
     weights = []
-    for place, ref in enumerate(x_refs):
+    for place in range(count):
         band = slice(place * part, (place + 1) * part)
+        cuts = x_refs[place::count]
         square = jnp.zeros((part, LANES), jnp.float32)
-        for start in range(0, dim, LANES):
-            piece = ref[:, start:start + LANES].astype(jnp.float32)
-            square += piece * piece
+        for ref in cuts:
+            for start in range(0, width_in, LANES):
+                piece = ref[:, start:start + LANES].astype(jnp.float32)
+                square += piece * piece
         inv = lax.rsqrt(jnp.sum(square, axis=1, keepdims=True) / dim + 1e-06)
-        for span in spans(dim):
-            scaled = ref[:, span].astype(jnp.float32) * inv * gain_ref[:, span]
-            rows_ref[band, span] = scaled.astype(jnp.bfloat16)
+        for number, ref in enumerate(cuts):
+            for span in spans(width_in):
+                there = slice(number * width_in + span.start, number * width_in + span.stop)
+                scaled = ref[:, span].astype(jnp.float32) * inv * gain_ref[:, there]
+                rows_ref[band, there] = scaled.astype(jnp.bfloat16)
         if step_no == 0:
-            tail = ref[:, dim:]
+            tail = cuts[-1][:, width_in:]
             refs[0][band, :] = tail
         else:
             tail = tail_ref[band, :]
         chosen = jnp.where(lane == column, tail.astype(jnp.float32), 0.0)
         weights.append(jnp.sum(chosen, axis=1, keepdims=True))
-    gated = jnp.zeros((8 * part, hidden), jnp.float32)
-    up_part = jnp.zeros((8 * part, hidden), jnp.float32)
+    gated = jnp.zeros((count * part, hidden), jnp.float32)
+    up_part = jnp.zeros((count * part, hidden), jnp.float32)
     for span in spans(dim):
         rows = rows_ref[:, span]
         gated += jnp.dot(rows, gate_ref[0, span, :], preferred_element_type=jnp.float32)
@@ -186,26 +201,32 @@
     inner = (gated / (1.0 + jnp.exp(-gated)) * up_part).astype(jnp.bfloat16)
     for span in spans(dim):
         terms = jnp.dot(inner, down_ref[0, :, span], preferred_element_type=jnp.float32)
-        for place, out_ref in enumerate(outs):
+        cut = span.start // width_out
+        there = slice(span.start - cut * width_out, span.stop - cut * width_out)
+        for place in range(count):
             weight = weights[place]
             mine = terms[place * part:(place + 1) * part]
-            out_ref[:, span] = jnp.where(weight > 0.0, weight * mine, 0.0).astype(jnp.bfloat16)
-
-
-def mlp(step_no, xs, tail, gain, gate, up, down):
+            chosen = jnp.where(weight > 0.0, weight * mine, 0.0)
+            outs[cut * count + place][:, there] = chosen.astype(jnp.bfloat16)
+
+
+def mlp(step_no, cuts, cuts_out, tail, gain, gate, up, down):
     dim, hidden = gate.shape[1:]
-    part = xs[0].shape[0]
+    part, count = cuts[0][0].shape[0], len(cuts[0])
     gate, up, down = [pltpu.with_memory_space_constraint(w, pltpu.VMEM) for w in (gate, up, down)]
     first = step_no == 0
-    args = list(xs) + ([] if first else [tail]) + [gain, gate, up, down]
+    xs = [piece for cut in cuts for piece in cut]
+    args = xs + ([] if first else [tail]) + [gain, gate, up, down]
     result = call(
-        functools.partial(mlp_kernel, step_no), [(part, dim)] * 8 + [(8 * part, LANES)] * first, *args,
-        scratch_shapes=[pltpu.VMEM((8 * part, dim), jnp.bfloat16)],
+        functools.partial(mlp_kernel, step_no, count, len(cuts), cuts_out),
+        [(part, dim // cuts_out)] * (count * cuts_out) + [(count * part, LANES)] * first, *args,
+        scratch_shapes=[pltpu.VMEM((count * part, dim), jnp.bfloat16)],
         cost_estimate=pl.CostEstimate(
-            flops=48 * part * dim * hidden, bytes_accessed=6 * dim * hidden, transcendentals=0
+            flops=6 * count * part * dim * hidden, bytes_accessed=6 * dim * hidden, transcendentals=0
         ),
     )
-    return result[:8], result[8] if first else tail
+    outs = [result[number * count:(number + 1) * count] for number in range(cuts_out)]
+    return outs, result[-1] if first else tail
 
 
 def add(*parts):
@@ -235,30 +256,46 @@
     other, other_lanes = exchange(own, top, 0), exchange(lanes, top, 0)
     other, other_lanes, *weights = lax.optimization_barrier((other, other_lanes, *weights))
     (pair,) = call(first_kernel, [(2 * row_dev, dim + LANES)], own, other, lanes, other_lanes)
+    pairs = [pair]
     for step_no in range(passes_count):
-        rows_a = pair
-        for flips in middle:
-            rows_a = join(rows_a, exchange(rows_a, flips, 0))
-        mine = [rows_a] + [exchange(rows_a, flips, 0) for flips in SQUARE]
-        outs, tail = mlp(step_no, mine + [exchange(rows, CORE, 0) for rows in mine], tail, norm_gain, *weights)
-
-        kept, sent = outs[:4], [exchange(rows, CORE, 0) for rows in outs[4:]]
-        parts = [kept[0], sent[0]]
-        for place in (3, 2, 1):
-            parts.append(exchange(add(kept[place], sent[place]), SQUARE[place - 1], 0))
-        for flips in middle[::-1]:
-            low, high = split(*parts)
-            parts = [low, exchange(high, flips, 0)]
-        if step_no < passes_count - 1:
-            total = add(*parts)
-            rest = exchange(pair, STAY, 1)
-            pair, own = call(
-                meet_kernel, [(2 * row_dev, dim), (row_dev, dim)], rest, exchange(total, STAY, 1), exchange(total, top, 1)
-            )
+        last = step_no == passes_count - 1
+        cuts_out = 1 if last else HALVES
+        cuts = []
+        for rows in pairs:
+            for flips in middle:
+                rows = join(rows, exchange(rows, flips, 0))
+            mine = [rows] + [exchange(rows, flips, 0) for flips in SQUARE]
+            cuts.append(mine + [exchange(rows, CORE, 0) for rows in mine])
+        outs, tail = mlp(step_no, cuts, cuts_out, tail, norm_gain, *weights)
+
+        sums = []
+        for cut in outs:
+            kept, sent = cut[:4], [exchange(rows, CORE, 0) for rows in cut[4:]]
+            parts = [kept[0], sent[0]]
+            for place in (3, 2, 1):
+                parts.append(exchange(add(kept[place], sent[place]), SQUARE[place - 1], 0))
+            for flips in middle[::-1]:
+                low, high = split(*parts)
+                parts = [low, exchange(high, flips, 0)]
+            sums.append(parts)
+        if not last:
+            rests = [exchange(rows, STAY, 1) for rows in pairs]
+            pairs, owns = [], []
+            width = dim // cuts_out
+            for number, parts in enumerate(sums):
+                total = add(*parts)
+                rest, offset = (rests[0], number * width) if len(rests) == 1 else (rests[number], 0)
+                rows, own = call(
+                    functools.partial(meet_kernel, offset), [(2 * row_dev, width), (row_dev, width)],
+                    rest, exchange(total, STAY, 1), exchange(total, top, 1),
+                )
+                pairs.append(rows)
+                owns.append(own)
+            (own,) = call(widen_kernel, [(row_dev, dim)], *owns)
         else:
-            low, high = split(*parts)
+            low, high = split(*sums[0])
             rest = exchange(own, STAY, 1)
-            own = add(rest, exchange(low, STAY, 1), exchange(high, top, 1))
+            own = add(rest, exchange(high, top, 1), exchange(low, STAY, 1))
     return own[None]
 
 

time: 72.8 us -> 74.4 us (1.022)
  starting transfers between devices: 32.3 us -> 45.6 us
  waiting for transfers between devices: 29.3 us -> 17.6 us
    ppermute x36 -> x52, starting transfers between devices: 32.3 us -> 45.6 us  [exchange(): return lax.ppermute(value, ('segment', 'expert'), pairs)]
    ppermute x36 -> x52, waiting for transfers between devices: 29.3 us -> 17.6 us  [exchange(): return lax.ppermute(value, ('segment', 'expert'), pairs)]
    pallas_call x14 -> x20, Pallas kernels: 6.62 us -> 6.56 us  [call(): pl.pallas_call(kernel, out_shape=[jax.ShapeDtypeStruct(shape, jnp.bfloat1...]
  transfers between devices with their start and end apart: 36 -> 52, of which waited for: 19 -> 16; matrix products, arithmetic and copies ran while one was open for 0% -> 0% of each run, Pallas kernels for 7% -> 7%
where the time goes in v10:
time: 74.4 us; the launch traced here: 74.2 us
  starting transfers between devices  45.6 us (61%)
  waiting for transfers between devices  17.6 us (24%)
  Pallas kernels  10.8 us (15%)
    ppermute x52, starting transfers between devices, exchange(): return lax.ppermute(value, ('segment', 'expert'), pairs)  45.6 us
    ppermute x52, waiting for transfers between devices, exchange(): return lax.ppermute(value, ('segment', 'expert'), pairs)  17.6 us
    pallas_call x20, Pallas kernels, call(): pl.pallas_call(kernel, out_shape=[jax.ShapeDtypeStruct(shape, jnp.bfloat1...  6.56 us
    pallas_call x1, Pallas kernels, load(): pl.pallas_call(load_kernel, out_shape=[pltpu.VMEM(w.shape, w.dtype) for w...  4.23 us
  transfers between devices with their start and end apart: 52, of which 16 were waited for; matrix products, arithmetic and copies ran while one was open for 0% of the time, Pallas kernels for 7%

profile of v10, /device:TPU:0, one launch (start us, length us, event | category | flops | bytes accessed | tf_op | source)
XLA Modules:
  0.0 74.2 jit_solution(5726633985369664207)
XLA Ops:
  0.0 4.0 %collective-permute-start = (bf16[4,7168]{1,0:T(4,128)(2,1)}, bf16[4,7168]{1,0:T(4,128)(2,1)S(1)}, u32[]{:S(2)}, u32[]{:S(2)}) collective-permute-start(bf16[4,7168]{1,0:T(4,128)(2,1)} %bitcast.4), channel_id=1, source_target_pairs={{0,8},{1,9},{2,10},{3,11},{4,12},{5,13},{6,14},{7,15},{8,0},{9,1},... | collective-permute-start | bytes 172040 | tf_op jit(solution)/shard_map/ppermute | solution.py:27
  4.0 0.8 %shard_map.73.own_tail_ref = bf16[4,128]{1,0:T(4,128)(2,1)S(1)} custom-call(s32[1,2,2,4]{3,2,1,0:T(2,128)} %bitcast.6, bf16[1,2,2,4]{3,2,1,0:T(2,128)(2,1)} %bitcast.7), custom_call_target="tpu_custom_call" | custom-call | tf_op jit(solution)/shard_map/pallas_call | solution.py:44
  4.9 0.1 collective-permute-start.1
  4.9 4.2 %shard_map.74 = (bf16[1,7168,256]{2,1,0:T(8,128)(2,1)S(1)}, bf16[1,7168,256]{2,1,0:T(8,128)(2,1)S(1)}, bf16[1,256,7168]{2,1,0:T(8,128)(2,1)S(1)}) custom-call(bf16[1,7168,256]{2,1,0:T(8,128)(2,1)} %gate_ref.1, bf16[1,7168,256]{2,1,0:T(8,128)(2,1)} %up_ref.1, bf16[1,256,7168]{2,1,0:T(8,128)(2,1)} %down_ref.1), custom_call_target="tpu_custom_call" | custom-call | bytes 11010048 | tf_op jit(solution)/shard_map/pallas_call | solution.py:66
  9.2 0.2 collective-permute-done.1.far_tail_ref
  9.4 2.7 %collective-permute-start.5 = (bf16[8,7296]{1,0:T(8,128)(2,1)S(1)}, bf16[8,7296]{1,0:T(8,128)(2,1)S(1)}, u32[]{:S(2)}, u32[]{:S(2)}) collective-permute-start(bf16[8,7296]{1,0:T(8,128)(2,1)S(1)} %shard_map.75.refs_0_), channel_id=1, source_target_pairs={{0,6},{1,7},{2,4},{3,5},{4,2},{5,3},{6,0},{7,1},{8,14},{9,15},{10,... | collective-permute-start | bytes 350216 | tf_op jit(solution)/shard_map/ppermute | solution.py:27
  12.2 0.5 collective-permute-start.4
  12.7 0.3 collective-permute-start.3
  13.0 3.3 %collective-permute-done.5.refs_3_ = bf16[8,7296]{1,0:T(8,128)(2,1)S(1)} collective-permute-done((bf16[8,7296]{1,0:T(8,128)(2,1)S(1)}, bf16[8,7296]{1,0:T(8,128)(2,1)S(1)}, u32[]{:S(2)}, u32[]{:S(2)}) %collective-permute-start.5) | collective-permute-done | bytes 116768 | tf_op jit(solution)/shard_map/ppermute | solution.py:27
  16.3 1.4 %collective-permute-done.4.refs_2_ = bf16[8,7296]{1,0:T(8,128)(2,1)S(1)} collective-permute-done((bf16[8,7296]{1,0:T(8,128)(2,1)S(1)}, bf16[8,7296]{1,0:T(8,128)(2,1)S(1)}, u32[]{:S(2)}, u32[]{:S(2)}) %collective-permute-start.4) | collective-permute-done | bytes 116768 | tf_op jit(solution)/shard_map/ppermute | solution.py:27
  17.7 0.5 collective-permute-start.7
  18.2 0.8 %collective-permute-done.8.refs_6_ = bf16[8,7296]{1,0:T(8,128)(2,1)S(1)} collective-permute-done((bf16[8,7296]{1,0:T(8,128)(2,1)S(1)}, bf16[8,7296]{1,0:T(8,128)(2,1)S(1)}, u32[]{:S(2)}, u32[]{:S(2)}) %collective-permute-start.8) | collective-permute-done | bytes 116768 | tf_op jit(solution)/shard_map/ppermute | solution.py:27
  19.0 0.2 collective-permute-done.7.refs_5_
  19.2 2.3 %shard_map.76 = (bf16[8,3584]{1,0:T(8,128)(2,1)S(1)}, bf16[8,3584]{1,0:T(8,128)(2,1)S(1)}, bf16[8,3584]{1,0:T(8,128)(2,1)S(1)}, bf16[8,3584]{1,0:T(8,128)(2,1)S(...) custom-call(bf16[8,7296]{1,0:T(8,128)(2,1)S(1)} %shard_map.75.refs_0, ...), custom_call_target="tpu_custom_call" | custom-call | flops 704643072 | bytes 11010048 | tf_op jit(solution)/shard_map/pallas_call | solution.py:44
  21.5 0.4 collective-permute-start.20
  21.9 0.2 collective-permute-start.22
  22.1 0.3 collective-permute-start.24
  22.4 0.2 collective-permute-start.11
  22.6 0.3 collective-permute-start.13
  22.9 0.2 collective-permute-start.15
  23.2 0.4 collective-permute-start.19
  23.6 2.3 %collective-permute-start.21 = (bf16[8,3584]{1,0:T(8,128)(2,1)S(1)}, bf16[8,3584]{1,0:T(8,128)(2,1)S(1)}, u32[]{:S(2)}, u32[]{:S(2)}) collective-permute-start(bf16[8,3584]{1,0:T(8,128)(2,1)S(1)} %shard_map.82), channel_id=1, source_target_pairs={{0,6},{1,7},{2,4},{3,5},{4,2},{5,3},{6,0},{7,1},{8,14},{9,15},{10,... | collective-permute-start | bytes 172040 | tf_op jit(solution)/shard_map/ppermute | solution.py:27
  25.9 0.8 %collective-permute-start.23 = (bf16[8,3584]{1,0:T(8,128)(2,1)S(1)}, bf16[8,3584]{1,0:T(8,128)(2,1)S(1)}, u32[]{:S(2)}, u32[]{:S(2)}) collective-permute-start(bf16[8,3584]{1,0:T(8,128)(2,1)S(1)} %shard_map.83), channel_id=1, source_target_pairs={{0,2},{1,5},{2,0},{3,7},{4,6},{5,1},{6,4},{7,3},{8,10},{9,13},{10,... | collective-permute-start | bytes 172040 | tf_op jit(solution)/shard_map/ppermute | solution.py:27
  26.8 0.4 collective-permute-start.25
  27.2 1.5 %collective-permute-start.2 = (bf16[8,7296]{1,0:T(8,128)(2,1)S(1)}, bf16[8,7296]{1,0:T(8,128)(2,1)S(1)}, u32[]{:S(2)}, u32[]{:S(2)}) collective-permute-start(bf16[8,7296]{1,0:T(8,128)(2,1)S(1)} %shard_map.75.refs_0_), channel_id=1, source_target_pairs={{0,16},{1,17},{2,18},{3,19},{4,20},{5,21},{6,22},{7,23},{8,24},{9,... | collective-permute-start | bytes 350216 | tf_op jit(solution)/shard_map/ppermute | solution.py:27
  28.9 2.6 %collective-permute-start.12 = (bf16[8,3584]{1,0:T(8,128)(2,1)S(1)}, bf16[8,3584]{1,0:T(8,128)(2,1)S(1)}, u32[]{:S(2)}, u32[]{:S(2)}) collective-permute-start(bf16[8,3584]{1,0:T(8,128)(2,1)S(1)} %shard_map.77), channel_id=1, source_target_pairs={{0,6},{1,7},{2,4},{3,5},{4,2},{5,3},{6,0},{7,1},{8,14},{9,15},{10,... | collective-permute-start | bytes 172040 | tf_op jit(solution)/shard_map/ppermute | solution.py:27
  31.5 0.9 %collective-permute-start.14 = (bf16[8,3584]{1,0:T(8,128)(2,1)S(1)}, bf16[8,3584]{1,0:T(8,128)(2,1)S(1)}, u32[]{:S(2)}, u32[]{:S(2)}) collective-permute-start(bf16[8,3584]{1,0:T(8,128)(2,1)S(1)} %shard_map.78), channel_id=1, source_target_pairs={{0,2},{1,5},{2,0},{3,7},{4,6},{5,1},{6,4},{7,3},{8,10},{9,13},{10,... | collective-permute-start | bytes 172040 | tf_op jit(solution)/shard_map/ppermute | solution.py:27
  32.4 0.1 collective-permute-start.16
  32.6 3.5 %collective-permute-start.27 = (bf16[8,3584]{1,0:T(8,128)(2,1)S(1)}, bf16[8,3584]{1,0:T(8,128)(2,1)S(1)}, u32[]{:S(2)}, u32[]{:S(2)}) collective-permute-start(bf16[8,3584]{1,0:T(8,128)(2,1)S(1)} %shard_map.85), channel_id=1, source_target_pairs={{0,24},{1,25},{2,26},{3,27},{4,28},{5,29},{6,30},{7,31},{8,16},{9,... | collective-permute-start | bytes 172040 | tf_op jit(solution)/shard_map/ppermute | solution.py:27
  36.1 0.6 collective-permute-start.26
  36.7 0.2 collective-permute-done.16.refs_4_
  37.0 3.3 %collective-permute-start.18 = (bf16[8,3584]{1,0:T(8,128)(2,1)S(1)}, bf16[8,3584]{1,0:T(8,128)(2,1)S(1)}, u32[]{:S(2)}, u32[]{:S(2)}) collective-permute-start(bf16[8,3584]{1,0:T(8,128)(2,1)S(1)} %shard_map.80), channel_id=1, source_target_pairs={{0,24},{1,25},{2,26},{3,27},{4,28},{5,29},{6,30},{7,31},{8,16},{9,... | collective-permute-start | bytes 172040 | tf_op jit(solution)/shard_map/ppermute | solution.py:27
  40.2 0.5 collective-permute-start.17
  40.8 0.1 collective-permute-start.39
  40.9 3.4 %collective-permute-start.38 = (bf16[8,3584]{1,0:T(8,128)(2,1)S(1)}, bf16[8,3584]{1,0:T(8,128)(2,1)S(1)}, u32[]{:S(2)}, u32[]{:S(2)}) collective-permute-start(bf16[8,3584]{1,0:T(8,128)(2,1)S(1)} %get-tuple-element.71.refs_8_), channel_id=1, source_target_pairs={{0,6},{1,7},{2,4},{3,5},{4,2},{5,3},{6,0},{7,1},{8,14},{9,15},{10,... | collective-permute-start | bytes 172040 | tf_op jit(solution)/shard_map/ppermute | solution.py:27
  44.3 0.6 collective-permute-start.37
  45.1 2.9 %collective-permute-start.31 = (bf16[8,3584]{1,0:T(8,128)(2,1)S(1)}, bf16[8,3584]{1,0:T(8,128)(2,1)S(1)}, u32[]{:S(2)}, u32[]{:S(2)}) collective-permute-start(bf16[8,3584]{1,0:T(8,128)(2,1)S(1)} %get-tuple-element.70.refs_0_), channel_id=1, source_target_pairs={{0,6},{1,7},{2,4},{3,5},{4,2},{5,3},{6,0},{7,1},{8,14},{9,15},{10,... | collective-permute-start | bytes 172040 | tf_op jit(solution)/shard_map/ppermute | solution.py:27
  48.0 0.6 collective-permute-start.30
  48.6 1.8 %collective-permute-start.29 = (bf16[8,3584]{1,0:T(8,128)(2,1)S(1)}, bf16[8,3584]{1,0:T(8,128)(2,1)S(1)}, u32[]{:S(2)}, u32[]{:S(2)}) collective-permute-start(bf16[8,3584]{1,0:T(8,128)(2,1)S(1)} %get-tuple-element.70.refs_0_), channel_id=1, source_target_pairs={{0,4},{1,3},{2,6},{3,1},{4,0},{5,7},{6,2},{7,5},{8,12},{9,11},{10,... | collective-permute-start | bytes 172040 | tf_op jit(solution)/shard_map/ppermute | solution.py:27
  50.5 0.5 collective-permute-start.41
  51.0 0.3 collective-permute-done.31.refs_3_
  51.3 1.0 %collective-permute-done.30.refs_2_ = bf16[8,3584]{1,0:T(8,128)(2,1)S(1)} collective-permute-done((bf16[8,3584]{1,0:T(8,128)(2,1)S(1)}, bf16[8,3584]{1,0:T(8,128)(2,1)S(1)}, u32[]{:S(2)}, u32[]{:S(2)}) %collective-permute-start.30) | collective-permute-done | bytes 57376 | tf_op jit(solution)/shard_map/ppermute | solution.py:27
  52.3 0.5 collective-permute-done.29.refs_1_
  52.8 0.5 collective-permute-start.33
  53.3 0.2 collective-permute-done.35.refs_7_
  53.5 0.5 collective-permute-done.34.refs_6_
  54.0 0.2 collective-permute-done.33.refs_5_
  54.2 2.3 %shard_map.88 = (bf16[8,7168]{1,0:T(8,128)(2,1)S(1)}, bf16[8,7168]{1,0:T(8,128)(2,1)S(1)}, bf16[8,7168]{1,0:T(8,128)(2,1)S(1)}, bf16[8,7168]{1,0:T(8,128)(2,1)S(...) custom-call(bf16[8,3584]{1,0:T(8,128)(2,1)S(1)} %get-tuple-element.7, ...), custom_call_target="tpu_custom_call" | custom-call | flops 704643072 | bytes 11010048 | tf_op jit(solution)/shard_map/pallas_call | solution.py:44
  56.5 0.4 collective-permute-start.44
  56.9 0.2 collective-permute-start.46
  57.1 0.4 collective-permute-start.48
  57.4 0.2 collective-permute-start.43
  57.6 0.3 collective-permute-done.44.refs_1_
  57.9 2.0 %collective-permute-start.45 = (bf16[8,7168]{1,0:T(8,128)(2,1)S(1)}, bf16[8,7168]{1,0:T(8,128)(2,1)S(1)}, u32[]{:S(2)}, u32[]{:S(2)}) collective-permute-start(bf16[8,7168]{1,0:T(8,128)(2,1)S(1)} %shard_map.89), channel_id=1, source_target_pairs={{0,6},{1,7},{2,4},{3,5},{4,2},{5,3},{6,0},{7,1},{8,14},{9,15},{10,... | collective-permute-start | bytes 344072 | tf_op jit(solution)/shard_map/ppermute | solution.py:27
  60.0 1.4 %collective-permute-start.47 = (bf16[8,7168]{1,0:T(8,128)(2,1)S(1)}, bf16[8,7168]{1,0:T(8,128)(2,1)S(1)}, u32[]{:S(2)}, u32[]{:S(2)}) collective-permute-start(bf16[8,7168]{1,0:T(8,128)(2,1)S(1)} %shard_map.90), channel_id=1, source_target_pairs={{0,2},{1,5},{2,0},{3,7},{4,6},{5,1},{6,4},{7,3},{8,10},{9,13},{10,... | collective-permute-start | bytes 344072 | tf_op jit(solution)/shard_map/ppermute | solution.py:27
  61.4 0.2 collective-permute-start.49
  61.7 0.6 collective-permute-start.28
  62.3 2.5 %collective-permute-done.45.refs_2_ = bf16[8,7168]{1,0:T(8,128)(2,1)S(1)} collective-permute-done((bf16[8,7168]{1,0:T(8,128)(2,1)S(1)}, bf16[8,7168]{1,0:T(8,128)(2,1)S(1)}, u32[]{:S(2)}, u32[]{:S(2)}) %collective-permute-start.45) | collective-permute-done | bytes 114720 | tf_op jit(solution)/shard_map/ppermute | solution.py:27
  64.9 1.9 %collective-permute-done.47.refs_3_ = bf16[8,7168]{1,0:T(8,128)(2,1)S(1)} collective-permute-done((bf16[8,7168]{1,0:T(8,128)(2,1)S(1)}, bf16[8,7168]{1,0:T(8,128)(2,1)S(1)}, u32[]{:S(2)}, u32[]{:S(2)}) %collective-permute-start.47) | collective-permute-done | bytes 114720 | tf_op jit(solution)/shard_map/ppermute | solution.py:27
  66.8 0.1 shard_map.92
  66.8 1.9 %collective-permute-start.50 = (bf16[4,7168]{1,0:T(4,128)(2,1)S(1)}, bf16[4,7168]{1,0:T(4,128)(2,1)S(1)}, u32[]{:S(2)}, u32[]{:S(2)}) collective-permute-start(bf16[4,7168]{1,0:T(4,128)(2,1)S(1)} %get-tuple-element.81), channel_id=1, source_target_pairs={{0,24},{1,25},{2,26},{3,27},{4,28},{5,29},{6,30},{7,31},{8,16},{9,... | collective-permute-start | bytes 172040 | tf_op jit(solution)/shard_map/ppermute | solution.py:27
  68.7 0.9 %collective-permute-start.51 = (bf16[4,7168]{1,0:T(4,128)(2,1)S(1)}, bf16[4,7168]{1,0:T(4,128)(2,1)S(1)}, u32[]{:S(2)}, u32[]{:S(2)}) collective-permute-start(bf16[4,7168]{1,0:T(4,128)(2,1)S(1)} %get-tuple-element.82), channel_id=1, source_target_pairs={{0,16},{1,17},{2,18},{3,19},{4,20},{5,21},{6,22},{7,23},{8,24},{9,... | collective-permute-start | bytes 172040 | tf_op jit(solution)/shard_map/ppermute | solution.py:27
  69.6 3.9 %collective-permute-done.50.refs_1_ = bf16[4,7168]{1,0:T(4,128)(2,1)S(1)} collective-permute-done((bf16[4,7168]{1,0:T(4,128)(2,1)S(1)}, bf16[4,7168]{1,0:T(4,128)(2,1)S(1)}, u32[]{:S(2)}, u32[]{:S(2)}) %collective-permute-start.50) | collective-permute-done | bytes 57376 | tf_op jit(solution)/shard_map/ppermute | solution.py:27
  73.6 0.7 shard_map.93
  (65 shorter events, 0.7 us)
Async XLA Ops:
  0.0 9.4 %collective-permute-start = (bf16[4,7168]{1,0:T(4,128)(2,1)}, bf16[4,7168]{1,0:T(4,128)(2,1)S(1)}, u32[]{:S(2)}, u32[]{:S(2)}) collective-permute-start(bf16[4,7168]{1,0:T(4,128)(2,1)} %bitcast.4), channel_id=1, source_target_pairs={{0,8},{1,9},{2,10},{3,11},{4,12},{5,13},{6,14},{7,15},{8,0},{9,1},... | collective-permute-start | bytes 172040 | tf_op jit(solution)/shard_map/ppermute | solution.py:27
  4.8 4.6 %copy-start.1 = (bf16[1,4,7168]{2,1,0:T(4,128)(2,1)S(1)}, bf16[1,4,7168]{2,1,0:T(4,128)(2,1)}, u32[]{:S(2)}) copy-start(bf16[1,4,7168]{2,1,0:T(4,128)(2,1)} %param.7) | copy-start | bytes 172036
  4.9 14.3 %copy-start = (f32[1,7168]{1,0:T(1,128)S(1)}, f32[1,7168]{1,0:T(1,128)}, u32[]{:S(2)}) copy-start(f32[1,7168]{1,0:T(1,128)} %refs_17_.1) | copy-start | bytes 86020
  4.9 4.5 %collective-permute-start.1 = (bf16[4,128]{1,0:T(4,128)(2,1)S(1)}, bf16[4,128]{1,0:T(4,128)(2,1)S(1)}, u32[]{:S(2)}, u32[]{:S(2)}) collective-permute-start(bf16[4,128]{1,0:T(4,128)(2,1)S(1)} %shard_map.73.own_tail_ref), channel_id=1, source_target_pairs={{0,8},{1,9},{2,10},{3,11},{4,12},{5,13},{6,14},{7,15},{8,0},{9,1},... | collective-permute-start | bytes 3080 | tf_op jit(solution)/shard_map/ppermute | solution.py:27
  9.4 6.9 %collective-permute-start.5 = (bf16[8,7296]{1,0:T(8,128)(2,1)S(1)}, bf16[8,7296]{1,0:T(8,128)(2,1)S(1)}, u32[]{:S(2)}, u32[]{:S(2)}) collective-permute-start(bf16[8,7296]{1,0:T(8,128)(2,1)S(1)} %shard_map.75.refs_0_), channel_id=1, source_target_pairs={{0,6},{1,7},{2,4},{3,5},{4,2},{5,3},{6,0},{7,1},{8,14},{9,15},{10,... | collective-permute-start | bytes 350216 | tf_op jit(solution)/shard_map/ppermute | solution.py:27
  12.2 5.5 %collective-permute-start.4 = (bf16[8,7296]{1,0:T(8,128)(2,1)S(1)}, bf16[8,7296]{1,0:T(8,128)(2,1)S(1)}, u32[]{:S(2)}, u32[]{:S(2)}) collective-permute-start(bf16[8,7296]{1,0:T(8,128)(2,1)S(1)} %shard_map.75.refs_0_), channel_id=1, source_target_pairs={{0,2},{1,5},{2,0},{3,7},{4,6},{5,1},{6,4},{7,3},{8,10},{9,13},{10,... | collective-permute-start | bytes 350216 | tf_op jit(solution)/shard_map/ppermute | solution.py:27
  12.7 5.0 %collective-permute-start.3 = (bf16[8,7296]{1,0:T(8,128)(2,1)S(1)}, bf16[8,7296]{1,0:T(8,128)(2,1)S(1)}, u32[]{:S(2)}, u32[]{:S(2)}) collective-permute-start(bf16[8,7296]{1,0:T(8,128)(2,1)S(1)} %shard_map.75.refs_0_), channel_id=1, source_target_pairs={{0,4},{1,3},{2,6},{3,1},{4,0},{5,7},{6,2},{7,5},{8,12},{9,11},{10,... | collective-permute-start | bytes 350216 | tf_op jit(solution)/shard_map/ppermute | solution.py:27
  13.0 5.2 %collective-permute-start.6 = (bf16[8,7296]{1,0:T(8,128)(2,1)S(1)}, bf16[8,7296]{1,0:T(8,128)(2,1)S(1)}, u32[]{:S(2)}, u32[]{:S(2)}) collective-permute-start(bf16[8,7296]{1,0:T(8,128)(2,1)S(1)} %shard_map.75.refs_0_), channel_id=1, source_target_pairs={{0,1},{1,0},{2,3},{3,2},{4,5},{5,4},{6,7},{7,6},{8,9},{9,8},{10,11... | collective-permute-start | bytes 350216 | tf_op jit(solution)/shard_map/ppermute | solution.py:27
  16.3 1.9 %collective-permute-start.9 = (bf16[8,7296]{1,0:T(8,128)(2,1)S(1)}, bf16[8,7296]{1,0:T(8,128)(2,1)S(1)}, u32[]{:S(2)}, u32[]{:S(2)}) collective-permute-start(bf16[8,7296]{1,0:T(8,128)(2,1)S(1)} %collective-permute-done.5.refs_3_), channel_id=1, source_target_pairs={{0,1},{1,0},{2,3},{3,2},{4,5},{5,4},{6,7},{7,6},{8,9},{9,8},{10,11... | collective-permute-start | bytes 350216 | tf_op jit(solution)/shard_map/ppermute | solution.py:27
  17.7 1.3 %collective-permute-start.8 = (bf16[8,7296]{1,0:T(8,128)(2,1)S(1)}, bf16[8,7296]{1,0:T(8,128)(2,1)S(1)}, u32[]{:S(2)}, u32[]{:S(2)}) collective-permute-start(bf16[8,7296]{1,0:T(8,128)(2,1)S(1)} %collective-permute-done.4.refs_2_), channel_id=1, source_target_pairs={{0,1},{1,0},{2,3},{3,2},{4,5},{5,4},{6,7},{7,6},{8,9},{9,8},{10,11... | collective-permute-start | bytes 350216 | tf_op jit(solution)/shard_map/ppermute | solution.py:27
  17.7 1.5 %collective-permute-start.7 = (bf16[8,7296]{1,0:T(8,128)(2,1)S(1)}, bf16[8,7296]{1,0:T(8,128)(2,1)S(1)}, u32[]{:S(2)}, u32[]{:S(2)}) collective-permute-start(bf16[8,7296]{1,0:T(8,128)(2,1)S(1)} %collective-permute-done.3.refs_1_), channel_id=1, source_target_pairs={{0,1},{1,0},{2,3},{3,2},{4,5},{5,4},{6,7},{7,6},{8,9},{9,8},{10,11... | collective-permute-start | bytes 350216 | tf_op jit(solution)/shard_map/ppermute | solution.py:27
  21.5 1.4 %collective-permute-start.20 = (bf16[8,3584]{1,0:T(8,128)(2,1)S(1)}, bf16[8,3584]{1,0:T(8,128)(2,1)S(1)}, u32[]{:S(2)}, u32[]{:S(2)}) collective-permute-start(bf16[8,3584]{1,0:T(8,128)(2,1)S(1)} %get-tuple-element.64), channel_id=1, source_target_pairs={{0,1},{1,0},{2,3},{3,2},{4,5},{5,4},{6,7},{7,6},{8,9},{9,8},{10,11... | collective-permute-start | bytes 172040 | tf_op jit(solution)/shard_map/ppermute | solution.py:27
  21.9 1.3 %collective-permute-start.22 = (bf16[8,3584]{1,0:T(8,128)(2,1)S(1)}, bf16[8,3584]{1,0:T(8,128)(2,1)S(1)}, u32[]{:S(2)}, u32[]{:S(2)}) collective-permute-start(bf16[8,3584]{1,0:T(8,128)(2,1)S(1)} %get-tuple-element.66), channel_id=1, source_target_pairs={{0,1},{1,0},{2,3},{3,2},{4,5},{5,4},{6,7},{7,6},{8,9},{9,8},{10,11... | collective-permute-start | bytes 172040 | tf_op jit(solution)/shard_map/ppermute | solution.py:27
  22.1 1.5 %collective-permute-start.24 = (bf16[8,3584]{1,0:T(8,128)(2,1)S(1)}, bf16[8,3584]{1,0:T(8,128)(2,1)S(1)}, u32[]{:S(2)}, u32[]{:S(2)}) collective-permute-start(bf16[8,3584]{1,0:T(8,128)(2,1)S(1)} %get-tuple-element.68), channel_id=1, source_target_pairs={{0,1},{1,0},{2,3},{3,2},{4,5},{5,4},{6,7},{7,6},{8,9},{9,8},{10,11... | collective-permute-start | bytes 172040 | tf_op jit(solution)/shard_map/ppermute | solution.py:27
  22.4 3.5 %collective-permute-start.11 = (bf16[8,3584]{1,0:T(8,128)(2,1)S(1)}, bf16[8,3584]{1,0:T(8,128)(2,1)S(1)}, u32[]{:S(2)}, u32[]{:S(2)}) collective-permute-start(bf16[8,3584]{1,0:T(8,128)(2,1)S(1)} %get-tuple-element.55), channel_id=1, source_target_pairs={{0,1},{1,0},{2,3},{3,2},{4,5},{5,4},{6,7},{7,6},{8,9},{9,8},{10,11... | collective-permute-start | bytes 172040 | tf_op jit(solution)/shard_map/ppermute | solution.py:27
  22.6 4.2 %collective-permute-start.13 = (bf16[8,3584]{1,0:T(8,128)(2,1)S(1)}, bf16[8,3584]{1,0:T(8,128)(2,1)S(1)}, u32[]{:S(2)}, u32[]{:S(2)}) collective-permute-start(bf16[8,3584]{1,0:T(8,128)(2,1)S(1)} %get-tuple-element.57), channel_id=1, source_target_pairs={{0,1},{1,0},{2,3},{3,2},{4,5},{5,4},{6,7},{7,6},{8,9},{9,8},{10,11... | collective-permute-start | bytes 172040 | tf_op jit(solution)/shard_map/ppermute | solution.py:27
  22.9 4.3 %collective-permute-start.15 = (bf16[8,3584]{1,0:T(8,128)(2,1)S(1)}, bf16[8,3584]{1,0:T(8,128)(2,1)S(1)}, u32[]{:S(2)}, u32[]{:S(2)}) collective-permute-start(bf16[8,3584]{1,0:T(8,128)(2,1)S(1)} %get-tuple-element.59), channel_id=1, source_target_pairs={{0,1},{1,0},{2,3},{3,2},{4,5},{5,4},{6,7},{7,6},{8,9},{9,8},{10,11... | collective-permute-start | bytes 172040 | tf_op jit(solution)/shard_map/ppermute | solution.py:27
  23.2 5.6 %collective-permute-start.19 = (bf16[8,3584]{1,0:T(8,128)(2,1)S(1)}, bf16[8,3584]{1,0:T(8,128)(2,1)S(1)}, u32[]{:S(2)}, u32[]{:S(2)}) collective-permute-start(bf16[8,3584]{1,0:T(8,128)(2,1)S(1)} %get-tuple-element.62), channel_id=1, source_target_pairs={{0,1},{1,0},{2,3},{3,2},{4,5},{5,4},{6,7},{7,6},{8,9},{9,8},{10,11... | collective-permute-start | bytes 172040 | tf_op jit(solution)/shard_map/ppermute | solution.py:27
  23.6 5.3 %collective-permute-start.21 = (bf16[8,3584]{1,0:T(8,128)(2,1)S(1)}, bf16[8,3584]{1,0:T(8,128)(2,1)S(1)}, u32[]{:S(2)}, u32[]{:S(2)}) collective-permute-start(bf16[8,3584]{1,0:T(8,128)(2,1)S(1)} %shard_map.82), channel_id=1, source_target_pairs={{0,6},{1,7},{2,4},{3,5},{4,2},{5,3},{6,0},{7,1},{8,14},{9,15},{10,... | collective-permute-start | bytes 172040 | tf_op jit(solution)/shard_map/ppermute | solution.py:27
  25.9 5.6 %collective-permute-start.23 = (bf16[8,3584]{1,0:T(8,128)(2,1)S(1)}, bf16[8,3584]{1,0:T(8,128)(2,1)S(1)}, u32[]{:S(2)}, u32[]{:S(2)}) collective-permute-start(bf16[8,3584]{1,0:T(8,128)(2,1)S(1)} %shard_map.83), channel_id=1, source_target_pairs={{0,2},{1,5},{2,0},{3,7},{4,6},{5,1},{6,4},{7,3},{8,10},{9,13},{10,... | collective-permute-start | bytes 172040 | tf_op jit(solution)/shard_map/ppermute | solution.py:27
  26.8 5.7 %collective-permute-start.25 = (bf16[8,3584]{1,0:T(8,128)(2,1)S(1)}, bf16[8,3584]{1,0:T(8,128)(2,1)S(1)}, u32[]{:S(2)}, u32[]{:S(2)}) collective-permute-start(bf16[8,3584]{1,0:T(8,128)(2,1)S(1)} %shard_map.84), channel_id=1, source_target_pairs={{0,4},{1,3},{2,6},{3,1},{4,0},{5,7},{6,2},{7,5},{8,12},{9,11},{10,... | collective-permute-start | bytes 172040 | tf_op jit(solution)/shard_map/ppermute | solution.py:27
  27.2 13.5 %collective-permute-start.2 = (bf16[8,7296]{1,0:T(8,128)(2,1)S(1)}, bf16[8,7296]{1,0:T(8,128)(2,1)S(1)}, u32[]{:S(2)}, u32[]{:S(2)}) collective-permute-start(bf16[8,7296]{1,0:T(8,128)(2,1)S(1)} %shard_map.75.refs_0_), channel_id=1, source_target_pairs={{0,16},{1,17},{2,18},{3,19},{4,20},{5,21},{6,22},{7,23},{8,24},{9,... | collective-permute-start | bytes 350216 | tf_op jit(solution)/shard_map/ppermute | solution.py:27
  28.8 3.8 %collective-permute-start.10 = (bf16[8,3584]{1,0:T(8,128)(2,1)S(1)}, bf16[8,3584]{1,0:T(8,128)(2,1)S(1)}, u32[]{:S(2)}, u32[]{:S(2)}) collective-permute-start(bf16[8,3584]{1,0:T(8,128)(2,1)S(1)} %get-tuple-element.53), channel_id=1, source_target_pairs={{0,1},{1,0},{2,3},{3,2},{4,5},{5,4},{6,7},{7,6},{8,9},{9,8},{10,11... | collective-permute-start | bytes 172040 | tf_op jit(solution)/shard_map/ppermute | solution.py:27
  28.9 7.2 %collective-permute-start.12 = (bf16[8,3584]{1,0:T(8,128)(2,1)S(1)}, bf16[8,3584]{1,0:T(8,128)(2,1)S(1)}, u32[]{:S(2)}, u32[]{:S(2)}) collective-permute-start(bf16[8,3584]{1,0:T(8,128)(2,1)S(1)} %shard_map.77), channel_id=1, source_target_pairs={{0,6},{1,7},{2,4},{3,5},{4,2},{5,3},{6,0},{7,1},{8,14},{9,15},{10,... | collective-permute-start | bytes 172040 | tf_op jit(solution)/shard_map/ppermute | solution.py:27
  31.5 5.2 %collective-permute-start.14 = (bf16[8,3584]{1,0:T(8,128)(2,1)S(1)}, bf16[8,3584]{1,0:T(8,128)(2,1)S(1)}, u32[]{:S(2)}, u32[]{:S(2)}) collective-permute-start(bf16[8,3584]{1,0:T(8,128)(2,1)S(1)} %shard_map.78), channel_id=1, source_target_pairs={{0,2},{1,5},{2,0},{3,7},{4,6},{5,1},{6,4},{7,3},{8,10},{9,13},{10,... | collective-permute-start | bytes 172040 | tf_op jit(solution)/shard_map/ppermute | solution.py:27
  32.4 4.5 %collective-permute-start.16 = (bf16[8,3584]{1,0:T(8,128)(2,1)S(1)}, bf16[8,3584]{1,0:T(8,128)(2,1)S(1)}, u32[]{:S(2)}, u32[]{:S(2)}) collective-permute-start(bf16[8,3584]{1,0:T(8,128)(2,1)S(1)} %shard_map.79), channel_id=1, source_target_pairs={{0,4},{1,3},{2,6},{3,1},{4,0},{5,7},{6,2},{7,5},{8,12},{9,11},{10,... | collective-permute-start | bytes 172040 | tf_op jit(solution)/shard_map/ppermute | solution.py:27
  32.6 8.2 %collective-permute-start.27 = (bf16[8,3584]{1,0:T(8,128)(2,1)S(1)}, bf16[8,3584]{1,0:T(8,128)(2,1)S(1)}, u32[]{:S(2)}, u32[]{:S(2)}) collective-permute-start(bf16[8,3584]{1,0:T(8,128)(2,1)S(1)} %shard_map.85), channel_id=1, source_target_pairs={{0,24},{1,25},{2,26},{3,27},{4,28},{5,29},{6,30},{7,31},{8,16},{9,... | collective-permute-start | bytes 172040 | tf_op jit(solution)/shard_map/ppermute | solution.py:27
  36.1 4.7 %collective-permute-start.26 = (bf16[8,3584]{1,0:T(8,128)(2,1)S(1)}, bf16[8,3584]{1,0:T(8,128)(2,1)S(1)}, u32[]{:S(2)}, u32[]{:S(2)}) collective-permute-start(bf16[8,3584]{1,0:T(8,128)(2,1)S(1)} %shard_map.85), channel_id=1, source_target_pairs={{0,16},{1,17},{2,18},{3,19},{4,20},{5,21},{6,22},{7,23},{8,24},{9,... | collective-permute-start | bytes 172040 | tf_op jit(solution)/shard_map/ppermute | solution.py:27
  37.0 7.9 %collective-permute-start.18 = (bf16[8,3584]{1,0:T(8,128)(2,1)S(1)}, bf16[8,3584]{1,0:T(8,128)(2,1)S(1)}, u32[]{:S(2)}, u32[]{:S(2)}) collective-permute-start(bf16[8,3584]{1,0:T(8,128)(2,1)S(1)} %shard_map.80), channel_id=1, source_target_pairs={{0,24},{1,25},{2,26},{3,27},{4,28},{5,29},{6,30},{7,31},{8,16},{9,... | collective-permute-start | bytes 172040 | tf_op jit(solution)/shard_map/ppermute | solution.py:27
  40.2 4.7 %collective-permute-start.17 = (bf16[8,3584]{1,0:T(8,128)(2,1)S(1)}, bf16[8,3584]{1,0:T(8,128)(2,1)S(1)}, u32[]{:S(2)}, u32[]{:S(2)}) collective-permute-start(bf16[8,3584]{1,0:T(8,128)(2,1)S(1)} %shard_map.80), channel_id=1, source_target_pairs={{0,16},{1,17},{2,18},{3,19},{4,20},{5,21},{6,22},{7,23},{8,24},{9,... | collective-permute-start | bytes 172040 | tf_op jit(solution)/shard_map/ppermute | solution.py:27
  40.8 4.2 %collective-permute-start.39 = (bf16[8,3584]{1,0:T(8,128)(2,1)S(1)}, bf16[8,3584]{1,0:T(8,128)(2,1)S(1)}, u32[]{:S(2)}, u32[]{:S(2)}) collective-permute-start(bf16[8,3584]{1,0:T(8,128)(2,1)S(1)} %get-tuple-element.71.refs_8_), channel_id=1, source_target_pairs={{0,1},{1,0},{2,3},{3,2},{4,5},{5,4},{6,7},{7,6},{8,9},{9,8},{10,11... | collective-permute-start | bytes 172040 | tf_op jit(solution)/shard_map/ppermute | solution.py:27
  40.9 7.0 %collective-permute-start.38 = (bf16[8,3584]{1,0:T(8,128)(2,1)S(1)}, bf16[8,3584]{1,0:T(8,128)(2,1)S(1)}, u32[]{:S(2)}, u32[]{:S(2)}) collective-permute-start(bf16[8,3584]{1,0:T(8,128)(2,1)S(1)} %get-tuple-element.71.refs_8_), channel_id=1, source_target_pairs={{0,6},{1,7},{2,4},{3,5},{4,2},{5,3},{6,0},{7,1},{8,14},{9,15},{10,... | collective-permute-start | bytes 172040 | tf_op jit(solution)/shard_map/ppermute | solution.py:27
  44.3 4.3 %collective-permute-start.37 = (bf16[8,3584]{1,0:T(8,128)(2,1)S(1)}, bf16[8,3584]{1,0:T(8,128)(2,1)S(1)}, u32[]{:S(2)}, u32[]{:S(2)}) collective-permute-start(bf16[8,3584]{1,0:T(8,128)(2,1)S(1)} %get-tuple-element.71.refs_8_), channel_id=1, source_target_pairs={{0,2},{1,5},{2,0},{3,7},{4,6},{5,1},{6,4},{7,3},{8,10},{9,13},{10,... | collective-permute-start | bytes 172040 | tf_op jit(solution)/shard_map/ppermute | solution.py:27
  44.9 5.5 %collective-permute-start.36 = (bf16[8,3584]{1,0:T(8,128)(2,1)S(1)}, bf16[8,3584]{1,0:T(8,128)(2,1)S(1)}, u32[]{:S(2)}, u32[]{:S(2)}) collective-permute-start(bf16[8,3584]{1,0:T(8,128)(2,1)S(1)} %get-tuple-element.71.refs_8_), channel_id=1, source_target_pairs={{0,4},{1,3},{2,6},{3,1},{4,0},{5,7},{6,2},{7,5},{8,12},{9,11},{10,... | collective-permute-start | bytes 172040 | tf_op jit(solution)/shard_map/ppermute | solution.py:27
  45.0 5.5 %collective-permute-start.32 = (bf16[8,3584]{1,0:T(8,128)(2,1)S(1)}, bf16[8,3584]{1,0:T(8,128)(2,1)S(1)}, u32[]{:S(2)}, u32[]{:S(2)}) collective-permute-start(bf16[8,3584]{1,0:T(8,128)(2,1)S(1)} %get-tuple-element.70.refs_0_), channel_id=1, source_target_pairs={{0,1},{1,0},{2,3},{3,2},{4,5},{5,4},{6,7},{7,6},{8,9},{9,8},{10,11... | collective-permute-start | bytes 172040 | tf_op jit(solution)/shard_map/ppermute | solution.py:27
  45.1 6.2 %collective-permute-start.31 = (bf16[8,3584]{1,0:T(8,128)(2,1)S(1)}, bf16[8,3584]{1,0:T(8,128)(2,1)S(1)}, u32[]{:S(2)}, u32[]{:S(2)}) collective-permute-start(bf16[8,3584]{1,0:T(8,128)(2,1)S(1)} %get-tuple-element.70.refs_0_), channel_id=1, source_target_pairs={{0,6},{1,7},{2,4},{3,5},{4,2},{5,3},{6,0},{7,1},{8,14},{9,15},{10,... | collective-permute-start | bytes 172040 | tf_op jit(solution)/shard_map/ppermute | solution.py:27
  48.0 4.3 %collective-permute-start.30 = (bf16[8,3584]{1,0:T(8,128)(2,1)S(1)}, bf16[8,3584]{1,0:T(8,128)(2,1)S(1)}, u32[]{:S(2)}, u32[]{:S(2)}) collective-permute-start(bf16[8,3584]{1,0:T(8,128)(2,1)S(1)} %get-tuple-element.70.refs_0_), channel_id=1, source_target_pairs={{0,2},{1,5},{2,0},{3,7},{4,6},{5,1},{6,4},{7,3},{8,10},{9,13},{10,... | collective-permute-start | bytes 172040 | tf_op jit(solution)/shard_map/ppermute | solution.py:27
  48.6 4.2 %collective-permute-start.29 = (bf16[8,3584]{1,0:T(8,128)(2,1)S(1)}, bf16[8,3584]{1,0:T(8,128)(2,1)S(1)}, u32[]{:S(2)}, u32[]{:S(2)}) collective-permute-start(bf16[8,3584]{1,0:T(8,128)(2,1)S(1)} %get-tuple-element.70.refs_0_), channel_id=1, source_target_pairs={{0,4},{1,3},{2,6},{3,1},{4,0},{5,7},{6,2},{7,5},{8,12},{9,11},{10,... | collective-permute-start | bytes 172040 | tf_op jit(solution)/shard_map/ppermute | solution.py:27
  50.5 2.4 %collective-permute-start.42 = (bf16[8,3584]{1,0:T(8,128)(2,1)S(1)}, bf16[8,3584]{1,0:T(8,128)(2,1)S(1)}, u32[]{:S(2)}, u32[]{:S(2)}) collective-permute-start(bf16[8,3584]{1,0:T(8,128)(2,1)S(1)} %collective-permute-done.38.refs_11_), channel_id=1, source_target_pairs={{0,1},{1,0},{2,3},{3,2},{4,5},{5,4},{6,7},{7,6},{8,9},{9,8},{10,11... | collective-permute-start | bytes 172040 | tf_op jit(solution)/shard_map/ppermute | solution.py:27
  50.5 2.8 %collective-permute-start.41 = (bf16[8,3584]{1,0:T(8,128)(2,1)S(1)}, bf16[8,3584]{1,0:T(8,128)(2,1)S(1)}, u32[]{:S(2)}, u32[]{:S(2)}) collective-permute-start(bf16[8,3584]{1,0:T(8,128)(2,1)S(1)} %collective-permute-done.37.refs_10_), channel_id=1, source_target_pairs={{0,1},{1,0},{2,3},{3,2},{4,5},{5,4},{6,7},{7,6},{8,9},{9,8},{10,11... | collective-permute-start | bytes 172040 | tf_op jit(solution)/shard_map/ppermute | solution.py:27
  51.3 2.0 %collective-permute-start.40 = (bf16[8,3584]{1,0:T(8,128)(2,1)S(1)}, bf16[8,3584]{1,0:T(8,128)(2,1)S(1)}, u32[]{:S(2)}, u32[]{:S(2)}) collective-permute-start(bf16[8,3584]{1,0:T(8,128)(2,1)S(1)} %collective-permute-done.36.refs_9_), channel_id=1, source_target_pairs={{0,1},{1,0},{2,3},{3,2},{4,5},{5,4},{6,7},{7,6},{8,9},{9,8},{10,11... | collective-permute-start | bytes 172040 | tf_op jit(solution)/shard_map/ppermute | solution.py:27
  52.3 1.2 %collective-permute-start.35 = (bf16[8,3584]{1,0:T(8,128)(2,1)S(1)}, bf16[8,3584]{1,0:T(8,128)(2,1)S(1)}, u32[]{:S(2)}, u32[]{:S(2)}) collective-permute-start(bf16[8,3584]{1,0:T(8,128)(2,1)S(1)} %collective-permute-done.31.refs_3_), channel_id=1, source_target_pairs={{0,1},{1,0},{2,3},{3,2},{4,5},{5,4},{6,7},{7,6},{8,9},{9,8},{10,11... | collective-permute-start | bytes 172040 | tf_op jit(solution)/shard_map/ppermute | solution.py:27
  52.8 1.2 %collective-permute-start.34 = (bf16[8,3584]{1,0:T(8,128)(2,1)S(1)}, bf16[8,3584]{1,0:T(8,128)(2,1)S(1)}, u32[]{:S(2)}, u32[]{:S(2)}) collective-permute-start(bf16[8,3584]{1,0:T(8,128)(2,1)S(1)} %collective-permute-done.30.refs_2_), channel_id=1, source_target_pairs={{0,1},{1,0},{2,3},{3,2},{4,5},{5,4},{6,7},{7,6},{8,9},{9,8},{10,11... | collective-permute-start | bytes 172040 | tf_op jit(solution)/shard_map/ppermute | solution.py:27
  52.8 1.4 %collective-permute-start.33 = (bf16[8,3584]{1,0:T(8,128)(2,1)S(1)}, bf16[8,3584]{1,0:T(8,128)(2,1)S(1)}, u32[]{:S(2)}, u32[]{:S(2)}) collective-permute-start(bf16[8,3584]{1,0:T(8,128)(2,1)S(1)} %collective-permute-done.29.refs_1_), channel_id=1, source_target_pairs={{0,1},{1,0},{2,3},{3,2},{4,5},{5,4},{6,7},{7,6},{8,9},{9,8},{10,11... | collective-permute-start | bytes 172040 | tf_op jit(solution)/shard_map/ppermute | solution.py:27
  56.5 1.4 %collective-permute-start.44 = (bf16[8,7168]{1,0:T(8,128)(2,1)S(1)}, bf16[8,7168]{1,0:T(8,128)(2,1)S(1)}, u32[]{:S(2)}, u32[]{:S(2)}) collective-permute-start(bf16[8,7168]{1,0:T(8,128)(2,1)S(1)} %get-tuple-element.76), channel_id=1, source_target_pairs={{0,1},{1,0},{2,3},{3,2},{4,5},{5,4},{6,7},{7,6},{8,9},{9,8},{10,11... | collective-permute-start | bytes 344072 | tf_op jit(solution)/shard_map/ppermute | solution.py:27
  56.9 3.0 %collective-permute-start.46 = (bf16[8,7168]{1,0:T(8,128)(2,1)S(1)}, bf16[8,7168]{1,0:T(8,128)(2,1)S(1)}, u32[]{:S(2)}, u32[]{:S(2)}) collective-permute-start(bf16[8,7168]{1,0:T(8,128)(2,1)S(1)} %get-tuple-element.78), channel_id=1, source_target_pairs={{0,1},{1,0},{2,3},{3,2},{4,5},{5,4},{6,7},{7,6},{8,9},{9,8},{10,11... | collective-permute-start | bytes 344072 | tf_op jit(solution)/shard_map/ppermute | solution.py:27
  57.1 4.3 %collective-permute-start.48 = (bf16[8,7168]{1,0:T(8,128)(2,1)S(1)}, bf16[8,7168]{1,0:T(8,128)(2,1)S(1)}, u32[]{:S(2)}, u32[]{:S(2)}) collective-permute-start(bf16[8,7168]{1,0:T(8,128)(2,1)S(1)} %get-tuple-element.80), channel_id=1, source_target_pairs={{0,1},{1,0},{2,3},{3,2},{4,5},{5,4},{6,7},{7,6},{8,9},{9,8},{10,11... | collective-permute-start | bytes 344072 | tf_op jit(solution)/shard_map/ppermute | solution.py:27
  57.4 4.9 %collective-permute-start.43 = (bf16[8,7168]{1,0:T(8,128)(2,1)S(1)}, bf16[8,7168]{1,0:T(8,128)(2,1)S(1)}, u32[]{:S(2)}, u32[]{:S(2)}) collective-permute-start(bf16[8,7168]{1,0:T(8,128)(2,1)S(1)} %get-tuple-element.74), channel_id=1, source_target_pairs={{0,1},{1,0},{2,3},{3,2},{4,5},{5,4},{6,7},{7,6},{8,9},{9,8},{10,11... | collective-permute-start | bytes 344072 | tf_op jit(solution)/shard_map/ppermute | solution.py:27
  57.9 6.9 %collective-permute-start.45 = (bf16[8,7168]{1,0:T(8,128)(2,1)S(1)}, bf16[8,7168]{1,0:T(8,128)(2,1)S(1)}, u32[]{:S(2)}, u32[]{:S(2)}) collective-permute-start(bf16[8,7168]{1,0:T(8,128)(2,1)S(1)} %shard_map.89), channel_id=1, source_target_pairs={{0,6},{1,7},{2,4},{3,5},{4,2},{5,3},{6,0},{7,1},{8,14},{9,15},{10,... | collective-permute-start | bytes 344072 | tf_op jit(solution)/shard_map/ppermute | solution.py:27
  60.0 6.8 %collective-permute-start.47 = (bf16[8,7168]{1,0:T(8,128)(2,1)S(1)}, bf16[8,7168]{1,0:T(8,128)(2,1)S(1)}, u32[]{:S(2)}, u32[]{:S(2)}) collective-permute-start(bf16[8,7168]{1,0:T(8,128)(2,1)S(1)} %shard_map.90), channel_id=1, source_target_pairs={{0,2},{1,5},{2,0},{3,7},{4,6},{5,1},{6,4},{7,3},{8,10},{9,13},{10,... | collective-permute-start | bytes 344072 | tf_op jit(solution)/shard_map/ppermute | solution.py:27
  61.4 5.3 %collective-permute-start.49 = (bf16[8,7168]{1,0:T(8,128)(2,1)S(1)}, bf16[8,7168]{1,0:T(8,128)(2,1)S(1)}, u32[]{:S(2)}, u32[]{:S(2)}) collective-permute-start(bf16[8,7168]{1,0:T(8,128)(2,1)S(1)} %shard_map.91), channel_id=1, source_target_pairs={{0,4},{1,3},{2,6},{3,1},{4,0},{5,7},{6,2},{7,5},{8,12},{9,11},{10,... | collective-permute-start | bytes 344072 | tf_op jit(solution)/shard_map/ppermute | solution.py:27
  61.7 7.9 %collective-permute-start.28 = (bf16[4,7168]{1,0:T(4,128)(2,1)S(1)}, bf16[4,7168]{1,0:T(4,128)(2,1)S(1)}, u32[]{:S(2)}, u32[]{:S(2)}) collective-permute-start(bf16[4,7168]{1,0:T(4,128)(2,1)S(1)} %shard_map.87), channel_id=1, source_target_pairs={{0,16},{1,17},{2,18},{3,19},{4,20},{5,21},{6,22},{7,23},{8,24},{9,... | collective-permute-start | bytes 172040 | tf_op jit(solution)/shard_map/ppermute | solution.py:27
  66.8 6.7 %collective-permute-start.50 = (bf16[4,7168]{1,0:T(4,128)(2,1)S(1)}, bf16[4,7168]{1,0:T(4,128)(2,1)S(1)}, u32[]{:S(2)}, u32[]{:S(2)}) collective-permute-start(bf16[4,7168]{1,0:T(4,128)(2,1)S(1)} %get-tuple-element.81), channel_id=1, source_target_pairs={{0,24},{1,25},{2,26},{3,27},{4,28},{5,29},{6,30},{7,31},{8,16},{9,... | collective-permute-start | bytes 172040 | tf_op jit(solution)/shard_map/ppermute | solution.py:27
  68.7 4.8 %collective-permute-start.51 = (bf16[4,7168]{1,0:T(4,128)(2,1)S(1)}, bf16[4,7168]{1,0:T(4,128)(2,1)S(1)}, u32[]{:S(2)}, u32[]{:S(2)}) collective-permute-start(bf16[4,7168]{1,0:T(4,128)(2,1)S(1)} %get-tuple-element.82), channel_id=1, source_target_pairs={{0,16},{1,17},{2,18},{3,19},{4,20},{5,21},{6,22},{7,23},{8,24},{9,... | collective-permute-start | bytes 172040 | tf_op jit(solution)/shard_map/ppermute | solution.py:27

commit v11 on v7

--- a/solution.py
+++ b/solution.py
@@ -31,8 +31,7 @@
 
 
 CORE = (1, 1)
-NEAR = (4, 2)
-BIG = (2, 4)
+SQUARE = ((4, 2), (2, 4), (6, 6))
 STAY = (0, 0)
 
 
@@ -134,22 +133,44 @@
             out_ref[:, span] = total[place * rows:(place + 1) * rows].astype(jnp.bfloat16)
 
 
-def meet_kernel(rest_ref, near_ref, far_ref, out_ref, own_ref):
+def normalise(raw_ref, gain_ref, out_ref):
+    rows, dim = raw_ref.shape
+    square = jnp.zeros((rows, LANES), jnp.float32)
+    for start in range(0, dim, LANES):
+        piece = raw_ref[:, start:start + LANES].astype(jnp.float32)
+        square += piece * piece
+    inv = lax.rsqrt(jnp.sum(square, axis=1, keepdims=True) / dim + 1e-06)
+    for span in spans(dim):
+        scaled = raw_ref[:, span].astype(jnp.float32) * inv * gain_ref[:, span]
+        out_ref[:, span] = scaled.astype(jnp.bfloat16)
+
+
+def first_kernel(own_ref, far_ref, gain_ref, out_ref, raw_ref):
+    dim = raw_ref.shape[1]
+    for span in spans(dim):
+        rows = [ref[:, span].astype(jnp.float32) for ref in (own_ref, far_ref)]
+        raw_ref[:, span] = jnp.concatenate(rows, axis=0).astype(jnp.bfloat16)
+    tails = [ref[:, dim:].astype(jnp.float32) for ref in (own_ref, far_ref)]
+    out_ref[:, dim:] = jnp.concatenate(tails, axis=0).astype(jnp.bfloat16)
+    normalise(raw_ref, gain_ref, out_ref)
+
+
+def meet_kernel(rest_ref, near_ref, far_ref, gain_ref, out_ref, raw_ref, own_ref):
     half = own_ref.shape[0]
     for span in spans(out_ref.shape[1]):
         far = far_ref[:, span].astype(jnp.float32)
         total = rest_ref[:, span].astype(jnp.float32) + near_ref[:, span].astype(jnp.float32)
         total = (total + jnp.concatenate([far[half:], far[:half]], axis=0)).astype(jnp.bfloat16)
-        out_ref[:, span] = total
+        raw_ref[:, span] = total
         own_ref[:, span] = total[:half]
+    normalise(raw_ref, gain_ref, out_ref)
 
 
 def mlp_kernel(step_no, *refs):
     x_refs, refs = refs[:8], refs[8:]
     if step_no > 0:
         tail_ref, refs = refs[0], refs[1:]
-    (gain_ref, gate_ref, up_ref, down_ref), outs, refs = refs[:4], refs[4:12], refs[12:]
-    rows_ref = refs[-1]
+    (gate_ref, up_ref, down_ref), outs, refs = refs[:3], refs[3:11], refs[11:]
     part = outs[0].shape[0]
     dim, hidden = gate_ref.shape[1:]
     experts = lax.axis_size("expert") // GROUP
@@ -158,14 +179,6 @@
     weights = []
     for place, ref in enumerate(x_refs):
         band = slice(place * part, (place + 1) * part)
-        square = jnp.zeros((part, LANES), jnp.float32)
-        for start in range(0, dim, LANES):
-            piece = ref[:, start:start + LANES].astype(jnp.float32)
-            square += piece * piece
-        inv = lax.rsqrt(jnp.sum(square, axis=1, keepdims=True) / dim + 1e-06)
-        for span in spans(dim):
-            scaled = ref[:, span].astype(jnp.float32) * inv * gain_ref[:, span]
-            rows_ref[band, span] = scaled.astype(jnp.bfloat16)
         if step_no == 0:
             tail = ref[:, dim:]
             refs[0][band, :] = tail
@@ -176,7 +189,7 @@
     gated = jnp.zeros((8 * part, hidden), jnp.float32)
     up_part = jnp.zeros((8 * part, hidden), jnp.float32)
     for span in spans(dim):
-        rows = rows_ref[:, span]
+        rows = jnp.concatenate([ref[:, span].astype(jnp.float32) for ref in x_refs], axis=0).astype(jnp.bfloat16)
         gated += jnp.dot(rows, gate_ref[0, span, :], preferred_element_type=jnp.float32)
         up_part += jnp.dot(rows, up_ref[0, span, :], preferred_element_type=jnp.float32)
     inner = (gated / (1.0 + jnp.exp(-gated)) * up_part).astype(jnp.bfloat16)
@@ -188,15 +201,14 @@
             out_ref[:, span] = jnp.where(weight > 0.0, weight * mine, 0.0).astype(jnp.bfloat16)
 
 
-def mlp(step_no, xs, tail, gain, gate, up, down):
+def mlp(step_no, xs, tail, gate, up, down):
     dim, hidden = gate.shape[1:]
     part = xs[0].shape[0]
     gate, up, down = [pltpu.with_memory_space_constraint(w, pltpu.VMEM) for w in (gate, up, down)]
     first = step_no == 0
-    args = list(xs) + ([] if first else [tail]) + [gain, gate, up, down]
+    args = list(xs) + ([] if first else [tail]) + [gate, up, down]
     result = call(
         functools.partial(mlp_kernel, step_no), [(part, dim)] * 8 + [(8 * part, LANES)] * first, *args,
-        scratch_shapes=[pltpu.VMEM((8 * part, dim), jnp.bfloat16)],
         cost_estimate=pl.CostEstimate(
             flops=48 * part * dim * hidden, bytes_accessed=6 * dim * hidden, transcendentals=0
         ),
@@ -229,36 +241,33 @@
     block = prepare(owners // GROUP, states, routing, route_weight)
     other = exchange(block, top, 0)
     block, other, *weights = lax.optimization_barrier((block, other, *weights))
-    pair, own, tail = join(block, other), states[0], None
+    pair, raw = call(first_kernel, [(2 * row_dev, dim + LANES), (2 * row_dev, dim)], block, other, norm_gain)
+    own, tail = states[0], None
     for step_no in range(passes_count):
         rows_a = pair
         for flips in middle:
             rows_a = join(rows_a, exchange(rows_a, flips, 0))
-        rows_b = exchange(rows_a, NEAR, 0)
-        rows_c = exchange(rows_a, BIG, 0)
-        rows_d = exchange(rows_b, BIG, 0)
-        mine = [rows_a, rows_b, rows_c, rows_d]
-        outs, tail = mlp(step_no, mine + [exchange(rows, CORE, 0) for rows in mine], tail, norm_gain, *weights)
-
-        kept_a, kept_b, kept_c, kept_d = outs[:4]
-        far_a, far_b, far_c, far_d = [exchange(rows, CORE, 0) for rows in outs[4:]]
-        big_b = exchange(add(kept_d, far_d), BIG, 0)
-        big_a = exchange(add(kept_c, far_c), BIG, 0)
-        near_a = exchange(add(kept_b, far_b, big_b), NEAR, 0)
-        parts = [kept_a, far_a, big_a, near_a]
+        mine = [rows_a] + [exchange(rows_a, flips, 0) for flips in SQUARE]
+        outs, tail = mlp(step_no, mine + [exchange(rows, CORE, 0) for rows in mine], tail, *weights)
+
+        kept, sent = outs[:4], [exchange(rows, CORE, 0) for rows in outs[4:]]
+        parts = [kept[0], sent[0]]
+        for place in (3, 2, 1):
+            parts.append(exchange(add(kept[place], sent[place]), SQUARE[place - 1], 0))
         for flips in middle[::-1]:
             low, high = split(*parts)
             parts = [low, exchange(high, flips, 0)]
         if step_no < passes_count - 1:
             total = add(*parts)
-            rest = exchange(pair, STAY, 1)
-            pair, own = call(
-                meet_kernel, [(2 * row_dev, dim), (row_dev, dim)], rest, exchange(total, STAY, 1), exchange(total, top, 1)
+            rest = exchange(raw, STAY, 1)
+            pair, raw, own = call(
+                meet_kernel, [(2 * row_dev, dim), (2 * row_dev, dim), (row_dev, dim)],
+                rest, exchange(total, STAY, 1), exchange(total, top, 1), norm_gain,
             )
         else:
             low, high = split(*parts)
             rest = exchange(own, STAY, 1)
-            own = add(rest, exchange(low, STAY, 1), exchange(high, top, 1))
+            own = add(rest, exchange(high, top, 1), exchange(low, STAY, 1))
     return own[None]
 
 

time: 77.5 us -> 72.1 us (0.930)
  waiting for transfers between devices: 37.8 us -> 30.9 us
  starting transfers between devices: 28.4 us -> 29.6 us
    ppermute x35, waiting for transfers between devices: 37.8 us -> 30.9 us  [exchange(): return lax.ppermute(value, ('segment', 'expert'), pairs)]
    ppermute x35, starting transfers between devices: 28.4 us -> 29.6 us  [exchange(): return lax.ppermute(value, ('segment', 'expert'), pairs)]
  transfers between devices with their start and end apart: 35 -> 35, of which waited for: 15 -> 16; matrix products, arithmetic and copies ran while one was open for 0% -> 0% of each run, Pallas kernels for 6% -> 6%
where the time goes in v11:
time: 72.1 us; the launch traced here: 71.9 us
  waiting for transfers between devices  30.9 us (43%)
  starting transfers between devices  29.6 us (41%)
  Pallas kernels  11.3 us (16%)
    ppermute x35, waiting for transfers between devices, exchange(): return lax.ppermute(value, ('segment', 'expert'), pairs)  30.9 us
    ppermute x35, starting transfers between devices, exchange(): return lax.ppermute(value, ('segment', 'expert'), pairs)  29.6 us
    pallas_call x14, Pallas kernels, call(): pl.pallas_call(kernel, out_shape=[jax.ShapeDtypeStruct(shape, jnp.bfloat1...  7.11 us
    pallas_call x1, Pallas kernels, load(): pl.pallas_call(load_kernel, out_shape=[pltpu.VMEM(w.shape, w.dtype) for w...  4.23 us
  transfers between devices with their start and end apart: 35, of which 16 were waited for; matrix products, arithmetic and copies ran while one was open for 0% of the time, Pallas kernels for 6%

profile of v11, /device:TPU:0, one launch (start us, length us, event | category | flops | bytes accessed | tf_op | source)
XLA Modules:
  0.0 71.9 jit_solution(3040139270220538081)
XLA Ops:
  0.0 1.0 %shard_map.73.own_ref = bf16[4,7296]{1,0:T(4,128)(2,1)S(1)} custom-call(bf16[1,4,7168]{2,1,0:T(4,128)(2,1)} %states_hbm.1, s32[1,2,2,4]{3,2,1,0:T(2,128)} %bitcast.3, bf16[1,2,2,4]{3,2,1,0:T(2,128)(2,1)} %bitcast.4), custom_call_target="tpu_custom_call" | custom-call | tf_op jit(solution)/shard_map/pallas_call | solution.py:43
  1.0 0.0 copy-start
  1.0 4.1 %collective-permute-start = (bf16[4,7296]{1,0:T(4,128)(2,1)S(1)}, bf16[4,7296]{1,0:T(4,128)(2,1)S(1)}, u32[]{:S(2)}, u32[]{:S(2)}) collective-permute-start(bf16[4,7296]{1,0:T(4,128)(2,1)S(1)} %shard_map.73.own_ref), channel_id=1, source_target_pairs={{0,8},{1,9},{2,10},{3,11},{4,12},{5,13},{6,14},{7,15},{8,0},{9,1},... | collective-permute-start | bytes 175112 | tf_op jit(solution)/shard_map/ppermute | solution.py:26
  5.1 4.2 %shard_map.74 = (bf16[1,7168,256]{2,1,0:T(8,128)(2,1)S(1)}, bf16[1,7168,256]{2,1,0:T(8,128)(2,1)S(1)}, bf16[1,256,7168]{2,1,0:T(8,128)(2,1)S(1)}) custom-call(bf16[1,7168,256]{2,1,0:T(8,128)(2,1)} %gate_ref.1, bf16[1,7168,256]{2,1,0:T(8,128)(2,1)} %up_ref.1, bf16[1,256,7168]{2,1,0:T(8,128)(2,1)} %down_ref.1), custom_call_target="tpu_custom_call" | custom-call | bytes 11010048 | tf_op jit(solution)/shard_map/pallas_call | solution.py:65
  9.3 0.0 collective-permute-done.far_ref
  9.3 0.2 shard_map.75
  9.5 2.6 %collective-permute-start.4 = (bf16[8,7296]{1,0:T(8,128)(2,1)S(1)}, bf16[8,7296]{1,0:T(8,128)(2,1)S(1)}, u32[]{:S(2)}, u32[]{:S(2)}) collective-permute-start(bf16[8,7296]{1,0:T(8,128)(2,1)S(1)} %get-tuple-element.42.refs_0_), channel_id=1, source_target_pairs={{0,6},{1,7},{2,4},{3,5},{4,2},{5,3},{6,0},{7,1},{8,14},{9,15},{10,... | collective-permute-start | bytes 350216 | tf_op jit(solution)/shard_map/ppermute | solution.py:26
  12.1 0.5 collective-permute-start.3
  12.7 0.4 collective-permute-start.2
  13.1 0.0 collective-permute-start.5
  13.1 3.5 %collective-permute-done.4.refs_3_ = bf16[8,7296]{1,0:T(8,128)(2,1)S(1)} collective-permute-done((bf16[8,7296]{1,0:T(8,128)(2,1)S(1)}, bf16[8,7296]{1,0:T(8,128)(2,1)S(1)}, u32[]{:S(2)}, u32[]{:S(2)}) %collective-permute-start.4) | collective-permute-done | bytes 116768 | tf_op jit(solution)/shard_map/ppermute | solution.py:26
  16.6 1.3 %collective-permute-done.3.refs_2_ = bf16[8,7296]{1,0:T(8,128)(2,1)S(1)} collective-permute-done((bf16[8,7296]{1,0:T(8,128)(2,1)S(1)}, bf16[8,7296]{1,0:T(8,128)(2,1)S(1)}, u32[]{:S(2)}, u32[]{:S(2)}) %collective-permute-start.3) | collective-permute-done | bytes 116768 | tf_op jit(solution)/shard_map/ppermute | solution.py:26
  17.9 0.5 collective-permute-start.6
  18.4 0.8 %collective-permute-done.7.refs_6_ = bf16[8,7296]{1,0:T(8,128)(2,1)S(1)} collective-permute-done((bf16[8,7296]{1,0:T(8,128)(2,1)S(1)}, bf16[8,7296]{1,0:T(8,128)(2,1)S(1)}, u32[]{:S(2)}, u32[]{:S(2)}) %collective-permute-start.7) | collective-permute-done | bytes 116768 | tf_op jit(solution)/shard_map/ppermute | solution.py:26
  19.2 0.2 collective-permute-done.6.refs_5_
  19.4 2.1 %shard_map.76 = (bf16[8,7168]{1,0:T(8,128)(2,1)S(1)}, bf16[8,7168]{1,0:T(8,128)(2,1)S(1)}, bf16[8,7168]{1,0:T(8,128)(2,1)S(1)}, bf16[8,7168]{1,0:T(8,128)(2,1)S(...) custom-call(bf16[8,7296]{1,0:T(8,128)(2,1)S(1)} %get-tuple-element.4, ...), custom_call_target="tpu_custom_call" | custom-call | flops 704643072 | bytes 11010048 | tf_op jit(solution)/shard_map/pallas_call | solution.py:43
  21.5 0.4 collective-permute-start.10
  21.9 0.2 collective-permute-start.12
  22.1 0.3 collective-permute-start.14
  22.4 0.2 collective-permute-start.9
  22.6 0.3 collective-permute-done.10.refs_1_
  22.9 2.4 %collective-permute-start.11 = (bf16[8,7168]{1,0:T(8,128)(2,1)S(1)}, bf16[8,7168]{1,0:T(8,128)(2,1)S(1)}, u32[]{:S(2)}, u32[]{:S(2)}) collective-permute-start(bf16[8,7168]{1,0:T(8,128)(2,1)S(1)} %shard_map.77), channel_id=1, source_target_pairs={{0,6},{1,7},{2,4},{3,5},{4,2},{5,3},{6,0},{7,1},{8,14},{9,15},{10,... | collective-permute-start | bytes 344072 | tf_op jit(solution)/shard_map/ppermute | solution.py:26
  25.4 0.8 %collective-permute-start.13 = (bf16[8,7168]{1,0:T(8,128)(2,1)S(1)}, bf16[8,7168]{1,0:T(8,128)(2,1)S(1)}, u32[]{:S(2)}, u32[]{:S(2)}) collective-permute-start(bf16[8,7168]{1,0:T(8,128)(2,1)S(1)} %shard_map.78), channel_id=1, source_target_pairs={{0,2},{1,5},{2,0},{3,7},{4,6},{5,1},{6,4},{7,3},{8,10},{9,13},{10,... | collective-permute-start | bytes 344072 | tf_op jit(solution)/shard_map/ppermute | solution.py:26
  26.2 0.0 collective-permute-done.14.refs_1_
  26.2 0.5 collective-permute-start.15
  26.7 1.5 %collective-permute-start.1 = (bf16[8,7168]{1,0:T(8,128)(2,1)S(1)}, bf16[8,7168]{1,0:T(8,128)(2,1)S(1)}, u32[]{:S(2)}, u32[]{:S(2)}) collective-permute-start(bf16[8,7168]{1,0:T(8,128)(2,1)S(1)} %get-tuple-element.41), channel_id=1, source_target_pairs={{0,16},{1,17},{2,18},{3,19},{4,20},{5,21},{6,22},{7,23},{8,24},{9,... | collective-permute-start | bytes 344072 | tf_op jit(solution)/shard_map/ppermute | solution.py:26
  28.2 1.7 %collective-permute-done.11.refs_2_ = bf16[8,7168]{1,0:T(8,128)(2,1)S(1)} collective-permute-done((bf16[8,7168]{1,0:T(8,128)(2,1)S(1)}, bf16[8,7168]{1,0:T(8,128)(2,1)S(1)}, u32[]{:S(2)}, u32[]{:S(2)}) %collective-permute-start.11) | collective-permute-done | bytes 114720 | tf_op jit(solution)/shard_map/ppermute | solution.py:26
  29.9 1.9 %collective-permute-done.13.refs_3_ = bf16[8,7168]{1,0:T(8,128)(2,1)S(1)} collective-permute-done((bf16[8,7168]{1,0:T(8,128)(2,1)S(1)}, bf16[8,7168]{1,0:T(8,128)(2,1)S(1)}, u32[]{:S(2)}, u32[]{:S(2)}) %collective-permute-start.13) | collective-permute-done | bytes 114720 | tf_op jit(solution)/shard_map/ppermute | solution.py:26
  31.8 0.1 shard_map.80
  31.9 2.0 %collective-permute-start.17 = (bf16[8,7168]{1,0:T(8,128)(2,1)S(1)}, bf16[8,7168]{1,0:T(8,128)(2,1)S(1)}, u32[]{:S(2)}, u32[]{:S(2)}) collective-permute-start(bf16[8,7168]{1,0:T(8,128)(2,1)S(1)} %shard_map.80), channel_id=1, source_target_pairs={{0,24},{1,25},{2,26},{3,27},{4,28},{5,29},{6,30},{7,31},{8,16},{9,... | collective-permute-start | bytes 344072 | tf_op jit(solution)/shard_map/ppermute | solution.py:26
  33.8 0.5 collective-permute-start.16
  34.4 0.0 collective-permute-done.1.rest_ref
  34.4 6.8 %collective-permute-done.17.far_ref = bf16[8,7168]{1,0:T(8,128)(2,1)S(1)} collective-permute-done((bf16[8,7168]{1,0:T(8,128)(2,1)S(1)}, bf16[8,7168]{1,0:T(8,128)(2,1)S(1)}, u32[]{:S(2)}, u32[]{:S(2)}) %collective-permute-start.17) | collective-permute-done | bytes 114720 | tf_op jit(solution)/shard_map/ppermute | solution.py:26
  41.2 0.7 shard_map.81
  41.9 2.3 %collective-permute-start.21 = (bf16[8,7168]{1,0:T(8,128)(2,1)S(1)}, bf16[8,7168]{1,0:T(8,128)(2,1)S(1)}, u32[]{:S(2)}, u32[]{:S(2)}) collective-permute-start(bf16[8,7168]{1,0:T(8,128)(2,1)S(1)} %get-tuple-element.55.refs_0_), channel_id=1, source_target_pairs={{0,6},{1,7},{2,4},{3,5},{4,2},{5,3},{6,0},{7,1},{8,14},{9,15},{10,... | collective-permute-start | bytes 344072 | tf_op jit(solution)/shard_map/ppermute | solution.py:26
  44.2 0.8 %collective-permute-start.20 = (bf16[8,7168]{1,0:T(8,128)(2,1)S(1)}, bf16[8,7168]{1,0:T(8,128)(2,1)S(1)}, u32[]{:S(2)}, u32[]{:S(2)}) collective-permute-start(bf16[8,7168]{1,0:T(8,128)(2,1)S(1)} %get-tuple-element.55.refs_0_), channel_id=1, source_target_pairs={{0,2},{1,5},{2,0},{3,7},{4,6},{5,1},{6,4},{7,3},{8,10},{9,13},{10,... | collective-permute-start | bytes 344072 | tf_op jit(solution)/shard_map/ppermute | solution.py:26
  45.0 0.4 collective-permute-start.19
  45.4 0.0 collective-permute-start.22
  45.4 3.2 %collective-permute-done.21.refs_3_ = bf16[8,7168]{1,0:T(8,128)(2,1)S(1)} collective-permute-done((bf16[8,7168]{1,0:T(8,128)(2,1)S(1)}, bf16[8,7168]{1,0:T(8,128)(2,1)S(1)}, u32[]{:S(2)}, u32[]{:S(2)}) %collective-permute-start.21) | collective-permute-done | bytes 114720 | tf_op jit(solution)/shard_map/ppermute | solution.py:26
  48.6 1.5 %collective-permute-done.20.refs_2_ = bf16[8,7168]{1,0:T(8,128)(2,1)S(1)} collective-permute-done((bf16[8,7168]{1,0:T(8,128)(2,1)S(1)}, bf16[8,7168]{1,0:T(8,128)(2,1)S(1)}, u32[]{:S(2)}, u32[]{:S(2)}) %collective-permute-start.20) | collective-permute-done | bytes 114720 | tf_op jit(solution)/shard_map/ppermute | solution.py:26
  50.1 0.0 collective-permute-start.24
  50.1 0.5 collective-permute-start.23
  50.6 0.8 %collective-permute-done.24.refs_6_ = bf16[8,7168]{1,0:T(8,128)(2,1)S(1)} collective-permute-done((bf16[8,7168]{1,0:T(8,128)(2,1)S(1)}, bf16[8,7168]{1,0:T(8,128)(2,1)S(1)}, u32[]{:S(2)}, u32[]{:S(2)}) %collective-permute-start.24) | collective-permute-done | bytes 114720 | tf_op jit(solution)/shard_map/ppermute | solution.py:26
  51.4 0.2 collective-permute-done.23.refs_5_
  51.6 2.1 %shard_map.82 = (bf16[8,7168]{1,0:T(8,128)(2,1)S(1)}, bf16[8,7168]{1,0:T(8,128)(2,1)S(1)}, bf16[8,7168]{1,0:T(8,128)(2,1)S(1)}, bf16[8,7168]{1,0:T(8,128)(2,1)S(...) custom-call(bf16[8,7168]{1,0:T(8,128)(2,1)S(1)} %get-tuple-element.5, ...), custom_call_target="tpu_custom_call" | custom-call | flops 704643072 | bytes 11010048 | tf_op jit(solution)/shard_map/pallas_call | solution.py:43
  53.7 0.4 collective-permute-start.27
  54.1 0.2 collective-permute-start.29
  54.2 0.3 collective-permute-start.31
  54.6 0.2 collective-permute-start.26
  54.8 0.3 collective-permute-done.27.refs_1_
  55.1 2.6 %collective-permute-start.28 = (bf16[8,7168]{1,0:T(8,128)(2,1)S(1)}, bf16[8,7168]{1,0:T(8,128)(2,1)S(1)}, u32[]{:S(2)}, u32[]{:S(2)}) collective-permute-start(bf16[8,7168]{1,0:T(8,128)(2,1)S(1)} %shard_map.83), channel_id=1, source_target_pairs={{0,6},{1,7},{2,4},{3,5},{4,2},{5,3},{6,0},{7,1},{8,14},{9,15},{10,... | collective-permute-start | bytes 344072 | tf_op jit(solution)/shard_map/ppermute | solution.py:26
  57.7 0.9 %collective-permute-start.30 = (bf16[8,7168]{1,0:T(8,128)(2,1)S(1)}, bf16[8,7168]{1,0:T(8,128)(2,1)S(1)}, u32[]{:S(2)}, u32[]{:S(2)}) collective-permute-start(bf16[8,7168]{1,0:T(8,128)(2,1)S(1)} %shard_map.84), channel_id=1, source_target_pairs={{0,2},{1,5},{2,0},{3,7},{4,6},{5,1},{6,4},{7,3},{8,10},{9,13},{10,... | collective-permute-start | bytes 344072 | tf_op jit(solution)/shard_map/ppermute | solution.py:26
  58.6 0.0 collective-permute-done.31.refs_1_
  58.6 0.2 collective-permute-start.32
  58.9 1.1 %collective-permute-start.18 = (bf16[4,7168]{1,0:T(4,128)(2,1)S(1)}, bf16[4,7168]{1,0:T(4,128)(2,1)S(1)}, u32[]{:S(2)}, u32[]{:S(2)}) collective-permute-start(bf16[4,7168]{1,0:T(4,128)(2,1)S(1)} %get-tuple-element.54), channel_id=1, source_target_pairs={{0,16},{1,17},{2,18},{3,19},{4,20},{5,21},{6,22},{7,23},{8,24},{9,... | collective-permute-start | bytes 172040 | tf_op jit(solution)/shard_map/ppermute | solution.py:26
  59.9 0.0 collective-permute-done.26.refs_1_
  59.9 2.1 %collective-permute-done.28.refs_2_ = bf16[8,7168]{1,0:T(8,128)(2,1)S(1)} collective-permute-done((bf16[8,7168]{1,0:T(8,128)(2,1)S(1)}, bf16[8,7168]{1,0:T(8,128)(2,1)S(1)}, u32[]{:S(2)}, u32[]{:S(2)}) %collective-permute-start.28) | collective-permute-done | bytes 114720 | tf_op jit(solution)/shard_map/ppermute | solution.py:26
  62.0 1.9 %collective-permute-done.30.refs_3_ = bf16[8,7168]{1,0:T(8,128)(2,1)S(1)} collective-permute-done((bf16[8,7168]{1,0:T(8,128)(2,1)S(1)}, bf16[8,7168]{1,0:T(8,128)(2,1)S(1)}, u32[]{:S(2)}, u32[]{:S(2)}) %collective-permute-start.30) | collective-permute-done | bytes 114720 | tf_op jit(solution)/shard_map/ppermute | solution.py:26
  63.9 0.0 collective-permute-done.32.refs_4_
  63.9 0.1 shard_map.86
  64.0 1.9 %collective-permute-start.33 = (bf16[4,7168]{1,0:T(4,128)(2,1)S(1)}, bf16[4,7168]{1,0:T(4,128)(2,1)S(1)}, u32[]{:S(2)}, u32[]{:S(2)}) collective-permute-start(bf16[4,7168]{1,0:T(4,128)(2,1)S(1)} %get-tuple-element.65), channel_id=1, source_target_pairs={{0,24},{1,25},{2,26},{3,27},{4,28},{5,29},{6,30},{7,31},{8,16},{9,... | collective-permute-start | bytes 172040 | tf_op jit(solution)/shard_map/ppermute | solution.py:26
  66.0 0.9 %collective-permute-start.34 = (bf16[4,7168]{1,0:T(4,128)(2,1)S(1)}, bf16[4,7168]{1,0:T(4,128)(2,1)S(1)}, u32[]{:S(2)}, u32[]{:S(2)}) collective-permute-start(bf16[4,7168]{1,0:T(4,128)(2,1)S(1)} %get-tuple-element.66), channel_id=1, source_target_pairs={{0,16},{1,17},{2,18},{3,19},{4,20},{5,21},{6,22},{7,23},{8,24},{9,... | collective-permute-start | bytes 172040 | tf_op jit(solution)/shard_map/ppermute | solution.py:26
  66.8 4.5 %collective-permute-done.33.refs_1_ = bf16[4,7168]{1,0:T(4,128)(2,1)S(1)} collective-permute-done((bf16[4,7168]{1,0:T(4,128)(2,1)S(1)}, bf16[4,7168]{1,0:T(4,128)(2,1)S(1)}, u32[]{:S(2)}, u32[]{:S(2)}) %collective-permute-start.33) | collective-permute-done | bytes 57376 | tf_op jit(solution)/shard_map/ppermute | solution.py:26
  71.3 0.7 shard_map.87
  (23 shorter events, 0.2 us)
Async XLA Ops:
  1.0 8.4 %copy-start = (f32[1,7168]{1,0:T(1,128)S(1)}, f32[1,7168]{1,0:T(1,128)}, u32[]{:S(2)}) copy-start(f32[1,7168]{1,0:T(1,128)} %gain_ref.3) | copy-start | bytes 86020
  1.0 8.3 %collective-permute-start = (bf16[4,7296]{1,0:T(4,128)(2,1)S(1)}, bf16[4,7296]{1,0:T(4,128)(2,1)S(1)}, u32[]{:S(2)}, u32[]{:S(2)}) collective-permute-start(bf16[4,7296]{1,0:T(4,128)(2,1)S(1)} %shard_map.73.own_ref), channel_id=1, source_target_pairs={{0,8},{1,9},{2,10},{3,11},{4,12},{5,13},{6,14},{7,15},{8,0},{9,1},... | collective-permute-start | bytes 175112 | tf_op jit(solution)/shard_map/ppermute | solution.py:26
  9.5 7.0 %collective-permute-start.4 = (bf16[8,7296]{1,0:T(8,128)(2,1)S(1)}, bf16[8,7296]{1,0:T(8,128)(2,1)S(1)}, u32[]{:S(2)}, u32[]{:S(2)}) collective-permute-start(bf16[8,7296]{1,0:T(8,128)(2,1)S(1)} %get-tuple-element.42.refs_0_), channel_id=1, source_target_pairs={{0,6},{1,7},{2,4},{3,5},{4,2},{5,3},{6,0},{7,1},{8,14},{9,15},{10,... | collective-permute-start | bytes 350216 | tf_op jit(solution)/shard_map/ppermute | solution.py:26
  12.1 5.7 %collective-permute-start.3 = (bf16[8,7296]{1,0:T(8,128)(2,1)S(1)}, bf16[8,7296]{1,0:T(8,128)(2,1)S(1)}, u32[]{:S(2)}, u32[]{:S(2)}) collective-permute-start(bf16[8,7296]{1,0:T(8,128)(2,1)S(1)} %get-tuple-element.42.refs_0_), channel_id=1, source_target_pairs={{0,2},{1,5},{2,0},{3,7},{4,6},{5,1},{6,4},{7,3},{8,10},{9,13},{10,... | collective-permute-start | bytes 350216 | tf_op jit(solution)/shard_map/ppermute | solution.py:26
  12.7 5.2 %collective-permute-start.2 = (bf16[8,7296]{1,0:T(8,128)(2,1)S(1)}, bf16[8,7296]{1,0:T(8,128)(2,1)S(1)}, u32[]{:S(2)}, u32[]{:S(2)}) collective-permute-start(bf16[8,7296]{1,0:T(8,128)(2,1)S(1)} %get-tuple-element.42.refs_0_), channel_id=1, source_target_pairs={{0,4},{1,3},{2,6},{3,1},{4,0},{5,7},{6,2},{7,5},{8,12},{9,11},{10,... | collective-permute-start | bytes 350216 | tf_op jit(solution)/shard_map/ppermute | solution.py:26
  13.1 5.3 %collective-permute-start.5 = (bf16[8,7296]{1,0:T(8,128)(2,1)S(1)}, bf16[8,7296]{1,0:T(8,128)(2,1)S(1)}, u32[]{:S(2)}, u32[]{:S(2)}) collective-permute-start(bf16[8,7296]{1,0:T(8,128)(2,1)S(1)} %get-tuple-element.42.refs_0_), channel_id=1, source_target_pairs={{0,1},{1,0},{2,3},{3,2},{4,5},{5,4},{6,7},{7,6},{8,9},{9,8},{10,11... | collective-permute-start | bytes 350216 | tf_op jit(solution)/shard_map/ppermute | solution.py:26
  16.6 1.8 %collective-permute-start.8 = (bf16[8,7296]{1,0:T(8,128)(2,1)S(1)}, bf16[8,7296]{1,0:T(8,128)(2,1)S(1)}, u32[]{:S(2)}, u32[]{:S(2)}) collective-permute-start(bf16[8,7296]{1,0:T(8,128)(2,1)S(1)} %collective-permute-done.4.refs_3_), channel_id=1, source_target_pairs={{0,1},{1,0},{2,3},{3,2},{4,5},{5,4},{6,7},{7,6},{8,9},{9,8},{10,11... | collective-permute-start | bytes 350216 | tf_op jit(solution)/shard_map/ppermute | solution.py:26
  17.9 1.3 %collective-permute-start.7 = (bf16[8,7296]{1,0:T(8,128)(2,1)S(1)}, bf16[8,7296]{1,0:T(8,128)(2,1)S(1)}, u32[]{:S(2)}, u32[]{:S(2)}) collective-permute-start(bf16[8,7296]{1,0:T(8,128)(2,1)S(1)} %collective-permute-done.3.refs_2_), channel_id=1, source_target_pairs={{0,1},{1,0},{2,3},{3,2},{4,5},{5,4},{6,7},{7,6},{8,9},{9,8},{10,11... | collective-permute-start | bytes 350216 | tf_op jit(solution)/shard_map/ppermute | solution.py:26
  17.9 1.5 %collective-permute-start.6 = (bf16[8,7296]{1,0:T(8,128)(2,1)S(1)}, bf16[8,7296]{1,0:T(8,128)(2,1)S(1)}, u32[]{:S(2)}, u32[]{:S(2)}) collective-permute-start(bf16[8,7296]{1,0:T(8,128)(2,1)S(1)} %collective-permute-done.2.refs_1_), channel_id=1, source_target_pairs={{0,1},{1,0},{2,3},{3,2},{4,5},{5,4},{6,7},{7,6},{8,9},{9,8},{10,11... | collective-permute-start | bytes 350216 | tf_op jit(solution)/shard_map/ppermute | solution.py:26
  21.5 1.4 %collective-permute-start.10 = (bf16[8,7168]{1,0:T(8,128)(2,1)S(1)}, bf16[8,7168]{1,0:T(8,128)(2,1)S(1)}, u32[]{:S(2)}, u32[]{:S(2)}) collective-permute-start(bf16[8,7168]{1,0:T(8,128)(2,1)S(1)} %get-tuple-element.49), channel_id=1, source_target_pairs={{0,1},{1,0},{2,3},{3,2},{4,5},{5,4},{6,7},{7,6},{8,9},{9,8},{10,11... | collective-permute-start | bytes 344072 | tf_op jit(solution)/shard_map/ppermute | solution.py:26
  21.9 3.4 %collective-permute-start.12 = (bf16[8,7168]{1,0:T(8,128)(2,1)S(1)}, bf16[8,7168]{1,0:T(8,128)(2,1)S(1)}, u32[]{:S(2)}, u32[]{:S(2)}) collective-permute-start(bf16[8,7168]{1,0:T(8,128)(2,1)S(1)} %get-tuple-element.51), channel_id=1, source_target_pairs={{0,1},{1,0},{2,3},{3,2},{4,5},{5,4},{6,7},{7,6},{8,9},{9,8},{10,11... | collective-permute-start | bytes 344072 | tf_op jit(solution)/shard_map/ppermute | solution.py:26
  22.1 4.1 %collective-permute-start.14 = (bf16[8,7168]{1,0:T(8,128)(2,1)S(1)}, bf16[8,7168]{1,0:T(8,128)(2,1)S(1)}, u32[]{:S(2)}, u32[]{:S(2)}) collective-permute-start(bf16[8,7168]{1,0:T(8,128)(2,1)S(1)} %get-tuple-element.53), channel_id=1, source_target_pairs={{0,1},{1,0},{2,3},{3,2},{4,5},{5,4},{6,7},{7,6},{8,9},{9,8},{10,11... | collective-permute-start | bytes 344072 | tf_op jit(solution)/shard_map/ppermute | solution.py:26
  22.4 5.8 %collective-permute-start.9 = (bf16[8,7168]{1,0:T(8,128)(2,1)S(1)}, bf16[8,7168]{1,0:T(8,128)(2,1)S(1)}, u32[]{:S(2)}, u32[]{:S(2)}) collective-permute-start(bf16[8,7168]{1,0:T(8,128)(2,1)S(1)} %get-tuple-element.47), channel_id=1, source_target_pairs={{0,1},{1,0},{2,3},{3,2},{4,5},{5,4},{6,7},{7,6},{8,9},{9,8},{10,11... | collective-permute-start | bytes 344072 | tf_op jit(solution)/shard_map/ppermute | solution.py:26
  22.9 6.9 %collective-permute-start.11 = (bf16[8,7168]{1,0:T(8,128)(2,1)S(1)}, bf16[8,7168]{1,0:T(8,128)(2,1)S(1)}, u32[]{:S(2)}, u32[]{:S(2)}) collective-permute-start(bf16[8,7168]{1,0:T(8,128)(2,1)S(1)} %shard_map.77), channel_id=1, source_target_pairs={{0,6},{1,7},{2,4},{3,5},{4,2},{5,3},{6,0},{7,1},{8,14},{9,15},{10,... | collective-permute-start | bytes 344072 | tf_op jit(solution)/shard_map/ppermute | solution.py:26
  25.4 6.4 %collective-permute-start.13 = (bf16[8,7168]{1,0:T(8,128)(2,1)S(1)}, bf16[8,7168]{1,0:T(8,128)(2,1)S(1)}, u32[]{:S(2)}, u32[]{:S(2)}) collective-permute-start(bf16[8,7168]{1,0:T(8,128)(2,1)S(1)} %shard_map.78), channel_id=1, source_target_pairs={{0,2},{1,5},{2,0},{3,7},{4,6},{5,1},{6,4},{7,3},{8,10},{9,13},{10,... | collective-permute-start | bytes 344072 | tf_op jit(solution)/shard_map/ppermute | solution.py:26
  26.2 5.6 %collective-permute-start.15 = (bf16[8,7168]{1,0:T(8,128)(2,1)S(1)}, bf16[8,7168]{1,0:T(8,128)(2,1)S(1)}, u32[]{:S(2)}, u32[]{:S(2)}) collective-permute-start(bf16[8,7168]{1,0:T(8,128)(2,1)S(1)} %shard_map.79), channel_id=1, source_target_pairs={{0,4},{1,3},{2,6},{3,1},{4,0},{5,7},{6,2},{7,5},{8,12},{9,11},{10,... | collective-permute-start | bytes 344072 | tf_op jit(solution)/shard_map/ppermute | solution.py:26
  26.7 7.7 %collective-permute-start.1 = (bf16[8,7168]{1,0:T(8,128)(2,1)S(1)}, bf16[8,7168]{1,0:T(8,128)(2,1)S(1)}, u32[]{:S(2)}, u32[]{:S(2)}) collective-permute-start(bf16[8,7168]{1,0:T(8,128)(2,1)S(1)} %get-tuple-element.41), channel_id=1, source_target_pairs={{0,16},{1,17},{2,18},{3,19},{4,20},{5,21},{6,22},{7,23},{8,24},{9,... | collective-permute-start | bytes 344072 | tf_op jit(solution)/shard_map/ppermute | solution.py:26
  31.9 9.4 %collective-permute-start.17 = (bf16[8,7168]{1,0:T(8,128)(2,1)S(1)}, bf16[8,7168]{1,0:T(8,128)(2,1)S(1)}, u32[]{:S(2)}, u32[]{:S(2)}) collective-permute-start(bf16[8,7168]{1,0:T(8,128)(2,1)S(1)} %shard_map.80), channel_id=1, source_target_pairs={{0,24},{1,25},{2,26},{3,27},{4,28},{5,29},{6,30},{7,31},{8,16},{9,... | collective-permute-start | bytes 344072 | tf_op jit(solution)/shard_map/ppermute | solution.py:26
  33.8 7.4 %collective-permute-start.16 = (bf16[8,7168]{1,0:T(8,128)(2,1)S(1)}, bf16[8,7168]{1,0:T(8,128)(2,1)S(1)}, u32[]{:S(2)}, u32[]{:S(2)}) collective-permute-start(bf16[8,7168]{1,0:T(8,128)(2,1)S(1)} %shard_map.80), channel_id=1, source_target_pairs={{0,16},{1,17},{2,18},{3,19},{4,20},{5,21},{6,22},{7,23},{8,24},{9,... | collective-permute-start | bytes 344072 | tf_op jit(solution)/shard_map/ppermute | solution.py:26
  41.9 6.7 %collective-permute-start.21 = (bf16[8,7168]{1,0:T(8,128)(2,1)S(1)}, bf16[8,7168]{1,0:T(8,128)(2,1)S(1)}, u32[]{:S(2)}, u32[]{:S(2)}) collective-permute-start(bf16[8,7168]{1,0:T(8,128)(2,1)S(1)} %get-tuple-element.55.refs_0_), channel_id=1, source_target_pairs={{0,6},{1,7},{2,4},{3,5},{4,2},{5,3},{6,0},{7,1},{8,14},{9,15},{10,... | collective-permute-start | bytes 344072 | tf_op jit(solution)/shard_map/ppermute | solution.py:26
  44.2 5.8 %collective-permute-start.20 = (bf16[8,7168]{1,0:T(8,128)(2,1)S(1)}, bf16[8,7168]{1,0:T(8,128)(2,1)S(1)}, u32[]{:S(2)}, u32[]{:S(2)}) collective-permute-start(bf16[8,7168]{1,0:T(8,128)(2,1)S(1)} %get-tuple-element.55.refs_0_), channel_id=1, source_target_pairs={{0,2},{1,5},{2,0},{3,7},{4,6},{5,1},{6,4},{7,3},{8,10},{9,13},{10,... | collective-permute-start | bytes 344072 | tf_op jit(solution)/shard_map/ppermute | solution.py:26
  45.0 5.0 %collective-permute-start.19 = (bf16[8,7168]{1,0:T(8,128)(2,1)S(1)}, bf16[8,7168]{1,0:T(8,128)(2,1)S(1)}, u32[]{:S(2)}, u32[]{:S(2)}) collective-permute-start(bf16[8,7168]{1,0:T(8,128)(2,1)S(1)} %get-tuple-element.55.refs_0_), channel_id=1, source_target_pairs={{0,4},{1,3},{2,6},{3,1},{4,0},{5,7},{6,2},{7,5},{8,12},{9,11},{10,... | collective-permute-start | bytes 344072 | tf_op jit(solution)/shard_map/ppermute | solution.py:26
  45.4 5.2 %collective-permute-start.22 = (bf16[8,7168]{1,0:T(8,128)(2,1)S(1)}, bf16[8,7168]{1,0:T(8,128)(2,1)S(1)}, u32[]{:S(2)}, u32[]{:S(2)}) collective-permute-start(bf16[8,7168]{1,0:T(8,128)(2,1)S(1)} %get-tuple-element.55.refs_0_), channel_id=1, source_target_pairs={{0,1},{1,0},{2,3},{3,2},{4,5},{5,4},{6,7},{7,6},{8,9},{9,8},{10,11... | collective-permute-start | bytes 344072 | tf_op jit(solution)/shard_map/ppermute | solution.py:26
  48.6 2.0 %collective-permute-start.25 = (bf16[8,7168]{1,0:T(8,128)(2,1)S(1)}, bf16[8,7168]{1,0:T(8,128)(2,1)S(1)}, u32[]{:S(2)}, u32[]{:S(2)}) collective-permute-start(bf16[8,7168]{1,0:T(8,128)(2,1)S(1)} %collective-permute-done.21.refs_3_), channel_id=1, source_target_pairs={{0,1},{1,0},{2,3},{3,2},{4,5},{5,4},{6,7},{7,6},{8,9},{9,8},{10,11... | collective-permute-start | bytes 344072 | tf_op jit(solution)/shard_map/ppermute | solution.py:26
  50.1 1.3 %collective-permute-start.24 = (bf16[8,7168]{1,0:T(8,128)(2,1)S(1)}, bf16[8,7168]{1,0:T(8,128)(2,1)S(1)}, u32[]{:S(2)}, u32[]{:S(2)}) collective-permute-start(bf16[8,7168]{1,0:T(8,128)(2,1)S(1)} %collective-permute-done.20.refs_2_), channel_id=1, source_target_pairs={{0,1},{1,0},{2,3},{3,2},{4,5},{5,4},{6,7},{7,6},{8,9},{9,8},{10,11... | collective-permute-start | bytes 344072 | tf_op jit(solution)/shard_map/ppermute | solution.py:26
  50.1 1.5 %collective-permute-start.23 = (bf16[8,7168]{1,0:T(8,128)(2,1)S(1)}, bf16[8,7168]{1,0:T(8,128)(2,1)S(1)}, u32[]{:S(2)}, u32[]{:S(2)}) collective-permute-start(bf16[8,7168]{1,0:T(8,128)(2,1)S(1)} %collective-permute-done.19.refs_1_), channel_id=1, source_target_pairs={{0,1},{1,0},{2,3},{3,2},{4,5},{5,4},{6,7},{7,6},{8,9},{9,8},{10,11... | collective-permute-start | bytes 344072 | tf_op jit(solution)/shard_map/ppermute | solution.py:26
  53.7 1.4 %collective-permute-start.27 = (bf16[8,7168]{1,0:T(8,128)(2,1)S(1)}, bf16[8,7168]{1,0:T(8,128)(2,1)S(1)}, u32[]{:S(2)}, u32[]{:S(2)}) collective-permute-start(bf16[8,7168]{1,0:T(8,128)(2,1)S(1)} %get-tuple-element.60), channel_id=1, source_target_pairs={{0,1},{1,0},{2,3},{3,2},{4,5},{5,4},{6,7},{7,6},{8,9},{9,8},{10,11... | collective-permute-start | bytes 344072 | tf_op jit(solution)/shard_map/ppermute | solution.py:26
  54.1 3.6 %collective-permute-start.29 = (bf16[8,7168]{1,0:T(8,128)(2,1)S(1)}, bf16[8,7168]{1,0:T(8,128)(2,1)S(1)}, u32[]{:S(2)}, u32[]{:S(2)}) collective-permute-start(bf16[8,7168]{1,0:T(8,128)(2,1)S(1)} %get-tuple-element.62), channel_id=1, source_target_pairs={{0,1},{1,0},{2,3},{3,2},{4,5},{5,4},{6,7},{7,6},{8,9},{9,8},{10,11... | collective-permute-start | bytes 344072 | tf_op jit(solution)/shard_map/ppermute | solution.py:26
  54.2 4.3 %collective-permute-start.31 = (bf16[8,7168]{1,0:T(8,128)(2,1)S(1)}, bf16[8,7168]{1,0:T(8,128)(2,1)S(1)}, u32[]{:S(2)}, u32[]{:S(2)}) collective-permute-start(bf16[8,7168]{1,0:T(8,128)(2,1)S(1)} %get-tuple-element.64), channel_id=1, source_target_pairs={{0,1},{1,0},{2,3},{3,2},{4,5},{5,4},{6,7},{7,6},{8,9},{9,8},{10,11... | collective-permute-start | bytes 344072 | tf_op jit(solution)/shard_map/ppermute | solution.py:26
  54.6 5.3 %collective-permute-start.26 = (bf16[8,7168]{1,0:T(8,128)(2,1)S(1)}, bf16[8,7168]{1,0:T(8,128)(2,1)S(1)}, u32[]{:S(2)}, u32[]{:S(2)}) collective-permute-start(bf16[8,7168]{1,0:T(8,128)(2,1)S(1)} %get-tuple-element.58), channel_id=1, source_target_pairs={{0,1},{1,0},{2,3},{3,2},{4,5},{5,4},{6,7},{7,6},{8,9},{9,8},{10,11... | collective-permute-start | bytes 344072 | tf_op jit(solution)/shard_map/ppermute | solution.py:26
  55.1 6.9 %collective-permute-start.28 = (bf16[8,7168]{1,0:T(8,128)(2,1)S(1)}, bf16[8,7168]{1,0:T(8,128)(2,1)S(1)}, u32[]{:S(2)}, u32[]{:S(2)}) collective-permute-start(bf16[8,7168]{1,0:T(8,128)(2,1)S(1)} %shard_map.83), channel_id=1, source_target_pairs={{0,6},{1,7},{2,4},{3,5},{4,2},{5,3},{6,0},{7,1},{8,14},{9,15},{10,... | collective-permute-start | bytes 344072 | tf_op jit(solution)/shard_map/ppermute | solution.py:26
  57.7 6.2 %collective-permute-start.30 = (bf16[8,7168]{1,0:T(8,128)(2,1)S(1)}, bf16[8,7168]{1,0:T(8,128)(2,1)S(1)}, u32[]{:S(2)}, u32[]{:S(2)}) collective-permute-start(bf16[8,7168]{1,0:T(8,128)(2,1)S(1)} %shard_map.84), channel_id=1, source_target_pairs={{0,2},{1,5},{2,0},{3,7},{4,6},{5,1},{6,4},{7,3},{8,10},{9,13},{10,... | collective-permute-start | bytes 344072 | tf_op jit(solution)/shard_map/ppermute | solution.py:26
  58.6 5.3 %collective-permute-start.32 = (bf16[8,7168]{1,0:T(8,128)(2,1)S(1)}, bf16[8,7168]{1,0:T(8,128)(2,1)S(1)}, u32[]{:S(2)}, u32[]{:S(2)}) collective-permute-start(bf16[8,7168]{1,0:T(8,128)(2,1)S(1)} %shard_map.85), channel_id=1, source_target_pairs={{0,4},{1,3},{2,6},{3,1},{4,0},{5,7},{6,2},{7,5},{8,12},{9,11},{10,... | collective-permute-start | bytes 344072 | tf_op jit(solution)/shard_map/ppermute | solution.py:26
  58.9 8.0 %collective-permute-start.18 = (bf16[4,7168]{1,0:T(4,128)(2,1)S(1)}, bf16[4,7168]{1,0:T(4,128)(2,1)S(1)}, u32[]{:S(2)}, u32[]{:S(2)}) collective-permute-start(bf16[4,7168]{1,0:T(4,128)(2,1)S(1)} %get-tuple-element.54), channel_id=1, source_target_pairs={{0,16},{1,17},{2,18},{3,19},{4,20},{5,21},{6,22},{7,23},{8,24},{9,... | collective-permute-start | bytes 172040 | tf_op jit(solution)/shard_map/ppermute | solution.py:26
  64.0 7.3 %collective-permute-start.33 = (bf16[4,7168]{1,0:T(4,128)(2,1)S(1)}, bf16[4,7168]{1,0:T(4,128)(2,1)S(1)}, u32[]{:S(2)}, u32[]{:S(2)}) collective-permute-start(bf16[4,7168]{1,0:T(4,128)(2,1)S(1)} %get-tuple-element.65), channel_id=1, source_target_pairs={{0,24},{1,25},{2,26},{3,27},{4,28},{5,29},{6,30},{7,31},{8,16},{9,... | collective-permute-start | bytes 172040 | tf_op jit(solution)/shard_map/ppermute | solution.py:26
  66.0 5.3 %collective-permute-start.34 = (bf16[4,7168]{1,0:T(4,128)(2,1)S(1)}, bf16[4,7168]{1,0:T(4,128)(2,1)S(1)}, u32[]{:S(2)}, u32[]{:S(2)}) collective-permute-start(bf16[4,7168]{1,0:T(4,128)(2,1)S(1)} %get-tuple-element.66), channel_id=1, source_target_pairs={{0,16},{1,17},{2,18},{3,19},{4,20},{5,21},{6,22},{7,23},{8,24},{9,... | collective-permute-start | bytes 172040 | tf_op jit(solution)/shard_map/ppermute | solution.py:26

commit v12 on v11

v12 whole, which is shorter than its diff:
```python
import functools

import jax
import jax.numpy as jnp
from jax import lax
from jax.experimental import pallas as pl
from jax.experimental.pallas import tpu as pltpu
from jax.sharding import PartitionSpec as P

GROUP = 4
LANES = 128
CHUNK = 1024
VMEM_LIMIT = 16 * 1024 * 1024
VMEM = pl.BlockSpec(memory_space=pltpu.VMEM)


def exchange(value, flips, hop):
    segments, owners = lax.axis_size("segment"), lax.axis_size("expert")
    if flips == (0, 0) and hop % segments == 0:
        return value
    pairs = []
    for seg in range(segments):
        for own in range(owners):
            target = (seg + hop) % segments * owners + (own ^ flips[own % 2])
            pairs.append((seg * owners + own, target))
    return lax.ppermute(value, ("segment", "expert"), pairs)


def upper_flips(owners):
    return [(1 << place,) * 2 for place in range(owners.bit_length() - 2, 2, -1)]


CORE = (1, 1)
SQUARE = ((4, 2), (2, 4), (6, 6))
STAY = (0, 0)


def spans(dim):
    return [slice(start, min(start + CHUNK, dim)) for start in range(0, dim, CHUNK)]


def call(kernel, outs, *args, **more):
    return pl.pallas_call(
        kernel,
        out_shape=[jax.ShapeDtypeStruct(shape, jnp.bfloat16) for shape in outs],
        in_specs=more.pop("in_specs", [VMEM] * len(args)),
        out_specs=[VMEM] * len(outs),
        compiler_params=pltpu.CompilerParams(vmem_limit_bytes=VMEM_LIMIT),
        **more,
    )(*args)


def load_kernel(count, *refs):
    sems = refs[-1]
    copies = [pltpu.make_async_copy(refs[place], refs[count + place], sems.at[place]) for place in range(count)]
    for copy in copies:
        copy.start()
    for copy in copies:
        copy.wait()


def load(*weights):
    count = len(weights)
    return pl.pallas_call(
        functools.partial(load_kernel, count),
        out_shape=[pltpu.VMEM(w.shape, w.dtype) for w in weights],
        in_specs=[pl.BlockSpec(memory_space=pltpu.HBM)] * count,
        out_specs=[VMEM] * count,
        scratch_shapes=[pltpu.SemaphoreType.DMA((count,))],
        compiler_params=pltpu.CompilerParams(vmem_limit_bytes=VMEM_LIMIT),
        cost_estimate=pl.CostEstimate(
            flops=0, bytes_accessed=sum(2 * w.size for w in weights), transcendentals=0
        ),
    )(*[pltpu.with_memory_space_constraint(w, pltpu.HBM) for w in weights])


def normalise(raw_ref, gain_ref, out_ref):
    rows, dim = raw_ref.shape[0], gain_ref.shape[1]
    square = jnp.zeros((rows, LANES), jnp.float32)
    for start in range(0, dim, LANES):
        piece = raw_ref[:, start:start + LANES].astype(jnp.float32)
        square += piece * piece
    inv = lax.rsqrt(jnp.sum(square, axis=1, keepdims=True) / dim + 1e-06)
    for span in spans(dim):
        scaled = raw_ref[:, span].astype(jnp.float32) * inv * gain_ref[:, span]
        out_ref[:, span] = scaled.astype(jnp.bfloat16)


def prepare_kernel(experts, states_hbm, routing_hbm, weight_hbm, gain_hbm, raw_ref, out_ref, gain_ref,
                   states_ref, routing_ref, weight_ref, sems):
    pairs = ((routing_hbm, routing_ref), (weight_hbm, weight_ref), (states_hbm, states_ref), (gain_hbm, gain_ref))
    copies = [pltpu.make_async_copy(source, target, sems.at[place]) for place, (source, target) in enumerate(pairs)]
    for copy in copies:
        copy.start()
    for copy in copies:
        copy.wait()
    rows, dim = states_ref.shape[1:]
    for span in spans(dim):
        raw_ref[:, span] = states_ref[0, :, span]
    lane = lax.broadcasted_iota(jnp.int32, (rows, LANES), 1).astype(jnp.float32)
    diagonal = lax.broadcasted_iota(jnp.int32, (rows, rows), 0) == lax.broadcasted_iota(jnp.int32, (rows, rows), 1)

    def upright(line):
        return jnp.sum(jnp.where(diagonal, line.astype(jnp.float32), 0.0), axis=1, keepdims=True)

    total = jnp.zeros((rows, LANES), jnp.float32)
    for step in range(routing_ref.shape[1]):
        for k in range(routing_ref.shape[2]):
            column = upright(routing_ref[0, step, k:k + 1, :]) + step * experts
            total += jnp.where(lane == column, upright(weight_ref[0, step, k:k + 1, :]), 0.0)
    raw_ref[:, dim:] = total.astype(jnp.bfloat16)
    out_ref[:, dim:] = total.astype(jnp.bfloat16)
    normalise(raw_ref, gain_ref, out_ref)


def prepare(experts, states, routing, weight, gain):
    args = [states, jnp.swapaxes(routing, 2, 3), jnp.swapaxes(weight, 2, 3), gain]
    rows, dim = states.shape[1:]
    block = jax.ShapeDtypeStruct((rows, dim + LANES), jnp.bfloat16)
    return pl.pallas_call(
        functools.partial(prepare_kernel, experts),
        out_shape=[block, block, pltpu.VMEM(gain.shape, gain.dtype)],
        in_specs=[pl.BlockSpec(memory_space=pltpu.HBM)] * 4,
        out_specs=[VMEM] * 3,
        scratch_shapes=[pltpu.VMEM(x.shape, x.dtype) for x in args[:3]] + [pltpu.SemaphoreType.DMA((4,))],
        compiler_params=pltpu.CompilerParams(vmem_limit_bytes=VMEM_LIMIT),
    )(*[pltpu.with_memory_space_constraint(x, pltpu.HBM) for x in args])


def join_kernel(*refs):
    *parts, out_ref = refs
    for span in spans(out_ref.shape[1]):
        rows = [part[:, span].astype(jnp.float32) for part in parts]
        out_ref[:, span] = jnp.concatenate(rows, axis=0).astype(jnp.bfloat16)


def add_kernel(*refs):
    *parts, out_ref = refs
    for span in spans(out_ref.shape[1]):
        out_ref[:, span] = sum(part[:, span].astype(jnp.float32) for part in parts).astype(jnp.bfloat16)


def split_kernel(count, *refs):
    parts, outs = refs[:-count], refs[-count:]
    rows = outs[0].shape[0]
    for span in spans(outs[0].shape[1]):
        total = sum(part[:, span].astype(jnp.float32) for part in parts)
        for place, out_ref in enumerate(outs):
            out_ref[:, span] = total[place * rows:(place + 1) * rows].astype(jnp.bfloat16)


def second_kernel(own_ref, far_ref, gain_ref, out_ref, raw_ref):
    dim = raw_ref.shape[1]
    for span in spans(dim):
        rows = [ref[:, span].astype(jnp.float32) for ref in (own_ref, far_ref)]
        raw_ref[:, span] = jnp.concatenate(rows, axis=0).astype(jnp.bfloat16)
    out_ref[:, dim:] = far_ref[:, dim:]
    normalise(far_ref, gain_ref, out_ref)


def meet_kernel(rest_ref, near_ref, far_ref, gain_ref, out_ref, raw_ref, own_ref):
    half = own_ref.shape[0]
    for span in spans(out_ref.shape[1]):
        far = far_ref[:, span].astype(jnp.float32)
        total = rest_ref[:, span].astype(jnp.float32) + near_ref[:, span].astype(jnp.float32)
        total = (total + jnp.concatenate([far[half:], far[:half]], axis=0)).astype(jnp.bfloat16)
        raw_ref[:, span] = total
        own_ref[:, span] = total[:half]
    normalise(raw_ref, gain_ref, out_ref)


def mlp_kernel(step_no, count, order, *refs):
    x_refs, refs = refs[:count], refs[count:]
    if step_no > 0:
        tail_ref, refs = refs[0], refs[1:]
    (gate_ref, up_ref, down_ref), outs, refs = refs[:3], refs[3:11], refs[11:]
    part = outs[0].shape[0]
    dim, hidden = gate_ref.shape[1:]
    experts = lax.axis_size("expert") // GROUP
    column = step_no * experts + lax.axis_index("expert") // GROUP
    def stack(span):
        values = [ref[:, span].astype(jnp.float32) for ref in x_refs]
        return jnp.concatenate([values[place][start:stop] for place, start, stop in order], axis=0)

    if step_no == 0:
        tails = stack(slice(dim, dim + LANES))
        refs[0][...] = tails.astype(jnp.bfloat16)
    else:
        tails = tail_ref[...].astype(jnp.float32)
    lane = lax.broadcasted_iota(jnp.int32, tails.shape, 1)
    weights = jnp.sum(jnp.where(lane == column, tails, 0.0), axis=1, keepdims=True)
    gated = jnp.zeros((8 * part, hidden), jnp.float32)
    up_part = jnp.zeros((8 * part, hidden), jnp.float32)
    for span in spans(dim):
        rows = stack(span).astype(jnp.bfloat16)
        gated += jnp.dot(rows, gate_ref[0, span, :], preferred_element_type=jnp.float32)
        up_part += jnp.dot(rows, up_ref[0, span, :], preferred_element_type=jnp.float32)
    inner = (gated / (1.0 + jnp.exp(-gated)) * up_part).astype(jnp.bfloat16)
    for span in spans(dim):
        terms = jnp.dot(inner, down_ref[0, :, span], preferred_element_type=jnp.float32)
        chosen = jnp.where(weights > 0.0, weights * terms, 0.0)
        for place, out_ref in enumerate(outs):
            out_ref[:, span] = chosen[place * part:(place + 1) * part].astype(jnp.bfloat16)


def mlp(step_no, xs, order, tail, gate, up, down):
    dim, hidden = gate.shape[1:]
    part = sum(x.shape[0] for x in xs) // 8
    gate, up, down = [pltpu.with_memory_space_constraint(w, pltpu.VMEM) for w in (gate, up, down)]
    first = step_no == 0
    args = list(xs) + ([] if first else [tail]) + [gate, up, down]
    result = call(
        functools.partial(mlp_kernel, step_no, len(xs), order), [(part, dim)] * 8 + [(8 * part, LANES)] * first, *args,
        cost_estimate=pl.CostEstimate(
            flops=48 * part * dim * hidden, bytes_accessed=6 * dim * hidden, transcendentals=0
        ),
    )
    return result[:8], result[8] if first else tail


def add(*parts):
    rows = parts[0].shape[0]
    dim = parts[-1].shape[1]
    return call(add_kernel, [(rows, dim)], *parts)[0]


def split(*parts):
    rows, dim = parts[0].shape
    return call(functools.partial(split_kernel, 2), [(rows // 2, dim)] * 2, *parts)


def join(*parts):
    return call(join_kernel, [(sum(part.shape[0] for part in parts), parts[0].shape[1])], *parts)[0]


def square(rows):
    return [rows] + [exchange(rows, flips, 0) for flips in SQUARE]


def both_cores(mine):
    xs = mine + [exchange(rows, CORE, 0) for rows in mine]
    return xs, [(place, 0, rows.shape[0]) for place, rows in enumerate(xs)]


def on_device(states, routing, route_weight, norm_gain, gate_proj, up_proj, down_proj):
    owners = lax.axis_size("expert")
    row_dev, dim = states.shape[1:]
    passes_count = routing.shape[1]
    top, *middle = upper_flips(owners)

    raw, pair, gain = prepare(owners // GROUP, states, routing, route_weight, norm_gain)
    gain = pltpu.with_memory_space_constraint(gain, pltpu.VMEM)
    other = exchange(raw, top, 0)
    (gate,) = load(gate_proj)
    firsts = square(pair)
    other, gate, firsts = lax.optimization_barrier((other, gate, firsts))
    pair, raw = call(second_kernel, [pair.shape, (2 * row_dev, dim)], raw, other, gain)
    pair, up_hbm, down_hbm = lax.optimization_barrier((pair, up_proj, down_proj))
    up, down = load(up_hbm, down_hbm)
    seconds = square(pair)
    seconds[3], up, down = lax.optimization_barrier((seconds[3], up, down))
    weights = (gate, up, down)
    if middle:
        rows_a = join(firsts[0], seconds[0])
        for flips in middle:
            rows_a = join(rows_a, exchange(rows_a, flips, 0))
        xs, order = both_cores(square(rows_a))
    else:
        far = exchange(join(*firsts), CORE, 0)
        xs = firsts + seconds + [far] + [exchange(rows, CORE, 0) for rows in seconds]
        order = [(place + late, 0, row_dev) for place in range(4) for late in (0, 4)]
        for place in range(4):
            order += [(8, place * row_dev, (place + 1) * row_dev), (9 + place, 0, row_dev)]
    own, tail = states[0], None
    for step_no in range(passes_count):
        outs, tail = mlp(step_no, xs, order, tail, *weights)

        kept, sent = outs[:4], [exchange(rows, CORE, 0) for rows in outs[4:]]
        parts = [kept[0], sent[0]]
        for place in (3, 2, 1):
            parts.append(exchange(add(kept[place], sent[place]), SQUARE[place - 1], 0))
        for flips in middle[::-1]:
            low, high = split(*parts)
            parts = [low, exchange(high, flips, 0)]
        if step_no < passes_count - 1:
            total = add(*parts)
            rest = exchange(raw, STAY, 1)
            pair, raw, own = call(
                meet_kernel, [(2 * row_dev, dim), (2 * row_dev, dim), (row_dev, dim)],
                rest, exchange(total, STAY, 1), exchange(total, top, 1), gain,
            )
            for flips in middle:
                pair = join(pair, exchange(pair, flips, 0))
            xs, order = both_cores(square(pair))
        else:
            low, high = split(*parts)
            rest = exchange(own, STAY, 1)
            own = add(rest, exchange(high, top, 1), exchange(low, STAY, 1))
    return own[None]


def solution(mesh):
    return jax.shard_map(
        on_device,
        mesh=mesh,
        in_specs=(
            P("segment", "expert", None),
            P("segment", None, "expert", None),
            P("segment", None, "expert", None),
            P("segment", None),
            P("segment", None, "expert"),
            P("segment", None, "expert"),
            P("segment", "expert", None),
        ),
        out_specs=P("segment", "expert", None),
        check_vma=False,
    )
```

time: 72.1 us -> 73.9 us (1.025)
  starting transfers between devices: 29.6 us -> 32.6 us
  waiting for transfers between devices: 30.9 us -> 28.4 us
  Pallas kernels: 11.3 us -> 12.5 us
    ppermute x35 -> x39, starting transfers between devices: 29.6 us -> 32.6 us  [exchange(): return lax.ppermute(value, ('segment', 'expert'), pairs)]
    ppermute x35 -> x39, waiting for transfers between devices: 30.9 us -> 28.4 us  [exchange(): return lax.ppermute(value, ('segment', 'expert'), pairs)]
    pallas_call x1 -> x3, Pallas kernels: 4.23 us -> 6.29 us  [the longest x2 5.22 us: load(): pl.pallas_call(functools.partial(load_kernel, count), out_shape=[pltpu.VM...]
    pallas_call x14, Pallas kernels: 7.11 us -> 6.23 us  [call(): pl.pallas_call(kernel, out_shape=[jax.ShapeDtypeStruct(shape, jnp.bfloat1...]
  transfers between devices with their start and end apart: 35 -> 39, of which waited for: 16 -> 21; matrix products, arithmetic and copies ran while one was open for 0% -> 0% of each run, Pallas kernels for 6% -> 8%
where the time goes in v12:
time: 73.9 us; the launch traced here: 73.7 us
  starting transfers between devices  32.6 us (44%)
  waiting for transfers between devices  28.4 us (38%)
  Pallas kernels  12.5 us (17%)
    ppermute x39, starting transfers between devices, exchange(): return lax.ppermute(value, ('segment', 'expert'), pairs)  32.6 us
    ppermute x39, waiting for transfers between devices, exchange(): return lax.ppermute(value, ('segment', 'expert'), pairs)  28.4 us
    pallas_call x14, Pallas kernels, call(): pl.pallas_call(kernel, out_shape=[jax.ShapeDtypeStruct(shape, jnp.bfloat1...  6.23 us
    pallas_call x2, Pallas kernels, load(): pl.pallas_call(functools.partial(load_kernel, count), out_shape=[pltpu.VM...  5.22 us
  transfers between devices with their start and end apart: 39, of which 21 were waited for; matrix products, arithmetic and copies ran while one was open for 0% of the time, Pallas kernels for 8%

profile of v12, /device:TPU:0, one launch (start us, length us, event | category | flops | bytes accessed | tf_op | source)
XLA Modules:
  0.0 73.7 jit_solution(14728267153350744651)
XLA Ops:
  0.0 1.1 %shard_map.73 = (bf16[4,7296]{1,0:T(4,128)(2,1)S(1)}, bf16[4,7296]{1,0:T(4,128)(2,1)S(1)}, f32[1,7168]{1,0:T(1,128)S(1)}) custom-call(bf16[1,4,7168]{2,1,0:T(4,128)(2,1)} %states_hbm.1, s32[1,2,2,4]{3,2,1,0:T(2,128)} %bitcast.3, bf16[1,2,2,4]{3,2,1,0:T(2,128)(2,1)} %bitcast.4, f32[1,7168]{1,0:T(1,128)} %gain_hbm.1), custom_call_target="tpu_custom_call" | custom-call | tf_op jit(solution)/shard_map/pallas_call | solution.py:120
  1.1 4.1 %collective-permute-start = (bf16[4,7296]{1,0:T(4,128)(2,1)S(1)}, bf16[4,7296]{1,0:T(4,128)(2,1)S(1)}, u32[]{:S(2)}, u32[]{:S(2)}) collective-permute-start(bf16[4,7296]{1,0:T(4,128)(2,1)S(1)} %get-tuple-element.45.own_ref), channel_id=1, source_target_pairs={{0,8},{1,9},{2,10},{3,11},{4,12},{5,13},{6,14},{7,15},{8,0},{9,1},... | collective-permute-start | bytes 175112 | tf_op jit(solution)/shard_map/ppermute | solution.py:26
  5.2 2.5 %collective-permute-start.3 = (bf16[4,7296]{1,0:T(4,128)(2,1)S(1)}, bf16[4,7296]{1,0:T(4,128)(2,1)S(1)}, u32[]{:S(2)}, u32[]{:S(2)}) collective-permute-start(bf16[4,7296]{1,0:T(4,128)(2,1)S(1)} %get-tuple-element.50.refs_0_), channel_id=1, source_target_pairs={{0,6},{1,7},{2,4},{3,5},{4,2},{5,3},{6,0},{7,1},{8,14},{9,15},{10,... | collective-permute-start | bytes 175112 | tf_op jit(solution)/shard_map/ppermute | solution.py:26
  7.7 0.5 collective-permute-start.2
  8.2 0.4 collective-permute-start.1
  8.7 2.0 %shard_map.74.refs_13_.refs_9_ = bf16[1,7168,256]{2,1,0:T(8,128)(2,1)S(1)} custom-call(bf16[1,7168,256]{2,1,0:T(8,128)(2,1)} %refs_0_.1), custom_call_target="tpu_custom_call" | custom-call | bytes 3670016 | tf_op jit(solution)/shard_map/pallas_call | solution.py:64
  10.7 0.1 collective-permute-done.3.refs_3_
  10.9 1.0 %collective-permute-done.2.refs_2_ = bf16[4,7296]{1,0:T(4,128)(2,1)S(1)} collective-permute-done((bf16[4,7296]{1,0:T(4,128)(2,1)S(1)}, bf16[4,7296]{1,0:T(4,128)(2,1)S(1)}, u32[]{:S(2)}, u32[]{:S(2)}) %collective-permute-start.2) | collective-permute-done | bytes 58400 | tf_op jit(solution)/shard_map/ppermute | solution.py:26
  11.9 0.5 collective-permute-done.1.refs_1_
  12.5 0.2 shard_map.75
  12.8 1.5 %collective-permute-start.7 = (bf16[4,7296]{1,0:T(4,128)(2,1)S(1)}, bf16[4,7296]{1,0:T(4,128)(2,1)S(1)}, u32[]{:S(2)}, u32[]{:S(2)}) collective-permute-start(bf16[4,7296]{1,0:T(4,128)(2,1)S(1)} %get-tuple-element.55.refs_4_), channel_id=1, source_target_pairs={{0,6},{1,7},{2,4},{3,5},{4,2},{5,3},{6,0},{7,1},{8,14},{9,15},{10,... | collective-permute-start | bytes 175112 | tf_op jit(solution)/shard_map/ppermute | solution.py:26
  14.2 0.8 %collective-permute-start.6 = (bf16[4,7296]{1,0:T(4,128)(2,1)S(1)}, bf16[4,7296]{1,0:T(4,128)(2,1)S(1)}, u32[]{:S(2)}, u32[]{:S(2)}) collective-permute-start(bf16[4,7296]{1,0:T(4,128)(2,1)S(1)} %get-tuple-element.55.refs_4_), channel_id=1, source_target_pairs={{0,2},{1,5},{2,0},{3,7},{4,6},{5,1},{6,4},{7,3},{8,10},{9,13},{10,... | collective-permute-start | bytes 175112 | tf_op jit(solution)/shard_map/ppermute | solution.py:26
  15.1 1.3 %collective-permute-start.5 = (bf16[4,7296]{1,0:T(4,128)(2,1)S(1)}, bf16[4,7296]{1,0:T(4,128)(2,1)S(1)}, u32[]{:S(2)}, u32[]{:S(2)}) collective-permute-start(bf16[4,7296]{1,0:T(4,128)(2,1)S(1)} %get-tuple-element.55.refs_4_), channel_id=1, source_target_pairs={{0,4},{1,3},{2,6},{3,1},{4,0},{5,7},{6,2},{7,5},{8,12},{9,11},{10,... | collective-permute-start | bytes 175112 | tf_op jit(solution)/shard_map/ppermute | solution.py:26
  16.3 3.2 %shard_map.76 = (bf16[1,7168,256]{2,1,0:T(8,128)(2,1)S(1)}, bf16[1,256,7168]{2,1,0:T(8,128)(2,1)S(1)}) custom-call(bf16[1,7168,256]{2,1,0:T(8,128)(2,1)} %refs_0_.2, bf16[1,256,7168]{2,1,0:T(8,128)(2,1)} %refs_1_), custom_call_target="tpu_custom_call" | custom-call | bytes 7340032 | tf_op jit(solution)/shard_map/pallas_call | solution.py:64
  19.5 0.6 collective-permute-start.11
  20.1 0.1 collective-permute-start.10
  20.2 0.4 collective-permute-start.12
  20.6 0.4 collective-permute-done.11.refs_11_
  21.0 0.4 collective-permute-done.10.refs_10_
  21.3 0.2 collective-permute-done.12.refs_12_
  21.5 2.1 %shard_map.78 = (bf16[8,7168]{1,0:T(8,128)(2,1)S(1)}, bf16[8,7168]{1,0:T(8,128)(2,1)S(1)}, bf16[8,7168]{1,0:T(8,128)(2,1)S(1)}, bf16[8,7168]{1,0:T(8,128)(2,1)S(...) custom-call(bf16[4,7296]{1,0:T(4,128)(2,1)S(1)} %get-tuple-element.5, ...), custom_call_target="tpu_custom_call" | custom-call | flops 704643072 | bytes 11010048 | tf_op jit(solution)/shard_map/pallas_call | solution.py:43
  23.6 0.4 collective-permute-start.14
  24.1 0.2 collective-permute-start.16
  24.2 0.3 collective-permute-start.18
  24.6 0.2 collective-permute-start.13
  24.7 0.3 collective-permute-done.14.refs_1_
  25.1 1.5 %collective-permute-start.15 = (bf16[8,7168]{1,0:T(8,128)(2,1)S(1)}, bf16[8,7168]{1,0:T(8,128)(2,1)S(1)}, u32[]{:S(2)}, u32[]{:S(2)}) collective-permute-start(bf16[8,7168]{1,0:T(8,128)(2,1)S(1)} %shard_map.79), channel_id=1, source_target_pairs={{0,6},{1,7},{2,4},{3,5},{4,2},{5,3},{6,0},{7,1},{8,14},{9,15},{10,... | collective-permute-start | bytes 344072 | tf_op jit(solution)/shard_map/ppermute | solution.py:26
  26.6 0.9 %collective-permute-start.17 = (bf16[8,7168]{1,0:T(8,128)(2,1)S(1)}, bf16[8,7168]{1,0:T(8,128)(2,1)S(1)}, u32[]{:S(2)}, u32[]{:S(2)}) collective-permute-start(bf16[8,7168]{1,0:T(8,128)(2,1)S(1)} %shard_map.80), channel_id=1, source_target_pairs={{0,2},{1,5},{2,0},{3,7},{4,6},{5,1},{6,4},{7,3},{8,10},{9,13},{10,... | collective-permute-start | bytes 344072 | tf_op jit(solution)/shard_map/ppermute | solution.py:26
  27.5 1.3 %collective-permute-start.19 = (bf16[8,7168]{1,0:T(8,128)(2,1)S(1)}, bf16[8,7168]{1,0:T(8,128)(2,1)S(1)}, u32[]{:S(2)}, u32[]{:S(2)}) collective-permute-start(bf16[8,7168]{1,0:T(8,128)(2,1)S(1)} %shard_map.81), channel_id=1, source_target_pairs={{0,4},{1,3},{2,6},{3,1},{4,0},{5,7},{6,2},{7,5},{8,12},{9,11},{10,... | collective-permute-start | bytes 344072 | tf_op jit(solution)/shard_map/ppermute | solution.py:26
  28.8 1.5 %collective-permute-start.4 = (bf16[8,7168]{1,0:T(8,128)(2,1)S(1)}, bf16[8,7168]{1,0:T(8,128)(2,1)S(1)}, u32[]{:S(2)}, u32[]{:S(2)}) collective-permute-start(bf16[8,7168]{1,0:T(8,128)(2,1)S(1)} %get-tuple-element.49), channel_id=1, source_target_pairs={{0,16},{1,17},{2,18},{3,19},{4,20},{5,21},{6,22},{7,23},{8,24},{9,... | collective-permute-start | bytes 344072 | tf_op jit(solution)/shard_map/ppermute | solution.py:26
  30.3 1.7 %collective-permute-done.15.refs_2_ = bf16[8,7168]{1,0:T(8,128)(2,1)S(1)} collective-permute-done((bf16[8,7168]{1,0:T(8,128)(2,1)S(1)}, bf16[8,7168]{1,0:T(8,128)(2,1)S(1)}, u32[]{:S(2)}, u32[]{:S(2)}) %collective-permute-start.15) | collective-permute-done | bytes 114720 | tf_op jit(solution)/shard_map/ppermute | solution.py:26
  32.0 1.8 %collective-permute-done.17.refs_3_ = bf16[8,7168]{1,0:T(8,128)(2,1)S(1)} collective-permute-done((bf16[8,7168]{1,0:T(8,128)(2,1)S(1)}, bf16[8,7168]{1,0:T(8,128)(2,1)S(1)}, u32[]{:S(2)}, u32[]{:S(2)}) %collective-permute-start.17) | collective-permute-done | bytes 114720 | tf_op jit(solution)/shard_map/ppermute | solution.py:26
  33.8 0.1 collective-permute-done.19.refs_4_
  34.0 1.3 %collective-permute-start.21 = (bf16[8,7168]{1,0:T(8,128)(2,1)S(1)}, bf16[8,7168]{1,0:T(8,128)(2,1)S(1)}, u32[]{:S(2)}, u32[]{:S(2)}) collective-permute-start(bf16[8,7168]{1,0:T(8,128)(2,1)S(1)} %shard_map.82), channel_id=1, source_target_pairs={{0,24},{1,25},{2,26},{3,27},{4,28},{5,29},{6,30},{7,31},{8,16},{9,... | collective-permute-start | bytes 344072 | tf_op jit(solution)/shard_map/ppermute | solution.py:26
  35.4 0.5 collective-permute-start.20
  35.9 7.6 %collective-permute-done.21.far_ref = bf16[8,7168]{1,0:T(8,128)(2,1)S(1)} collective-permute-done((bf16[8,7168]{1,0:T(8,128)(2,1)S(1)}, bf16[8,7168]{1,0:T(8,128)(2,1)S(1)}, u32[]{:S(2)}, u32[]{:S(2)}) %collective-permute-start.21) | collective-permute-done | bytes 114720 | tf_op jit(solution)/shard_map/ppermute | solution.py:26
  43.5 0.7 shard_map.83
  44.2 0.7 collective-permute-start.25
  44.8 1.1 %collective-permute-start.24 = (bf16[8,7168]{1,0:T(8,128)(2,1)S(1)}, bf16[8,7168]{1,0:T(8,128)(2,1)S(1)}, u32[]{:S(2)}, u32[]{:S(2)}) collective-permute-start(bf16[8,7168]{1,0:T(8,128)(2,1)S(1)} %get-tuple-element.73.refs_0_), channel_id=1, source_target_pairs={{0,2},{1,5},{2,0},{3,7},{4,6},{5,1},{6,4},{7,3},{8,10},{9,13},{10,... | collective-permute-start | bytes 344072 | tf_op jit(solution)/shard_map/ppermute | solution.py:26
  46.0 1.7 %collective-permute-start.23 = (bf16[8,7168]{1,0:T(8,128)(2,1)S(1)}, bf16[8,7168]{1,0:T(8,128)(2,1)S(1)}, u32[]{:S(2)}, u32[]{:S(2)}) collective-permute-start(bf16[8,7168]{1,0:T(8,128)(2,1)S(1)} %get-tuple-element.73.refs_0_), channel_id=1, source_target_pairs={{0,4},{1,3},{2,6},{3,1},{4,0},{5,7},{6,2},{7,5},{8,12},{9,11},{10,... | collective-permute-start | bytes 344072 | tf_op jit(solution)/shard_map/ppermute | solution.py:26
  47.7 3.4 %collective-permute-done.25.refs_3_ = bf16[8,7168]{1,0:T(8,128)(2,1)S(1)} collective-permute-done((bf16[8,7168]{1,0:T(8,128)(2,1)S(1)}, bf16[8,7168]{1,0:T(8,128)(2,1)S(1)}, u32[]{:S(2)}, u32[]{:S(2)}) %collective-permute-start.25) | collective-permute-done | bytes 114720 | tf_op jit(solution)/shard_map/ppermute | solution.py:26
  51.1 1.3 %collective-permute-done.24.refs_2_ = bf16[8,7168]{1,0:T(8,128)(2,1)S(1)} collective-permute-done((bf16[8,7168]{1,0:T(8,128)(2,1)S(1)}, bf16[8,7168]{1,0:T(8,128)(2,1)S(1)}, u32[]{:S(2)}, u32[]{:S(2)}) %collective-permute-start.24) | collective-permute-done | bytes 114720 | tf_op jit(solution)/shard_map/ppermute | solution.py:26
  52.4 0.1 collective-permute-done.23.refs_1_
  52.5 0.4 collective-permute-start.27
  52.9 0.8 %collective-permute-done.28.refs_6_ = bf16[8,7168]{1,0:T(8,128)(2,1)S(1)} collective-permute-done((bf16[8,7168]{1,0:T(8,128)(2,1)S(1)}, bf16[8,7168]{1,0:T(8,128)(2,1)S(1)}, u32[]{:S(2)}, u32[]{:S(2)}) %collective-permute-start.28) | collective-permute-done | bytes 114720 | tf_op jit(solution)/shard_map/ppermute | solution.py:26
  53.7 0.2 collective-permute-done.27.refs_5_
  53.9 2.1 %shard_map.84 = (bf16[8,7168]{1,0:T(8,128)(2,1)S(1)}, bf16[8,7168]{1,0:T(8,128)(2,1)S(1)}, bf16[8,7168]{1,0:T(8,128)(2,1)S(1)}, bf16[8,7168]{1,0:T(8,128)(2,1)S(...) custom-call(bf16[8,7168]{1,0:T(8,128)(2,1)S(1)} %get-tuple-element.7, ...), custom_call_target="tpu_custom_call" | custom-call | flops 704643072 | bytes 11010048 | tf_op jit(solution)/shard_map/pallas_call | solution.py:43
  56.0 0.4 collective-permute-start.31
  56.4 0.2 collective-permute-start.33
  56.6 0.3 collective-permute-start.35
  56.9 0.2 collective-permute-start.30
  57.1 0.3 collective-permute-done.31.refs_1_
  57.4 0.8 %collective-permute-start.32 = (bf16[8,7168]{1,0:T(8,128)(2,1)S(1)}, bf16[8,7168]{1,0:T(8,128)(2,1)S(1)}, u32[]{:S(2)}, u32[]{:S(2)}) collective-permute-start(bf16[8,7168]{1,0:T(8,128)(2,1)S(1)} %shard_map.85), channel_id=1, source_target_pairs={{0,6},{1,7},{2,4},{3,5},{4,2},{5,3},{6,0},{7,1},{8,14},{9,15},{10,... | collective-permute-start | bytes 344072 | tf_op jit(solution)/shard_map/ppermute | solution.py:26
  58.3 1.3 %collective-permute-start.34 = (bf16[8,7168]{1,0:T(8,128)(2,1)S(1)}, bf16[8,7168]{1,0:T(8,128)(2,1)S(1)}, u32[]{:S(2)}, u32[]{:S(2)}) collective-permute-start(bf16[8,7168]{1,0:T(8,128)(2,1)S(1)} %shard_map.86), channel_id=1, source_target_pairs={{0,2},{1,5},{2,0},{3,7},{4,6},{5,1},{6,4},{7,3},{8,10},{9,13},{10,... | collective-permute-start | bytes 344072 | tf_op jit(solution)/shard_map/ppermute | solution.py:26
  59.6 1.6 %collective-permute-start.36 = (bf16[8,7168]{1,0:T(8,128)(2,1)S(1)}, bf16[8,7168]{1,0:T(8,128)(2,1)S(1)}, u32[]{:S(2)}, u32[]{:S(2)}) collective-permute-start(bf16[8,7168]{1,0:T(8,128)(2,1)S(1)} %shard_map.87), channel_id=1, source_target_pairs={{0,4},{1,3},{2,6},{3,1},{4,0},{5,7},{6,2},{7,5},{8,12},{9,11},{10,... | collective-permute-start | bytes 344072 | tf_op jit(solution)/shard_map/ppermute | solution.py:26
  61.2 1.5 %collective-permute-start.22 = (bf16[4,7168]{1,0:T(4,128)(2,1)S(1)}, bf16[4,7168]{1,0:T(4,128)(2,1)S(1)}, u32[]{:S(2)}, u32[]{:S(2)}) collective-permute-start(bf16[4,7168]{1,0:T(4,128)(2,1)S(1)} %get-tuple-element.72), channel_id=1, source_target_pairs={{0,16},{1,17},{2,18},{3,19},{4,20},{5,21},{6,22},{7,23},{8,24},{9,... | collective-permute-start | bytes 172040 | tf_op jit(solution)/shard_map/ppermute | solution.py:26
  62.7 1.7 %collective-permute-done.32.refs_2_ = bf16[8,7168]{1,0:T(8,128)(2,1)S(1)} collective-permute-done((bf16[8,7168]{1,0:T(8,128)(2,1)S(1)}, bf16[8,7168]{1,0:T(8,128)(2,1)S(1)}, u32[]{:S(2)}, u32[]{:S(2)}) %collective-permute-start.32) | collective-permute-done | bytes 114720 | tf_op jit(solution)/shard_map/ppermute | solution.py:26
  64.4 1.8 %collective-permute-done.34.refs_3_ = bf16[8,7168]{1,0:T(8,128)(2,1)S(1)} collective-permute-done((bf16[8,7168]{1,0:T(8,128)(2,1)S(1)}, bf16[8,7168]{1,0:T(8,128)(2,1)S(1)}, u32[]{:S(2)}, u32[]{:S(2)}) %collective-permute-start.34) | collective-permute-done | bytes 114720 | tf_op jit(solution)/shard_map/ppermute | solution.py:26
  66.2 0.3 collective-permute-done.36.refs_4_
  66.4 0.1 shard_map.88
  66.5 1.5 %collective-permute-start.37 = (bf16[4,7168]{1,0:T(4,128)(2,1)S(1)}, bf16[4,7168]{1,0:T(4,128)(2,1)S(1)}, u32[]{:S(2)}, u32[]{:S(2)}) collective-permute-start(bf16[4,7168]{1,0:T(4,128)(2,1)S(1)} %get-tuple-element.83), channel_id=1, source_target_pairs={{0,24},{1,25},{2,26},{3,27},{4,28},{5,29},{6,30},{7,31},{8,16},{9,... | collective-permute-start | bytes 172040 | tf_op jit(solution)/shard_map/ppermute | solution.py:26
  68.0 0.5 collective-permute-start.38
  68.6 4.4 %collective-permute-done.37.refs_1_ = bf16[4,7168]{1,0:T(4,128)(2,1)S(1)} collective-permute-done((bf16[4,7168]{1,0:T(4,128)(2,1)S(1)}, bf16[4,7168]{1,0:T(4,128)(2,1)S(1)}, u32[]{:S(2)}, u32[]{:S(2)}) %collective-permute-start.37) | collective-permute-done | bytes 57376 | tf_op jit(solution)/shard_map/ppermute | solution.py:26
  73.0 0.7 shard_map.89
  (31 shorter events, 0.4 us)
Async XLA Ops:
  1.1 9.6 %collective-permute-start = (bf16[4,7296]{1,0:T(4,128)(2,1)S(1)}, bf16[4,7296]{1,0:T(4,128)(2,1)S(1)}, u32[]{:S(2)}, u32[]{:S(2)}) collective-permute-start(bf16[4,7296]{1,0:T(4,128)(2,1)S(1)} %get-tuple-element.45.own_ref), channel_id=1, source_target_pairs={{0,8},{1,9},{2,10},{3,11},{4,12},{5,13},{6,14},{7,15},{8,0},{9,1},... | collective-permute-start | bytes 175112 | tf_op jit(solution)/shard_map/ppermute | solution.py:26
  5.2 5.7 %collective-permute-start.3 = (bf16[4,7296]{1,0:T(4,128)(2,1)S(1)}, bf16[4,7296]{1,0:T(4,128)(2,1)S(1)}, u32[]{:S(2)}, u32[]{:S(2)}) collective-permute-start(bf16[4,7296]{1,0:T(4,128)(2,1)S(1)} %get-tuple-element.50.refs_0_), channel_id=1, source_target_pairs={{0,6},{1,7},{2,4},{3,5},{4,2},{5,3},{6,0},{7,1},{8,14},{9,15},{10,... | collective-permute-start | bytes 175112 | tf_op jit(solution)/shard_map/ppermute | solution.py:26
  7.7 4.2 %collective-permute-start.2 = (bf16[4,7296]{1,0:T(4,128)(2,1)S(1)}, bf16[4,7296]{1,0:T(4,128)(2,1)S(1)}, u32[]{:S(2)}, u32[]{:S(2)}) collective-permute-start(bf16[4,7296]{1,0:T(4,128)(2,1)S(1)} %get-tuple-element.50.refs_0_), channel_id=1, source_target_pairs={{0,2},{1,5},{2,0},{3,7},{4,6},{5,1},{6,4},{7,3},{8,10},{9,13},{10,... | collective-permute-start | bytes 175112 | tf_op jit(solution)/shard_map/ppermute | solution.py:26
  8.2 4.2 %collective-permute-start.1 = (bf16[4,7296]{1,0:T(4,128)(2,1)S(1)}, bf16[4,7296]{1,0:T(4,128)(2,1)S(1)}, u32[]{:S(2)}, u32[]{:S(2)}) collective-permute-start(bf16[4,7296]{1,0:T(4,128)(2,1)S(1)} %get-tuple-element.50.refs_0_), channel_id=1, source_target_pairs={{0,4},{1,3},{2,6},{3,1},{4,0},{5,7},{6,2},{7,5},{8,12},{9,11},{10,... | collective-permute-start | bytes 175112 | tf_op jit(solution)/shard_map/ppermute | solution.py:26
  12.5 9.0 %collective-permute-start.8 = (bf16[16,7296]{1,0:T(8,128)(2,1)S(1)}, bf16[16,7296]{1,0:T(8,128)(2,1)S(1)}, u32[]{:S(2)}, u32[]{:S(2)}) collective-permute-start(bf16[16,7296]{1,0:T(8,128)(2,1)S(1)} %shard_map.77), channel_id=1, source_target_pairs={{0,1},{1,0},{2,3},{3,2},{4,5},{5,4},{6,7},{7,6},{8,9},{9,8},{10,11... | collective-permute-start | bytes 700424 | tf_op jit(solution)/shard_map/ppermute | solution.py:26
  12.8 6.7 %collective-permute-start.7 = (bf16[4,7296]{1,0:T(4,128)(2,1)S(1)}, bf16[4,7296]{1,0:T(4,128)(2,1)S(1)}, u32[]{:S(2)}, u32[]{:S(2)}) collective-permute-start(bf16[4,7296]{1,0:T(4,128)(2,1)S(1)} %get-tuple-element.55.refs_4_), channel_id=1, source_target_pairs={{0,6},{1,7},{2,4},{3,5},{4,2},{5,3},{6,0},{7,1},{8,14},{9,15},{10,... | collective-permute-start | bytes 175112 | tf_op jit(solution)/shard_map/ppermute | solution.py:26
  14.2 5.3 %collective-permute-start.6 = (bf16[4,7296]{1,0:T(4,128)(2,1)S(1)}, bf16[4,7296]{1,0:T(4,128)(2,1)S(1)}, u32[]{:S(2)}, u32[]{:S(2)}) collective-permute-start(bf16[4,7296]{1,0:T(4,128)(2,1)S(1)} %get-tuple-element.55.refs_4_), channel_id=1, source_target_pairs={{0,2},{1,5},{2,0},{3,7},{4,6},{5,1},{6,4},{7,3},{8,10},{9,13},{10,... | collective-permute-start | bytes 175112 | tf_op jit(solution)/shard_map/ppermute | solution.py:26
  15.1 5.0 %collective-permute-start.5 = (bf16[4,7296]{1,0:T(4,128)(2,1)S(1)}, bf16[4,7296]{1,0:T(4,128)(2,1)S(1)}, u32[]{:S(2)}, u32[]{:S(2)}) collective-permute-start(bf16[4,7296]{1,0:T(4,128)(2,1)S(1)} %get-tuple-element.55.refs_4_), channel_id=1, source_target_pairs={{0,4},{1,3},{2,6},{3,1},{4,0},{5,7},{6,2},{7,5},{8,12},{9,11},{10,... | collective-permute-start | bytes 175112 | tf_op jit(solution)/shard_map/ppermute | solution.py:26
  16.3 4.3 %collective-permute-start.9 = (bf16[4,7296]{1,0:T(4,128)(2,1)S(1)}, bf16[4,7296]{1,0:T(4,128)(2,1)S(1)}, u32[]{:S(2)}, u32[]{:S(2)}) collective-permute-start(bf16[4,7296]{1,0:T(4,128)(2,1)S(1)} %get-tuple-element.55.refs_4_), channel_id=1, source_target_pairs={{0,1},{1,0},{2,3},{3,2},{4,5},{5,4},{6,7},{7,6},{8,9},{9,8},{10,11... | collective-permute-start | bytes 175112 | tf_op jit(solution)/shard_map/ppermute | solution.py:26
  19.5 1.5 %collective-permute-start.11 = (bf16[4,7296]{1,0:T(4,128)(2,1)S(1)}, bf16[4,7296]{1,0:T(4,128)(2,1)S(1)}, u32[]{:S(2)}, u32[]{:S(2)}) collective-permute-start(bf16[4,7296]{1,0:T(4,128)(2,1)S(1)} %collective-permute-done.6.refs_6_), channel_id=1, source_target_pairs={{0,1},{1,0},{2,3},{3,2},{4,5},{5,4},{6,7},{7,6},{8,9},{9,8},{10,11... | collective-permute-start | bytes 175112 | tf_op jit(solution)/shard_map/ppermute | solution.py:26
  20.1 1.2 %collective-permute-start.10 = (bf16[4,7296]{1,0:T(4,128)(2,1)S(1)}, bf16[4,7296]{1,0:T(4,128)(2,1)S(1)}, u32[]{:S(2)}, u32[]{:S(2)}) collective-permute-start(bf16[4,7296]{1,0:T(4,128)(2,1)S(1)} %collective-permute-done.5.refs_5_), channel_id=1, source_target_pairs={{0,1},{1,0},{2,3},{3,2},{4,5},{5,4},{6,7},{7,6},{8,9},{9,8},{10,11... | collective-permute-start | bytes 175112 | tf_op jit(solution)/shard_map/ppermute | solution.py:26
  20.2 1.3 %collective-permute-start.12 = (bf16[4,7296]{1,0:T(4,128)(2,1)S(1)}, bf16[4,7296]{1,0:T(4,128)(2,1)S(1)}, u32[]{:S(2)}, u32[]{:S(2)}) collective-permute-start(bf16[4,7296]{1,0:T(4,128)(2,1)S(1)} %collective-permute-done.7.refs_7_), channel_id=1, source_target_pairs={{0,1},{1,0},{2,3},{3,2},{4,5},{5,4},{6,7},{7,6},{8,9},{9,8},{10,11... | collective-permute-start | bytes 175112 | tf_op jit(solution)/shard_map/ppermute | solution.py:26
  23.6 1.4 %collective-permute-start.14 = (bf16[8,7168]{1,0:T(8,128)(2,1)S(1)}, bf16[8,7168]{1,0:T(8,128)(2,1)S(1)}, u32[]{:S(2)}, u32[]{:S(2)}) collective-permute-start(bf16[8,7168]{1,0:T(8,128)(2,1)S(1)} %get-tuple-element.67), channel_id=1, source_target_pairs={{0,1},{1,0},{2,3},{3,2},{4,5},{5,4},{6,7},{7,6},{8,9},{9,8},{10,11... | collective-permute-start | bytes 344072 | tf_op jit(solution)/shard_map/ppermute | solution.py:26
  24.1 2.5 %collective-permute-start.16 = (bf16[8,7168]{1,0:T(8,128)(2,1)S(1)}, bf16[8,7168]{1,0:T(8,128)(2,1)S(1)}, u32[]{:S(2)}, u32[]{:S(2)}) collective-permute-start(bf16[8,7168]{1,0:T(8,128)(2,1)S(1)} %get-tuple-element.69), channel_id=1, source_target_pairs={{0,1},{1,0},{2,3},{3,2},{4,5},{5,4},{6,7},{7,6},{8,9},{9,8},{10,11... | collective-permute-start | bytes 344072 | tf_op jit(solution)/shard_map/ppermute | solution.py:26
  24.2 3.2 %collective-permute-start.18 = (bf16[8,7168]{1,0:T(8,128)(2,1)S(1)}, bf16[8,7168]{1,0:T(8,128)(2,1)S(1)}, u32[]{:S(2)}, u32[]{:S(2)}) collective-permute-start(bf16[8,7168]{1,0:T(8,128)(2,1)S(1)} %get-tuple-element.71), channel_id=1, source_target_pairs={{0,1},{1,0},{2,3},{3,2},{4,5},{5,4},{6,7},{7,6},{8,9},{9,8},{10,11... | collective-permute-start | bytes 344072 | tf_op jit(solution)/shard_map/ppermute | solution.py:26
  24.6 5.7 %collective-permute-start.13 = (bf16[8,7168]{1,0:T(8,128)(2,1)S(1)}, bf16[8,7168]{1,0:T(8,128)(2,1)S(1)}, u32[]{:S(2)}, u32[]{:S(2)}) collective-permute-start(bf16[8,7168]{1,0:T(8,128)(2,1)S(1)} %get-tuple-element.65), channel_id=1, source_target_pairs={{0,1},{1,0},{2,3},{3,2},{4,5},{5,4},{6,7},{7,6},{8,9},{9,8},{10,11... | collective-permute-start | bytes 344072 | tf_op jit(solution)/shard_map/ppermute | solution.py:26
  25.1 6.9 %collective-permute-start.15 = (bf16[8,7168]{1,0:T(8,128)(2,1)S(1)}, bf16[8,7168]{1,0:T(8,128)(2,1)S(1)}, u32[]{:S(2)}, u32[]{:S(2)}) collective-permute-start(bf16[8,7168]{1,0:T(8,128)(2,1)S(1)} %shard_map.79), channel_id=1, source_target_pairs={{0,6},{1,7},{2,4},{3,5},{4,2},{5,3},{6,0},{7,1},{8,14},{9,15},{10,... | collective-permute-start | bytes 344072 | tf_op jit(solution)/shard_map/ppermute | solution.py:26
  26.6 7.3 %collective-permute-start.17 = (bf16[8,7168]{1,0:T(8,128)(2,1)S(1)}, bf16[8,7168]{1,0:T(8,128)(2,1)S(1)}, u32[]{:S(2)}, u32[]{:S(2)}) collective-permute-start(bf16[8,7168]{1,0:T(8,128)(2,1)S(1)} %shard_map.80), channel_id=1, source_target_pairs={{0,2},{1,5},{2,0},{3,7},{4,6},{5,1},{6,4},{7,3},{8,10},{9,13},{10,... | collective-permute-start | bytes 344072 | tf_op jit(solution)/shard_map/ppermute | solution.py:26
  27.5 6.5 %collective-permute-start.19 = (bf16[8,7168]{1,0:T(8,128)(2,1)S(1)}, bf16[8,7168]{1,0:T(8,128)(2,1)S(1)}, u32[]{:S(2)}, u32[]{:S(2)}) collective-permute-start(bf16[8,7168]{1,0:T(8,128)(2,1)S(1)} %shard_map.81), channel_id=1, source_target_pairs={{0,4},{1,3},{2,6},{3,1},{4,0},{5,7},{6,2},{7,5},{8,12},{9,11},{10,... | collective-permute-start | bytes 344072 | tf_op jit(solution)/shard_map/ppermute | solution.py:26
  28.8 7.1 %collective-permute-start.4 = (bf16[8,7168]{1,0:T(8,128)(2,1)S(1)}, bf16[8,7168]{1,0:T(8,128)(2,1)S(1)}, u32[]{:S(2)}, u32[]{:S(2)}) collective-permute-start(bf16[8,7168]{1,0:T(8,128)(2,1)S(1)} %get-tuple-element.49), channel_id=1, source_target_pairs={{0,16},{1,17},{2,18},{3,19},{4,20},{5,21},{6,22},{7,23},{8,24},{9,... | collective-permute-start | bytes 344072 | tf_op jit(solution)/shard_map/ppermute | solution.py:26
  34.0 9.4 %collective-permute-start.21 = (bf16[8,7168]{1,0:T(8,128)(2,1)S(1)}, bf16[8,7168]{1,0:T(8,128)(2,1)S(1)}, u32[]{:S(2)}, u32[]{:S(2)}) collective-permute-start(bf16[8,7168]{1,0:T(8,128)(2,1)S(1)} %shard_map.82), channel_id=1, source_target_pairs={{0,24},{1,25},{2,26},{3,27},{4,28},{5,29},{6,30},{7,31},{8,16},{9,... | collective-permute-start | bytes 344072 | tf_op jit(solution)/shard_map/ppermute | solution.py:26
  35.4 8.1 %collective-permute-start.20 = (bf16[8,7168]{1,0:T(8,128)(2,1)S(1)}, bf16[8,7168]{1,0:T(8,128)(2,1)S(1)}, u32[]{:S(2)}, u32[]{:S(2)}) collective-permute-start(bf16[8,7168]{1,0:T(8,128)(2,1)S(1)} %shard_map.82), channel_id=1, source_target_pairs={{0,16},{1,17},{2,18},{3,19},{4,20},{5,21},{6,22},{7,23},{8,24},{9,... | collective-permute-start | bytes 344072 | tf_op jit(solution)/shard_map/ppermute | solution.py:26
  44.2 6.9 %collective-permute-start.25 = (bf16[8,7168]{1,0:T(8,128)(2,1)S(1)}, bf16[8,7168]{1,0:T(8,128)(2,1)S(1)}, u32[]{:S(2)}, u32[]{:S(2)}) collective-permute-start(bf16[8,7168]{1,0:T(8,128)(2,1)S(1)} %get-tuple-element.73.refs_0_), channel_id=1, source_target_pairs={{0,6},{1,7},{2,4},{3,5},{4,2},{5,3},{6,0},{7,1},{8,14},{9,15},{10,... | collective-permute-start | bytes 344072 | tf_op jit(solution)/shard_map/ppermute | solution.py:26
  44.8 7.5 %collective-permute-start.24 = (bf16[8,7168]{1,0:T(8,128)(2,1)S(1)}, bf16[8,7168]{1,0:T(8,128)(2,1)S(1)}, u32[]{:S(2)}, u32[]{:S(2)}) collective-permute-start(bf16[8,7168]{1,0:T(8,128)(2,1)S(1)} %get-tuple-element.73.refs_0_), channel_id=1, source_target_pairs={{0,2},{1,5},{2,0},{3,7},{4,6},{5,1},{6,4},{7,3},{8,10},{9,13},{10,... | collective-permute-start | bytes 344072 | tf_op jit(solution)/shard_map/ppermute | solution.py:26
  46.0 6.5 %collective-permute-start.23 = (bf16[8,7168]{1,0:T(8,128)(2,1)S(1)}, bf16[8,7168]{1,0:T(8,128)(2,1)S(1)}, u32[]{:S(2)}, u32[]{:S(2)}) collective-permute-start(bf16[8,7168]{1,0:T(8,128)(2,1)S(1)} %get-tuple-element.73.refs_0_), channel_id=1, source_target_pairs={{0,4},{1,3},{2,6},{3,1},{4,0},{5,7},{6,2},{7,5},{8,12},{9,11},{10,... | collective-permute-start | bytes 344072 | tf_op jit(solution)/shard_map/ppermute | solution.py:26
  47.7 5.2 %collective-permute-start.26 = (bf16[8,7168]{1,0:T(8,128)(2,1)S(1)}, bf16[8,7168]{1,0:T(8,128)(2,1)S(1)}, u32[]{:S(2)}, u32[]{:S(2)}) collective-permute-start(bf16[8,7168]{1,0:T(8,128)(2,1)S(1)} %get-tuple-element.73.refs_0_), channel_id=1, source_target_pairs={{0,1},{1,0},{2,3},{3,2},{4,5},{5,4},{6,7},{7,6},{8,9},{9,8},{10,11... | collective-permute-start | bytes 344072 | tf_op jit(solution)/shard_map/ppermute | solution.py:26
  51.1 1.8 %collective-permute-start.29 = (bf16[8,7168]{1,0:T(8,128)(2,1)S(1)}, bf16[8,7168]{1,0:T(8,128)(2,1)S(1)}, u32[]{:S(2)}, u32[]{:S(2)}) collective-permute-start(bf16[8,7168]{1,0:T(8,128)(2,1)S(1)} %collective-permute-done.25.refs_3_), channel_id=1, source_target_pairs={{0,1},{1,0},{2,3},{3,2},{4,5},{5,4},{6,7},{7,6},{8,9},{9,8},{10,11... | collective-permute-start | bytes 344072 | tf_op jit(solution)/shard_map/ppermute | solution.py:26
  52.4 1.3 %collective-permute-start.28 = (bf16[8,7168]{1,0:T(8,128)(2,1)S(1)}, bf16[8,7168]{1,0:T(8,128)(2,1)S(1)}, u32[]{:S(2)}, u32[]{:S(2)}) collective-permute-start(bf16[8,7168]{1,0:T(8,128)(2,1)S(1)} %collective-permute-done.24.refs_2_), channel_id=1, source_target_pairs={{0,1},{1,0},{2,3},{3,2},{4,5},{5,4},{6,7},{7,6},{8,9},{9,8},{10,11... | collective-permute-start | bytes 344072 | tf_op jit(solution)/shard_map/ppermute | solution.py:26
  52.5 1.3 %collective-permute-start.27 = (bf16[8,7168]{1,0:T(8,128)(2,1)S(1)}, bf16[8,7168]{1,0:T(8,128)(2,1)S(1)}, u32[]{:S(2)}, u32[]{:S(2)}) collective-permute-start(bf16[8,7168]{1,0:T(8,128)(2,1)S(1)} %collective-permute-done.23.refs_1_), channel_id=1, source_target_pairs={{0,1},{1,0},{2,3},{3,2},{4,5},{5,4},{6,7},{7,6},{8,9},{9,8},{10,11... | collective-permute-start | bytes 344072 | tf_op jit(solution)/shard_map/ppermute | solution.py:26
  56.0 1.4 %collective-permute-start.31 = (bf16[8,7168]{1,0:T(8,128)(2,1)S(1)}, bf16[8,7168]{1,0:T(8,128)(2,1)S(1)}, u32[]{:S(2)}, u32[]{:S(2)}) collective-permute-start(bf16[8,7168]{1,0:T(8,128)(2,1)S(1)} %get-tuple-element.78), channel_id=1, source_target_pairs={{0,1},{1,0},{2,3},{3,2},{4,5},{5,4},{6,7},{7,6},{8,9},{9,8},{10,11... | collective-permute-start | bytes 344072 | tf_op jit(solution)/shard_map/ppermute | solution.py:26
  56.4 1.8 %collective-permute-start.33 = (bf16[8,7168]{1,0:T(8,128)(2,1)S(1)}, bf16[8,7168]{1,0:T(8,128)(2,1)S(1)}, u32[]{:S(2)}, u32[]{:S(2)}) collective-permute-start(bf16[8,7168]{1,0:T(8,128)(2,1)S(1)} %get-tuple-element.80), channel_id=1, source_target_pairs={{0,1},{1,0},{2,3},{3,2},{4,5},{5,4},{6,7},{7,6},{8,9},{9,8},{10,11... | collective-permute-start | bytes 344072 | tf_op jit(solution)/shard_map/ppermute | solution.py:26
  56.6 2.9 %collective-permute-start.35 = (bf16[8,7168]{1,0:T(8,128)(2,1)S(1)}, bf16[8,7168]{1,0:T(8,128)(2,1)S(1)}, u32[]{:S(2)}, u32[]{:S(2)}) collective-permute-start(bf16[8,7168]{1,0:T(8,128)(2,1)S(1)} %get-tuple-element.82), channel_id=1, source_target_pairs={{0,1},{1,0},{2,3},{3,2},{4,5},{5,4},{6,7},{7,6},{8,9},{9,8},{10,11... | collective-permute-start | bytes 344072 | tf_op jit(solution)/shard_map/ppermute | solution.py:26
  56.9 5.7 %collective-permute-start.30 = (bf16[8,7168]{1,0:T(8,128)(2,1)S(1)}, bf16[8,7168]{1,0:T(8,128)(2,1)S(1)}, u32[]{:S(2)}, u32[]{:S(2)}) collective-permute-start(bf16[8,7168]{1,0:T(8,128)(2,1)S(1)} %get-tuple-element.76), channel_id=1, source_target_pairs={{0,1},{1,0},{2,3},{3,2},{4,5},{5,4},{6,7},{7,6},{8,9},{9,8},{10,11... | collective-permute-start | bytes 344072 | tf_op jit(solution)/shard_map/ppermute | solution.py:26
  57.4 6.9 %collective-permute-start.32 = (bf16[8,7168]{1,0:T(8,128)(2,1)S(1)}, bf16[8,7168]{1,0:T(8,128)(2,1)S(1)}, u32[]{:S(2)}, u32[]{:S(2)}) collective-permute-start(bf16[8,7168]{1,0:T(8,128)(2,1)S(1)} %shard_map.85), channel_id=1, source_target_pairs={{0,6},{1,7},{2,4},{3,5},{4,2},{5,3},{6,0},{7,1},{8,14},{9,15},{10,... | collective-permute-start | bytes 344072 | tf_op jit(solution)/shard_map/ppermute | solution.py:26
  58.3 7.9 %collective-permute-start.34 = (bf16[8,7168]{1,0:T(8,128)(2,1)S(1)}, bf16[8,7168]{1,0:T(8,128)(2,1)S(1)}, u32[]{:S(2)}, u32[]{:S(2)}) collective-permute-start(bf16[8,7168]{1,0:T(8,128)(2,1)S(1)} %shard_map.86), channel_id=1, source_target_pairs={{0,2},{1,5},{2,0},{3,7},{4,6},{5,1},{6,4},{7,3},{8,10},{9,13},{10,... | collective-permute-start | bytes 344072 | tf_op jit(solution)/shard_map/ppermute | solution.py:26
  59.6 6.9 %collective-permute-start.36 = (bf16[8,7168]{1,0:T(8,128)(2,1)S(1)}, bf16[8,7168]{1,0:T(8,128)(2,1)S(1)}, u32[]{:S(2)}, u32[]{:S(2)}) collective-permute-start(bf16[8,7168]{1,0:T(8,128)(2,1)S(1)} %shard_map.87), channel_id=1, source_target_pairs={{0,4},{1,3},{2,6},{3,1},{4,0},{5,7},{6,2},{7,5},{8,12},{9,11},{10,... | collective-permute-start | bytes 344072 | tf_op jit(solution)/shard_map/ppermute | solution.py:26
  61.2 7.4 %collective-permute-start.22 = (bf16[4,7168]{1,0:T(4,128)(2,1)S(1)}, bf16[4,7168]{1,0:T(4,128)(2,1)S(1)}, u32[]{:S(2)}, u32[]{:S(2)}) collective-permute-start(bf16[4,7168]{1,0:T(4,128)(2,1)S(1)} %get-tuple-element.72), channel_id=1, source_target_pairs={{0,16},{1,17},{2,18},{3,19},{4,20},{5,21},{6,22},{7,23},{8,24},{9,... | collective-permute-start | bytes 172040 | tf_op jit(solution)/shard_map/ppermute | solution.py:26
  66.5 6.5 %collective-permute-start.37 = (bf16[4,7168]{1,0:T(4,128)(2,1)S(1)}, bf16[4,7168]{1,0:T(4,128)(2,1)S(1)}, u32[]{:S(2)}, u32[]{:S(2)}) collective-permute-start(bf16[4,7168]{1,0:T(4,128)(2,1)S(1)} %get-tuple-element.83), channel_id=1, source_target_pairs={{0,24},{1,25},{2,26},{3,27},{4,28},{5,29},{6,30},{7,31},{8,16},{9,... | collective-permute-start | bytes 172040 | tf_op jit(solution)/shard_map/ppermute | solution.py:26
  68.0 5.0 %collective-permute-start.38 = (bf16[4,7168]{1,0:T(4,128)(2,1)S(1)}, bf16[4,7168]{1,0:T(4,128)(2,1)S(1)}, u32[]{:S(2)}, u32[]{:S(2)}) collective-permute-start(bf16[4,7168]{1,0:T(4,128)(2,1)S(1)} %get-tuple-element.84), channel_id=1, source_target_pairs={{0,16},{1,17},{2,18},{3,19},{4,20},{5,21},{6,22},{7,23},{8,24},{9,... | collective-permute-start | bytes 172040 | tf_op jit(solution)/shard_map/ppermute | solution.py:26

commit v13 on v11

--- a/solution.py
+++ b/solution.py
@@ -50,24 +50,23 @@
     )(*args)
 
 
-def load_kernel(gate_ref, up_ref, down_ref, gate_out, up_out, down_out, sems):
-    copies = [
-        pltpu.make_async_copy(source, target, sems.at[place])
-        for place, (source, target) in enumerate(((gate_ref, gate_out), (up_ref, up_out), (down_ref, down_out)))
-    ]
+def load_kernel(count, *refs):
+    sems = refs[-1]
+    copies = [pltpu.make_async_copy(refs[place], refs[count + place], sems.at[place]) for place in range(count)]
     for copy in copies:
         copy.start()
     for copy in copies:
         copy.wait()
 
 
-def load(weights):
+def load(*weights):
+    count = len(weights)
     return pl.pallas_call(
-        load_kernel,
+        functools.partial(load_kernel, count),
         out_shape=[pltpu.VMEM(w.shape, w.dtype) for w in weights],
-        in_specs=[pl.BlockSpec(memory_space=pltpu.HBM)] * 3,
-        out_specs=[VMEM] * 3,
-        scratch_shapes=[pltpu.SemaphoreType.DMA((3,))],
+        in_specs=[pl.BlockSpec(memory_space=pltpu.HBM)] * count,
+        out_specs=[VMEM] * count,
+        scratch_shapes=[pltpu.SemaphoreType.DMA((count,))],
         compiler_params=pltpu.CompilerParams(vmem_limit_bytes=VMEM_LIMIT),
         cost_estimate=pl.CostEstimate(
             flops=0, bytes_accessed=sum(2 * w.size for w in weights), transcendentals=0
@@ -155,7 +154,7 @@
     normalise(raw_ref, gain_ref, out_ref)
 
 
-def meet_kernel(rest_ref, near_ref, far_ref, gain_ref, out_ref, raw_ref, own_ref):
+def meet_kernel(rest_ref, near_ref, far_ref, gain_ref, out_ref, own_ref, raw_ref):
     half = own_ref.shape[0]
     for span in spans(out_ref.shape[1]):
         far = far_ref[:, span].astype(jnp.float32)
@@ -189,7 +188,7 @@
     gated = jnp.zeros((8 * part, hidden), jnp.float32)
     up_part = jnp.zeros((8 * part, hidden), jnp.float32)
     for span in spans(dim):
-        rows = jnp.concatenate([ref[:, span].astype(jnp.float32) for ref in x_refs], axis=0).astype(jnp.bfloat16)
+        rows = jnp.concatenate([ref[:, span] for ref in x_refs], axis=0)
         gated += jnp.dot(rows, gate_ref[0, span, :], preferred_element_type=jnp.float32)
         up_part += jnp.dot(rows, up_ref[0, span, :], preferred_element_type=jnp.float32)
     inner = (gated / (1.0 + jnp.exp(-gated)) * up_part).astype(jnp.bfloat16)
@@ -237,18 +236,24 @@
     passes_count = routing.shape[1]
     top, *middle = upper_flips(owners)
 
-    weights = load((gate_proj, up_proj, down_proj))
+    gate, up = load(gate_proj, up_proj)
     block = prepare(owners // GROUP, states, routing, route_weight)
     other = exchange(block, top, 0)
-    block, other, *weights = lax.optimization_barrier((block, other, *weights))
+    other, gate, up = lax.optimization_barrier((other, gate, up))
     pair, raw = call(first_kernel, [(2 * row_dev, dim + LANES), (2 * row_dev, dim)], block, other, norm_gain)
+    pair, down_hbm = lax.optimization_barrier((pair, down_proj))
+    (down,) = load(down_hbm)
     own, tail = states[0], None
     for step_no in range(passes_count):
         rows_a = pair
         for flips in middle:
             rows_a = join(rows_a, exchange(rows_a, flips, 0))
         mine = [rows_a] + [exchange(rows_a, flips, 0) for flips in SQUARE]
-        outs, tail = mlp(step_no, mine + [exchange(rows, CORE, 0) for rows in mine], tail, *weights)
+        near = rows_a
+        if step_no == 0:
+            near, down = lax.optimization_barrier((near, down))
+        fars = [exchange(rows, CORE, 0) for rows in [near] + mine[1:]]
+        outs, tail = mlp(step_no, mine + fars, tail, gate, up, down)
 
         kept, sent = outs[:4], [exchange(rows, CORE, 0) for rows in outs[4:]]
         parts = [kept[0], sent[0]]
@@ -260,10 +265,13 @@
         if step_no < passes_count - 1:
             total = add(*parts)
             rest = exchange(raw, STAY, 1)
-            pair, raw, own = call(
-                meet_kernel, [(2 * row_dev, dim), (2 * row_dev, dim), (row_dev, dim)],
+            more = step_no < passes_count - 2
+            pair, own, *raws = call(
+                meet_kernel, [(2 * row_dev, dim), (row_dev, dim)] + [(2 * row_dev, dim)] * more,
                 rest, exchange(total, STAY, 1), exchange(total, top, 1), norm_gain,
+                scratch_shapes=[] if more else [pltpu.VMEM((2 * row_dev, dim), jnp.bfloat16)],
             )
+            raw = raws[0] if more else None
         else:
             low, high = split(*parts)
             rest = exchange(own, STAY, 1)

time: 72.1 us -> 70.5 us (0.978)
  waiting for transfers between devices: 30.9 us -> 26.6 us
  starting transfers between devices: 29.6 us -> 31.8 us
    ppermute x35, waiting for transfers between devices: 30.9 us -> 26.6 us  [exchange(): return lax.ppermute(value, ('segment', 'expert'), pairs)]
    ppermute x35, starting transfers between devices: 29.6 us -> 31.8 us  [exchange(): return lax.ppermute(value, ('segment', 'expert'), pairs)]
    pallas_call x1 -> x2, Pallas kernels: 4.23 us -> 5.22 us  [load(): pl.pallas_call(functools.partial(load_kernel, count), out_shape=[pltpu.VM...]
  transfers between devices with their start and end apart: 35 -> 35, of which waited for: 16 -> 17; matrix products, arithmetic and copies ran while one was open for 0% -> 0% of each run, Pallas kernels for 6% -> 8%
where the time goes in v13:
time: 70.5 us; the launch traced here: 70.3 us
  starting transfers between devices  31.8 us (45%)
  waiting for transfers between devices  26.6 us (38%)
  Pallas kernels  11.8 us (17%)
    ppermute x35, starting transfers between devices, exchange(): return lax.ppermute(value, ('segment', 'expert'), pairs)  31.8 us
    ppermute x35, waiting for transfers between devices, exchange(): return lax.ppermute(value, ('segment', 'expert'), pairs)  26.6 us
    pallas_call x14, Pallas kernels, call(): pl.pallas_call(kernel, out_shape=[jax.ShapeDtypeStruct(shape, jnp.bfloat1...  6.6 us
    pallas_call x2, Pallas kernels, load(): pl.pallas_call(functools.partial(load_kernel, count), out_shape=[pltpu.VM...  5.22 us
  transfers between devices with their start and end apart: 35, of which 17 were waited for; matrix products, arithmetic and copies ran while one was open for 0% of the time, Pallas kernels for 8%

profile of v13, /device:TPU:0, one launch (start us, length us, event | category | flops | bytes accessed | tf_op | source)
XLA Modules:
  0.0 70.3 jit_solution(7790324759333275005)
XLA Ops:
  0.0 1.0 %shard_map.73.own_ref = bf16[4,7296]{1,0:T(4,128)(2,1)S(1)} custom-call(bf16[1,4,7168]{2,1,0:T(4,128)(2,1)} %states_hbm.1, s32[1,2,2,4]{3,2,1,0:T(2,128)} %bitcast.3, bf16[1,2,2,4]{3,2,1,0:T(2,128)(2,1)} %bitcast.4), custom_call_target="tpu_custom_call" | custom-call | tf_op jit(solution)/shard_map/pallas_call | solution.py:43
  1.0 0.0 copy-start
  1.0 4.1 %collective-permute-start = (bf16[4,7296]{1,0:T(4,128)(2,1)S(1)}, bf16[4,7296]{1,0:T(4,128)(2,1)S(1)}, u32[]{:S(2)}, u32[]{:S(2)}) collective-permute-start(bf16[4,7296]{1,0:T(4,128)(2,1)S(1)} %shard_map.73.own_ref), channel_id=1, source_target_pairs={{0,8},{1,9},{2,10},{3,11},{4,12},{5,13},{6,14},{7,15},{8,0},{9,1},... | collective-permute-start | bytes 175112 | tf_op jit(solution)/shard_map/ppermute | solution.py:26
  5.1 3.2 %shard_map.74 = (bf16[1,7168,256]{2,1,0:T(8,128)(2,1)S(1)}, bf16[1,7168,256]{2,1,0:T(8,128)(2,1)S(1)}) custom-call(bf16[1,7168,256]{2,1,0:T(8,128)(2,1)} %refs_0_.1, bf16[1,7168,256]{2,1,0:T(8,128)(2,1)} %refs_1_.1), custom_call_target="tpu_custom_call" | custom-call | bytes 7340032 | tf_op jit(solution)/shard_map/pallas_call | solution.py:64
  8.3 0.2 shard_map.75
  8.5 2.6 %collective-permute-start.4 = (bf16[8,7296]{1,0:T(8,128)(2,1)S(1)}, bf16[8,7296]{1,0:T(8,128)(2,1)S(1)}, u32[]{:S(2)}, u32[]{:S(2)}) collective-permute-start(bf16[8,7296]{1,0:T(8,128)(2,1)S(1)} %get-tuple-element.44.refs_0_), channel_id=1, source_target_pairs={{0,6},{1,7},{2,4},{3,5},{4,2},{5,3},{6,0},{7,1},{8,14},{9,15},{10,... | collective-permute-start | bytes 350216 | tf_op jit(solution)/shard_map/ppermute | solution.py:26
  11.1 0.5 collective-permute-start.3
  11.6 0.4 collective-permute-start.2
  12.0 2.0 %shard_map.76.refs_10_.refs_11_ = bf16[1,256,7168]{2,1,0:T(8,128)(2,1)S(1)} custom-call(bf16[1,256,7168]{2,1,0:T(8,128)(2,1)} %refs_0_.2), custom_call_target="tpu_custom_call" | custom-call | bytes 3670016 | tf_op jit(solution)/shard_map/pallas_call | solution.py:64
  14.1 0.1 collective-permute-start.5
  14.2 1.3 %collective-permute-done.4.refs_3_ = bf16[8,7296]{1,0:T(8,128)(2,1)S(1)} collective-permute-done((bf16[8,7296]{1,0:T(8,128)(2,1)S(1)}, bf16[8,7296]{1,0:T(8,128)(2,1)S(1)}, u32[]{:S(2)}, u32[]{:S(2)}) %collective-permute-start.4) | collective-permute-done | bytes 116768 | tf_op jit(solution)/shard_map/ppermute | solution.py:26
  15.5 1.3 %collective-permute-done.3.refs_2_ = bf16[8,7296]{1,0:T(8,128)(2,1)S(1)} collective-permute-done((bf16[8,7296]{1,0:T(8,128)(2,1)S(1)}, bf16[8,7296]{1,0:T(8,128)(2,1)S(1)}, u32[]{:S(2)}, u32[]{:S(2)}) %collective-permute-start.3) | collective-permute-done | bytes 116768 | tf_op jit(solution)/shard_map/ppermute | solution.py:26
  16.8 0.5 collective-permute-start.6
  17.3 0.0 collective-permute-done.8.refs_7_
  17.3 0.8 %collective-permute-done.7.refs_6_ = bf16[8,7296]{1,0:T(8,128)(2,1)S(1)} collective-permute-done((bf16[8,7296]{1,0:T(8,128)(2,1)S(1)}, bf16[8,7296]{1,0:T(8,128)(2,1)S(1)}, u32[]{:S(2)}, u32[]{:S(2)}) %collective-permute-start.7) | collective-permute-done | bytes 116768 | tf_op jit(solution)/shard_map/ppermute | solution.py:26
  18.2 0.2 collective-permute-done.6.refs_5_
  18.3 2.1 %shard_map.77 = (bf16[8,7168]{1,0:T(8,128)(2,1)S(1)}, bf16[8,7168]{1,0:T(8,128)(2,1)S(1)}, bf16[8,7168]{1,0:T(8,128)(2,1)S(1)}, bf16[8,7168]{1,0:T(8,128)(2,1)S(...) custom-call(bf16[8,7296]{1,0:T(8,128)(2,1)S(1)} %get-tuple-element.4, ...), custom_call_target="tpu_custom_call" | custom-call | flops 704643072 | bytes 11010048 | tf_op jit(solution)/shard_map/pallas_call | solution.py:43
  20.4 0.4 collective-permute-start.10
  20.9 0.2 collective-permute-start.12
  21.0 0.3 collective-permute-start.14
  21.4 0.2 collective-permute-start.9
  21.5 0.3 collective-permute-done.10.refs_1_
  21.9 2.4 %collective-permute-start.11 = (bf16[8,7168]{1,0:T(8,128)(2,1)S(1)}, bf16[8,7168]{1,0:T(8,128)(2,1)S(1)}, u32[]{:S(2)}, u32[]{:S(2)}) collective-permute-start(bf16[8,7168]{1,0:T(8,128)(2,1)S(1)} %shard_map.78), channel_id=1, source_target_pairs={{0,6},{1,7},{2,4},{3,5},{4,2},{5,3},{6,0},{7,1},{8,14},{9,15},{10,... | collective-permute-start | bytes 344072 | tf_op jit(solution)/shard_map/ppermute | solution.py:26
  24.2 0.0 collective-permute-done.12.refs_1_
  24.3 0.8 %collective-permute-start.13 = (bf16[8,7168]{1,0:T(8,128)(2,1)S(1)}, bf16[8,7168]{1,0:T(8,128)(2,1)S(1)}, u32[]{:S(2)}, u32[]{:S(2)}) collective-permute-start(bf16[8,7168]{1,0:T(8,128)(2,1)S(1)} %shard_map.79), channel_id=1, source_target_pairs={{0,2},{1,5},{2,0},{3,7},{4,6},{5,1},{6,4},{7,3},{8,10},{9,13},{10,... | collective-permute-start | bytes 344072 | tf_op jit(solution)/shard_map/ppermute | solution.py:26
  25.1 0.5 collective-permute-start.15
  25.6 1.5 %collective-permute-start.1 = (bf16[8,7168]{1,0:T(8,128)(2,1)S(1)}, bf16[8,7168]{1,0:T(8,128)(2,1)S(1)}, u32[]{:S(2)}, u32[]{:S(2)}) collective-permute-start(bf16[8,7168]{1,0:T(8,128)(2,1)S(1)} %get-tuple-element.40), channel_id=1, source_target_pairs={{0,16},{1,17},{2,18},{3,19},{4,20},{5,21},{6,22},{7,23},{8,24},{9,... | collective-permute-start | bytes 344072 | tf_op jit(solution)/shard_map/ppermute | solution.py:26
  27.2 1.6 %collective-permute-done.11.refs_2_ = bf16[8,7168]{1,0:T(8,128)(2,1)S(1)} collective-permute-done((bf16[8,7168]{1,0:T(8,128)(2,1)S(1)}, bf16[8,7168]{1,0:T(8,128)(2,1)S(1)}, u32[]{:S(2)}, u32[]{:S(2)}) %collective-permute-start.11) | collective-permute-done | bytes 114720 | tf_op jit(solution)/shard_map/ppermute | solution.py:26
  28.8 1.9 %collective-permute-done.13.refs_3_ = bf16[8,7168]{1,0:T(8,128)(2,1)S(1)} collective-permute-done((bf16[8,7168]{1,0:T(8,128)(2,1)S(1)}, bf16[8,7168]{1,0:T(8,128)(2,1)S(1)}, u32[]{:S(2)}, u32[]{:S(2)}) %collective-permute-start.13) | collective-permute-done | bytes 114720 | tf_op jit(solution)/shard_map/ppermute | solution.py:26
  30.7 0.1 shard_map.81
  30.8 3.0 %collective-permute-start.17 = (bf16[8,7168]{1,0:T(8,128)(2,1)S(1)}, bf16[8,7168]{1,0:T(8,128)(2,1)S(1)}, u32[]{:S(2)}, u32[]{:S(2)}) collective-permute-start(bf16[8,7168]{1,0:T(8,128)(2,1)S(1)} %shard_map.81), channel_id=1, source_target_pairs={{0,24},{1,25},{2,26},{3,27},{4,28},{5,29},{6,30},{7,31},{8,16},{9,... | collective-permute-start | bytes 344072 | tf_op jit(solution)/shard_map/ppermute | solution.py:26
  33.8 0.5 collective-permute-start.16
  34.3 5.8 %collective-permute-done.17.far_ref = bf16[8,7168]{1,0:T(8,128)(2,1)S(1)} collective-permute-done((bf16[8,7168]{1,0:T(8,128)(2,1)S(1)}, bf16[8,7168]{1,0:T(8,128)(2,1)S(1)}, u32[]{:S(2)}, u32[]{:S(2)}) %collective-permute-start.17) | collective-permute-done | bytes 114720 | tf_op jit(solution)/shard_map/ppermute | solution.py:26
  40.1 0.0 collective-permute-done.16.near_ref
  40.1 0.2 shard_map.82
  40.4 2.6 %collective-permute-start.21 = (bf16[8,7168]{1,0:T(8,128)(2,1)S(1)}, bf16[8,7168]{1,0:T(8,128)(2,1)S(1)}, u32[]{:S(2)}, u32[]{:S(2)}) collective-permute-start(bf16[8,7168]{1,0:T(8,128)(2,1)S(1)} %get-tuple-element.57.refs_0_), channel_id=1, source_target_pairs={{0,6},{1,7},{2,4},{3,5},{4,2},{5,3},{6,0},{7,1},{8,14},{9,15},{10,... | collective-permute-start | bytes 344072 | tf_op jit(solution)/shard_map/ppermute | solution.py:26
  42.9 0.8 %collective-permute-start.20 = (bf16[8,7168]{1,0:T(8,128)(2,1)S(1)}, bf16[8,7168]{1,0:T(8,128)(2,1)S(1)}, u32[]{:S(2)}, u32[]{:S(2)}) collective-permute-start(bf16[8,7168]{1,0:T(8,128)(2,1)S(1)} %get-tuple-element.57.refs_0_), channel_id=1, source_target_pairs={{0,2},{1,5},{2,0},{3,7},{4,6},{5,1},{6,4},{7,3},{8,10},{9,13},{10,... | collective-permute-start | bytes 344072 | tf_op jit(solution)/shard_map/ppermute | solution.py:26
  43.7 0.2 collective-permute-start.19
  43.9 3.2 %collective-permute-done.21.refs_3_ = bf16[8,7168]{1,0:T(8,128)(2,1)S(1)} collective-permute-done((bf16[8,7168]{1,0:T(8,128)(2,1)S(1)}, bf16[8,7168]{1,0:T(8,128)(2,1)S(1)}, u32[]{:S(2)}, u32[]{:S(2)}) %collective-permute-start.21) | collective-permute-done | bytes 114720 | tf_op jit(solution)/shard_map/ppermute | solution.py:26
  47.1 1.6 %collective-permute-done.20.refs_2_ = bf16[8,7168]{1,0:T(8,128)(2,1)S(1)} collective-permute-done((bf16[8,7168]{1,0:T(8,128)(2,1)S(1)}, bf16[8,7168]{1,0:T(8,128)(2,1)S(1)}, u32[]{:S(2)}, u32[]{:S(2)}) %collective-permute-start.20) | collective-permute-done | bytes 114720 | tf_op jit(solution)/shard_map/ppermute | solution.py:26
  48.7 0.0 collective-permute-start.24
  48.7 0.0 collective-permute-done.19.refs_1_
  48.7 0.5 collective-permute-start.23
  49.2 0.0 collective-permute-done.22.refs_4_
  49.2 0.8 %collective-permute-done.24.refs_6_ = bf16[8,7168]{1,0:T(8,128)(2,1)S(1)} collective-permute-done((bf16[8,7168]{1,0:T(8,128)(2,1)S(1)}, bf16[8,7168]{1,0:T(8,128)(2,1)S(1)}, u32[]{:S(2)}, u32[]{:S(2)}) %collective-permute-start.24) | collective-permute-done | bytes 114720 | tf_op jit(solution)/shard_map/ppermute | solution.py:26
  50.0 0.2 collective-permute-done.23.refs_5_
  50.2 2.1 %shard_map.83 = (bf16[8,7168]{1,0:T(8,128)(2,1)S(1)}, bf16[8,7168]{1,0:T(8,128)(2,1)S(1)}, bf16[8,7168]{1,0:T(8,128)(2,1)S(1)}, bf16[8,7168]{1,0:T(8,128)(2,1)S(...) custom-call(bf16[8,7168]{1,0:T(8,128)(2,1)S(1)} %get-tuple-element.5, ...), custom_call_target="tpu_custom_call" | custom-call | flops 704643072 | bytes 11010048 | tf_op jit(solution)/shard_map/pallas_call | solution.py:43
  52.3 0.4 collective-permute-start.27
  52.7 0.2 collective-permute-start.29
  52.9 0.3 collective-permute-start.31
  53.2 0.2 collective-permute-start.26
  53.4 0.3 collective-permute-done.27.refs_1_
  53.7 2.7 %collective-permute-start.28 = (bf16[8,7168]{1,0:T(8,128)(2,1)S(1)}, bf16[8,7168]{1,0:T(8,128)(2,1)S(1)}, u32[]{:S(2)}, u32[]{:S(2)}) collective-permute-start(bf16[8,7168]{1,0:T(8,128)(2,1)S(1)} %shard_map.84), channel_id=1, source_target_pairs={{0,6},{1,7},{2,4},{3,5},{4,2},{5,3},{6,0},{7,1},{8,14},{9,15},{10,... | collective-permute-start | bytes 344072 | tf_op jit(solution)/shard_map/ppermute | solution.py:26
  56.4 0.8 %collective-permute-start.30 = (bf16[8,7168]{1,0:T(8,128)(2,1)S(1)}, bf16[8,7168]{1,0:T(8,128)(2,1)S(1)}, u32[]{:S(2)}, u32[]{:S(2)}) collective-permute-start(bf16[8,7168]{1,0:T(8,128)(2,1)S(1)} %shard_map.85), channel_id=1, source_target_pairs={{0,2},{1,5},{2,0},{3,7},{4,6},{5,1},{6,4},{7,3},{8,10},{9,13},{10,... | collective-permute-start | bytes 344072 | tf_op jit(solution)/shard_map/ppermute | solution.py:26
  57.3 0.2 collective-permute-start.32
  57.5 1.4 %collective-permute-start.18 = (bf16[4,7168]{1,0:T(4,128)(2,1)S(1)}, bf16[4,7168]{1,0:T(4,128)(2,1)S(1)}, u32[]{:S(2)}, u32[]{:S(2)}) collective-permute-start(bf16[4,7168]{1,0:T(4,128)(2,1)S(1)} %get-tuple-element.56), channel_id=1, source_target_pairs={{0,16},{1,17},{2,18},{3,19},{4,20},{5,21},{6,22},{7,23},{8,24},{9,... | collective-permute-start | bytes 172040 | tf_op jit(solution)/shard_map/ppermute | solution.py:26
  58.9 1.7 %collective-permute-done.28.refs_2_ = bf16[8,7168]{1,0:T(8,128)(2,1)S(1)} collective-permute-done((bf16[8,7168]{1,0:T(8,128)(2,1)S(1)}, bf16[8,7168]{1,0:T(8,128)(2,1)S(1)}, u32[]{:S(2)}, u32[]{:S(2)}) %collective-permute-start.28) | collective-permute-done | bytes 114720 | tf_op jit(solution)/shard_map/ppermute | solution.py:26
  60.7 1.9 %collective-permute-done.30.refs_3_ = bf16[8,7168]{1,0:T(8,128)(2,1)S(1)} collective-permute-done((bf16[8,7168]{1,0:T(8,128)(2,1)S(1)}, bf16[8,7168]{1,0:T(8,128)(2,1)S(1)}, u32[]{:S(2)}, u32[]{:S(2)}) %collective-permute-start.30) | collective-permute-done | bytes 114720 | tf_op jit(solution)/shard_map/ppermute | solution.py:26
  62.6 0.1 shard_map.87
  62.6 2.7 %collective-permute-start.33 = (bf16[4,7168]{1,0:T(4,128)(2,1)S(1)}, bf16[4,7168]{1,0:T(4,128)(2,1)S(1)}, u32[]{:S(2)}, u32[]{:S(2)}) collective-permute-start(bf16[4,7168]{1,0:T(4,128)(2,1)S(1)} %get-tuple-element.67), channel_id=1, source_target_pairs={{0,24},{1,25},{2,26},{3,27},{4,28},{5,29},{6,30},{7,31},{8,16},{9,... | collective-permute-start | bytes 172040 | tf_op jit(solution)/shard_map/ppermute | solution.py:26
  65.4 0.7 collective-permute-start.34
  66.0 3.4 %collective-permute-done.33.refs_1_ = bf16[4,7168]{1,0:T(4,128)(2,1)S(1)} collective-permute-done((bf16[4,7168]{1,0:T(4,128)(2,1)S(1)}, bf16[4,7168]{1,0:T(4,128)(2,1)S(1)}, u32[]{:S(2)}, u32[]{:S(2)}) %collective-permute-start.33) | collective-permute-done | bytes 57376 | tf_op jit(solution)/shard_map/ppermute | solution.py:26
  69.4 0.3 collective-permute-done.34.refs_2_
  69.7 0.7 shard_map.88
  (24 shorter events, 0.2 us)
Async XLA Ops:
  1.0 7.3 %copy-start = (f32[1,7168]{1,0:T(1,128)S(1)}, f32[1,7168]{1,0:T(1,128)}, u32[]{:S(2)}) copy-start(f32[1,7168]{1,0:T(1,128)} %gain_ref.3) | copy-start | bytes 86020
  1.0 7.3 %collective-permute-start = (bf16[4,7296]{1,0:T(4,128)(2,1)S(1)}, bf16[4,7296]{1,0:T(4,128)(2,1)S(1)}, u32[]{:S(2)}, u32[]{:S(2)}) collective-permute-start(bf16[4,7296]{1,0:T(4,128)(2,1)S(1)} %shard_map.73.own_ref), channel_id=1, source_target_pairs={{0,8},{1,9},{2,10},{3,11},{4,12},{5,13},{6,14},{7,15},{8,0},{9,1},... | collective-permute-start | bytes 175112 | tf_op jit(solution)/shard_map/ppermute | solution.py:26
  8.5 7.0 %collective-permute-start.4 = (bf16[8,7296]{1,0:T(8,128)(2,1)S(1)}, bf16[8,7296]{1,0:T(8,128)(2,1)S(1)}, u32[]{:S(2)}, u32[]{:S(2)}) collective-permute-start(bf16[8,7296]{1,0:T(8,128)(2,1)S(1)} %get-tuple-element.44.refs_0_), channel_id=1, source_target_pairs={{0,6},{1,7},{2,4},{3,5},{4,2},{5,3},{6,0},{7,1},{8,14},{9,15},{10,... | collective-permute-start | bytes 350216 | tf_op jit(solution)/shard_map/ppermute | solution.py:26
  11.1 5.7 %collective-permute-start.3 = (bf16[8,7296]{1,0:T(8,128)(2,1)S(1)}, bf16[8,7296]{1,0:T(8,128)(2,1)S(1)}, u32[]{:S(2)}, u32[]{:S(2)}) collective-permute-start(bf16[8,7296]{1,0:T(8,128)(2,1)S(1)} %get-tuple-element.44.refs_0_), channel_id=1, source_target_pairs={{0,2},{1,5},{2,0},{3,7},{4,6},{5,1},{6,4},{7,3},{8,10},{9,13},{10,... | collective-permute-start | bytes 350216 | tf_op jit(solution)/shard_map/ppermute | solution.py:26
  11.6 5.2 %collective-permute-start.2 = (bf16[8,7296]{1,0:T(8,128)(2,1)S(1)}, bf16[8,7296]{1,0:T(8,128)(2,1)S(1)}, u32[]{:S(2)}, u32[]{:S(2)}) collective-permute-start(bf16[8,7296]{1,0:T(8,128)(2,1)S(1)} %get-tuple-element.44.refs_0_), channel_id=1, source_target_pairs={{0,4},{1,3},{2,6},{3,1},{4,0},{5,7},{6,2},{7,5},{8,12},{9,11},{10,... | collective-permute-start | bytes 350216 | tf_op jit(solution)/shard_map/ppermute | solution.py:26
  14.1 3.2 %collective-permute-start.5 = (bf16[8,7296]{1,0:T(8,128)(2,1)S(1)}, bf16[8,7296]{1,0:T(8,128)(2,1)S(1)}, u32[]{:S(2)}, u32[]{:S(2)}) collective-permute-start(bf16[8,7296]{1,0:T(8,128)(2,1)S(1)} %get-tuple-element.44.refs_0_), channel_id=1, source_target_pairs={{0,1},{1,0},{2,3},{3,2},{4,5},{5,4},{6,7},{7,6},{8,9},{9,8},{10,11... | collective-permute-start | bytes 350216 | tf_op jit(solution)/shard_map/ppermute | solution.py:26
  15.5 1.8 %collective-permute-start.8 = (bf16[8,7296]{1,0:T(8,128)(2,1)S(1)}, bf16[8,7296]{1,0:T(8,128)(2,1)S(1)}, u32[]{:S(2)}, u32[]{:S(2)}) collective-permute-start(bf16[8,7296]{1,0:T(8,128)(2,1)S(1)} %collective-permute-done.4.refs_3_), channel_id=1, source_target_pairs={{0,1},{1,0},{2,3},{3,2},{4,5},{5,4},{6,7},{7,6},{8,9},{9,8},{10,11... | collective-permute-start | bytes 350216 | tf_op jit(solution)/shard_map/ppermute | solution.py:26
  16.8 1.3 %collective-permute-start.7 = (bf16[8,7296]{1,0:T(8,128)(2,1)S(1)}, bf16[8,7296]{1,0:T(8,128)(2,1)S(1)}, u32[]{:S(2)}, u32[]{:S(2)}) collective-permute-start(bf16[8,7296]{1,0:T(8,128)(2,1)S(1)} %collective-permute-done.3.refs_2_), channel_id=1, source_target_pairs={{0,1},{1,0},{2,3},{3,2},{4,5},{5,4},{6,7},{7,6},{8,9},{9,8},{10,11... | collective-permute-start | bytes 350216 | tf_op jit(solution)/shard_map/ppermute | solution.py:26
  16.8 1.5 %collective-permute-start.6 = (bf16[8,7296]{1,0:T(8,128)(2,1)S(1)}, bf16[8,7296]{1,0:T(8,128)(2,1)S(1)}, u32[]{:S(2)}, u32[]{:S(2)}) collective-permute-start(bf16[8,7296]{1,0:T(8,128)(2,1)S(1)} %collective-permute-done.2.refs_1_), channel_id=1, source_target_pairs={{0,1},{1,0},{2,3},{3,2},{4,5},{5,4},{6,7},{7,6},{8,9},{9,8},{10,11... | collective-permute-start | bytes 350216 | tf_op jit(solution)/shard_map/ppermute | solution.py:26
  20.4 1.4 %collective-permute-start.10 = (bf16[8,7168]{1,0:T(8,128)(2,1)S(1)}, bf16[8,7168]{1,0:T(8,128)(2,1)S(1)}, u32[]{:S(2)}, u32[]{:S(2)}) collective-permute-start(bf16[8,7168]{1,0:T(8,128)(2,1)S(1)} %get-tuple-element.51), channel_id=1, source_target_pairs={{0,1},{1,0},{2,3},{3,2},{4,5},{5,4},{6,7},{7,6},{8,9},{9,8},{10,11... | collective-permute-start | bytes 344072 | tf_op jit(solution)/shard_map/ppermute | solution.py:26
  20.9 3.4 %collective-permute-start.12 = (bf16[8,7168]{1,0:T(8,128)(2,1)S(1)}, bf16[8,7168]{1,0:T(8,128)(2,1)S(1)}, u32[]{:S(2)}, u32[]{:S(2)}) collective-permute-start(bf16[8,7168]{1,0:T(8,128)(2,1)S(1)} %get-tuple-element.53), channel_id=1, source_target_pairs={{0,1},{1,0},{2,3},{3,2},{4,5},{5,4},{6,7},{7,6},{8,9},{9,8},{10,11... | collective-permute-start | bytes 344072 | tf_op jit(solution)/shard_map/ppermute | solution.py:26
  21.0 4.1 %collective-permute-start.14 = (bf16[8,7168]{1,0:T(8,128)(2,1)S(1)}, bf16[8,7168]{1,0:T(8,128)(2,1)S(1)}, u32[]{:S(2)}, u32[]{:S(2)}) collective-permute-start(bf16[8,7168]{1,0:T(8,128)(2,1)S(1)} %get-tuple-element.55), channel_id=1, source_target_pairs={{0,1},{1,0},{2,3},{3,2},{4,5},{5,4},{6,7},{7,6},{8,9},{9,8},{10,11... | collective-permute-start | bytes 344072 | tf_op jit(solution)/shard_map/ppermute | solution.py:26
  21.4 5.8 %collective-permute-start.9 = (bf16[8,7168]{1,0:T(8,128)(2,1)S(1)}, bf16[8,7168]{1,0:T(8,128)(2,1)S(1)}, u32[]{:S(2)}, u32[]{:S(2)}) collective-permute-start(bf16[8,7168]{1,0:T(8,128)(2,1)S(1)} %get-tuple-element.49), channel_id=1, source_target_pairs={{0,1},{1,0},{2,3},{3,2},{4,5},{5,4},{6,7},{7,6},{8,9},{9,8},{10,11... | collective-permute-start | bytes 344072 | tf_op jit(solution)/shard_map/ppermute | solution.py:26
  21.9 6.9 %collective-permute-start.11 = (bf16[8,7168]{1,0:T(8,128)(2,1)S(1)}, bf16[8,7168]{1,0:T(8,128)(2,1)S(1)}, u32[]{:S(2)}, u32[]{:S(2)}) collective-permute-start(bf16[8,7168]{1,0:T(8,128)(2,1)S(1)} %shard_map.78), channel_id=1, source_target_pairs={{0,6},{1,7},{2,4},{3,5},{4,2},{5,3},{6,0},{7,1},{8,14},{9,15},{10,... | collective-permute-start | bytes 344072 | tf_op jit(solution)/shard_map/ppermute | solution.py:26
  24.3 6.4 %collective-permute-start.13 = (bf16[8,7168]{1,0:T(8,128)(2,1)S(1)}, bf16[8,7168]{1,0:T(8,128)(2,1)S(1)}, u32[]{:S(2)}, u32[]{:S(2)}) collective-permute-start(bf16[8,7168]{1,0:T(8,128)(2,1)S(1)} %shard_map.79), channel_id=1, source_target_pairs={{0,2},{1,5},{2,0},{3,7},{4,6},{5,1},{6,4},{7,3},{8,10},{9,13},{10,... | collective-permute-start | bytes 344072 | tf_op jit(solution)/shard_map/ppermute | solution.py:26
  25.1 5.6 %collective-permute-start.15 = (bf16[8,7168]{1,0:T(8,128)(2,1)S(1)}, bf16[8,7168]{1,0:T(8,128)(2,1)S(1)}, u32[]{:S(2)}, u32[]{:S(2)}) collective-permute-start(bf16[8,7168]{1,0:T(8,128)(2,1)S(1)} %shard_map.80), channel_id=1, source_target_pairs={{0,4},{1,3},{2,6},{3,1},{4,0},{5,7},{6,2},{7,5},{8,12},{9,11},{10,... | collective-permute-start | bytes 344072 | tf_op jit(solution)/shard_map/ppermute | solution.py:26
  25.6 8.7 %collective-permute-start.1 = (bf16[8,7168]{1,0:T(8,128)(2,1)S(1)}, bf16[8,7168]{1,0:T(8,128)(2,1)S(1)}, u32[]{:S(2)}, u32[]{:S(2)}) collective-permute-start(bf16[8,7168]{1,0:T(8,128)(2,1)S(1)} %get-tuple-element.40), channel_id=1, source_target_pairs={{0,16},{1,17},{2,18},{3,19},{4,20},{5,21},{6,22},{7,23},{8,24},{9,... | collective-permute-start | bytes 344072 | tf_op jit(solution)/shard_map/ppermute | solution.py:26
  30.8 9.4 %collective-permute-start.17 = (bf16[8,7168]{1,0:T(8,128)(2,1)S(1)}, bf16[8,7168]{1,0:T(8,128)(2,1)S(1)}, u32[]{:S(2)}, u32[]{:S(2)}) collective-permute-start(bf16[8,7168]{1,0:T(8,128)(2,1)S(1)} %shard_map.81), channel_id=1, source_target_pairs={{0,24},{1,25},{2,26},{3,27},{4,28},{5,29},{6,30},{7,31},{8,16},{9,... | collective-permute-start | bytes 344072 | tf_op jit(solution)/shard_map/ppermute | solution.py:26
  33.8 6.3 %collective-permute-start.16 = (bf16[8,7168]{1,0:T(8,128)(2,1)S(1)}, bf16[8,7168]{1,0:T(8,128)(2,1)S(1)}, u32[]{:S(2)}, u32[]{:S(2)}) collective-permute-start(bf16[8,7168]{1,0:T(8,128)(2,1)S(1)} %shard_map.81), channel_id=1, source_target_pairs={{0,16},{1,17},{2,18},{3,19},{4,20},{5,21},{6,22},{7,23},{8,24},{9,... | collective-permute-start | bytes 344072 | tf_op jit(solution)/shard_map/ppermute | solution.py:26
  40.4 6.7 %collective-permute-start.21 = (bf16[8,7168]{1,0:T(8,128)(2,1)S(1)}, bf16[8,7168]{1,0:T(8,128)(2,1)S(1)}, u32[]{:S(2)}, u32[]{:S(2)}) collective-permute-start(bf16[8,7168]{1,0:T(8,128)(2,1)S(1)} %get-tuple-element.57.refs_0_), channel_id=1, source_target_pairs={{0,6},{1,7},{2,4},{3,5},{4,2},{5,3},{6,0},{7,1},{8,14},{9,15},{10,... | collective-permute-start | bytes 344072 | tf_op jit(solution)/shard_map/ppermute | solution.py:26
  42.9 5.8 %collective-permute-start.20 = (bf16[8,7168]{1,0:T(8,128)(2,1)S(1)}, bf16[8,7168]{1,0:T(8,128)(2,1)S(1)}, u32[]{:S(2)}, u32[]{:S(2)}) collective-permute-start(bf16[8,7168]{1,0:T(8,128)(2,1)S(1)} %get-tuple-element.57.refs_0_), channel_id=1, source_target_pairs={{0,2},{1,5},{2,0},{3,7},{4,6},{5,1},{6,4},{7,3},{8,10},{9,13},{10,... | collective-permute-start | bytes 344072 | tf_op jit(solution)/shard_map/ppermute | solution.py:26
  43.7 5.0 %collective-permute-start.19 = (bf16[8,7168]{1,0:T(8,128)(2,1)S(1)}, bf16[8,7168]{1,0:T(8,128)(2,1)S(1)}, u32[]{:S(2)}, u32[]{:S(2)}) collective-permute-start(bf16[8,7168]{1,0:T(8,128)(2,1)S(1)} %get-tuple-element.57.refs_0_), channel_id=1, source_target_pairs={{0,4},{1,3},{2,6},{3,1},{4,0},{5,7},{6,2},{7,5},{8,12},{9,11},{10,... | collective-permute-start | bytes 344072 | tf_op jit(solution)/shard_map/ppermute | solution.py:26
  43.9 5.3 %collective-permute-start.22 = (bf16[8,7168]{1,0:T(8,128)(2,1)S(1)}, bf16[8,7168]{1,0:T(8,128)(2,1)S(1)}, u32[]{:S(2)}, u32[]{:S(2)}) collective-permute-start(bf16[8,7168]{1,0:T(8,128)(2,1)S(1)} %get-tuple-element.57.refs_0_), channel_id=1, source_target_pairs={{0,1},{1,0},{2,3},{3,2},{4,5},{5,4},{6,7},{7,6},{8,9},{9,8},{10,11... | collective-permute-start | bytes 344072 | tf_op jit(solution)/shard_map/ppermute | solution.py:26
  47.1 2.1 %collective-permute-start.25 = (bf16[8,7168]{1,0:T(8,128)(2,1)S(1)}, bf16[8,7168]{1,0:T(8,128)(2,1)S(1)}, u32[]{:S(2)}, u32[]{:S(2)}) collective-permute-start(bf16[8,7168]{1,0:T(8,128)(2,1)S(1)} %collective-permute-done.21.refs_3_), channel_id=1, source_target_pairs={{0,1},{1,0},{2,3},{3,2},{4,5},{5,4},{6,7},{7,6},{8,9},{9,8},{10,11... | collective-permute-start | bytes 344072 | tf_op jit(solution)/shard_map/ppermute | solution.py:26
  48.7 1.3 %collective-permute-start.24 = (bf16[8,7168]{1,0:T(8,128)(2,1)S(1)}, bf16[8,7168]{1,0:T(8,128)(2,1)S(1)}, u32[]{:S(2)}, u32[]{:S(2)}) collective-permute-start(bf16[8,7168]{1,0:T(8,128)(2,1)S(1)} %collective-permute-done.20.refs_2_), channel_id=1, source_target_pairs={{0,1},{1,0},{2,3},{3,2},{4,5},{5,4},{6,7},{7,6},{8,9},{9,8},{10,11... | collective-permute-start | bytes 344072 | tf_op jit(solution)/shard_map/ppermute | solution.py:26
  48.7 1.5 %collective-permute-start.23 = (bf16[8,7168]{1,0:T(8,128)(2,1)S(1)}, bf16[8,7168]{1,0:T(8,128)(2,1)S(1)}, u32[]{:S(2)}, u32[]{:S(2)}) collective-permute-start(bf16[8,7168]{1,0:T(8,128)(2,1)S(1)} %collective-permute-done.19.refs_1_), channel_id=1, source_target_pairs={{0,1},{1,0},{2,3},{3,2},{4,5},{5,4},{6,7},{7,6},{8,9},{9,8},{10,11... | collective-permute-start | bytes 344072 | tf_op jit(solution)/shard_map/ppermute | solution.py:26
  52.3 1.4 %collective-permute-start.27 = (bf16[8,7168]{1,0:T(8,128)(2,1)S(1)}, bf16[8,7168]{1,0:T(8,128)(2,1)S(1)}, u32[]{:S(2)}, u32[]{:S(2)}) collective-permute-start(bf16[8,7168]{1,0:T(8,128)(2,1)S(1)} %get-tuple-element.62), channel_id=1, source_target_pairs={{0,1},{1,0},{2,3},{3,2},{4,5},{5,4},{6,7},{7,6},{8,9},{9,8},{10,11... | collective-permute-start | bytes 344072 | tf_op jit(solution)/shard_map/ppermute | solution.py:26
  52.7 3.7 %collective-permute-start.29 = (bf16[8,7168]{1,0:T(8,128)(2,1)S(1)}, bf16[8,7168]{1,0:T(8,128)(2,1)S(1)}, u32[]{:S(2)}, u32[]{:S(2)}) collective-permute-start(bf16[8,7168]{1,0:T(8,128)(2,1)S(1)} %get-tuple-element.64), channel_id=1, source_target_pairs={{0,1},{1,0},{2,3},{3,2},{4,5},{5,4},{6,7},{7,6},{8,9},{9,8},{10,11... | collective-permute-start | bytes 344072 | tf_op jit(solution)/shard_map/ppermute | solution.py:26
  52.9 4.4 %collective-permute-start.31 = (bf16[8,7168]{1,0:T(8,128)(2,1)S(1)}, bf16[8,7168]{1,0:T(8,128)(2,1)S(1)}, u32[]{:S(2)}, u32[]{:S(2)}) collective-permute-start(bf16[8,7168]{1,0:T(8,128)(2,1)S(1)} %get-tuple-element.66), channel_id=1, source_target_pairs={{0,1},{1,0},{2,3},{3,2},{4,5},{5,4},{6,7},{7,6},{8,9},{9,8},{10,11... | collective-permute-start | bytes 344072 | tf_op jit(solution)/shard_map/ppermute | solution.py:26
  53.2 5.7 %collective-permute-start.26 = (bf16[8,7168]{1,0:T(8,128)(2,1)S(1)}, bf16[8,7168]{1,0:T(8,128)(2,1)S(1)}, u32[]{:S(2)}, u32[]{:S(2)}) collective-permute-start(bf16[8,7168]{1,0:T(8,128)(2,1)S(1)} %get-tuple-element.60), channel_id=1, source_target_pairs={{0,1},{1,0},{2,3},{3,2},{4,5},{5,4},{6,7},{7,6},{8,9},{9,8},{10,11... | collective-permute-start | bytes 344072 | tf_op jit(solution)/shard_map/ppermute | solution.py:26
  53.7 6.9 %collective-permute-start.28 = (bf16[8,7168]{1,0:T(8,128)(2,1)S(1)}, bf16[8,7168]{1,0:T(8,128)(2,1)S(1)}, u32[]{:S(2)}, u32[]{:S(2)}) collective-permute-start(bf16[8,7168]{1,0:T(8,128)(2,1)S(1)} %shard_map.84), channel_id=1, source_target_pairs={{0,6},{1,7},{2,4},{3,5},{4,2},{5,3},{6,0},{7,1},{8,14},{9,15},{10,... | collective-permute-start | bytes 344072 | tf_op jit(solution)/shard_map/ppermute | solution.py:26
  56.4 6.1 %collective-permute-start.30 = (bf16[8,7168]{1,0:T(8,128)(2,1)S(1)}, bf16[8,7168]{1,0:T(8,128)(2,1)S(1)}, u32[]{:S(2)}, u32[]{:S(2)}) collective-permute-start(bf16[8,7168]{1,0:T(8,128)(2,1)S(1)} %shard_map.85), channel_id=1, source_target_pairs={{0,2},{1,5},{2,0},{3,7},{4,6},{5,1},{6,4},{7,3},{8,10},{9,13},{10,... | collective-permute-start | bytes 344072 | tf_op jit(solution)/shard_map/ppermute | solution.py:26
  57.3 5.2 %collective-permute-start.32 = (bf16[8,7168]{1,0:T(8,128)(2,1)S(1)}, bf16[8,7168]{1,0:T(8,128)(2,1)S(1)}, u32[]{:S(2)}, u32[]{:S(2)}) collective-permute-start(bf16[8,7168]{1,0:T(8,128)(2,1)S(1)} %shard_map.86), channel_id=1, source_target_pairs={{0,4},{1,3},{2,6},{3,1},{4,0},{5,7},{6,2},{7,5},{8,12},{9,11},{10,... | collective-permute-start | bytes 344072 | tf_op jit(solution)/shard_map/ppermute | solution.py:26
  57.5 8.5 %collective-permute-start.18 = (bf16[4,7168]{1,0:T(4,128)(2,1)S(1)}, bf16[4,7168]{1,0:T(4,128)(2,1)S(1)}, u32[]{:S(2)}, u32[]{:S(2)}) collective-permute-start(bf16[4,7168]{1,0:T(4,128)(2,1)S(1)} %get-tuple-element.56), channel_id=1, source_target_pairs={{0,16},{1,17},{2,18},{3,19},{4,20},{5,21},{6,22},{7,23},{8,24},{9,... | collective-permute-start | bytes 172040 | tf_op jit(solution)/shard_map/ppermute | solution.py:26
  62.6 6.8 %collective-permute-start.33 = (bf16[4,7168]{1,0:T(4,128)(2,1)S(1)}, bf16[4,7168]{1,0:T(4,128)(2,1)S(1)}, u32[]{:S(2)}, u32[]{:S(2)}) collective-permute-start(bf16[4,7168]{1,0:T(4,128)(2,1)S(1)} %get-tuple-element.67), channel_id=1, source_target_pairs={{0,24},{1,25},{2,26},{3,27},{4,28},{5,29},{6,30},{7,31},{8,16},{9,... | collective-permute-start | bytes 172040 | tf_op jit(solution)/shard_map/ppermute | solution.py:26
  65.4 4.3 %collective-permute-start.34 = (bf16[4,7168]{1,0:T(4,128)(2,1)S(1)}, bf16[4,7168]{1,0:T(4,128)(2,1)S(1)}, u32[]{:S(2)}, u32[]{:S(2)}) collective-permute-start(bf16[4,7168]{1,0:T(4,128)(2,1)S(1)} %get-tuple-element.68), channel_id=1, source_target_pairs={{0,16},{1,17},{2,18},{3,19},{4,20},{5,21},{6,22},{7,23},{8,24},{9,... | collective-permute-start | bytes 172040 | tf_op jit(solution)/shard_map/ppermute | solution.py:26

commit v14 on v13

--- a/solution.py
+++ b/solution.py
@@ -74,16 +74,14 @@
     )(*[pltpu.with_memory_space_constraint(w, pltpu.HBM) for w in weights])
 
 
-def prepare_kernel(experts, states_hbm, routing_hbm, weight_hbm, out_ref, states_ref, routing_ref, weight_ref, sems):
-    pairs = ((routing_hbm, routing_ref), (weight_hbm, weight_ref), (states_hbm, states_ref))
+def route_kernel(experts, routing_hbm, weight_hbm, out_ref, routing_ref, weight_ref, sems):
+    pairs = ((routing_hbm, routing_ref), (weight_hbm, weight_ref))
     copies = [pltpu.make_async_copy(source, target, sems.at[place]) for place, (source, target) in enumerate(pairs)]
     for copy in copies:
         copy.start()
     for copy in copies:
         copy.wait()
-    rows, dim = states_ref.shape[1:]
-    for span in spans(dim):
-        out_ref[:, span] = states_ref[0, :, span]
+    rows = out_ref.shape[0]
     lane = lax.broadcasted_iota(jnp.int32, (rows, LANES), 1).astype(jnp.float32)
     diagonal = lax.broadcasted_iota(jnp.int32, (rows, rows), 0) == lax.broadcasted_iota(jnp.int32, (rows, rows), 1)
 
@@ -95,19 +93,17 @@
         for k in range(routing_ref.shape[2]):
             column = upright(routing_ref[0, step, k:k + 1, :]) + step * experts
             total += jnp.where(lane == column, upright(weight_ref[0, step, k:k + 1, :]), 0.0)
-    out_ref[:, dim:] = total.astype(jnp.bfloat16)
-
-
-def prepare(experts, states, routing, weight):
-    args = [states, jnp.swapaxes(routing, 2, 3), jnp.swapaxes(weight, 2, 3)]
-    rows, dim = states.shape[1:]
-    (block,) = call(
-        functools.partial(prepare_kernel, experts), [(rows, dim + LANES)],
+    out_ref[...] = total.astype(jnp.bfloat16)
+
+
+def route(experts, routing, weight):
+    args = [jnp.swapaxes(routing, 2, 3), jnp.swapaxes(weight, 2, 3)]
+    return call(
+        functools.partial(route_kernel, experts), [(routing.shape[2], LANES)],
         *[pltpu.with_memory_space_constraint(x, pltpu.HBM) for x in args],
-        in_specs=[pl.BlockSpec(memory_space=pltpu.HBM)] * 3,
-        scratch_shapes=[pltpu.VMEM(x.shape, x.dtype) for x in args] + [pltpu.SemaphoreType.DMA((3,))],
-    )
-    return block
+        in_specs=[pl.BlockSpec(memory_space=pltpu.HBM)] * 2,
+        scratch_shapes=[pltpu.VMEM(x.shape, x.dtype) for x in args] + [pltpu.SemaphoreType.DMA((2,))],
+    )[0]
 
 
 def join_kernel(*refs):
@@ -144,12 +140,12 @@
         out_ref[:, span] = scaled.astype(jnp.bfloat16)
 
 
-def first_kernel(own_ref, far_ref, gain_ref, out_ref, raw_ref):
+def first_kernel(own_ref, far_ref, own_tail_ref, far_tail_ref, gain_ref, out_ref, raw_ref):
     dim = raw_ref.shape[1]
     for span in spans(dim):
         rows = [ref[:, span].astype(jnp.float32) for ref in (own_ref, far_ref)]
         raw_ref[:, span] = jnp.concatenate(rows, axis=0).astype(jnp.bfloat16)
-    tails = [ref[:, dim:].astype(jnp.float32) for ref in (own_ref, far_ref)]
+    tails = [ref[...].astype(jnp.float32) for ref in (own_tail_ref, far_tail_ref)]
     out_ref[:, dim:] = jnp.concatenate(tails, axis=0).astype(jnp.bfloat16)
     normalise(raw_ref, gain_ref, out_ref)
 
@@ -236,14 +232,17 @@
     passes_count = routing.shape[1]
     top, *middle = upper_flips(owners)
 
-    gate, up = load(gate_proj, up_proj)
-    block = prepare(owners // GROUP, states, routing, route_weight)
-    other = exchange(block, top, 0)
-    other, gate, up = lax.optimization_barrier((other, gate, up))
-    pair, raw = call(first_kernel, [(2 * row_dev, dim + LANES), (2 * row_dev, dim)], block, other, norm_gain)
-    pair, down_hbm = lax.optimization_barrier((pair, down_proj))
-    (down,) = load(down_hbm)
     own, tail = states[0], None
+    other = exchange(own, top, 0)
+    lanes = route(owners // GROUP, routing, route_weight)
+    other_lanes = exchange(lanes, top, 0)
+    (gate,) = load(gate_proj)
+    other, other_lanes, gate = lax.optimization_barrier((other, other_lanes, gate))
+    pair, raw = call(
+        first_kernel, [(2 * row_dev, dim + LANES), (2 * row_dev, dim)], own, other, lanes, other_lanes, norm_gain
+    )
+    pair, up_hbm, down_hbm = lax.optimization_barrier((pair, up_proj, down_proj))
+    up, down = load(up_hbm, down_hbm)
     for step_no in range(passes_count):
         rows_a = pair
         for flips in middle:
@@ -251,7 +250,7 @@
         mine = [rows_a] + [exchange(rows_a, flips, 0) for flips in SQUARE]
         near = rows_a
         if step_no == 0:
-            near, down = lax.optimization_barrier((near, down))
+            near, up, down = lax.optimization_barrier((near, up, down))
         fars = [exchange(rows, CORE, 0) for rows in [near] + mine[1:]]
         outs, tail = mlp(step_no, mine + fars, tail, gate, up, down)
 

time: 70.5 us -> 71.1 us (level)
  waiting for transfers between devices: 26.6 us -> 29.1 us
  starting transfers between devices: 31.8 us -> 30.1 us
    ppermute x35 -> x36, waiting for transfers between devices: 26.6 us -> 29.1 us  [exchange(): return lax.ppermute(value, ('segment', 'expert'), pairs)]
    ppermute x35 -> x36, starting transfers between devices: 31.8 us -> 30.1 us  [exchange(): return lax.ppermute(value, ('segment', 'expert'), pairs)]
  transfers between devices with their start and end apart: 35 -> 36, of which waited for: 17 -> 19; matrix products, arithmetic and copies ran while one was open for 0% -> 0% of each run, Pallas kernels for 8% -> 9%
where the time goes in v14:
time: 71.1 us; the launch traced here: 71 us
  starting transfers between devices  30.1 us (42%)
  waiting for transfers between devices  29.1 us (41%)
  Pallas kernels  11.7 us (16%)
    ppermute x36, starting transfers between devices, exchange(): return lax.ppermute(value, ('segment', 'expert'), pairs)  30.1 us
    ppermute x36, waiting for transfers between devices, exchange(): return lax.ppermute(value, ('segment', 'expert'), pairs)  29.1 us
    pallas_call x14, Pallas kernels, call(): pl.pallas_call(kernel, out_shape=[jax.ShapeDtypeStruct(shape, jnp.bfloat1...  6.43 us
    pallas_call x2, Pallas kernels, load(): pl.pallas_call(functools.partial(load_kernel, count), out_shape=[pltpu.VM...  5.22 us
  transfers between devices with their start and end apart: 36, of which 19 were waited for; matrix products, arithmetic and copies ran while one was open for 0% of the time, Pallas kernels for 9%

profile of v14, /device:TPU:0, one launch (start us, length us, event | category | flops | bytes accessed | tf_op | source)
XLA Modules:
  0.0 71.0 jit_solution(18335097150928110126)
XLA Ops:
  0.0 4.0 %collective-permute-start = (bf16[4,7168]{1,0:T(4,128)(2,1)}, bf16[4,7168]{1,0:T(4,128)(2,1)S(1)}, u32[]{:S(2)}, u32[]{:S(2)}) collective-permute-start(bf16[4,7168]{1,0:T(4,128)(2,1)} %bitcast.4), channel_id=1, source_target_pairs={{0,8},{1,9},{2,10},{3,11},{4,12},{5,13},{6,14},{7,15},{8,0},{9,1},... | collective-permute-start | bytes 172040 | tf_op jit(solution)/shard_map/ppermute | solution.py:26
  4.0 0.8 %shard_map.73.own_tail_ref = bf16[4,128]{1,0:T(4,128)(2,1)S(1)} custom-call(s32[1,2,2,4]{3,2,1,0:T(2,128)} %bitcast.6, bf16[1,2,2,4]{3,2,1,0:T(2,128)(2,1)} %bitcast.7), custom_call_target="tpu_custom_call" | custom-call | tf_op jit(solution)/shard_map/pallas_call | solution.py:43
  4.8 0.0 copy-start
  4.9 0.0 copy-start.1
  4.9 0.1 collective-permute-start.1
  4.9 2.0 %shard_map.74.refs_8_.refs_9_ = bf16[1,7168,256]{2,1,0:T(8,128)(2,1)S(1)} custom-call(bf16[1,7168,256]{2,1,0:T(8,128)(2,1)} %refs_0_.1), custom_call_target="tpu_custom_call" | custom-call | bytes 3670016 | tf_op jit(solution)/shard_map/pallas_call | solution.py:64
  7.0 2.4 %collective-permute-done.1.far_tail_ref = bf16[4,128]{1,0:T(4,128)(2,1)S(1)} collective-permute-done((bf16[4,128]{1,0:T(4,128)(2,1)S(1)}, bf16[4,128]{1,0:T(4,128)(2,1)S(1)}, u32[]{:S(2)}, u32[]{:S(2)}) %collective-permute-start.1) | collective-permute-done | bytes 1056 | tf_op jit(solution)/shard_map/ppermute | solution.py:26
  9.4 0.2 shard_map.75
  9.6 2.6 %collective-permute-start.5 = (bf16[8,7296]{1,0:T(8,128)(2,1)S(1)}, bf16[8,7296]{1,0:T(8,128)(2,1)S(1)}, u32[]{:S(2)}, u32[]{:S(2)}) collective-permute-start(bf16[8,7296]{1,0:T(8,128)(2,1)S(1)} %get-tuple-element.48.refs_0_), channel_id=1, source_target_pairs={{0,6},{1,7},{2,4},{3,5},{4,2},{5,3},{6,0},{7,1},{8,14},{9,15},{10,... | collective-permute-start | bytes 350216 | tf_op jit(solution)/shard_map/ppermute | solution.py:26
  12.2 0.5 collective-permute-start.4
  12.7 0.4 collective-permute-start.3
  13.2 3.2 %shard_map.76 = (bf16[1,7168,256]{2,1,0:T(8,128)(2,1)S(1)}, bf16[1,256,7168]{2,1,0:T(8,128)(2,1)S(1)}) custom-call(bf16[1,7168,256]{2,1,0:T(8,128)(2,1)} %refs_0_.2, bf16[1,256,7168]{2,1,0:T(8,128)(2,1)} %refs_1_), custom_call_target="tpu_custom_call" | custom-call | bytes 7340032 | tf_op jit(solution)/shard_map/pallas_call | solution.py:64
  16.3 0.1 collective-permute-start.6
  16.4 0.5 collective-permute-start.9
  16.9 0.1 collective-permute-done.4.refs_2_
  17.0 0.5 collective-permute-done.3.refs_1_
  17.5 0.0 collective-permute-start.7
  17.5 0.2 collective-permute-done.6.refs_4_
  17.7 0.2 collective-permute-done.9.refs_7_
  17.9 0.4 collective-permute-done.8.refs_6_
  18.4 0.5 collective-permute-done.7.refs_5_
  18.9 2.1 %shard_map.77 = (bf16[8,7168]{1,0:T(8,128)(2,1)S(1)}, bf16[8,7168]{1,0:T(8,128)(2,1)S(1)}, bf16[8,7168]{1,0:T(8,128)(2,1)S(1)}, bf16[8,7168]{1,0:T(8,128)(2,1)S(...) custom-call(bf16[8,7296]{1,0:T(8,128)(2,1)S(1)} %get-tuple-element.4, ...), custom_call_target="tpu_custom_call" | custom-call | flops 704643072 | bytes 11010048 | tf_op jit(solution)/shard_map/pallas_call | solution.py:43
  21.0 0.2 collective-permute-start.11
  21.2 0.4 collective-permute-start.13
  21.6 0.2 collective-permute-start.15
  21.7 0.4 collective-permute-start.10
  22.1 0.3 collective-permute-done.11.refs_1_
  22.4 2.2 %collective-permute-start.12 = (bf16[8,7168]{1,0:T(8,128)(2,1)S(1)}, bf16[8,7168]{1,0:T(8,128)(2,1)S(1)}, u32[]{:S(2)}, u32[]{:S(2)}) collective-permute-start(bf16[8,7168]{1,0:T(8,128)(2,1)S(1)} %shard_map.78), channel_id=1, source_target_pairs={{0,6},{1,7},{2,4},{3,5},{4,2},{5,3},{6,0},{7,1},{8,14},{9,15},{10,... | collective-permute-start | bytes 344072 | tf_op jit(solution)/shard_map/ppermute | solution.py:26
  24.6 0.6 collective-permute-start.14
  25.2 0.9 %collective-permute-start.16 = (bf16[8,7168]{1,0:T(8,128)(2,1)S(1)}, bf16[8,7168]{1,0:T(8,128)(2,1)S(1)}, u32[]{:S(2)}, u32[]{:S(2)}) collective-permute-start(bf16[8,7168]{1,0:T(8,128)(2,1)S(1)} %shard_map.80), channel_id=1, source_target_pairs={{0,4},{1,3},{2,6},{3,1},{4,0},{5,7},{6,2},{7,5},{8,12},{9,11},{10,... | collective-permute-start | bytes 344072 | tf_op jit(solution)/shard_map/ppermute | solution.py:26
  26.2 1.5 %collective-permute-start.2 = (bf16[8,7168]{1,0:T(8,128)(2,1)S(1)}, bf16[8,7168]{1,0:T(8,128)(2,1)S(1)}, u32[]{:S(2)}, u32[]{:S(2)}) collective-permute-start(bf16[8,7168]{1,0:T(8,128)(2,1)S(1)} %get-tuple-element.41), channel_id=1, source_target_pairs={{0,16},{1,17},{2,18},{3,19},{4,20},{5,21},{6,22},{7,23},{8,24},{9,... | collective-permute-start | bytes 344072 | tf_op jit(solution)/shard_map/ppermute | solution.py:26
  27.7 1.7 %collective-permute-done.12.refs_2_ = bf16[8,7168]{1,0:T(8,128)(2,1)S(1)} collective-permute-done((bf16[8,7168]{1,0:T(8,128)(2,1)S(1)}, bf16[8,7168]{1,0:T(8,128)(2,1)S(1)}, u32[]{:S(2)}, u32[]{:S(2)}) %collective-permute-start.12) | collective-permute-done | bytes 114720 | tf_op jit(solution)/shard_map/ppermute | solution.py:26
  29.4 1.7 %collective-permute-done.14.refs_3_ = bf16[8,7168]{1,0:T(8,128)(2,1)S(1)} collective-permute-done((bf16[8,7168]{1,0:T(8,128)(2,1)S(1)}, bf16[8,7168]{1,0:T(8,128)(2,1)S(1)}, u32[]{:S(2)}, u32[]{:S(2)}) %collective-permute-start.14) | collective-permute-done | bytes 114720 | tf_op jit(solution)/shard_map/ppermute | solution.py:26
  31.1 0.0 collective-permute-done.16.refs_4_
  31.1 0.1 shard_map.81
  31.2 2.2 %collective-permute-start.18 = (bf16[8,7168]{1,0:T(8,128)(2,1)S(1)}, bf16[8,7168]{1,0:T(8,128)(2,1)S(1)}, u32[]{:S(2)}, u32[]{:S(2)}) collective-permute-start(bf16[8,7168]{1,0:T(8,128)(2,1)S(1)} %shard_map.81), channel_id=1, source_target_pairs={{0,24},{1,25},{2,26},{3,27},{4,28},{5,29},{6,30},{7,31},{8,16},{9,... | collective-permute-start | bytes 344072 | tf_op jit(solution)/shard_map/ppermute | solution.py:26
  33.4 0.5 collective-permute-start.17
  33.9 6.5 %collective-permute-done.18.far_ref = bf16[8,7168]{1,0:T(8,128)(2,1)S(1)} collective-permute-done((bf16[8,7168]{1,0:T(8,128)(2,1)S(1)}, bf16[8,7168]{1,0:T(8,128)(2,1)S(1)}, u32[]{:S(2)}, u32[]{:S(2)}) %collective-permute-start.18) | collective-permute-done | bytes 114720 | tf_op jit(solution)/shard_map/ppermute | solution.py:26
  40.4 0.2 shard_map.82
  40.7 2.6 %collective-permute-start.22 = (bf16[8,7168]{1,0:T(8,128)(2,1)S(1)}, bf16[8,7168]{1,0:T(8,128)(2,1)S(1)}, u32[]{:S(2)}, u32[]{:S(2)}) collective-permute-start(bf16[8,7168]{1,0:T(8,128)(2,1)S(1)} %get-tuple-element.61.refs_0_), channel_id=1, source_target_pairs={{0,6},{1,7},{2,4},{3,5},{4,2},{5,3},{6,0},{7,1},{8,14},{9,15},{10,... | collective-permute-start | bytes 344072 | tf_op jit(solution)/shard_map/ppermute | solution.py:26
  43.3 0.5 collective-permute-start.21
  43.8 0.4 collective-permute-start.20
  44.2 3.4 %collective-permute-done.22.refs_3_ = bf16[8,7168]{1,0:T(8,128)(2,1)S(1)} collective-permute-done((bf16[8,7168]{1,0:T(8,128)(2,1)S(1)}, bf16[8,7168]{1,0:T(8,128)(2,1)S(1)}, u32[]{:S(2)}, u32[]{:S(2)}) %collective-permute-start.22) | collective-permute-done | bytes 114720 | tf_op jit(solution)/shard_map/ppermute | solution.py:26
  47.6 1.4 %collective-permute-done.21.refs_2_ = bf16[8,7168]{1,0:T(8,128)(2,1)S(1)} collective-permute-done((bf16[8,7168]{1,0:T(8,128)(2,1)S(1)}, bf16[8,7168]{1,0:T(8,128)(2,1)S(1)}, u32[]{:S(2)}, u32[]{:S(2)}) %collective-permute-start.21) | collective-permute-done | bytes 114720 | tf_op jit(solution)/shard_map/ppermute | solution.py:26
  49.1 0.5 collective-permute-start.24
  49.6 0.8 %collective-permute-done.25.refs_6_ = bf16[8,7168]{1,0:T(8,128)(2,1)S(1)} collective-permute-done((bf16[8,7168]{1,0:T(8,128)(2,1)S(1)}, bf16[8,7168]{1,0:T(8,128)(2,1)S(1)}, u32[]{:S(2)}, u32[]{:S(2)}) %collective-permute-start.25) | collective-permute-done | bytes 114720 | tf_op jit(solution)/shard_map/ppermute | solution.py:26
  50.4 0.2 collective-permute-done.24.refs_5_
  50.6 2.1 %shard_map.83 = (bf16[8,7168]{1,0:T(8,128)(2,1)S(1)}, bf16[8,7168]{1,0:T(8,128)(2,1)S(1)}, bf16[8,7168]{1,0:T(8,128)(2,1)S(1)}, bf16[8,7168]{1,0:T(8,128)(2,1)S(...) custom-call(bf16[8,7168]{1,0:T(8,128)(2,1)S(1)} %get-tuple-element.6, ...), custom_call_target="tpu_custom_call" | custom-call | flops 704643072 | bytes 11010048 | tf_op jit(solution)/shard_map/pallas_call | solution.py:43
  52.7 0.4 collective-permute-start.28
  53.1 0.2 collective-permute-start.30
  53.3 0.3 collective-permute-start.32
  53.6 0.2 collective-permute-start.27
  53.8 0.3 collective-permute-done.28.refs_1_
  54.1 2.7 %collective-permute-start.29 = (bf16[8,7168]{1,0:T(8,128)(2,1)S(1)}, bf16[8,7168]{1,0:T(8,128)(2,1)S(1)}, u32[]{:S(2)}, u32[]{:S(2)}) collective-permute-start(bf16[8,7168]{1,0:T(8,128)(2,1)S(1)} %shard_map.84), channel_id=1, source_target_pairs={{0,6},{1,7},{2,4},{3,5},{4,2},{5,3},{6,0},{7,1},{8,14},{9,15},{10,... | collective-permute-start | bytes 344072 | tf_op jit(solution)/shard_map/ppermute | solution.py:26
  56.8 0.6 collective-permute-start.31
  57.5 0.4 collective-permute-start.33
  57.9 1.2 %collective-permute-start.19 = (bf16[4,7168]{1,0:T(4,128)(2,1)S(1)}, bf16[4,7168]{1,0:T(4,128)(2,1)S(1)}, u32[]{:S(2)}, u32[]{:S(2)}) collective-permute-start(bf16[4,7168]{1,0:T(4,128)(2,1)S(1)} %get-tuple-element.60), channel_id=1, source_target_pairs={{0,16},{1,17},{2,18},{3,19},{4,20},{5,21},{6,22},{7,23},{8,24},{9,... | collective-permute-start | bytes 172040 | tf_op jit(solution)/shard_map/ppermute | solution.py:26
  59.1 2.0 %collective-permute-done.29.refs_2_ = bf16[8,7168]{1,0:T(8,128)(2,1)S(1)} collective-permute-done((bf16[8,7168]{1,0:T(8,128)(2,1)S(1)}, bf16[8,7168]{1,0:T(8,128)(2,1)S(1)}, u32[]{:S(2)}, u32[]{:S(2)}) %collective-permute-start.29) | collective-permute-done | bytes 114720 | tf_op jit(solution)/shard_map/ppermute | solution.py:26
  61.0 1.9 %collective-permute-done.31.refs_3_ = bf16[8,7168]{1,0:T(8,128)(2,1)S(1)} collective-permute-done((bf16[8,7168]{1,0:T(8,128)(2,1)S(1)}, bf16[8,7168]{1,0:T(8,128)(2,1)S(1)}, u32[]{:S(2)}, u32[]{:S(2)}) %collective-permute-start.31) | collective-permute-done | bytes 114720 | tf_op jit(solution)/shard_map/ppermute | solution.py:26
  62.9 0.1 shard_map.87
  63.0 2.0 %collective-permute-start.34 = (bf16[4,7168]{1,0:T(4,128)(2,1)S(1)}, bf16[4,7168]{1,0:T(4,128)(2,1)S(1)}, u32[]{:S(2)}, u32[]{:S(2)}) collective-permute-start(bf16[4,7168]{1,0:T(4,128)(2,1)S(1)} %get-tuple-element.71), channel_id=1, source_target_pairs={{0,24},{1,25},{2,26},{3,27},{4,28},{5,29},{6,30},{7,31},{8,16},{9,... | collective-permute-start | bytes 172040 | tf_op jit(solution)/shard_map/ppermute | solution.py:26
  65.0 0.8 %collective-permute-start.35 = (bf16[4,7168]{1,0:T(4,128)(2,1)S(1)}, bf16[4,7168]{1,0:T(4,128)(2,1)S(1)}, u32[]{:S(2)}, u32[]{:S(2)}) collective-permute-start(bf16[4,7168]{1,0:T(4,128)(2,1)S(1)} %get-tuple-element.72), channel_id=1, source_target_pairs={{0,16},{1,17},{2,18},{3,19},{4,20},{5,21},{6,22},{7,23},{8,24},{9,... | collective-permute-start | bytes 172040 | tf_op jit(solution)/shard_map/ppermute | solution.py:26
  65.8 4.5 %collective-permute-done.34.refs_1_ = bf16[4,7168]{1,0:T(4,128)(2,1)S(1)} collective-permute-done((bf16[4,7168]{1,0:T(4,128)(2,1)S(1)}, bf16[4,7168]{1,0:T(4,128)(2,1)S(1)}, u32[]{:S(2)}, u32[]{:S(2)}) %collective-permute-start.34) | collective-permute-done | bytes 57376 | tf_op jit(solution)/shard_map/ppermute | solution.py:26
  70.3 0.7 shard_map.88
  (28 shorter events, 0.2 us)
Async XLA Ops:
  0.0 9.4 %collective-permute-start = (bf16[4,7168]{1,0:T(4,128)(2,1)}, bf16[4,7168]{1,0:T(4,128)(2,1)S(1)}, u32[]{:S(2)}, u32[]{:S(2)}) collective-permute-start(bf16[4,7168]{1,0:T(4,128)(2,1)} %bitcast.4), channel_id=1, source_target_pairs={{0,8},{1,9},{2,10},{3,11},{4,12},{5,13},{6,14},{7,15},{8,0},{9,1},... | collective-permute-start | bytes 172040 | tf_op jit(solution)/shard_map/ppermute | solution.py:26
  4.8 4.6 %copy-start = (f32[1,7168]{1,0:T(1,128)S(1)}, f32[1,7168]{1,0:T(1,128)}, u32[]{:S(2)}) copy-start(f32[1,7168]{1,0:T(1,128)} %gain_ref.3) | copy-start | bytes 86020
  4.9 4.6 %copy-start.1 = (bf16[1,4,7168]{2,1,0:T(4,128)(2,1)S(1)}, bf16[1,4,7168]{2,1,0:T(4,128)(2,1)}, u32[]{:S(2)}) copy-start(bf16[1,4,7168]{2,1,0:T(4,128)(2,1)} %param.7) | copy-start | bytes 172036
  4.9 4.5 %collective-permute-start.1 = (bf16[4,128]{1,0:T(4,128)(2,1)S(1)}, bf16[4,128]{1,0:T(4,128)(2,1)S(1)}, u32[]{:S(2)}, u32[]{:S(2)}) collective-permute-start(bf16[4,128]{1,0:T(4,128)(2,1)S(1)} %shard_map.73.own_tail_ref), channel_id=1, source_target_pairs={{0,8},{1,9},{2,10},{3,11},{4,12},{5,13},{6,14},{7,15},{8,0},{9,1},... | collective-permute-start | bytes 3080 | tf_op jit(solution)/shard_map/ppermute | solution.py:26
  9.6 6.8 %collective-permute-start.5 = (bf16[8,7296]{1,0:T(8,128)(2,1)S(1)}, bf16[8,7296]{1,0:T(8,128)(2,1)S(1)}, u32[]{:S(2)}, u32[]{:S(2)}) collective-permute-start(bf16[8,7296]{1,0:T(8,128)(2,1)S(1)} %get-tuple-element.48.refs_0_), channel_id=1, source_target_pairs={{0,6},{1,7},{2,4},{3,5},{4,2},{5,3},{6,0},{7,1},{8,14},{9,15},{10,... | collective-permute-start | bytes 350216 | tf_op jit(solution)/shard_map/ppermute | solution.py:26
  12.2 4.8 %collective-permute-start.4 = (bf16[8,7296]{1,0:T(8,128)(2,1)S(1)}, bf16[8,7296]{1,0:T(8,128)(2,1)S(1)}, u32[]{:S(2)}, u32[]{:S(2)}) collective-permute-start(bf16[8,7296]{1,0:T(8,128)(2,1)S(1)} %get-tuple-element.48.refs_0_), channel_id=1, source_target_pairs={{0,2},{1,5},{2,0},{3,7},{4,6},{5,1},{6,4},{7,3},{8,10},{9,13},{10,... | collective-permute-start | bytes 350216 | tf_op jit(solution)/shard_map/ppermute | solution.py:26
  12.7 4.8 %collective-permute-start.3 = (bf16[8,7296]{1,0:T(8,128)(2,1)S(1)}, bf16[8,7296]{1,0:T(8,128)(2,1)S(1)}, u32[]{:S(2)}, u32[]{:S(2)}) collective-permute-start(bf16[8,7296]{1,0:T(8,128)(2,1)S(1)} %get-tuple-element.48.refs_0_), channel_id=1, source_target_pairs={{0,4},{1,3},{2,6},{3,1},{4,0},{5,7},{6,2},{7,5},{8,12},{9,11},{10,... | collective-permute-start | bytes 350216 | tf_op jit(solution)/shard_map/ppermute | solution.py:26
  16.3 1.4 %collective-permute-start.6 = (bf16[8,7296]{1,0:T(8,128)(2,1)S(1)}, bf16[8,7296]{1,0:T(8,128)(2,1)S(1)}, u32[]{:S(2)}, u32[]{:S(2)}) collective-permute-start(bf16[8,7296]{1,0:T(8,128)(2,1)S(1)} %get-tuple-element.48.refs_0_), channel_id=1, source_target_pairs={{0,1},{1,0},{2,3},{3,2},{4,5},{5,4},{6,7},{7,6},{8,9},{9,8},{10,11... | collective-permute-start | bytes 350216 | tf_op jit(solution)/shard_map/ppermute | solution.py:26
  16.4 1.5 %collective-permute-start.9 = (bf16[8,7296]{1,0:T(8,128)(2,1)S(1)}, bf16[8,7296]{1,0:T(8,128)(2,1)S(1)}, u32[]{:S(2)}, u32[]{:S(2)}) collective-permute-start(bf16[8,7296]{1,0:T(8,128)(2,1)S(1)} %collective-permute-done.5.refs_3_), channel_id=1, source_target_pairs={{0,1},{1,0},{2,3},{3,2},{4,5},{5,4},{6,7},{7,6},{8,9},{9,8},{10,11... | collective-permute-start | bytes 350216 | tf_op jit(solution)/shard_map/ppermute | solution.py:26
  17.0 1.3 %collective-permute-start.8 = (bf16[8,7296]{1,0:T(8,128)(2,1)S(1)}, bf16[8,7296]{1,0:T(8,128)(2,1)S(1)}, u32[]{:S(2)}, u32[]{:S(2)}) collective-permute-start(bf16[8,7296]{1,0:T(8,128)(2,1)S(1)} %collective-permute-done.4.refs_2_), channel_id=1, source_target_pairs={{0,1},{1,0},{2,3},{3,2},{4,5},{5,4},{6,7},{7,6},{8,9},{9,8},{10,11... | collective-permute-start | bytes 350216 | tf_op jit(solution)/shard_map/ppermute | solution.py:26
  17.5 1.3 %collective-permute-start.7 = (bf16[8,7296]{1,0:T(8,128)(2,1)S(1)}, bf16[8,7296]{1,0:T(8,128)(2,1)S(1)}, u32[]{:S(2)}, u32[]{:S(2)}) collective-permute-start(bf16[8,7296]{1,0:T(8,128)(2,1)S(1)} %collective-permute-done.3.refs_1_), channel_id=1, source_target_pairs={{0,1},{1,0},{2,3},{3,2},{4,5},{5,4},{6,7},{7,6},{8,9},{9,8},{10,11... | collective-permute-start | bytes 350216 | tf_op jit(solution)/shard_map/ppermute | solution.py:26
  21.0 1.4 %collective-permute-start.11 = (bf16[8,7168]{1,0:T(8,128)(2,1)S(1)}, bf16[8,7168]{1,0:T(8,128)(2,1)S(1)}, u32[]{:S(2)}, u32[]{:S(2)}) collective-permute-start(bf16[8,7168]{1,0:T(8,128)(2,1)S(1)} %get-tuple-element.55), channel_id=1, source_target_pairs={{0,1},{1,0},{2,3},{3,2},{4,5},{5,4},{6,7},{7,6},{8,9},{9,8},{10,11... | collective-permute-start | bytes 344072 | tf_op jit(solution)/shard_map/ppermute | solution.py:26
  21.2 3.4 %collective-permute-start.13 = (bf16[8,7168]{1,0:T(8,128)(2,1)S(1)}, bf16[8,7168]{1,0:T(8,128)(2,1)S(1)}, u32[]{:S(2)}, u32[]{:S(2)}) collective-permute-start(bf16[8,7168]{1,0:T(8,128)(2,1)S(1)} %get-tuple-element.57), channel_id=1, source_target_pairs={{0,1},{1,0},{2,3},{3,2},{4,5},{5,4},{6,7},{7,6},{8,9},{9,8},{10,11... | collective-permute-start | bytes 344072 | tf_op jit(solution)/shard_map/ppermute | solution.py:26
  21.6 3.6 %collective-permute-start.15 = (bf16[8,7168]{1,0:T(8,128)(2,1)S(1)}, bf16[8,7168]{1,0:T(8,128)(2,1)S(1)}, u32[]{:S(2)}, u32[]{:S(2)}) collective-permute-start(bf16[8,7168]{1,0:T(8,128)(2,1)S(1)} %get-tuple-element.59), channel_id=1, source_target_pairs={{0,1},{1,0},{2,3},{3,2},{4,5},{5,4},{6,7},{7,6},{8,9},{9,8},{10,11... | collective-permute-start | bytes 344072 | tf_op jit(solution)/shard_map/ppermute | solution.py:26
  21.7 5.9 %collective-permute-start.10 = (bf16[8,7168]{1,0:T(8,128)(2,1)S(1)}, bf16[8,7168]{1,0:T(8,128)(2,1)S(1)}, u32[]{:S(2)}, u32[]{:S(2)}) collective-permute-start(bf16[8,7168]{1,0:T(8,128)(2,1)S(1)} %get-tuple-element.53), channel_id=1, source_target_pairs={{0,1},{1,0},{2,3},{3,2},{4,5},{5,4},{6,7},{7,6},{8,9},{9,8},{10,11... | collective-permute-start | bytes 344072 | tf_op jit(solution)/shard_map/ppermute | solution.py:26
  22.4 7.0 %collective-permute-start.12 = (bf16[8,7168]{1,0:T(8,128)(2,1)S(1)}, bf16[8,7168]{1,0:T(8,128)(2,1)S(1)}, u32[]{:S(2)}, u32[]{:S(2)}) collective-permute-start(bf16[8,7168]{1,0:T(8,128)(2,1)S(1)} %shard_map.78), channel_id=1, source_target_pairs={{0,6},{1,7},{2,4},{3,5},{4,2},{5,3},{6,0},{7,1},{8,14},{9,15},{10,... | collective-permute-start | bytes 344072 | tf_op jit(solution)/shard_map/ppermute | solution.py:26
  24.6 6.5 %collective-permute-start.14 = (bf16[8,7168]{1,0:T(8,128)(2,1)S(1)}, bf16[8,7168]{1,0:T(8,128)(2,1)S(1)}, u32[]{:S(2)}, u32[]{:S(2)}) collective-permute-start(bf16[8,7168]{1,0:T(8,128)(2,1)S(1)} %shard_map.79), channel_id=1, source_target_pairs={{0,2},{1,5},{2,0},{3,7},{4,6},{5,1},{6,4},{7,3},{8,10},{9,13},{10,... | collective-permute-start | bytes 344072 | tf_op jit(solution)/shard_map/ppermute | solution.py:26
  25.2 5.9 %collective-permute-start.16 = (bf16[8,7168]{1,0:T(8,128)(2,1)S(1)}, bf16[8,7168]{1,0:T(8,128)(2,1)S(1)}, u32[]{:S(2)}, u32[]{:S(2)}) collective-permute-start(bf16[8,7168]{1,0:T(8,128)(2,1)S(1)} %shard_map.80), channel_id=1, source_target_pairs={{0,4},{1,3},{2,6},{3,1},{4,0},{5,7},{6,2},{7,5},{8,12},{9,11},{10,... | collective-permute-start | bytes 344072 | tf_op jit(solution)/shard_map/ppermute | solution.py:26
  26.2 7.7 %collective-permute-start.2 = (bf16[8,7168]{1,0:T(8,128)(2,1)S(1)}, bf16[8,7168]{1,0:T(8,128)(2,1)S(1)}, u32[]{:S(2)}, u32[]{:S(2)}) collective-permute-start(bf16[8,7168]{1,0:T(8,128)(2,1)S(1)} %get-tuple-element.41), channel_id=1, source_target_pairs={{0,16},{1,17},{2,18},{3,19},{4,20},{5,21},{6,22},{7,23},{8,24},{9,... | collective-permute-start | bytes 344072 | tf_op jit(solution)/shard_map/ppermute | solution.py:26
  31.2 9.3 %collective-permute-start.18 = (bf16[8,7168]{1,0:T(8,128)(2,1)S(1)}, bf16[8,7168]{1,0:T(8,128)(2,1)S(1)}, u32[]{:S(2)}, u32[]{:S(2)}) collective-permute-start(bf16[8,7168]{1,0:T(8,128)(2,1)S(1)} %shard_map.81), channel_id=1, source_target_pairs={{0,24},{1,25},{2,26},{3,27},{4,28},{5,29},{6,30},{7,31},{8,16},{9,... | collective-permute-start | bytes 344072 | tf_op jit(solution)/shard_map/ppermute | solution.py:26
  33.4 7.1 %collective-permute-start.17 = (bf16[8,7168]{1,0:T(8,128)(2,1)S(1)}, bf16[8,7168]{1,0:T(8,128)(2,1)S(1)}, u32[]{:S(2)}, u32[]{:S(2)}) collective-permute-start(bf16[8,7168]{1,0:T(8,128)(2,1)S(1)} %shard_map.81), channel_id=1, source_target_pairs={{0,16},{1,17},{2,18},{3,19},{4,20},{5,21},{6,22},{7,23},{8,24},{9,... | collective-permute-start | bytes 344072 | tf_op jit(solution)/shard_map/ppermute | solution.py:26
  40.7 7.0 %collective-permute-start.22 = (bf16[8,7168]{1,0:T(8,128)(2,1)S(1)}, bf16[8,7168]{1,0:T(8,128)(2,1)S(1)}, u32[]{:S(2)}, u32[]{:S(2)}) collective-permute-start(bf16[8,7168]{1,0:T(8,128)(2,1)S(1)} %get-tuple-element.61.refs_0_), channel_id=1, source_target_pairs={{0,6},{1,7},{2,4},{3,5},{4,2},{5,3},{6,0},{7,1},{8,14},{9,15},{10,... | collective-permute-start | bytes 344072 | tf_op jit(solution)/shard_map/ppermute | solution.py:26
  43.3 5.8 %collective-permute-start.21 = (bf16[8,7168]{1,0:T(8,128)(2,1)S(1)}, bf16[8,7168]{1,0:T(8,128)(2,1)S(1)}, u32[]{:S(2)}, u32[]{:S(2)}) collective-permute-start(bf16[8,7168]{1,0:T(8,128)(2,1)S(1)} %get-tuple-element.61.refs_0_), channel_id=1, source_target_pairs={{0,2},{1,5},{2,0},{3,7},{4,6},{5,1},{6,4},{7,3},{8,10},{9,13},{10,... | collective-permute-start | bytes 344072 | tf_op jit(solution)/shard_map/ppermute | solution.py:26
  43.8 5.3 %collective-permute-start.20 = (bf16[8,7168]{1,0:T(8,128)(2,1)S(1)}, bf16[8,7168]{1,0:T(8,128)(2,1)S(1)}, u32[]{:S(2)}, u32[]{:S(2)}) collective-permute-start(bf16[8,7168]{1,0:T(8,128)(2,1)S(1)} %get-tuple-element.61.refs_0_), channel_id=1, source_target_pairs={{0,4},{1,3},{2,6},{3,1},{4,0},{5,7},{6,2},{7,5},{8,12},{9,11},{10,... | collective-permute-start | bytes 344072 | tf_op jit(solution)/shard_map/ppermute | solution.py:26
  44.2 5.4 %collective-permute-start.23 = (bf16[8,7168]{1,0:T(8,128)(2,1)S(1)}, bf16[8,7168]{1,0:T(8,128)(2,1)S(1)}, u32[]{:S(2)}, u32[]{:S(2)}) collective-permute-start(bf16[8,7168]{1,0:T(8,128)(2,1)S(1)} %get-tuple-element.61.refs_0_), channel_id=1, source_target_pairs={{0,1},{1,0},{2,3},{3,2},{4,5},{5,4},{6,7},{7,6},{8,9},{9,8},{10,11... | collective-permute-start | bytes 344072 | tf_op jit(solution)/shard_map/ppermute | solution.py:26
  47.6 2.0 %collective-permute-start.26 = (bf16[8,7168]{1,0:T(8,128)(2,1)S(1)}, bf16[8,7168]{1,0:T(8,128)(2,1)S(1)}, u32[]{:S(2)}, u32[]{:S(2)}) collective-permute-start(bf16[8,7168]{1,0:T(8,128)(2,1)S(1)} %collective-permute-done.22.refs_3_), channel_id=1, source_target_pairs={{0,1},{1,0},{2,3},{3,2},{4,5},{5,4},{6,7},{7,6},{8,9},{9,8},{10,11... | collective-permute-start | bytes 344072 | tf_op jit(solution)/shard_map/ppermute | solution.py:26
  49.1 1.3 %collective-permute-start.25 = (bf16[8,7168]{1,0:T(8,128)(2,1)S(1)}, bf16[8,7168]{1,0:T(8,128)(2,1)S(1)}, u32[]{:S(2)}, u32[]{:S(2)}) collective-permute-start(bf16[8,7168]{1,0:T(8,128)(2,1)S(1)} %collective-permute-done.21.refs_2_), channel_id=1, source_target_pairs={{0,1},{1,0},{2,3},{3,2},{4,5},{5,4},{6,7},{7,6},{8,9},{9,8},{10,11... | collective-permute-start | bytes 344072 | tf_op jit(solution)/shard_map/ppermute | solution.py:26
  49.1 1.5 %collective-permute-start.24 = (bf16[8,7168]{1,0:T(8,128)(2,1)S(1)}, bf16[8,7168]{1,0:T(8,128)(2,1)S(1)}, u32[]{:S(2)}, u32[]{:S(2)}) collective-permute-start(bf16[8,7168]{1,0:T(8,128)(2,1)S(1)} %collective-permute-done.20.refs_1_), channel_id=1, source_target_pairs={{0,1},{1,0},{2,3},{3,2},{4,5},{5,4},{6,7},{7,6},{8,9},{9,8},{10,11... | collective-permute-start | bytes 344072 | tf_op jit(solution)/shard_map/ppermute | solution.py:26
  52.7 1.4 %collective-permute-start.28 = (bf16[8,7168]{1,0:T(8,128)(2,1)S(1)}, bf16[8,7168]{1,0:T(8,128)(2,1)S(1)}, u32[]{:S(2)}, u32[]{:S(2)}) collective-permute-start(bf16[8,7168]{1,0:T(8,128)(2,1)S(1)} %get-tuple-element.66), channel_id=1, source_target_pairs={{0,1},{1,0},{2,3},{3,2},{4,5},{5,4},{6,7},{7,6},{8,9},{9,8},{10,11... | collective-permute-start | bytes 344072 | tf_op jit(solution)/shard_map/ppermute | solution.py:26
  53.1 3.7 %collective-permute-start.30 = (bf16[8,7168]{1,0:T(8,128)(2,1)S(1)}, bf16[8,7168]{1,0:T(8,128)(2,1)S(1)}, u32[]{:S(2)}, u32[]{:S(2)}) collective-permute-start(bf16[8,7168]{1,0:T(8,128)(2,1)S(1)} %get-tuple-element.68), channel_id=1, source_target_pairs={{0,1},{1,0},{2,3},{3,2},{4,5},{5,4},{6,7},{7,6},{8,9},{9,8},{10,11... | collective-permute-start | bytes 344072 | tf_op jit(solution)/shard_map/ppermute | solution.py:26
  53.3 4.1 %collective-permute-start.32 = (bf16[8,7168]{1,0:T(8,128)(2,1)S(1)}, bf16[8,7168]{1,0:T(8,128)(2,1)S(1)}, u32[]{:S(2)}, u32[]{:S(2)}) collective-permute-start(bf16[8,7168]{1,0:T(8,128)(2,1)S(1)} %get-tuple-element.70), channel_id=1, source_target_pairs={{0,1},{1,0},{2,3},{3,2},{4,5},{5,4},{6,7},{7,6},{8,9},{9,8},{10,11... | collective-permute-start | bytes 344072 | tf_op jit(solution)/shard_map/ppermute | solution.py:26
  53.6 5.5 %collective-permute-start.27 = (bf16[8,7168]{1,0:T(8,128)(2,1)S(1)}, bf16[8,7168]{1,0:T(8,128)(2,1)S(1)}, u32[]{:S(2)}, u32[]{:S(2)}) collective-permute-start(bf16[8,7168]{1,0:T(8,128)(2,1)S(1)} %get-tuple-element.64), channel_id=1, source_target_pairs={{0,1},{1,0},{2,3},{3,2},{4,5},{5,4},{6,7},{7,6},{8,9},{9,8},{10,11... | collective-permute-start | bytes 344072 | tf_op jit(solution)/shard_map/ppermute | solution.py:26
  54.1 6.9 %collective-permute-start.29 = (bf16[8,7168]{1,0:T(8,128)(2,1)S(1)}, bf16[8,7168]{1,0:T(8,128)(2,1)S(1)}, u32[]{:S(2)}, u32[]{:S(2)}) collective-permute-start(bf16[8,7168]{1,0:T(8,128)(2,1)S(1)} %shard_map.84), channel_id=1, source_target_pairs={{0,6},{1,7},{2,4},{3,5},{4,2},{5,3},{6,0},{7,1},{8,14},{9,15},{10,... | collective-permute-start | bytes 344072 | tf_op jit(solution)/shard_map/ppermute | solution.py:26
  56.8 6.1 %collective-permute-start.31 = (bf16[8,7168]{1,0:T(8,128)(2,1)S(1)}, bf16[8,7168]{1,0:T(8,128)(2,1)S(1)}, u32[]{:S(2)}, u32[]{:S(2)}) collective-permute-start(bf16[8,7168]{1,0:T(8,128)(2,1)S(1)} %shard_map.85), channel_id=1, source_target_pairs={{0,2},{1,5},{2,0},{3,7},{4,6},{5,1},{6,4},{7,3},{8,10},{9,13},{10,... | collective-permute-start | bytes 344072 | tf_op jit(solution)/shard_map/ppermute | solution.py:26
  57.5 5.5 %collective-permute-start.33 = (bf16[8,7168]{1,0:T(8,128)(2,1)S(1)}, bf16[8,7168]{1,0:T(8,128)(2,1)S(1)}, u32[]{:S(2)}, u32[]{:S(2)}) collective-permute-start(bf16[8,7168]{1,0:T(8,128)(2,1)S(1)} %shard_map.86), channel_id=1, source_target_pairs={{0,4},{1,3},{2,6},{3,1},{4,0},{5,7},{6,2},{7,5},{8,12},{9,11},{10,... | collective-permute-start | bytes 344072 | tf_op jit(solution)/shard_map/ppermute | solution.py:26
  57.9 8.0 %collective-permute-start.19 = (bf16[4,7168]{1,0:T(4,128)(2,1)S(1)}, bf16[4,7168]{1,0:T(4,128)(2,1)S(1)}, u32[]{:S(2)}, u32[]{:S(2)}) collective-permute-start(bf16[4,7168]{1,0:T(4,128)(2,1)S(1)} %get-tuple-element.60), channel_id=1, source_target_pairs={{0,16},{1,17},{2,18},{3,19},{4,20},{5,21},{6,22},{7,23},{8,24},{9,... | collective-permute-start | bytes 172040 | tf_op jit(solution)/shard_map/ppermute | solution.py:26
  63.0 7.3 %collective-permute-start.34 = (bf16[4,7168]{1,0:T(4,128)(2,1)S(1)}, bf16[4,7168]{1,0:T(4,128)(2,1)S(1)}, u32[]{:S(2)}, u32[]{:S(2)}) collective-permute-start(bf16[4,7168]{1,0:T(4,128)(2,1)S(1)} %get-tuple-element.71), channel_id=1, source_target_pairs={{0,24},{1,25},{2,26},{3,27},{4,28},{5,29},{6,30},{7,31},{8,16},{9,... | collective-permute-start | bytes 172040 | tf_op jit(solution)/shard_map/ppermute | solution.py:26
  65.0 5.3 %collective-permute-start.35 = (bf16[4,7168]{1,0:T(4,128)(2,1)S(1)}, bf16[4,7168]{1,0:T(4,128)(2,1)S(1)}, u32[]{:S(2)}, u32[]{:S(2)}) collective-permute-start(bf16[4,7168]{1,0:T(4,128)(2,1)S(1)} %get-tuple-element.72), channel_id=1, source_target_pairs={{0,16},{1,17},{2,18},{3,19},{4,20},{5,21},{6,22},{7,23},{8,24},{9,... | collective-permute-start | bytes 172040 | tf_op jit(solution)/shard_map/ppermute | solution.py:26

commit v15 on v13

--- a/solution.py
+++ b/solution.py
@@ -51,8 +51,12 @@
 
 
 def load_kernel(count, *refs):
-    sems = refs[-1]
-    copies = [pltpu.make_async_copy(refs[place], refs[count + place], sems.at[place]) for place in range(count)]
+    out_ref, sems = refs[count:]
+    copies, start = [], 0
+    for place, ref in enumerate(refs[:count]):
+        columns = pl.ds(start, ref.shape[2])
+        copies.append(pltpu.make_async_copy(ref, out_ref.at[:, :, columns], sems.at[place]))
+        start += ref.shape[2]
     for copy in copies:
         copy.start()
     for copy in copies:
@@ -61,11 +65,12 @@
 
 def load(*weights):
     count = len(weights)
+    columns = sum(w.shape[2] for w in weights)
     return pl.pallas_call(
         functools.partial(load_kernel, count),
-        out_shape=[pltpu.VMEM(w.shape, w.dtype) for w in weights],
+        out_shape=pltpu.VMEM(weights[0].shape[:2] + (columns,), weights[0].dtype),
         in_specs=[pl.BlockSpec(memory_space=pltpu.HBM)] * count,
-        out_specs=[VMEM] * count,
+        out_specs=VMEM,
         scratch_shapes=[pltpu.SemaphoreType.DMA((count,))],
         compiler_params=pltpu.CompilerParams(vmem_limit_bytes=VMEM_LIMIT),
         cost_estimate=pl.CostEstimate(
@@ -169,9 +174,9 @@
     x_refs, refs = refs[:8], refs[8:]
     if step_no > 0:
         tail_ref, refs = refs[0], refs[1:]
-    (gate_ref, up_ref, down_ref), outs, refs = refs[:3], refs[3:11], refs[11:]
+    (wide_ref, down_ref), outs, refs = refs[:2], refs[2:10], refs[10:]
     part = outs[0].shape[0]
-    dim, hidden = gate_ref.shape[1:]
+    hidden, dim = down_ref.shape[1:]
     experts = lax.axis_size("expert") // GROUP
     column = step_no * experts + lax.axis_index("expert") // GROUP
     lane = lax.broadcasted_iota(jnp.int32, (part, LANES), 1)
@@ -185,12 +190,11 @@
             tail = tail_ref[band, :]
         chosen = jnp.where(lane == column, tail.astype(jnp.float32), 0.0)
         weights.append(jnp.sum(chosen, axis=1, keepdims=True))
-    gated = jnp.zeros((8 * part, hidden), jnp.float32)
-    up_part = jnp.zeros((8 * part, hidden), jnp.float32)
+    both = jnp.zeros((8 * part, 2 * hidden), jnp.float32)
     for span in spans(dim):
         rows = jnp.concatenate([ref[:, span] for ref in x_refs], axis=0)
-        gated += jnp.dot(rows, gate_ref[0, span, :], preferred_element_type=jnp.float32)
-        up_part += jnp.dot(rows, up_ref[0, span, :], preferred_element_type=jnp.float32)
+        both += jnp.dot(rows, wide_ref[0, span, :], preferred_element_type=jnp.float32)
+    gated, up_part = both[:, :hidden], both[:, hidden:]
     inner = (gated / (1.0 + jnp.exp(-gated)) * up_part).astype(jnp.bfloat16)
     for span in spans(dim):
         terms = jnp.dot(inner, down_ref[0, :, span], preferred_element_type=jnp.float32)
@@ -200,12 +204,12 @@
             out_ref[:, span] = jnp.where(weight > 0.0, weight * mine, 0.0).astype(jnp.bfloat16)
 
 
-def mlp(step_no, xs, tail, gate, up, down):
-    dim, hidden = gate.shape[1:]
+def mlp(step_no, xs, tail, wide, down):
+    hidden, dim = down.shape[1:]
     part = xs[0].shape[0]
-    gate, up, down = [pltpu.with_memory_space_constraint(w, pltpu.VMEM) for w in (gate, up, down)]
+    wide, down = [pltpu.with_memory_space_constraint(w, pltpu.VMEM) for w in (wide, down)]
     first = step_no == 0
-    args = list(xs) + ([] if first else [tail]) + [gate, up, down]
+    args = list(xs) + ([] if first else [tail]) + [wide, down]
     result = call(
         functools.partial(mlp_kernel, step_no), [(part, dim)] * 8 + [(8 * part, LANES)] * first, *args,
         cost_estimate=pl.CostEstimate(
@@ -236,13 +240,13 @@
     passes_count = routing.shape[1]
     top, *middle = upper_flips(owners)
 
-    gate, up = load(gate_proj, up_proj)
+    wide = load(gate_proj, up_proj)
     block = prepare(owners // GROUP, states, routing, route_weight)
     other = exchange(block, top, 0)
-    other, gate, up = lax.optimization_barrier((other, gate, up))
+    other, wide = lax.optimization_barrier((other, wide))
     pair, raw = call(first_kernel, [(2 * row_dev, dim + LANES), (2 * row_dev, dim)], block, other, norm_gain)
     pair, down_hbm = lax.optimization_barrier((pair, down_proj))
-    (down,) = load(down_hbm)
+    down = load(down_hbm)
     own, tail = states[0], None
     for step_no in range(passes_count):
         rows_a = pair
@@ -253,7 +257,7 @@
         if step_no == 0:
             near, down = lax.optimization_barrier((near, down))
         fars = [exchange(rows, CORE, 0) for rows in [near] + mine[1:]]
-        outs, tail = mlp(step_no, mine + fars, tail, gate, up, down)
+        outs, tail = mlp(step_no, mine + fars, tail, wide, down)
 
         kept, sent = outs[:4], [exchange(rows, CORE, 0) for rows in outs[4:]]
         parts = [kept[0], sent[0]]

time: 70.5 us -> 70.5 us (level)
  no operation moved by 1% of the time
where the time goes in v15:
time: 70.5 us; the launch traced here: 70.3 us
  starting transfers between devices  31.8 us (45%)
  waiting for transfers between devices  26.5 us (38%)
  Pallas kernels  11.8 us (17%)
    ppermute x35, starting transfers between devices, exchange(): return lax.ppermute(value, ('segment', 'expert'), pairs)  31.8 us
    ppermute x35, waiting for transfers between devices, exchange(): return lax.ppermute(value, ('segment', 'expert'), pairs)  26.5 us
    pallas_call x14, Pallas kernels, call(): pl.pallas_call(kernel, out_shape=[jax.ShapeDtypeStruct(shape, jnp.bfloat1...  6.59 us
    pallas_call x2, Pallas kernels, load(): pl.pallas_call(functools.partial(load_kernel, count), out_shape=pltpu.VME...  5.22 us
  transfers between devices with their start and end apart: 35, of which 17 were waited for; matrix products, arithmetic and copies ran while one was open for 0% of the time, Pallas kernels for 8%

profile of v15, /device:TPU:0, one launch (start us, length us, event | category | flops | bytes accessed | tf_op | source)
XLA Modules:
  0.0 70.3 jit_solution(11207807093978387111)
XLA Ops:
  0.0 1.0 %shard_map.73.own_ref = bf16[4,7296]{1,0:T(4,128)(2,1)S(1)} custom-call(bf16[1,4,7168]{2,1,0:T(4,128)(2,1)} %states_hbm.1, s32[1,2,2,4]{3,2,1,0:T(2,128)} %bitcast.3, bf16[1,2,2,4]{3,2,1,0:T(2,128)(2,1)} %bitcast.4), custom_call_target="tpu_custom_call" | custom-call | tf_op jit(solution)/shard_map/pallas_call | solution.py:43
  1.0 0.0 copy-start
  1.0 4.1 %collective-permute-start = (bf16[4,7296]{1,0:T(4,128)(2,1)S(1)}, bf16[4,7296]{1,0:T(4,128)(2,1)S(1)}, u32[]{:S(2)}, u32[]{:S(2)}) collective-permute-start(bf16[4,7296]{1,0:T(4,128)(2,1)S(1)} %shard_map.73.own_ref), channel_id=1, source_target_pairs={{0,8},{1,9},{2,10},{3,11},{4,12},{5,13},{6,14},{7,15},{8,0},{9,1},... | collective-permute-start | bytes 175112 | tf_op jit(solution)/shard_map/ppermute | solution.py:26
  5.1 3.2 %shard_map.74.refs_8_.refs_9_ = bf16[1,7168,512]{2,1,0:T(8,128)(2,1)S(1)} custom-call(bf16[1,7168,256]{2,1,0:T(8,128)(2,1)} %refs_0_.1, bf16[1,7168,256]{2,1,0:T(8,128)(2,1)} %refs_1_.1), custom_call_target="tpu_custom_call" | custom-call | bytes 7340032 | tf_op jit(solution)/shard_map/pallas_call | solution.py:69
  8.3 0.0 collective-permute-done.far_ref
  8.3 0.2 shard_map.75
  8.5 2.6 %collective-permute-start.4 = (bf16[8,7296]{1,0:T(8,128)(2,1)S(1)}, bf16[8,7296]{1,0:T(8,128)(2,1)S(1)}, u32[]{:S(2)}, u32[]{:S(2)}) collective-permute-start(bf16[8,7296]{1,0:T(8,128)(2,1)S(1)} %get-tuple-element.39.refs_0_), channel_id=1, source_target_pairs={{0,6},{1,7},{2,4},{3,5},{4,2},{5,3},{6,0},{7,1},{8,14},{9,15},{10,... | collective-permute-start | bytes 350216 | tf_op jit(solution)/shard_map/ppermute | solution.py:26
  11.1 0.5 collective-permute-start.3
  11.6 0.4 collective-permute-start.2
  12.0 2.0 %shard_map.76.refs_9_.refs_10_ = bf16[1,256,7168]{2,1,0:T(8,128)(2,1)S(1)} custom-call(bf16[1,256,7168]{2,1,0:T(8,128)(2,1)} %refs_0_.2), custom_call_target="tpu_custom_call" | custom-call | bytes 3670016 | tf_op jit(solution)/shard_map/pallas_call | solution.py:69
  14.1 0.1 collective-permute-start.5
  14.2 1.3 %collective-permute-done.4.refs_3_ = bf16[8,7296]{1,0:T(8,128)(2,1)S(1)} collective-permute-done((bf16[8,7296]{1,0:T(8,128)(2,1)S(1)}, bf16[8,7296]{1,0:T(8,128)(2,1)S(1)}, u32[]{:S(2)}, u32[]{:S(2)}) %collective-permute-start.4) | collective-permute-done | bytes 116768 | tf_op jit(solution)/shard_map/ppermute | solution.py:26
  15.5 1.3 %collective-permute-done.3.refs_2_ = bf16[8,7296]{1,0:T(8,128)(2,1)S(1)} collective-permute-done((bf16[8,7296]{1,0:T(8,128)(2,1)S(1)}, bf16[8,7296]{1,0:T(8,128)(2,1)S(1)}, u32[]{:S(2)}, u32[]{:S(2)}) %collective-permute-start.3) | collective-permute-done | bytes 116768 | tf_op jit(solution)/shard_map/ppermute | solution.py:26
  16.8 0.0 collective-permute-start.7
  16.8 0.5 collective-permute-start.6
  17.3 0.8 %collective-permute-done.7.refs_6_ = bf16[8,7296]{1,0:T(8,128)(2,1)S(1)} collective-permute-done((bf16[8,7296]{1,0:T(8,128)(2,1)S(1)}, bf16[8,7296]{1,0:T(8,128)(2,1)S(1)}, u32[]{:S(2)}, u32[]{:S(2)}) %collective-permute-start.7) | collective-permute-done | bytes 116768 | tf_op jit(solution)/shard_map/ppermute | solution.py:26
  18.2 0.2 collective-permute-done.6.refs_5_
  18.3 2.1 %shard_map.77 = (bf16[8,7168]{1,0:T(8,128)(2,1)S(1)}, bf16[8,7168]{1,0:T(8,128)(2,1)S(1)}, bf16[8,7168]{1,0:T(8,128)(2,1)S(1)}, bf16[8,7168]{1,0:T(8,128)(2,1)S(...) custom-call(bf16[8,7296]{1,0:T(8,128)(2,1)S(1)} %get-tuple-element.3, ...), custom_call_target="tpu_custom_call" | custom-call | flops 704643072 | bytes 11010048 | tf_op jit(solution)/shard_map/pallas_call | solution.py:43
  20.4 0.4 collective-permute-start.10
  20.9 0.2 collective-permute-start.12
  21.0 0.3 collective-permute-start.14
  21.4 0.2 collective-permute-start.9
  21.5 0.3 collective-permute-done.10.refs_1_
  21.9 2.4 %collective-permute-start.11 = (bf16[8,7168]{1,0:T(8,128)(2,1)S(1)}, bf16[8,7168]{1,0:T(8,128)(2,1)S(1)}, u32[]{:S(2)}, u32[]{:S(2)}) collective-permute-start(bf16[8,7168]{1,0:T(8,128)(2,1)S(1)} %shard_map.78), channel_id=1, source_target_pairs={{0,6},{1,7},{2,4},{3,5},{4,2},{5,3},{6,0},{7,1},{8,14},{9,15},{10,... | collective-permute-start | bytes 344072 | tf_op jit(solution)/shard_map/ppermute | solution.py:26
  24.2 0.0 collective-permute-done.12.refs_1_
  24.3 0.8 %collective-permute-start.13 = (bf16[8,7168]{1,0:T(8,128)(2,1)S(1)}, bf16[8,7168]{1,0:T(8,128)(2,1)S(1)}, u32[]{:S(2)}, u32[]{:S(2)}) collective-permute-start(bf16[8,7168]{1,0:T(8,128)(2,1)S(1)} %shard_map.79), channel_id=1, source_target_pairs={{0,2},{1,5},{2,0},{3,7},{4,6},{5,1},{6,4},{7,3},{8,10},{9,13},{10,... | collective-permute-start | bytes 344072 | tf_op jit(solution)/shard_map/ppermute | solution.py:26
  25.1 0.5 collective-permute-start.15
  25.6 1.5 %collective-permute-start.1 = (bf16[8,7168]{1,0:T(8,128)(2,1)S(1)}, bf16[8,7168]{1,0:T(8,128)(2,1)S(1)}, u32[]{:S(2)}, u32[]{:S(2)}) collective-permute-start(bf16[8,7168]{1,0:T(8,128)(2,1)S(1)} %get-tuple-element.35), channel_id=1, source_target_pairs={{0,16},{1,17},{2,18},{3,19},{4,20},{5,21},{6,22},{7,23},{8,24},{9,... | collective-permute-start | bytes 344072 | tf_op jit(solution)/shard_map/ppermute | solution.py:26
  27.2 0.0 collective-permute-done.9.refs_1_
  27.2 1.6 %collective-permute-done.11.refs_2_ = bf16[8,7168]{1,0:T(8,128)(2,1)S(1)} collective-permute-done((bf16[8,7168]{1,0:T(8,128)(2,1)S(1)}, bf16[8,7168]{1,0:T(8,128)(2,1)S(1)}, u32[]{:S(2)}, u32[]{:S(2)}) %collective-permute-start.11) | collective-permute-done | bytes 114720 | tf_op jit(solution)/shard_map/ppermute | solution.py:26
  28.8 1.9 %collective-permute-done.13.refs_3_ = bf16[8,7168]{1,0:T(8,128)(2,1)S(1)} collective-permute-done((bf16[8,7168]{1,0:T(8,128)(2,1)S(1)}, bf16[8,7168]{1,0:T(8,128)(2,1)S(1)}, u32[]{:S(2)}, u32[]{:S(2)}) %collective-permute-start.13) | collective-permute-done | bytes 114720 | tf_op jit(solution)/shard_map/ppermute | solution.py:26
  30.7 0.0 collective-permute-done.15.refs_4_
  30.7 0.1 shard_map.81
  30.8 3.0 %collective-permute-start.17 = (bf16[8,7168]{1,0:T(8,128)(2,1)S(1)}, bf16[8,7168]{1,0:T(8,128)(2,1)S(1)}, u32[]{:S(2)}, u32[]{:S(2)}) collective-permute-start(bf16[8,7168]{1,0:T(8,128)(2,1)S(1)} %shard_map.81), channel_id=1, source_target_pairs={{0,24},{1,25},{2,26},{3,27},{4,28},{5,29},{6,30},{7,31},{8,16},{9,... | collective-permute-start | bytes 344072 | tf_op jit(solution)/shard_map/ppermute | solution.py:26
  33.8 0.5 collective-permute-start.16
  34.3 0.0 collective-permute-done.1.rest_ref
  34.3 5.8 %collective-permute-done.17.far_ref = bf16[8,7168]{1,0:T(8,128)(2,1)S(1)} collective-permute-done((bf16[8,7168]{1,0:T(8,128)(2,1)S(1)}, bf16[8,7168]{1,0:T(8,128)(2,1)S(1)}, u32[]{:S(2)}, u32[]{:S(2)}) %collective-permute-start.17) | collective-permute-done | bytes 114720 | tf_op jit(solution)/shard_map/ppermute | solution.py:26
  40.1 0.2 shard_map.82
  40.3 2.6 %collective-permute-start.21 = (bf16[8,7168]{1,0:T(8,128)(2,1)S(1)}, bf16[8,7168]{1,0:T(8,128)(2,1)S(1)}, u32[]{:S(2)}, u32[]{:S(2)}) collective-permute-start(bf16[8,7168]{1,0:T(8,128)(2,1)S(1)} %get-tuple-element.51.refs_0_), channel_id=1, source_target_pairs={{0,6},{1,7},{2,4},{3,5},{4,2},{5,3},{6,0},{7,1},{8,14},{9,15},{10,... | collective-permute-start | bytes 344072 | tf_op jit(solution)/shard_map/ppermute | solution.py:26
  42.9 0.8 %collective-permute-start.20 = (bf16[8,7168]{1,0:T(8,128)(2,1)S(1)}, bf16[8,7168]{1,0:T(8,128)(2,1)S(1)}, u32[]{:S(2)}, u32[]{:S(2)}) collective-permute-start(bf16[8,7168]{1,0:T(8,128)(2,1)S(1)} %get-tuple-element.51.refs_0_), channel_id=1, source_target_pairs={{0,2},{1,5},{2,0},{3,7},{4,6},{5,1},{6,4},{7,3},{8,10},{9,13},{10,... | collective-permute-start | bytes 344072 | tf_op jit(solution)/shard_map/ppermute | solution.py:26
  43.7 0.2 collective-permute-start.19
  43.9 3.2 %collective-permute-done.21.refs_3_ = bf16[8,7168]{1,0:T(8,128)(2,1)S(1)} collective-permute-done((bf16[8,7168]{1,0:T(8,128)(2,1)S(1)}, bf16[8,7168]{1,0:T(8,128)(2,1)S(1)}, u32[]{:S(2)}, u32[]{:S(2)}) %collective-permute-start.21) | collective-permute-done | bytes 114720 | tf_op jit(solution)/shard_map/ppermute | solution.py:26
  47.1 1.6 %collective-permute-done.20.refs_2_ = bf16[8,7168]{1,0:T(8,128)(2,1)S(1)} collective-permute-done((bf16[8,7168]{1,0:T(8,128)(2,1)S(1)}, bf16[8,7168]{1,0:T(8,128)(2,1)S(1)}, u32[]{:S(2)}, u32[]{:S(2)}) %collective-permute-start.20) | collective-permute-done | bytes 114720 | tf_op jit(solution)/shard_map/ppermute | solution.py:26
  48.7 0.5 collective-permute-start.23
  49.2 0.8 %collective-permute-done.24.refs_6_ = bf16[8,7168]{1,0:T(8,128)(2,1)S(1)} collective-permute-done((bf16[8,7168]{1,0:T(8,128)(2,1)S(1)}, bf16[8,7168]{1,0:T(8,128)(2,1)S(1)}, u32[]{:S(2)}, u32[]{:S(2)}) %collective-permute-start.24) | collective-permute-done | bytes 114720 | tf_op jit(solution)/shard_map/ppermute | solution.py:26
  50.0 0.2 collective-permute-done.23.refs_5_
  50.2 2.1 %shard_map.83 = (bf16[8,7168]{1,0:T(8,128)(2,1)S(1)}, bf16[8,7168]{1,0:T(8,128)(2,1)S(1)}, bf16[8,7168]{1,0:T(8,128)(2,1)S(1)}, bf16[8,7168]{1,0:T(8,128)(2,1)S(...) custom-call(bf16[8,7168]{1,0:T(8,128)(2,1)S(1)} %get-tuple-element.5, ...), custom_call_target="tpu_custom_call" | custom-call | flops 704643072 | bytes 11010048 | tf_op jit(solution)/shard_map/pallas_call | solution.py:43
  52.3 0.4 collective-permute-start.27
  52.7 0.2 collective-permute-start.29
  52.9 0.3 collective-permute-start.31
  53.2 0.2 collective-permute-start.26
  53.4 0.3 collective-permute-done.27.refs_1_
  53.7 2.7 %collective-permute-start.28 = (bf16[8,7168]{1,0:T(8,128)(2,1)S(1)}, bf16[8,7168]{1,0:T(8,128)(2,1)S(1)}, u32[]{:S(2)}, u32[]{:S(2)}) collective-permute-start(bf16[8,7168]{1,0:T(8,128)(2,1)S(1)} %shard_map.84), channel_id=1, source_target_pairs={{0,6},{1,7},{2,4},{3,5},{4,2},{5,3},{6,0},{7,1},{8,14},{9,15},{10,... | collective-permute-start | bytes 344072 | tf_op jit(solution)/shard_map/ppermute | solution.py:26
  56.4 0.8 %collective-permute-start.30 = (bf16[8,7168]{1,0:T(8,128)(2,1)S(1)}, bf16[8,7168]{1,0:T(8,128)(2,1)S(1)}, u32[]{:S(2)}, u32[]{:S(2)}) collective-permute-start(bf16[8,7168]{1,0:T(8,128)(2,1)S(1)} %shard_map.85), channel_id=1, source_target_pairs={{0,2},{1,5},{2,0},{3,7},{4,6},{5,1},{6,4},{7,3},{8,10},{9,13},{10,... | collective-permute-start | bytes 344072 | tf_op jit(solution)/shard_map/ppermute | solution.py:26
  57.3 0.2 collective-permute-start.32
  57.5 1.5 %collective-permute-start.18 = (bf16[4,7168]{1,0:T(4,128)(2,1)S(1)}, bf16[4,7168]{1,0:T(4,128)(2,1)S(1)}, u32[]{:S(2)}, u32[]{:S(2)}) collective-permute-start(bf16[4,7168]{1,0:T(4,128)(2,1)S(1)} %get-tuple-element.50), channel_id=1, source_target_pairs={{0,16},{1,17},{2,18},{3,19},{4,20},{5,21},{6,22},{7,23},{8,24},{9,... | collective-permute-start | bytes 172040 | tf_op jit(solution)/shard_map/ppermute | solution.py:26
  58.9 1.7 %collective-permute-done.28.refs_2_ = bf16[8,7168]{1,0:T(8,128)(2,1)S(1)} collective-permute-done((bf16[8,7168]{1,0:T(8,128)(2,1)S(1)}, bf16[8,7168]{1,0:T(8,128)(2,1)S(1)}, u32[]{:S(2)}, u32[]{:S(2)}) %collective-permute-start.28) | collective-permute-done | bytes 114720 | tf_op jit(solution)/shard_map/ppermute | solution.py:26
  60.6 1.9 %collective-permute-done.30.refs_3_ = bf16[8,7168]{1,0:T(8,128)(2,1)S(1)} collective-permute-done((bf16[8,7168]{1,0:T(8,128)(2,1)S(1)}, bf16[8,7168]{1,0:T(8,128)(2,1)S(1)}, u32[]{:S(2)}, u32[]{:S(2)}) %collective-permute-start.30) | collective-permute-done | bytes 114720 | tf_op jit(solution)/shard_map/ppermute | solution.py:26
  62.5 0.1 shard_map.87
  62.6 2.7 %collective-permute-start.33 = (bf16[4,7168]{1,0:T(4,128)(2,1)S(1)}, bf16[4,7168]{1,0:T(4,128)(2,1)S(1)}, u32[]{:S(2)}, u32[]{:S(2)}) collective-permute-start(bf16[4,7168]{1,0:T(4,128)(2,1)S(1)} %get-tuple-element.61), channel_id=1, source_target_pairs={{0,24},{1,25},{2,26},{3,27},{4,28},{5,29},{6,30},{7,31},{8,16},{9,... | collective-permute-start | bytes 172040 | tf_op jit(solution)/shard_map/ppermute | solution.py:26
  65.4 0.7 collective-permute-start.34
  66.0 3.4 %collective-permute-done.33.refs_1_ = bf16[4,7168]{1,0:T(4,128)(2,1)S(1)} collective-permute-done((bf16[4,7168]{1,0:T(4,128)(2,1)S(1)}, bf16[4,7168]{1,0:T(4,128)(2,1)S(1)}, u32[]{:S(2)}, u32[]{:S(2)}) %collective-permute-start.33) | collective-permute-done | bytes 57376 | tf_op jit(solution)/shard_map/ppermute | solution.py:26
  69.4 0.3 collective-permute-done.34.refs_2_
  69.6 0.7 shard_map.88
  (24 shorter events, 0.2 us)
Async XLA Ops:
  1.0 7.3 %copy-start = (f32[1,7168]{1,0:T(1,128)S(1)}, f32[1,7168]{1,0:T(1,128)}, u32[]{:S(2)}) copy-start(f32[1,7168]{1,0:T(1,128)} %gain_ref.3) | copy-start | bytes 86020
  1.0 7.3 %collective-permute-start = (bf16[4,7296]{1,0:T(4,128)(2,1)S(1)}, bf16[4,7296]{1,0:T(4,128)(2,1)S(1)}, u32[]{:S(2)}, u32[]{:S(2)}) collective-permute-start(bf16[4,7296]{1,0:T(4,128)(2,1)S(1)} %shard_map.73.own_ref), channel_id=1, source_target_pairs={{0,8},{1,9},{2,10},{3,11},{4,12},{5,13},{6,14},{7,15},{8,0},{9,1},... | collective-permute-start | bytes 175112 | tf_op jit(solution)/shard_map/ppermute | solution.py:26
  8.5 7.0 %collective-permute-start.4 = (bf16[8,7296]{1,0:T(8,128)(2,1)S(1)}, bf16[8,7296]{1,0:T(8,128)(2,1)S(1)}, u32[]{:S(2)}, u32[]{:S(2)}) collective-permute-start(bf16[8,7296]{1,0:T(8,128)(2,1)S(1)} %get-tuple-element.39.refs_0_), channel_id=1, source_target_pairs={{0,6},{1,7},{2,4},{3,5},{4,2},{5,3},{6,0},{7,1},{8,14},{9,15},{10,... | collective-permute-start | bytes 350216 | tf_op jit(solution)/shard_map/ppermute | solution.py:26
  11.1 5.7 %collective-permute-start.3 = (bf16[8,7296]{1,0:T(8,128)(2,1)S(1)}, bf16[8,7296]{1,0:T(8,128)(2,1)S(1)}, u32[]{:S(2)}, u32[]{:S(2)}) collective-permute-start(bf16[8,7296]{1,0:T(8,128)(2,1)S(1)} %get-tuple-element.39.refs_0_), channel_id=1, source_target_pairs={{0,2},{1,5},{2,0},{3,7},{4,6},{5,1},{6,4},{7,3},{8,10},{9,13},{10,... | collective-permute-start | bytes 350216 | tf_op jit(solution)/shard_map/ppermute | solution.py:26
  11.6 5.2 %collective-permute-start.2 = (bf16[8,7296]{1,0:T(8,128)(2,1)S(1)}, bf16[8,7296]{1,0:T(8,128)(2,1)S(1)}, u32[]{:S(2)}, u32[]{:S(2)}) collective-permute-start(bf16[8,7296]{1,0:T(8,128)(2,1)S(1)} %get-tuple-element.39.refs_0_), channel_id=1, source_target_pairs={{0,4},{1,3},{2,6},{3,1},{4,0},{5,7},{6,2},{7,5},{8,12},{9,11},{10,... | collective-permute-start | bytes 350216 | tf_op jit(solution)/shard_map/ppermute | solution.py:26
  14.1 3.2 %collective-permute-start.5 = (bf16[8,7296]{1,0:T(8,128)(2,1)S(1)}, bf16[8,7296]{1,0:T(8,128)(2,1)S(1)}, u32[]{:S(2)}, u32[]{:S(2)}) collective-permute-start(bf16[8,7296]{1,0:T(8,128)(2,1)S(1)} %get-tuple-element.39.refs_0_), channel_id=1, source_target_pairs={{0,1},{1,0},{2,3},{3,2},{4,5},{5,4},{6,7},{7,6},{8,9},{9,8},{10,11... | collective-permute-start | bytes 350216 | tf_op jit(solution)/shard_map/ppermute | solution.py:26
  15.5 1.8 %collective-permute-start.8 = (bf16[8,7296]{1,0:T(8,128)(2,1)S(1)}, bf16[8,7296]{1,0:T(8,128)(2,1)S(1)}, u32[]{:S(2)}, u32[]{:S(2)}) collective-permute-start(bf16[8,7296]{1,0:T(8,128)(2,1)S(1)} %collective-permute-done.4.refs_3_), channel_id=1, source_target_pairs={{0,1},{1,0},{2,3},{3,2},{4,5},{5,4},{6,7},{7,6},{8,9},{9,8},{10,11... | collective-permute-start | bytes 350216 | tf_op jit(solution)/shard_map/ppermute | solution.py:26
  16.8 1.3 %collective-permute-start.7 = (bf16[8,7296]{1,0:T(8,128)(2,1)S(1)}, bf16[8,7296]{1,0:T(8,128)(2,1)S(1)}, u32[]{:S(2)}, u32[]{:S(2)}) collective-permute-start(bf16[8,7296]{1,0:T(8,128)(2,1)S(1)} %collective-permute-done.3.refs_2_), channel_id=1, source_target_pairs={{0,1},{1,0},{2,3},{3,2},{4,5},{5,4},{6,7},{7,6},{8,9},{9,8},{10,11... | collective-permute-start | bytes 350216 | tf_op jit(solution)/shard_map/ppermute | solution.py:26
  16.8 1.5 %collective-permute-start.6 = (bf16[8,7296]{1,0:T(8,128)(2,1)S(1)}, bf16[8,7296]{1,0:T(8,128)(2,1)S(1)}, u32[]{:S(2)}, u32[]{:S(2)}) collective-permute-start(bf16[8,7296]{1,0:T(8,128)(2,1)S(1)} %collective-permute-done.2.refs_1_), channel_id=1, source_target_pairs={{0,1},{1,0},{2,3},{3,2},{4,5},{5,4},{6,7},{7,6},{8,9},{9,8},{10,11... | collective-permute-start | bytes 350216 | tf_op jit(solution)/shard_map/ppermute | solution.py:26
  20.4 1.4 %collective-permute-start.10 = (bf16[8,7168]{1,0:T(8,128)(2,1)S(1)}, bf16[8,7168]{1,0:T(8,128)(2,1)S(1)}, u32[]{:S(2)}, u32[]{:S(2)}) collective-permute-start(bf16[8,7168]{1,0:T(8,128)(2,1)S(1)} %get-tuple-element.45), channel_id=1, source_target_pairs={{0,1},{1,0},{2,3},{3,2},{4,5},{5,4},{6,7},{7,6},{8,9},{9,8},{10,11... | collective-permute-start | bytes 344072 | tf_op jit(solution)/shard_map/ppermute | solution.py:26
  20.9 3.4 %collective-permute-start.12 = (bf16[8,7168]{1,0:T(8,128)(2,1)S(1)}, bf16[8,7168]{1,0:T(8,128)(2,1)S(1)}, u32[]{:S(2)}, u32[]{:S(2)}) collective-permute-start(bf16[8,7168]{1,0:T(8,128)(2,1)S(1)} %get-tuple-element.47), channel_id=1, source_target_pairs={{0,1},{1,0},{2,3},{3,2},{4,5},{5,4},{6,7},{7,6},{8,9},{9,8},{10,11... | collective-permute-start | bytes 344072 | tf_op jit(solution)/shard_map/ppermute | solution.py:26
  21.0 4.1 %collective-permute-start.14 = (bf16[8,7168]{1,0:T(8,128)(2,1)S(1)}, bf16[8,7168]{1,0:T(8,128)(2,1)S(1)}, u32[]{:S(2)}, u32[]{:S(2)}) collective-permute-start(bf16[8,7168]{1,0:T(8,128)(2,1)S(1)} %get-tuple-element.49), channel_id=1, source_target_pairs={{0,1},{1,0},{2,3},{3,2},{4,5},{5,4},{6,7},{7,6},{8,9},{9,8},{10,11... | collective-permute-start | bytes 344072 | tf_op jit(solution)/shard_map/ppermute | solution.py:26
  21.4 5.8 %collective-permute-start.9 = (bf16[8,7168]{1,0:T(8,128)(2,1)S(1)}, bf16[8,7168]{1,0:T(8,128)(2,1)S(1)}, u32[]{:S(2)}, u32[]{:S(2)}) collective-permute-start(bf16[8,7168]{1,0:T(8,128)(2,1)S(1)} %get-tuple-element.43), channel_id=1, source_target_pairs={{0,1},{1,0},{2,3},{3,2},{4,5},{5,4},{6,7},{7,6},{8,9},{9,8},{10,11... | collective-permute-start | bytes 344072 | tf_op jit(solution)/shard_map/ppermute | solution.py:26
  21.9 6.9 %collective-permute-start.11 = (bf16[8,7168]{1,0:T(8,128)(2,1)S(1)}, bf16[8,7168]{1,0:T(8,128)(2,1)S(1)}, u32[]{:S(2)}, u32[]{:S(2)}) collective-permute-start(bf16[8,7168]{1,0:T(8,128)(2,1)S(1)} %shard_map.78), channel_id=1, source_target_pairs={{0,6},{1,7},{2,4},{3,5},{4,2},{5,3},{6,0},{7,1},{8,14},{9,15},{10,... | collective-permute-start | bytes 344072 | tf_op jit(solution)/shard_map/ppermute | solution.py:26
  24.3 6.4 %collective-permute-start.13 = (bf16[8,7168]{1,0:T(8,128)(2,1)S(1)}, bf16[8,7168]{1,0:T(8,128)(2,1)S(1)}, u32[]{:S(2)}, u32[]{:S(2)}) collective-permute-start(bf16[8,7168]{1,0:T(8,128)(2,1)S(1)} %shard_map.79), channel_id=1, source_target_pairs={{0,2},{1,5},{2,0},{3,7},{4,6},{5,1},{6,4},{7,3},{8,10},{9,13},{10,... | collective-permute-start | bytes 344072 | tf_op jit(solution)/shard_map/ppermute | solution.py:26
  25.1 5.6 %collective-permute-start.15 = (bf16[8,7168]{1,0:T(8,128)(2,1)S(1)}, bf16[8,7168]{1,0:T(8,128)(2,1)S(1)}, u32[]{:S(2)}, u32[]{:S(2)}) collective-permute-start(bf16[8,7168]{1,0:T(8,128)(2,1)S(1)} %shard_map.80), channel_id=1, source_target_pairs={{0,4},{1,3},{2,6},{3,1},{4,0},{5,7},{6,2},{7,5},{8,12},{9,11},{10,... | collective-permute-start | bytes 344072 | tf_op jit(solution)/shard_map/ppermute | solution.py:26
  25.6 8.7 %collective-permute-start.1 = (bf16[8,7168]{1,0:T(8,128)(2,1)S(1)}, bf16[8,7168]{1,0:T(8,128)(2,1)S(1)}, u32[]{:S(2)}, u32[]{:S(2)}) collective-permute-start(bf16[8,7168]{1,0:T(8,128)(2,1)S(1)} %get-tuple-element.35), channel_id=1, source_target_pairs={{0,16},{1,17},{2,18},{3,19},{4,20},{5,21},{6,22},{7,23},{8,24},{9,... | collective-permute-start | bytes 344072 | tf_op jit(solution)/shard_map/ppermute | solution.py:26
  30.8 9.4 %collective-permute-start.17 = (bf16[8,7168]{1,0:T(8,128)(2,1)S(1)}, bf16[8,7168]{1,0:T(8,128)(2,1)S(1)}, u32[]{:S(2)}, u32[]{:S(2)}) collective-permute-start(bf16[8,7168]{1,0:T(8,128)(2,1)S(1)} %shard_map.81), channel_id=1, source_target_pairs={{0,24},{1,25},{2,26},{3,27},{4,28},{5,29},{6,30},{7,31},{8,16},{9,... | collective-permute-start | bytes 344072 | tf_op jit(solution)/shard_map/ppermute | solution.py:26
  33.8 6.3 %collective-permute-start.16 = (bf16[8,7168]{1,0:T(8,128)(2,1)S(1)}, bf16[8,7168]{1,0:T(8,128)(2,1)S(1)}, u32[]{:S(2)}, u32[]{:S(2)}) collective-permute-start(bf16[8,7168]{1,0:T(8,128)(2,1)S(1)} %shard_map.81), channel_id=1, source_target_pairs={{0,16},{1,17},{2,18},{3,19},{4,20},{5,21},{6,22},{7,23},{8,24},{9,... | collective-permute-start | bytes 344072 | tf_op jit(solution)/shard_map/ppermute | solution.py:26
  40.3 6.7 %collective-permute-start.21 = (bf16[8,7168]{1,0:T(8,128)(2,1)S(1)}, bf16[8,7168]{1,0:T(8,128)(2,1)S(1)}, u32[]{:S(2)}, u32[]{:S(2)}) collective-permute-start(bf16[8,7168]{1,0:T(8,128)(2,1)S(1)} %get-tuple-element.51.refs_0_), channel_id=1, source_target_pairs={{0,6},{1,7},{2,4},{3,5},{4,2},{5,3},{6,0},{7,1},{8,14},{9,15},{10,... | collective-permute-start | bytes 344072 | tf_op jit(solution)/shard_map/ppermute | solution.py:26
  42.9 5.8 %collective-permute-start.20 = (bf16[8,7168]{1,0:T(8,128)(2,1)S(1)}, bf16[8,7168]{1,0:T(8,128)(2,1)S(1)}, u32[]{:S(2)}, u32[]{:S(2)}) collective-permute-start(bf16[8,7168]{1,0:T(8,128)(2,1)S(1)} %get-tuple-element.51.refs_0_), channel_id=1, source_target_pairs={{0,2},{1,5},{2,0},{3,7},{4,6},{5,1},{6,4},{7,3},{8,10},{9,13},{10,... | collective-permute-start | bytes 344072 | tf_op jit(solution)/shard_map/ppermute | solution.py:26
  43.7 5.0 %collective-permute-start.19 = (bf16[8,7168]{1,0:T(8,128)(2,1)S(1)}, bf16[8,7168]{1,0:T(8,128)(2,1)S(1)}, u32[]{:S(2)}, u32[]{:S(2)}) collective-permute-start(bf16[8,7168]{1,0:T(8,128)(2,1)S(1)} %get-tuple-element.51.refs_0_), channel_id=1, source_target_pairs={{0,4},{1,3},{2,6},{3,1},{4,0},{5,7},{6,2},{7,5},{8,12},{9,11},{10,... | collective-permute-start | bytes 344072 | tf_op jit(solution)/shard_map/ppermute | solution.py:26
  43.9 5.3 %collective-permute-start.22 = (bf16[8,7168]{1,0:T(8,128)(2,1)S(1)}, bf16[8,7168]{1,0:T(8,128)(2,1)S(1)}, u32[]{:S(2)}, u32[]{:S(2)}) collective-permute-start(bf16[8,7168]{1,0:T(8,128)(2,1)S(1)} %get-tuple-element.51.refs_0_), channel_id=1, source_target_pairs={{0,1},{1,0},{2,3},{3,2},{4,5},{5,4},{6,7},{7,6},{8,9},{9,8},{10,11... | collective-permute-start | bytes 344072 | tf_op jit(solution)/shard_map/ppermute | solution.py:26
  47.1 2.1 %collective-permute-start.25 = (bf16[8,7168]{1,0:T(8,128)(2,1)S(1)}, bf16[8,7168]{1,0:T(8,128)(2,1)S(1)}, u32[]{:S(2)}, u32[]{:S(2)}) collective-permute-start(bf16[8,7168]{1,0:T(8,128)(2,1)S(1)} %collective-permute-done.21.refs_3_), channel_id=1, source_target_pairs={{0,1},{1,0},{2,3},{3,2},{4,5},{5,4},{6,7},{7,6},{8,9},{9,8},{10,11... | collective-permute-start | bytes 344072 | tf_op jit(solution)/shard_map/ppermute | solution.py:26
  48.7 1.3 %collective-permute-start.24 = (bf16[8,7168]{1,0:T(8,128)(2,1)S(1)}, bf16[8,7168]{1,0:T(8,128)(2,1)S(1)}, u32[]{:S(2)}, u32[]{:S(2)}) collective-permute-start(bf16[8,7168]{1,0:T(8,128)(2,1)S(1)} %collective-permute-done.20.refs_2_), channel_id=1, source_target_pairs={{0,1},{1,0},{2,3},{3,2},{4,5},{5,4},{6,7},{7,6},{8,9},{9,8},{10,11... | collective-permute-start | bytes 344072 | tf_op jit(solution)/shard_map/ppermute | solution.py:26
  48.7 1.5 %collective-permute-start.23 = (bf16[8,7168]{1,0:T(8,128)(2,1)S(1)}, bf16[8,7168]{1,0:T(8,128)(2,1)S(1)}, u32[]{:S(2)}, u32[]{:S(2)}) collective-permute-start(bf16[8,7168]{1,0:T(8,128)(2,1)S(1)} %collective-permute-done.19.refs_1_), channel_id=1, source_target_pairs={{0,1},{1,0},{2,3},{3,2},{4,5},{5,4},{6,7},{7,6},{8,9},{9,8},{10,11... | collective-permute-start | bytes 344072 | tf_op jit(solution)/shard_map/ppermute | solution.py:26
  52.3 1.4 %collective-permute-start.27 = (bf16[8,7168]{1,0:T(8,128)(2,1)S(1)}, bf16[8,7168]{1,0:T(8,128)(2,1)S(1)}, u32[]{:S(2)}, u32[]{:S(2)}) collective-permute-start(bf16[8,7168]{1,0:T(8,128)(2,1)S(1)} %get-tuple-element.56), channel_id=1, source_target_pairs={{0,1},{1,0},{2,3},{3,2},{4,5},{5,4},{6,7},{7,6},{8,9},{9,8},{10,11... | collective-permute-start | bytes 344072 | tf_op jit(solution)/shard_map/ppermute | solution.py:26
  52.7 3.7 %collective-permute-start.29 = (bf16[8,7168]{1,0:T(8,128)(2,1)S(1)}, bf16[8,7168]{1,0:T(8,128)(2,1)S(1)}, u32[]{:S(2)}, u32[]{:S(2)}) collective-permute-start(bf16[8,7168]{1,0:T(8,128)(2,1)S(1)} %get-tuple-element.58), channel_id=1, source_target_pairs={{0,1},{1,0},{2,3},{3,2},{4,5},{5,4},{6,7},{7,6},{8,9},{9,8},{10,11... | collective-permute-start | bytes 344072 | tf_op jit(solution)/shard_map/ppermute | solution.py:26
  52.9 4.4 %collective-permute-start.31 = (bf16[8,7168]{1,0:T(8,128)(2,1)S(1)}, bf16[8,7168]{1,0:T(8,128)(2,1)S(1)}, u32[]{:S(2)}, u32[]{:S(2)}) collective-permute-start(bf16[8,7168]{1,0:T(8,128)(2,1)S(1)} %get-tuple-element.60), channel_id=1, source_target_pairs={{0,1},{1,0},{2,3},{3,2},{4,5},{5,4},{6,7},{7,6},{8,9},{9,8},{10,11... | collective-permute-start | bytes 344072 | tf_op jit(solution)/shard_map/ppermute | solution.py:26
  53.2 5.7 %collective-permute-start.26 = (bf16[8,7168]{1,0:T(8,128)(2,1)S(1)}, bf16[8,7168]{1,0:T(8,128)(2,1)S(1)}, u32[]{:S(2)}, u32[]{:S(2)}) collective-permute-start(bf16[8,7168]{1,0:T(8,128)(2,1)S(1)} %get-tuple-element.54), channel_id=1, source_target_pairs={{0,1},{1,0},{2,3},{3,2},{4,5},{5,4},{6,7},{7,6},{8,9},{9,8},{10,11... | collective-permute-start | bytes 344072 | tf_op jit(solution)/shard_map/ppermute | solution.py:26
  53.7 6.9 %collective-permute-start.28 = (bf16[8,7168]{1,0:T(8,128)(2,1)S(1)}, bf16[8,7168]{1,0:T(8,128)(2,1)S(1)}, u32[]{:S(2)}, u32[]{:S(2)}) collective-permute-start(bf16[8,7168]{1,0:T(8,128)(2,1)S(1)} %shard_map.84), channel_id=1, source_target_pairs={{0,6},{1,7},{2,4},{3,5},{4,2},{5,3},{6,0},{7,1},{8,14},{9,15},{10,... | collective-permute-start | bytes 344072 | tf_op jit(solution)/shard_map/ppermute | solution.py:26
  56.4 6.1 %collective-permute-start.30 = (bf16[8,7168]{1,0:T(8,128)(2,1)S(1)}, bf16[8,7168]{1,0:T(8,128)(2,1)S(1)}, u32[]{:S(2)}, u32[]{:S(2)}) collective-permute-start(bf16[8,7168]{1,0:T(8,128)(2,1)S(1)} %shard_map.85), channel_id=1, source_target_pairs={{0,2},{1,5},{2,0},{3,7},{4,6},{5,1},{6,4},{7,3},{8,10},{9,13},{10,... | collective-permute-start | bytes 344072 | tf_op jit(solution)/shard_map/ppermute | solution.py:26
  57.3 5.2 %collective-permute-start.32 = (bf16[8,7168]{1,0:T(8,128)(2,1)S(1)}, bf16[8,7168]{1,0:T(8,128)(2,1)S(1)}, u32[]{:S(2)}, u32[]{:S(2)}) collective-permute-start(bf16[8,7168]{1,0:T(8,128)(2,1)S(1)} %shard_map.86), channel_id=1, source_target_pairs={{0,4},{1,3},{2,6},{3,1},{4,0},{5,7},{6,2},{7,5},{8,12},{9,11},{10,... | collective-permute-start | bytes 344072 | tf_op jit(solution)/shard_map/ppermute | solution.py:26
  57.5 8.6 %collective-permute-start.18 = (bf16[4,7168]{1,0:T(4,128)(2,1)S(1)}, bf16[4,7168]{1,0:T(4,128)(2,1)S(1)}, u32[]{:S(2)}, u32[]{:S(2)}) collective-permute-start(bf16[4,7168]{1,0:T(4,128)(2,1)S(1)} %get-tuple-element.50), channel_id=1, source_target_pairs={{0,16},{1,17},{2,18},{3,19},{4,20},{5,21},{6,22},{7,23},{8,24},{9,... | collective-permute-start | bytes 172040 | tf_op jit(solution)/shard_map/ppermute | solution.py:26
  62.6 6.8 %collective-permute-start.33 = (bf16[4,7168]{1,0:T(4,128)(2,1)S(1)}, bf16[4,7168]{1,0:T(4,128)(2,1)S(1)}, u32[]{:S(2)}, u32[]{:S(2)}) collective-permute-start(bf16[4,7168]{1,0:T(4,128)(2,1)S(1)} %get-tuple-element.61), channel_id=1, source_target_pairs={{0,24},{1,25},{2,26},{3,27},{4,28},{5,29},{6,30},{7,31},{8,16},{9,... | collective-permute-start | bytes 172040 | tf_op jit(solution)/shard_map/ppermute | solution.py:26
  65.4 4.3 %collective-permute-start.34 = (bf16[4,7168]{1,0:T(4,128)(2,1)S(1)}, bf16[4,7168]{1,0:T(4,128)(2,1)S(1)}, u32[]{:S(2)}, u32[]{:S(2)}) collective-permute-start(bf16[4,7168]{1,0:T(4,128)(2,1)S(1)} %get-tuple-element.62), channel_id=1, source_target_pairs={{0,16},{1,17},{2,18},{3,19},{4,20},{5,21},{6,22},{7,23},{8,24},{9,... | collective-permute-start | bytes 172040 | tf_op jit(solution)/shard_map/ppermute | solution.py:26

commit v16 on v13

--- a/solution.py
+++ b/solution.py
@@ -31,7 +31,7 @@
 
 
 CORE = (1, 1)
-SQUARE = ((4, 2), (2, 4), (6, 6))
+SQUARE = ((2, 2), (4, 4), (6, 6))
 STAY = (0, 0)
 
 

time: 70.5 us -> 69.7 us (0.989)
  starting transfers between devices: 31.8 us -> 30.8 us
    ppermute x35, starting transfers between devices: 31.8 us -> 30.8 us  [exchange(): return lax.ppermute(value, ('segment', 'expert'), pairs)]
  transfers between devices with their start and end apart: 35 -> 35, of which waited for: 17 -> 23; matrix products, arithmetic and copies ran while one was open for 0% -> 0% of each run, Pallas kernels for 8% -> 8%
where the time goes in v16:
time: 69.7 us; the launch traced here: 69.6 us
  starting transfers between devices  30.8 us (44%)
  waiting for transfers between devices  26.7 us (38%)
  Pallas kernels  11.8 us (17%)
    ppermute x35, starting transfers between devices, exchange(): return lax.ppermute(value, ('segment', 'expert'), pairs)  30.8 us
    ppermute x35, waiting for transfers between devices, exchange(): return lax.ppermute(value, ('segment', 'expert'), pairs)  26.7 us
    pallas_call x14, Pallas kernels, call(): pl.pallas_call(kernel, out_shape=[jax.ShapeDtypeStruct(shape, jnp.bfloat1...  6.6 us
    pallas_call x2, Pallas kernels, load(): pl.pallas_call(functools.partial(load_kernel, count), out_shape=[pltpu.VM...  5.22 us
  transfers between devices with their start and end apart: 35, of which 23 were waited for; matrix products, arithmetic and copies ran while one was open for 0% of the time, Pallas kernels for 8%

profile of v16, /device:TPU:0, one launch (start us, length us, event | category | flops | bytes accessed | tf_op | source)
XLA Modules:
  0.0 69.6 jit_solution(17921227754743392225)
XLA Ops:
  0.0 1.0 %shard_map.73.own_ref = bf16[4,7296]{1,0:T(4,128)(2,1)S(1)} custom-call(bf16[1,4,7168]{2,1,0:T(4,128)(2,1)} %states_hbm.1, s32[1,2,2,4]{3,2,1,0:T(2,128)} %bitcast.3, bf16[1,2,2,4]{3,2,1,0:T(2,128)(2,1)} %bitcast.4), custom_call_target="tpu_custom_call" | custom-call | tf_op jit(solution)/shard_map/pallas_call | solution.py:43
  1.0 0.0 copy-start
  1.0 4.1 %collective-permute-start = (bf16[4,7296]{1,0:T(4,128)(2,1)S(1)}, bf16[4,7296]{1,0:T(4,128)(2,1)S(1)}, u32[]{:S(2)}, u32[]{:S(2)}) collective-permute-start(bf16[4,7296]{1,0:T(4,128)(2,1)S(1)} %shard_map.73.own_ref), channel_id=1, source_target_pairs={{0,8},{1,9},{2,10},{3,11},{4,12},{5,13},{6,14},{7,15},{8,0},{9,1},... | collective-permute-start | bytes 175112 | tf_op jit(solution)/shard_map/ppermute | solution.py:26
  5.1 3.2 %shard_map.74 = (bf16[1,7168,256]{2,1,0:T(8,128)(2,1)S(1)}, bf16[1,7168,256]{2,1,0:T(8,128)(2,1)S(1)}) custom-call(bf16[1,7168,256]{2,1,0:T(8,128)(2,1)} %refs_0_.1, bf16[1,7168,256]{2,1,0:T(8,128)(2,1)} %refs_1_.1), custom_call_target="tpu_custom_call" | custom-call | bytes 7340032 | tf_op jit(solution)/shard_map/pallas_call | solution.py:64
  8.3 0.2 shard_map.75
  8.5 2.6 %collective-permute-start.4 = (bf16[8,7296]{1,0:T(8,128)(2,1)S(1)}, bf16[8,7296]{1,0:T(8,128)(2,1)S(1)}, u32[]{:S(2)}, u32[]{:S(2)}) collective-permute-start(bf16[8,7296]{1,0:T(8,128)(2,1)S(1)} %get-tuple-element.44.refs_0_), channel_id=1, source_target_pairs={{0,6},{1,7},{2,4},{3,5},{4,2},{5,3},{6,0},{7,1},{8,14},{9,15},{10,... | collective-permute-start | bytes 350216 | tf_op jit(solution)/shard_map/ppermute | solution.py:26
  11.1 0.9 %collective-permute-start.3 = (bf16[8,7296]{1,0:T(8,128)(2,1)S(1)}, bf16[8,7296]{1,0:T(8,128)(2,1)S(1)}, u32[]{:S(2)}, u32[]{:S(2)}) collective-permute-start(bf16[8,7296]{1,0:T(8,128)(2,1)S(1)} %get-tuple-element.44.refs_0_), channel_id=1, source_target_pairs={{0,4},{1,5},{2,6},{3,7},{4,0},{5,1},{6,2},{7,3},{8,12},{9,13},{10,... | collective-permute-start | bytes 350216 | tf_op jit(solution)/shard_map/ppermute | solution.py:26
  12.0 0.1 collective-permute-start.2
  12.0 2.0 %shard_map.76.refs_10_.refs_11_ = bf16[1,256,7168]{2,1,0:T(8,128)(2,1)S(1)} custom-call(bf16[1,256,7168]{2,1,0:T(8,128)(2,1)} %refs_0_.2), custom_call_target="tpu_custom_call" | custom-call | bytes 3670016 | tf_op jit(solution)/shard_map/pallas_call | solution.py:64
  14.1 0.1 collective-permute-start.5
  14.2 1.3 %collective-permute-done.4.refs_3_ = bf16[8,7296]{1,0:T(8,128)(2,1)S(1)} collective-permute-done((bf16[8,7296]{1,0:T(8,128)(2,1)S(1)}, bf16[8,7296]{1,0:T(8,128)(2,1)S(1)}, u32[]{:S(2)}, u32[]{:S(2)}) %collective-permute-start.4) | collective-permute-done | bytes 116768 | tf_op jit(solution)/shard_map/ppermute | solution.py:26
  15.5 1.2 %collective-permute-done.3.refs_2_ = bf16[8,7296]{1,0:T(8,128)(2,1)S(1)} collective-permute-done((bf16[8,7296]{1,0:T(8,128)(2,1)S(1)}, bf16[8,7296]{1,0:T(8,128)(2,1)S(1)}, u32[]{:S(2)}, u32[]{:S(2)}) %collective-permute-start.3) | collective-permute-done | bytes 116768 | tf_op jit(solution)/shard_map/ppermute | solution.py:26
  16.7 0.1 collective-permute-done.2.refs_1_
  16.8 0.4 collective-permute-start.6
  17.2 0.8 %collective-permute-done.7.refs_6_ = bf16[8,7296]{1,0:T(8,128)(2,1)S(1)} collective-permute-done((bf16[8,7296]{1,0:T(8,128)(2,1)S(1)}, bf16[8,7296]{1,0:T(8,128)(2,1)S(1)}, u32[]{:S(2)}, u32[]{:S(2)}) %collective-permute-start.7) | collective-permute-done | bytes 116768 | tf_op jit(solution)/shard_map/ppermute | solution.py:26
  18.0 0.2 collective-permute-done.6.refs_5_
  18.2 2.1 %shard_map.77 = (bf16[8,7168]{1,0:T(8,128)(2,1)S(1)}, bf16[8,7168]{1,0:T(8,128)(2,1)S(1)}, bf16[8,7168]{1,0:T(8,128)(2,1)S(1)}, bf16[8,7168]{1,0:T(8,128)(2,1)S(...) custom-call(bf16[8,7296]{1,0:T(8,128)(2,1)S(1)} %get-tuple-element.4, ...), custom_call_target="tpu_custom_call" | custom-call | flops 704643072 | bytes 11010048 | tf_op jit(solution)/shard_map/pallas_call | solution.py:43
  20.3 0.4 collective-permute-start.10
  20.7 0.2 collective-permute-start.12
  20.9 0.3 collective-permute-start.14
  21.3 0.2 collective-permute-start.9
  21.4 0.3 collective-permute-done.10.refs_1_
  21.7 2.3 %collective-permute-start.11 = (bf16[8,7168]{1,0:T(8,128)(2,1)S(1)}, bf16[8,7168]{1,0:T(8,128)(2,1)S(1)}, u32[]{:S(2)}, u32[]{:S(2)}) collective-permute-start(bf16[8,7168]{1,0:T(8,128)(2,1)S(1)} %shard_map.78), channel_id=1, source_target_pairs={{0,6},{1,7},{2,4},{3,5},{4,2},{5,3},{6,0},{7,1},{8,14},{9,15},{10,... | collective-permute-start | bytes 344072 | tf_op jit(solution)/shard_map/ppermute | solution.py:26
  24.1 0.5 collective-permute-start.13
  24.7 0.8 %collective-permute-start.15 = (bf16[8,7168]{1,0:T(8,128)(2,1)S(1)}, bf16[8,7168]{1,0:T(8,128)(2,1)S(1)}, u32[]{:S(2)}, u32[]{:S(2)}) collective-permute-start(bf16[8,7168]{1,0:T(8,128)(2,1)S(1)} %shard_map.80), channel_id=1, source_target_pairs={{0,2},{1,3},{2,0},{3,1},{4,6},{5,7},{6,4},{7,5},{8,10},{9,11},{10,... | collective-permute-start | bytes 344072 | tf_op jit(solution)/shard_map/ppermute | solution.py:26
  25.5 1.5 %collective-permute-start.1 = (bf16[8,7168]{1,0:T(8,128)(2,1)S(1)}, bf16[8,7168]{1,0:T(8,128)(2,1)S(1)}, u32[]{:S(2)}, u32[]{:S(2)}) collective-permute-start(bf16[8,7168]{1,0:T(8,128)(2,1)S(1)} %get-tuple-element.40), channel_id=1, source_target_pairs={{0,16},{1,17},{2,18},{3,19},{4,20},{5,21},{6,22},{7,23},{8,24},{9,... | collective-permute-start | bytes 344072 | tf_op jit(solution)/shard_map/ppermute | solution.py:26
  27.0 1.7 %collective-permute-done.11.refs_2_ = bf16[8,7168]{1,0:T(8,128)(2,1)S(1)} collective-permute-done((bf16[8,7168]{1,0:T(8,128)(2,1)S(1)}, bf16[8,7168]{1,0:T(8,128)(2,1)S(1)}, u32[]{:S(2)}, u32[]{:S(2)}) %collective-permute-start.11) | collective-permute-done | bytes 114720 | tf_op jit(solution)/shard_map/ppermute | solution.py:26
  28.7 1.5 %collective-permute-done.13.refs_3_ = bf16[8,7168]{1,0:T(8,128)(2,1)S(1)} collective-permute-done((bf16[8,7168]{1,0:T(8,128)(2,1)S(1)}, bf16[8,7168]{1,0:T(8,128)(2,1)S(1)}, u32[]{:S(2)}, u32[]{:S(2)}) %collective-permute-start.13) | collective-permute-done | bytes 114720 | tf_op jit(solution)/shard_map/ppermute | solution.py:26
  30.2 0.4 collective-permute-done.15.refs_4_
  30.6 0.1 shard_map.81
  30.6 3.1 %collective-permute-start.17 = (bf16[8,7168]{1,0:T(8,128)(2,1)S(1)}, bf16[8,7168]{1,0:T(8,128)(2,1)S(1)}, u32[]{:S(2)}, u32[]{:S(2)}) collective-permute-start(bf16[8,7168]{1,0:T(8,128)(2,1)S(1)} %shard_map.81), channel_id=1, source_target_pairs={{0,24},{1,25},{2,26},{3,27},{4,28},{5,29},{6,30},{7,31},{8,16},{9,... | collective-permute-start | bytes 344072 | tf_op jit(solution)/shard_map/ppermute | solution.py:26
  33.7 0.5 collective-permute-start.16
  34.3 5.5 %collective-permute-done.17.far_ref = bf16[8,7168]{1,0:T(8,128)(2,1)S(1)} collective-permute-done((bf16[8,7168]{1,0:T(8,128)(2,1)S(1)}, bf16[8,7168]{1,0:T(8,128)(2,1)S(1)}, u32[]{:S(2)}, u32[]{:S(2)}) %collective-permute-start.17) | collective-permute-done | bytes 114720 | tf_op jit(solution)/shard_map/ppermute | solution.py:26
  39.8 0.1 collective-permute-done.16.near_ref
  40.0 0.2 shard_map.82
  40.2 2.1 %collective-permute-start.21 = (bf16[8,7168]{1,0:T(8,128)(2,1)S(1)}, bf16[8,7168]{1,0:T(8,128)(2,1)S(1)}, u32[]{:S(2)}, u32[]{:S(2)}) collective-permute-start(bf16[8,7168]{1,0:T(8,128)(2,1)S(1)} %get-tuple-element.57.refs_0_), channel_id=1, source_target_pairs={{0,6},{1,7},{2,4},{3,5},{4,2},{5,3},{6,0},{7,1},{8,14},{9,15},{10,... | collective-permute-start | bytes 344072 | tf_op jit(solution)/shard_map/ppermute | solution.py:26
  42.3 0.3 collective-permute-start.20
  42.6 1.1 %collective-permute-start.19 = (bf16[8,7168]{1,0:T(8,128)(2,1)S(1)}, bf16[8,7168]{1,0:T(8,128)(2,1)S(1)}, u32[]{:S(2)}, u32[]{:S(2)}) collective-permute-start(bf16[8,7168]{1,0:T(8,128)(2,1)S(1)} %get-tuple-element.57.refs_0_), channel_id=1, source_target_pairs={{0,2},{1,3},{2,0},{3,1},{4,6},{5,7},{6,4},{7,5},{8,10},{9,11},{10,... | collective-permute-start | bytes 344072 | tf_op jit(solution)/shard_map/ppermute | solution.py:26
  43.8 3.3 %collective-permute-done.21.refs_3_ = bf16[8,7168]{1,0:T(8,128)(2,1)S(1)} collective-permute-done((bf16[8,7168]{1,0:T(8,128)(2,1)S(1)}, bf16[8,7168]{1,0:T(8,128)(2,1)S(1)}, u32[]{:S(2)}, u32[]{:S(2)}) %collective-permute-start.21) | collective-permute-done | bytes 114720 | tf_op jit(solution)/shard_map/ppermute | solution.py:26
  47.1 0.7 %collective-permute-done.20.refs_2_ = bf16[8,7168]{1,0:T(8,128)(2,1)S(1)} collective-permute-done((bf16[8,7168]{1,0:T(8,128)(2,1)S(1)}, bf16[8,7168]{1,0:T(8,128)(2,1)S(1)}, u32[]{:S(2)}, u32[]{:S(2)}) %collective-permute-start.20) | collective-permute-done | bytes 114720 | tf_op jit(solution)/shard_map/ppermute | solution.py:26
  47.8 0.5 collective-permute-done.19.refs_1_
  48.3 0.1 collective-permute-start.23
  48.3 0.1 collective-permute-done.25.refs_7_
  48.4 0.8 %collective-permute-done.24.refs_6_ = bf16[8,7168]{1,0:T(8,128)(2,1)S(1)} collective-permute-done((bf16[8,7168]{1,0:T(8,128)(2,1)S(1)}, bf16[8,7168]{1,0:T(8,128)(2,1)S(1)}, u32[]{:S(2)}, u32[]{:S(2)}) %collective-permute-start.24) | collective-permute-done | bytes 114720 | tf_op jit(solution)/shard_map/ppermute | solution.py:26
  49.1 0.5 collective-permute-done.23.refs_5_
  49.6 2.1 %shard_map.83 = (bf16[8,7168]{1,0:T(8,128)(2,1)S(1)}, bf16[8,7168]{1,0:T(8,128)(2,1)S(1)}, bf16[8,7168]{1,0:T(8,128)(2,1)S(1)}, bf16[8,7168]{1,0:T(8,128)(2,1)S(...) custom-call(bf16[8,7168]{1,0:T(8,128)(2,1)S(1)} %get-tuple-element.5, ...), custom_call_target="tpu_custom_call" | custom-call | flops 704643072 | bytes 11010048 | tf_op jit(solution)/shard_map/pallas_call | solution.py:43
  51.7 0.2 collective-permute-start.27
  51.9 0.4 collective-permute-start.29
  52.3 0.1 collective-permute-start.31
  52.5 0.4 collective-permute-start.26
  52.8 0.3 collective-permute-done.27.refs_1_
  53.1 2.5 %collective-permute-start.28 = (bf16[8,7168]{1,0:T(8,128)(2,1)S(1)}, bf16[8,7168]{1,0:T(8,128)(2,1)S(1)}, u32[]{:S(2)}, u32[]{:S(2)}) collective-permute-start(bf16[8,7168]{1,0:T(8,128)(2,1)S(1)} %shard_map.84), channel_id=1, source_target_pairs={{0,6},{1,7},{2,4},{3,5},{4,2},{5,3},{6,0},{7,1},{8,14},{9,15},{10,... | collective-permute-start | bytes 344072 | tf_op jit(solution)/shard_map/ppermute | solution.py:26
  55.7 0.1 collective-permute-start.30
  55.8 1.1 %collective-permute-start.32 = (bf16[8,7168]{1,0:T(8,128)(2,1)S(1)}, bf16[8,7168]{1,0:T(8,128)(2,1)S(1)}, u32[]{:S(2)}, u32[]{:S(2)}) collective-permute-start(bf16[8,7168]{1,0:T(8,128)(2,1)S(1)} %shard_map.86), channel_id=1, source_target_pairs={{0,2},{1,3},{2,0},{3,1},{4,6},{5,7},{6,4},{7,5},{8,10},{9,11},{10,... | collective-permute-start | bytes 344072 | tf_op jit(solution)/shard_map/ppermute | solution.py:26
  56.9 1.3 %collective-permute-start.18 = (bf16[4,7168]{1,0:T(4,128)(2,1)S(1)}, bf16[4,7168]{1,0:T(4,128)(2,1)S(1)}, u32[]{:S(2)}, u32[]{:S(2)}) collective-permute-start(bf16[4,7168]{1,0:T(4,128)(2,1)S(1)} %get-tuple-element.56), channel_id=1, source_target_pairs={{0,16},{1,17},{2,18},{3,19},{4,20},{5,21},{6,22},{7,23},{8,24},{9,... | collective-permute-start | bytes 172040 | tf_op jit(solution)/shard_map/ppermute | solution.py:26
  58.2 1.9 %collective-permute-done.28.refs_2_ = bf16[8,7168]{1,0:T(8,128)(2,1)S(1)} collective-permute-done((bf16[8,7168]{1,0:T(8,128)(2,1)S(1)}, bf16[8,7168]{1,0:T(8,128)(2,1)S(1)}, u32[]{:S(2)}, u32[]{:S(2)}) %collective-permute-start.28) | collective-permute-done | bytes 114720 | tf_op jit(solution)/shard_map/ppermute | solution.py:26
  60.1 1.3 %collective-permute-done.30.refs_3_ = bf16[8,7168]{1,0:T(8,128)(2,1)S(1)} collective-permute-done((bf16[8,7168]{1,0:T(8,128)(2,1)S(1)}, bf16[8,7168]{1,0:T(8,128)(2,1)S(1)}, u32[]{:S(2)}, u32[]{:S(2)}) %collective-permute-start.30) | collective-permute-done | bytes 114720 | tf_op jit(solution)/shard_map/ppermute | solution.py:26
  61.4 0.4 collective-permute-done.32.refs_4_
  61.8 0.1 shard_map.87
  61.9 2.3 %collective-permute-start.33 = (bf16[4,7168]{1,0:T(4,128)(2,1)S(1)}, bf16[4,7168]{1,0:T(4,128)(2,1)S(1)}, u32[]{:S(2)}, u32[]{:S(2)}) collective-permute-start(bf16[4,7168]{1,0:T(4,128)(2,1)S(1)} %get-tuple-element.67), channel_id=1, source_target_pairs={{0,24},{1,25},{2,26},{3,27},{4,28},{5,29},{6,30},{7,31},{8,16},{9,... | collective-permute-start | bytes 172040 | tf_op jit(solution)/shard_map/ppermute | solution.py:26
  64.1 0.9 %collective-permute-start.34 = (bf16[4,7168]{1,0:T(4,128)(2,1)S(1)}, bf16[4,7168]{1,0:T(4,128)(2,1)S(1)}, u32[]{:S(2)}, u32[]{:S(2)}) collective-permute-start(bf16[4,7168]{1,0:T(4,128)(2,1)S(1)} %get-tuple-element.68), channel_id=1, source_target_pairs={{0,16},{1,17},{2,18},{3,19},{4,20},{5,21},{6,22},{7,23},{8,24},{9,... | collective-permute-start | bytes 172040 | tf_op jit(solution)/shard_map/ppermute | solution.py:26
  65.0 3.6 %collective-permute-done.33.refs_1_ = bf16[4,7168]{1,0:T(4,128)(2,1)S(1)} collective-permute-done((bf16[4,7168]{1,0:T(4,128)(2,1)S(1)}, bf16[4,7168]{1,0:T(4,128)(2,1)S(1)}, u32[]{:S(2)}, u32[]{:S(2)}) %collective-permute-start.33) | collective-permute-done | bytes 57376 | tf_op jit(solution)/shard_map/ppermute | solution.py:26
  68.6 0.3 collective-permute-done.34.refs_2_
  68.9 0.7 shard_map.88
  (24 shorter events, 0.2 us)
Async XLA Ops:
  1.0 7.3 %copy-start = (f32[1,7168]{1,0:T(1,128)S(1)}, f32[1,7168]{1,0:T(1,128)}, u32[]{:S(2)}) copy-start(f32[1,7168]{1,0:T(1,128)} %gain_ref.3) | copy-start | bytes 86020
  1.0 7.3 %collective-permute-start = (bf16[4,7296]{1,0:T(4,128)(2,1)S(1)}, bf16[4,7296]{1,0:T(4,128)(2,1)S(1)}, u32[]{:S(2)}, u32[]{:S(2)}) collective-permute-start(bf16[4,7296]{1,0:T(4,128)(2,1)S(1)} %shard_map.73.own_ref), channel_id=1, source_target_pairs={{0,8},{1,9},{2,10},{3,11},{4,12},{5,13},{6,14},{7,15},{8,0},{9,1},... | collective-permute-start | bytes 175112 | tf_op jit(solution)/shard_map/ppermute | solution.py:26
  8.5 7.0 %collective-permute-start.4 = (bf16[8,7296]{1,0:T(8,128)(2,1)S(1)}, bf16[8,7296]{1,0:T(8,128)(2,1)S(1)}, u32[]{:S(2)}, u32[]{:S(2)}) collective-permute-start(bf16[8,7296]{1,0:T(8,128)(2,1)S(1)} %get-tuple-element.44.refs_0_), channel_id=1, source_target_pairs={{0,6},{1,7},{2,4},{3,5},{4,2},{5,3},{6,0},{7,1},{8,14},{9,15},{10,... | collective-permute-start | bytes 350216 | tf_op jit(solution)/shard_map/ppermute | solution.py:26
  11.1 5.6 %collective-permute-start.3 = (bf16[8,7296]{1,0:T(8,128)(2,1)S(1)}, bf16[8,7296]{1,0:T(8,128)(2,1)S(1)}, u32[]{:S(2)}, u32[]{:S(2)}) collective-permute-start(bf16[8,7296]{1,0:T(8,128)(2,1)S(1)} %get-tuple-element.44.refs_0_), channel_id=1, source_target_pairs={{0,4},{1,5},{2,6},{3,7},{4,0},{5,1},{6,2},{7,3},{8,12},{9,13},{10,... | collective-permute-start | bytes 350216 | tf_op jit(solution)/shard_map/ppermute | solution.py:26
  12.0 4.9 %collective-permute-start.2 = (bf16[8,7296]{1,0:T(8,128)(2,1)S(1)}, bf16[8,7296]{1,0:T(8,128)(2,1)S(1)}, u32[]{:S(2)}, u32[]{:S(2)}) collective-permute-start(bf16[8,7296]{1,0:T(8,128)(2,1)S(1)} %get-tuple-element.44.refs_0_), channel_id=1, source_target_pairs={{0,2},{1,3},{2,0},{3,1},{4,6},{5,7},{6,4},{7,5},{8,10},{9,11},{10,... | collective-permute-start | bytes 350216 | tf_op jit(solution)/shard_map/ppermute | solution.py:26
  14.1 3.1 %collective-permute-start.5 = (bf16[8,7296]{1,0:T(8,128)(2,1)S(1)}, bf16[8,7296]{1,0:T(8,128)(2,1)S(1)}, u32[]{:S(2)}, u32[]{:S(2)}) collective-permute-start(bf16[8,7296]{1,0:T(8,128)(2,1)S(1)} %get-tuple-element.44.refs_0_), channel_id=1, source_target_pairs={{0,1},{1,0},{2,3},{3,2},{4,5},{5,4},{6,7},{7,6},{8,9},{9,8},{10,11... | collective-permute-start | bytes 350216 | tf_op jit(solution)/shard_map/ppermute | solution.py:26
  15.5 1.7 %collective-permute-start.8 = (bf16[8,7296]{1,0:T(8,128)(2,1)S(1)}, bf16[8,7296]{1,0:T(8,128)(2,1)S(1)}, u32[]{:S(2)}, u32[]{:S(2)}) collective-permute-start(bf16[8,7296]{1,0:T(8,128)(2,1)S(1)} %collective-permute-done.4.refs_3_), channel_id=1, source_target_pairs={{0,1},{1,0},{2,3},{3,2},{4,5},{5,4},{6,7},{7,6},{8,9},{9,8},{10,11... | collective-permute-start | bytes 350216 | tf_op jit(solution)/shard_map/ppermute | solution.py:26
  16.7 1.3 %collective-permute-start.7 = (bf16[8,7296]{1,0:T(8,128)(2,1)S(1)}, bf16[8,7296]{1,0:T(8,128)(2,1)S(1)}, u32[]{:S(2)}, u32[]{:S(2)}) collective-permute-start(bf16[8,7296]{1,0:T(8,128)(2,1)S(1)} %collective-permute-done.3.refs_2_), channel_id=1, source_target_pairs={{0,1},{1,0},{2,3},{3,2},{4,5},{5,4},{6,7},{7,6},{8,9},{9,8},{10,11... | collective-permute-start | bytes 350216 | tf_op jit(solution)/shard_map/ppermute | solution.py:26
  16.8 1.4 %collective-permute-start.6 = (bf16[8,7296]{1,0:T(8,128)(2,1)S(1)}, bf16[8,7296]{1,0:T(8,128)(2,1)S(1)}, u32[]{:S(2)}, u32[]{:S(2)}) collective-permute-start(bf16[8,7296]{1,0:T(8,128)(2,1)S(1)} %collective-permute-done.2.refs_1_), channel_id=1, source_target_pairs={{0,1},{1,0},{2,3},{3,2},{4,5},{5,4},{6,7},{7,6},{8,9},{9,8},{10,11... | collective-permute-start | bytes 350216 | tf_op jit(solution)/shard_map/ppermute | solution.py:26
  20.3 1.4 %collective-permute-start.10 = (bf16[8,7168]{1,0:T(8,128)(2,1)S(1)}, bf16[8,7168]{1,0:T(8,128)(2,1)S(1)}, u32[]{:S(2)}, u32[]{:S(2)}) collective-permute-start(bf16[8,7168]{1,0:T(8,128)(2,1)S(1)} %get-tuple-element.51), channel_id=1, source_target_pairs={{0,1},{1,0},{2,3},{3,2},{4,5},{5,4},{6,7},{7,6},{8,9},{9,8},{10,11... | collective-permute-start | bytes 344072 | tf_op jit(solution)/shard_map/ppermute | solution.py:26
  20.7 3.3 %collective-permute-start.12 = (bf16[8,7168]{1,0:T(8,128)(2,1)S(1)}, bf16[8,7168]{1,0:T(8,128)(2,1)S(1)}, u32[]{:S(2)}, u32[]{:S(2)}) collective-permute-start(bf16[8,7168]{1,0:T(8,128)(2,1)S(1)} %get-tuple-element.53), channel_id=1, source_target_pairs={{0,1},{1,0},{2,3},{3,2},{4,5},{5,4},{6,7},{7,6},{8,9},{9,8},{10,11... | collective-permute-start | bytes 344072 | tf_op jit(solution)/shard_map/ppermute | solution.py:26
  20.9 3.7 %collective-permute-start.14 = (bf16[8,7168]{1,0:T(8,128)(2,1)S(1)}, bf16[8,7168]{1,0:T(8,128)(2,1)S(1)}, u32[]{:S(2)}, u32[]{:S(2)}) collective-permute-start(bf16[8,7168]{1,0:T(8,128)(2,1)S(1)} %get-tuple-element.55), channel_id=1, source_target_pairs={{0,1},{1,0},{2,3},{3,2},{4,5},{5,4},{6,7},{7,6},{8,9},{9,8},{10,11... | collective-permute-start | bytes 344072 | tf_op jit(solution)/shard_map/ppermute | solution.py:26
  21.3 5.8 %collective-permute-start.9 = (bf16[8,7168]{1,0:T(8,128)(2,1)S(1)}, bf16[8,7168]{1,0:T(8,128)(2,1)S(1)}, u32[]{:S(2)}, u32[]{:S(2)}) collective-permute-start(bf16[8,7168]{1,0:T(8,128)(2,1)S(1)} %get-tuple-element.49), channel_id=1, source_target_pairs={{0,1},{1,0},{2,3},{3,2},{4,5},{5,4},{6,7},{7,6},{8,9},{9,8},{10,11... | collective-permute-start | bytes 344072 | tf_op jit(solution)/shard_map/ppermute | solution.py:26
  21.7 6.9 %collective-permute-start.11 = (bf16[8,7168]{1,0:T(8,128)(2,1)S(1)}, bf16[8,7168]{1,0:T(8,128)(2,1)S(1)}, u32[]{:S(2)}, u32[]{:S(2)}) collective-permute-start(bf16[8,7168]{1,0:T(8,128)(2,1)S(1)} %shard_map.78), channel_id=1, source_target_pairs={{0,6},{1,7},{2,4},{3,5},{4,2},{5,3},{6,0},{7,1},{8,14},{9,15},{10,... | collective-permute-start | bytes 344072 | tf_op jit(solution)/shard_map/ppermute | solution.py:26
  24.1 6.0 %collective-permute-start.13 = (bf16[8,7168]{1,0:T(8,128)(2,1)S(1)}, bf16[8,7168]{1,0:T(8,128)(2,1)S(1)}, u32[]{:S(2)}, u32[]{:S(2)}) collective-permute-start(bf16[8,7168]{1,0:T(8,128)(2,1)S(1)} %shard_map.79), channel_id=1, source_target_pairs={{0,4},{1,5},{2,6},{3,7},{4,0},{5,1},{6,2},{7,3},{8,12},{9,13},{10,... | collective-permute-start | bytes 344072 | tf_op jit(solution)/shard_map/ppermute | solution.py:26
  24.7 5.9 %collective-permute-start.15 = (bf16[8,7168]{1,0:T(8,128)(2,1)S(1)}, bf16[8,7168]{1,0:T(8,128)(2,1)S(1)}, u32[]{:S(2)}, u32[]{:S(2)}) collective-permute-start(bf16[8,7168]{1,0:T(8,128)(2,1)S(1)} %shard_map.80), channel_id=1, source_target_pairs={{0,2},{1,3},{2,0},{3,1},{4,6},{5,7},{6,4},{7,5},{8,10},{9,11},{10,... | collective-permute-start | bytes 344072 | tf_op jit(solution)/shard_map/ppermute | solution.py:26
  25.5 8.8 %collective-permute-start.1 = (bf16[8,7168]{1,0:T(8,128)(2,1)S(1)}, bf16[8,7168]{1,0:T(8,128)(2,1)S(1)}, u32[]{:S(2)}, u32[]{:S(2)}) collective-permute-start(bf16[8,7168]{1,0:T(8,128)(2,1)S(1)} %get-tuple-element.40), channel_id=1, source_target_pairs={{0,16},{1,17},{2,18},{3,19},{4,20},{5,21},{6,22},{7,23},{8,24},{9,... | collective-permute-start | bytes 344072 | tf_op jit(solution)/shard_map/ppermute | solution.py:26
  30.6 9.2 %collective-permute-start.17 = (bf16[8,7168]{1,0:T(8,128)(2,1)S(1)}, bf16[8,7168]{1,0:T(8,128)(2,1)S(1)}, u32[]{:S(2)}, u32[]{:S(2)}) collective-permute-start(bf16[8,7168]{1,0:T(8,128)(2,1)S(1)} %shard_map.81), channel_id=1, source_target_pairs={{0,24},{1,25},{2,26},{3,27},{4,28},{5,29},{6,30},{7,31},{8,16},{9,... | collective-permute-start | bytes 344072 | tf_op jit(solution)/shard_map/ppermute | solution.py:26
  33.7 6.2 %collective-permute-start.16 = (bf16[8,7168]{1,0:T(8,128)(2,1)S(1)}, bf16[8,7168]{1,0:T(8,128)(2,1)S(1)}, u32[]{:S(2)}, u32[]{:S(2)}) collective-permute-start(bf16[8,7168]{1,0:T(8,128)(2,1)S(1)} %shard_map.81), channel_id=1, source_target_pairs={{0,16},{1,17},{2,18},{3,19},{4,20},{5,21},{6,22},{7,23},{8,24},{9,... | collective-permute-start | bytes 344072 | tf_op jit(solution)/shard_map/ppermute | solution.py:26
  40.2 6.9 %collective-permute-start.21 = (bf16[8,7168]{1,0:T(8,128)(2,1)S(1)}, bf16[8,7168]{1,0:T(8,128)(2,1)S(1)}, u32[]{:S(2)}, u32[]{:S(2)}) collective-permute-start(bf16[8,7168]{1,0:T(8,128)(2,1)S(1)} %get-tuple-element.57.refs_0_), channel_id=1, source_target_pairs={{0,6},{1,7},{2,4},{3,5},{4,2},{5,3},{6,0},{7,1},{8,14},{9,15},{10,... | collective-permute-start | bytes 344072 | tf_op jit(solution)/shard_map/ppermute | solution.py:26
  42.3 5.6 %collective-permute-start.20 = (bf16[8,7168]{1,0:T(8,128)(2,1)S(1)}, bf16[8,7168]{1,0:T(8,128)(2,1)S(1)}, u32[]{:S(2)}, u32[]{:S(2)}) collective-permute-start(bf16[8,7168]{1,0:T(8,128)(2,1)S(1)} %get-tuple-element.57.refs_0_), channel_id=1, source_target_pairs={{0,4},{1,5},{2,6},{3,7},{4,0},{5,1},{6,2},{7,3},{8,12},{9,13},{10,... | collective-permute-start | bytes 344072 | tf_op jit(solution)/shard_map/ppermute | solution.py:26
  42.6 5.7 %collective-permute-start.19 = (bf16[8,7168]{1,0:T(8,128)(2,1)S(1)}, bf16[8,7168]{1,0:T(8,128)(2,1)S(1)}, u32[]{:S(2)}, u32[]{:S(2)}) collective-permute-start(bf16[8,7168]{1,0:T(8,128)(2,1)S(1)} %get-tuple-element.57.refs_0_), channel_id=1, source_target_pairs={{0,2},{1,3},{2,0},{3,1},{4,6},{5,7},{6,4},{7,5},{8,10},{9,11},{10,... | collective-permute-start | bytes 344072 | tf_op jit(solution)/shard_map/ppermute | solution.py:26
  43.7 4.6 %collective-permute-start.22 = (bf16[8,7168]{1,0:T(8,128)(2,1)S(1)}, bf16[8,7168]{1,0:T(8,128)(2,1)S(1)}, u32[]{:S(2)}, u32[]{:S(2)}) collective-permute-start(bf16[8,7168]{1,0:T(8,128)(2,1)S(1)} %get-tuple-element.57.refs_0_), channel_id=1, source_target_pairs={{0,1},{1,0},{2,3},{3,2},{4,5},{5,4},{6,7},{7,6},{8,9},{9,8},{10,11... | collective-permute-start | bytes 344072 | tf_op jit(solution)/shard_map/ppermute | solution.py:26
  47.1 1.3 %collective-permute-start.25 = (bf16[8,7168]{1,0:T(8,128)(2,1)S(1)}, bf16[8,7168]{1,0:T(8,128)(2,1)S(1)}, u32[]{:S(2)}, u32[]{:S(2)}) collective-permute-start(bf16[8,7168]{1,0:T(8,128)(2,1)S(1)} %collective-permute-done.21.refs_3_), channel_id=1, source_target_pairs={{0,1},{1,0},{2,3},{3,2},{4,5},{5,4},{6,7},{7,6},{8,9},{9,8},{10,11... | collective-permute-start | bytes 344072 | tf_op jit(solution)/shard_map/ppermute | solution.py:26
  47.8 1.3 %collective-permute-start.24 = (bf16[8,7168]{1,0:T(8,128)(2,1)S(1)}, bf16[8,7168]{1,0:T(8,128)(2,1)S(1)}, u32[]{:S(2)}, u32[]{:S(2)}) collective-permute-start(bf16[8,7168]{1,0:T(8,128)(2,1)S(1)} %collective-permute-done.20.refs_2_), channel_id=1, source_target_pairs={{0,1},{1,0},{2,3},{3,2},{4,5},{5,4},{6,7},{7,6},{8,9},{9,8},{10,11... | collective-permute-start | bytes 344072 | tf_op jit(solution)/shard_map/ppermute | solution.py:26
  48.3 1.3 %collective-permute-start.23 = (bf16[8,7168]{1,0:T(8,128)(2,1)S(1)}, bf16[8,7168]{1,0:T(8,128)(2,1)S(1)}, u32[]{:S(2)}, u32[]{:S(2)}) collective-permute-start(bf16[8,7168]{1,0:T(8,128)(2,1)S(1)} %collective-permute-done.19.refs_1_), channel_id=1, source_target_pairs={{0,1},{1,0},{2,3},{3,2},{4,5},{5,4},{6,7},{7,6},{8,9},{9,8},{10,11... | collective-permute-start | bytes 344072 | tf_op jit(solution)/shard_map/ppermute | solution.py:26
  51.7 1.4 %collective-permute-start.27 = (bf16[8,7168]{1,0:T(8,128)(2,1)S(1)}, bf16[8,7168]{1,0:T(8,128)(2,1)S(1)}, u32[]{:S(2)}, u32[]{:S(2)}) collective-permute-start(bf16[8,7168]{1,0:T(8,128)(2,1)S(1)} %get-tuple-element.62), channel_id=1, source_target_pairs={{0,1},{1,0},{2,3},{3,2},{4,5},{5,4},{6,7},{7,6},{8,9},{9,8},{10,11... | collective-permute-start | bytes 344072 | tf_op jit(solution)/shard_map/ppermute | solution.py:26
  51.9 3.7 %collective-permute-start.29 = (bf16[8,7168]{1,0:T(8,128)(2,1)S(1)}, bf16[8,7168]{1,0:T(8,128)(2,1)S(1)}, u32[]{:S(2)}, u32[]{:S(2)}) collective-permute-start(bf16[8,7168]{1,0:T(8,128)(2,1)S(1)} %get-tuple-element.64), channel_id=1, source_target_pairs={{0,1},{1,0},{2,3},{3,2},{4,5},{5,4},{6,7},{7,6},{8,9},{9,8},{10,11... | collective-permute-start | bytes 344072 | tf_op jit(solution)/shard_map/ppermute | solution.py:26
  52.3 3.4 %collective-permute-start.31 = (bf16[8,7168]{1,0:T(8,128)(2,1)S(1)}, bf16[8,7168]{1,0:T(8,128)(2,1)S(1)}, u32[]{:S(2)}, u32[]{:S(2)}) collective-permute-start(bf16[8,7168]{1,0:T(8,128)(2,1)S(1)} %get-tuple-element.66), channel_id=1, source_target_pairs={{0,1},{1,0},{2,3},{3,2},{4,5},{5,4},{6,7},{7,6},{8,9},{9,8},{10,11... | collective-permute-start | bytes 344072 | tf_op jit(solution)/shard_map/ppermute | solution.py:26
  52.5 5.7 %collective-permute-start.26 = (bf16[8,7168]{1,0:T(8,128)(2,1)S(1)}, bf16[8,7168]{1,0:T(8,128)(2,1)S(1)}, u32[]{:S(2)}, u32[]{:S(2)}) collective-permute-start(bf16[8,7168]{1,0:T(8,128)(2,1)S(1)} %get-tuple-element.60), channel_id=1, source_target_pairs={{0,1},{1,0},{2,3},{3,2},{4,5},{5,4},{6,7},{7,6},{8,9},{9,8},{10,11... | collective-permute-start | bytes 344072 | tf_op jit(solution)/shard_map/ppermute | solution.py:26
  53.1 7.0 %collective-permute-start.28 = (bf16[8,7168]{1,0:T(8,128)(2,1)S(1)}, bf16[8,7168]{1,0:T(8,128)(2,1)S(1)}, u32[]{:S(2)}, u32[]{:S(2)}) collective-permute-start(bf16[8,7168]{1,0:T(8,128)(2,1)S(1)} %shard_map.84), channel_id=1, source_target_pairs={{0,6},{1,7},{2,4},{3,5},{4,2},{5,3},{6,0},{7,1},{8,14},{9,15},{10,... | collective-permute-start | bytes 344072 | tf_op jit(solution)/shard_map/ppermute | solution.py:26
  55.7 5.7 %collective-permute-start.30 = (bf16[8,7168]{1,0:T(8,128)(2,1)S(1)}, bf16[8,7168]{1,0:T(8,128)(2,1)S(1)}, u32[]{:S(2)}, u32[]{:S(2)}) collective-permute-start(bf16[8,7168]{1,0:T(8,128)(2,1)S(1)} %shard_map.85), channel_id=1, source_target_pairs={{0,4},{1,5},{2,6},{3,7},{4,0},{5,1},{6,2},{7,3},{8,12},{9,13},{10,... | collective-permute-start | bytes 344072 | tf_op jit(solution)/shard_map/ppermute | solution.py:26
  55.8 6.0 %collective-permute-start.32 = (bf16[8,7168]{1,0:T(8,128)(2,1)S(1)}, bf16[8,7168]{1,0:T(8,128)(2,1)S(1)}, u32[]{:S(2)}, u32[]{:S(2)}) collective-permute-start(bf16[8,7168]{1,0:T(8,128)(2,1)S(1)} %shard_map.86), channel_id=1, source_target_pairs={{0,2},{1,3},{2,0},{3,1},{4,6},{5,7},{6,4},{7,5},{8,10},{9,11},{10,... | collective-permute-start | bytes 344072 | tf_op jit(solution)/shard_map/ppermute | solution.py:26
  56.9 8.1 %collective-permute-start.18 = (bf16[4,7168]{1,0:T(4,128)(2,1)S(1)}, bf16[4,7168]{1,0:T(4,128)(2,1)S(1)}, u32[]{:S(2)}, u32[]{:S(2)}) collective-permute-start(bf16[4,7168]{1,0:T(4,128)(2,1)S(1)} %get-tuple-element.56), channel_id=1, source_target_pairs={{0,16},{1,17},{2,18},{3,19},{4,20},{5,21},{6,22},{7,23},{8,24},{9,... | collective-permute-start | bytes 172040 | tf_op jit(solution)/shard_map/ppermute | solution.py:26
  61.9 6.7 %collective-permute-start.33 = (bf16[4,7168]{1,0:T(4,128)(2,1)S(1)}, bf16[4,7168]{1,0:T(4,128)(2,1)S(1)}, u32[]{:S(2)}, u32[]{:S(2)}) collective-permute-start(bf16[4,7168]{1,0:T(4,128)(2,1)S(1)} %get-tuple-element.67), channel_id=1, source_target_pairs={{0,24},{1,25},{2,26},{3,27},{4,28},{5,29},{6,30},{7,31},{8,16},{9,... | collective-permute-start | bytes 172040 | tf_op jit(solution)/shard_map/ppermute | solution.py:26
  64.1 4.8 %collective-permute-start.34 = (bf16[4,7168]{1,0:T(4,128)(2,1)S(1)}, bf16[4,7168]{1,0:T(4,128)(2,1)S(1)}, u32[]{:S(2)}, u32[]{:S(2)}) collective-permute-start(bf16[4,7168]{1,0:T(4,128)(2,1)S(1)} %get-tuple-element.68), channel_id=1, source_target_pairs={{0,16},{1,17},{2,18},{3,19},{4,20},{5,21},{6,22},{7,23},{8,24},{9,... | collective-permute-start | bytes 172040 | tf_op jit(solution)/shard_map/ppermute | solution.py:26

commit v17 on v16

--- a/solution.py
+++ b/solution.py
@@ -31,7 +31,7 @@
 
 
 CORE = (1, 1)
-SQUARE = ((2, 2), (4, 4), (6, 6))
+SQUARE = ((4, 4), (2, 2), (6, 6))
 STAY = (0, 0)
 
 

time: 69.7 us -> 70.6 us (1.013)
  waiting for transfers between devices: 26.7 us -> 27.7 us
    ppermute x35, waiting for transfers between devices: 26.7 us -> 27.7 us  [exchange(): return lax.ppermute(value, ('segment', 'expert'), pairs)]
  transfers between devices with their start and end apart: 35 -> 35, of which waited for: 23 -> 18; matrix products, arithmetic and copies ran while one was open for 0% -> 0% of each run, Pallas kernels for 8% -> 8%
where the time goes in v17:
time: 70.6 us; the launch traced here: 70.4 us
  starting transfers between devices  30.7 us (43%)
  waiting for transfers between devices  27.7 us (39%)
  Pallas kernels  11.8 us (17%)
    ppermute x35, starting transfers between devices, exchange(): return lax.ppermute(value, ('segment', 'expert'), pairs)  30.7 us
    ppermute x35, waiting for transfers between devices, exchange(): return lax.ppermute(value, ('segment', 'expert'), pairs)  27.7 us
    pallas_call x14, Pallas kernels, call(): pl.pallas_call(kernel, out_shape=[jax.ShapeDtypeStruct(shape, jnp.bfloat1...  6.6 us
    pallas_call x2, Pallas kernels, load(): pl.pallas_call(functools.partial(load_kernel, count), out_shape=[pltpu.VM...  5.22 us
  transfers between devices with their start and end apart: 35, of which 18 were waited for; matrix products, arithmetic and copies ran while one was open for 0% of the time, Pallas kernels for 8%

profile of v17, /device:TPU:0, one launch (start us, length us, event | category | flops | bytes accessed | tf_op | source)
XLA Modules:
  0.0 70.4 jit_solution(6893854013804425375)
XLA Ops:
  0.0 1.0 %shard_map.73.own_ref = bf16[4,7296]{1,0:T(4,128)(2,1)S(1)} custom-call(bf16[1,4,7168]{2,1,0:T(4,128)(2,1)} %states_hbm.1, s32[1,2,2,4]{3,2,1,0:T(2,128)} %bitcast.3, bf16[1,2,2,4]{3,2,1,0:T(2,128)(2,1)} %bitcast.4), custom_call_target="tpu_custom_call" | custom-call | tf_op jit(solution)/shard_map/pallas_call | solution.py:43
  1.0 0.0 copy-start
  1.0 4.1 %collective-permute-start = (bf16[4,7296]{1,0:T(4,128)(2,1)S(1)}, bf16[4,7296]{1,0:T(4,128)(2,1)S(1)}, u32[]{:S(2)}, u32[]{:S(2)}) collective-permute-start(bf16[4,7296]{1,0:T(4,128)(2,1)S(1)} %shard_map.73.own_ref), channel_id=1, source_target_pairs={{0,8},{1,9},{2,10},{3,11},{4,12},{5,13},{6,14},{7,15},{8,0},{9,1},... | collective-permute-start | bytes 175112 | tf_op jit(solution)/shard_map/ppermute | solution.py:26
  5.1 3.2 %shard_map.74 = (bf16[1,7168,256]{2,1,0:T(8,128)(2,1)S(1)}, bf16[1,7168,256]{2,1,0:T(8,128)(2,1)S(1)}) custom-call(bf16[1,7168,256]{2,1,0:T(8,128)(2,1)} %refs_0_.1, bf16[1,7168,256]{2,1,0:T(8,128)(2,1)} %refs_1_.1), custom_call_target="tpu_custom_call" | custom-call | bytes 7340032 | tf_op jit(solution)/shard_map/pallas_call | solution.py:64
  8.3 0.2 shard_map.75
  8.5 2.6 %collective-permute-start.4 = (bf16[8,7296]{1,0:T(8,128)(2,1)S(1)}, bf16[8,7296]{1,0:T(8,128)(2,1)S(1)}, u32[]{:S(2)}, u32[]{:S(2)}) collective-permute-start(bf16[8,7296]{1,0:T(8,128)(2,1)S(1)} %get-tuple-element.44.refs_0_), channel_id=1, source_target_pairs={{0,6},{1,7},{2,4},{3,5},{4,2},{5,3},{6,0},{7,1},{8,14},{9,15},{10,... | collective-permute-start | bytes 350216 | tf_op jit(solution)/shard_map/ppermute | solution.py:26
  11.1 0.5 collective-permute-start.3
  11.6 0.4 collective-permute-start.2
  12.0 2.0 %shard_map.76.refs_10_.refs_11_ = bf16[1,256,7168]{2,1,0:T(8,128)(2,1)S(1)} custom-call(bf16[1,256,7168]{2,1,0:T(8,128)(2,1)} %refs_0_.2), custom_call_target="tpu_custom_call" | custom-call | bytes 3670016 | tf_op jit(solution)/shard_map/pallas_call | solution.py:64
  14.1 0.1 collective-permute-start.5
  14.2 0.4 collective-permute-done.4.refs_3_
  14.6 0.1 collective-permute-start.8
  14.7 2.0 %collective-permute-done.3.refs_2_ = bf16[8,7296]{1,0:T(8,128)(2,1)S(1)} collective-permute-done((bf16[8,7296]{1,0:T(8,128)(2,1)S(1)}, bf16[8,7296]{1,0:T(8,128)(2,1)S(1)}, u32[]{:S(2)}, u32[]{:S(2)}) %collective-permute-start.3) | collective-permute-done | bytes 116768 | tf_op jit(solution)/shard_map/ppermute | solution.py:26
  16.7 0.0 collective-permute-start.7
  16.7 0.2 collective-permute-done.2.refs_1_
  16.9 0.3 collective-permute-start.6
  17.2 0.0 collective-permute-done.5.refs_4_
  17.2 0.0 collective-permute-done.8.refs_7_
  17.2 0.8 %collective-permute-done.7.refs_6_ = bf16[8,7296]{1,0:T(8,128)(2,1)S(1)} collective-permute-done((bf16[8,7296]{1,0:T(8,128)(2,1)S(1)}, bf16[8,7296]{1,0:T(8,128)(2,1)S(1)}, u32[]{:S(2)}, u32[]{:S(2)}) %collective-permute-start.7) | collective-permute-done | bytes 116768 | tf_op jit(solution)/shard_map/ppermute | solution.py:26
  18.0 0.2 collective-permute-done.6.refs_5_
  18.3 2.1 %shard_map.77 = (bf16[8,7168]{1,0:T(8,128)(2,1)S(1)}, bf16[8,7168]{1,0:T(8,128)(2,1)S(1)}, bf16[8,7168]{1,0:T(8,128)(2,1)S(1)}, bf16[8,7168]{1,0:T(8,128)(2,1)S(...) custom-call(bf16[8,7296]{1,0:T(8,128)(2,1)S(1)} %get-tuple-element.4, ...), custom_call_target="tpu_custom_call" | custom-call | flops 704643072 | bytes 11010048 | tf_op jit(solution)/shard_map/pallas_call | solution.py:43
  20.4 0.3 collective-permute-start.10
  20.7 0.2 collective-permute-start.12
  21.0 0.3 collective-permute-start.14
  21.3 0.2 collective-permute-start.9
  21.5 0.3 collective-permute-done.10.refs_1_
  21.8 1.6 %collective-permute-start.11 = (bf16[8,7168]{1,0:T(8,128)(2,1)S(1)}, bf16[8,7168]{1,0:T(8,128)(2,1)S(1)}, u32[]{:S(2)}, u32[]{:S(2)}) collective-permute-start(bf16[8,7168]{1,0:T(8,128)(2,1)S(1)} %shard_map.78), channel_id=1, source_target_pairs={{0,6},{1,7},{2,4},{3,5},{4,2},{5,3},{6,0},{7,1},{8,14},{9,15},{10,... | collective-permute-start | bytes 344072 | tf_op jit(solution)/shard_map/ppermute | solution.py:26
  23.5 0.0 collective-permute-done.12.refs_1_
  23.5 1.4 %collective-permute-start.13 = (bf16[8,7168]{1,0:T(8,128)(2,1)S(1)}, bf16[8,7168]{1,0:T(8,128)(2,1)S(1)}, u32[]{:S(2)}, u32[]{:S(2)}) collective-permute-start(bf16[8,7168]{1,0:T(8,128)(2,1)S(1)} %shard_map.79), channel_id=1, source_target_pairs={{0,2},{1,3},{2,0},{3,1},{4,6},{5,7},{6,4},{7,5},{8,10},{9,11},{10,... | collective-permute-start | bytes 344072 | tf_op jit(solution)/shard_map/ppermute | solution.py:26
  24.9 0.0 collective-permute-done.14.refs_1_
  24.9 0.7 collective-permute-start.15
  25.6 1.5 %collective-permute-start.1 = (bf16[8,7168]{1,0:T(8,128)(2,1)S(1)}, bf16[8,7168]{1,0:T(8,128)(2,1)S(1)}, u32[]{:S(2)}, u32[]{:S(2)}) collective-permute-start(bf16[8,7168]{1,0:T(8,128)(2,1)S(1)} %get-tuple-element.40), channel_id=1, source_target_pairs={{0,16},{1,17},{2,18},{3,19},{4,20},{5,21},{6,22},{7,23},{8,24},{9,... | collective-permute-start | bytes 344072 | tf_op jit(solution)/shard_map/ppermute | solution.py:26
  27.1 1.6 %collective-permute-done.11.refs_2_ = bf16[8,7168]{1,0:T(8,128)(2,1)S(1)} collective-permute-done((bf16[8,7168]{1,0:T(8,128)(2,1)S(1)}, bf16[8,7168]{1,0:T(8,128)(2,1)S(1)}, u32[]{:S(2)}, u32[]{:S(2)}) %collective-permute-start.11) | collective-permute-done | bytes 114720 | tf_op jit(solution)/shard_map/ppermute | solution.py:26
  28.7 1.9 %collective-permute-done.13.refs_3_ = bf16[8,7168]{1,0:T(8,128)(2,1)S(1)} collective-permute-done((bf16[8,7168]{1,0:T(8,128)(2,1)S(1)}, bf16[8,7168]{1,0:T(8,128)(2,1)S(1)}, u32[]{:S(2)}, u32[]{:S(2)}) %collective-permute-start.13) | collective-permute-done | bytes 114720 | tf_op jit(solution)/shard_map/ppermute | solution.py:26
  30.6 0.1 shard_map.81
  30.7 3.2 %collective-permute-start.17 = (bf16[8,7168]{1,0:T(8,128)(2,1)S(1)}, bf16[8,7168]{1,0:T(8,128)(2,1)S(1)}, u32[]{:S(2)}, u32[]{:S(2)}) collective-permute-start(bf16[8,7168]{1,0:T(8,128)(2,1)S(1)} %shard_map.81), channel_id=1, source_target_pairs={{0,24},{1,25},{2,26},{3,27},{4,28},{5,29},{6,30},{7,31},{8,16},{9,... | collective-permute-start | bytes 344072 | tf_op jit(solution)/shard_map/ppermute | solution.py:26
  33.8 0.5 collective-permute-start.16
  34.3 5.7 %collective-permute-done.17.far_ref = bf16[8,7168]{1,0:T(8,128)(2,1)S(1)} collective-permute-done((bf16[8,7168]{1,0:T(8,128)(2,1)S(1)}, bf16[8,7168]{1,0:T(8,128)(2,1)S(1)}, u32[]{:S(2)}, u32[]{:S(2)}) %collective-permute-start.17) | collective-permute-done | bytes 114720 | tf_op jit(solution)/shard_map/ppermute | solution.py:26
  40.1 0.2 shard_map.82
  40.3 1.8 %collective-permute-start.21 = (bf16[8,7168]{1,0:T(8,128)(2,1)S(1)}, bf16[8,7168]{1,0:T(8,128)(2,1)S(1)}, u32[]{:S(2)}, u32[]{:S(2)}) collective-permute-start(bf16[8,7168]{1,0:T(8,128)(2,1)S(1)} %get-tuple-element.57.refs_0_), channel_id=1, source_target_pairs={{0,6},{1,7},{2,4},{3,5},{4,2},{5,3},{6,0},{7,1},{8,14},{9,15},{10,... | collective-permute-start | bytes 344072 | tf_op jit(solution)/shard_map/ppermute | solution.py:26
  42.1 1.3 %collective-permute-start.20 = (bf16[8,7168]{1,0:T(8,128)(2,1)S(1)}, bf16[8,7168]{1,0:T(8,128)(2,1)S(1)}, u32[]{:S(2)}, u32[]{:S(2)}) collective-permute-start(bf16[8,7168]{1,0:T(8,128)(2,1)S(1)} %get-tuple-element.57.refs_0_), channel_id=1, source_target_pairs={{0,2},{1,3},{2,0},{3,1},{4,6},{5,7},{6,4},{7,5},{8,10},{9,11},{10,... | collective-permute-start | bytes 344072 | tf_op jit(solution)/shard_map/ppermute | solution.py:26
  43.4 0.5 collective-permute-start.19
  43.9 2.7 %collective-permute-done.21.refs_3_ = bf16[8,7168]{1,0:T(8,128)(2,1)S(1)} collective-permute-done((bf16[8,7168]{1,0:T(8,128)(2,1)S(1)}, bf16[8,7168]{1,0:T(8,128)(2,1)S(1)}, u32[]{:S(2)}, u32[]{:S(2)}) %collective-permute-start.21) | collective-permute-done | bytes 114720 | tf_op jit(solution)/shard_map/ppermute | solution.py:26
  46.5 1.6 %collective-permute-done.20.refs_2_ = bf16[8,7168]{1,0:T(8,128)(2,1)S(1)} collective-permute-done((bf16[8,7168]{1,0:T(8,128)(2,1)S(1)}, bf16[8,7168]{1,0:T(8,128)(2,1)S(1)}, u32[]{:S(2)}, u32[]{:S(2)}) %collective-permute-start.20) | collective-permute-done | bytes 114720 | tf_op jit(solution)/shard_map/ppermute | solution.py:26
  48.1 0.8 %collective-permute-done.19.refs_1_ = bf16[8,7168]{1,0:T(8,128)(2,1)S(1)} collective-permute-done((bf16[8,7168]{1,0:T(8,128)(2,1)S(1)}, bf16[8,7168]{1,0:T(8,128)(2,1)S(1)}, u32[]{:S(2)}, u32[]{:S(2)}) %collective-permute-start.19) | collective-permute-done | bytes 114720 | tf_op jit(solution)/shard_map/ppermute | solution.py:26
  48.9 0.5 collective-permute-done.24.refs_6_
  49.4 0.8 %collective-permute-done.23.refs_5_ = bf16[8,7168]{1,0:T(8,128)(2,1)S(1)} collective-permute-done((bf16[8,7168]{1,0:T(8,128)(2,1)S(1)}, bf16[8,7168]{1,0:T(8,128)(2,1)S(1)}, u32[]{:S(2)}, u32[]{:S(2)}) %collective-permute-start.23) | collective-permute-done | bytes 114720 | tf_op jit(solution)/shard_map/ppermute | solution.py:26
  50.2 2.1 %shard_map.83 = (bf16[8,7168]{1,0:T(8,128)(2,1)S(1)}, bf16[8,7168]{1,0:T(8,128)(2,1)S(1)}, bf16[8,7168]{1,0:T(8,128)(2,1)S(1)}, bf16[8,7168]{1,0:T(8,128)(2,1)S(...) custom-call(bf16[8,7168]{1,0:T(8,128)(2,1)S(1)} %get-tuple-element.5, ...), custom_call_target="tpu_custom_call" | custom-call | flops 704643072 | bytes 11010048 | tf_op jit(solution)/shard_map/pallas_call | solution.py:43
  52.4 0.2 collective-permute-start.27
  52.6 0.4 collective-permute-start.29
  52.9 0.1 collective-permute-start.31
  53.1 0.4 collective-permute-start.26
  53.5 0.3 collective-permute-done.27.refs_1_
  53.8 1.5 %collective-permute-start.28 = (bf16[8,7168]{1,0:T(8,128)(2,1)S(1)}, bf16[8,7168]{1,0:T(8,128)(2,1)S(1)}, u32[]{:S(2)}, u32[]{:S(2)}) collective-permute-start(bf16[8,7168]{1,0:T(8,128)(2,1)S(1)} %shard_map.84), channel_id=1, source_target_pairs={{0,6},{1,7},{2,4},{3,5},{4,2},{5,3},{6,0},{7,1},{8,14},{9,15},{10,... | collective-permute-start | bytes 344072 | tf_op jit(solution)/shard_map/ppermute | solution.py:26
  55.4 1.5 %collective-permute-start.30 = (bf16[8,7168]{1,0:T(8,128)(2,1)S(1)}, bf16[8,7168]{1,0:T(8,128)(2,1)S(1)}, u32[]{:S(2)}, u32[]{:S(2)}) collective-permute-start(bf16[8,7168]{1,0:T(8,128)(2,1)S(1)} %shard_map.85), channel_id=1, source_target_pairs={{0,2},{1,3},{2,0},{3,1},{4,6},{5,7},{6,4},{7,5},{8,10},{9,11},{10,... | collective-permute-start | bytes 344072 | tf_op jit(solution)/shard_map/ppermute | solution.py:26
  56.9 0.6 collective-permute-start.32
  57.5 1.1 %collective-permute-start.18 = (bf16[4,7168]{1,0:T(4,128)(2,1)S(1)}, bf16[4,7168]{1,0:T(4,128)(2,1)S(1)}, u32[]{:S(2)}, u32[]{:S(2)}) collective-permute-start(bf16[4,7168]{1,0:T(4,128)(2,1)S(1)} %get-tuple-element.56), channel_id=1, source_target_pairs={{0,16},{1,17},{2,18},{3,19},{4,20},{5,21},{6,22},{7,23},{8,24},{9,... | collective-permute-start | bytes 172040 | tf_op jit(solution)/shard_map/ppermute | solution.py:26
  58.6 2.1 %collective-permute-done.28.refs_2_ = bf16[8,7168]{1,0:T(8,128)(2,1)S(1)} collective-permute-done((bf16[8,7168]{1,0:T(8,128)(2,1)S(1)}, bf16[8,7168]{1,0:T(8,128)(2,1)S(1)}, u32[]{:S(2)}, u32[]{:S(2)}) %collective-permute-start.28) | collective-permute-done | bytes 114720 | tf_op jit(solution)/shard_map/ppermute | solution.py:26
  60.8 1.7 %collective-permute-done.30.refs_3_ = bf16[8,7168]{1,0:T(8,128)(2,1)S(1)} collective-permute-done((bf16[8,7168]{1,0:T(8,128)(2,1)S(1)}, bf16[8,7168]{1,0:T(8,128)(2,1)S(1)}, u32[]{:S(2)}, u32[]{:S(2)}) %collective-permute-start.30) | collective-permute-done | bytes 114720 | tf_op jit(solution)/shard_map/ppermute | solution.py:26
  62.4 0.1 shard_map.87
  62.5 2.0 %collective-permute-start.33 = (bf16[4,7168]{1,0:T(4,128)(2,1)S(1)}, bf16[4,7168]{1,0:T(4,128)(2,1)S(1)}, u32[]{:S(2)}, u32[]{:S(2)}) collective-permute-start(bf16[4,7168]{1,0:T(4,128)(2,1)S(1)} %get-tuple-element.67), channel_id=1, source_target_pairs={{0,24},{1,25},{2,26},{3,27},{4,28},{5,29},{6,30},{7,31},{8,16},{9,... | collective-permute-start | bytes 172040 | tf_op jit(solution)/shard_map/ppermute | solution.py:26
  64.5 1.2 %collective-permute-start.34 = (bf16[4,7168]{1,0:T(4,128)(2,1)S(1)}, bf16[4,7168]{1,0:T(4,128)(2,1)S(1)}, u32[]{:S(2)}, u32[]{:S(2)}) collective-permute-start(bf16[4,7168]{1,0:T(4,128)(2,1)S(1)} %get-tuple-element.68), channel_id=1, source_target_pairs={{0,16},{1,17},{2,18},{3,19},{4,20},{5,21},{6,22},{7,23},{8,24},{9,... | collective-permute-start | bytes 172040 | tf_op jit(solution)/shard_map/ppermute | solution.py:26
  65.7 4.0 %collective-permute-done.33.refs_1_ = bf16[4,7168]{1,0:T(4,128)(2,1)S(1)} collective-permute-done((bf16[4,7168]{1,0:T(4,128)(2,1)S(1)}, bf16[4,7168]{1,0:T(4,128)(2,1)S(1)}, u32[]{:S(2)}, u32[]{:S(2)}) %collective-permute-start.33) | collective-permute-done | bytes 57376 | tf_op jit(solution)/shard_map/ppermute | solution.py:26
  69.8 0.7 shard_map.88
  (24 shorter events, 0.2 us)
Async XLA Ops:
  1.0 7.3 %copy-start = (f32[1,7168]{1,0:T(1,128)S(1)}, f32[1,7168]{1,0:T(1,128)}, u32[]{:S(2)}) copy-start(f32[1,7168]{1,0:T(1,128)} %gain_ref.3) | copy-start | bytes 86020
  1.0 7.3 %collective-permute-start = (bf16[4,7296]{1,0:T(4,128)(2,1)S(1)}, bf16[4,7296]{1,0:T(4,128)(2,1)S(1)}, u32[]{:S(2)}, u32[]{:S(2)}) collective-permute-start(bf16[4,7296]{1,0:T(4,128)(2,1)S(1)} %shard_map.73.own_ref), channel_id=1, source_target_pairs={{0,8},{1,9},{2,10},{3,11},{4,12},{5,13},{6,14},{7,15},{8,0},{9,1},... | collective-permute-start | bytes 175112 | tf_op jit(solution)/shard_map/ppermute | solution.py:26
  8.5 6.1 %collective-permute-start.4 = (bf16[8,7296]{1,0:T(8,128)(2,1)S(1)}, bf16[8,7296]{1,0:T(8,128)(2,1)S(1)}, u32[]{:S(2)}, u32[]{:S(2)}) collective-permute-start(bf16[8,7296]{1,0:T(8,128)(2,1)S(1)} %get-tuple-element.44.refs_0_), channel_id=1, source_target_pairs={{0,6},{1,7},{2,4},{3,5},{4,2},{5,3},{6,0},{7,1},{8,14},{9,15},{10,... | collective-permute-start | bytes 350216 | tf_op jit(solution)/shard_map/ppermute | solution.py:26
  11.1 5.6 %collective-permute-start.3 = (bf16[8,7296]{1,0:T(8,128)(2,1)S(1)}, bf16[8,7296]{1,0:T(8,128)(2,1)S(1)}, u32[]{:S(2)}, u32[]{:S(2)}) collective-permute-start(bf16[8,7296]{1,0:T(8,128)(2,1)S(1)} %get-tuple-element.44.refs_0_), channel_id=1, source_target_pairs={{0,2},{1,3},{2,0},{3,1},{4,6},{5,7},{6,4},{7,5},{8,10},{9,11},{10,... | collective-permute-start | bytes 350216 | tf_op jit(solution)/shard_map/ppermute | solution.py:26
  11.6 5.3 %collective-permute-start.2 = (bf16[8,7296]{1,0:T(8,128)(2,1)S(1)}, bf16[8,7296]{1,0:T(8,128)(2,1)S(1)}, u32[]{:S(2)}, u32[]{:S(2)}) collective-permute-start(bf16[8,7296]{1,0:T(8,128)(2,1)S(1)} %get-tuple-element.44.refs_0_), channel_id=1, source_target_pairs={{0,4},{1,5},{2,6},{3,7},{4,0},{5,1},{6,2},{7,3},{8,12},{9,13},{10,... | collective-permute-start | bytes 350216 | tf_op jit(solution)/shard_map/ppermute | solution.py:26
  14.1 3.1 %collective-permute-start.5 = (bf16[8,7296]{1,0:T(8,128)(2,1)S(1)}, bf16[8,7296]{1,0:T(8,128)(2,1)S(1)}, u32[]{:S(2)}, u32[]{:S(2)}) collective-permute-start(bf16[8,7296]{1,0:T(8,128)(2,1)S(1)} %get-tuple-element.44.refs_0_), channel_id=1, source_target_pairs={{0,1},{1,0},{2,3},{3,2},{4,5},{5,4},{6,7},{7,6},{8,9},{9,8},{10,11... | collective-permute-start | bytes 350216 | tf_op jit(solution)/shard_map/ppermute | solution.py:26
  14.6 2.7 %collective-permute-start.8 = (bf16[8,7296]{1,0:T(8,128)(2,1)S(1)}, bf16[8,7296]{1,0:T(8,128)(2,1)S(1)}, u32[]{:S(2)}, u32[]{:S(2)}) collective-permute-start(bf16[8,7296]{1,0:T(8,128)(2,1)S(1)} %collective-permute-done.4.refs_3_), channel_id=1, source_target_pairs={{0,1},{1,0},{2,3},{3,2},{4,5},{5,4},{6,7},{7,6},{8,9},{9,8},{10,11... | collective-permute-start | bytes 350216 | tf_op jit(solution)/shard_map/ppermute | solution.py:26
  16.7 1.3 %collective-permute-start.7 = (bf16[8,7296]{1,0:T(8,128)(2,1)S(1)}, bf16[8,7296]{1,0:T(8,128)(2,1)S(1)}, u32[]{:S(2)}, u32[]{:S(2)}) collective-permute-start(bf16[8,7296]{1,0:T(8,128)(2,1)S(1)} %collective-permute-done.3.refs_2_), channel_id=1, source_target_pairs={{0,1},{1,0},{2,3},{3,2},{4,5},{5,4},{6,7},{7,6},{8,9},{9,8},{10,11... | collective-permute-start | bytes 350216 | tf_op jit(solution)/shard_map/ppermute | solution.py:26
  16.9 1.3 %collective-permute-start.6 = (bf16[8,7296]{1,0:T(8,128)(2,1)S(1)}, bf16[8,7296]{1,0:T(8,128)(2,1)S(1)}, u32[]{:S(2)}, u32[]{:S(2)}) collective-permute-start(bf16[8,7296]{1,0:T(8,128)(2,1)S(1)} %collective-permute-done.2.refs_1_), channel_id=1, source_target_pairs={{0,1},{1,0},{2,3},{3,2},{4,5},{5,4},{6,7},{7,6},{8,9},{9,8},{10,11... | collective-permute-start | bytes 350216 | tf_op jit(solution)/shard_map/ppermute | solution.py:26
  20.4 1.4 %collective-permute-start.10 = (bf16[8,7168]{1,0:T(8,128)(2,1)S(1)}, bf16[8,7168]{1,0:T(8,128)(2,1)S(1)}, u32[]{:S(2)}, u32[]{:S(2)}) collective-permute-start(bf16[8,7168]{1,0:T(8,128)(2,1)S(1)} %get-tuple-element.51), channel_id=1, source_target_pairs={{0,1},{1,0},{2,3},{3,2},{4,5},{5,4},{6,7},{7,6},{8,9},{9,8},{10,11... | collective-permute-start | bytes 344072 | tf_op jit(solution)/shard_map/ppermute | solution.py:26
  20.7 2.7 %collective-permute-start.12 = (bf16[8,7168]{1,0:T(8,128)(2,1)S(1)}, bf16[8,7168]{1,0:T(8,128)(2,1)S(1)}, u32[]{:S(2)}, u32[]{:S(2)}) collective-permute-start(bf16[8,7168]{1,0:T(8,128)(2,1)S(1)} %get-tuple-element.53), channel_id=1, source_target_pairs={{0,1},{1,0},{2,3},{3,2},{4,5},{5,4},{6,7},{7,6},{8,9},{9,8},{10,11... | collective-permute-start | bytes 344072 | tf_op jit(solution)/shard_map/ppermute | solution.py:26
  21.0 3.9 %collective-permute-start.14 = (bf16[8,7168]{1,0:T(8,128)(2,1)S(1)}, bf16[8,7168]{1,0:T(8,128)(2,1)S(1)}, u32[]{:S(2)}, u32[]{:S(2)}) collective-permute-start(bf16[8,7168]{1,0:T(8,128)(2,1)S(1)} %get-tuple-element.55), channel_id=1, source_target_pairs={{0,1},{1,0},{2,3},{3,2},{4,5},{5,4},{6,7},{7,6},{8,9},{9,8},{10,11... | collective-permute-start | bytes 344072 | tf_op jit(solution)/shard_map/ppermute | solution.py:26
  21.3 5.8 %collective-permute-start.9 = (bf16[8,7168]{1,0:T(8,128)(2,1)S(1)}, bf16[8,7168]{1,0:T(8,128)(2,1)S(1)}, u32[]{:S(2)}, u32[]{:S(2)}) collective-permute-start(bf16[8,7168]{1,0:T(8,128)(2,1)S(1)} %get-tuple-element.49), channel_id=1, source_target_pairs={{0,1},{1,0},{2,3},{3,2},{4,5},{5,4},{6,7},{7,6},{8,9},{9,8},{10,11... | collective-permute-start | bytes 344072 | tf_op jit(solution)/shard_map/ppermute | solution.py:26
  21.8 6.9 %collective-permute-start.11 = (bf16[8,7168]{1,0:T(8,128)(2,1)S(1)}, bf16[8,7168]{1,0:T(8,128)(2,1)S(1)}, u32[]{:S(2)}, u32[]{:S(2)}) collective-permute-start(bf16[8,7168]{1,0:T(8,128)(2,1)S(1)} %shard_map.78), channel_id=1, source_target_pairs={{0,6},{1,7},{2,4},{3,5},{4,2},{5,3},{6,0},{7,1},{8,14},{9,15},{10,... | collective-permute-start | bytes 344072 | tf_op jit(solution)/shard_map/ppermute | solution.py:26
  23.5 7.1 %collective-permute-start.13 = (bf16[8,7168]{1,0:T(8,128)(2,1)S(1)}, bf16[8,7168]{1,0:T(8,128)(2,1)S(1)}, u32[]{:S(2)}, u32[]{:S(2)}) collective-permute-start(bf16[8,7168]{1,0:T(8,128)(2,1)S(1)} %shard_map.79), channel_id=1, source_target_pairs={{0,2},{1,3},{2,0},{3,1},{4,6},{5,7},{6,4},{7,5},{8,10},{9,11},{10,... | collective-permute-start | bytes 344072 | tf_op jit(solution)/shard_map/ppermute | solution.py:26
  24.9 5.7 %collective-permute-start.15 = (bf16[8,7168]{1,0:T(8,128)(2,1)S(1)}, bf16[8,7168]{1,0:T(8,128)(2,1)S(1)}, u32[]{:S(2)}, u32[]{:S(2)}) collective-permute-start(bf16[8,7168]{1,0:T(8,128)(2,1)S(1)} %shard_map.80), channel_id=1, source_target_pairs={{0,4},{1,5},{2,6},{3,7},{4,0},{5,1},{6,2},{7,3},{8,12},{9,13},{10,... | collective-permute-start | bytes 344072 | tf_op jit(solution)/shard_map/ppermute | solution.py:26
  25.6 8.8 %collective-permute-start.1 = (bf16[8,7168]{1,0:T(8,128)(2,1)S(1)}, bf16[8,7168]{1,0:T(8,128)(2,1)S(1)}, u32[]{:S(2)}, u32[]{:S(2)}) collective-permute-start(bf16[8,7168]{1,0:T(8,128)(2,1)S(1)} %get-tuple-element.40), channel_id=1, source_target_pairs={{0,16},{1,17},{2,18},{3,19},{4,20},{5,21},{6,22},{7,23},{8,24},{9,... | collective-permute-start | bytes 344072 | tf_op jit(solution)/shard_map/ppermute | solution.py:26
  30.7 9.4 %collective-permute-start.17 = (bf16[8,7168]{1,0:T(8,128)(2,1)S(1)}, bf16[8,7168]{1,0:T(8,128)(2,1)S(1)}, u32[]{:S(2)}, u32[]{:S(2)}) collective-permute-start(bf16[8,7168]{1,0:T(8,128)(2,1)S(1)} %shard_map.81), channel_id=1, source_target_pairs={{0,24},{1,25},{2,26},{3,27},{4,28},{5,29},{6,30},{7,31},{8,16},{9,... | collective-permute-start | bytes 344072 | tf_op jit(solution)/shard_map/ppermute | solution.py:26
  33.8 6.3 %collective-permute-start.16 = (bf16[8,7168]{1,0:T(8,128)(2,1)S(1)}, bf16[8,7168]{1,0:T(8,128)(2,1)S(1)}, u32[]{:S(2)}, u32[]{:S(2)}) collective-permute-start(bf16[8,7168]{1,0:T(8,128)(2,1)S(1)} %shard_map.81), channel_id=1, source_target_pairs={{0,16},{1,17},{2,18},{3,19},{4,20},{5,21},{6,22},{7,23},{8,24},{9,... | collective-permute-start | bytes 344072 | tf_op jit(solution)/shard_map/ppermute | solution.py:26
  40.3 6.2 %collective-permute-start.21 = (bf16[8,7168]{1,0:T(8,128)(2,1)S(1)}, bf16[8,7168]{1,0:T(8,128)(2,1)S(1)}, u32[]{:S(2)}, u32[]{:S(2)}) collective-permute-start(bf16[8,7168]{1,0:T(8,128)(2,1)S(1)} %get-tuple-element.57.refs_0_), channel_id=1, source_target_pairs={{0,6},{1,7},{2,4},{3,5},{4,2},{5,3},{6,0},{7,1},{8,14},{9,15},{10,... | collective-permute-start | bytes 344072 | tf_op jit(solution)/shard_map/ppermute | solution.py:26
  42.1 6.0 %collective-permute-start.20 = (bf16[8,7168]{1,0:T(8,128)(2,1)S(1)}, bf16[8,7168]{1,0:T(8,128)(2,1)S(1)}, u32[]{:S(2)}, u32[]{:S(2)}) collective-permute-start(bf16[8,7168]{1,0:T(8,128)(2,1)S(1)} %get-tuple-element.57.refs_0_), channel_id=1, source_target_pairs={{0,2},{1,3},{2,0},{3,1},{4,6},{5,7},{6,4},{7,5},{8,10},{9,11},{10,... | collective-permute-start | bytes 344072 | tf_op jit(solution)/shard_map/ppermute | solution.py:26
  43.4 5.5 %collective-permute-start.19 = (bf16[8,7168]{1,0:T(8,128)(2,1)S(1)}, bf16[8,7168]{1,0:T(8,128)(2,1)S(1)}, u32[]{:S(2)}, u32[]{:S(2)}) collective-permute-start(bf16[8,7168]{1,0:T(8,128)(2,1)S(1)} %get-tuple-element.57.refs_0_), channel_id=1, source_target_pairs={{0,4},{1,5},{2,6},{3,7},{4,0},{5,1},{6,2},{7,3},{8,12},{9,13},{10,... | collective-permute-start | bytes 344072 | tf_op jit(solution)/shard_map/ppermute | solution.py:26
  43.8 5.1 %collective-permute-start.22 = (bf16[8,7168]{1,0:T(8,128)(2,1)S(1)}, bf16[8,7168]{1,0:T(8,128)(2,1)S(1)}, u32[]{:S(2)}, u32[]{:S(2)}) collective-permute-start(bf16[8,7168]{1,0:T(8,128)(2,1)S(1)} %get-tuple-element.57.refs_0_), channel_id=1, source_target_pairs={{0,1},{1,0},{2,3},{3,2},{4,5},{5,4},{6,7},{7,6},{8,9},{9,8},{10,11... | collective-permute-start | bytes 344072 | tf_op jit(solution)/shard_map/ppermute | solution.py:26
  46.5 2.4 %collective-permute-start.25 = (bf16[8,7168]{1,0:T(8,128)(2,1)S(1)}, bf16[8,7168]{1,0:T(8,128)(2,1)S(1)}, u32[]{:S(2)}, u32[]{:S(2)}) collective-permute-start(bf16[8,7168]{1,0:T(8,128)(2,1)S(1)} %collective-permute-done.21.refs_3_), channel_id=1, source_target_pairs={{0,1},{1,0},{2,3},{3,2},{4,5},{5,4},{6,7},{7,6},{8,9},{9,8},{10,11... | collective-permute-start | bytes 344072 | tf_op jit(solution)/shard_map/ppermute | solution.py:26
  48.1 1.3 %collective-permute-start.24 = (bf16[8,7168]{1,0:T(8,128)(2,1)S(1)}, bf16[8,7168]{1,0:T(8,128)(2,1)S(1)}, u32[]{:S(2)}, u32[]{:S(2)}) collective-permute-start(bf16[8,7168]{1,0:T(8,128)(2,1)S(1)} %collective-permute-done.20.refs_2_), channel_id=1, source_target_pairs={{0,1},{1,0},{2,3},{3,2},{4,5},{5,4},{6,7},{7,6},{8,9},{9,8},{10,11... | collective-permute-start | bytes 344072 | tf_op jit(solution)/shard_map/ppermute | solution.py:26
  48.9 1.3 %collective-permute-start.23 = (bf16[8,7168]{1,0:T(8,128)(2,1)S(1)}, bf16[8,7168]{1,0:T(8,128)(2,1)S(1)}, u32[]{:S(2)}, u32[]{:S(2)}) collective-permute-start(bf16[8,7168]{1,0:T(8,128)(2,1)S(1)} %collective-permute-done.19.refs_1_), channel_id=1, source_target_pairs={{0,1},{1,0},{2,3},{3,2},{4,5},{5,4},{6,7},{7,6},{8,9},{9,8},{10,11... | collective-permute-start | bytes 344072 | tf_op jit(solution)/shard_map/ppermute | solution.py:26
  52.4 1.4 %collective-permute-start.27 = (bf16[8,7168]{1,0:T(8,128)(2,1)S(1)}, bf16[8,7168]{1,0:T(8,128)(2,1)S(1)}, u32[]{:S(2)}, u32[]{:S(2)}) collective-permute-start(bf16[8,7168]{1,0:T(8,128)(2,1)S(1)} %get-tuple-element.62), channel_id=1, source_target_pairs={{0,1},{1,0},{2,3},{3,2},{4,5},{5,4},{6,7},{7,6},{8,9},{9,8},{10,11... | collective-permute-start | bytes 344072 | tf_op jit(solution)/shard_map/ppermute | solution.py:26
  52.6 2.7 %collective-permute-start.29 = (bf16[8,7168]{1,0:T(8,128)(2,1)S(1)}, bf16[8,7168]{1,0:T(8,128)(2,1)S(1)}, u32[]{:S(2)}, u32[]{:S(2)}) collective-permute-start(bf16[8,7168]{1,0:T(8,128)(2,1)S(1)} %get-tuple-element.64), channel_id=1, source_target_pairs={{0,1},{1,0},{2,3},{3,2},{4,5},{5,4},{6,7},{7,6},{8,9},{9,8},{10,11... | collective-permute-start | bytes 344072 | tf_op jit(solution)/shard_map/ppermute | solution.py:26
  52.9 4.0 %collective-permute-start.31 = (bf16[8,7168]{1,0:T(8,128)(2,1)S(1)}, bf16[8,7168]{1,0:T(8,128)(2,1)S(1)}, u32[]{:S(2)}, u32[]{:S(2)}) collective-permute-start(bf16[8,7168]{1,0:T(8,128)(2,1)S(1)} %get-tuple-element.66), channel_id=1, source_target_pairs={{0,1},{1,0},{2,3},{3,2},{4,5},{5,4},{6,7},{7,6},{8,9},{9,8},{10,11... | collective-permute-start | bytes 344072 | tf_op jit(solution)/shard_map/ppermute | solution.py:26
  53.1 5.5 %collective-permute-start.26 = (bf16[8,7168]{1,0:T(8,128)(2,1)S(1)}, bf16[8,7168]{1,0:T(8,128)(2,1)S(1)}, u32[]{:S(2)}, u32[]{:S(2)}) collective-permute-start(bf16[8,7168]{1,0:T(8,128)(2,1)S(1)} %get-tuple-element.60), channel_id=1, source_target_pairs={{0,1},{1,0},{2,3},{3,2},{4,5},{5,4},{6,7},{7,6},{8,9},{9,8},{10,11... | collective-permute-start | bytes 344072 | tf_op jit(solution)/shard_map/ppermute | solution.py:26
  53.8 7.0 %collective-permute-start.28 = (bf16[8,7168]{1,0:T(8,128)(2,1)S(1)}, bf16[8,7168]{1,0:T(8,128)(2,1)S(1)}, u32[]{:S(2)}, u32[]{:S(2)}) collective-permute-start(bf16[8,7168]{1,0:T(8,128)(2,1)S(1)} %shard_map.84), channel_id=1, source_target_pairs={{0,6},{1,7},{2,4},{3,5},{4,2},{5,3},{6,0},{7,1},{8,14},{9,15},{10,... | collective-permute-start | bytes 344072 | tf_op jit(solution)/shard_map/ppermute | solution.py:26
  55.4 7.0 %collective-permute-start.30 = (bf16[8,7168]{1,0:T(8,128)(2,1)S(1)}, bf16[8,7168]{1,0:T(8,128)(2,1)S(1)}, u32[]{:S(2)}, u32[]{:S(2)}) collective-permute-start(bf16[8,7168]{1,0:T(8,128)(2,1)S(1)} %shard_map.85), channel_id=1, source_target_pairs={{0,2},{1,3},{2,0},{3,1},{4,6},{5,7},{6,4},{7,5},{8,10},{9,11},{10,... | collective-permute-start | bytes 344072 | tf_op jit(solution)/shard_map/ppermute | solution.py:26
  56.9 5.5 %collective-permute-start.32 = (bf16[8,7168]{1,0:T(8,128)(2,1)S(1)}, bf16[8,7168]{1,0:T(8,128)(2,1)S(1)}, u32[]{:S(2)}, u32[]{:S(2)}) collective-permute-start(bf16[8,7168]{1,0:T(8,128)(2,1)S(1)} %shard_map.86), channel_id=1, source_target_pairs={{0,4},{1,5},{2,6},{3,7},{4,0},{5,1},{6,2},{7,3},{8,12},{9,13},{10,... | collective-permute-start | bytes 344072 | tf_op jit(solution)/shard_map/ppermute | solution.py:26
  57.5 8.2 %collective-permute-start.18 = (bf16[4,7168]{1,0:T(4,128)(2,1)S(1)}, bf16[4,7168]{1,0:T(4,128)(2,1)S(1)}, u32[]{:S(2)}, u32[]{:S(2)}) collective-permute-start(bf16[4,7168]{1,0:T(4,128)(2,1)S(1)} %get-tuple-element.56), channel_id=1, source_target_pairs={{0,16},{1,17},{2,18},{3,19},{4,20},{5,21},{6,22},{7,23},{8,24},{9,... | collective-permute-start | bytes 172040 | tf_op jit(solution)/shard_map/ppermute | solution.py:26
  62.5 7.3 %collective-permute-start.33 = (bf16[4,7168]{1,0:T(4,128)(2,1)S(1)}, bf16[4,7168]{1,0:T(4,128)(2,1)S(1)}, u32[]{:S(2)}, u32[]{:S(2)}) collective-permute-start(bf16[4,7168]{1,0:T(4,128)(2,1)S(1)} %get-tuple-element.67), channel_id=1, source_target_pairs={{0,24},{1,25},{2,26},{3,27},{4,28},{5,29},{6,30},{7,31},{8,16},{9,... | collective-permute-start | bytes 172040 | tf_op jit(solution)/shard_map/ppermute | solution.py:26
  64.5 5.2 %collective-permute-start.34 = (bf16[4,7168]{1,0:T(4,128)(2,1)S(1)}, bf16[4,7168]{1,0:T(4,128)(2,1)S(1)}, u32[]{:S(2)}, u32[]{:S(2)}) collective-permute-start(bf16[4,7168]{1,0:T(4,128)(2,1)S(1)} %get-tuple-element.68), channel_id=1, source_target_pairs={{0,16},{1,17},{2,18},{3,19},{4,20},{5,21},{6,22},{7,23},{8,24},{9,... | collective-permute-start | bytes 172040 | tf_op jit(solution)/shard_map/ppermute | solution.py:26

commit v18 on v17

--- a/solution.py
+++ b/solution.py
@@ -31,7 +31,7 @@
 
 
 CORE = (1, 1)
-SQUARE = ((4, 4), (2, 2), (6, 6))
+SQUARE = ((4, 4), (6, 6), (2, 2))
 STAY = (0, 0)
 
 
@@ -257,7 +257,7 @@
 
         kept, sent = outs[:4], [exchange(rows, CORE, 0) for rows in outs[4:]]
         parts = [kept[0], sent[0]]
-        for place in (3, 2, 1):
+        for place in (1, 2, 3):
             parts.append(exchange(add(kept[place], sent[place]), SQUARE[place - 1], 0))
         for flips in middle[::-1]:
             low, high = split(*parts)

time: 70.6 us -> 72.3 us (1.024)
  waiting for transfers between devices: 27.7 us -> 29.1 us
    ppermute x35, waiting for transfers between devices: 27.7 us -> 29.1 us  [exchange(): return lax.ppermute(value, ('segment', 'expert'), pairs)]
  transfers between devices with their start and end apart: 35 -> 35, of which waited for: 18 -> 22; matrix products, arithmetic and copies ran while one was open for 0% -> 0% of each run, Pallas kernels for 8% -> 8%
where the time goes in v18:
time: 72.3 us; the launch traced here: 72.1 us
  starting transfers between devices  31 us (43%)
  waiting for transfers between devices  29.1 us (40%)
  Pallas kernels  11.8 us (16%)
    ppermute x35, starting transfers between devices, exchange(): return lax.ppermute(value, ('segment', 'expert'), pairs)  31 us
    ppermute x35, waiting for transfers between devices, exchange(): return lax.ppermute(value, ('segment', 'expert'), pairs)  29.1 us
    pallas_call x14, Pallas kernels, call(): pl.pallas_call(kernel, out_shape=[jax.ShapeDtypeStruct(shape, jnp.bfloat1...  6.6 us
    pallas_call x2, Pallas kernels, load(): pl.pallas_call(functools.partial(load_kernel, count), out_shape=[pltpu.VM...  5.22 us
  transfers between devices with their start and end apart: 35, of which 22 were waited for; matrix products, arithmetic and copies ran while one was open for 0% of the time, Pallas kernels for 8%

profile of v18, /device:TPU:0, one launch (start us, length us, event | category | flops | bytes accessed | tf_op | source)
XLA Modules:
  0.0 72.1 jit_solution(4001799112675563996)
XLA Ops:
  0.0 1.0 %shard_map.73.own_ref = bf16[4,7296]{1,0:T(4,128)(2,1)S(1)} custom-call(bf16[1,4,7168]{2,1,0:T(4,128)(2,1)} %states_hbm.1, s32[1,2,2,4]{3,2,1,0:T(2,128)} %bitcast.3, bf16[1,2,2,4]{3,2,1,0:T(2,128)(2,1)} %bitcast.4), custom_call_target="tpu_custom_call" | custom-call | tf_op jit(solution)/shard_map/pallas_call | solution.py:43
  1.0 0.0 copy-start
  1.0 4.1 %collective-permute-start = (bf16[4,7296]{1,0:T(4,128)(2,1)S(1)}, bf16[4,7296]{1,0:T(4,128)(2,1)S(1)}, u32[]{:S(2)}, u32[]{:S(2)}) collective-permute-start(bf16[4,7296]{1,0:T(4,128)(2,1)S(1)} %shard_map.73.own_ref), channel_id=1, source_target_pairs={{0,8},{1,9},{2,10},{3,11},{4,12},{5,13},{6,14},{7,15},{8,0},{9,1},... | collective-permute-start | bytes 175112 | tf_op jit(solution)/shard_map/ppermute | solution.py:26
  5.1 3.2 %shard_map.74 = (bf16[1,7168,256]{2,1,0:T(8,128)(2,1)S(1)}, bf16[1,7168,256]{2,1,0:T(8,128)(2,1)S(1)}) custom-call(bf16[1,7168,256]{2,1,0:T(8,128)(2,1)} %refs_0_.1, bf16[1,7168,256]{2,1,0:T(8,128)(2,1)} %refs_1_.1), custom_call_target="tpu_custom_call" | custom-call | bytes 7340032 | tf_op jit(solution)/shard_map/pallas_call | solution.py:64
  8.3 0.2 shard_map.75
  8.5 2.0 %collective-permute-start.4 = (bf16[8,7296]{1,0:T(8,128)(2,1)S(1)}, bf16[8,7296]{1,0:T(8,128)(2,1)S(1)}, u32[]{:S(2)}, u32[]{:S(2)}) collective-permute-start(bf16[8,7296]{1,0:T(8,128)(2,1)S(1)} %get-tuple-element.44.refs_0_), channel_id=1, source_target_pairs={{0,2},{1,3},{2,0},{3,1},{4,6},{5,7},{6,4},{7,5},{8,10},{9,11},{10,... | collective-permute-start | bytes 350216 | tf_op jit(solution)/shard_map/ppermute | solution.py:26
  10.5 1.1 %collective-permute-start.3 = (bf16[8,7296]{1,0:T(8,128)(2,1)S(1)}, bf16[8,7296]{1,0:T(8,128)(2,1)S(1)}, u32[]{:S(2)}, u32[]{:S(2)}) collective-permute-start(bf16[8,7296]{1,0:T(8,128)(2,1)S(1)} %get-tuple-element.44.refs_0_), channel_id=1, source_target_pairs={{0,6},{1,7},{2,4},{3,5},{4,2},{5,3},{6,0},{7,1},{8,14},{9,15},{10,... | collective-permute-start | bytes 350216 | tf_op jit(solution)/shard_map/ppermute | solution.py:26
  11.6 0.4 collective-permute-start.2
  12.0 2.0 %shard_map.76.refs_10_.refs_11_ = bf16[1,256,7168]{2,1,0:T(8,128)(2,1)S(1)} custom-call(bf16[1,256,7168]{2,1,0:T(8,128)(2,1)} %refs_0_.2), custom_call_target="tpu_custom_call" | custom-call | bytes 3670016 | tf_op jit(solution)/shard_map/pallas_call | solution.py:64
  14.1 0.1 collective-permute-start.5
  14.2 0.4 collective-permute-done.4.refs_3_
  14.6 0.1 collective-permute-start.8
  14.7 2.0 %collective-permute-done.3.refs_2_ = bf16[8,7296]{1,0:T(8,128)(2,1)S(1)} collective-permute-done((bf16[8,7296]{1,0:T(8,128)(2,1)S(1)}, bf16[8,7296]{1,0:T(8,128)(2,1)S(1)}, u32[]{:S(2)}, u32[]{:S(2)}) %collective-permute-start.3) | collective-permute-done | bytes 116768 | tf_op jit(solution)/shard_map/ppermute | solution.py:26
  16.6 0.0 collective-permute-start.7
  16.6 0.3 collective-permute-done.2.refs_1_
  16.9 0.2 collective-permute-start.6
  17.2 0.8 %collective-permute-done.7.refs_6_ = bf16[8,7296]{1,0:T(8,128)(2,1)S(1)} collective-permute-done((bf16[8,7296]{1,0:T(8,128)(2,1)S(1)}, bf16[8,7296]{1,0:T(8,128)(2,1)S(1)}, u32[]{:S(2)}, u32[]{:S(2)}) %collective-permute-start.7) | collective-permute-done | bytes 116768 | tf_op jit(solution)/shard_map/ppermute | solution.py:26
  18.0 0.3 collective-permute-done.6.refs_5_
  18.3 2.1 %shard_map.77 = (bf16[8,7168]{1,0:T(8,128)(2,1)S(1)}, bf16[8,7168]{1,0:T(8,128)(2,1)S(1)}, bf16[8,7168]{1,0:T(8,128)(2,1)S(1)}, bf16[8,7168]{1,0:T(8,128)(2,1)S(...) custom-call(bf16[8,7296]{1,0:T(8,128)(2,1)S(1)} %get-tuple-element.4, ...), custom_call_target="tpu_custom_call" | custom-call | flops 704643072 | bytes 11010048 | tf_op jit(solution)/shard_map/pallas_call | solution.py:43
  20.4 0.3 collective-permute-start.10
  20.7 0.3 collective-permute-start.12
  21.0 0.2 collective-permute-start.14
  21.2 0.3 collective-permute-start.9
  21.5 0.3 collective-permute-done.10.refs_1_
  21.8 1.6 %collective-permute-start.11 = (bf16[8,7168]{1,0:T(8,128)(2,1)S(1)}, bf16[8,7168]{1,0:T(8,128)(2,1)S(1)}, u32[]{:S(2)}, u32[]{:S(2)}) collective-permute-start(bf16[8,7168]{1,0:T(8,128)(2,1)S(1)} %shard_map.78), channel_id=1, source_target_pairs={{0,4},{1,5},{2,6},{3,7},{4,0},{5,1},{6,2},{7,3},{8,12},{9,13},{10,... | collective-permute-start | bytes 344072 | tf_op jit(solution)/shard_map/ppermute | solution.py:26
  23.5 1.5 %collective-permute-start.13 = (bf16[8,7168]{1,0:T(8,128)(2,1)S(1)}, bf16[8,7168]{1,0:T(8,128)(2,1)S(1)}, u32[]{:S(2)}, u32[]{:S(2)}) collective-permute-start(bf16[8,7168]{1,0:T(8,128)(2,1)S(1)} %shard_map.79), channel_id=1, source_target_pairs={{0,6},{1,7},{2,4},{3,5},{4,2},{5,3},{6,0},{7,1},{8,14},{9,15},{10,... | collective-permute-start | bytes 344072 | tf_op jit(solution)/shard_map/ppermute | solution.py:26
  25.0 0.6 collective-permute-start.15
  25.6 1.5 %collective-permute-start.1 = (bf16[8,7168]{1,0:T(8,128)(2,1)S(1)}, bf16[8,7168]{1,0:T(8,128)(2,1)S(1)}, u32[]{:S(2)}, u32[]{:S(2)}) collective-permute-start(bf16[8,7168]{1,0:T(8,128)(2,1)S(1)} %get-tuple-element.40), channel_id=1, source_target_pairs={{0,16},{1,17},{2,18},{3,19},{4,20},{5,21},{6,22},{7,23},{8,24},{9,... | collective-permute-start | bytes 344072 | tf_op jit(solution)/shard_map/ppermute | solution.py:26
  27.1 0.2 collective-permute-done.11.refs_2_
  27.2 3.4 %collective-permute-done.13.refs_3_ = bf16[8,7168]{1,0:T(8,128)(2,1)S(1)} collective-permute-done((bf16[8,7168]{1,0:T(8,128)(2,1)S(1)}, bf16[8,7168]{1,0:T(8,128)(2,1)S(1)}, u32[]{:S(2)}, u32[]{:S(2)}) %collective-permute-start.13) | collective-permute-done | bytes 114720 | tf_op jit(solution)/shard_map/ppermute | solution.py:26
  30.6 1.6 %collective-permute-done.15.refs_4_ = bf16[8,7168]{1,0:T(8,128)(2,1)S(1)} collective-permute-done((bf16[8,7168]{1,0:T(8,128)(2,1)S(1)}, bf16[8,7168]{1,0:T(8,128)(2,1)S(1)}, u32[]{:S(2)}, u32[]{:S(2)}) %collective-permute-start.15) | collective-permute-done | bytes 114720 | tf_op jit(solution)/shard_map/ppermute | solution.py:26
  32.2 0.1 shard_map.81
  32.3 3.1 %collective-permute-start.17 = (bf16[8,7168]{1,0:T(8,128)(2,1)S(1)}, bf16[8,7168]{1,0:T(8,128)(2,1)S(1)}, u32[]{:S(2)}, u32[]{:S(2)}) collective-permute-start(bf16[8,7168]{1,0:T(8,128)(2,1)S(1)} %shard_map.81), channel_id=1, source_target_pairs={{0,24},{1,25},{2,26},{3,27},{4,28},{5,29},{6,30},{7,31},{8,16},{9,... | collective-permute-start | bytes 344072 | tf_op jit(solution)/shard_map/ppermute | solution.py:26
  35.4 0.5 collective-permute-start.16
  36.0 5.2 %collective-permute-done.17.far_ref = bf16[8,7168]{1,0:T(8,128)(2,1)S(1)} collective-permute-done((bf16[8,7168]{1,0:T(8,128)(2,1)S(1)}, bf16[8,7168]{1,0:T(8,128)(2,1)S(1)}, u32[]{:S(2)}, u32[]{:S(2)}) %collective-permute-start.17) | collective-permute-done | bytes 114720 | tf_op jit(solution)/shard_map/ppermute | solution.py:26
  41.2 0.2 collective-permute-done.16.near_ref
  41.4 0.2 shard_map.82
  41.6 0.4 collective-permute-start.21
  42.0 2.4 %collective-permute-start.20 = (bf16[8,7168]{1,0:T(8,128)(2,1)S(1)}, bf16[8,7168]{1,0:T(8,128)(2,1)S(1)}, u32[]{:S(2)}, u32[]{:S(2)}) collective-permute-start(bf16[8,7168]{1,0:T(8,128)(2,1)S(1)} %get-tuple-element.57.refs_0_), channel_id=1, source_target_pairs={{0,6},{1,7},{2,4},{3,5},{4,2},{5,3},{6,0},{7,1},{8,14},{9,15},{10,... | collective-permute-start | bytes 344072 | tf_op jit(solution)/shard_map/ppermute | solution.py:26
  44.4 0.8 %collective-permute-start.19 = (bf16[8,7168]{1,0:T(8,128)(2,1)S(1)}, bf16[8,7168]{1,0:T(8,128)(2,1)S(1)}, u32[]{:S(2)}, u32[]{:S(2)}) collective-permute-start(bf16[8,7168]{1,0:T(8,128)(2,1)S(1)} %get-tuple-element.57.refs_0_), channel_id=1, source_target_pairs={{0,4},{1,5},{2,6},{3,7},{4,0},{5,1},{6,2},{7,3},{8,12},{9,13},{10,... | collective-permute-start | bytes 344072 | tf_op jit(solution)/shard_map/ppermute | solution.py:26
  45.2 2.8 %collective-permute-done.21.refs_3_ = bf16[8,7168]{1,0:T(8,128)(2,1)S(1)} collective-permute-done((bf16[8,7168]{1,0:T(8,128)(2,1)S(1)}, bf16[8,7168]{1,0:T(8,128)(2,1)S(1)}, u32[]{:S(2)}, u32[]{:S(2)}) %collective-permute-start.21) | collective-permute-done | bytes 114720 | tf_op jit(solution)/shard_map/ppermute | solution.py:26
  48.0 0.7 collective-permute-done.20.refs_2_
  48.7 1.2 %collective-permute-done.19.refs_1_ = bf16[8,7168]{1,0:T(8,128)(2,1)S(1)} collective-permute-done((bf16[8,7168]{1,0:T(8,128)(2,1)S(1)}, bf16[8,7168]{1,0:T(8,128)(2,1)S(1)}, u32[]{:S(2)}, u32[]{:S(2)}) %collective-permute-start.19) | collective-permute-done | bytes 114720 | tf_op jit(solution)/shard_map/ppermute | solution.py:26
  49.9 0.1 collective-permute-done.24.refs_6_
  50.0 1.2 %collective-permute-done.23.refs_5_ = bf16[8,7168]{1,0:T(8,128)(2,1)S(1)} collective-permute-done((bf16[8,7168]{1,0:T(8,128)(2,1)S(1)}, bf16[8,7168]{1,0:T(8,128)(2,1)S(1)}, u32[]{:S(2)}, u32[]{:S(2)}) %collective-permute-start.23) | collective-permute-done | bytes 114720 | tf_op jit(solution)/shard_map/ppermute | solution.py:26
  51.3 2.1 %shard_map.83 = (bf16[8,7168]{1,0:T(8,128)(2,1)S(1)}, bf16[8,7168]{1,0:T(8,128)(2,1)S(1)}, bf16[8,7168]{1,0:T(8,128)(2,1)S(1)}, bf16[8,7168]{1,0:T(8,128)(2,1)S(...) custom-call(bf16[8,7168]{1,0:T(8,128)(2,1)S(1)} %get-tuple-element.5, ...), custom_call_target="tpu_custom_call" | custom-call | flops 704643072 | bytes 11010048 | tf_op jit(solution)/shard_map/pallas_call | solution.py:43
  53.4 0.2 collective-permute-start.27
  53.6 0.4 collective-permute-start.29
  54.0 0.1 collective-permute-start.31
  54.1 0.4 collective-permute-start.26
  54.5 0.3 collective-permute-done.27.refs_1_
  54.8 1.6 %collective-permute-start.28 = (bf16[8,7168]{1,0:T(8,128)(2,1)S(1)}, bf16[8,7168]{1,0:T(8,128)(2,1)S(1)}, u32[]{:S(2)}, u32[]{:S(2)}) collective-permute-start(bf16[8,7168]{1,0:T(8,128)(2,1)S(1)} %shard_map.84), channel_id=1, source_target_pairs={{0,4},{1,5},{2,6},{3,7},{4,0},{5,1},{6,2},{7,3},{8,12},{9,13},{10,... | collective-permute-start | bytes 344072 | tf_op jit(solution)/shard_map/ppermute | solution.py:26
  56.5 0.5 collective-permute-start.30
  57.0 1.5 %collective-permute-start.32 = (bf16[8,7168]{1,0:T(8,128)(2,1)S(1)}, bf16[8,7168]{1,0:T(8,128)(2,1)S(1)}, u32[]{:S(2)}, u32[]{:S(2)}) collective-permute-start(bf16[8,7168]{1,0:T(8,128)(2,1)S(1)} %shard_map.86), channel_id=1, source_target_pairs={{0,2},{1,3},{2,0},{3,1},{4,6},{5,7},{6,4},{7,5},{8,10},{9,11},{10,... | collective-permute-start | bytes 344072 | tf_op jit(solution)/shard_map/ppermute | solution.py:26
  58.6 1.3 %collective-permute-start.18 = (bf16[4,7168]{1,0:T(4,128)(2,1)S(1)}, bf16[4,7168]{1,0:T(4,128)(2,1)S(1)}, u32[]{:S(2)}, u32[]{:S(2)}) collective-permute-start(bf16[4,7168]{1,0:T(4,128)(2,1)S(1)} %get-tuple-element.56), channel_id=1, source_target_pairs={{0,16},{1,17},{2,18},{3,19},{4,20},{5,21},{6,22},{7,23},{8,24},{9,... | collective-permute-start | bytes 172040 | tf_op jit(solution)/shard_map/ppermute | solution.py:26
  59.9 1.0 %collective-permute-done.28.refs_2_ = bf16[8,7168]{1,0:T(8,128)(2,1)S(1)} collective-permute-done((bf16[8,7168]{1,0:T(8,128)(2,1)S(1)}, bf16[8,7168]{1,0:T(8,128)(2,1)S(1)}, u32[]{:S(2)}, u32[]{:S(2)}) %collective-permute-start.28) | collective-permute-done | bytes 114720 | tf_op jit(solution)/shard_map/ppermute | solution.py:26
  60.9 1.8 %collective-permute-done.30.refs_3_ = bf16[8,7168]{1,0:T(8,128)(2,1)S(1)} collective-permute-done((bf16[8,7168]{1,0:T(8,128)(2,1)S(1)}, bf16[8,7168]{1,0:T(8,128)(2,1)S(1)}, u32[]{:S(2)}, u32[]{:S(2)}) %collective-permute-start.30) | collective-permute-done | bytes 114720 | tf_op jit(solution)/shard_map/ppermute | solution.py:26
  62.7 1.6 %collective-permute-done.32.refs_4_ = bf16[8,7168]{1,0:T(8,128)(2,1)S(1)} collective-permute-done((bf16[8,7168]{1,0:T(8,128)(2,1)S(1)}, bf16[8,7168]{1,0:T(8,128)(2,1)S(1)}, u32[]{:S(2)}, u32[]{:S(2)}) %collective-permute-start.32) | collective-permute-done | bytes 114720 | tf_op jit(solution)/shard_map/ppermute | solution.py:26
  64.3 0.1 shard_map.87
  64.4 2.9 %collective-permute-start.33 = (bf16[4,7168]{1,0:T(4,128)(2,1)S(1)}, bf16[4,7168]{1,0:T(4,128)(2,1)S(1)}, u32[]{:S(2)}, u32[]{:S(2)}) collective-permute-start(bf16[4,7168]{1,0:T(4,128)(2,1)S(1)} %get-tuple-element.67), channel_id=1, source_target_pairs={{0,24},{1,25},{2,26},{3,27},{4,28},{5,29},{6,30},{7,31},{8,16},{9,... | collective-permute-start | bytes 172040 | tf_op jit(solution)/shard_map/ppermute | solution.py:26
  67.2 0.5 collective-permute-start.34
  67.8 2.6 %collective-permute-done.33.refs_1_ = bf16[4,7168]{1,0:T(4,128)(2,1)S(1)} collective-permute-done((bf16[4,7168]{1,0:T(4,128)(2,1)S(1)}, bf16[4,7168]{1,0:T(4,128)(2,1)S(1)}, u32[]{:S(2)}, u32[]{:S(2)}) %collective-permute-start.33) | collective-permute-done | bytes 57376 | tf_op jit(solution)/shard_map/ppermute | solution.py:26
  70.4 1.0 %collective-permute-done.34.refs_2_ = bf16[4,7168]{1,0:T(4,128)(2,1)S(1)} collective-permute-done((bf16[4,7168]{1,0:T(4,128)(2,1)S(1)}, bf16[4,7168]{1,0:T(4,128)(2,1)S(1)}, u32[]{:S(2)}, u32[]{:S(2)}) %collective-permute-start.34) | collective-permute-done | bytes 57376 | tf_op jit(solution)/shard_map/ppermute | solution.py:26
  71.4 0.7 shard_map.88
  (24 shorter events, 0.2 us)
Async XLA Ops:
  1.0 7.3 %copy-start = (f32[1,7168]{1,0:T(1,128)S(1)}, f32[1,7168]{1,0:T(1,128)}, u32[]{:S(2)}) copy-start(f32[1,7168]{1,0:T(1,128)} %gain_ref.3) | copy-start | bytes 86020
  1.0 7.3 %collective-permute-start = (bf16[4,7296]{1,0:T(4,128)(2,1)S(1)}, bf16[4,7296]{1,0:T(4,128)(2,1)S(1)}, u32[]{:S(2)}, u32[]{:S(2)}) collective-permute-start(bf16[4,7296]{1,0:T(4,128)(2,1)S(1)} %shard_map.73.own_ref), channel_id=1, source_target_pairs={{0,8},{1,9},{2,10},{3,11},{4,12},{5,13},{6,14},{7,15},{8,0},{9,1},... | collective-permute-start | bytes 175112 | tf_op jit(solution)/shard_map/ppermute | solution.py:26
  8.5 6.1 %collective-permute-start.4 = (bf16[8,7296]{1,0:T(8,128)(2,1)S(1)}, bf16[8,7296]{1,0:T(8,128)(2,1)S(1)}, u32[]{:S(2)}, u32[]{:S(2)}) collective-permute-start(bf16[8,7296]{1,0:T(8,128)(2,1)S(1)} %get-tuple-element.44.refs_0_), channel_id=1, source_target_pairs={{0,2},{1,3},{2,0},{3,1},{4,6},{5,7},{6,4},{7,5},{8,10},{9,11},{10,... | collective-permute-start | bytes 350216 | tf_op jit(solution)/shard_map/ppermute | solution.py:26
  10.5 6.1 %collective-permute-start.3 = (bf16[8,7296]{1,0:T(8,128)(2,1)S(1)}, bf16[8,7296]{1,0:T(8,128)(2,1)S(1)}, u32[]{:S(2)}, u32[]{:S(2)}) collective-permute-start(bf16[8,7296]{1,0:T(8,128)(2,1)S(1)} %get-tuple-element.44.refs_0_), channel_id=1, source_target_pairs={{0,6},{1,7},{2,4},{3,5},{4,2},{5,3},{6,0},{7,1},{8,14},{9,15},{10,... | collective-permute-start | bytes 350216 | tf_op jit(solution)/shard_map/ppermute | solution.py:26
  11.6 5.3 %collective-permute-start.2 = (bf16[8,7296]{1,0:T(8,128)(2,1)S(1)}, bf16[8,7296]{1,0:T(8,128)(2,1)S(1)}, u32[]{:S(2)}, u32[]{:S(2)}) collective-permute-start(bf16[8,7296]{1,0:T(8,128)(2,1)S(1)} %get-tuple-element.44.refs_0_), channel_id=1, source_target_pairs={{0,4},{1,5},{2,6},{3,7},{4,0},{5,1},{6,2},{7,3},{8,12},{9,13},{10,... | collective-permute-start | bytes 350216 | tf_op jit(solution)/shard_map/ppermute | solution.py:26
  14.1 3.1 %collective-permute-start.5 = (bf16[8,7296]{1,0:T(8,128)(2,1)S(1)}, bf16[8,7296]{1,0:T(8,128)(2,1)S(1)}, u32[]{:S(2)}, u32[]{:S(2)}) collective-permute-start(bf16[8,7296]{1,0:T(8,128)(2,1)S(1)} %get-tuple-element.44.refs_0_), channel_id=1, source_target_pairs={{0,1},{1,0},{2,3},{3,2},{4,5},{5,4},{6,7},{7,6},{8,9},{9,8},{10,11... | collective-permute-start | bytes 350216 | tf_op jit(solution)/shard_map/ppermute | solution.py:26
  14.6 2.5 %collective-permute-start.8 = (bf16[8,7296]{1,0:T(8,128)(2,1)S(1)}, bf16[8,7296]{1,0:T(8,128)(2,1)S(1)}, u32[]{:S(2)}, u32[]{:S(2)}) collective-permute-start(bf16[8,7296]{1,0:T(8,128)(2,1)S(1)} %collective-permute-done.4.refs_3_), channel_id=1, source_target_pairs={{0,1},{1,0},{2,3},{3,2},{4,5},{5,4},{6,7},{7,6},{8,9},{9,8},{10,11... | collective-permute-start | bytes 350216 | tf_op jit(solution)/shard_map/ppermute | solution.py:26
  16.6 1.3 %collective-permute-start.7 = (bf16[8,7296]{1,0:T(8,128)(2,1)S(1)}, bf16[8,7296]{1,0:T(8,128)(2,1)S(1)}, u32[]{:S(2)}, u32[]{:S(2)}) collective-permute-start(bf16[8,7296]{1,0:T(8,128)(2,1)S(1)} %collective-permute-done.3.refs_2_), channel_id=1, source_target_pairs={{0,1},{1,0},{2,3},{3,2},{4,5},{5,4},{6,7},{7,6},{8,9},{9,8},{10,11... | collective-permute-start | bytes 350216 | tf_op jit(solution)/shard_map/ppermute | solution.py:26
  16.9 1.3 %collective-permute-start.6 = (bf16[8,7296]{1,0:T(8,128)(2,1)S(1)}, bf16[8,7296]{1,0:T(8,128)(2,1)S(1)}, u32[]{:S(2)}, u32[]{:S(2)}) collective-permute-start(bf16[8,7296]{1,0:T(8,128)(2,1)S(1)} %collective-permute-done.2.refs_1_), channel_id=1, source_target_pairs={{0,1},{1,0},{2,3},{3,2},{4,5},{5,4},{6,7},{7,6},{8,9},{9,8},{10,11... | collective-permute-start | bytes 350216 | tf_op jit(solution)/shard_map/ppermute | solution.py:26
  20.4 1.4 %collective-permute-start.10 = (bf16[8,7168]{1,0:T(8,128)(2,1)S(1)}, bf16[8,7168]{1,0:T(8,128)(2,1)S(1)}, u32[]{:S(2)}, u32[]{:S(2)}) collective-permute-start(bf16[8,7168]{1,0:T(8,128)(2,1)S(1)} %get-tuple-element.51), channel_id=1, source_target_pairs={{0,1},{1,0},{2,3},{3,2},{4,5},{5,4},{6,7},{7,6},{8,9},{9,8},{10,11... | collective-permute-start | bytes 344072 | tf_op jit(solution)/shard_map/ppermute | solution.py:26
  20.7 2.8 %collective-permute-start.12 = (bf16[8,7168]{1,0:T(8,128)(2,1)S(1)}, bf16[8,7168]{1,0:T(8,128)(2,1)S(1)}, u32[]{:S(2)}, u32[]{:S(2)}) collective-permute-start(bf16[8,7168]{1,0:T(8,128)(2,1)S(1)} %get-tuple-element.53), channel_id=1, source_target_pairs={{0,1},{1,0},{2,3},{3,2},{4,5},{5,4},{6,7},{7,6},{8,9},{9,8},{10,11... | collective-permute-start | bytes 344072 | tf_op jit(solution)/shard_map/ppermute | solution.py:26
  21.0 4.0 %collective-permute-start.14 = (bf16[8,7168]{1,0:T(8,128)(2,1)S(1)}, bf16[8,7168]{1,0:T(8,128)(2,1)S(1)}, u32[]{:S(2)}, u32[]{:S(2)}) collective-permute-start(bf16[8,7168]{1,0:T(8,128)(2,1)S(1)} %get-tuple-element.55), channel_id=1, source_target_pairs={{0,1},{1,0},{2,3},{3,2},{4,5},{5,4},{6,7},{7,6},{8,9},{9,8},{10,11... | collective-permute-start | bytes 344072 | tf_op jit(solution)/shard_map/ppermute | solution.py:26
  21.2 5.9 %collective-permute-start.9 = (bf16[8,7168]{1,0:T(8,128)(2,1)S(1)}, bf16[8,7168]{1,0:T(8,128)(2,1)S(1)}, u32[]{:S(2)}, u32[]{:S(2)}) collective-permute-start(bf16[8,7168]{1,0:T(8,128)(2,1)S(1)} %get-tuple-element.49), channel_id=1, source_target_pairs={{0,1},{1,0},{2,3},{3,2},{4,5},{5,4},{6,7},{7,6},{8,9},{9,8},{10,11... | collective-permute-start | bytes 344072 | tf_op jit(solution)/shard_map/ppermute | solution.py:26
  21.8 5.4 %collective-permute-start.11 = (bf16[8,7168]{1,0:T(8,128)(2,1)S(1)}, bf16[8,7168]{1,0:T(8,128)(2,1)S(1)}, u32[]{:S(2)}, u32[]{:S(2)}) collective-permute-start(bf16[8,7168]{1,0:T(8,128)(2,1)S(1)} %shard_map.78), channel_id=1, source_target_pairs={{0,4},{1,5},{2,6},{3,7},{4,0},{5,1},{6,2},{7,3},{8,12},{9,13},{10,... | collective-permute-start | bytes 344072 | tf_op jit(solution)/shard_map/ppermute | solution.py:26
  23.5 7.1 %collective-permute-start.13 = (bf16[8,7168]{1,0:T(8,128)(2,1)S(1)}, bf16[8,7168]{1,0:T(8,128)(2,1)S(1)}, u32[]{:S(2)}, u32[]{:S(2)}) collective-permute-start(bf16[8,7168]{1,0:T(8,128)(2,1)S(1)} %shard_map.79), channel_id=1, source_target_pairs={{0,6},{1,7},{2,4},{3,5},{4,2},{5,3},{6,0},{7,1},{8,14},{9,15},{10,... | collective-permute-start | bytes 344072 | tf_op jit(solution)/shard_map/ppermute | solution.py:26
  25.0 7.2 %collective-permute-start.15 = (bf16[8,7168]{1,0:T(8,128)(2,1)S(1)}, bf16[8,7168]{1,0:T(8,128)(2,1)S(1)}, u32[]{:S(2)}, u32[]{:S(2)}) collective-permute-start(bf16[8,7168]{1,0:T(8,128)(2,1)S(1)} %shard_map.80), channel_id=1, source_target_pairs={{0,2},{1,3},{2,0},{3,1},{4,6},{5,7},{6,4},{7,5},{8,10},{9,11},{10,... | collective-permute-start | bytes 344072 | tf_op jit(solution)/shard_map/ppermute | solution.py:26
  25.6 10.4 %collective-permute-start.1 = (bf16[8,7168]{1,0:T(8,128)(2,1)S(1)}, bf16[8,7168]{1,0:T(8,128)(2,1)S(1)}, u32[]{:S(2)}, u32[]{:S(2)}) collective-permute-start(bf16[8,7168]{1,0:T(8,128)(2,1)S(1)} %get-tuple-element.40), channel_id=1, source_target_pairs={{0,16},{1,17},{2,18},{3,19},{4,20},{5,21},{6,22},{7,23},{8,24},{9,... | collective-permute-start | bytes 344072 | tf_op jit(solution)/shard_map/ppermute | solution.py:26
  32.3 8.9 %collective-permute-start.17 = (bf16[8,7168]{1,0:T(8,128)(2,1)S(1)}, bf16[8,7168]{1,0:T(8,128)(2,1)S(1)}, u32[]{:S(2)}, u32[]{:S(2)}) collective-permute-start(bf16[8,7168]{1,0:T(8,128)(2,1)S(1)} %shard_map.81), channel_id=1, source_target_pairs={{0,24},{1,25},{2,26},{3,27},{4,28},{5,29},{6,30},{7,31},{8,16},{9,... | collective-permute-start | bytes 344072 | tf_op jit(solution)/shard_map/ppermute | solution.py:26
  35.4 6.0 %collective-permute-start.16 = (bf16[8,7168]{1,0:T(8,128)(2,1)S(1)}, bf16[8,7168]{1,0:T(8,128)(2,1)S(1)}, u32[]{:S(2)}, u32[]{:S(2)}) collective-permute-start(bf16[8,7168]{1,0:T(8,128)(2,1)S(1)} %shard_map.81), channel_id=1, source_target_pairs={{0,16},{1,17},{2,18},{3,19},{4,20},{5,21},{6,22},{7,23},{8,24},{9,... | collective-permute-start | bytes 344072 | tf_op jit(solution)/shard_map/ppermute | solution.py:26
  41.6 6.4 %collective-permute-start.21 = (bf16[8,7168]{1,0:T(8,128)(2,1)S(1)}, bf16[8,7168]{1,0:T(8,128)(2,1)S(1)}, u32[]{:S(2)}, u32[]{:S(2)}) collective-permute-start(bf16[8,7168]{1,0:T(8,128)(2,1)S(1)} %get-tuple-element.57.refs_0_), channel_id=1, source_target_pairs={{0,2},{1,3},{2,0},{3,1},{4,6},{5,7},{6,4},{7,5},{8,10},{9,11},{10,... | collective-permute-start | bytes 344072 | tf_op jit(solution)/shard_map/ppermute | solution.py:26
  42.0 6.7 %collective-permute-start.20 = (bf16[8,7168]{1,0:T(8,128)(2,1)S(1)}, bf16[8,7168]{1,0:T(8,128)(2,1)S(1)}, u32[]{:S(2)}, u32[]{:S(2)}) collective-permute-start(bf16[8,7168]{1,0:T(8,128)(2,1)S(1)} %get-tuple-element.57.refs_0_), channel_id=1, source_target_pairs={{0,6},{1,7},{2,4},{3,5},{4,2},{5,3},{6,0},{7,1},{8,14},{9,15},{10,... | collective-permute-start | bytes 344072 | tf_op jit(solution)/shard_map/ppermute | solution.py:26
  44.4 5.5 %collective-permute-start.19 = (bf16[8,7168]{1,0:T(8,128)(2,1)S(1)}, bf16[8,7168]{1,0:T(8,128)(2,1)S(1)}, u32[]{:S(2)}, u32[]{:S(2)}) collective-permute-start(bf16[8,7168]{1,0:T(8,128)(2,1)S(1)} %get-tuple-element.57.refs_0_), channel_id=1, source_target_pairs={{0,4},{1,5},{2,6},{3,7},{4,0},{5,1},{6,2},{7,3},{8,12},{9,13},{10,... | collective-permute-start | bytes 344072 | tf_op jit(solution)/shard_map/ppermute | solution.py:26
  45.2 4.8 %collective-permute-start.22 = (bf16[8,7168]{1,0:T(8,128)(2,1)S(1)}, bf16[8,7168]{1,0:T(8,128)(2,1)S(1)}, u32[]{:S(2)}, u32[]{:S(2)}) collective-permute-start(bf16[8,7168]{1,0:T(8,128)(2,1)S(1)} %get-tuple-element.57.refs_0_), channel_id=1, source_target_pairs={{0,1},{1,0},{2,3},{3,2},{4,5},{5,4},{6,7},{7,6},{8,9},{9,8},{10,11... | collective-permute-start | bytes 344072 | tf_op jit(solution)/shard_map/ppermute | solution.py:26
  48.0 1.9 %collective-permute-start.25 = (bf16[8,7168]{1,0:T(8,128)(2,1)S(1)}, bf16[8,7168]{1,0:T(8,128)(2,1)S(1)}, u32[]{:S(2)}, u32[]{:S(2)}) collective-permute-start(bf16[8,7168]{1,0:T(8,128)(2,1)S(1)} %collective-permute-done.21.refs_3_), channel_id=1, source_target_pairs={{0,1},{1,0},{2,3},{3,2},{4,5},{5,4},{6,7},{7,6},{8,9},{9,8},{10,11... | collective-permute-start | bytes 344072 | tf_op jit(solution)/shard_map/ppermute | solution.py:26
  48.7 1.3 %collective-permute-start.24 = (bf16[8,7168]{1,0:T(8,128)(2,1)S(1)}, bf16[8,7168]{1,0:T(8,128)(2,1)S(1)}, u32[]{:S(2)}, u32[]{:S(2)}) collective-permute-start(bf16[8,7168]{1,0:T(8,128)(2,1)S(1)} %collective-permute-done.20.refs_2_), channel_id=1, source_target_pairs={{0,1},{1,0},{2,3},{3,2},{4,5},{5,4},{6,7},{7,6},{8,9},{9,8},{10,11... | collective-permute-start | bytes 344072 | tf_op jit(solution)/shard_map/ppermute | solution.py:26
  49.9 1.3 %collective-permute-start.23 = (bf16[8,7168]{1,0:T(8,128)(2,1)S(1)}, bf16[8,7168]{1,0:T(8,128)(2,1)S(1)}, u32[]{:S(2)}, u32[]{:S(2)}) collective-permute-start(bf16[8,7168]{1,0:T(8,128)(2,1)S(1)} %collective-permute-done.19.refs_1_), channel_id=1, source_target_pairs={{0,1},{1,0},{2,3},{3,2},{4,5},{5,4},{6,7},{7,6},{8,9},{9,8},{10,11... | collective-permute-start | bytes 344072 | tf_op jit(solution)/shard_map/ppermute | solution.py:26
  53.4 1.4 %collective-permute-start.27 = (bf16[8,7168]{1,0:T(8,128)(2,1)S(1)}, bf16[8,7168]{1,0:T(8,128)(2,1)S(1)}, u32[]{:S(2)}, u32[]{:S(2)}) collective-permute-start(bf16[8,7168]{1,0:T(8,128)(2,1)S(1)} %get-tuple-element.62), channel_id=1, source_target_pairs={{0,1},{1,0},{2,3},{3,2},{4,5},{5,4},{6,7},{7,6},{8,9},{9,8},{10,11... | collective-permute-start | bytes 344072 | tf_op jit(solution)/shard_map/ppermute | solution.py:26
  53.6 2.8 %collective-permute-start.29 = (bf16[8,7168]{1,0:T(8,128)(2,1)S(1)}, bf16[8,7168]{1,0:T(8,128)(2,1)S(1)}, u32[]{:S(2)}, u32[]{:S(2)}) collective-permute-start(bf16[8,7168]{1,0:T(8,128)(2,1)S(1)} %get-tuple-element.64), channel_id=1, source_target_pairs={{0,1},{1,0},{2,3},{3,2},{4,5},{5,4},{6,7},{7,6},{8,9},{9,8},{10,11... | collective-permute-start | bytes 344072 | tf_op jit(solution)/shard_map/ppermute | solution.py:26
  54.0 3.0 %collective-permute-start.31 = (bf16[8,7168]{1,0:T(8,128)(2,1)S(1)}, bf16[8,7168]{1,0:T(8,128)(2,1)S(1)}, u32[]{:S(2)}, u32[]{:S(2)}) collective-permute-start(bf16[8,7168]{1,0:T(8,128)(2,1)S(1)} %get-tuple-element.66), channel_id=1, source_target_pairs={{0,1},{1,0},{2,3},{3,2},{4,5},{5,4},{6,7},{7,6},{8,9},{9,8},{10,11... | collective-permute-start | bytes 344072 | tf_op jit(solution)/shard_map/ppermute | solution.py:26
  54.1 5.8 %collective-permute-start.26 = (bf16[8,7168]{1,0:T(8,128)(2,1)S(1)}, bf16[8,7168]{1,0:T(8,128)(2,1)S(1)}, u32[]{:S(2)}, u32[]{:S(2)}) collective-permute-start(bf16[8,7168]{1,0:T(8,128)(2,1)S(1)} %get-tuple-element.60), channel_id=1, source_target_pairs={{0,1},{1,0},{2,3},{3,2},{4,5},{5,4},{6,7},{7,6},{8,9},{9,8},{10,11... | collective-permute-start | bytes 344072 | tf_op jit(solution)/shard_map/ppermute | solution.py:26
  54.8 6.1 %collective-permute-start.28 = (bf16[8,7168]{1,0:T(8,128)(2,1)S(1)}, bf16[8,7168]{1,0:T(8,128)(2,1)S(1)}, u32[]{:S(2)}, u32[]{:S(2)}) collective-permute-start(bf16[8,7168]{1,0:T(8,128)(2,1)S(1)} %shard_map.84), channel_id=1, source_target_pairs={{0,4},{1,5},{2,6},{3,7},{4,0},{5,1},{6,2},{7,3},{8,12},{9,13},{10,... | collective-permute-start | bytes 344072 | tf_op jit(solution)/shard_map/ppermute | solution.py:26
  56.5 6.2 %collective-permute-start.30 = (bf16[8,7168]{1,0:T(8,128)(2,1)S(1)}, bf16[8,7168]{1,0:T(8,128)(2,1)S(1)}, u32[]{:S(2)}, u32[]{:S(2)}) collective-permute-start(bf16[8,7168]{1,0:T(8,128)(2,1)S(1)} %shard_map.85), channel_id=1, source_target_pairs={{0,6},{1,7},{2,4},{3,5},{4,2},{5,3},{6,0},{7,1},{8,14},{9,15},{10,... | collective-permute-start | bytes 344072 | tf_op jit(solution)/shard_map/ppermute | solution.py:26
  57.0 7.2 %collective-permute-start.32 = (bf16[8,7168]{1,0:T(8,128)(2,1)S(1)}, bf16[8,7168]{1,0:T(8,128)(2,1)S(1)}, u32[]{:S(2)}, u32[]{:S(2)}) collective-permute-start(bf16[8,7168]{1,0:T(8,128)(2,1)S(1)} %shard_map.86), channel_id=1, source_target_pairs={{0,2},{1,3},{2,0},{3,1},{4,6},{5,7},{6,4},{7,5},{8,10},{9,11},{10,... | collective-permute-start | bytes 344072 | tf_op jit(solution)/shard_map/ppermute | solution.py:26
  58.6 9.2 %collective-permute-start.18 = (bf16[4,7168]{1,0:T(4,128)(2,1)S(1)}, bf16[4,7168]{1,0:T(4,128)(2,1)S(1)}, u32[]{:S(2)}, u32[]{:S(2)}) collective-permute-start(bf16[4,7168]{1,0:T(4,128)(2,1)S(1)} %get-tuple-element.56), channel_id=1, source_target_pairs={{0,16},{1,17},{2,18},{3,19},{4,20},{5,21},{6,22},{7,23},{8,24},{9,... | collective-permute-start | bytes 172040 | tf_op jit(solution)/shard_map/ppermute | solution.py:26
  64.4 6.0 %collective-permute-start.33 = (bf16[4,7168]{1,0:T(4,128)(2,1)S(1)}, bf16[4,7168]{1,0:T(4,128)(2,1)S(1)}, u32[]{:S(2)}, u32[]{:S(2)}) collective-permute-start(bf16[4,7168]{1,0:T(4,128)(2,1)S(1)} %get-tuple-element.67), channel_id=1, source_target_pairs={{0,24},{1,25},{2,26},{3,27},{4,28},{5,29},{6,30},{7,31},{8,16},{9,... | collective-permute-start | bytes 172040 | tf_op jit(solution)/shard_map/ppermute | solution.py:26
  67.2 4.2 %collective-permute-start.34 = (bf16[4,7168]{1,0:T(4,128)(2,1)S(1)}, bf16[4,7168]{1,0:T(4,128)(2,1)S(1)}, u32[]{:S(2)}, u32[]{:S(2)}) collective-permute-start(bf16[4,7168]{1,0:T(4,128)(2,1)S(1)} %get-tuple-element.68), channel_id=1, source_target_pairs={{0,16},{1,17},{2,18},{3,19},{4,20},{5,21},{6,22},{7,23},{8,24},{9,... | collective-permute-start | bytes 172040 | tf_op jit(solution)/shard_map/ppermute | solution.py:26

commit v19 on v17

--- a/solution.py
+++ b/solution.py
@@ -257,7 +257,7 @@
 
         kept, sent = outs[:4], [exchange(rows, CORE, 0) for rows in outs[4:]]
         parts = [kept[0], sent[0]]
-        for place in (3, 2, 1):
+        for place in (3, 1, 2):
             parts.append(exchange(add(kept[place], sent[place]), SQUARE[place - 1], 0))
         for flips in middle[::-1]:
             low, high = split(*parts)

time: 70.6 us -> 70.7 us (level)
  no operation moved by 1% of the time
where the time goes in v19:
time: 70.7 us; the launch traced here: 70.5 us
  starting transfers between devices  31.2 us (44%)
  waiting for transfers between devices  27.3 us (39%)
  Pallas kernels  11.8 us (17%)
    ppermute x35, starting transfers between devices, exchange(): return lax.ppermute(value, ('segment', 'expert'), pairs)  31.2 us
    ppermute x35, waiting for transfers between devices, exchange(): return lax.ppermute(value, ('segment', 'expert'), pairs)  27.3 us
    pallas_call x14, Pallas kernels, call(): pl.pallas_call(kernel, out_shape=[jax.ShapeDtypeStruct(shape, jnp.bfloat1...  6.6 us
    pallas_call x2, Pallas kernels, load(): pl.pallas_call(functools.partial(load_kernel, count), out_shape=[pltpu.VM...  5.22 us
  transfers between devices with their start and end apart: 35, of which 18 were waited for; matrix products, arithmetic and copies ran while one was open for 0% of the time, Pallas kernels for 8%

profile of v19, /device:TPU:0, one launch (start us, length us, event | category | flops | bytes accessed | tf_op | source)
XLA Modules:
  0.0 70.5 jit_solution(14539999325108349552)
XLA Ops:
  0.0 1.0 %shard_map.73.own_ref = bf16[4,7296]{1,0:T(4,128)(2,1)S(1)} custom-call(bf16[1,4,7168]{2,1,0:T(4,128)(2,1)} %states_hbm.1, s32[1,2,2,4]{3,2,1,0:T(2,128)} %bitcast.3, bf16[1,2,2,4]{3,2,1,0:T(2,128)(2,1)} %bitcast.4), custom_call_target="tpu_custom_call" | custom-call | tf_op jit(solution)/shard_map/pallas_call | solution.py:43
  1.0 0.0 copy-start
  1.0 4.1 %collective-permute-start = (bf16[4,7296]{1,0:T(4,128)(2,1)S(1)}, bf16[4,7296]{1,0:T(4,128)(2,1)S(1)}, u32[]{:S(2)}, u32[]{:S(2)}) collective-permute-start(bf16[4,7296]{1,0:T(4,128)(2,1)S(1)} %shard_map.73.own_ref), channel_id=1, source_target_pairs={{0,8},{1,9},{2,10},{3,11},{4,12},{5,13},{6,14},{7,15},{8,0},{9,1},... | collective-permute-start | bytes 175112 | tf_op jit(solution)/shard_map/ppermute | solution.py:26
  5.1 3.2 %shard_map.74 = (bf16[1,7168,256]{2,1,0:T(8,128)(2,1)S(1)}, bf16[1,7168,256]{2,1,0:T(8,128)(2,1)S(1)}) custom-call(bf16[1,7168,256]{2,1,0:T(8,128)(2,1)} %refs_0_.1, bf16[1,7168,256]{2,1,0:T(8,128)(2,1)} %refs_1_.1), custom_call_target="tpu_custom_call" | custom-call | bytes 7340032 | tf_op jit(solution)/shard_map/pallas_call | solution.py:64
  8.3 0.2 shard_map.75
  8.5 2.6 %collective-permute-start.4 = (bf16[8,7296]{1,0:T(8,128)(2,1)S(1)}, bf16[8,7296]{1,0:T(8,128)(2,1)S(1)}, u32[]{:S(2)}, u32[]{:S(2)}) collective-permute-start(bf16[8,7296]{1,0:T(8,128)(2,1)S(1)} %get-tuple-element.44.refs_0_), channel_id=1, source_target_pairs={{0,6},{1,7},{2,4},{3,5},{4,2},{5,3},{6,0},{7,1},{8,14},{9,15},{10,... | collective-permute-start | bytes 350216 | tf_op jit(solution)/shard_map/ppermute | solution.py:26
  11.1 0.5 collective-permute-start.3
  11.6 0.4 collective-permute-start.2
  12.0 2.0 %shard_map.76.refs_10_.refs_11_ = bf16[1,256,7168]{2,1,0:T(8,128)(2,1)S(1)} custom-call(bf16[1,256,7168]{2,1,0:T(8,128)(2,1)} %refs_0_.2), custom_call_target="tpu_custom_call" | custom-call | bytes 3670016 | tf_op jit(solution)/shard_map/pallas_call | solution.py:64
  14.1 0.1 collective-permute-start.5
  14.2 0.4 collective-permute-done.4.refs_3_
  14.6 0.1 collective-permute-start.8
  14.7 2.0 %collective-permute-done.3.refs_2_ = bf16[8,7296]{1,0:T(8,128)(2,1)S(1)} collective-permute-done((bf16[8,7296]{1,0:T(8,128)(2,1)S(1)}, bf16[8,7296]{1,0:T(8,128)(2,1)S(1)}, u32[]{:S(2)}, u32[]{:S(2)}) %collective-permute-start.3) | collective-permute-done | bytes 116768 | tf_op jit(solution)/shard_map/ppermute | solution.py:26
  16.7 0.2 collective-permute-done.2.refs_1_
  16.9 0.3 collective-permute-start.6
  17.2 0.0 collective-permute-done.5.refs_4_
  17.2 0.0 collective-permute-done.8.refs_7_
  17.2 0.8 %collective-permute-done.7.refs_6_ = bf16[8,7296]{1,0:T(8,128)(2,1)S(1)} collective-permute-done((bf16[8,7296]{1,0:T(8,128)(2,1)S(1)}, bf16[8,7296]{1,0:T(8,128)(2,1)S(1)}, u32[]{:S(2)}, u32[]{:S(2)}) %collective-permute-start.7) | collective-permute-done | bytes 116768 | tf_op jit(solution)/shard_map/ppermute | solution.py:26
  18.0 0.2 collective-permute-done.6.refs_5_
  18.3 2.1 %shard_map.77 = (bf16[8,7168]{1,0:T(8,128)(2,1)S(1)}, bf16[8,7168]{1,0:T(8,128)(2,1)S(1)}, bf16[8,7168]{1,0:T(8,128)(2,1)S(1)}, bf16[8,7168]{1,0:T(8,128)(2,1)S(...) custom-call(bf16[8,7296]{1,0:T(8,128)(2,1)S(1)} %get-tuple-element.4, ...), custom_call_target="tpu_custom_call" | custom-call | flops 704643072 | bytes 11010048 | tf_op jit(solution)/shard_map/pallas_call | solution.py:43
  20.4 0.3 collective-permute-start.10
  20.7 0.2 collective-permute-start.12
  21.0 0.3 collective-permute-start.14
  21.3 0.2 collective-permute-start.9
  21.5 0.3 collective-permute-done.10.refs_1_
  21.8 1.6 %collective-permute-start.11 = (bf16[8,7168]{1,0:T(8,128)(2,1)S(1)}, bf16[8,7168]{1,0:T(8,128)(2,1)S(1)}, u32[]{:S(2)}, u32[]{:S(2)}) collective-permute-start(bf16[8,7168]{1,0:T(8,128)(2,1)S(1)} %shard_map.78), channel_id=1, source_target_pairs={{0,6},{1,7},{2,4},{3,5},{4,2},{5,3},{6,0},{7,1},{8,14},{9,15},{10,... | collective-permute-start | bytes 344072 | tf_op jit(solution)/shard_map/ppermute | solution.py:26
  23.5 0.0 collective-permute-done.12.refs_1_
  23.5 1.3 %collective-permute-start.13 = (bf16[8,7168]{1,0:T(8,128)(2,1)S(1)}, bf16[8,7168]{1,0:T(8,128)(2,1)S(1)}, u32[]{:S(2)}, u32[]{:S(2)}) collective-permute-start(bf16[8,7168]{1,0:T(8,128)(2,1)S(1)} %shard_map.79), channel_id=1, source_target_pairs={{0,4},{1,5},{2,6},{3,7},{4,0},{5,1},{6,2},{7,3},{8,12},{9,13},{10,... | collective-permute-start | bytes 344072 | tf_op jit(solution)/shard_map/ppermute | solution.py:26
  24.8 0.7 %collective-permute-start.15 = (bf16[8,7168]{1,0:T(8,128)(2,1)S(1)}, bf16[8,7168]{1,0:T(8,128)(2,1)S(1)}, u32[]{:S(2)}, u32[]{:S(2)}) collective-permute-start(bf16[8,7168]{1,0:T(8,128)(2,1)S(1)} %shard_map.80), channel_id=1, source_target_pairs={{0,2},{1,3},{2,0},{3,1},{4,6},{5,7},{6,4},{7,5},{8,10},{9,11},{10,... | collective-permute-start | bytes 344072 | tf_op jit(solution)/shard_map/ppermute | solution.py:26
  25.6 1.5 %collective-permute-start.1 = (bf16[8,7168]{1,0:T(8,128)(2,1)S(1)}, bf16[8,7168]{1,0:T(8,128)(2,1)S(1)}, u32[]{:S(2)}, u32[]{:S(2)}) collective-permute-start(bf16[8,7168]{1,0:T(8,128)(2,1)S(1)} %get-tuple-element.40), channel_id=1, source_target_pairs={{0,16},{1,17},{2,18},{3,19},{4,20},{5,21},{6,22},{7,23},{8,24},{9,... | collective-permute-start | bytes 344072 | tf_op jit(solution)/shard_map/ppermute | solution.py:26
  27.1 1.7 %collective-permute-done.11.refs_2_ = bf16[8,7168]{1,0:T(8,128)(2,1)S(1)} collective-permute-done((bf16[8,7168]{1,0:T(8,128)(2,1)S(1)}, bf16[8,7168]{1,0:T(8,128)(2,1)S(1)}, u32[]{:S(2)}, u32[]{:S(2)}) %collective-permute-start.11) | collective-permute-done | bytes 114720 | tf_op jit(solution)/shard_map/ppermute | solution.py:26
  28.8 1.8 %collective-permute-done.13.refs_3_ = bf16[8,7168]{1,0:T(8,128)(2,1)S(1)} collective-permute-done((bf16[8,7168]{1,0:T(8,128)(2,1)S(1)}, bf16[8,7168]{1,0:T(8,128)(2,1)S(1)}, u32[]{:S(2)}, u32[]{:S(2)}) %collective-permute-start.13) | collective-permute-done | bytes 114720 | tf_op jit(solution)/shard_map/ppermute | solution.py:26
  30.5 0.0 collective-permute-done.15.refs_4_
  30.6 0.1 shard_map.81
  30.6 3.2 %collective-permute-start.17 = (bf16[8,7168]{1,0:T(8,128)(2,1)S(1)}, bf16[8,7168]{1,0:T(8,128)(2,1)S(1)}, u32[]{:S(2)}, u32[]{:S(2)}) collective-permute-start(bf16[8,7168]{1,0:T(8,128)(2,1)S(1)} %shard_map.81), channel_id=1, source_target_pairs={{0,24},{1,25},{2,26},{3,27},{4,28},{5,29},{6,30},{7,31},{8,16},{9,... | collective-permute-start | bytes 344072 | tf_op jit(solution)/shard_map/ppermute | solution.py:26
  33.8 0.5 collective-permute-start.16
  34.3 5.4 %collective-permute-done.17.far_ref = bf16[8,7168]{1,0:T(8,128)(2,1)S(1)} collective-permute-done((bf16[8,7168]{1,0:T(8,128)(2,1)S(1)}, bf16[8,7168]{1,0:T(8,128)(2,1)S(1)}, u32[]{:S(2)}, u32[]{:S(2)}) %collective-permute-start.17) | collective-permute-done | bytes 114720 | tf_op jit(solution)/shard_map/ppermute | solution.py:26
  39.7 0.2 shard_map.82
  40.0 1.8 %collective-permute-start.21 = (bf16[8,7168]{1,0:T(8,128)(2,1)S(1)}, bf16[8,7168]{1,0:T(8,128)(2,1)S(1)}, u32[]{:S(2)}, u32[]{:S(2)}) collective-permute-start(bf16[8,7168]{1,0:T(8,128)(2,1)S(1)} %get-tuple-element.57.refs_0_), channel_id=1, source_target_pairs={{0,6},{1,7},{2,4},{3,5},{4,2},{5,3},{6,0},{7,1},{8,14},{9,15},{10,... | collective-permute-start | bytes 344072 | tf_op jit(solution)/shard_map/ppermute | solution.py:26
  41.7 1.5 %collective-permute-start.20 = (bf16[8,7168]{1,0:T(8,128)(2,1)S(1)}, bf16[8,7168]{1,0:T(8,128)(2,1)S(1)}, u32[]{:S(2)}, u32[]{:S(2)}) collective-permute-start(bf16[8,7168]{1,0:T(8,128)(2,1)S(1)} %get-tuple-element.57.refs_0_), channel_id=1, source_target_pairs={{0,2},{1,3},{2,0},{3,1},{4,6},{5,7},{6,4},{7,5},{8,10},{9,11},{10,... | collective-permute-start | bytes 344072 | tf_op jit(solution)/shard_map/ppermute | solution.py:26
  43.3 0.6 collective-permute-start.19
  43.9 2.3 %collective-permute-done.21.refs_3_ = bf16[8,7168]{1,0:T(8,128)(2,1)S(1)} collective-permute-done((bf16[8,7168]{1,0:T(8,128)(2,1)S(1)}, bf16[8,7168]{1,0:T(8,128)(2,1)S(1)}, u32[]{:S(2)}, u32[]{:S(2)}) %collective-permute-start.21) | collective-permute-done | bytes 114720 | tf_op jit(solution)/shard_map/ppermute | solution.py:26
  46.2 1.5 %collective-permute-done.20.refs_2_ = bf16[8,7168]{1,0:T(8,128)(2,1)S(1)} collective-permute-done((bf16[8,7168]{1,0:T(8,128)(2,1)S(1)}, bf16[8,7168]{1,0:T(8,128)(2,1)S(1)}, u32[]{:S(2)}, u32[]{:S(2)}) %collective-permute-start.20) | collective-permute-done | bytes 114720 | tf_op jit(solution)/shard_map/ppermute | solution.py:26
  47.8 1.3 %collective-permute-done.19.refs_1_ = bf16[8,7168]{1,0:T(8,128)(2,1)S(1)} collective-permute-done((bf16[8,7168]{1,0:T(8,128)(2,1)S(1)}, bf16[8,7168]{1,0:T(8,128)(2,1)S(1)}, u32[]{:S(2)}, u32[]{:S(2)}) %collective-permute-start.19) | collective-permute-done | bytes 114720 | tf_op jit(solution)/shard_map/ppermute | solution.py:26
  49.0 0.1 collective-permute-done.24.refs_6_
  49.1 1.3 %collective-permute-done.23.refs_5_ = bf16[8,7168]{1,0:T(8,128)(2,1)S(1)} collective-permute-done((bf16[8,7168]{1,0:T(8,128)(2,1)S(1)}, bf16[8,7168]{1,0:T(8,128)(2,1)S(1)}, u32[]{:S(2)}, u32[]{:S(2)}) %collective-permute-start.23) | collective-permute-done | bytes 114720 | tf_op jit(solution)/shard_map/ppermute | solution.py:26
  50.3 2.1 %shard_map.83 = (bf16[8,7168]{1,0:T(8,128)(2,1)S(1)}, bf16[8,7168]{1,0:T(8,128)(2,1)S(1)}, bf16[8,7168]{1,0:T(8,128)(2,1)S(1)}, bf16[8,7168]{1,0:T(8,128)(2,1)S(...) custom-call(bf16[8,7168]{1,0:T(8,128)(2,1)S(1)} %get-tuple-element.5, ...), custom_call_target="tpu_custom_call" | custom-call | flops 704643072 | bytes 11010048 | tf_op jit(solution)/shard_map/pallas_call | solution.py:43
  52.5 0.2 collective-permute-start.27
  52.7 0.4 collective-permute-start.29
  53.0 0.1 collective-permute-start.31
  53.2 0.4 collective-permute-start.26
  53.5 0.3 collective-permute-done.27.refs_1_
  53.9 1.3 %collective-permute-start.28 = (bf16[8,7168]{1,0:T(8,128)(2,1)S(1)}, bf16[8,7168]{1,0:T(8,128)(2,1)S(1)}, u32[]{:S(2)}, u32[]{:S(2)}) collective-permute-start(bf16[8,7168]{1,0:T(8,128)(2,1)S(1)} %shard_map.84), channel_id=1, source_target_pairs={{0,6},{1,7},{2,4},{3,5},{4,2},{5,3},{6,0},{7,1},{8,14},{9,15},{10,... | collective-permute-start | bytes 344072 | tf_op jit(solution)/shard_map/ppermute | solution.py:26
  55.2 1.5 %collective-permute-start.30 = (bf16[8,7168]{1,0:T(8,128)(2,1)S(1)}, bf16[8,7168]{1,0:T(8,128)(2,1)S(1)}, u32[]{:S(2)}, u32[]{:S(2)}) collective-permute-start(bf16[8,7168]{1,0:T(8,128)(2,1)S(1)} %shard_map.85), channel_id=1, source_target_pairs={{0,4},{1,5},{2,6},{3,7},{4,0},{5,1},{6,2},{7,3},{8,12},{9,13},{10,... | collective-permute-start | bytes 344072 | tf_op jit(solution)/shard_map/ppermute | solution.py:26
  56.8 0.8 %collective-permute-start.32 = (bf16[8,7168]{1,0:T(8,128)(2,1)S(1)}, bf16[8,7168]{1,0:T(8,128)(2,1)S(1)}, u32[]{:S(2)}, u32[]{:S(2)}) collective-permute-start(bf16[8,7168]{1,0:T(8,128)(2,1)S(1)} %shard_map.86), channel_id=1, source_target_pairs={{0,2},{1,3},{2,0},{3,1},{4,6},{5,7},{6,4},{7,5},{8,10},{9,11},{10,... | collective-permute-start | bytes 344072 | tf_op jit(solution)/shard_map/ppermute | solution.py:26
  57.6 1.2 %collective-permute-start.18 = (bf16[4,7168]{1,0:T(4,128)(2,1)S(1)}, bf16[4,7168]{1,0:T(4,128)(2,1)S(1)}, u32[]{:S(2)}, u32[]{:S(2)}) collective-permute-start(bf16[4,7168]{1,0:T(4,128)(2,1)S(1)} %get-tuple-element.56), channel_id=1, source_target_pairs={{0,16},{1,17},{2,18},{3,19},{4,20},{5,21},{6,22},{7,23},{8,24},{9,... | collective-permute-start | bytes 172040 | tf_op jit(solution)/shard_map/ppermute | solution.py:26
  58.8 2.0 %collective-permute-done.28.refs_2_ = bf16[8,7168]{1,0:T(8,128)(2,1)S(1)} collective-permute-done((bf16[8,7168]{1,0:T(8,128)(2,1)S(1)}, bf16[8,7168]{1,0:T(8,128)(2,1)S(1)}, u32[]{:S(2)}, u32[]{:S(2)}) %collective-permute-start.28) | collective-permute-done | bytes 114720 | tf_op jit(solution)/shard_map/ppermute | solution.py:26
  60.8 1.7 %collective-permute-done.30.refs_3_ = bf16[8,7168]{1,0:T(8,128)(2,1)S(1)} collective-permute-done((bf16[8,7168]{1,0:T(8,128)(2,1)S(1)}, bf16[8,7168]{1,0:T(8,128)(2,1)S(1)}, u32[]{:S(2)}, u32[]{:S(2)}) %collective-permute-start.30) | collective-permute-done | bytes 114720 | tf_op jit(solution)/shard_map/ppermute | solution.py:26
  62.5 0.0 collective-permute-done.32.refs_4_
  62.5 0.1 shard_map.87
  62.6 1.6 %collective-permute-start.33 = (bf16[4,7168]{1,0:T(4,128)(2,1)S(1)}, bf16[4,7168]{1,0:T(4,128)(2,1)S(1)}, u32[]{:S(2)}, u32[]{:S(2)}) collective-permute-start(bf16[4,7168]{1,0:T(4,128)(2,1)S(1)} %get-tuple-element.67), channel_id=1, source_target_pairs={{0,24},{1,25},{2,26},{3,27},{4,28},{5,29},{6,30},{7,31},{8,16},{9,... | collective-permute-start | bytes 172040 | tf_op jit(solution)/shard_map/ppermute | solution.py:26
  64.2 1.7 %collective-permute-start.34 = (bf16[4,7168]{1,0:T(4,128)(2,1)S(1)}, bf16[4,7168]{1,0:T(4,128)(2,1)S(1)}, u32[]{:S(2)}, u32[]{:S(2)}) collective-permute-start(bf16[4,7168]{1,0:T(4,128)(2,1)S(1)} %get-tuple-element.68), channel_id=1, source_target_pairs={{0,16},{1,17},{2,18},{3,19},{4,20},{5,21},{6,22},{7,23},{8,24},{9,... | collective-permute-start | bytes 172040 | tf_op jit(solution)/shard_map/ppermute | solution.py:26
  65.9 4.0 %collective-permute-done.33.refs_1_ = bf16[4,7168]{1,0:T(4,128)(2,1)S(1)} collective-permute-done((bf16[4,7168]{1,0:T(4,128)(2,1)S(1)}, bf16[4,7168]{1,0:T(4,128)(2,1)S(1)}, u32[]{:S(2)}, u32[]{:S(2)}) %collective-permute-start.33) | collective-permute-done | bytes 57376 | tf_op jit(solution)/shard_map/ppermute | solution.py:26
  69.9 0.7 shard_map.88
  (24 shorter events, 0.2 us)
Async XLA Ops:
  1.0 7.3 %copy-start = (f32[1,7168]{1,0:T(1,128)S(1)}, f32[1,7168]{1,0:T(1,128)}, u32[]{:S(2)}) copy-start(f32[1,7168]{1,0:T(1,128)} %gain_ref.3) | copy-start | bytes 86020
  1.0 7.3 %collective-permute-start = (bf16[4,7296]{1,0:T(4,128)(2,1)S(1)}, bf16[4,7296]{1,0:T(4,128)(2,1)S(1)}, u32[]{:S(2)}, u32[]{:S(2)}) collective-permute-start(bf16[4,7296]{1,0:T(4,128)(2,1)S(1)} %shard_map.73.own_ref), channel_id=1, source_target_pairs={{0,8},{1,9},{2,10},{3,11},{4,12},{5,13},{6,14},{7,15},{8,0},{9,1},... | collective-permute-start | bytes 175112 | tf_op jit(solution)/shard_map/ppermute | solution.py:26
  8.5 6.1 %collective-permute-start.4 = (bf16[8,7296]{1,0:T(8,128)(2,1)S(1)}, bf16[8,7296]{1,0:T(8,128)(2,1)S(1)}, u32[]{:S(2)}, u32[]{:S(2)}) collective-permute-start(bf16[8,7296]{1,0:T(8,128)(2,1)S(1)} %get-tuple-element.44.refs_0_), channel_id=1, source_target_pairs={{0,6},{1,7},{2,4},{3,5},{4,2},{5,3},{6,0},{7,1},{8,14},{9,15},{10,... | collective-permute-start | bytes 350216 | tf_op jit(solution)/shard_map/ppermute | solution.py:26
  11.1 5.6 %collective-permute-start.3 = (bf16[8,7296]{1,0:T(8,128)(2,1)S(1)}, bf16[8,7296]{1,0:T(8,128)(2,1)S(1)}, u32[]{:S(2)}, u32[]{:S(2)}) collective-permute-start(bf16[8,7296]{1,0:T(8,128)(2,1)S(1)} %get-tuple-element.44.refs_0_), channel_id=1, source_target_pairs={{0,2},{1,3},{2,0},{3,1},{4,6},{5,7},{6,4},{7,5},{8,10},{9,11},{10,... | collective-permute-start | bytes 350216 | tf_op jit(solution)/shard_map/ppermute | solution.py:26
  11.6 5.3 %collective-permute-start.2 = (bf16[8,7296]{1,0:T(8,128)(2,1)S(1)}, bf16[8,7296]{1,0:T(8,128)(2,1)S(1)}, u32[]{:S(2)}, u32[]{:S(2)}) collective-permute-start(bf16[8,7296]{1,0:T(8,128)(2,1)S(1)} %get-tuple-element.44.refs_0_), channel_id=1, source_target_pairs={{0,4},{1,5},{2,6},{3,7},{4,0},{5,1},{6,2},{7,3},{8,12},{9,13},{10,... | collective-permute-start | bytes 350216 | tf_op jit(solution)/shard_map/ppermute | solution.py:26
  14.1 3.1 %collective-permute-start.5 = (bf16[8,7296]{1,0:T(8,128)(2,1)S(1)}, bf16[8,7296]{1,0:T(8,128)(2,1)S(1)}, u32[]{:S(2)}, u32[]{:S(2)}) collective-permute-start(bf16[8,7296]{1,0:T(8,128)(2,1)S(1)} %get-tuple-element.44.refs_0_), channel_id=1, source_target_pairs={{0,1},{1,0},{2,3},{3,2},{4,5},{5,4},{6,7},{7,6},{8,9},{9,8},{10,11... | collective-permute-start | bytes 350216 | tf_op jit(solution)/shard_map/ppermute | solution.py:26
  14.6 2.7 %collective-permute-start.8 = (bf16[8,7296]{1,0:T(8,128)(2,1)S(1)}, bf16[8,7296]{1,0:T(8,128)(2,1)S(1)}, u32[]{:S(2)}, u32[]{:S(2)}) collective-permute-start(bf16[8,7296]{1,0:T(8,128)(2,1)S(1)} %collective-permute-done.4.refs_3_), channel_id=1, source_target_pairs={{0,1},{1,0},{2,3},{3,2},{4,5},{5,4},{6,7},{7,6},{8,9},{9,8},{10,11... | collective-permute-start | bytes 350216 | tf_op jit(solution)/shard_map/ppermute | solution.py:26
  16.7 1.3 %collective-permute-start.7 = (bf16[8,7296]{1,0:T(8,128)(2,1)S(1)}, bf16[8,7296]{1,0:T(8,128)(2,1)S(1)}, u32[]{:S(2)}, u32[]{:S(2)}) collective-permute-start(bf16[8,7296]{1,0:T(8,128)(2,1)S(1)} %collective-permute-done.3.refs_2_), channel_id=1, source_target_pairs={{0,1},{1,0},{2,3},{3,2},{4,5},{5,4},{6,7},{7,6},{8,9},{9,8},{10,11... | collective-permute-start | bytes 350216 | tf_op jit(solution)/shard_map/ppermute | solution.py:26
  16.9 1.3 %collective-permute-start.6 = (bf16[8,7296]{1,0:T(8,128)(2,1)S(1)}, bf16[8,7296]{1,0:T(8,128)(2,1)S(1)}, u32[]{:S(2)}, u32[]{:S(2)}) collective-permute-start(bf16[8,7296]{1,0:T(8,128)(2,1)S(1)} %collective-permute-done.2.refs_1_), channel_id=1, source_target_pairs={{0,1},{1,0},{2,3},{3,2},{4,5},{5,4},{6,7},{7,6},{8,9},{9,8},{10,11... | collective-permute-start | bytes 350216 | tf_op jit(solution)/shard_map/ppermute | solution.py:26
  20.4 1.4 %collective-permute-start.10 = (bf16[8,7168]{1,0:T(8,128)(2,1)S(1)}, bf16[8,7168]{1,0:T(8,128)(2,1)S(1)}, u32[]{:S(2)}, u32[]{:S(2)}) collective-permute-start(bf16[8,7168]{1,0:T(8,128)(2,1)S(1)} %get-tuple-element.51), channel_id=1, source_target_pairs={{0,1},{1,0},{2,3},{3,2},{4,5},{5,4},{6,7},{7,6},{8,9},{9,8},{10,11... | collective-permute-start | bytes 344072 | tf_op jit(solution)/shard_map/ppermute | solution.py:26
  20.7 2.7 %collective-permute-start.12 = (bf16[8,7168]{1,0:T(8,128)(2,1)S(1)}, bf16[8,7168]{1,0:T(8,128)(2,1)S(1)}, u32[]{:S(2)}, u32[]{:S(2)}) collective-permute-start(bf16[8,7168]{1,0:T(8,128)(2,1)S(1)} %get-tuple-element.53), channel_id=1, source_target_pairs={{0,1},{1,0},{2,3},{3,2},{4,5},{5,4},{6,7},{7,6},{8,9},{9,8},{10,11... | collective-permute-start | bytes 344072 | tf_op jit(solution)/shard_map/ppermute | solution.py:26
  21.0 3.8 %collective-permute-start.14 = (bf16[8,7168]{1,0:T(8,128)(2,1)S(1)}, bf16[8,7168]{1,0:T(8,128)(2,1)S(1)}, u32[]{:S(2)}, u32[]{:S(2)}) collective-permute-start(bf16[8,7168]{1,0:T(8,128)(2,1)S(1)} %get-tuple-element.55), channel_id=1, source_target_pairs={{0,1},{1,0},{2,3},{3,2},{4,5},{5,4},{6,7},{7,6},{8,9},{9,8},{10,11... | collective-permute-start | bytes 344072 | tf_op jit(solution)/shard_map/ppermute | solution.py:26
  21.3 5.8 %collective-permute-start.9 = (bf16[8,7168]{1,0:T(8,128)(2,1)S(1)}, bf16[8,7168]{1,0:T(8,128)(2,1)S(1)}, u32[]{:S(2)}, u32[]{:S(2)}) collective-permute-start(bf16[8,7168]{1,0:T(8,128)(2,1)S(1)} %get-tuple-element.49), channel_id=1, source_target_pairs={{0,1},{1,0},{2,3},{3,2},{4,5},{5,4},{6,7},{7,6},{8,9},{9,8},{10,11... | collective-permute-start | bytes 344072 | tf_op jit(solution)/shard_map/ppermute | solution.py:26
  21.8 6.9 %collective-permute-start.11 = (bf16[8,7168]{1,0:T(8,128)(2,1)S(1)}, bf16[8,7168]{1,0:T(8,128)(2,1)S(1)}, u32[]{:S(2)}, u32[]{:S(2)}) collective-permute-start(bf16[8,7168]{1,0:T(8,128)(2,1)S(1)} %shard_map.78), channel_id=1, source_target_pairs={{0,6},{1,7},{2,4},{3,5},{4,2},{5,3},{6,0},{7,1},{8,14},{9,15},{10,... | collective-permute-start | bytes 344072 | tf_op jit(solution)/shard_map/ppermute | solution.py:26
  23.5 7.0 %collective-permute-start.13 = (bf16[8,7168]{1,0:T(8,128)(2,1)S(1)}, bf16[8,7168]{1,0:T(8,128)(2,1)S(1)}, u32[]{:S(2)}, u32[]{:S(2)}) collective-permute-start(bf16[8,7168]{1,0:T(8,128)(2,1)S(1)} %shard_map.79), channel_id=1, source_target_pairs={{0,4},{1,5},{2,6},{3,7},{4,0},{5,1},{6,2},{7,3},{8,12},{9,13},{10,... | collective-permute-start | bytes 344072 | tf_op jit(solution)/shard_map/ppermute | solution.py:26
  24.8 5.7 %collective-permute-start.15 = (bf16[8,7168]{1,0:T(8,128)(2,1)S(1)}, bf16[8,7168]{1,0:T(8,128)(2,1)S(1)}, u32[]{:S(2)}, u32[]{:S(2)}) collective-permute-start(bf16[8,7168]{1,0:T(8,128)(2,1)S(1)} %shard_map.80), channel_id=1, source_target_pairs={{0,2},{1,3},{2,0},{3,1},{4,6},{5,7},{6,4},{7,5},{8,10},{9,11},{10,... | collective-permute-start | bytes 344072 | tf_op jit(solution)/shard_map/ppermute | solution.py:26
  25.6 8.8 %collective-permute-start.1 = (bf16[8,7168]{1,0:T(8,128)(2,1)S(1)}, bf16[8,7168]{1,0:T(8,128)(2,1)S(1)}, u32[]{:S(2)}, u32[]{:S(2)}) collective-permute-start(bf16[8,7168]{1,0:T(8,128)(2,1)S(1)} %get-tuple-element.40), channel_id=1, source_target_pairs={{0,16},{1,17},{2,18},{3,19},{4,20},{5,21},{6,22},{7,23},{8,24},{9,... | collective-permute-start | bytes 344072 | tf_op jit(solution)/shard_map/ppermute | solution.py:26
  30.6 9.1 %collective-permute-start.17 = (bf16[8,7168]{1,0:T(8,128)(2,1)S(1)}, bf16[8,7168]{1,0:T(8,128)(2,1)S(1)}, u32[]{:S(2)}, u32[]{:S(2)}) collective-permute-start(bf16[8,7168]{1,0:T(8,128)(2,1)S(1)} %shard_map.81), channel_id=1, source_target_pairs={{0,24},{1,25},{2,26},{3,27},{4,28},{5,29},{6,30},{7,31},{8,16},{9,... | collective-permute-start | bytes 344072 | tf_op jit(solution)/shard_map/ppermute | solution.py:26
  33.8 5.9 %collective-permute-start.16 = (bf16[8,7168]{1,0:T(8,128)(2,1)S(1)}, bf16[8,7168]{1,0:T(8,128)(2,1)S(1)}, u32[]{:S(2)}, u32[]{:S(2)}) collective-permute-start(bf16[8,7168]{1,0:T(8,128)(2,1)S(1)} %shard_map.81), channel_id=1, source_target_pairs={{0,16},{1,17},{2,18},{3,19},{4,20},{5,21},{6,22},{7,23},{8,24},{9,... | collective-permute-start | bytes 344072 | tf_op jit(solution)/shard_map/ppermute | solution.py:26
  40.0 6.3 %collective-permute-start.21 = (bf16[8,7168]{1,0:T(8,128)(2,1)S(1)}, bf16[8,7168]{1,0:T(8,128)(2,1)S(1)}, u32[]{:S(2)}, u32[]{:S(2)}) collective-permute-start(bf16[8,7168]{1,0:T(8,128)(2,1)S(1)} %get-tuple-element.57.refs_0_), channel_id=1, source_target_pairs={{0,6},{1,7},{2,4},{3,5},{4,2},{5,3},{6,0},{7,1},{8,14},{9,15},{10,... | collective-permute-start | bytes 344072 | tf_op jit(solution)/shard_map/ppermute | solution.py:26
  41.7 6.0 %collective-permute-start.20 = (bf16[8,7168]{1,0:T(8,128)(2,1)S(1)}, bf16[8,7168]{1,0:T(8,128)(2,1)S(1)}, u32[]{:S(2)}, u32[]{:S(2)}) collective-permute-start(bf16[8,7168]{1,0:T(8,128)(2,1)S(1)} %get-tuple-element.57.refs_0_), channel_id=1, source_target_pairs={{0,2},{1,3},{2,0},{3,1},{4,6},{5,7},{6,4},{7,5},{8,10},{9,11},{10,... | collective-permute-start | bytes 344072 | tf_op jit(solution)/shard_map/ppermute | solution.py:26
  43.3 5.7 %collective-permute-start.19 = (bf16[8,7168]{1,0:T(8,128)(2,1)S(1)}, bf16[8,7168]{1,0:T(8,128)(2,1)S(1)}, u32[]{:S(2)}, u32[]{:S(2)}) collective-permute-start(bf16[8,7168]{1,0:T(8,128)(2,1)S(1)} %get-tuple-element.57.refs_0_), channel_id=1, source_target_pairs={{0,4},{1,5},{2,6},{3,7},{4,0},{5,1},{6,2},{7,3},{8,12},{9,13},{10,... | collective-permute-start | bytes 344072 | tf_op jit(solution)/shard_map/ppermute | solution.py:26
  43.9 5.1 %collective-permute-start.22 = (bf16[8,7168]{1,0:T(8,128)(2,1)S(1)}, bf16[8,7168]{1,0:T(8,128)(2,1)S(1)}, u32[]{:S(2)}, u32[]{:S(2)}) collective-permute-start(bf16[8,7168]{1,0:T(8,128)(2,1)S(1)} %get-tuple-element.57.refs_0_), channel_id=1, source_target_pairs={{0,1},{1,0},{2,3},{3,2},{4,5},{5,4},{6,7},{7,6},{8,9},{9,8},{10,11... | collective-permute-start | bytes 344072 | tf_op jit(solution)/shard_map/ppermute | solution.py:26
  46.2 2.8 %collective-permute-start.25 = (bf16[8,7168]{1,0:T(8,128)(2,1)S(1)}, bf16[8,7168]{1,0:T(8,128)(2,1)S(1)}, u32[]{:S(2)}, u32[]{:S(2)}) collective-permute-start(bf16[8,7168]{1,0:T(8,128)(2,1)S(1)} %collective-permute-done.21.refs_3_), channel_id=1, source_target_pairs={{0,1},{1,0},{2,3},{3,2},{4,5},{5,4},{6,7},{7,6},{8,9},{9,8},{10,11... | collective-permute-start | bytes 344072 | tf_op jit(solution)/shard_map/ppermute | solution.py:26
  47.7 1.3 %collective-permute-start.24 = (bf16[8,7168]{1,0:T(8,128)(2,1)S(1)}, bf16[8,7168]{1,0:T(8,128)(2,1)S(1)}, u32[]{:S(2)}, u32[]{:S(2)}) collective-permute-start(bf16[8,7168]{1,0:T(8,128)(2,1)S(1)} %collective-permute-done.20.refs_2_), channel_id=1, source_target_pairs={{0,1},{1,0},{2,3},{3,2},{4,5},{5,4},{6,7},{7,6},{8,9},{9,8},{10,11... | collective-permute-start | bytes 344072 | tf_op jit(solution)/shard_map/ppermute | solution.py:26
  49.0 1.3 %collective-permute-start.23 = (bf16[8,7168]{1,0:T(8,128)(2,1)S(1)}, bf16[8,7168]{1,0:T(8,128)(2,1)S(1)}, u32[]{:S(2)}, u32[]{:S(2)}) collective-permute-start(bf16[8,7168]{1,0:T(8,128)(2,1)S(1)} %collective-permute-done.19.refs_1_), channel_id=1, source_target_pairs={{0,1},{1,0},{2,3},{3,2},{4,5},{5,4},{6,7},{7,6},{8,9},{9,8},{10,11... | collective-permute-start | bytes 344072 | tf_op jit(solution)/shard_map/ppermute | solution.py:26
  52.5 1.4 %collective-permute-start.27 = (bf16[8,7168]{1,0:T(8,128)(2,1)S(1)}, bf16[8,7168]{1,0:T(8,128)(2,1)S(1)}, u32[]{:S(2)}, u32[]{:S(2)}) collective-permute-start(bf16[8,7168]{1,0:T(8,128)(2,1)S(1)} %get-tuple-element.62), channel_id=1, source_target_pairs={{0,1},{1,0},{2,3},{3,2},{4,5},{5,4},{6,7},{7,6},{8,9},{9,8},{10,11... | collective-permute-start | bytes 344072 | tf_op jit(solution)/shard_map/ppermute | solution.py:26
  52.7 2.5 %collective-permute-start.29 = (bf16[8,7168]{1,0:T(8,128)(2,1)S(1)}, bf16[8,7168]{1,0:T(8,128)(2,1)S(1)}, u32[]{:S(2)}, u32[]{:S(2)}) collective-permute-start(bf16[8,7168]{1,0:T(8,128)(2,1)S(1)} %get-tuple-element.64), channel_id=1, source_target_pairs={{0,1},{1,0},{2,3},{3,2},{4,5},{5,4},{6,7},{7,6},{8,9},{9,8},{10,11... | collective-permute-start | bytes 344072 | tf_op jit(solution)/shard_map/ppermute | solution.py:26
  53.0 3.7 %collective-permute-start.31 = (bf16[8,7168]{1,0:T(8,128)(2,1)S(1)}, bf16[8,7168]{1,0:T(8,128)(2,1)S(1)}, u32[]{:S(2)}, u32[]{:S(2)}) collective-permute-start(bf16[8,7168]{1,0:T(8,128)(2,1)S(1)} %get-tuple-element.66), channel_id=1, source_target_pairs={{0,1},{1,0},{2,3},{3,2},{4,5},{5,4},{6,7},{7,6},{8,9},{9,8},{10,11... | collective-permute-start | bytes 344072 | tf_op jit(solution)/shard_map/ppermute | solution.py:26
  53.2 5.6 %collective-permute-start.26 = (bf16[8,7168]{1,0:T(8,128)(2,1)S(1)}, bf16[8,7168]{1,0:T(8,128)(2,1)S(1)}, u32[]{:S(2)}, u32[]{:S(2)}) collective-permute-start(bf16[8,7168]{1,0:T(8,128)(2,1)S(1)} %get-tuple-element.60), channel_id=1, source_target_pairs={{0,1},{1,0},{2,3},{3,2},{4,5},{5,4},{6,7},{7,6},{8,9},{9,8},{10,11... | collective-permute-start | bytes 344072 | tf_op jit(solution)/shard_map/ppermute | solution.py:26
  53.9 7.0 %collective-permute-start.28 = (bf16[8,7168]{1,0:T(8,128)(2,1)S(1)}, bf16[8,7168]{1,0:T(8,128)(2,1)S(1)}, u32[]{:S(2)}, u32[]{:S(2)}) collective-permute-start(bf16[8,7168]{1,0:T(8,128)(2,1)S(1)} %shard_map.84), channel_id=1, source_target_pairs={{0,6},{1,7},{2,4},{3,5},{4,2},{5,3},{6,0},{7,1},{8,14},{9,15},{10,... | collective-permute-start | bytes 344072 | tf_op jit(solution)/shard_map/ppermute | solution.py:26
  55.2 7.3 %collective-permute-start.30 = (bf16[8,7168]{1,0:T(8,128)(2,1)S(1)}, bf16[8,7168]{1,0:T(8,128)(2,1)S(1)}, u32[]{:S(2)}, u32[]{:S(2)}) collective-permute-start(bf16[8,7168]{1,0:T(8,128)(2,1)S(1)} %shard_map.85), channel_id=1, source_target_pairs={{0,4},{1,5},{2,6},{3,7},{4,0},{5,1},{6,2},{7,3},{8,12},{9,13},{10,... | collective-permute-start | bytes 344072 | tf_op jit(solution)/shard_map/ppermute | solution.py:26
  56.8 5.7 %collective-permute-start.32 = (bf16[8,7168]{1,0:T(8,128)(2,1)S(1)}, bf16[8,7168]{1,0:T(8,128)(2,1)S(1)}, u32[]{:S(2)}, u32[]{:S(2)}) collective-permute-start(bf16[8,7168]{1,0:T(8,128)(2,1)S(1)} %shard_map.86), channel_id=1, source_target_pairs={{0,2},{1,3},{2,0},{3,1},{4,6},{5,7},{6,4},{7,5},{8,10},{9,11},{10,... | collective-permute-start | bytes 344072 | tf_op jit(solution)/shard_map/ppermute | solution.py:26
  57.6 8.2 %collective-permute-start.18 = (bf16[4,7168]{1,0:T(4,128)(2,1)S(1)}, bf16[4,7168]{1,0:T(4,128)(2,1)S(1)}, u32[]{:S(2)}, u32[]{:S(2)}) collective-permute-start(bf16[4,7168]{1,0:T(4,128)(2,1)S(1)} %get-tuple-element.56), channel_id=1, source_target_pairs={{0,16},{1,17},{2,18},{3,19},{4,20},{5,21},{6,22},{7,23},{8,24},{9,... | collective-permute-start | bytes 172040 | tf_op jit(solution)/shard_map/ppermute | solution.py:26
  62.6 7.3 %collective-permute-start.33 = (bf16[4,7168]{1,0:T(4,128)(2,1)S(1)}, bf16[4,7168]{1,0:T(4,128)(2,1)S(1)}, u32[]{:S(2)}, u32[]{:S(2)}) collective-permute-start(bf16[4,7168]{1,0:T(4,128)(2,1)S(1)} %get-tuple-element.67), channel_id=1, source_target_pairs={{0,24},{1,25},{2,26},{3,27},{4,28},{5,29},{6,30},{7,31},{8,16},{9,... | collective-permute-start | bytes 172040 | tf_op jit(solution)/shard_map/ppermute | solution.py:26
  64.2 5.6 %collective-permute-start.34 = (bf16[4,7168]{1,0:T(4,128)(2,1)S(1)}, bf16[4,7168]{1,0:T(4,128)(2,1)S(1)}, u32[]{:S(2)}, u32[]{:S(2)}) collective-permute-start(bf16[4,7168]{1,0:T(4,128)(2,1)S(1)} %get-tuple-element.68), channel_id=1, source_target_pairs={{0,16},{1,17},{2,18},{3,19},{4,20},{5,21},{6,22},{7,23},{8,24},{9,... | collective-permute-start | bytes 172040 | tf_op jit(solution)/shard_map/ppermute | solution.py:26

commit v20 on v16

--- a/solution.py
+++ b/solution.py
@@ -79,11 +79,9 @@
     copies = [pltpu.make_async_copy(source, target, sems.at[place]) for place, (source, target) in enumerate(pairs)]
     for copy in copies:
         copy.start()
-    for copy in copies:
-        copy.wait()
     rows, dim = states_ref.shape[1:]
-    for span in spans(dim):
-        out_ref[:, span] = states_ref[0, :, span]
+    copies[0].wait()
+    copies[1].wait()
     lane = lax.broadcasted_iota(jnp.int32, (rows, LANES), 1).astype(jnp.float32)
     diagonal = lax.broadcasted_iota(jnp.int32, (rows, rows), 0) == lax.broadcasted_iota(jnp.int32, (rows, rows), 1)
 
@@ -96,6 +94,9 @@
             column = upright(routing_ref[0, step, k:k + 1, :]) + step * experts
             total += jnp.where(lane == column, upright(weight_ref[0, step, k:k + 1, :]), 0.0)
     out_ref[:, dim:] = total.astype(jnp.bfloat16)
+    copies[2].wait()
+    for span in spans(dim):
+        out_ref[:, span] = states_ref[0, :, span]
 
 
 def prepare(experts, states, routing, weight):
@@ -236,13 +237,13 @@
     passes_count = routing.shape[1]
     top, *middle = upper_flips(owners)
 
-    gate, up = load(gate_proj, up_proj)
+    (gate,) = load(gate_proj)
     block = prepare(owners // GROUP, states, routing, route_weight)
     other = exchange(block, top, 0)
-    other, gate, up = lax.optimization_barrier((other, gate, up))
+    other, gate = lax.optimization_barrier((other, gate))
     pair, raw = call(first_kernel, [(2 * row_dev, dim + LANES), (2 * row_dev, dim)], block, other, norm_gain)
-    pair, down_hbm = lax.optimization_barrier((pair, down_proj))
-    (down,) = load(down_hbm)
+    pair, up_hbm, down_hbm = lax.optimization_barrier((pair, up_proj, down_proj))
+    up, down = load(up_hbm, down_hbm)
     own, tail = states[0], None
     for step_no in range(passes_count):
         rows_a = pair
@@ -251,7 +252,7 @@
         mine = [rows_a] + [exchange(rows_a, flips, 0) for flips in SQUARE]
         near = rows_a
         if step_no == 0:
-            near, down = lax.optimization_barrier((near, down))
+            near, up, down = lax.optimization_barrier((near, up, down))
         fars = [exchange(rows, CORE, 0) for rows in [near] + mine[1:]]
         outs, tail = mlp(step_no, mine + fars, tail, gate, up, down)
 

time: 69.7 us -> 69.2 us (level)
  waiting for transfers between devices: 26.7 us -> 24.8 us
  starting transfers between devices: 30.8 us -> 32.3 us
    ppermute x35, waiting for transfers between devices: 26.7 us -> 24.8 us  [exchange(): return lax.ppermute(value, ('segment', 'expert'), pairs)]
    ppermute x35, starting transfers between devices: 30.8 us -> 32.3 us  [exchange(): return lax.ppermute(value, ('segment', 'expert'), pairs)]
  transfers between devices with their start and end apart: 35 -> 35, of which waited for: 23 -> 21; matrix products, arithmetic and copies ran while one was open for 0% -> 0% of each run, Pallas kernels for 8% -> 8%
where the time goes in v20:
time: 69.2 us; the launch traced here: 69 us
  starting transfers between devices  32.3 us (47%)
  waiting for transfers between devices  24.8 us (36%)
  Pallas kernels  11.7 us (17%)
    ppermute x35, starting transfers between devices, exchange(): return lax.ppermute(value, ('segment', 'expert'), pairs)  32.3 us
    ppermute x35, waiting for transfers between devices, exchange(): return lax.ppermute(value, ('segment', 'expert'), pairs)  24.8 us
    pallas_call x14, Pallas kernels, call(): pl.pallas_call(kernel, out_shape=[jax.ShapeDtypeStruct(shape, jnp.bfloat1...  6.52 us
    pallas_call x2, Pallas kernels, load(): pl.pallas_call(functools.partial(load_kernel, count), out_shape=[pltpu.VM...  5.22 us
  transfers between devices with their start and end apart: 35, of which 21 were waited for; matrix products, arithmetic and copies ran while one was open for 0% of the time, Pallas kernels for 8%

profile of v20, /device:TPU:0, one launch (start us, length us, event | category | flops | bytes accessed | tf_op | source)
XLA Modules:
  0.0 69.0 jit_solution(3162966866141094452)
XLA Ops:
  0.0 0.9 %shard_map.73.own_ref = bf16[4,7296]{1,0:T(4,128)(2,1)S(1)} custom-call(bf16[1,4,7168]{2,1,0:T(4,128)(2,1)} %states_hbm.1, s32[1,2,2,4]{3,2,1,0:T(2,128)} %bitcast.3, bf16[1,2,2,4]{3,2,1,0:T(2,128)(2,1)} %bitcast.4), custom_call_target="tpu_custom_call" | custom-call | tf_op jit(solution)/shard_map/pallas_call | solution.py:43
  0.9 0.0 copy-start
  0.9 4.1 %collective-permute-start = (bf16[4,7296]{1,0:T(4,128)(2,1)S(1)}, bf16[4,7296]{1,0:T(4,128)(2,1)S(1)}, u32[]{:S(2)}, u32[]{:S(2)}) collective-permute-start(bf16[4,7296]{1,0:T(4,128)(2,1)S(1)} %shard_map.73.own_ref), channel_id=1, source_target_pairs={{0,8},{1,9},{2,10},{3,11},{4,12},{5,13},{6,14},{7,15},{8,0},{9,1},... | collective-permute-start | bytes 175112 | tf_op jit(solution)/shard_map/ppermute | solution.py:26
  5.0 2.0 %shard_map.74.refs_8_.refs_9_ = bf16[1,7168,256]{2,1,0:T(8,128)(2,1)S(1)} custom-call(bf16[1,7168,256]{2,1,0:T(8,128)(2,1)} %refs_0_.1), custom_call_target="tpu_custom_call" | custom-call | bytes 3670016 | tf_op jit(solution)/shard_map/pallas_call | solution.py:64
  7.1 0.7 %collective-permute-done.far_ref = bf16[4,7296]{1,0:T(4,128)(2,1)S(1)} collective-permute-done((bf16[4,7296]{1,0:T(4,128)(2,1)S(1)}, bf16[4,7296]{1,0:T(4,128)(2,1)S(1)}, u32[]{:S(2)}, u32[]{:S(2)}) %collective-permute-start) | collective-permute-done | bytes 58400 | tf_op jit(solution)/shard_map/ppermute | solution.py:26
  7.8 0.2 shard_map.75
  8.0 2.4 %collective-permute-start.4 = (bf16[8,7296]{1,0:T(8,128)(2,1)S(1)}, bf16[8,7296]{1,0:T(8,128)(2,1)S(1)}, u32[]{:S(2)}, u32[]{:S(2)}) collective-permute-start(bf16[8,7296]{1,0:T(8,128)(2,1)S(1)} %get-tuple-element.46.refs_0_), channel_id=1, source_target_pairs={{0,6},{1,7},{2,4},{3,5},{4,2},{5,3},{6,0},{7,1},{8,14},{9,15},{10,... | collective-permute-start | bytes 350216 | tf_op jit(solution)/shard_map/ppermute | solution.py:26
  10.4 1.5 %collective-permute-start.3 = (bf16[8,7296]{1,0:T(8,128)(2,1)S(1)}, bf16[8,7296]{1,0:T(8,128)(2,1)S(1)}, u32[]{:S(2)}, u32[]{:S(2)}) collective-permute-start(bf16[8,7296]{1,0:T(8,128)(2,1)S(1)} %get-tuple-element.46.refs_0_), channel_id=1, source_target_pairs={{0,4},{1,5},{2,6},{3,7},{4,0},{5,1},{6,2},{7,3},{8,12},{9,13},{10,... | collective-permute-start | bytes 350216 | tf_op jit(solution)/shard_map/ppermute | solution.py:26
  11.9 3.2 %shard_map.76 = (bf16[1,7168,256]{2,1,0:T(8,128)(2,1)S(1)}, bf16[1,256,7168]{2,1,0:T(8,128)(2,1)S(1)}) custom-call(bf16[1,7168,256]{2,1,0:T(8,128)(2,1)} %refs_0_.2, bf16[1,256,7168]{2,1,0:T(8,128)(2,1)} %refs_1_), custom_call_target="tpu_custom_call" | custom-call | bytes 7340032 | tf_op jit(solution)/shard_map/pallas_call | solution.py:64
  15.1 0.1 collective-permute-start.5
  15.1 0.0 collective-permute-done.4.refs_3_
  15.2 0.5 collective-permute-start.8
  15.6 0.3 collective-permute-done.3.refs_2_
  15.9 0.0 collective-permute-start.7
  15.9 0.8 %collective-permute-done.2.refs_1_ = bf16[8,7296]{1,0:T(8,128)(2,1)S(1)} collective-permute-done((bf16[8,7296]{1,0:T(8,128)(2,1)S(1)}, bf16[8,7296]{1,0:T(8,128)(2,1)S(1)}, u32[]{:S(2)}, u32[]{:S(2)}) %collective-permute-start.2) | collective-permute-done | bytes 116768 | tf_op jit(solution)/shard_map/ppermute | solution.py:26
  16.7 0.5 collective-permute-done.7.refs_6_
  17.2 0.8 %collective-permute-done.6.refs_5_ = bf16[8,7296]{1,0:T(8,128)(2,1)S(1)} collective-permute-done((bf16[8,7296]{1,0:T(8,128)(2,1)S(1)}, bf16[8,7296]{1,0:T(8,128)(2,1)S(1)}, u32[]{:S(2)}, u32[]{:S(2)}) %collective-permute-start.6) | collective-permute-done | bytes 116768 | tf_op jit(solution)/shard_map/ppermute | solution.py:26
  18.0 2.1 %shard_map.77 = (bf16[8,7168]{1,0:T(8,128)(2,1)S(1)}, bf16[8,7168]{1,0:T(8,128)(2,1)S(1)}, bf16[8,7168]{1,0:T(8,128)(2,1)S(1)}, bf16[8,7168]{1,0:T(8,128)(2,1)S(...) custom-call(bf16[8,7296]{1,0:T(8,128)(2,1)S(1)} %get-tuple-element.4, ...), custom_call_target="tpu_custom_call" | custom-call | flops 704643072 | bytes 11010048 | tf_op jit(solution)/shard_map/pallas_call | solution.py:43
  20.1 0.2 collective-permute-start.10
  20.4 0.4 collective-permute-start.12
  20.7 0.1 collective-permute-start.14
  20.9 0.4 collective-permute-start.9
  21.2 0.3 collective-permute-done.10.refs_1_
  21.6 1.3 %collective-permute-start.11 = (bf16[8,7168]{1,0:T(8,128)(2,1)S(1)}, bf16[8,7168]{1,0:T(8,128)(2,1)S(1)}, u32[]{:S(2)}, u32[]{:S(2)}) collective-permute-start(bf16[8,7168]{1,0:T(8,128)(2,1)S(1)} %shard_map.78), channel_id=1, source_target_pairs={{0,6},{1,7},{2,4},{3,5},{4,2},{5,3},{6,0},{7,1},{8,14},{9,15},{10,... | collective-permute-start | bytes 344072 | tf_op jit(solution)/shard_map/ppermute | solution.py:26
  22.9 0.0 collective-permute-done.12.refs_1_
  22.9 1.4 %collective-permute-start.13 = (bf16[8,7168]{1,0:T(8,128)(2,1)S(1)}, bf16[8,7168]{1,0:T(8,128)(2,1)S(1)}, u32[]{:S(2)}, u32[]{:S(2)}) collective-permute-start(bf16[8,7168]{1,0:T(8,128)(2,1)S(1)} %shard_map.79), channel_id=1, source_target_pairs={{0,4},{1,5},{2,6},{3,7},{4,0},{5,1},{6,2},{7,3},{8,12},{9,13},{10,... | collective-permute-start | bytes 344072 | tf_op jit(solution)/shard_map/ppermute | solution.py:26
  24.4 1.0 %collective-permute-start.15 = (bf16[8,7168]{1,0:T(8,128)(2,1)S(1)}, bf16[8,7168]{1,0:T(8,128)(2,1)S(1)}, u32[]{:S(2)}, u32[]{:S(2)}) collective-permute-start(bf16[8,7168]{1,0:T(8,128)(2,1)S(1)} %shard_map.80), channel_id=1, source_target_pairs={{0,2},{1,3},{2,0},{3,1},{4,6},{5,7},{6,4},{7,5},{8,10},{9,11},{10,... | collective-permute-start | bytes 344072 | tf_op jit(solution)/shard_map/ppermute | solution.py:26
  25.3 1.5 %collective-permute-start.1 = (bf16[8,7168]{1,0:T(8,128)(2,1)S(1)}, bf16[8,7168]{1,0:T(8,128)(2,1)S(1)}, u32[]{:S(2)}, u32[]{:S(2)}) collective-permute-start(bf16[8,7168]{1,0:T(8,128)(2,1)S(1)} %get-tuple-element.39), channel_id=1, source_target_pairs={{0,16},{1,17},{2,18},{3,19},{4,20},{5,21},{6,22},{7,23},{8,24},{9,... | collective-permute-start | bytes 344072 | tf_op jit(solution)/shard_map/ppermute | solution.py:26
  26.8 1.7 %collective-permute-done.11.refs_2_ = bf16[8,7168]{1,0:T(8,128)(2,1)S(1)} collective-permute-done((bf16[8,7168]{1,0:T(8,128)(2,1)S(1)}, bf16[8,7168]{1,0:T(8,128)(2,1)S(1)}, u32[]{:S(2)}, u32[]{:S(2)}) %collective-permute-start.11) | collective-permute-done | bytes 114720 | tf_op jit(solution)/shard_map/ppermute | solution.py:26
  28.5 1.5 %collective-permute-done.13.refs_3_ = bf16[8,7168]{1,0:T(8,128)(2,1)S(1)} collective-permute-done((bf16[8,7168]{1,0:T(8,128)(2,1)S(1)}, bf16[8,7168]{1,0:T(8,128)(2,1)S(1)}, u32[]{:S(2)}, u32[]{:S(2)}) %collective-permute-start.13) | collective-permute-done | bytes 114720 | tf_op jit(solution)/shard_map/ppermute | solution.py:26
  30.1 0.1 collective-permute-done.15.refs_4_
  30.2 0.1 shard_map.81
  30.3 3.4 %collective-permute-start.17 = (bf16[8,7168]{1,0:T(8,128)(2,1)S(1)}, bf16[8,7168]{1,0:T(8,128)(2,1)S(1)}, u32[]{:S(2)}, u32[]{:S(2)}) collective-permute-start(bf16[8,7168]{1,0:T(8,128)(2,1)S(1)} %shard_map.81), channel_id=1, source_target_pairs={{0,24},{1,25},{2,26},{3,27},{4,28},{5,29},{6,30},{7,31},{8,16},{9,... | collective-permute-start | bytes 344072 | tf_op jit(solution)/shard_map/ppermute | solution.py:26
  33.7 0.5 collective-permute-start.16
  34.2 5.3 %collective-permute-done.17.far_ref = bf16[8,7168]{1,0:T(8,128)(2,1)S(1)} collective-permute-done((bf16[8,7168]{1,0:T(8,128)(2,1)S(1)}, bf16[8,7168]{1,0:T(8,128)(2,1)S(1)}, u32[]{:S(2)}, u32[]{:S(2)}) %collective-permute-start.17) | collective-permute-done | bytes 114720 | tf_op jit(solution)/shard_map/ppermute | solution.py:26
  39.5 0.6 collective-permute-done.16.near_ref
  40.1 0.2 shard_map.82
  40.3 1.4 %collective-permute-start.21 = (bf16[8,7168]{1,0:T(8,128)(2,1)S(1)}, bf16[8,7168]{1,0:T(8,128)(2,1)S(1)}, u32[]{:S(2)}, u32[]{:S(2)}) collective-permute-start(bf16[8,7168]{1,0:T(8,128)(2,1)S(1)} %get-tuple-element.59.refs_0_), channel_id=1, source_target_pairs={{0,6},{1,7},{2,4},{3,5},{4,2},{5,3},{6,0},{7,1},{8,14},{9,15},{10,... | collective-permute-start | bytes 344072 | tf_op jit(solution)/shard_map/ppermute | solution.py:26
  41.7 1.1 %collective-permute-start.20 = (bf16[8,7168]{1,0:T(8,128)(2,1)S(1)}, bf16[8,7168]{1,0:T(8,128)(2,1)S(1)}, u32[]{:S(2)}, u32[]{:S(2)}) collective-permute-start(bf16[8,7168]{1,0:T(8,128)(2,1)S(1)} %get-tuple-element.59.refs_0_), channel_id=1, source_target_pairs={{0,4},{1,5},{2,6},{3,7},{4,0},{5,1},{6,2},{7,3},{8,12},{9,13},{10,... | collective-permute-start | bytes 344072 | tf_op jit(solution)/shard_map/ppermute | solution.py:26
  42.8 1.1 %collective-permute-start.19 = (bf16[8,7168]{1,0:T(8,128)(2,1)S(1)}, bf16[8,7168]{1,0:T(8,128)(2,1)S(1)}, u32[]{:S(2)}, u32[]{:S(2)}) collective-permute-start(bf16[8,7168]{1,0:T(8,128)(2,1)S(1)} %get-tuple-element.59.refs_0_), channel_id=1, source_target_pairs={{0,2},{1,3},{2,0},{3,1},{4,6},{5,7},{6,4},{7,5},{8,10},{9,11},{10,... | collective-permute-start | bytes 344072 | tf_op jit(solution)/shard_map/ppermute | solution.py:26
  43.9 2.5 %collective-permute-done.21.refs_3_ = bf16[8,7168]{1,0:T(8,128)(2,1)S(1)} collective-permute-done((bf16[8,7168]{1,0:T(8,128)(2,1)S(1)}, bf16[8,7168]{1,0:T(8,128)(2,1)S(1)}, u32[]{:S(2)}, u32[]{:S(2)}) %collective-permute-start.21) | collective-permute-done | bytes 114720 | tf_op jit(solution)/shard_map/ppermute | solution.py:26
  46.4 1.4 %collective-permute-done.20.refs_2_ = bf16[8,7168]{1,0:T(8,128)(2,1)S(1)} collective-permute-done((bf16[8,7168]{1,0:T(8,128)(2,1)S(1)}, bf16[8,7168]{1,0:T(8,128)(2,1)S(1)}, u32[]{:S(2)}, u32[]{:S(2)}) %collective-permute-start.20) | collective-permute-done | bytes 114720 | tf_op jit(solution)/shard_map/ppermute | solution.py:26
  47.8 0.2 collective-permute-done.19.refs_1_
  48.0 0.3 collective-permute-start.23
  48.3 0.8 %collective-permute-done.24.refs_6_ = bf16[8,7168]{1,0:T(8,128)(2,1)S(1)} collective-permute-done((bf16[8,7168]{1,0:T(8,128)(2,1)S(1)}, bf16[8,7168]{1,0:T(8,128)(2,1)S(1)}, u32[]{:S(2)}, u32[]{:S(2)}) %collective-permute-start.24) | collective-permute-done | bytes 114720 | tf_op jit(solution)/shard_map/ppermute | solution.py:26
  49.1 0.2 collective-permute-done.23.refs_5_
  49.3 2.1 %shard_map.83 = (bf16[8,7168]{1,0:T(8,128)(2,1)S(1)}, bf16[8,7168]{1,0:T(8,128)(2,1)S(1)}, bf16[8,7168]{1,0:T(8,128)(2,1)S(1)}, bf16[8,7168]{1,0:T(8,128)(2,1)S(...) custom-call(bf16[8,7168]{1,0:T(8,128)(2,1)S(1)} %get-tuple-element.5, ...), custom_call_target="tpu_custom_call" | custom-call | flops 704643072 | bytes 11010048 | tf_op jit(solution)/shard_map/pallas_call | solution.py:43
  51.5 0.3 collective-permute-start.27
  51.8 0.2 collective-permute-start.29
  52.0 0.3 collective-permute-start.31
  52.3 0.2 collective-permute-start.26
  52.5 0.3 collective-permute-done.27.refs_1_
  52.9 1.8 %collective-permute-start.28 = (bf16[8,7168]{1,0:T(8,128)(2,1)S(1)}, bf16[8,7168]{1,0:T(8,128)(2,1)S(1)}, u32[]{:S(2)}, u32[]{:S(2)}) collective-permute-start(bf16[8,7168]{1,0:T(8,128)(2,1)S(1)} %shard_map.84), channel_id=1, source_target_pairs={{0,6},{1,7},{2,4},{3,5},{4,2},{5,3},{6,0},{7,1},{8,14},{9,15},{10,... | collective-permute-start | bytes 344072 | tf_op jit(solution)/shard_map/ppermute | solution.py:26
  54.7 1.0 %collective-permute-start.30 = (bf16[8,7168]{1,0:T(8,128)(2,1)S(1)}, bf16[8,7168]{1,0:T(8,128)(2,1)S(1)}, u32[]{:S(2)}, u32[]{:S(2)}) collective-permute-start(bf16[8,7168]{1,0:T(8,128)(2,1)S(1)} %shard_map.85), channel_id=1, source_target_pairs={{0,4},{1,5},{2,6},{3,7},{4,0},{5,1},{6,2},{7,3},{8,12},{9,13},{10,... | collective-permute-start | bytes 344072 | tf_op jit(solution)/shard_map/ppermute | solution.py:26
  55.8 0.9 %collective-permute-start.32 = (bf16[8,7168]{1,0:T(8,128)(2,1)S(1)}, bf16[8,7168]{1,0:T(8,128)(2,1)S(1)}, u32[]{:S(2)}, u32[]{:S(2)}) collective-permute-start(bf16[8,7168]{1,0:T(8,128)(2,1)S(1)} %shard_map.86), channel_id=1, source_target_pairs={{0,2},{1,3},{2,0},{3,1},{4,6},{5,7},{6,4},{7,5},{8,10},{9,11},{10,... | collective-permute-start | bytes 344072 | tf_op jit(solution)/shard_map/ppermute | solution.py:26
  56.6 1.7 %collective-permute-start.18 = (bf16[4,7168]{1,0:T(4,128)(2,1)S(1)}, bf16[4,7168]{1,0:T(4,128)(2,1)S(1)}, u32[]{:S(2)}, u32[]{:S(2)}) collective-permute-start(bf16[4,7168]{1,0:T(4,128)(2,1)S(1)} %get-tuple-element.58), channel_id=1, source_target_pairs={{0,16},{1,17},{2,18},{3,19},{4,20},{5,21},{6,22},{7,23},{8,24},{9,... | collective-permute-start | bytes 172040 | tf_op jit(solution)/shard_map/ppermute | solution.py:26
  58.4 1.4 %collective-permute-done.28.refs_2_ = bf16[8,7168]{1,0:T(8,128)(2,1)S(1)} collective-permute-done((bf16[8,7168]{1,0:T(8,128)(2,1)S(1)}, bf16[8,7168]{1,0:T(8,128)(2,1)S(1)}, u32[]{:S(2)}, u32[]{:S(2)}) %collective-permute-start.28) | collective-permute-done | bytes 114720 | tf_op jit(solution)/shard_map/ppermute | solution.py:26
  59.8 1.4 %collective-permute-done.30.refs_3_ = bf16[8,7168]{1,0:T(8,128)(2,1)S(1)} collective-permute-done((bf16[8,7168]{1,0:T(8,128)(2,1)S(1)}, bf16[8,7168]{1,0:T(8,128)(2,1)S(1)}, u32[]{:S(2)}, u32[]{:S(2)}) %collective-permute-start.30) | collective-permute-done | bytes 114720 | tf_op jit(solution)/shard_map/ppermute | solution.py:26
  61.3 0.4 collective-permute-done.32.refs_4_
  61.6 0.1 shard_map.87
  61.7 2.4 %collective-permute-start.33 = (bf16[4,7168]{1,0:T(4,128)(2,1)S(1)}, bf16[4,7168]{1,0:T(4,128)(2,1)S(1)}, u32[]{:S(2)}, u32[]{:S(2)}) collective-permute-start(bf16[4,7168]{1,0:T(4,128)(2,1)S(1)} %get-tuple-element.69), channel_id=1, source_target_pairs={{0,24},{1,25},{2,26},{3,27},{4,28},{5,29},{6,30},{7,31},{8,16},{9,... | collective-permute-start | bytes 172040 | tf_op jit(solution)/shard_map/ppermute | solution.py:26
  64.1 0.9 %collective-permute-start.34 = (bf16[4,7168]{1,0:T(4,128)(2,1)S(1)}, bf16[4,7168]{1,0:T(4,128)(2,1)S(1)}, u32[]{:S(2)}, u32[]{:S(2)}) collective-permute-start(bf16[4,7168]{1,0:T(4,128)(2,1)S(1)} %get-tuple-element.70), channel_id=1, source_target_pairs={{0,16},{1,17},{2,18},{3,19},{4,20},{5,21},{6,22},{7,23},{8,24},{9,... | collective-permute-start | bytes 172040 | tf_op jit(solution)/shard_map/ppermute | solution.py:26
  65.0 3.4 %collective-permute-done.33.refs_1_ = bf16[4,7168]{1,0:T(4,128)(2,1)S(1)} collective-permute-done((bf16[4,7168]{1,0:T(4,128)(2,1)S(1)}, bf16[4,7168]{1,0:T(4,128)(2,1)S(1)}, u32[]{:S(2)}, u32[]{:S(2)}) %collective-permute-start.33) | collective-permute-done | bytes 57376 | tf_op jit(solution)/shard_map/ppermute | solution.py:26
  68.4 0.7 shard_map.88
  (24 shorter events, 0.2 us)
Async XLA Ops:
  0.9 6.9 %copy-start = (f32[1,7168]{1,0:T(1,128)S(1)}, f32[1,7168]{1,0:T(1,128)}, u32[]{:S(2)}) copy-start(f32[1,7168]{1,0:T(1,128)} %gain_ref.3) | copy-start | bytes 86020
  0.9 6.9 %collective-permute-start = (bf16[4,7296]{1,0:T(4,128)(2,1)S(1)}, bf16[4,7296]{1,0:T(4,128)(2,1)S(1)}, u32[]{:S(2)}, u32[]{:S(2)}) collective-permute-start(bf16[4,7296]{1,0:T(4,128)(2,1)S(1)} %shard_map.73.own_ref), channel_id=1, source_target_pairs={{0,8},{1,9},{2,10},{3,11},{4,12},{5,13},{6,14},{7,15},{8,0},{9,1},... | collective-permute-start | bytes 175112 | tf_op jit(solution)/shard_map/ppermute | solution.py:26
  8.0 7.1 %collective-permute-start.4 = (bf16[8,7296]{1,0:T(8,128)(2,1)S(1)}, bf16[8,7296]{1,0:T(8,128)(2,1)S(1)}, u32[]{:S(2)}, u32[]{:S(2)}) collective-permute-start(bf16[8,7296]{1,0:T(8,128)(2,1)S(1)} %get-tuple-element.46.refs_0_), channel_id=1, source_target_pairs={{0,6},{1,7},{2,4},{3,5},{4,2},{5,3},{6,0},{7,1},{8,14},{9,15},{10,... | collective-permute-start | bytes 350216 | tf_op jit(solution)/shard_map/ppermute | solution.py:26
  10.4 5.5 %collective-permute-start.3 = (bf16[8,7296]{1,0:T(8,128)(2,1)S(1)}, bf16[8,7296]{1,0:T(8,128)(2,1)S(1)}, u32[]{:S(2)}, u32[]{:S(2)}) collective-permute-start(bf16[8,7296]{1,0:T(8,128)(2,1)S(1)} %get-tuple-element.46.refs_0_), channel_id=1, source_target_pairs={{0,4},{1,5},{2,6},{3,7},{4,0},{5,1},{6,2},{7,3},{8,12},{9,13},{10,... | collective-permute-start | bytes 350216 | tf_op jit(solution)/shard_map/ppermute | solution.py:26
  11.9 4.8 %collective-permute-start.2 = (bf16[8,7296]{1,0:T(8,128)(2,1)S(1)}, bf16[8,7296]{1,0:T(8,128)(2,1)S(1)}, u32[]{:S(2)}, u32[]{:S(2)}) collective-permute-start(bf16[8,7296]{1,0:T(8,128)(2,1)S(1)} %get-tuple-element.46.refs_0_), channel_id=1, source_target_pairs={{0,2},{1,3},{2,0},{3,1},{4,6},{5,7},{6,4},{7,5},{8,10},{9,11},{10,... | collective-permute-start | bytes 350216 | tf_op jit(solution)/shard_map/ppermute | solution.py:26
  15.1 1.6 %collective-permute-start.5 = (bf16[8,7296]{1,0:T(8,128)(2,1)S(1)}, bf16[8,7296]{1,0:T(8,128)(2,1)S(1)}, u32[]{:S(2)}, u32[]{:S(2)}) collective-permute-start(bf16[8,7296]{1,0:T(8,128)(2,1)S(1)} %get-tuple-element.46.refs_0_), channel_id=1, source_target_pairs={{0,1},{1,0},{2,3},{3,2},{4,5},{5,4},{6,7},{7,6},{8,9},{9,8},{10,11... | collective-permute-start | bytes 350216 | tf_op jit(solution)/shard_map/ppermute | solution.py:26
  15.2 1.5 %collective-permute-start.8 = (bf16[8,7296]{1,0:T(8,128)(2,1)S(1)}, bf16[8,7296]{1,0:T(8,128)(2,1)S(1)}, u32[]{:S(2)}, u32[]{:S(2)}) collective-permute-start(bf16[8,7296]{1,0:T(8,128)(2,1)S(1)} %collective-permute-done.4.refs_3_), channel_id=1, source_target_pairs={{0,1},{1,0},{2,3},{3,2},{4,5},{5,4},{6,7},{7,6},{8,9},{9,8},{10,11... | collective-permute-start | bytes 350216 | tf_op jit(solution)/shard_map/ppermute | solution.py:26
  15.9 1.3 %collective-permute-start.7 = (bf16[8,7296]{1,0:T(8,128)(2,1)S(1)}, bf16[8,7296]{1,0:T(8,128)(2,1)S(1)}, u32[]{:S(2)}, u32[]{:S(2)}) collective-permute-start(bf16[8,7296]{1,0:T(8,128)(2,1)S(1)} %collective-permute-done.3.refs_2_), channel_id=1, source_target_pairs={{0,1},{1,0},{2,3},{3,2},{4,5},{5,4},{6,7},{7,6},{8,9},{9,8},{10,11... | collective-permute-start | bytes 350216 | tf_op jit(solution)/shard_map/ppermute | solution.py:26
  16.7 1.3 %collective-permute-start.6 = (bf16[8,7296]{1,0:T(8,128)(2,1)S(1)}, bf16[8,7296]{1,0:T(8,128)(2,1)S(1)}, u32[]{:S(2)}, u32[]{:S(2)}) collective-permute-start(bf16[8,7296]{1,0:T(8,128)(2,1)S(1)} %collective-permute-done.2.refs_1_), channel_id=1, source_target_pairs={{0,1},{1,0},{2,3},{3,2},{4,5},{5,4},{6,7},{7,6},{8,9},{9,8},{10,11... | collective-permute-start | bytes 350216 | tf_op jit(solution)/shard_map/ppermute | solution.py:26
  20.1 1.4 %collective-permute-start.10 = (bf16[8,7168]{1,0:T(8,128)(2,1)S(1)}, bf16[8,7168]{1,0:T(8,128)(2,1)S(1)}, u32[]{:S(2)}, u32[]{:S(2)}) collective-permute-start(bf16[8,7168]{1,0:T(8,128)(2,1)S(1)} %get-tuple-element.53), channel_id=1, source_target_pairs={{0,1},{1,0},{2,3},{3,2},{4,5},{5,4},{6,7},{7,6},{8,9},{9,8},{10,11... | collective-permute-start | bytes 344072 | tf_op jit(solution)/shard_map/ppermute | solution.py:26
  20.4 2.5 %collective-permute-start.12 = (bf16[8,7168]{1,0:T(8,128)(2,1)S(1)}, bf16[8,7168]{1,0:T(8,128)(2,1)S(1)}, u32[]{:S(2)}, u32[]{:S(2)}) collective-permute-start(bf16[8,7168]{1,0:T(8,128)(2,1)S(1)} %get-tuple-element.55), channel_id=1, source_target_pairs={{0,1},{1,0},{2,3},{3,2},{4,5},{5,4},{6,7},{7,6},{8,9},{9,8},{10,11... | collective-permute-start | bytes 344072 | tf_op jit(solution)/shard_map/ppermute | solution.py:26
  20.7 3.6 %collective-permute-start.14 = (bf16[8,7168]{1,0:T(8,128)(2,1)S(1)}, bf16[8,7168]{1,0:T(8,128)(2,1)S(1)}, u32[]{:S(2)}, u32[]{:S(2)}) collective-permute-start(bf16[8,7168]{1,0:T(8,128)(2,1)S(1)} %get-tuple-element.57), channel_id=1, source_target_pairs={{0,1},{1,0},{2,3},{3,2},{4,5},{5,4},{6,7},{7,6},{8,9},{9,8},{10,11... | collective-permute-start | bytes 344072 | tf_op jit(solution)/shard_map/ppermute | solution.py:26
  20.9 5.9 %collective-permute-start.9 = (bf16[8,7168]{1,0:T(8,128)(2,1)S(1)}, bf16[8,7168]{1,0:T(8,128)(2,1)S(1)}, u32[]{:S(2)}, u32[]{:S(2)}) collective-permute-start(bf16[8,7168]{1,0:T(8,128)(2,1)S(1)} %get-tuple-element.51), channel_id=1, source_target_pairs={{0,1},{1,0},{2,3},{3,2},{4,5},{5,4},{6,7},{7,6},{8,9},{9,8},{10,11... | collective-permute-start | bytes 344072 | tf_op jit(solution)/shard_map/ppermute | solution.py:26
  21.6 7.0 %collective-permute-start.11 = (bf16[8,7168]{1,0:T(8,128)(2,1)S(1)}, bf16[8,7168]{1,0:T(8,128)(2,1)S(1)}, u32[]{:S(2)}, u32[]{:S(2)}) collective-permute-start(bf16[8,7168]{1,0:T(8,128)(2,1)S(1)} %shard_map.78), channel_id=1, source_target_pairs={{0,6},{1,7},{2,4},{3,5},{4,2},{5,3},{6,0},{7,1},{8,14},{9,15},{10,... | collective-permute-start | bytes 344072 | tf_op jit(solution)/shard_map/ppermute | solution.py:26
  22.9 7.2 %collective-permute-start.13 = (bf16[8,7168]{1,0:T(8,128)(2,1)S(1)}, bf16[8,7168]{1,0:T(8,128)(2,1)S(1)}, u32[]{:S(2)}, u32[]{:S(2)}) collective-permute-start(bf16[8,7168]{1,0:T(8,128)(2,1)S(1)} %shard_map.79), channel_id=1, source_target_pairs={{0,4},{1,5},{2,6},{3,7},{4,0},{5,1},{6,2},{7,3},{8,12},{9,13},{10,... | collective-permute-start | bytes 344072 | tf_op jit(solution)/shard_map/ppermute | solution.py:26
  24.4 5.8 %collective-permute-start.15 = (bf16[8,7168]{1,0:T(8,128)(2,1)S(1)}, bf16[8,7168]{1,0:T(8,128)(2,1)S(1)}, u32[]{:S(2)}, u32[]{:S(2)}) collective-permute-start(bf16[8,7168]{1,0:T(8,128)(2,1)S(1)} %shard_map.80), channel_id=1, source_target_pairs={{0,2},{1,3},{2,0},{3,1},{4,6},{5,7},{6,4},{7,5},{8,10},{9,11},{10,... | collective-permute-start | bytes 344072 | tf_op jit(solution)/shard_map/ppermute | solution.py:26
  25.3 8.9 %collective-permute-start.1 = (bf16[8,7168]{1,0:T(8,128)(2,1)S(1)}, bf16[8,7168]{1,0:T(8,128)(2,1)S(1)}, u32[]{:S(2)}, u32[]{:S(2)}) collective-permute-start(bf16[8,7168]{1,0:T(8,128)(2,1)S(1)} %get-tuple-element.39), channel_id=1, source_target_pairs={{0,16},{1,17},{2,18},{3,19},{4,20},{5,21},{6,22},{7,23},{8,24},{9,... | collective-permute-start | bytes 344072 | tf_op jit(solution)/shard_map/ppermute | solution.py:26
  30.3 9.2 %collective-permute-start.17 = (bf16[8,7168]{1,0:T(8,128)(2,1)S(1)}, bf16[8,7168]{1,0:T(8,128)(2,1)S(1)}, u32[]{:S(2)}, u32[]{:S(2)}) collective-permute-start(bf16[8,7168]{1,0:T(8,128)(2,1)S(1)} %shard_map.81), channel_id=1, source_target_pairs={{0,24},{1,25},{2,26},{3,27},{4,28},{5,29},{6,30},{7,31},{8,16},{9,... | collective-permute-start | bytes 344072 | tf_op jit(solution)/shard_map/ppermute | solution.py:26
  33.7 6.4 %collective-permute-start.16 = (bf16[8,7168]{1,0:T(8,128)(2,1)S(1)}, bf16[8,7168]{1,0:T(8,128)(2,1)S(1)}, u32[]{:S(2)}, u32[]{:S(2)}) collective-permute-start(bf16[8,7168]{1,0:T(8,128)(2,1)S(1)} %shard_map.81), channel_id=1, source_target_pairs={{0,16},{1,17},{2,18},{3,19},{4,20},{5,21},{6,22},{7,23},{8,24},{9,... | collective-permute-start | bytes 344072 | tf_op jit(solution)/shard_map/ppermute | solution.py:26
  40.3 6.1 %collective-permute-start.21 = (bf16[8,7168]{1,0:T(8,128)(2,1)S(1)}, bf16[8,7168]{1,0:T(8,128)(2,1)S(1)}, u32[]{:S(2)}, u32[]{:S(2)}) collective-permute-start(bf16[8,7168]{1,0:T(8,128)(2,1)S(1)} %get-tuple-element.59.refs_0_), channel_id=1, source_target_pairs={{0,6},{1,7},{2,4},{3,5},{4,2},{5,3},{6,0},{7,1},{8,14},{9,15},{10,... | collective-permute-start | bytes 344072 | tf_op jit(solution)/shard_map/ppermute | solution.py:26
  41.7 6.1 %collective-permute-start.20 = (bf16[8,7168]{1,0:T(8,128)(2,1)S(1)}, bf16[8,7168]{1,0:T(8,128)(2,1)S(1)}, u32[]{:S(2)}, u32[]{:S(2)}) collective-permute-start(bf16[8,7168]{1,0:T(8,128)(2,1)S(1)} %get-tuple-element.59.refs_0_), channel_id=1, source_target_pairs={{0,4},{1,5},{2,6},{3,7},{4,0},{5,1},{6,2},{7,3},{8,12},{9,13},{10,... | collective-permute-start | bytes 344072 | tf_op jit(solution)/shard_map/ppermute | solution.py:26
  42.8 5.2 %collective-permute-start.19 = (bf16[8,7168]{1,0:T(8,128)(2,1)S(1)}, bf16[8,7168]{1,0:T(8,128)(2,1)S(1)}, u32[]{:S(2)}, u32[]{:S(2)}) collective-permute-start(bf16[8,7168]{1,0:T(8,128)(2,1)S(1)} %get-tuple-element.59.refs_0_), channel_id=1, source_target_pairs={{0,2},{1,3},{2,0},{3,1},{4,6},{5,7},{6,4},{7,5},{8,10},{9,11},{10,... | collective-permute-start | bytes 344072 | tf_op jit(solution)/shard_map/ppermute | solution.py:26
  43.9 4.4 %collective-permute-start.22 = (bf16[8,7168]{1,0:T(8,128)(2,1)S(1)}, bf16[8,7168]{1,0:T(8,128)(2,1)S(1)}, u32[]{:S(2)}, u32[]{:S(2)}) collective-permute-start(bf16[8,7168]{1,0:T(8,128)(2,1)S(1)} %get-tuple-element.59.refs_0_), channel_id=1, source_target_pairs={{0,1},{1,0},{2,3},{3,2},{4,5},{5,4},{6,7},{7,6},{8,9},{9,8},{10,11... | collective-permute-start | bytes 344072 | tf_op jit(solution)/shard_map/ppermute | solution.py:26
  46.4 1.9 %collective-permute-start.25 = (bf16[8,7168]{1,0:T(8,128)(2,1)S(1)}, bf16[8,7168]{1,0:T(8,128)(2,1)S(1)}, u32[]{:S(2)}, u32[]{:S(2)}) collective-permute-start(bf16[8,7168]{1,0:T(8,128)(2,1)S(1)} %collective-permute-done.21.refs_3_), channel_id=1, source_target_pairs={{0,1},{1,0},{2,3},{3,2},{4,5},{5,4},{6,7},{7,6},{8,9},{9,8},{10,11... | collective-permute-start | bytes 344072 | tf_op jit(solution)/shard_map/ppermute | solution.py:26
  47.8 1.3 %collective-permute-start.24 = (bf16[8,7168]{1,0:T(8,128)(2,1)S(1)}, bf16[8,7168]{1,0:T(8,128)(2,1)S(1)}, u32[]{:S(2)}, u32[]{:S(2)}) collective-permute-start(bf16[8,7168]{1,0:T(8,128)(2,1)S(1)} %collective-permute-done.20.refs_2_), channel_id=1, source_target_pairs={{0,1},{1,0},{2,3},{3,2},{4,5},{5,4},{6,7},{7,6},{8,9},{9,8},{10,11... | collective-permute-start | bytes 344072 | tf_op jit(solution)/shard_map/ppermute | solution.py:26
  48.0 1.3 %collective-permute-start.23 = (bf16[8,7168]{1,0:T(8,128)(2,1)S(1)}, bf16[8,7168]{1,0:T(8,128)(2,1)S(1)}, u32[]{:S(2)}, u32[]{:S(2)}) collective-permute-start(bf16[8,7168]{1,0:T(8,128)(2,1)S(1)} %collective-permute-done.19.refs_1_), channel_id=1, source_target_pairs={{0,1},{1,0},{2,3},{3,2},{4,5},{5,4},{6,7},{7,6},{8,9},{9,8},{10,11... | collective-permute-start | bytes 344072 | tf_op jit(solution)/shard_map/ppermute | solution.py:26
  51.5 1.4 %collective-permute-start.27 = (bf16[8,7168]{1,0:T(8,128)(2,1)S(1)}, bf16[8,7168]{1,0:T(8,128)(2,1)S(1)}, u32[]{:S(2)}, u32[]{:S(2)}) collective-permute-start(bf16[8,7168]{1,0:T(8,128)(2,1)S(1)} %get-tuple-element.64), channel_id=1, source_target_pairs={{0,1},{1,0},{2,3},{3,2},{4,5},{5,4},{6,7},{7,6},{8,9},{9,8},{10,11... | collective-permute-start | bytes 344072 | tf_op jit(solution)/shard_map/ppermute | solution.py:26
  51.8 2.9 %collective-permute-start.29 = (bf16[8,7168]{1,0:T(8,128)(2,1)S(1)}, bf16[8,7168]{1,0:T(8,128)(2,1)S(1)}, u32[]{:S(2)}, u32[]{:S(2)}) collective-permute-start(bf16[8,7168]{1,0:T(8,128)(2,1)S(1)} %get-tuple-element.66), channel_id=1, source_target_pairs={{0,1},{1,0},{2,3},{3,2},{4,5},{5,4},{6,7},{7,6},{8,9},{9,8},{10,11... | collective-permute-start | bytes 344072 | tf_op jit(solution)/shard_map/ppermute | solution.py:26
  52.0 3.7 %collective-permute-start.31 = (bf16[8,7168]{1,0:T(8,128)(2,1)S(1)}, bf16[8,7168]{1,0:T(8,128)(2,1)S(1)}, u32[]{:S(2)}, u32[]{:S(2)}) collective-permute-start(bf16[8,7168]{1,0:T(8,128)(2,1)S(1)} %get-tuple-element.68), channel_id=1, source_target_pairs={{0,1},{1,0},{2,3},{3,2},{4,5},{5,4},{6,7},{7,6},{8,9},{9,8},{10,11... | collective-permute-start | bytes 344072 | tf_op jit(solution)/shard_map/ppermute | solution.py:26
  52.3 6.1 %collective-permute-start.26 = (bf16[8,7168]{1,0:T(8,128)(2,1)S(1)}, bf16[8,7168]{1,0:T(8,128)(2,1)S(1)}, u32[]{:S(2)}, u32[]{:S(2)}) collective-permute-start(bf16[8,7168]{1,0:T(8,128)(2,1)S(1)} %get-tuple-element.62), channel_id=1, source_target_pairs={{0,1},{1,0},{2,3},{3,2},{4,5},{5,4},{6,7},{7,6},{8,9},{9,8},{10,11... | collective-permute-start | bytes 344072 | tf_op jit(solution)/shard_map/ppermute | solution.py:26
  52.9 6.9 %collective-permute-start.28 = (bf16[8,7168]{1,0:T(8,128)(2,1)S(1)}, bf16[8,7168]{1,0:T(8,128)(2,1)S(1)}, u32[]{:S(2)}, u32[]{:S(2)}) collective-permute-start(bf16[8,7168]{1,0:T(8,128)(2,1)S(1)} %shard_map.84), channel_id=1, source_target_pairs={{0,6},{1,7},{2,4},{3,5},{4,2},{5,3},{6,0},{7,1},{8,14},{9,15},{10,... | collective-permute-start | bytes 344072 | tf_op jit(solution)/shard_map/ppermute | solution.py:26
  54.7 6.6 %collective-permute-start.30 = (bf16[8,7168]{1,0:T(8,128)(2,1)S(1)}, bf16[8,7168]{1,0:T(8,128)(2,1)S(1)}, u32[]{:S(2)}, u32[]{:S(2)}) collective-permute-start(bf16[8,7168]{1,0:T(8,128)(2,1)S(1)} %shard_map.85), channel_id=1, source_target_pairs={{0,4},{1,5},{2,6},{3,7},{4,0},{5,1},{6,2},{7,3},{8,12},{9,13},{10,... | collective-permute-start | bytes 344072 | tf_op jit(solution)/shard_map/ppermute | solution.py:26
  55.8 5.9 %collective-permute-start.32 = (bf16[8,7168]{1,0:T(8,128)(2,1)S(1)}, bf16[8,7168]{1,0:T(8,128)(2,1)S(1)}, u32[]{:S(2)}, u32[]{:S(2)}) collective-permute-start(bf16[8,7168]{1,0:T(8,128)(2,1)S(1)} %shard_map.86), channel_id=1, source_target_pairs={{0,2},{1,3},{2,0},{3,1},{4,6},{5,7},{6,4},{7,5},{8,10},{9,11},{10,... | collective-permute-start | bytes 344072 | tf_op jit(solution)/shard_map/ppermute | solution.py:26
  56.6 8.3 %collective-permute-start.18 = (bf16[4,7168]{1,0:T(4,128)(2,1)S(1)}, bf16[4,7168]{1,0:T(4,128)(2,1)S(1)}, u32[]{:S(2)}, u32[]{:S(2)}) collective-permute-start(bf16[4,7168]{1,0:T(4,128)(2,1)S(1)} %get-tuple-element.58), channel_id=1, source_target_pairs={{0,16},{1,17},{2,18},{3,19},{4,20},{5,21},{6,22},{7,23},{8,24},{9,... | collective-permute-start | bytes 172040 | tf_op jit(solution)/shard_map/ppermute | solution.py:26
  61.7 6.7 %collective-permute-start.33 = (bf16[4,7168]{1,0:T(4,128)(2,1)S(1)}, bf16[4,7168]{1,0:T(4,128)(2,1)S(1)}, u32[]{:S(2)}, u32[]{:S(2)}) collective-permute-start(bf16[4,7168]{1,0:T(4,128)(2,1)S(1)} %get-tuple-element.69), channel_id=1, source_target_pairs={{0,24},{1,25},{2,26},{3,27},{4,28},{5,29},{6,30},{7,31},{8,16},{9,... | collective-permute-start | bytes 172040 | tf_op jit(solution)/shard_map/ppermute | solution.py:26
  64.1 4.3 %collective-permute-start.34 = (bf16[4,7168]{1,0:T(4,128)(2,1)S(1)}, bf16[4,7168]{1,0:T(4,128)(2,1)S(1)}, u32[]{:S(2)}, u32[]{:S(2)}) collective-permute-start(bf16[4,7168]{1,0:T(4,128)(2,1)S(1)} %get-tuple-element.70), channel_id=1, source_target_pairs={{0,16},{1,17},{2,18},{3,19},{4,20},{5,21},{6,22},{7,23},{8,24},{9,... | collective-permute-start | bytes 172040 | tf_op jit(solution)/shard_map/ppermute | solution.py:26

commit v21 on v20

--- a/solution.py
+++ b/solution.py
@@ -124,6 +124,24 @@
         out_ref[:, span] = sum(part[:, span].astype(jnp.float32) for part in parts).astype(jnp.bfloat16)
 
 
+def total_kernel(own_ref, *refs):
+    *parts, out_ref = refs
+    half = own_ref.shape[0]
+    for span in spans(out_ref.shape[1]):
+        total = sum(part[:, span].astype(jnp.float32) for part in parts)
+        own = own_ref[:, span].astype(jnp.float32)
+        out_ref[:, span] = jnp.concatenate([total[:half] + own, total[half:]], axis=0).astype(jnp.bfloat16)
+
+
+def last_kernel(own_ref, *refs):
+    *parts, low_ref, high_ref = refs
+    half = own_ref.shape[0]
+    for span in spans(low_ref.shape[1]):
+        total = sum(part[:, span].astype(jnp.float32) for part in parts)
+        low_ref[:, span] = (total[:half] + own_ref[:, span].astype(jnp.float32)).astype(jnp.bfloat16)
+        high_ref[:, span] = total[half:].astype(jnp.bfloat16)
+
+
 def split_kernel(count, *refs):
     parts, outs = refs[:-count], refs[-count:]
     rows = outs[0].shape[0]
@@ -155,12 +173,12 @@
     normalise(raw_ref, gain_ref, out_ref)
 
 
-def meet_kernel(rest_ref, near_ref, far_ref, gain_ref, out_ref, own_ref, raw_ref):
+def meet_kernel(near_ref, far_ref, gain_ref, out_ref, own_ref, raw_ref):
     half = own_ref.shape[0]
     for span in spans(out_ref.shape[1]):
         far = far_ref[:, span].astype(jnp.float32)
-        total = rest_ref[:, span].astype(jnp.float32) + near_ref[:, span].astype(jnp.float32)
-        total = (total + jnp.concatenate([far[half:], far[:half]], axis=0)).astype(jnp.bfloat16)
+        total = near_ref[:, span].astype(jnp.float32) + jnp.concatenate([far[half:], far[:half]], axis=0)
+        total = total.astype(jnp.bfloat16)
         raw_ref[:, span] = total
         own_ref[:, span] = total[:half]
     normalise(raw_ref, gain_ref, out_ref)
@@ -241,7 +259,10 @@
     block = prepare(owners // GROUP, states, routing, route_weight)
     other = exchange(block, top, 0)
     other, gate = lax.optimization_barrier((other, gate))
-    pair, raw = call(first_kernel, [(2 * row_dev, dim + LANES), (2 * row_dev, dim)], block, other, norm_gain)
+    pair_rows = pltpu.VMEM((2 * row_dev, dim), jnp.bfloat16)
+    (pair,) = call(
+        first_kernel, [(2 * row_dev, dim + LANES)], block, other, norm_gain, scratch_shapes=[pair_rows]
+    )
     pair, up_hbm, down_hbm = lax.optimization_barrier((pair, up_proj, down_proj))
     up, down = load(up_hbm, down_hbm)
     own, tail = states[0], None
@@ -264,19 +285,14 @@
             low, high = split(*parts)
             parts = [low, exchange(high, flips, 0)]
         if step_no < passes_count - 1:
-            total = add(*parts)
-            rest = exchange(raw, STAY, 1)
-            more = step_no < passes_count - 2
-            pair, own, *raws = call(
-                meet_kernel, [(2 * row_dev, dim), (row_dev, dim)] + [(2 * row_dev, dim)] * more,
-                rest, exchange(total, STAY, 1), exchange(total, top, 1), norm_gain,
-                scratch_shapes=[] if more else [pltpu.VMEM((2 * row_dev, dim), jnp.bfloat16)],
+            (total,) = call(total_kernel, [(2 * row_dev, dim)], own, *parts)
+            pair, own = call(
+                meet_kernel, [(2 * row_dev, dim), (row_dev, dim)],
+                exchange(total, STAY, 1), exchange(total, top, 1), norm_gain, scratch_shapes=[pair_rows],
             )
-            raw = raws[0] if more else None
         else:
-            low, high = split(*parts)
-            rest = exchange(own, STAY, 1)
-            own = add(rest, exchange(high, top, 1), exchange(low, STAY, 1))
+            low, high = call(last_kernel, [(row_dev, dim)] * 2, own, *parts)
+            own = add(exchange(high, top, 1), exchange(low, STAY, 1))
     return own[None]
 
 

time: 69.2 us -> 69.3 us (level)
  waiting for transfers between devices: 24.8 us -> 28.1 us
  starting transfers between devices: 32.3 us -> 29.1 us
    ppermute x35 -> x33, waiting for transfers between devices: 24.8 us -> 28.1 us  [exchange(): return lax.ppermute(value, ('segment', 'expert'), pairs)]
    ppermute x35 -> x33, starting transfers between devices: 32.3 us -> 29.1 us  [exchange(): return lax.ppermute(value, ('segment', 'expert'), pairs)]
  transfers between devices with their start and end apart: 35 -> 33, of which waited for: 21 -> 21; matrix products, arithmetic and copies ran while one was open for 0% -> 0% of each run, Pallas kernels for 8% -> 8%
where the time goes in v21:
time: 69.3 us; the launch traced here: 69.1 us
  starting transfers between devices  29.1 us (42%)
  waiting for transfers between devices  28.1 us (41%)
  Pallas kernels  11.7 us (17%)
    ppermute x33, starting transfers between devices, exchange(): return lax.ppermute(value, ('segment', 'expert'), pairs)  29.1 us
    ppermute x33, waiting for transfers between devices, exchange(): return lax.ppermute(value, ('segment', 'expert'), pairs)  28.1 us
    pallas_call x14, Pallas kernels, call(): pl.pallas_call(kernel, out_shape=[jax.ShapeDtypeStruct(shape, jnp.bfloat1...  6.52 us
    pallas_call x2, Pallas kernels, load(): pl.pallas_call(functools.partial(load_kernel, count), out_shape=[pltpu.VM...  5.22 us
  transfers between devices with their start and end apart: 33, of which 21 were waited for; matrix products, arithmetic and copies ran while one was open for 0% of the time, Pallas kernels for 8%

profile of v21, /device:TPU:0, one launch (start us, length us, event | category | flops | bytes accessed | tf_op | source)
XLA Modules:
  0.0 69.1 jit_solution(17852138484619607575)
XLA Ops:
  0.0 0.9 %shard_map.73.own_ref = bf16[4,7296]{1,0:T(4,128)(2,1)S(1)} custom-call(bf16[1,4,7168]{2,1,0:T(4,128)(2,1)} %states_hbm.1, s32[1,2,2,4]{3,2,1,0:T(2,128)} %bitcast.5, bf16[1,2,2,4]{3,2,1,0:T(2,128)(2,1)} %bitcast.6), custom_call_target="tpu_custom_call" | custom-call | tf_op jit(solution)/shard_map/pallas_call | solution.py:43
  0.9 0.0 copy-start.1
  0.9 4.1 %collective-permute-start = (bf16[4,7296]{1,0:T(4,128)(2,1)S(1)}, bf16[4,7296]{1,0:T(4,128)(2,1)S(1)}, u32[]{:S(2)}, u32[]{:S(2)}) collective-permute-start(bf16[4,7296]{1,0:T(4,128)(2,1)S(1)} %shard_map.73.own_ref), channel_id=1, source_target_pairs={{0,8},{1,9},{2,10},{3,11},{4,12},{5,13},{6,14},{7,15},{8,0},{9,1},... | collective-permute-start | bytes 175112 | tf_op jit(solution)/shard_map/ppermute | solution.py:26
  5.0 2.0 %shard_map.74.refs_8_.refs_9_ = bf16[1,7168,256]{2,1,0:T(8,128)(2,1)S(1)} custom-call(bf16[1,7168,256]{2,1,0:T(8,128)(2,1)} %refs_0_.1), custom_call_target="tpu_custom_call" | custom-call | bytes 3670016 | tf_op jit(solution)/shard_map/pallas_call | solution.py:64
  7.1 0.7 %collective-permute-done.far_ref = bf16[4,7296]{1,0:T(4,128)(2,1)S(1)} collective-permute-done((bf16[4,7296]{1,0:T(4,128)(2,1)S(1)}, bf16[4,7296]{1,0:T(4,128)(2,1)S(1)}, u32[]{:S(2)}, u32[]{:S(2)}) %collective-permute-start) | collective-permute-done | bytes 58400 | tf_op jit(solution)/shard_map/ppermute | solution.py:26
  7.8 0.2 shard_map.75.refs_0_
  8.0 2.4 %collective-permute-start.3 = (bf16[8,7296]{1,0:T(8,128)(2,1)S(1)}, bf16[8,7296]{1,0:T(8,128)(2,1)S(1)}, u32[]{:S(2)}, u32[]{:S(2)}) collective-permute-start(bf16[8,7296]{1,0:T(8,128)(2,1)S(1)} %shard_map.75.refs_0_), channel_id=1, source_target_pairs={{0,6},{1,7},{2,4},{3,5},{4,2},{5,3},{6,0},{7,1},{8,14},{9,15},{10,... | collective-permute-start | bytes 350216 | tf_op jit(solution)/shard_map/ppermute | solution.py:26
  10.4 1.5 %collective-permute-start.2 = (bf16[8,7296]{1,0:T(8,128)(2,1)S(1)}, bf16[8,7296]{1,0:T(8,128)(2,1)S(1)}, u32[]{:S(2)}, u32[]{:S(2)}) collective-permute-start(bf16[8,7296]{1,0:T(8,128)(2,1)S(1)} %shard_map.75.refs_0_), channel_id=1, source_target_pairs={{0,4},{1,5},{2,6},{3,7},{4,0},{5,1},{6,2},{7,3},{8,12},{9,13},{10,... | collective-permute-start | bytes 350216 | tf_op jit(solution)/shard_map/ppermute | solution.py:26
  11.9 3.2 %shard_map.76 = (bf16[1,7168,256]{2,1,0:T(8,128)(2,1)S(1)}, bf16[1,256,7168]{2,1,0:T(8,128)(2,1)S(1)}) custom-call(bf16[1,7168,256]{2,1,0:T(8,128)(2,1)} %refs_0_.2, bf16[1,256,7168]{2,1,0:T(8,128)(2,1)} %refs_1_), custom_call_target="tpu_custom_call" | custom-call | bytes 7340032 | tf_op jit(solution)/shard_map/pallas_call | solution.py:64
  15.0 0.0 copy-start
  15.1 0.1 collective-permute-start.4
  15.1 0.0 collective-permute-done.3.refs_3_
  15.1 0.5 collective-permute-start.7
  15.6 0.3 collective-permute-done.2.refs_2_
  15.9 0.0 collective-permute-start.6
  15.9 0.8 %collective-permute-done.1.refs_1_ = bf16[8,7296]{1,0:T(8,128)(2,1)S(1)} collective-permute-done((bf16[8,7296]{1,0:T(8,128)(2,1)S(1)}, bf16[8,7296]{1,0:T(8,128)(2,1)S(1)}, u32[]{:S(2)}, u32[]{:S(2)}) %collective-permute-start.1) | collective-permute-done | bytes 116768 | tf_op jit(solution)/shard_map/ppermute | solution.py:26
  16.7 0.0 collective-permute-done.7.refs_7_
  16.7 0.5 collective-permute-done.6.refs_6_
  17.2 0.8 %collective-permute-done.5.refs_5_ = bf16[8,7296]{1,0:T(8,128)(2,1)S(1)} collective-permute-done((bf16[8,7296]{1,0:T(8,128)(2,1)S(1)}, bf16[8,7296]{1,0:T(8,128)(2,1)S(1)}, u32[]{:S(2)}, u32[]{:S(2)}) %collective-permute-start.5) | collective-permute-done | bytes 116768 | tf_op jit(solution)/shard_map/ppermute | solution.py:26
  18.0 2.1 %shard_map.77 = (bf16[8,7168]{1,0:T(8,128)(2,1)S(1)}, bf16[8,7168]{1,0:T(8,128)(2,1)S(1)}, bf16[8,7168]{1,0:T(8,128)(2,1)S(1)}, bf16[8,7168]{1,0:T(8,128)(2,1)S(...) custom-call(bf16[8,7296]{1,0:T(8,128)(2,1)S(1)} %shard_map.75.refs_0, ...), custom_call_target="tpu_custom_call" | custom-call | flops 704643072 | bytes 11010048 | tf_op jit(solution)/shard_map/pallas_call | solution.py:43
  20.1 0.2 collective-permute-start.9
  20.3 0.4 collective-permute-start.11
  20.7 0.1 collective-permute-start.13
  20.9 0.4 collective-permute-start.8
  21.2 0.3 collective-permute-done.9.refs_1_
  21.6 1.3 %collective-permute-start.10 = (bf16[8,7168]{1,0:T(8,128)(2,1)S(1)}, bf16[8,7168]{1,0:T(8,128)(2,1)S(1)}, u32[]{:S(2)}, u32[]{:S(2)}) collective-permute-start(bf16[8,7168]{1,0:T(8,128)(2,1)S(1)} %shard_map.78), channel_id=1, source_target_pairs={{0,6},{1,7},{2,4},{3,5},{4,2},{5,3},{6,0},{7,1},{8,14},{9,15},{10,... | collective-permute-start | bytes 344072 | tf_op jit(solution)/shard_map/ppermute | solution.py:26
  22.8 0.0 collective-permute-done.11.refs_1_
  22.9 1.4 %collective-permute-start.12 = (bf16[8,7168]{1,0:T(8,128)(2,1)S(1)}, bf16[8,7168]{1,0:T(8,128)(2,1)S(1)}, u32[]{:S(2)}, u32[]{:S(2)}) collective-permute-start(bf16[8,7168]{1,0:T(8,128)(2,1)S(1)} %shard_map.79), channel_id=1, source_target_pairs={{0,4},{1,5},{2,6},{3,7},{4,0},{5,1},{6,2},{7,3},{8,12},{9,13},{10,... | collective-permute-start | bytes 344072 | tf_op jit(solution)/shard_map/ppermute | solution.py:26
  24.4 0.9 %collective-permute-start.14 = (bf16[8,7168]{1,0:T(8,128)(2,1)S(1)}, bf16[8,7168]{1,0:T(8,128)(2,1)S(1)}, u32[]{:S(2)}, u32[]{:S(2)}) collective-permute-start(bf16[8,7168]{1,0:T(8,128)(2,1)S(1)} %shard_map.80), channel_id=1, source_target_pairs={{0,2},{1,3},{2,0},{3,1},{4,6},{5,7},{6,4},{7,5},{8,10},{9,11},{10,... | collective-permute-start | bytes 344072 | tf_op jit(solution)/shard_map/ppermute | solution.py:26
  25.3 3.2 %collective-permute-done.10.refs_2_ = bf16[8,7168]{1,0:T(8,128)(2,1)S(1)} collective-permute-done((bf16[8,7168]{1,0:T(8,128)(2,1)S(1)}, bf16[8,7168]{1,0:T(8,128)(2,1)S(1)}, u32[]{:S(2)}, u32[]{:S(2)}) %collective-permute-start.10) | collective-permute-done | bytes 114720 | tf_op jit(solution)/shard_map/ppermute | solution.py:26
  28.5 1.6 %collective-permute-done.12.refs_3_ = bf16[8,7168]{1,0:T(8,128)(2,1)S(1)} collective-permute-done((bf16[8,7168]{1,0:T(8,128)(2,1)S(1)}, bf16[8,7168]{1,0:T(8,128)(2,1)S(1)}, u32[]{:S(2)}, u32[]{:S(2)}) %collective-permute-start.12) | collective-permute-done | bytes 114720 | tf_op jit(solution)/shard_map/ppermute | solution.py:26
  30.1 0.1 collective-permute-done.14.refs_4_
  30.2 0.1 shard_map.81
  30.3 3.4 %collective-permute-start.16 = (bf16[8,7168]{1,0:T(8,128)(2,1)S(1)}, bf16[8,7168]{1,0:T(8,128)(2,1)S(1)}, u32[]{:S(2)}, u32[]{:S(2)}) collective-permute-start(bf16[8,7168]{1,0:T(8,128)(2,1)S(1)} %shard_map.81), channel_id=1, source_target_pairs={{0,24},{1,25},{2,26},{3,27},{4,28},{5,29},{6,30},{7,31},{8,16},{9,... | collective-permute-start | bytes 344072 | tf_op jit(solution)/shard_map/ppermute | solution.py:26
  33.7 0.5 collective-permute-start.15
  34.2 5.3 %collective-permute-done.16.far_ref = bf16[8,7168]{1,0:T(8,128)(2,1)S(1)} collective-permute-done((bf16[8,7168]{1,0:T(8,128)(2,1)S(1)}, bf16[8,7168]{1,0:T(8,128)(2,1)S(1)}, u32[]{:S(2)}, u32[]{:S(2)}) %collective-permute-start.16) | collective-permute-done | bytes 114720 | tf_op jit(solution)/shard_map/ppermute | solution.py:26
  39.5 0.6 collective-permute-done.15.near_ref
  40.1 0.2 shard_map.82
  40.3 1.4 %collective-permute-start.19 = (bf16[8,7168]{1,0:T(8,128)(2,1)S(1)}, bf16[8,7168]{1,0:T(8,128)(2,1)S(1)}, u32[]{:S(2)}, u32[]{:S(2)}) collective-permute-start(bf16[8,7168]{1,0:T(8,128)(2,1)S(1)} %get-tuple-element.55.refs_0_), channel_id=1, source_target_pairs={{0,6},{1,7},{2,4},{3,5},{4,2},{5,3},{6,0},{7,1},{8,14},{9,15},{10,... | collective-permute-start | bytes 344072 | tf_op jit(solution)/shard_map/ppermute | solution.py:26
  41.7 1.1 %collective-permute-start.18 = (bf16[8,7168]{1,0:T(8,128)(2,1)S(1)}, bf16[8,7168]{1,0:T(8,128)(2,1)S(1)}, u32[]{:S(2)}, u32[]{:S(2)}) collective-permute-start(bf16[8,7168]{1,0:T(8,128)(2,1)S(1)} %get-tuple-element.55.refs_0_), channel_id=1, source_target_pairs={{0,4},{1,5},{2,6},{3,7},{4,0},{5,1},{6,2},{7,3},{8,12},{9,13},{10,... | collective-permute-start | bytes 344072 | tf_op jit(solution)/shard_map/ppermute | solution.py:26
  42.8 1.1 %collective-permute-start.17 = (bf16[8,7168]{1,0:T(8,128)(2,1)S(1)}, bf16[8,7168]{1,0:T(8,128)(2,1)S(1)}, u32[]{:S(2)}, u32[]{:S(2)}) collective-permute-start(bf16[8,7168]{1,0:T(8,128)(2,1)S(1)} %get-tuple-element.55.refs_0_), channel_id=1, source_target_pairs={{0,2},{1,3},{2,0},{3,1},{4,6},{5,7},{6,4},{7,5},{8,10},{9,11},{10,... | collective-permute-start | bytes 344072 | tf_op jit(solution)/shard_map/ppermute | solution.py:26
  43.9 2.5 %collective-permute-done.19.refs_3_ = bf16[8,7168]{1,0:T(8,128)(2,1)S(1)} collective-permute-done((bf16[8,7168]{1,0:T(8,128)(2,1)S(1)}, bf16[8,7168]{1,0:T(8,128)(2,1)S(1)}, u32[]{:S(2)}, u32[]{:S(2)}) %collective-permute-start.19) | collective-permute-done | bytes 114720 | tf_op jit(solution)/shard_map/ppermute | solution.py:26
  46.4 1.4 %collective-permute-done.18.refs_2_ = bf16[8,7168]{1,0:T(8,128)(2,1)S(1)} collective-permute-done((bf16[8,7168]{1,0:T(8,128)(2,1)S(1)}, bf16[8,7168]{1,0:T(8,128)(2,1)S(1)}, u32[]{:S(2)}, u32[]{:S(2)}) %collective-permute-start.18) | collective-permute-done | bytes 114720 | tf_op jit(solution)/shard_map/ppermute | solution.py:26
  47.8 0.2 collective-permute-done.17.refs_1_
  48.0 0.3 collective-permute-start.21
  48.3 0.8 %collective-permute-done.22.refs_6_ = bf16[8,7168]{1,0:T(8,128)(2,1)S(1)} collective-permute-done((bf16[8,7168]{1,0:T(8,128)(2,1)S(1)}, bf16[8,7168]{1,0:T(8,128)(2,1)S(1)}, u32[]{:S(2)}, u32[]{:S(2)}) %collective-permute-start.22) | collective-permute-done | bytes 114720 | tf_op jit(solution)/shard_map/ppermute | solution.py:26
  49.1 0.2 collective-permute-done.21.refs_5_
  49.4 2.1 %shard_map.83 = (bf16[8,7168]{1,0:T(8,128)(2,1)S(1)}, bf16[8,7168]{1,0:T(8,128)(2,1)S(1)}, bf16[8,7168]{1,0:T(8,128)(2,1)S(1)}, bf16[8,7168]{1,0:T(8,128)(2,1)S(...) custom-call(bf16[8,7168]{1,0:T(8,128)(2,1)S(1)} %get-tuple-element.5, ...), custom_call_target="tpu_custom_call" | custom-call | flops 704643072 | bytes 11010048 | tf_op jit(solution)/shard_map/pallas_call | solution.py:43
  51.5 0.3 collective-permute-start.25
  51.8 0.2 collective-permute-start.27
  52.1 0.3 collective-permute-start.29
  52.3 0.2 collective-permute-start.24
  52.6 0.3 collective-permute-done.25.refs_1_
  52.9 1.7 %collective-permute-start.26 = (bf16[8,7168]{1,0:T(8,128)(2,1)S(1)}, bf16[8,7168]{1,0:T(8,128)(2,1)S(1)}, u32[]{:S(2)}, u32[]{:S(2)}) collective-permute-start(bf16[8,7168]{1,0:T(8,128)(2,1)S(1)} %shard_map.84), channel_id=1, source_target_pairs={{0,6},{1,7},{2,4},{3,5},{4,2},{5,3},{6,0},{7,1},{8,14},{9,15},{10,... | collective-permute-start | bytes 344072 | tf_op jit(solution)/shard_map/ppermute | solution.py:26
  54.7 1.1 %collective-permute-start.28 = (bf16[8,7168]{1,0:T(8,128)(2,1)S(1)}, bf16[8,7168]{1,0:T(8,128)(2,1)S(1)}, u32[]{:S(2)}, u32[]{:S(2)}) collective-permute-start(bf16[8,7168]{1,0:T(8,128)(2,1)S(1)} %shard_map.85), channel_id=1, source_target_pairs={{0,4},{1,5},{2,6},{3,7},{4,0},{5,1},{6,2},{7,3},{8,12},{9,13},{10,... | collective-permute-start | bytes 344072 | tf_op jit(solution)/shard_map/ppermute | solution.py:26
  55.8 0.9 %collective-permute-start.30 = (bf16[8,7168]{1,0:T(8,128)(2,1)S(1)}, bf16[8,7168]{1,0:T(8,128)(2,1)S(1)}, u32[]{:S(2)}, u32[]{:S(2)}) collective-permute-start(bf16[8,7168]{1,0:T(8,128)(2,1)S(1)} %shard_map.86), channel_id=1, source_target_pairs={{0,2},{1,3},{2,0},{3,1},{4,6},{5,7},{6,4},{7,5},{8,10},{9,11},{10,... | collective-permute-start | bytes 344072 | tf_op jit(solution)/shard_map/ppermute | solution.py:26
  56.7 3.2 %collective-permute-done.26.refs_2_ = bf16[8,7168]{1,0:T(8,128)(2,1)S(1)} collective-permute-done((bf16[8,7168]{1,0:T(8,128)(2,1)S(1)}, bf16[8,7168]{1,0:T(8,128)(2,1)S(1)}, u32[]{:S(2)}, u32[]{:S(2)}) %collective-permute-start.26) | collective-permute-done | bytes 114720 | tf_op jit(solution)/shard_map/ppermute | solution.py:26
  59.8 1.4 %collective-permute-done.28.refs_3_ = bf16[8,7168]{1,0:T(8,128)(2,1)S(1)} collective-permute-done((bf16[8,7168]{1,0:T(8,128)(2,1)S(1)}, bf16[8,7168]{1,0:T(8,128)(2,1)S(1)}, u32[]{:S(2)}, u32[]{:S(2)}) %collective-permute-start.28) | collective-permute-done | bytes 114720 | tf_op jit(solution)/shard_map/ppermute | solution.py:26
  61.3 0.4 collective-permute-done.30.refs_4_
  61.7 0.1 shard_map.87
  61.8 2.4 %collective-permute-start.31 = (bf16[4,7168]{1,0:T(4,128)(2,1)S(1)}, bf16[4,7168]{1,0:T(4,128)(2,1)S(1)}, u32[]{:S(2)}, u32[]{:S(2)}) collective-permute-start(bf16[4,7168]{1,0:T(4,128)(2,1)S(1)} %get-tuple-element.65), channel_id=1, source_target_pairs={{0,24},{1,25},{2,26},{3,27},{4,28},{5,29},{6,30},{7,31},{8,16},{9,... | collective-permute-start | bytes 172040 | tf_op jit(solution)/shard_map/ppermute | solution.py:26
  64.1 0.9 %collective-permute-start.32 = (bf16[4,7168]{1,0:T(4,128)(2,1)S(1)}, bf16[4,7168]{1,0:T(4,128)(2,1)S(1)}, u32[]{:S(2)}, u32[]{:S(2)}) collective-permute-start(bf16[4,7168]{1,0:T(4,128)(2,1)S(1)} %get-tuple-element.66), channel_id=1, source_target_pairs={{0,16},{1,17},{2,18},{3,19},{4,20},{5,21},{6,22},{7,23},{8,24},{9,... | collective-permute-start | bytes 172040 | tf_op jit(solution)/shard_map/ppermute | solution.py:26
  65.0 3.4 %collective-permute-done.31.refs_0_ = bf16[4,7168]{1,0:T(4,128)(2,1)S(1)} collective-permute-done((bf16[4,7168]{1,0:T(4,128)(2,1)S(1)}, bf16[4,7168]{1,0:T(4,128)(2,1)S(1)}, u32[]{:S(2)}, u32[]{:S(2)}) %collective-permute-start.31) | collective-permute-done | bytes 57376 | tf_op jit(solution)/shard_map/ppermute | solution.py:26
  68.4 0.7 shard_map.88
  (22 shorter events, 0.2 us)
Async XLA Ops:
  0.9 6.9 %copy-start.1 = (f32[1,7168]{1,0:T(1,128)S(1)}, f32[1,7168]{1,0:T(1,128)}, u32[]{:S(2)}) copy-start(f32[1,7168]{1,0:T(1,128)} %gain_ref.3) | copy-start | bytes 86020
  0.9 6.9 %collective-permute-start = (bf16[4,7296]{1,0:T(4,128)(2,1)S(1)}, bf16[4,7296]{1,0:T(4,128)(2,1)S(1)}, u32[]{:S(2)}, u32[]{:S(2)}) collective-permute-start(bf16[4,7296]{1,0:T(4,128)(2,1)S(1)} %shard_map.73.own_ref), channel_id=1, source_target_pairs={{0,8},{1,9},{2,10},{3,11},{4,12},{5,13},{6,14},{7,15},{8,0},{9,1},... | collective-permute-start | bytes 175112 | tf_op jit(solution)/shard_map/ppermute | solution.py:26
  8.0 7.2 %collective-permute-start.3 = (bf16[8,7296]{1,0:T(8,128)(2,1)S(1)}, bf16[8,7296]{1,0:T(8,128)(2,1)S(1)}, u32[]{:S(2)}, u32[]{:S(2)}) collective-permute-start(bf16[8,7296]{1,0:T(8,128)(2,1)S(1)} %shard_map.75.refs_0_), channel_id=1, source_target_pairs={{0,6},{1,7},{2,4},{3,5},{4,2},{5,3},{6,0},{7,1},{8,14},{9,15},{10,... | collective-permute-start | bytes 350216 | tf_op jit(solution)/shard_map/ppermute | solution.py:26
  10.4 5.5 %collective-permute-start.2 = (bf16[8,7296]{1,0:T(8,128)(2,1)S(1)}, bf16[8,7296]{1,0:T(8,128)(2,1)S(1)}, u32[]{:S(2)}, u32[]{:S(2)}) collective-permute-start(bf16[8,7296]{1,0:T(8,128)(2,1)S(1)} %shard_map.75.refs_0_), channel_id=1, source_target_pairs={{0,4},{1,5},{2,6},{3,7},{4,0},{5,1},{6,2},{7,3},{8,12},{9,13},{10,... | collective-permute-start | bytes 350216 | tf_op jit(solution)/shard_map/ppermute | solution.py:26
  11.9 4.8 %collective-permute-start.1 = (bf16[8,7296]{1,0:T(8,128)(2,1)S(1)}, bf16[8,7296]{1,0:T(8,128)(2,1)S(1)}, u32[]{:S(2)}, u32[]{:S(2)}) collective-permute-start(bf16[8,7296]{1,0:T(8,128)(2,1)S(1)} %shard_map.75.refs_0_), channel_id=1, source_target_pairs={{0,2},{1,3},{2,0},{3,1},{4,6},{5,7},{6,4},{7,5},{8,10},{9,11},{10,... | collective-permute-start | bytes 350216 | tf_op jit(solution)/shard_map/ppermute | solution.py:26
  15.0 15.1 %copy-start = (bf16[1,4,7168]{2,1,0:T(4,128)(2,1)S(1)}, bf16[1,4,7168]{2,1,0:T(4,128)(2,1)}, u32[]{:S(2)}) copy-start(bf16[1,4,7168]{2,1,0:T(4,128)(2,1)} %states_hbm.1) | copy-start | bytes 172036
  15.1 1.6 %collective-permute-start.4 = (bf16[8,7296]{1,0:T(8,128)(2,1)S(1)}, bf16[8,7296]{1,0:T(8,128)(2,1)S(1)}, u32[]{:S(2)}, u32[]{:S(2)}) collective-permute-start(bf16[8,7296]{1,0:T(8,128)(2,1)S(1)} %shard_map.75.refs_0_), channel_id=1, source_target_pairs={{0,1},{1,0},{2,3},{3,2},{4,5},{5,4},{6,7},{7,6},{8,9},{9,8},{10,11... | collective-permute-start | bytes 350216 | tf_op jit(solution)/shard_map/ppermute | solution.py:26
  15.1 1.5 %collective-permute-start.7 = (bf16[8,7296]{1,0:T(8,128)(2,1)S(1)}, bf16[8,7296]{1,0:T(8,128)(2,1)S(1)}, u32[]{:S(2)}, u32[]{:S(2)}) collective-permute-start(bf16[8,7296]{1,0:T(8,128)(2,1)S(1)} %collective-permute-done.3.refs_3_), channel_id=1, source_target_pairs={{0,1},{1,0},{2,3},{3,2},{4,5},{5,4},{6,7},{7,6},{8,9},{9,8},{10,11... | collective-permute-start | bytes 350216 | tf_op jit(solution)/shard_map/ppermute | solution.py:26
  15.9 1.3 %collective-permute-start.6 = (bf16[8,7296]{1,0:T(8,128)(2,1)S(1)}, bf16[8,7296]{1,0:T(8,128)(2,1)S(1)}, u32[]{:S(2)}, u32[]{:S(2)}) collective-permute-start(bf16[8,7296]{1,0:T(8,128)(2,1)S(1)} %collective-permute-done.2.refs_2_), channel_id=1, source_target_pairs={{0,1},{1,0},{2,3},{3,2},{4,5},{5,4},{6,7},{7,6},{8,9},{9,8},{10,11... | collective-permute-start | bytes 350216 | tf_op jit(solution)/shard_map/ppermute | solution.py:26
  16.7 1.3 %collective-permute-start.5 = (bf16[8,7296]{1,0:T(8,128)(2,1)S(1)}, bf16[8,7296]{1,0:T(8,128)(2,1)S(1)}, u32[]{:S(2)}, u32[]{:S(2)}) collective-permute-start(bf16[8,7296]{1,0:T(8,128)(2,1)S(1)} %collective-permute-done.1.refs_1_), channel_id=1, source_target_pairs={{0,1},{1,0},{2,3},{3,2},{4,5},{5,4},{6,7},{7,6},{8,9},{9,8},{10,11... | collective-permute-start | bytes 350216 | tf_op jit(solution)/shard_map/ppermute | solution.py:26
  20.1 1.4 %collective-permute-start.9 = (bf16[8,7168]{1,0:T(8,128)(2,1)S(1)}, bf16[8,7168]{1,0:T(8,128)(2,1)S(1)}, u32[]{:S(2)}, u32[]{:S(2)}) collective-permute-start(bf16[8,7168]{1,0:T(8,128)(2,1)S(1)} %get-tuple-element.49), channel_id=1, source_target_pairs={{0,1},{1,0},{2,3},{3,2},{4,5},{5,4},{6,7},{7,6},{8,9},{9,8},{10,11... | collective-permute-start | bytes 344072 | tf_op jit(solution)/shard_map/ppermute | solution.py:26
  20.3 2.5 %collective-permute-start.11 = (bf16[8,7168]{1,0:T(8,128)(2,1)S(1)}, bf16[8,7168]{1,0:T(8,128)(2,1)S(1)}, u32[]{:S(2)}, u32[]{:S(2)}) collective-permute-start(bf16[8,7168]{1,0:T(8,128)(2,1)S(1)} %get-tuple-element.51), channel_id=1, source_target_pairs={{0,1},{1,0},{2,3},{3,2},{4,5},{5,4},{6,7},{7,6},{8,9},{9,8},{10,11... | collective-permute-start | bytes 344072 | tf_op jit(solution)/shard_map/ppermute | solution.py:26
  20.7 3.6 %collective-permute-start.13 = (bf16[8,7168]{1,0:T(8,128)(2,1)S(1)}, bf16[8,7168]{1,0:T(8,128)(2,1)S(1)}, u32[]{:S(2)}, u32[]{:S(2)}) collective-permute-start(bf16[8,7168]{1,0:T(8,128)(2,1)S(1)} %get-tuple-element.53), channel_id=1, source_target_pairs={{0,1},{1,0},{2,3},{3,2},{4,5},{5,4},{6,7},{7,6},{8,9},{9,8},{10,11... | collective-permute-start | bytes 344072 | tf_op jit(solution)/shard_map/ppermute | solution.py:26
  20.9 4.5 %collective-permute-start.8 = (bf16[8,7168]{1,0:T(8,128)(2,1)S(1)}, bf16[8,7168]{1,0:T(8,128)(2,1)S(1)}, u32[]{:S(2)}, u32[]{:S(2)}) collective-permute-start(bf16[8,7168]{1,0:T(8,128)(2,1)S(1)} %get-tuple-element.47), channel_id=1, source_target_pairs={{0,1},{1,0},{2,3},{3,2},{4,5},{5,4},{6,7},{7,6},{8,9},{9,8},{10,11... | collective-permute-start | bytes 344072 | tf_op jit(solution)/shard_map/ppermute | solution.py:26
  21.6 7.0 %collective-permute-start.10 = (bf16[8,7168]{1,0:T(8,128)(2,1)S(1)}, bf16[8,7168]{1,0:T(8,128)(2,1)S(1)}, u32[]{:S(2)}, u32[]{:S(2)}) collective-permute-start(bf16[8,7168]{1,0:T(8,128)(2,1)S(1)} %shard_map.78), channel_id=1, source_target_pairs={{0,6},{1,7},{2,4},{3,5},{4,2},{5,3},{6,0},{7,1},{8,14},{9,15},{10,... | collective-permute-start | bytes 344072 | tf_op jit(solution)/shard_map/ppermute | solution.py:26
  22.9 7.2 %collective-permute-start.12 = (bf16[8,7168]{1,0:T(8,128)(2,1)S(1)}, bf16[8,7168]{1,0:T(8,128)(2,1)S(1)}, u32[]{:S(2)}, u32[]{:S(2)}) collective-permute-start(bf16[8,7168]{1,0:T(8,128)(2,1)S(1)} %shard_map.79), channel_id=1, source_target_pairs={{0,4},{1,5},{2,6},{3,7},{4,0},{5,1},{6,2},{7,3},{8,12},{9,13},{10,... | collective-permute-start | bytes 344072 | tf_op jit(solution)/shard_map/ppermute | solution.py:26
  24.4 5.8 %collective-permute-start.14 = (bf16[8,7168]{1,0:T(8,128)(2,1)S(1)}, bf16[8,7168]{1,0:T(8,128)(2,1)S(1)}, u32[]{:S(2)}, u32[]{:S(2)}) collective-permute-start(bf16[8,7168]{1,0:T(8,128)(2,1)S(1)} %shard_map.80), channel_id=1, source_target_pairs={{0,2},{1,3},{2,0},{3,1},{4,6},{5,7},{6,4},{7,5},{8,10},{9,11},{10,... | collective-permute-start | bytes 344072 | tf_op jit(solution)/shard_map/ppermute | solution.py:26
  30.3 9.2 %collective-permute-start.16 = (bf16[8,7168]{1,0:T(8,128)(2,1)S(1)}, bf16[8,7168]{1,0:T(8,128)(2,1)S(1)}, u32[]{:S(2)}, u32[]{:S(2)}) collective-permute-start(bf16[8,7168]{1,0:T(8,128)(2,1)S(1)} %shard_map.81), channel_id=1, source_target_pairs={{0,24},{1,25},{2,26},{3,27},{4,28},{5,29},{6,30},{7,31},{8,16},{9,... | collective-permute-start | bytes 344072 | tf_op jit(solution)/shard_map/ppermute | solution.py:26
  33.7 6.4 %collective-permute-start.15 = (bf16[8,7168]{1,0:T(8,128)(2,1)S(1)}, bf16[8,7168]{1,0:T(8,128)(2,1)S(1)}, u32[]{:S(2)}, u32[]{:S(2)}) collective-permute-start(bf16[8,7168]{1,0:T(8,128)(2,1)S(1)} %shard_map.81), channel_id=1, source_target_pairs={{0,16},{1,17},{2,18},{3,19},{4,20},{5,21},{6,22},{7,23},{8,24},{9,... | collective-permute-start | bytes 344072 | tf_op jit(solution)/shard_map/ppermute | solution.py:26
  40.3 6.1 %collective-permute-start.19 = (bf16[8,7168]{1,0:T(8,128)(2,1)S(1)}, bf16[8,7168]{1,0:T(8,128)(2,1)S(1)}, u32[]{:S(2)}, u32[]{:S(2)}) collective-permute-start(bf16[8,7168]{1,0:T(8,128)(2,1)S(1)} %get-tuple-element.55.refs_0_), channel_id=1, source_target_pairs={{0,6},{1,7},{2,4},{3,5},{4,2},{5,3},{6,0},{7,1},{8,14},{9,15},{10,... | collective-permute-start | bytes 344072 | tf_op jit(solution)/shard_map/ppermute | solution.py:26
  41.7 6.1 %collective-permute-start.18 = (bf16[8,7168]{1,0:T(8,128)(2,1)S(1)}, bf16[8,7168]{1,0:T(8,128)(2,1)S(1)}, u32[]{:S(2)}, u32[]{:S(2)}) collective-permute-start(bf16[8,7168]{1,0:T(8,128)(2,1)S(1)} %get-tuple-element.55.refs_0_), channel_id=1, source_target_pairs={{0,4},{1,5},{2,6},{3,7},{4,0},{5,1},{6,2},{7,3},{8,12},{9,13},{10,... | collective-permute-start | bytes 344072 | tf_op jit(solution)/shard_map/ppermute | solution.py:26
  42.8 5.2 %collective-permute-start.17 = (bf16[8,7168]{1,0:T(8,128)(2,1)S(1)}, bf16[8,7168]{1,0:T(8,128)(2,1)S(1)}, u32[]{:S(2)}, u32[]{:S(2)}) collective-permute-start(bf16[8,7168]{1,0:T(8,128)(2,1)S(1)} %get-tuple-element.55.refs_0_), channel_id=1, source_target_pairs={{0,2},{1,3},{2,0},{3,1},{4,6},{5,7},{6,4},{7,5},{8,10},{9,11},{10,... | collective-permute-start | bytes 344072 | tf_op jit(solution)/shard_map/ppermute | solution.py:26
  43.9 4.5 %collective-permute-start.20 = (bf16[8,7168]{1,0:T(8,128)(2,1)S(1)}, bf16[8,7168]{1,0:T(8,128)(2,1)S(1)}, u32[]{:S(2)}, u32[]{:S(2)}) collective-permute-start(bf16[8,7168]{1,0:T(8,128)(2,1)S(1)} %get-tuple-element.55.refs_0_), channel_id=1, source_target_pairs={{0,1},{1,0},{2,3},{3,2},{4,5},{5,4},{6,7},{7,6},{8,9},{9,8},{10,11... | collective-permute-start | bytes 344072 | tf_op jit(solution)/shard_map/ppermute | solution.py:26
  46.3 2.0 %collective-permute-start.23 = (bf16[8,7168]{1,0:T(8,128)(2,1)S(1)}, bf16[8,7168]{1,0:T(8,128)(2,1)S(1)}, u32[]{:S(2)}, u32[]{:S(2)}) collective-permute-start(bf16[8,7168]{1,0:T(8,128)(2,1)S(1)} %collective-permute-done.19.refs_3_), channel_id=1, source_target_pairs={{0,1},{1,0},{2,3},{3,2},{4,5},{5,4},{6,7},{7,6},{8,9},{9,8},{10,11... | collective-permute-start | bytes 344072 | tf_op jit(solution)/shard_map/ppermute | solution.py:26
  47.8 1.3 %collective-permute-start.22 = (bf16[8,7168]{1,0:T(8,128)(2,1)S(1)}, bf16[8,7168]{1,0:T(8,128)(2,1)S(1)}, u32[]{:S(2)}, u32[]{:S(2)}) collective-permute-start(bf16[8,7168]{1,0:T(8,128)(2,1)S(1)} %collective-permute-done.18.refs_2_), channel_id=1, source_target_pairs={{0,1},{1,0},{2,3},{3,2},{4,5},{5,4},{6,7},{7,6},{8,9},{9,8},{10,11... | collective-permute-start | bytes 344072 | tf_op jit(solution)/shard_map/ppermute | solution.py:26
  48.0 1.3 %collective-permute-start.21 = (bf16[8,7168]{1,0:T(8,128)(2,1)S(1)}, bf16[8,7168]{1,0:T(8,128)(2,1)S(1)}, u32[]{:S(2)}, u32[]{:S(2)}) collective-permute-start(bf16[8,7168]{1,0:T(8,128)(2,1)S(1)} %collective-permute-done.17.refs_1_), channel_id=1, source_target_pairs={{0,1},{1,0},{2,3},{3,2},{4,5},{5,4},{6,7},{7,6},{8,9},{9,8},{10,11... | collective-permute-start | bytes 344072 | tf_op jit(solution)/shard_map/ppermute | solution.py:26
  51.5 1.4 %collective-permute-start.25 = (bf16[8,7168]{1,0:T(8,128)(2,1)S(1)}, bf16[8,7168]{1,0:T(8,128)(2,1)S(1)}, u32[]{:S(2)}, u32[]{:S(2)}) collective-permute-start(bf16[8,7168]{1,0:T(8,128)(2,1)S(1)} %get-tuple-element.60), channel_id=1, source_target_pairs={{0,1},{1,0},{2,3},{3,2},{4,5},{5,4},{6,7},{7,6},{8,9},{9,8},{10,11... | collective-permute-start | bytes 344072 | tf_op jit(solution)/shard_map/ppermute | solution.py:26
  51.8 2.8 %collective-permute-start.27 = (bf16[8,7168]{1,0:T(8,128)(2,1)S(1)}, bf16[8,7168]{1,0:T(8,128)(2,1)S(1)}, u32[]{:S(2)}, u32[]{:S(2)}) collective-permute-start(bf16[8,7168]{1,0:T(8,128)(2,1)S(1)} %get-tuple-element.62), channel_id=1, source_target_pairs={{0,1},{1,0},{2,3},{3,2},{4,5},{5,4},{6,7},{7,6},{8,9},{9,8},{10,11... | collective-permute-start | bytes 344072 | tf_op jit(solution)/shard_map/ppermute | solution.py:26
  52.1 3.7 %collective-permute-start.29 = (bf16[8,7168]{1,0:T(8,128)(2,1)S(1)}, bf16[8,7168]{1,0:T(8,128)(2,1)S(1)}, u32[]{:S(2)}, u32[]{:S(2)}) collective-permute-start(bf16[8,7168]{1,0:T(8,128)(2,1)S(1)} %get-tuple-element.64), channel_id=1, source_target_pairs={{0,1},{1,0},{2,3},{3,2},{4,5},{5,4},{6,7},{7,6},{8,9},{9,8},{10,11... | collective-permute-start | bytes 344072 | tf_op jit(solution)/shard_map/ppermute | solution.py:26
  52.3 4.3 %collective-permute-start.24 = (bf16[8,7168]{1,0:T(8,128)(2,1)S(1)}, bf16[8,7168]{1,0:T(8,128)(2,1)S(1)}, u32[]{:S(2)}, u32[]{:S(2)}) collective-permute-start(bf16[8,7168]{1,0:T(8,128)(2,1)S(1)} %get-tuple-element.58), channel_id=1, source_target_pairs={{0,1},{1,0},{2,3},{3,2},{4,5},{5,4},{6,7},{7,6},{8,9},{9,8},{10,11... | collective-permute-start | bytes 344072 | tf_op jit(solution)/shard_map/ppermute | solution.py:26
  52.9 6.9 %collective-permute-start.26 = (bf16[8,7168]{1,0:T(8,128)(2,1)S(1)}, bf16[8,7168]{1,0:T(8,128)(2,1)S(1)}, u32[]{:S(2)}, u32[]{:S(2)}) collective-permute-start(bf16[8,7168]{1,0:T(8,128)(2,1)S(1)} %shard_map.84), channel_id=1, source_target_pairs={{0,6},{1,7},{2,4},{3,5},{4,2},{5,3},{6,0},{7,1},{8,14},{9,15},{10,... | collective-permute-start | bytes 344072 | tf_op jit(solution)/shard_map/ppermute | solution.py:26
  54.7 6.6 %collective-permute-start.28 = (bf16[8,7168]{1,0:T(8,128)(2,1)S(1)}, bf16[8,7168]{1,0:T(8,128)(2,1)S(1)}, u32[]{:S(2)}, u32[]{:S(2)}) collective-permute-start(bf16[8,7168]{1,0:T(8,128)(2,1)S(1)} %shard_map.85), channel_id=1, source_target_pairs={{0,4},{1,5},{2,6},{3,7},{4,0},{5,1},{6,2},{7,3},{8,12},{9,13},{10,... | collective-permute-start | bytes 344072 | tf_op jit(solution)/shard_map/ppermute | solution.py:26
  55.8 5.9 %collective-permute-start.30 = (bf16[8,7168]{1,0:T(8,128)(2,1)S(1)}, bf16[8,7168]{1,0:T(8,128)(2,1)S(1)}, u32[]{:S(2)}, u32[]{:S(2)}) collective-permute-start(bf16[8,7168]{1,0:T(8,128)(2,1)S(1)} %shard_map.86), channel_id=1, source_target_pairs={{0,2},{1,3},{2,0},{3,1},{4,6},{5,7},{6,4},{7,5},{8,10},{9,11},{10,... | collective-permute-start | bytes 344072 | tf_op jit(solution)/shard_map/ppermute | solution.py:26
  61.8 6.7 %collective-permute-start.31 = (bf16[4,7168]{1,0:T(4,128)(2,1)S(1)}, bf16[4,7168]{1,0:T(4,128)(2,1)S(1)}, u32[]{:S(2)}, u32[]{:S(2)}) collective-permute-start(bf16[4,7168]{1,0:T(4,128)(2,1)S(1)} %get-tuple-element.65), channel_id=1, source_target_pairs={{0,24},{1,25},{2,26},{3,27},{4,28},{5,29},{6,30},{7,31},{8,16},{9,... | collective-permute-start | bytes 172040 | tf_op jit(solution)/shard_map/ppermute | solution.py:26
  64.1 4.3 %collective-permute-start.32 = (bf16[4,7168]{1,0:T(4,128)(2,1)S(1)}, bf16[4,7168]{1,0:T(4,128)(2,1)S(1)}, u32[]{:S(2)}, u32[]{:S(2)}) collective-permute-start(bf16[4,7168]{1,0:T(4,128)(2,1)S(1)} %get-tuple-element.66), channel_id=1, source_target_pairs={{0,16},{1,17},{2,18},{3,19},{4,20},{5,21},{6,22},{7,23},{8,24},{9,... | collective-permute-start | bytes 172040 | tf_op jit(solution)/shard_map/ppermute | solution.py:26

commit v22 on v20

--- a/solution.py
+++ b/solution.py
@@ -133,12 +133,13 @@
             out_ref[:, span] = total[place * rows:(place + 1) * rows].astype(jnp.bfloat16)
 
 
-def normalise(raw_ref, gain_ref, out_ref):
-    rows, dim = raw_ref.shape
-    square = jnp.zeros((rows, LANES), jnp.float32)
-    for start in range(0, dim, LANES):
-        piece = raw_ref[:, start:start + LANES].astype(jnp.float32)
-        square += piece * piece
+def squares(piece):
+    piece = piece.astype(jnp.float32)
+    return sum(piece[:, start:start + LANES] * piece[:, start:start + LANES] for start in range(0, piece.shape[1], LANES))
+
+
+def normalise(raw_ref, square, gain_ref, out_ref):
+    dim = raw_ref.shape[1]
     inv = lax.rsqrt(jnp.sum(square, axis=1, keepdims=True) / dim + 1e-06)
     for span in spans(dim):
         scaled = raw_ref[:, span].astype(jnp.float32) * inv * gain_ref[:, span]
@@ -147,23 +148,28 @@
 
 def first_kernel(own_ref, far_ref, gain_ref, out_ref, raw_ref):
     dim = raw_ref.shape[1]
+    square = 0.0
     for span in spans(dim):
         rows = [ref[:, span].astype(jnp.float32) for ref in (own_ref, far_ref)]
-        raw_ref[:, span] = jnp.concatenate(rows, axis=0).astype(jnp.bfloat16)
+        joined = jnp.concatenate(rows, axis=0)
+        square += squares(joined)
+        raw_ref[:, span] = joined.astype(jnp.bfloat16)
     tails = [ref[:, dim:].astype(jnp.float32) for ref in (own_ref, far_ref)]
     out_ref[:, dim:] = jnp.concatenate(tails, axis=0).astype(jnp.bfloat16)
-    normalise(raw_ref, gain_ref, out_ref)
+    normalise(raw_ref, square, gain_ref, out_ref)
 
 
 def meet_kernel(rest_ref, near_ref, far_ref, gain_ref, out_ref, own_ref, raw_ref):
     half = own_ref.shape[0]
+    square = 0.0
     for span in spans(out_ref.shape[1]):
         far = far_ref[:, span].astype(jnp.float32)
         total = rest_ref[:, span].astype(jnp.float32) + near_ref[:, span].astype(jnp.float32)
         total = (total + jnp.concatenate([far[half:], far[:half]], axis=0)).astype(jnp.bfloat16)
+        square += squares(total)
         raw_ref[:, span] = total
         own_ref[:, span] = total[:half]
-    normalise(raw_ref, gain_ref, out_ref)
+    normalise(raw_ref, square, gain_ref, out_ref)
 
 
 def mlp_kernel(step_no, *refs):

time: 69.2 us -> 69.2 us (level)
  no operation moved by 1% of the time
where the time goes in v22:
time: 69.2 us; the launch traced here: 69 us
  starting transfers between devices  32.3 us (47%)
  waiting for transfers between devices  24.9 us (36%)
  Pallas kernels  11.7 us (17%)
    ppermute x35, starting transfers between devices, exchange(): return lax.ppermute(value, ('segment', 'expert'), pairs)  32.3 us
    ppermute x35, waiting for transfers between devices, exchange(): return lax.ppermute(value, ('segment', 'expert'), pairs)  24.9 us
    pallas_call x14, Pallas kernels, call(): pl.pallas_call(kernel, out_shape=[jax.ShapeDtypeStruct(shape, jnp.bfloat1...  6.45 us
    pallas_call x2, Pallas kernels, load(): pl.pallas_call(functools.partial(load_kernel, count), out_shape=[pltpu.VM...  5.22 us
  transfers between devices with their start and end apart: 35, of which 21 were waited for; matrix products, arithmetic and copies ran while one was open for 0% of the time, Pallas kernels for 8%

profile of v22, /device:TPU:0, one launch (start us, length us, event | category | flops | bytes accessed | tf_op | source)
XLA Modules:
  0.0 69.0 jit_solution(2799432185845170891)
XLA Ops:
  0.0 0.9 %shard_map.73.own_ref = bf16[4,7296]{1,0:T(4,128)(2,1)S(1)} custom-call(bf16[1,4,7168]{2,1,0:T(4,128)(2,1)} %states_hbm.1, s32[1,2,2,4]{3,2,1,0:T(2,128)} %bitcast.3, bf16[1,2,2,4]{3,2,1,0:T(2,128)(2,1)} %bitcast.4), custom_call_target="tpu_custom_call" | custom-call | tf_op jit(solution)/shard_map/pallas_call | solution.py:43
  0.9 0.0 copy-start
  0.9 4.1 %collective-permute-start = (bf16[4,7296]{1,0:T(4,128)(2,1)S(1)}, bf16[4,7296]{1,0:T(4,128)(2,1)S(1)}, u32[]{:S(2)}, u32[]{:S(2)}) collective-permute-start(bf16[4,7296]{1,0:T(4,128)(2,1)S(1)} %shard_map.73.own_ref), channel_id=1, source_target_pairs={{0,8},{1,9},{2,10},{3,11},{4,12},{5,13},{6,14},{7,15},{8,0},{9,1},... | collective-permute-start | bytes 175112 | tf_op jit(solution)/shard_map/ppermute | solution.py:26
  5.0 2.0 %shard_map.74.refs_8_.refs_9_ = bf16[1,7168,256]{2,1,0:T(8,128)(2,1)S(1)} custom-call(bf16[1,7168,256]{2,1,0:T(8,128)(2,1)} %refs_0_.1), custom_call_target="tpu_custom_call" | custom-call | bytes 3670016 | tf_op jit(solution)/shard_map/pallas_call | solution.py:64
  7.1 0.7 %collective-permute-done.far_ref = bf16[4,7296]{1,0:T(4,128)(2,1)S(1)} collective-permute-done((bf16[4,7296]{1,0:T(4,128)(2,1)S(1)}, bf16[4,7296]{1,0:T(4,128)(2,1)S(1)}, u32[]{:S(2)}, u32[]{:S(2)}) %collective-permute-start) | collective-permute-done | bytes 58400 | tf_op jit(solution)/shard_map/ppermute | solution.py:26
  7.8 0.2 shard_map.75
  8.0 2.4 %collective-permute-start.4 = (bf16[8,7296]{1,0:T(8,128)(2,1)S(1)}, bf16[8,7296]{1,0:T(8,128)(2,1)S(1)}, u32[]{:S(2)}, u32[]{:S(2)}) collective-permute-start(bf16[8,7296]{1,0:T(8,128)(2,1)S(1)} %get-tuple-element.46.refs_0_), channel_id=1, source_target_pairs={{0,6},{1,7},{2,4},{3,5},{4,2},{5,3},{6,0},{7,1},{8,14},{9,15},{10,... | collective-permute-start | bytes 350216 | tf_op jit(solution)/shard_map/ppermute | solution.py:26
  10.4 1.5 %collective-permute-start.3 = (bf16[8,7296]{1,0:T(8,128)(2,1)S(1)}, bf16[8,7296]{1,0:T(8,128)(2,1)S(1)}, u32[]{:S(2)}, u32[]{:S(2)}) collective-permute-start(bf16[8,7296]{1,0:T(8,128)(2,1)S(1)} %get-tuple-element.46.refs_0_), channel_id=1, source_target_pairs={{0,4},{1,5},{2,6},{3,7},{4,0},{5,1},{6,2},{7,3},{8,12},{9,13},{10,... | collective-permute-start | bytes 350216 | tf_op jit(solution)/shard_map/ppermute | solution.py:26
  11.8 3.2 %shard_map.76 = (bf16[1,7168,256]{2,1,0:T(8,128)(2,1)S(1)}, bf16[1,256,7168]{2,1,0:T(8,128)(2,1)S(1)}) custom-call(bf16[1,7168,256]{2,1,0:T(8,128)(2,1)} %refs_0_.2, bf16[1,256,7168]{2,1,0:T(8,128)(2,1)} %refs_1_), custom_call_target="tpu_custom_call" | custom-call | bytes 7340032 | tf_op jit(solution)/shard_map/pallas_call | solution.py:64
  15.0 0.1 collective-permute-start.5
  15.1 0.5 collective-permute-start.8
  15.6 0.3 collective-permute-done.3.refs_2_
  15.9 0.0 collective-permute-start.7
  15.9 0.8 %collective-permute-done.2.refs_1_ = bf16[8,7296]{1,0:T(8,128)(2,1)S(1)} collective-permute-done((bf16[8,7296]{1,0:T(8,128)(2,1)S(1)}, bf16[8,7296]{1,0:T(8,128)(2,1)S(1)}, u32[]{:S(2)}, u32[]{:S(2)}) %collective-permute-start.2) | collective-permute-done | bytes 116768 | tf_op jit(solution)/shard_map/ppermute | solution.py:26
  16.7 0.0 collective-permute-start.6
  16.7 0.0 collective-permute-done.5.refs_4_
  16.7 0.5 collective-permute-done.7.refs_6_
  17.2 0.8 %collective-permute-done.6.refs_5_ = bf16[8,7296]{1,0:T(8,128)(2,1)S(1)} collective-permute-done((bf16[8,7296]{1,0:T(8,128)(2,1)S(1)}, bf16[8,7296]{1,0:T(8,128)(2,1)S(1)}, u32[]{:S(2)}, u32[]{:S(2)}) %collective-permute-start.6) | collective-permute-done | bytes 116768 | tf_op jit(solution)/shard_map/ppermute | solution.py:26
  18.0 2.1 %shard_map.77 = (bf16[8,7168]{1,0:T(8,128)(2,1)S(1)}, bf16[8,7168]{1,0:T(8,128)(2,1)S(1)}, bf16[8,7168]{1,0:T(8,128)(2,1)S(1)}, bf16[8,7168]{1,0:T(8,128)(2,1)S(...) custom-call(bf16[8,7296]{1,0:T(8,128)(2,1)S(1)} %get-tuple-element.4, ...), custom_call_target="tpu_custom_call" | custom-call | flops 704643072 | bytes 11010048 | tf_op jit(solution)/shard_map/pallas_call | solution.py:43
  20.1 0.2 collective-permute-start.10
  20.3 0.4 collective-permute-start.12
  20.7 0.1 collective-permute-start.14
  20.8 0.4 collective-permute-start.9
  21.2 0.3 collective-permute-done.10.refs_1_
  21.5 1.3 %collective-permute-start.11 = (bf16[8,7168]{1,0:T(8,128)(2,1)S(1)}, bf16[8,7168]{1,0:T(8,128)(2,1)S(1)}, u32[]{:S(2)}, u32[]{:S(2)}) collective-permute-start(bf16[8,7168]{1,0:T(8,128)(2,1)S(1)} %shard_map.78), channel_id=1, source_target_pairs={{0,6},{1,7},{2,4},{3,5},{4,2},{5,3},{6,0},{7,1},{8,14},{9,15},{10,... | collective-permute-start | bytes 344072 | tf_op jit(solution)/shard_map/ppermute | solution.py:26
  22.9 1.4 %collective-permute-start.13 = (bf16[8,7168]{1,0:T(8,128)(2,1)S(1)}, bf16[8,7168]{1,0:T(8,128)(2,1)S(1)}, u32[]{:S(2)}, u32[]{:S(2)}) collective-permute-start(bf16[8,7168]{1,0:T(8,128)(2,1)S(1)} %shard_map.79), channel_id=1, source_target_pairs={{0,4},{1,5},{2,6},{3,7},{4,0},{5,1},{6,2},{7,3},{8,12},{9,13},{10,... | collective-permute-start | bytes 344072 | tf_op jit(solution)/shard_map/ppermute | solution.py:26
  24.3 0.9 %collective-permute-start.15 = (bf16[8,7168]{1,0:T(8,128)(2,1)S(1)}, bf16[8,7168]{1,0:T(8,128)(2,1)S(1)}, u32[]{:S(2)}, u32[]{:S(2)}) collective-permute-start(bf16[8,7168]{1,0:T(8,128)(2,1)S(1)} %shard_map.80), channel_id=1, source_target_pairs={{0,2},{1,3},{2,0},{3,1},{4,6},{5,7},{6,4},{7,5},{8,10},{9,11},{10,... | collective-permute-start | bytes 344072 | tf_op jit(solution)/shard_map/ppermute | solution.py:26
  25.3 1.5 %collective-permute-start.1 = (bf16[8,7168]{1,0:T(8,128)(2,1)S(1)}, bf16[8,7168]{1,0:T(8,128)(2,1)S(1)}, u32[]{:S(2)}, u32[]{:S(2)}) collective-permute-start(bf16[8,7168]{1,0:T(8,128)(2,1)S(1)} %get-tuple-element.39), channel_id=1, source_target_pairs={{0,16},{1,17},{2,18},{3,19},{4,20},{5,21},{6,22},{7,23},{8,24},{9,... | collective-permute-start | bytes 344072 | tf_op jit(solution)/shard_map/ppermute | solution.py:26
  26.8 1.7 %collective-permute-done.11.refs_2_ = bf16[8,7168]{1,0:T(8,128)(2,1)S(1)} collective-permute-done((bf16[8,7168]{1,0:T(8,128)(2,1)S(1)}, bf16[8,7168]{1,0:T(8,128)(2,1)S(1)}, u32[]{:S(2)}, u32[]{:S(2)}) %collective-permute-start.11) | collective-permute-done | bytes 114720 | tf_op jit(solution)/shard_map/ppermute | solution.py:26
  28.5 1.5 %collective-permute-done.13.refs_3_ = bf16[8,7168]{1,0:T(8,128)(2,1)S(1)} collective-permute-done((bf16[8,7168]{1,0:T(8,128)(2,1)S(1)}, bf16[8,7168]{1,0:T(8,128)(2,1)S(1)}, u32[]{:S(2)}, u32[]{:S(2)}) %collective-permute-start.13) | collective-permute-done | bytes 114720 | tf_op jit(solution)/shard_map/ppermute | solution.py:26
  30.0 0.1 collective-permute-done.15.refs_4_
  30.2 0.1 shard_map.81
  30.2 3.4 %collective-permute-start.17 = (bf16[8,7168]{1,0:T(8,128)(2,1)S(1)}, bf16[8,7168]{1,0:T(8,128)(2,1)S(1)}, u32[]{:S(2)}, u32[]{:S(2)}) collective-permute-start(bf16[8,7168]{1,0:T(8,128)(2,1)S(1)} %shard_map.81), channel_id=1, source_target_pairs={{0,24},{1,25},{2,26},{3,27},{4,28},{5,29},{6,30},{7,31},{8,16},{9,... | collective-permute-start | bytes 344072 | tf_op jit(solution)/shard_map/ppermute | solution.py:26
  33.6 0.5 collective-permute-start.16
  34.2 5.3 %collective-permute-done.17.far_ref = bf16[8,7168]{1,0:T(8,128)(2,1)S(1)} collective-permute-done((bf16[8,7168]{1,0:T(8,128)(2,1)S(1)}, bf16[8,7168]{1,0:T(8,128)(2,1)S(1)}, u32[]{:S(2)}, u32[]{:S(2)}) %collective-permute-start.17) | collective-permute-done | bytes 114720 | tf_op jit(solution)/shard_map/ppermute | solution.py:26
  39.4 0.6 collective-permute-done.16.near_ref
  40.0 0.2 shard_map.82
  40.2 1.4 %collective-permute-start.21 = (bf16[8,7168]{1,0:T(8,128)(2,1)S(1)}, bf16[8,7168]{1,0:T(8,128)(2,1)S(1)}, u32[]{:S(2)}, u32[]{:S(2)}) collective-permute-start(bf16[8,7168]{1,0:T(8,128)(2,1)S(1)} %get-tuple-element.59.refs_0_), channel_id=1, source_target_pairs={{0,6},{1,7},{2,4},{3,5},{4,2},{5,3},{6,0},{7,1},{8,14},{9,15},{10,... | collective-permute-start | bytes 344072 | tf_op jit(solution)/shard_map/ppermute | solution.py:26
  41.6 1.1 %collective-permute-start.20 = (bf16[8,7168]{1,0:T(8,128)(2,1)S(1)}, bf16[8,7168]{1,0:T(8,128)(2,1)S(1)}, u32[]{:S(2)}, u32[]{:S(2)}) collective-permute-start(bf16[8,7168]{1,0:T(8,128)(2,1)S(1)} %get-tuple-element.59.refs_0_), channel_id=1, source_target_pairs={{0,4},{1,5},{2,6},{3,7},{4,0},{5,1},{6,2},{7,3},{8,12},{9,13},{10,... | collective-permute-start | bytes 344072 | tf_op jit(solution)/shard_map/ppermute | solution.py:26
  42.7 1.1 %collective-permute-start.19 = (bf16[8,7168]{1,0:T(8,128)(2,1)S(1)}, bf16[8,7168]{1,0:T(8,128)(2,1)S(1)}, u32[]{:S(2)}, u32[]{:S(2)}) collective-permute-start(bf16[8,7168]{1,0:T(8,128)(2,1)S(1)} %get-tuple-element.59.refs_0_), channel_id=1, source_target_pairs={{0,2},{1,3},{2,0},{3,1},{4,6},{5,7},{6,4},{7,5},{8,10},{9,11},{10,... | collective-permute-start | bytes 344072 | tf_op jit(solution)/shard_map/ppermute | solution.py:26
  43.8 2.5 %collective-permute-done.21.refs_3_ = bf16[8,7168]{1,0:T(8,128)(2,1)S(1)} collective-permute-done((bf16[8,7168]{1,0:T(8,128)(2,1)S(1)}, bf16[8,7168]{1,0:T(8,128)(2,1)S(1)}, u32[]{:S(2)}, u32[]{:S(2)}) %collective-permute-start.21) | collective-permute-done | bytes 114720 | tf_op jit(solution)/shard_map/ppermute | solution.py:26
  46.3 1.4 %collective-permute-done.20.refs_2_ = bf16[8,7168]{1,0:T(8,128)(2,1)S(1)} collective-permute-done((bf16[8,7168]{1,0:T(8,128)(2,1)S(1)}, bf16[8,7168]{1,0:T(8,128)(2,1)S(1)}, u32[]{:S(2)}, u32[]{:S(2)}) %collective-permute-start.20) | collective-permute-done | bytes 114720 | tf_op jit(solution)/shard_map/ppermute | solution.py:26
  47.7 0.2 collective-permute-done.19.refs_1_
  48.0 0.3 collective-permute-start.23
  48.2 0.8 %collective-permute-done.24.refs_6_ = bf16[8,7168]{1,0:T(8,128)(2,1)S(1)} collective-permute-done((bf16[8,7168]{1,0:T(8,128)(2,1)S(1)}, bf16[8,7168]{1,0:T(8,128)(2,1)S(1)}, u32[]{:S(2)}, u32[]{:S(2)}) %collective-permute-start.24) | collective-permute-done | bytes 114720 | tf_op jit(solution)/shard_map/ppermute | solution.py:26
  49.0 0.2 collective-permute-done.23.refs_5_
  49.3 2.1 %shard_map.83 = (bf16[8,7168]{1,0:T(8,128)(2,1)S(1)}, bf16[8,7168]{1,0:T(8,128)(2,1)S(1)}, bf16[8,7168]{1,0:T(8,128)(2,1)S(1)}, bf16[8,7168]{1,0:T(8,128)(2,1)S(...) custom-call(bf16[8,7168]{1,0:T(8,128)(2,1)S(1)} %get-tuple-element.5, ...), custom_call_target="tpu_custom_call" | custom-call | flops 704643072 | bytes 11010048 | tf_op jit(solution)/shard_map/pallas_call | solution.py:43
  51.4 0.3 collective-permute-start.27
  51.7 0.2 collective-permute-start.29
  52.0 0.3 collective-permute-start.31
  52.3 0.2 collective-permute-start.26
  52.5 0.3 collective-permute-done.27.refs_1_
  52.8 1.8 %collective-permute-start.28 = (bf16[8,7168]{1,0:T(8,128)(2,1)S(1)}, bf16[8,7168]{1,0:T(8,128)(2,1)S(1)}, u32[]{:S(2)}, u32[]{:S(2)}) collective-permute-start(bf16[8,7168]{1,0:T(8,128)(2,1)S(1)} %shard_map.84), channel_id=1, source_target_pairs={{0,6},{1,7},{2,4},{3,5},{4,2},{5,3},{6,0},{7,1},{8,14},{9,15},{10,... | collective-permute-start | bytes 344072 | tf_op jit(solution)/shard_map/ppermute | solution.py:26
  54.6 1.1 %collective-permute-start.30 = (bf16[8,7168]{1,0:T(8,128)(2,1)S(1)}, bf16[8,7168]{1,0:T(8,128)(2,1)S(1)}, u32[]{:S(2)}, u32[]{:S(2)}) collective-permute-start(bf16[8,7168]{1,0:T(8,128)(2,1)S(1)} %shard_map.85), channel_id=1, source_target_pairs={{0,4},{1,5},{2,6},{3,7},{4,0},{5,1},{6,2},{7,3},{8,12},{9,13},{10,... | collective-permute-start | bytes 344072 | tf_op jit(solution)/shard_map/ppermute | solution.py:26
  55.7 0.9 %collective-permute-start.32 = (bf16[8,7168]{1,0:T(8,128)(2,1)S(1)}, bf16[8,7168]{1,0:T(8,128)(2,1)S(1)}, u32[]{:S(2)}, u32[]{:S(2)}) collective-permute-start(bf16[8,7168]{1,0:T(8,128)(2,1)S(1)} %shard_map.86), channel_id=1, source_target_pairs={{0,2},{1,3},{2,0},{3,1},{4,6},{5,7},{6,4},{7,5},{8,10},{9,11},{10,... | collective-permute-start | bytes 344072 | tf_op jit(solution)/shard_map/ppermute | solution.py:26
  56.6 1.7 %collective-permute-start.18 = (bf16[4,7168]{1,0:T(4,128)(2,1)S(1)}, bf16[4,7168]{1,0:T(4,128)(2,1)S(1)}, u32[]{:S(2)}, u32[]{:S(2)}) collective-permute-start(bf16[4,7168]{1,0:T(4,128)(2,1)S(1)} %get-tuple-element.58), channel_id=1, source_target_pairs={{0,16},{1,17},{2,18},{3,19},{4,20},{5,21},{6,22},{7,23},{8,24},{9,... | collective-permute-start | bytes 172040 | tf_op jit(solution)/shard_map/ppermute | solution.py:26
  58.3 1.4 %collective-permute-done.28.refs_2_ = bf16[8,7168]{1,0:T(8,128)(2,1)S(1)} collective-permute-done((bf16[8,7168]{1,0:T(8,128)(2,1)S(1)}, bf16[8,7168]{1,0:T(8,128)(2,1)S(1)}, u32[]{:S(2)}, u32[]{:S(2)}) %collective-permute-start.28) | collective-permute-done | bytes 114720 | tf_op jit(solution)/shard_map/ppermute | solution.py:26
  59.8 1.4 %collective-permute-done.30.refs_3_ = bf16[8,7168]{1,0:T(8,128)(2,1)S(1)} collective-permute-done((bf16[8,7168]{1,0:T(8,128)(2,1)S(1)}, bf16[8,7168]{1,0:T(8,128)(2,1)S(1)}, u32[]{:S(2)}, u32[]{:S(2)}) %collective-permute-start.30) | collective-permute-done | bytes 114720 | tf_op jit(solution)/shard_map/ppermute | solution.py:26
  61.2 0.4 collective-permute-done.32.refs_4_
  61.6 0.1 shard_map.87
  61.7 2.4 %collective-permute-start.33 = (bf16[4,7168]{1,0:T(4,128)(2,1)S(1)}, bf16[4,7168]{1,0:T(4,128)(2,1)S(1)}, u32[]{:S(2)}, u32[]{:S(2)}) collective-permute-start(bf16[4,7168]{1,0:T(4,128)(2,1)S(1)} %get-tuple-element.69), channel_id=1, source_target_pairs={{0,24},{1,25},{2,26},{3,27},{4,28},{5,29},{6,30},{7,31},{8,16},{9,... | collective-permute-start | bytes 172040 | tf_op jit(solution)/shard_map/ppermute | solution.py:26
  64.0 0.9 %collective-permute-start.34 = (bf16[4,7168]{1,0:T(4,128)(2,1)S(1)}, bf16[4,7168]{1,0:T(4,128)(2,1)S(1)}, u32[]{:S(2)}, u32[]{:S(2)}) collective-permute-start(bf16[4,7168]{1,0:T(4,128)(2,1)S(1)} %get-tuple-element.70), channel_id=1, source_target_pairs={{0,16},{1,17},{2,18},{3,19},{4,20},{5,21},{6,22},{7,23},{8,24},{9,... | collective-permute-start | bytes 172040 | tf_op jit(solution)/shard_map/ppermute | solution.py:26
  64.9 3.4 %collective-permute-done.33.refs_1_ = bf16[4,7168]{1,0:T(4,128)(2,1)S(1)} collective-permute-done((bf16[4,7168]{1,0:T(4,128)(2,1)S(1)}, bf16[4,7168]{1,0:T(4,128)(2,1)S(1)}, u32[]{:S(2)}, u32[]{:S(2)}) %collective-permute-start.33) | collective-permute-done | bytes 57376 | tf_op jit(solution)/shard_map/ppermute | solution.py:26
  68.3 0.7 shard_map.88
  (24 shorter events, 0.2 us)
Async XLA Ops:
  0.9 6.9 %copy-start = (f32[1,7168]{1,0:T(1,128)S(1)}, f32[1,7168]{1,0:T(1,128)}, u32[]{:S(2)}) copy-start(f32[1,7168]{1,0:T(1,128)} %gain_ref.3) | copy-start | bytes 86020
  0.9 6.9 %collective-permute-start = (bf16[4,7296]{1,0:T(4,128)(2,1)S(1)}, bf16[4,7296]{1,0:T(4,128)(2,1)S(1)}, u32[]{:S(2)}, u32[]{:S(2)}) collective-permute-start(bf16[4,7296]{1,0:T(4,128)(2,1)S(1)} %shard_map.73.own_ref), channel_id=1, source_target_pairs={{0,8},{1,9},{2,10},{3,11},{4,12},{5,13},{6,14},{7,15},{8,0},{9,1},... | collective-permute-start | bytes 175112 | tf_op jit(solution)/shard_map/ppermute | solution.py:26
  8.0 7.1 %collective-permute-start.4 = (bf16[8,7296]{1,0:T(8,128)(2,1)S(1)}, bf16[8,7296]{1,0:T(8,128)(2,1)S(1)}, u32[]{:S(2)}, u32[]{:S(2)}) collective-permute-start(bf16[8,7296]{1,0:T(8,128)(2,1)S(1)} %get-tuple-element.46.refs_0_), channel_id=1, source_target_pairs={{0,6},{1,7},{2,4},{3,5},{4,2},{5,3},{6,0},{7,1},{8,14},{9,15},{10,... | collective-permute-start | bytes 350216 | tf_op jit(solution)/shard_map/ppermute | solution.py:26
  10.4 5.5 %collective-permute-start.3 = (bf16[8,7296]{1,0:T(8,128)(2,1)S(1)}, bf16[8,7296]{1,0:T(8,128)(2,1)S(1)}, u32[]{:S(2)}, u32[]{:S(2)}) collective-permute-start(bf16[8,7296]{1,0:T(8,128)(2,1)S(1)} %get-tuple-element.46.refs_0_), channel_id=1, source_target_pairs={{0,4},{1,5},{2,6},{3,7},{4,0},{5,1},{6,2},{7,3},{8,12},{9,13},{10,... | collective-permute-start | bytes 350216 | tf_op jit(solution)/shard_map/ppermute | solution.py:26
  11.8 4.8 %collective-permute-start.2 = (bf16[8,7296]{1,0:T(8,128)(2,1)S(1)}, bf16[8,7296]{1,0:T(8,128)(2,1)S(1)}, u32[]{:S(2)}, u32[]{:S(2)}) collective-permute-start(bf16[8,7296]{1,0:T(8,128)(2,1)S(1)} %get-tuple-element.46.refs_0_), channel_id=1, source_target_pairs={{0,2},{1,3},{2,0},{3,1},{4,6},{5,7},{6,4},{7,5},{8,10},{9,11},{10,... | collective-permute-start | bytes 350216 | tf_op jit(solution)/shard_map/ppermute | solution.py:26
  15.0 1.6 %collective-permute-start.5 = (bf16[8,7296]{1,0:T(8,128)(2,1)S(1)}, bf16[8,7296]{1,0:T(8,128)(2,1)S(1)}, u32[]{:S(2)}, u32[]{:S(2)}) collective-permute-start(bf16[8,7296]{1,0:T(8,128)(2,1)S(1)} %get-tuple-element.46.refs_0_), channel_id=1, source_target_pairs={{0,1},{1,0},{2,3},{3,2},{4,5},{5,4},{6,7},{7,6},{8,9},{9,8},{10,11... | collective-permute-start | bytes 350216 | tf_op jit(solution)/shard_map/ppermute | solution.py:26
  15.1 1.5 %collective-permute-start.8 = (bf16[8,7296]{1,0:T(8,128)(2,1)S(1)}, bf16[8,7296]{1,0:T(8,128)(2,1)S(1)}, u32[]{:S(2)}, u32[]{:S(2)}) collective-permute-start(bf16[8,7296]{1,0:T(8,128)(2,1)S(1)} %collective-permute-done.4.refs_3_), channel_id=1, source_target_pairs={{0,1},{1,0},{2,3},{3,2},{4,5},{5,4},{6,7},{7,6},{8,9},{9,8},{10,11... | collective-permute-start | bytes 350216 | tf_op jit(solution)/shard_map/ppermute | solution.py:26
  15.9 1.3 %collective-permute-start.7 = (bf16[8,7296]{1,0:T(8,128)(2,1)S(1)}, bf16[8,7296]{1,0:T(8,128)(2,1)S(1)}, u32[]{:S(2)}, u32[]{:S(2)}) collective-permute-start(bf16[8,7296]{1,0:T(8,128)(2,1)S(1)} %collective-permute-done.3.refs_2_), channel_id=1, source_target_pairs={{0,1},{1,0},{2,3},{3,2},{4,5},{5,4},{6,7},{7,6},{8,9},{9,8},{10,11... | collective-permute-start | bytes 350216 | tf_op jit(solution)/shard_map/ppermute | solution.py:26
  16.7 1.3 %collective-permute-start.6 = (bf16[8,7296]{1,0:T(8,128)(2,1)S(1)}, bf16[8,7296]{1,0:T(8,128)(2,1)S(1)}, u32[]{:S(2)}, u32[]{:S(2)}) collective-permute-start(bf16[8,7296]{1,0:T(8,128)(2,1)S(1)} %collective-permute-done.2.refs_1_), channel_id=1, source_target_pairs={{0,1},{1,0},{2,3},{3,2},{4,5},{5,4},{6,7},{7,6},{8,9},{9,8},{10,11... | collective-permute-start | bytes 350216 | tf_op jit(solution)/shard_map/ppermute | solution.py:26
  20.1 1.4 %collective-permute-start.10 = (bf16[8,7168]{1,0:T(8,128)(2,1)S(1)}, bf16[8,7168]{1,0:T(8,128)(2,1)S(1)}, u32[]{:S(2)}, u32[]{:S(2)}) collective-permute-start(bf16[8,7168]{1,0:T(8,128)(2,1)S(1)} %get-tuple-element.53), channel_id=1, source_target_pairs={{0,1},{1,0},{2,3},{3,2},{4,5},{5,4},{6,7},{7,6},{8,9},{9,8},{10,11... | collective-permute-start | bytes 344072 | tf_op jit(solution)/shard_map/ppermute | solution.py:26
  20.3 2.5 %collective-permute-start.12 = (bf16[8,7168]{1,0:T(8,128)(2,1)S(1)}, bf16[8,7168]{1,0:T(8,128)(2,1)S(1)}, u32[]{:S(2)}, u32[]{:S(2)}) collective-permute-start(bf16[8,7168]{1,0:T(8,128)(2,1)S(1)} %get-tuple-element.55), channel_id=1, source_target_pairs={{0,1},{1,0},{2,3},{3,2},{4,5},{5,4},{6,7},{7,6},{8,9},{9,8},{10,11... | collective-permute-start | bytes 344072 | tf_op jit(solution)/shard_map/ppermute | solution.py:26
  20.7 3.6 %collective-permute-start.14 = (bf16[8,7168]{1,0:T(8,128)(2,1)S(1)}, bf16[8,7168]{1,0:T(8,128)(2,1)S(1)}, u32[]{:S(2)}, u32[]{:S(2)}) collective-permute-start(bf16[8,7168]{1,0:T(8,128)(2,1)S(1)} %get-tuple-element.57), channel_id=1, source_target_pairs={{0,1},{1,0},{2,3},{3,2},{4,5},{5,4},{6,7},{7,6},{8,9},{9,8},{10,11... | collective-permute-start | bytes 344072 | tf_op jit(solution)/shard_map/ppermute | solution.py:26
  20.8 5.9 %collective-permute-start.9 = (bf16[8,7168]{1,0:T(8,128)(2,1)S(1)}, bf16[8,7168]{1,0:T(8,128)(2,1)S(1)}, u32[]{:S(2)}, u32[]{:S(2)}) collective-permute-start(bf16[8,7168]{1,0:T(8,128)(2,1)S(1)} %get-tuple-element.51), channel_id=1, source_target_pairs={{0,1},{1,0},{2,3},{3,2},{4,5},{5,4},{6,7},{7,6},{8,9},{9,8},{10,11... | collective-permute-start | bytes 344072 | tf_op jit(solution)/shard_map/ppermute | solution.py:26
  21.5 7.0 %collective-permute-start.11 = (bf16[8,7168]{1,0:T(8,128)(2,1)S(1)}, bf16[8,7168]{1,0:T(8,128)(2,1)S(1)}, u32[]{:S(2)}, u32[]{:S(2)}) collective-permute-start(bf16[8,7168]{1,0:T(8,128)(2,1)S(1)} %shard_map.78), channel_id=1, source_target_pairs={{0,6},{1,7},{2,4},{3,5},{4,2},{5,3},{6,0},{7,1},{8,14},{9,15},{10,... | collective-permute-start | bytes 344072 | tf_op jit(solution)/shard_map/ppermute | solution.py:26
  22.9 7.2 %collective-permute-start.13 = (bf16[8,7168]{1,0:T(8,128)(2,1)S(1)}, bf16[8,7168]{1,0:T(8,128)(2,1)S(1)}, u32[]{:S(2)}, u32[]{:S(2)}) collective-permute-start(bf16[8,7168]{1,0:T(8,128)(2,1)S(1)} %shard_map.79), channel_id=1, source_target_pairs={{0,4},{1,5},{2,6},{3,7},{4,0},{5,1},{6,2},{7,3},{8,12},{9,13},{10,... | collective-permute-start | bytes 344072 | tf_op jit(solution)/shard_map/ppermute | solution.py:26
  24.3 5.8 %collective-permute-start.15 = (bf16[8,7168]{1,0:T(8,128)(2,1)S(1)}, bf16[8,7168]{1,0:T(8,128)(2,1)S(1)}, u32[]{:S(2)}, u32[]{:S(2)}) collective-permute-start(bf16[8,7168]{1,0:T(8,128)(2,1)S(1)} %shard_map.80), channel_id=1, source_target_pairs={{0,2},{1,3},{2,0},{3,1},{4,6},{5,7},{6,4},{7,5},{8,10},{9,11},{10,... | collective-permute-start | bytes 344072 | tf_op jit(solution)/shard_map/ppermute | solution.py:26
  25.3 8.9 %collective-permute-start.1 = (bf16[8,7168]{1,0:T(8,128)(2,1)S(1)}, bf16[8,7168]{1,0:T(8,128)(2,1)S(1)}, u32[]{:S(2)}, u32[]{:S(2)}) collective-permute-start(bf16[8,7168]{1,0:T(8,128)(2,1)S(1)} %get-tuple-element.39), channel_id=1, source_target_pairs={{0,16},{1,17},{2,18},{3,19},{4,20},{5,21},{6,22},{7,23},{8,24},{9,... | collective-permute-start | bytes 344072 | tf_op jit(solution)/shard_map/ppermute | solution.py:26
  30.2 9.2 %collective-permute-start.17 = (bf16[8,7168]{1,0:T(8,128)(2,1)S(1)}, bf16[8,7168]{1,0:T(8,128)(2,1)S(1)}, u32[]{:S(2)}, u32[]{:S(2)}) collective-permute-start(bf16[8,7168]{1,0:T(8,128)(2,1)S(1)} %shard_map.81), channel_id=1, source_target_pairs={{0,24},{1,25},{2,26},{3,27},{4,28},{5,29},{6,30},{7,31},{8,16},{9,... | collective-permute-start | bytes 344072 | tf_op jit(solution)/shard_map/ppermute | solution.py:26
  33.6 6.4 %collective-permute-start.16 = (bf16[8,7168]{1,0:T(8,128)(2,1)S(1)}, bf16[8,7168]{1,0:T(8,128)(2,1)S(1)}, u32[]{:S(2)}, u32[]{:S(2)}) collective-permute-start(bf16[8,7168]{1,0:T(8,128)(2,1)S(1)} %shard_map.81), channel_id=1, source_target_pairs={{0,16},{1,17},{2,18},{3,19},{4,20},{5,21},{6,22},{7,23},{8,24},{9,... | collective-permute-start | bytes 344072 | tf_op jit(solution)/shard_map/ppermute | solution.py:26
  40.2 6.0 %collective-permute-start.21 = (bf16[8,7168]{1,0:T(8,128)(2,1)S(1)}, bf16[8,7168]{1,0:T(8,128)(2,1)S(1)}, u32[]{:S(2)}, u32[]{:S(2)}) collective-permute-start(bf16[8,7168]{1,0:T(8,128)(2,1)S(1)} %get-tuple-element.59.refs_0_), channel_id=1, source_target_pairs={{0,6},{1,7},{2,4},{3,5},{4,2},{5,3},{6,0},{7,1},{8,14},{9,15},{10,... | collective-permute-start | bytes 344072 | tf_op jit(solution)/shard_map/ppermute | solution.py:26
  41.6 6.1 %collective-permute-start.20 = (bf16[8,7168]{1,0:T(8,128)(2,1)S(1)}, bf16[8,7168]{1,0:T(8,128)(2,1)S(1)}, u32[]{:S(2)}, u32[]{:S(2)}) collective-permute-start(bf16[8,7168]{1,0:T(8,128)(2,1)S(1)} %get-tuple-element.59.refs_0_), channel_id=1, source_target_pairs={{0,4},{1,5},{2,6},{3,7},{4,0},{5,1},{6,2},{7,3},{8,12},{9,13},{10,... | collective-permute-start | bytes 344072 | tf_op jit(solution)/shard_map/ppermute | solution.py:26
  42.7 5.2 %collective-permute-start.19 = (bf16[8,7168]{1,0:T(8,128)(2,1)S(1)}, bf16[8,7168]{1,0:T(8,128)(2,1)S(1)}, u32[]{:S(2)}, u32[]{:S(2)}) collective-permute-start(bf16[8,7168]{1,0:T(8,128)(2,1)S(1)} %get-tuple-element.59.refs_0_), channel_id=1, source_target_pairs={{0,2},{1,3},{2,0},{3,1},{4,6},{5,7},{6,4},{7,5},{8,10},{9,11},{10,... | collective-permute-start | bytes 344072 | tf_op jit(solution)/shard_map/ppermute | solution.py:26
  43.8 4.4 %collective-permute-start.22 = (bf16[8,7168]{1,0:T(8,128)(2,1)S(1)}, bf16[8,7168]{1,0:T(8,128)(2,1)S(1)}, u32[]{:S(2)}, u32[]{:S(2)}) collective-permute-start(bf16[8,7168]{1,0:T(8,128)(2,1)S(1)} %get-tuple-element.59.refs_0_), channel_id=1, source_target_pairs={{0,1},{1,0},{2,3},{3,2},{4,5},{5,4},{6,7},{7,6},{8,9},{9,8},{10,11... | collective-permute-start | bytes 344072 | tf_op jit(solution)/shard_map/ppermute | solution.py:26
  46.3 1.9 %collective-permute-start.25 = (bf16[8,7168]{1,0:T(8,128)(2,1)S(1)}, bf16[8,7168]{1,0:T(8,128)(2,1)S(1)}, u32[]{:S(2)}, u32[]{:S(2)}) collective-permute-start(bf16[8,7168]{1,0:T(8,128)(2,1)S(1)} %collective-permute-done.21.refs_3_), channel_id=1, source_target_pairs={{0,1},{1,0},{2,3},{3,2},{4,5},{5,4},{6,7},{7,6},{8,9},{9,8},{10,11... | collective-permute-start | bytes 344072 | tf_op jit(solution)/shard_map/ppermute | solution.py:26
  47.7 1.3 %collective-permute-start.24 = (bf16[8,7168]{1,0:T(8,128)(2,1)S(1)}, bf16[8,7168]{1,0:T(8,128)(2,1)S(1)}, u32[]{:S(2)}, u32[]{:S(2)}) collective-permute-start(bf16[8,7168]{1,0:T(8,128)(2,1)S(1)} %collective-permute-done.20.refs_2_), channel_id=1, source_target_pairs={{0,1},{1,0},{2,3},{3,2},{4,5},{5,4},{6,7},{7,6},{8,9},{9,8},{10,11... | collective-permute-start | bytes 344072 | tf_op jit(solution)/shard_map/ppermute | solution.py:26
  48.0 1.3 %collective-permute-start.23 = (bf16[8,7168]{1,0:T(8,128)(2,1)S(1)}, bf16[8,7168]{1,0:T(8,128)(2,1)S(1)}, u32[]{:S(2)}, u32[]{:S(2)}) collective-permute-start(bf16[8,7168]{1,0:T(8,128)(2,1)S(1)} %collective-permute-done.19.refs_1_), channel_id=1, source_target_pairs={{0,1},{1,0},{2,3},{3,2},{4,5},{5,4},{6,7},{7,6},{8,9},{9,8},{10,11... | collective-permute-start | bytes 344072 | tf_op jit(solution)/shard_map/ppermute | solution.py:26
  51.4 1.4 %collective-permute-start.27 = (bf16[8,7168]{1,0:T(8,128)(2,1)S(1)}, bf16[8,7168]{1,0:T(8,128)(2,1)S(1)}, u32[]{:S(2)}, u32[]{:S(2)}) collective-permute-start(bf16[8,7168]{1,0:T(8,128)(2,1)S(1)} %get-tuple-element.64), channel_id=1, source_target_pairs={{0,1},{1,0},{2,3},{3,2},{4,5},{5,4},{6,7},{7,6},{8,9},{9,8},{10,11... | collective-permute-start | bytes 344072 | tf_op jit(solution)/shard_map/ppermute | solution.py:26
  51.7 2.8 %collective-permute-start.29 = (bf16[8,7168]{1,0:T(8,128)(2,1)S(1)}, bf16[8,7168]{1,0:T(8,128)(2,1)S(1)}, u32[]{:S(2)}, u32[]{:S(2)}) collective-permute-start(bf16[8,7168]{1,0:T(8,128)(2,1)S(1)} %get-tuple-element.66), channel_id=1, source_target_pairs={{0,1},{1,0},{2,3},{3,2},{4,5},{5,4},{6,7},{7,6},{8,9},{9,8},{10,11... | collective-permute-start | bytes 344072 | tf_op jit(solution)/shard_map/ppermute | solution.py:26
  52.0 3.7 %collective-permute-start.31 = (bf16[8,7168]{1,0:T(8,128)(2,1)S(1)}, bf16[8,7168]{1,0:T(8,128)(2,1)S(1)}, u32[]{:S(2)}, u32[]{:S(2)}) collective-permute-start(bf16[8,7168]{1,0:T(8,128)(2,1)S(1)} %get-tuple-element.68), channel_id=1, source_target_pairs={{0,1},{1,0},{2,3},{3,2},{4,5},{5,4},{6,7},{7,6},{8,9},{9,8},{10,11... | collective-permute-start | bytes 344072 | tf_op jit(solution)/shard_map/ppermute | solution.py:26
  52.3 6.1 %collective-permute-start.26 = (bf16[8,7168]{1,0:T(8,128)(2,1)S(1)}, bf16[8,7168]{1,0:T(8,128)(2,1)S(1)}, u32[]{:S(2)}, u32[]{:S(2)}) collective-permute-start(bf16[8,7168]{1,0:T(8,128)(2,1)S(1)} %get-tuple-element.62), channel_id=1, source_target_pairs={{0,1},{1,0},{2,3},{3,2},{4,5},{5,4},{6,7},{7,6},{8,9},{9,8},{10,11... | collective-permute-start | bytes 344072 | tf_op jit(solution)/shard_map/ppermute | solution.py:26
  52.8 6.9 %collective-permute-start.28 = (bf16[8,7168]{1,0:T(8,128)(2,1)S(1)}, bf16[8,7168]{1,0:T(8,128)(2,1)S(1)}, u32[]{:S(2)}, u32[]{:S(2)}) collective-permute-start(bf16[8,7168]{1,0:T(8,128)(2,1)S(1)} %shard_map.84), channel_id=1, source_target_pairs={{0,6},{1,7},{2,4},{3,5},{4,2},{5,3},{6,0},{7,1},{8,14},{9,15},{10,... | collective-permute-start | bytes 344072 | tf_op jit(solution)/shard_map/ppermute | solution.py:26
  54.6 6.6 %collective-permute-start.30 = (bf16[8,7168]{1,0:T(8,128)(2,1)S(1)}, bf16[8,7168]{1,0:T(8,128)(2,1)S(1)}, u32[]{:S(2)}, u32[]{:S(2)}) collective-permute-start(bf16[8,7168]{1,0:T(8,128)(2,1)S(1)} %shard_map.85), channel_id=1, source_target_pairs={{0,4},{1,5},{2,6},{3,7},{4,0},{5,1},{6,2},{7,3},{8,12},{9,13},{10,... | collective-permute-start | bytes 344072 | tf_op jit(solution)/shard_map/ppermute | solution.py:26
  55.7 5.9 %collective-permute-start.32 = (bf16[8,7168]{1,0:T(8,128)(2,1)S(1)}, bf16[8,7168]{1,0:T(8,128)(2,1)S(1)}, u32[]{:S(2)}, u32[]{:S(2)}) collective-permute-start(bf16[8,7168]{1,0:T(8,128)(2,1)S(1)} %shard_map.86), channel_id=1, source_target_pairs={{0,2},{1,3},{2,0},{3,1},{4,6},{5,7},{6,4},{7,5},{8,10},{9,11},{10,... | collective-permute-start | bytes 344072 | tf_op jit(solution)/shard_map/ppermute | solution.py:26
  56.6 8.3 %collective-permute-start.18 = (bf16[4,7168]{1,0:T(4,128)(2,1)S(1)}, bf16[4,7168]{1,0:T(4,128)(2,1)S(1)}, u32[]{:S(2)}, u32[]{:S(2)}) collective-permute-start(bf16[4,7168]{1,0:T(4,128)(2,1)S(1)} %get-tuple-element.58), channel_id=1, source_target_pairs={{0,16},{1,17},{2,18},{3,19},{4,20},{5,21},{6,22},{7,23},{8,24},{9,... | collective-permute-start | bytes 172040 | tf_op jit(solution)/shard_map/ppermute | solution.py:26
  61.7 6.7 %collective-permute-start.33 = (bf16[4,7168]{1,0:T(4,128)(2,1)S(1)}, bf16[4,7168]{1,0:T(4,128)(2,1)S(1)}, u32[]{:S(2)}, u32[]{:S(2)}) collective-permute-start(bf16[4,7168]{1,0:T(4,128)(2,1)S(1)} %get-tuple-element.69), channel_id=1, source_target_pairs={{0,24},{1,25},{2,26},{3,27},{4,28},{5,29},{6,30},{7,31},{8,16},{9,... | collective-permute-start | bytes 172040 | tf_op jit(solution)/shard_map/ppermute | solution.py:26
  64.0 4.3 %collective-permute-start.34 = (bf16[4,7168]{1,0:T(4,128)(2,1)S(1)}, bf16[4,7168]{1,0:T(4,128)(2,1)S(1)}, u32[]{:S(2)}, u32[]{:S(2)}) collective-permute-start(bf16[4,7168]{1,0:T(4,128)(2,1)S(1)} %get-tuple-element.70), channel_id=1, source_target_pairs={{0,16},{1,17},{2,18},{3,19},{4,20},{5,21},{6,22},{7,23},{8,24},{9,... | collective-permute-start | bytes 172040 | tf_op jit(solution)/shard_map/ppermute | solution.py:26

commit v23 on v22

--- a/solution.py
+++ b/solution.py
@@ -9,7 +9,7 @@
 
 GROUP = 4
 LANES = 128
-CHUNK = 1024
+CHUNK = 1792
 VMEM_LIMIT = 16 * 1024 * 1024
 VMEM = pl.BlockSpec(memory_space=pltpu.VMEM)
 

time: 69.2 us -> 69.2 us (level)
  no operation moved by 1% of the time
where the time goes in v23:
time: 69.2 us; the launch traced here: 69 us
  starting transfers between devices  32.3 us (47%)
  waiting for transfers between devices  24.9 us (36%)
  Pallas kernels  11.7 us (17%)
    ppermute x35, starting transfers between devices, exchange(): return lax.ppermute(value, ('segment', 'expert'), pairs)  32.3 us
    ppermute x35, waiting for transfers between devices, exchange(): return lax.ppermute(value, ('segment', 'expert'), pairs)  24.9 us
    pallas_call x14, Pallas kernels, call(): pl.pallas_call(kernel, out_shape=[jax.ShapeDtypeStruct(shape, jnp.bfloat1...  6.46 us
    pallas_call x2, Pallas kernels, load(): pl.pallas_call(functools.partial(load_kernel, count), out_shape=[pltpu.VM...  5.22 us
  transfers between devices with their start and end apart: 35, of which 21 were waited for; matrix products, arithmetic and copies ran while one was open for 0% of the time, Pallas kernels for 8%

profile of v23, /device:TPU:0, one launch (start us, length us, event | category | flops | bytes accessed | tf_op | source)
XLA Modules:
  0.0 69.0 jit_solution(79820364301289603)
XLA Ops:
  0.0 0.9 %shard_map.73.own_ref = bf16[4,7296]{1,0:T(4,128)(2,1)S(1)} custom-call(bf16[1,4,7168]{2,1,0:T(4,128)(2,1)} %states_hbm.1, s32[1,2,2,4]{3,2,1,0:T(2,128)} %bitcast.3, bf16[1,2,2,4]{3,2,1,0:T(2,128)(2,1)} %bitcast.4), custom_call_target="tpu_custom_call" | custom-call | tf_op jit(solution)/shard_map/pallas_call | solution.py:43
  0.9 0.0 copy-start
  0.9 4.1 %collective-permute-start = (bf16[4,7296]{1,0:T(4,128)(2,1)S(1)}, bf16[4,7296]{1,0:T(4,128)(2,1)S(1)}, u32[]{:S(2)}, u32[]{:S(2)}) collective-permute-start(bf16[4,7296]{1,0:T(4,128)(2,1)S(1)} %shard_map.73.own_ref), channel_id=1, source_target_pairs={{0,8},{1,9},{2,10},{3,11},{4,12},{5,13},{6,14},{7,15},{8,0},{9,1},... | collective-permute-start | bytes 175112 | tf_op jit(solution)/shard_map/ppermute | solution.py:26
  5.0 2.0 %shard_map.74.refs_8_.refs_9_ = bf16[1,7168,256]{2,1,0:T(8,128)(2,1)S(1)} custom-call(bf16[1,7168,256]{2,1,0:T(8,128)(2,1)} %refs_0_.1), custom_call_target="tpu_custom_call" | custom-call | bytes 3670016 | tf_op jit(solution)/shard_map/pallas_call | solution.py:64
  7.1 0.7 %collective-permute-done.far_ref = bf16[4,7296]{1,0:T(4,128)(2,1)S(1)} collective-permute-done((bf16[4,7296]{1,0:T(4,128)(2,1)S(1)}, bf16[4,7296]{1,0:T(4,128)(2,1)S(1)}, u32[]{:S(2)}, u32[]{:S(2)}) %collective-permute-start) | collective-permute-done | bytes 58400 | tf_op jit(solution)/shard_map/ppermute | solution.py:26
  7.8 0.2 shard_map.75
  8.0 2.4 %collective-permute-start.4 = (bf16[8,7296]{1,0:T(8,128)(2,1)S(1)}, bf16[8,7296]{1,0:T(8,128)(2,1)S(1)}, u32[]{:S(2)}, u32[]{:S(2)}) collective-permute-start(bf16[8,7296]{1,0:T(8,128)(2,1)S(1)} %get-tuple-element.46.refs_0_), channel_id=1, source_target_pairs={{0,6},{1,7},{2,4},{3,5},{4,2},{5,3},{6,0},{7,1},{8,14},{9,15},{10,... | collective-permute-start | bytes 350216 | tf_op jit(solution)/shard_map/ppermute | solution.py:26
  10.4 1.5 %collective-permute-start.3 = (bf16[8,7296]{1,0:T(8,128)(2,1)S(1)}, bf16[8,7296]{1,0:T(8,128)(2,1)S(1)}, u32[]{:S(2)}, u32[]{:S(2)}) collective-permute-start(bf16[8,7296]{1,0:T(8,128)(2,1)S(1)} %get-tuple-element.46.refs_0_), channel_id=1, source_target_pairs={{0,4},{1,5},{2,6},{3,7},{4,0},{5,1},{6,2},{7,3},{8,12},{9,13},{10,... | collective-permute-start | bytes 350216 | tf_op jit(solution)/shard_map/ppermute | solution.py:26
  11.8 0.0 collective-permute-start.2
  11.8 3.2 %shard_map.76 = (bf16[1,7168,256]{2,1,0:T(8,128)(2,1)S(1)}, bf16[1,256,7168]{2,1,0:T(8,128)(2,1)S(1)}) custom-call(bf16[1,7168,256]{2,1,0:T(8,128)(2,1)} %refs_0_.2, bf16[1,256,7168]{2,1,0:T(8,128)(2,1)} %refs_1_), custom_call_target="tpu_custom_call" | custom-call | bytes 7340032 | tf_op jit(solution)/shard_map/pallas_call | solution.py:64
  15.0 0.1 collective-permute-start.5
  15.1 0.0 collective-permute-done.4.refs_3_
  15.1 0.5 collective-permute-start.8
  15.6 0.3 collective-permute-done.3.refs_2_
  15.9 0.8 %collective-permute-done.2.refs_1_ = bf16[8,7296]{1,0:T(8,128)(2,1)S(1)} collective-permute-done((bf16[8,7296]{1,0:T(8,128)(2,1)S(1)}, bf16[8,7296]{1,0:T(8,128)(2,1)S(1)}, u32[]{:S(2)}, u32[]{:S(2)}) %collective-permute-start.2) | collective-permute-done | bytes 116768 | tf_op jit(solution)/shard_map/ppermute | solution.py:26
  16.7 0.0 collective-permute-start.6
  16.7 0.5 collective-permute-done.7.refs_6_
  17.2 0.8 %collective-permute-done.6.refs_5_ = bf16[8,7296]{1,0:T(8,128)(2,1)S(1)} collective-permute-done((bf16[8,7296]{1,0:T(8,128)(2,1)S(1)}, bf16[8,7296]{1,0:T(8,128)(2,1)S(1)}, u32[]{:S(2)}, u32[]{:S(2)}) %collective-permute-start.6) | collective-permute-done | bytes 116768 | tf_op jit(solution)/shard_map/ppermute | solution.py:26
  18.0 2.1 %shard_map.77 = (bf16[8,7168]{1,0:T(8,128)(2,1)S(1)}, bf16[8,7168]{1,0:T(8,128)(2,1)S(1)}, bf16[8,7168]{1,0:T(8,128)(2,1)S(1)}, bf16[8,7168]{1,0:T(8,128)(2,1)S(...) custom-call(bf16[8,7296]{1,0:T(8,128)(2,1)S(1)} %get-tuple-element.4, ...), custom_call_target="tpu_custom_call" | custom-call | flops 704643072 | bytes 11010048 | tf_op jit(solution)/shard_map/pallas_call | solution.py:43
  20.1 0.2 collective-permute-start.10
  20.3 0.4 collective-permute-start.12
  20.7 0.2 collective-permute-start.14
  20.8 0.4 collective-permute-start.9
  21.2 0.3 collective-permute-done.10.refs_1_
  21.5 1.3 %collective-permute-start.11 = (bf16[8,7168]{1,0:T(8,128)(2,1)S(1)}, bf16[8,7168]{1,0:T(8,128)(2,1)S(1)}, u32[]{:S(2)}, u32[]{:S(2)}) collective-permute-start(bf16[8,7168]{1,0:T(8,128)(2,1)S(1)} %shard_map.78), channel_id=1, source_target_pairs={{0,6},{1,7},{2,4},{3,5},{4,2},{5,3},{6,0},{7,1},{8,14},{9,15},{10,... | collective-permute-start | bytes 344072 | tf_op jit(solution)/shard_map/ppermute | solution.py:26
  22.9 1.4 %collective-permute-start.13 = (bf16[8,7168]{1,0:T(8,128)(2,1)S(1)}, bf16[8,7168]{1,0:T(8,128)(2,1)S(1)}, u32[]{:S(2)}, u32[]{:S(2)}) collective-permute-start(bf16[8,7168]{1,0:T(8,128)(2,1)S(1)} %shard_map.79), channel_id=1, source_target_pairs={{0,4},{1,5},{2,6},{3,7},{4,0},{5,1},{6,2},{7,3},{8,12},{9,13},{10,... | collective-permute-start | bytes 344072 | tf_op jit(solution)/shard_map/ppermute | solution.py:26
  24.3 0.9 %collective-permute-start.15 = (bf16[8,7168]{1,0:T(8,128)(2,1)S(1)}, bf16[8,7168]{1,0:T(8,128)(2,1)S(1)}, u32[]{:S(2)}, u32[]{:S(2)}) collective-permute-start(bf16[8,7168]{1,0:T(8,128)(2,1)S(1)} %shard_map.80), channel_id=1, source_target_pairs={{0,2},{1,3},{2,0},{3,1},{4,6},{5,7},{6,4},{7,5},{8,10},{9,11},{10,... | collective-permute-start | bytes 344072 | tf_op jit(solution)/shard_map/ppermute | solution.py:26
  25.3 1.5 %collective-permute-start.1 = (bf16[8,7168]{1,0:T(8,128)(2,1)S(1)}, bf16[8,7168]{1,0:T(8,128)(2,1)S(1)}, u32[]{:S(2)}, u32[]{:S(2)}) collective-permute-start(bf16[8,7168]{1,0:T(8,128)(2,1)S(1)} %get-tuple-element.39), channel_id=1, source_target_pairs={{0,16},{1,17},{2,18},{3,19},{4,20},{5,21},{6,22},{7,23},{8,24},{9,... | collective-permute-start | bytes 344072 | tf_op jit(solution)/shard_map/ppermute | solution.py:26
  26.8 1.7 %collective-permute-done.11.refs_2_ = bf16[8,7168]{1,0:T(8,128)(2,1)S(1)} collective-permute-done((bf16[8,7168]{1,0:T(8,128)(2,1)S(1)}, bf16[8,7168]{1,0:T(8,128)(2,1)S(1)}, u32[]{:S(2)}, u32[]{:S(2)}) %collective-permute-start.11) | collective-permute-done | bytes 114720 | tf_op jit(solution)/shard_map/ppermute | solution.py:26
  28.5 1.6 %collective-permute-done.13.refs_3_ = bf16[8,7168]{1,0:T(8,128)(2,1)S(1)} collective-permute-done((bf16[8,7168]{1,0:T(8,128)(2,1)S(1)}, bf16[8,7168]{1,0:T(8,128)(2,1)S(1)}, u32[]{:S(2)}, u32[]{:S(2)}) %collective-permute-start.13) | collective-permute-done | bytes 114720 | tf_op jit(solution)/shard_map/ppermute | solution.py:26
  30.0 0.1 collective-permute-done.15.refs_4_
  30.2 0.1 shard_map.81
  30.2 3.4 %collective-permute-start.17 = (bf16[8,7168]{1,0:T(8,128)(2,1)S(1)}, bf16[8,7168]{1,0:T(8,128)(2,1)S(1)}, u32[]{:S(2)}, u32[]{:S(2)}) collective-permute-start(bf16[8,7168]{1,0:T(8,128)(2,1)S(1)} %shard_map.81), channel_id=1, source_target_pairs={{0,24},{1,25},{2,26},{3,27},{4,28},{5,29},{6,30},{7,31},{8,16},{9,... | collective-permute-start | bytes 344072 | tf_op jit(solution)/shard_map/ppermute | solution.py:26
  33.6 0.5 collective-permute-start.16
  34.2 5.3 %collective-permute-done.17.far_ref = bf16[8,7168]{1,0:T(8,128)(2,1)S(1)} collective-permute-done((bf16[8,7168]{1,0:T(8,128)(2,1)S(1)}, bf16[8,7168]{1,0:T(8,128)(2,1)S(1)}, u32[]{:S(2)}, u32[]{:S(2)}) %collective-permute-start.17) | collective-permute-done | bytes 114720 | tf_op jit(solution)/shard_map/ppermute | solution.py:26
  39.4 0.6 collective-permute-done.16.near_ref
  40.0 0.2 shard_map.82
  40.2 1.4 %collective-permute-start.21 = (bf16[8,7168]{1,0:T(8,128)(2,1)S(1)}, bf16[8,7168]{1,0:T(8,128)(2,1)S(1)}, u32[]{:S(2)}, u32[]{:S(2)}) collective-permute-start(bf16[8,7168]{1,0:T(8,128)(2,1)S(1)} %get-tuple-element.59.refs_0_), channel_id=1, source_target_pairs={{0,6},{1,7},{2,4},{3,5},{4,2},{5,3},{6,0},{7,1},{8,14},{9,15},{10,... | collective-permute-start | bytes 344072 | tf_op jit(solution)/shard_map/ppermute | solution.py:26
  41.6 1.1 %collective-permute-start.20 = (bf16[8,7168]{1,0:T(8,128)(2,1)S(1)}, bf16[8,7168]{1,0:T(8,128)(2,1)S(1)}, u32[]{:S(2)}, u32[]{:S(2)}) collective-permute-start(bf16[8,7168]{1,0:T(8,128)(2,1)S(1)} %get-tuple-element.59.refs_0_), channel_id=1, source_target_pairs={{0,4},{1,5},{2,6},{3,7},{4,0},{5,1},{6,2},{7,3},{8,12},{9,13},{10,... | collective-permute-start | bytes 344072 | tf_op jit(solution)/shard_map/ppermute | solution.py:26
  42.7 1.1 %collective-permute-start.19 = (bf16[8,7168]{1,0:T(8,128)(2,1)S(1)}, bf16[8,7168]{1,0:T(8,128)(2,1)S(1)}, u32[]{:S(2)}, u32[]{:S(2)}) collective-permute-start(bf16[8,7168]{1,0:T(8,128)(2,1)S(1)} %get-tuple-element.59.refs_0_), channel_id=1, source_target_pairs={{0,2},{1,3},{2,0},{3,1},{4,6},{5,7},{6,4},{7,5},{8,10},{9,11},{10,... | collective-permute-start | bytes 344072 | tf_op jit(solution)/shard_map/ppermute | solution.py:26
  43.8 2.5 %collective-permute-done.21.refs_3_ = bf16[8,7168]{1,0:T(8,128)(2,1)S(1)} collective-permute-done((bf16[8,7168]{1,0:T(8,128)(2,1)S(1)}, bf16[8,7168]{1,0:T(8,128)(2,1)S(1)}, u32[]{:S(2)}, u32[]{:S(2)}) %collective-permute-start.21) | collective-permute-done | bytes 114720 | tf_op jit(solution)/shard_map/ppermute | solution.py:26
  46.3 1.4 %collective-permute-done.20.refs_2_ = bf16[8,7168]{1,0:T(8,128)(2,1)S(1)} collective-permute-done((bf16[8,7168]{1,0:T(8,128)(2,1)S(1)}, bf16[8,7168]{1,0:T(8,128)(2,1)S(1)}, u32[]{:S(2)}, u32[]{:S(2)}) %collective-permute-start.20) | collective-permute-done | bytes 114720 | tf_op jit(solution)/shard_map/ppermute | solution.py:26
  47.7 0.2 collective-permute-done.19.refs_1_
  48.0 0.3 collective-permute-start.23
  48.2 0.8 %collective-permute-done.24.refs_6_ = bf16[8,7168]{1,0:T(8,128)(2,1)S(1)} collective-permute-done((bf16[8,7168]{1,0:T(8,128)(2,1)S(1)}, bf16[8,7168]{1,0:T(8,128)(2,1)S(1)}, u32[]{:S(2)}, u32[]{:S(2)}) %collective-permute-start.24) | collective-permute-done | bytes 114720 | tf_op jit(solution)/shard_map/ppermute | solution.py:26
  49.1 0.2 collective-permute-done.23.refs_5_
  49.3 2.1 %shard_map.83 = (bf16[8,7168]{1,0:T(8,128)(2,1)S(1)}, bf16[8,7168]{1,0:T(8,128)(2,1)S(1)}, bf16[8,7168]{1,0:T(8,128)(2,1)S(1)}, bf16[8,7168]{1,0:T(8,128)(2,1)S(...) custom-call(bf16[8,7168]{1,0:T(8,128)(2,1)S(1)} %get-tuple-element.5, ...), custom_call_target="tpu_custom_call" | custom-call | flops 704643072 | bytes 11010048 | tf_op jit(solution)/shard_map/pallas_call | solution.py:43
  51.4 0.3 collective-permute-start.27
  51.8 0.2 collective-permute-start.29
  52.0 0.3 collective-permute-start.31
  52.3 0.2 collective-permute-start.26
  52.5 0.3 collective-permute-done.27.refs_1_
  52.8 1.8 %collective-permute-start.28 = (bf16[8,7168]{1,0:T(8,128)(2,1)S(1)}, bf16[8,7168]{1,0:T(8,128)(2,1)S(1)}, u32[]{:S(2)}, u32[]{:S(2)}) collective-permute-start(bf16[8,7168]{1,0:T(8,128)(2,1)S(1)} %shard_map.84), channel_id=1, source_target_pairs={{0,6},{1,7},{2,4},{3,5},{4,2},{5,3},{6,0},{7,1},{8,14},{9,15},{10,... | collective-permute-start | bytes 344072 | tf_op jit(solution)/shard_map/ppermute | solution.py:26
  54.6 1.1 %collective-permute-start.30 = (bf16[8,7168]{1,0:T(8,128)(2,1)S(1)}, bf16[8,7168]{1,0:T(8,128)(2,1)S(1)}, u32[]{:S(2)}, u32[]{:S(2)}) collective-permute-start(bf16[8,7168]{1,0:T(8,128)(2,1)S(1)} %shard_map.85), channel_id=1, source_target_pairs={{0,4},{1,5},{2,6},{3,7},{4,0},{5,1},{6,2},{7,3},{8,12},{9,13},{10,... | collective-permute-start | bytes 344072 | tf_op jit(solution)/shard_map/ppermute | solution.py:26
  55.7 0.9 %collective-permute-start.32 = (bf16[8,7168]{1,0:T(8,128)(2,1)S(1)}, bf16[8,7168]{1,0:T(8,128)(2,1)S(1)}, u32[]{:S(2)}, u32[]{:S(2)}) collective-permute-start(bf16[8,7168]{1,0:T(8,128)(2,1)S(1)} %shard_map.86), channel_id=1, source_target_pairs={{0,2},{1,3},{2,0},{3,1},{4,6},{5,7},{6,4},{7,5},{8,10},{9,11},{10,... | collective-permute-start | bytes 344072 | tf_op jit(solution)/shard_map/ppermute | solution.py:26
  56.6 1.7 %collective-permute-start.18 = (bf16[4,7168]{1,0:T(4,128)(2,1)S(1)}, bf16[4,7168]{1,0:T(4,128)(2,1)S(1)}, u32[]{:S(2)}, u32[]{:S(2)}) collective-permute-start(bf16[4,7168]{1,0:T(4,128)(2,1)S(1)} %get-tuple-element.58), channel_id=1, source_target_pairs={{0,16},{1,17},{2,18},{3,19},{4,20},{5,21},{6,22},{7,23},{8,24},{9,... | collective-permute-start | bytes 172040 | tf_op jit(solution)/shard_map/ppermute | solution.py:26
  58.3 1.4 %collective-permute-done.28.refs_2_ = bf16[8,7168]{1,0:T(8,128)(2,1)S(1)} collective-permute-done((bf16[8,7168]{1,0:T(8,128)(2,1)S(1)}, bf16[8,7168]{1,0:T(8,128)(2,1)S(1)}, u32[]{:S(2)}, u32[]{:S(2)}) %collective-permute-start.28) | collective-permute-done | bytes 114720 | tf_op jit(solution)/shard_map/ppermute | solution.py:26
  59.8 1.4 %collective-permute-done.30.refs_3_ = bf16[8,7168]{1,0:T(8,128)(2,1)S(1)} collective-permute-done((bf16[8,7168]{1,0:T(8,128)(2,1)S(1)}, bf16[8,7168]{1,0:T(8,128)(2,1)S(1)}, u32[]{:S(2)}, u32[]{:S(2)}) %collective-permute-start.30) | collective-permute-done | bytes 114720 | tf_op jit(solution)/shard_map/ppermute | solution.py:26
  61.2 0.4 collective-permute-done.32.refs_4_
  61.6 0.1 shard_map.87
  61.7 2.4 %collective-permute-start.33 = (bf16[4,7168]{1,0:T(4,128)(2,1)S(1)}, bf16[4,7168]{1,0:T(4,128)(2,1)S(1)}, u32[]{:S(2)}, u32[]{:S(2)}) collective-permute-start(bf16[4,7168]{1,0:T(4,128)(2,1)S(1)} %get-tuple-element.69), channel_id=1, source_target_pairs={{0,24},{1,25},{2,26},{3,27},{4,28},{5,29},{6,30},{7,31},{8,16},{9,... | collective-permute-start | bytes 172040 | tf_op jit(solution)/shard_map/ppermute | solution.py:26
  64.1 0.8 %collective-permute-start.34 = (bf16[4,7168]{1,0:T(4,128)(2,1)S(1)}, bf16[4,7168]{1,0:T(4,128)(2,1)S(1)}, u32[]{:S(2)}, u32[]{:S(2)}) collective-permute-start(bf16[4,7168]{1,0:T(4,128)(2,1)S(1)} %get-tuple-element.70), channel_id=1, source_target_pairs={{0,16},{1,17},{2,18},{3,19},{4,20},{5,21},{6,22},{7,23},{8,24},{9,... | collective-permute-start | bytes 172040 | tf_op jit(solution)/shard_map/ppermute | solution.py:26
  64.9 3.4 %collective-permute-done.33.refs_1_ = bf16[4,7168]{1,0:T(4,128)(2,1)S(1)} collective-permute-done((bf16[4,7168]{1,0:T(4,128)(2,1)S(1)}, bf16[4,7168]{1,0:T(4,128)(2,1)S(1)}, u32[]{:S(2)}, u32[]{:S(2)}) %collective-permute-start.33) | collective-permute-done | bytes 57376 | tf_op jit(solution)/shard_map/ppermute | solution.py:26
  68.3 0.7 shard_map.88
  (24 shorter events, 0.2 us)
Async XLA Ops:
  0.9 6.9 %copy-start = (f32[1,7168]{1,0:T(1,128)S(1)}, f32[1,7168]{1,0:T(1,128)}, u32[]{:S(2)}) copy-start(f32[1,7168]{1,0:T(1,128)} %gain_ref.3) | copy-start | bytes 86020
  0.9 6.9 %collective-permute-start = (bf16[4,7296]{1,0:T(4,128)(2,1)S(1)}, bf16[4,7296]{1,0:T(4,128)(2,1)S(1)}, u32[]{:S(2)}, u32[]{:S(2)}) collective-permute-start(bf16[4,7296]{1,0:T(4,128)(2,1)S(1)} %shard_map.73.own_ref), channel_id=1, source_target_pairs={{0,8},{1,9},{2,10},{3,11},{4,12},{5,13},{6,14},{7,15},{8,0},{9,1},... | collective-permute-start | bytes 175112 | tf_op jit(solution)/shard_map/ppermute | solution.py:26
  8.0 7.1 %collective-permute-start.4 = (bf16[8,7296]{1,0:T(8,128)(2,1)S(1)}, bf16[8,7296]{1,0:T(8,128)(2,1)S(1)}, u32[]{:S(2)}, u32[]{:S(2)}) collective-permute-start(bf16[8,7296]{1,0:T(8,128)(2,1)S(1)} %get-tuple-element.46.refs_0_), channel_id=1, source_target_pairs={{0,6},{1,7},{2,4},{3,5},{4,2},{5,3},{6,0},{7,1},{8,14},{9,15},{10,... | collective-permute-start | bytes 350216 | tf_op jit(solution)/shard_map/ppermute | solution.py:26
  10.4 5.5 %collective-permute-start.3 = (bf16[8,7296]{1,0:T(8,128)(2,1)S(1)}, bf16[8,7296]{1,0:T(8,128)(2,1)S(1)}, u32[]{:S(2)}, u32[]{:S(2)}) collective-permute-start(bf16[8,7296]{1,0:T(8,128)(2,1)S(1)} %get-tuple-element.46.refs_0_), channel_id=1, source_target_pairs={{0,4},{1,5},{2,6},{3,7},{4,0},{5,1},{6,2},{7,3},{8,12},{9,13},{10,... | collective-permute-start | bytes 350216 | tf_op jit(solution)/shard_map/ppermute | solution.py:26
  11.8 4.8 %collective-permute-start.2 = (bf16[8,7296]{1,0:T(8,128)(2,1)S(1)}, bf16[8,7296]{1,0:T(8,128)(2,1)S(1)}, u32[]{:S(2)}, u32[]{:S(2)}) collective-permute-start(bf16[8,7296]{1,0:T(8,128)(2,1)S(1)} %get-tuple-element.46.refs_0_), channel_id=1, source_target_pairs={{0,2},{1,3},{2,0},{3,1},{4,6},{5,7},{6,4},{7,5},{8,10},{9,11},{10,... | collective-permute-start | bytes 350216 | tf_op jit(solution)/shard_map/ppermute | solution.py:26
  15.0 1.6 %collective-permute-start.5 = (bf16[8,7296]{1,0:T(8,128)(2,1)S(1)}, bf16[8,7296]{1,0:T(8,128)(2,1)S(1)}, u32[]{:S(2)}, u32[]{:S(2)}) collective-permute-start(bf16[8,7296]{1,0:T(8,128)(2,1)S(1)} %get-tuple-element.46.refs_0_), channel_id=1, source_target_pairs={{0,1},{1,0},{2,3},{3,2},{4,5},{5,4},{6,7},{7,6},{8,9},{9,8},{10,11... | collective-permute-start | bytes 350216 | tf_op jit(solution)/shard_map/ppermute | solution.py:26
  15.1 1.5 %collective-permute-start.8 = (bf16[8,7296]{1,0:T(8,128)(2,1)S(1)}, bf16[8,7296]{1,0:T(8,128)(2,1)S(1)}, u32[]{:S(2)}, u32[]{:S(2)}) collective-permute-start(bf16[8,7296]{1,0:T(8,128)(2,1)S(1)} %collective-permute-done.4.refs_3_), channel_id=1, source_target_pairs={{0,1},{1,0},{2,3},{3,2},{4,5},{5,4},{6,7},{7,6},{8,9},{9,8},{10,11... | collective-permute-start | bytes 350216 | tf_op jit(solution)/shard_map/ppermute | solution.py:26
  15.9 1.3 %collective-permute-start.7 = (bf16[8,7296]{1,0:T(8,128)(2,1)S(1)}, bf16[8,7296]{1,0:T(8,128)(2,1)S(1)}, u32[]{:S(2)}, u32[]{:S(2)}) collective-permute-start(bf16[8,7296]{1,0:T(8,128)(2,1)S(1)} %collective-permute-done.3.refs_2_), channel_id=1, source_target_pairs={{0,1},{1,0},{2,3},{3,2},{4,5},{5,4},{6,7},{7,6},{8,9},{9,8},{10,11... | collective-permute-start | bytes 350216 | tf_op jit(solution)/shard_map/ppermute | solution.py:26
  16.7 1.3 %collective-permute-start.6 = (bf16[8,7296]{1,0:T(8,128)(2,1)S(1)}, bf16[8,7296]{1,0:T(8,128)(2,1)S(1)}, u32[]{:S(2)}, u32[]{:S(2)}) collective-permute-start(bf16[8,7296]{1,0:T(8,128)(2,1)S(1)} %collective-permute-done.2.refs_1_), channel_id=1, source_target_pairs={{0,1},{1,0},{2,3},{3,2},{4,5},{5,4},{6,7},{7,6},{8,9},{9,8},{10,11... | collective-permute-start | bytes 350216 | tf_op jit(solution)/shard_map/ppermute | solution.py:26
  20.1 1.4 %collective-permute-start.10 = (bf16[8,7168]{1,0:T(8,128)(2,1)S(1)}, bf16[8,7168]{1,0:T(8,128)(2,1)S(1)}, u32[]{:S(2)}, u32[]{:S(2)}) collective-permute-start(bf16[8,7168]{1,0:T(8,128)(2,1)S(1)} %get-tuple-element.53), channel_id=1, source_target_pairs={{0,1},{1,0},{2,3},{3,2},{4,5},{5,4},{6,7},{7,6},{8,9},{9,8},{10,11... | collective-permute-start | bytes 344072 | tf_op jit(solution)/shard_map/ppermute | solution.py:26
  20.3 2.5 %collective-permute-start.12 = (bf16[8,7168]{1,0:T(8,128)(2,1)S(1)}, bf16[8,7168]{1,0:T(8,128)(2,1)S(1)}, u32[]{:S(2)}, u32[]{:S(2)}) collective-permute-start(bf16[8,7168]{1,0:T(8,128)(2,1)S(1)} %get-tuple-element.55), channel_id=1, source_target_pairs={{0,1},{1,0},{2,3},{3,2},{4,5},{5,4},{6,7},{7,6},{8,9},{9,8},{10,11... | collective-permute-start | bytes 344072 | tf_op jit(solution)/shard_map/ppermute | solution.py:26
  20.7 3.6 %collective-permute-start.14 = (bf16[8,7168]{1,0:T(8,128)(2,1)S(1)}, bf16[8,7168]{1,0:T(8,128)(2,1)S(1)}, u32[]{:S(2)}, u32[]{:S(2)}) collective-permute-start(bf16[8,7168]{1,0:T(8,128)(2,1)S(1)} %get-tuple-element.57), channel_id=1, source_target_pairs={{0,1},{1,0},{2,3},{3,2},{4,5},{5,4},{6,7},{7,6},{8,9},{9,8},{10,11... | collective-permute-start | bytes 344072 | tf_op jit(solution)/shard_map/ppermute | solution.py:26
  20.8 5.9 %collective-permute-start.9 = (bf16[8,7168]{1,0:T(8,128)(2,1)S(1)}, bf16[8,7168]{1,0:T(8,128)(2,1)S(1)}, u32[]{:S(2)}, u32[]{:S(2)}) collective-permute-start(bf16[8,7168]{1,0:T(8,128)(2,1)S(1)} %get-tuple-element.51), channel_id=1, source_target_pairs={{0,1},{1,0},{2,3},{3,2},{4,5},{5,4},{6,7},{7,6},{8,9},{9,8},{10,11... | collective-permute-start | bytes 344072 | tf_op jit(solution)/shard_map/ppermute | solution.py:26
  21.5 7.0 %collective-permute-start.11 = (bf16[8,7168]{1,0:T(8,128)(2,1)S(1)}, bf16[8,7168]{1,0:T(8,128)(2,1)S(1)}, u32[]{:S(2)}, u32[]{:S(2)}) collective-permute-start(bf16[8,7168]{1,0:T(8,128)(2,1)S(1)} %shard_map.78), channel_id=1, source_target_pairs={{0,6},{1,7},{2,4},{3,5},{4,2},{5,3},{6,0},{7,1},{8,14},{9,15},{10,... | collective-permute-start | bytes 344072 | tf_op jit(solution)/shard_map/ppermute | solution.py:26
  22.9 7.2 %collective-permute-start.13 = (bf16[8,7168]{1,0:T(8,128)(2,1)S(1)}, bf16[8,7168]{1,0:T(8,128)(2,1)S(1)}, u32[]{:S(2)}, u32[]{:S(2)}) collective-permute-start(bf16[8,7168]{1,0:T(8,128)(2,1)S(1)} %shard_map.79), channel_id=1, source_target_pairs={{0,4},{1,5},{2,6},{3,7},{4,0},{5,1},{6,2},{7,3},{8,12},{9,13},{10,... | collective-permute-start | bytes 344072 | tf_op jit(solution)/shard_map/ppermute | solution.py:26
  24.3 5.8 %collective-permute-start.15 = (bf16[8,7168]{1,0:T(8,128)(2,1)S(1)}, bf16[8,7168]{1,0:T(8,128)(2,1)S(1)}, u32[]{:S(2)}, u32[]{:S(2)}) collective-permute-start(bf16[8,7168]{1,0:T(8,128)(2,1)S(1)} %shard_map.80), channel_id=1, source_target_pairs={{0,2},{1,3},{2,0},{3,1},{4,6},{5,7},{6,4},{7,5},{8,10},{9,11},{10,... | collective-permute-start | bytes 344072 | tf_op jit(solution)/shard_map/ppermute | solution.py:26
  25.3 8.9 %collective-permute-start.1 = (bf16[8,7168]{1,0:T(8,128)(2,1)S(1)}, bf16[8,7168]{1,0:T(8,128)(2,1)S(1)}, u32[]{:S(2)}, u32[]{:S(2)}) collective-permute-start(bf16[8,7168]{1,0:T(8,128)(2,1)S(1)} %get-tuple-element.39), channel_id=1, source_target_pairs={{0,16},{1,17},{2,18},{3,19},{4,20},{5,21},{6,22},{7,23},{8,24},{9,... | collective-permute-start | bytes 344072 | tf_op jit(solution)/shard_map/ppermute | solution.py:26
  30.2 9.2 %collective-permute-start.17 = (bf16[8,7168]{1,0:T(8,128)(2,1)S(1)}, bf16[8,7168]{1,0:T(8,128)(2,1)S(1)}, u32[]{:S(2)}, u32[]{:S(2)}) collective-permute-start(bf16[8,7168]{1,0:T(8,128)(2,1)S(1)} %shard_map.81), channel_id=1, source_target_pairs={{0,24},{1,25},{2,26},{3,27},{4,28},{5,29},{6,30},{7,31},{8,16},{9,... | collective-permute-start | bytes 344072 | tf_op jit(solution)/shard_map/ppermute | solution.py:26
  33.6 6.4 %collective-permute-start.16 = (bf16[8,7168]{1,0:T(8,128)(2,1)S(1)}, bf16[8,7168]{1,0:T(8,128)(2,1)S(1)}, u32[]{:S(2)}, u32[]{:S(2)}) collective-permute-start(bf16[8,7168]{1,0:T(8,128)(2,1)S(1)} %shard_map.81), channel_id=1, source_target_pairs={{0,16},{1,17},{2,18},{3,19},{4,20},{5,21},{6,22},{7,23},{8,24},{9,... | collective-permute-start | bytes 344072 | tf_op jit(solution)/shard_map/ppermute | solution.py:26
  40.2 6.1 %collective-permute-start.21 = (bf16[8,7168]{1,0:T(8,128)(2,1)S(1)}, bf16[8,7168]{1,0:T(8,128)(2,1)S(1)}, u32[]{:S(2)}, u32[]{:S(2)}) collective-permute-start(bf16[8,7168]{1,0:T(8,128)(2,1)S(1)} %get-tuple-element.59.refs_0_), channel_id=1, source_target_pairs={{0,6},{1,7},{2,4},{3,5},{4,2},{5,3},{6,0},{7,1},{8,14},{9,15},{10,... | collective-permute-start | bytes 344072 | tf_op jit(solution)/shard_map/ppermute | solution.py:26
  41.6 6.1 %collective-permute-start.20 = (bf16[8,7168]{1,0:T(8,128)(2,1)S(1)}, bf16[8,7168]{1,0:T(8,128)(2,1)S(1)}, u32[]{:S(2)}, u32[]{:S(2)}) collective-permute-start(bf16[8,7168]{1,0:T(8,128)(2,1)S(1)} %get-tuple-element.59.refs_0_), channel_id=1, source_target_pairs={{0,4},{1,5},{2,6},{3,7},{4,0},{5,1},{6,2},{7,3},{8,12},{9,13},{10,... | collective-permute-start | bytes 344072 | tf_op jit(solution)/shard_map/ppermute | solution.py:26
  42.7 5.2 %collective-permute-start.19 = (bf16[8,7168]{1,0:T(8,128)(2,1)S(1)}, bf16[8,7168]{1,0:T(8,128)(2,1)S(1)}, u32[]{:S(2)}, u32[]{:S(2)}) collective-permute-start(bf16[8,7168]{1,0:T(8,128)(2,1)S(1)} %get-tuple-element.59.refs_0_), channel_id=1, source_target_pairs={{0,2},{1,3},{2,0},{3,1},{4,6},{5,7},{6,4},{7,5},{8,10},{9,11},{10,... | collective-permute-start | bytes 344072 | tf_op jit(solution)/shard_map/ppermute | solution.py:26
  43.8 4.4 %collective-permute-start.22 = (bf16[8,7168]{1,0:T(8,128)(2,1)S(1)}, bf16[8,7168]{1,0:T(8,128)(2,1)S(1)}, u32[]{:S(2)}, u32[]{:S(2)}) collective-permute-start(bf16[8,7168]{1,0:T(8,128)(2,1)S(1)} %get-tuple-element.59.refs_0_), channel_id=1, source_target_pairs={{0,1},{1,0},{2,3},{3,2},{4,5},{5,4},{6,7},{7,6},{8,9},{9,8},{10,11... | collective-permute-start | bytes 344072 | tf_op jit(solution)/shard_map/ppermute | solution.py:26
  46.3 1.9 %collective-permute-start.25 = (bf16[8,7168]{1,0:T(8,128)(2,1)S(1)}, bf16[8,7168]{1,0:T(8,128)(2,1)S(1)}, u32[]{:S(2)}, u32[]{:S(2)}) collective-permute-start(bf16[8,7168]{1,0:T(8,128)(2,1)S(1)} %collective-permute-done.21.refs_3_), channel_id=1, source_target_pairs={{0,1},{1,0},{2,3},{3,2},{4,5},{5,4},{6,7},{7,6},{8,9},{9,8},{10,11... | collective-permute-start | bytes 344072 | tf_op jit(solution)/shard_map/ppermute | solution.py:26
  47.7 1.3 %collective-permute-start.24 = (bf16[8,7168]{1,0:T(8,128)(2,1)S(1)}, bf16[8,7168]{1,0:T(8,128)(2,1)S(1)}, u32[]{:S(2)}, u32[]{:S(2)}) collective-permute-start(bf16[8,7168]{1,0:T(8,128)(2,1)S(1)} %collective-permute-done.20.refs_2_), channel_id=1, source_target_pairs={{0,1},{1,0},{2,3},{3,2},{4,5},{5,4},{6,7},{7,6},{8,9},{9,8},{10,11... | collective-permute-start | bytes 344072 | tf_op jit(solution)/shard_map/ppermute | solution.py:26
  48.0 1.3 %collective-permute-start.23 = (bf16[8,7168]{1,0:T(8,128)(2,1)S(1)}, bf16[8,7168]{1,0:T(8,128)(2,1)S(1)}, u32[]{:S(2)}, u32[]{:S(2)}) collective-permute-start(bf16[8,7168]{1,0:T(8,128)(2,1)S(1)} %collective-permute-done.19.refs_1_), channel_id=1, source_target_pairs={{0,1},{1,0},{2,3},{3,2},{4,5},{5,4},{6,7},{7,6},{8,9},{9,8},{10,11... | collective-permute-start | bytes 344072 | tf_op jit(solution)/shard_map/ppermute | solution.py:26
  51.4 1.4 %collective-permute-start.27 = (bf16[8,7168]{1,0:T(8,128)(2,1)S(1)}, bf16[8,7168]{1,0:T(8,128)(2,1)S(1)}, u32[]{:S(2)}, u32[]{:S(2)}) collective-permute-start(bf16[8,7168]{1,0:T(8,128)(2,1)S(1)} %get-tuple-element.64), channel_id=1, source_target_pairs={{0,1},{1,0},{2,3},{3,2},{4,5},{5,4},{6,7},{7,6},{8,9},{9,8},{10,11... | collective-permute-start | bytes 344072 | tf_op jit(solution)/shard_map/ppermute | solution.py:26
  51.8 2.8 %collective-permute-start.29 = (bf16[8,7168]{1,0:T(8,128)(2,1)S(1)}, bf16[8,7168]{1,0:T(8,128)(2,1)S(1)}, u32[]{:S(2)}, u32[]{:S(2)}) collective-permute-start(bf16[8,7168]{1,0:T(8,128)(2,1)S(1)} %get-tuple-element.66), channel_id=1, source_target_pairs={{0,1},{1,0},{2,3},{3,2},{4,5},{5,4},{6,7},{7,6},{8,9},{9,8},{10,11... | collective-permute-start | bytes 344072 | tf_op jit(solution)/shard_map/ppermute | solution.py:26
  52.0 3.7 %collective-permute-start.31 = (bf16[8,7168]{1,0:T(8,128)(2,1)S(1)}, bf16[8,7168]{1,0:T(8,128)(2,1)S(1)}, u32[]{:S(2)}, u32[]{:S(2)}) collective-permute-start(bf16[8,7168]{1,0:T(8,128)(2,1)S(1)} %get-tuple-element.68), channel_id=1, source_target_pairs={{0,1},{1,0},{2,3},{3,2},{4,5},{5,4},{6,7},{7,6},{8,9},{9,8},{10,11... | collective-permute-start | bytes 344072 | tf_op jit(solution)/shard_map/ppermute | solution.py:26
  52.3 6.1 %collective-permute-start.26 = (bf16[8,7168]{1,0:T(8,128)(2,1)S(1)}, bf16[8,7168]{1,0:T(8,128)(2,1)S(1)}, u32[]{:S(2)}, u32[]{:S(2)}) collective-permute-start(bf16[8,7168]{1,0:T(8,128)(2,1)S(1)} %get-tuple-element.62), channel_id=1, source_target_pairs={{0,1},{1,0},{2,3},{3,2},{4,5},{5,4},{6,7},{7,6},{8,9},{9,8},{10,11... | collective-permute-start | bytes 344072 | tf_op jit(solution)/shard_map/ppermute | solution.py:26
  52.8 6.9 %collective-permute-start.28 = (bf16[8,7168]{1,0:T(8,128)(2,1)S(1)}, bf16[8,7168]{1,0:T(8,128)(2,1)S(1)}, u32[]{:S(2)}, u32[]{:S(2)}) collective-permute-start(bf16[8,7168]{1,0:T(8,128)(2,1)S(1)} %shard_map.84), channel_id=1, source_target_pairs={{0,6},{1,7},{2,4},{3,5},{4,2},{5,3},{6,0},{7,1},{8,14},{9,15},{10,... | collective-permute-start | bytes 344072 | tf_op jit(solution)/shard_map/ppermute | solution.py:26
  54.6 6.6 %collective-permute-start.30 = (bf16[8,7168]{1,0:T(8,128)(2,1)S(1)}, bf16[8,7168]{1,0:T(8,128)(2,1)S(1)}, u32[]{:S(2)}, u32[]{:S(2)}) collective-permute-start(bf16[8,7168]{1,0:T(8,128)(2,1)S(1)} %shard_map.85), channel_id=1, source_target_pairs={{0,4},{1,5},{2,6},{3,7},{4,0},{5,1},{6,2},{7,3},{8,12},{9,13},{10,... | collective-permute-start | bytes 344072 | tf_op jit(solution)/shard_map/ppermute | solution.py:26
  55.7 5.9 %collective-permute-start.32 = (bf16[8,7168]{1,0:T(8,128)(2,1)S(1)}, bf16[8,7168]{1,0:T(8,128)(2,1)S(1)}, u32[]{:S(2)}, u32[]{:S(2)}) collective-permute-start(bf16[8,7168]{1,0:T(8,128)(2,1)S(1)} %shard_map.86), channel_id=1, source_target_pairs={{0,2},{1,3},{2,0},{3,1},{4,6},{5,7},{6,4},{7,5},{8,10},{9,11},{10,... | collective-permute-start | bytes 344072 | tf_op jit(solution)/shard_map/ppermute | solution.py:26
  56.6 8.3 %collective-permute-start.18 = (bf16[4,7168]{1,0:T(4,128)(2,1)S(1)}, bf16[4,7168]{1,0:T(4,128)(2,1)S(1)}, u32[]{:S(2)}, u32[]{:S(2)}) collective-permute-start(bf16[4,7168]{1,0:T(4,128)(2,1)S(1)} %get-tuple-element.58), channel_id=1, source_target_pairs={{0,16},{1,17},{2,18},{3,19},{4,20},{5,21},{6,22},{7,23},{8,24},{9,... | collective-permute-start | bytes 172040 | tf_op jit(solution)/shard_map/ppermute | solution.py:26
  61.7 6.7 %collective-permute-start.33 = (bf16[4,7168]{1,0:T(4,128)(2,1)S(1)}, bf16[4,7168]{1,0:T(4,128)(2,1)S(1)}, u32[]{:S(2)}, u32[]{:S(2)}) collective-permute-start(bf16[4,7168]{1,0:T(4,128)(2,1)S(1)} %get-tuple-element.69), channel_id=1, source_target_pairs={{0,24},{1,25},{2,26},{3,27},{4,28},{5,29},{6,30},{7,31},{8,16},{9,... | collective-permute-start | bytes 172040 | tf_op jit(solution)/shard_map/ppermute | solution.py:26
  64.1 4.3 %collective-permute-start.34 = (bf16[4,7168]{1,0:T(4,128)(2,1)S(1)}, bf16[4,7168]{1,0:T(4,128)(2,1)S(1)}, u32[]{:S(2)}, u32[]{:S(2)}) collective-permute-start(bf16[4,7168]{1,0:T(4,128)(2,1)S(1)} %get-tuple-element.70), channel_id=1, source_target_pairs={{0,16},{1,17},{2,18},{3,19},{4,20},{5,21},{6,22},{7,23},{8,24},{9,... | collective-permute-start | bytes 172040 | tf_op jit(solution)/shard_map/ppermute | solution.py:26
